TPU v7x, 32 devices: a whole 2x2x4 slice. The times are simulated.
32 devices in a mesh: grp: 2 (over x), sv: 8 (over z, y), tv: 2 (over core).
Axes of the slice: x: 2, y: 2, z: 4, core: 2. Of those that a mesh axis runs over, the one named last changes fastest.
Arguments:
- teacher_probs: bfloat16 [256, 81920], P(('grp', 'sv'), 'tv'), parts along dimension 0, may hold values from 9.983778e-07 to 0.0099487305
- align_owner: int32 [640, 2], replicated, may hold values from 0 to 7, all different within a row; in each aligned block of 320 rows (0 to 319, 320 to 639, ...) at most 160 rows name the same one
- align_local: int32 [640, 2], replicated, may hold values from 0 to 31
- align_weight: bfloat16 [640, 2], replicated, may hold values from 0.099609375 to 1
- student_logits: bfloat16 [256, 32768], P(('grp', 'tv'), 'sv'), parts along dimension 0, may hold values from -15 to 250
- hidden: bfloat16 [256, 1920], P(('grp', 'sv', 'tv')), parts along dimension 0, may hold values from -6 to 6
Outputs:
- divergence: float32 [256], P(('grp', 'tv')), parts along dimension 0
- logit_grad: bfloat16 [256, 32768], P(('grp', 'tv'), 'sv'), parts along dimension 0
- weight_grad: bfloat16 [1920, 65536], P(None, ('grp', 'sv', 'tv')), parts along dimension 1
There are 2 independent parts, one for each index of `grp`. A program takes and returns all parts, laid end to end along the dimension named above; an argument that names none is the same for every part. Nothing has to cross between parts.
Inputs may be any that keep to these rules, and one draw needn't show every extreme that they name: `align_owner`: the 2 entries of a row name different sv indices. Among the rows of one aligned block of 320 teacher blocks (one half of the teacher vocabulary) no index is named more than 160 times, and in some block an index is named exactly 160 times.
All inputs are finite; a program needn't handle non-finite values.
Results may differ from a plain program's by a relative error of at most 0.0053.
Values may be sent and summed in bfloat16 or wider, within the bound.
No kernel may reach another device: no remote copies, remote signals or barrier semaphores. Data moves between devices by JAX's collectives and lax.ppermute only.
A program may use at most 128 MiB of HBM per device.

v0:
```python
import jax
import jax.numpy as jnp
from jax import lax
from jax.sharding import PartitionSpec as P

BLK = 128
TB = 640
TOPA = 2


def half_pairs(table, half_index, per_half):
    return lax.dynamic_slice_in_dim(table, half_index * per_half, per_half, 0).reshape(-1)


def pair_ranks(owner_list, owners):
    onehot = (owner_list[:, None] == jnp.arange(owners, dtype=jnp.int32)[None, :]).astype(jnp.int32)
    before = jnp.cumsum(onehot, axis=0) - onehot
    return jnp.sum(before * onehot, axis=1)


def send_blocks(owner_list, slot_rank, owners, capacity):
    slot_index = owner_list * capacity + slot_rank
    wanted = jnp.arange(owners * capacity, dtype=jnp.int32)
    matches = slot_index[None, :] == wanted[:, None]
    pair_ids = jnp.arange(owner_list.shape[0], dtype=jnp.int32)
    source = jnp.sum(jnp.where(matches, pair_ids[None, :], 0), axis=1)
    return source // TOPA


def slot_matrix(owner_list, local_list, weight_list, slot_rank, owner_index, capacity, blocks):
    slot_ids = jnp.arange(capacity, dtype=jnp.int32)
    matches = (owner_list[None, :] == owner_index) & (slot_rank[None, :] == slot_ids[:, None])
    weighted = jnp.where(matches, weight_list[None, :], jnp.zeros((), jnp.bfloat16))
    placing = (local_list[:, None] == jnp.arange(blocks, dtype=jnp.int32)[None, :]).astype(
        jnp.bfloat16
    )
    return jnp.dot(weighted, placing, preferred_element_type=jnp.float32).astype(jnp.bfloat16)


def body(teacher_probs, align_owner, align_local, align_weight, student_logits, hidden):
    owners = lax.axis_size("sv")
    halves = lax.axis_size("tv")
    owner_index = lax.axis_index("sv")
    half_index = lax.axis_index("tv")
    row_count = teacher_probs.shape[0]
    blocks = student_logits.shape[1] // BLK
    per_half = TB // halves
    capacity = max(2, 2 * per_half * TOPA // owners)
    own_list = half_pairs(align_owner, half_index, per_half)
    slot_rank = pair_ranks(own_list, owners)
    source = send_blocks(own_list, slot_rank, owners, capacity)
    tile_view = teacher_probs.reshape(row_count, per_half, BLK)
    outgoing = jnp.take(tile_view, source, axis=1).reshape(row_count, owners, capacity, BLK)
    incoming = lax.all_to_all(
        lax.all_to_all(outgoing, "sv", split_axis=1, concat_axis=1, tiled=True),
        "tv",
        split_axis=1,
        concat_axis=2,
        tiled=True,
    )
    tables = []
    for which_half in range(halves):
        part_owner = align_owner[which_half * per_half : (which_half + 1) * per_half].reshape(-1)
        part_local = align_local[which_half * per_half : (which_half + 1) * per_half].reshape(-1)
        part_weight = align_weight[which_half * per_half : (which_half + 1) * per_half].reshape(-1)
        part_rank = pair_ranks(part_owner, owners)
        tables.append(
            slot_matrix(
                part_owner, part_local, part_weight, part_rank, owner_index, capacity, blocks
            )
        )
    slot_weights = jnp.concatenate(tables, axis=0)
    mapped = jnp.einsum("rsck,cb->srbk", incoming, slot_weights, preferred_element_type=jnp.float32)
    mapped = mapped.reshape(owners // halves * row_count, blocks * BLK)
    logits = student_logits.astype(jnp.float32)
    positive = mapped > 0
    safe_mapped = jnp.where(positive, mapped, 1.0)
    mass_local = jnp.sum(mapped, axis=1)
    entropy_local = jnp.sum(jnp.where(positive, mapped * jnp.log(safe_mapped), 0.0), axis=1)
    cross_local = jnp.sum(mapped * logits, axis=1)
    peak_local = jnp.max(logits, axis=1)
    peak_value = lax.pmax(peak_local, "sv")
    exp_local = jnp.sum(jnp.exp(logits - peak_value[:, None]), axis=1)
    exp_total, mass_total, entropy_part, cross_part = lax.psum(
        (exp_local, mass_local, entropy_local, cross_local), "sv"
    )
    log_norm = peak_value + jnp.log(exp_total)
    divergence = (entropy_part - cross_part) / mass_total - jnp.log(mass_total) + log_norm
    target = mapped / mass_total[:, None]
    scale_factor = float(blocks * BLK * owners)
    logit_grad = ((jnp.exp(logits - log_norm[:, None]) - target) * scale_factor).astype(
        jnp.bfloat16
    )
    grad_columns = lax.all_to_all(logit_grad, "tv", split_axis=1, concat_axis=0, tiled=True)
    hidden_all = lax.all_gather(hidden, ("sv", "tv"), axis=0, tiled=True)
    weight_grad = lax.dot_general(
        hidden_all, grad_columns, (((0,), (0,)), ((), ())), preferred_element_type=jnp.float32
    )
    return (divergence, logit_grad, weight_grad.astype(jnp.bfloat16))


def solution(mesh):
    return jax.shard_map(
        body,
        mesh=mesh,
        in_specs=(
            P(("grp", "sv"), "tv"),
            P(),
            P(),
            P(),
            P(("grp", "tv"), "sv"),
            P(("grp", "sv", "tv"), None),
        ),
        out_specs=(P(("grp", "tv")), P(("grp", "tv"), "sv"), P(None, ("grp", "sv", "tv"))),
        check_vma=False,
    )
```

profile of v0, /device:TPU:0, one launch (start us, length us, event | category | flops | bytes accessed | tf_op | source)
XLA Modules:
  0.0 225.0 jit_solution(12094418232159165311)
XLA Ops:
  0.7 0.9 fusion.44
  2.0 1.4 reduce-window.26
  4.0 0.4 select_reduce_fusion
  4.6 0.2 copy_bitcast_fusion
  4.8 5.0 %gather_fusion = bf16[1280,16,128]{2,1,0:T(8,128)(2,1)} fusion(bf16[16,320,128]{2,0,1:T(8,128)(2,1)S(1)} %copy_bitcast_fusion, s32[2048]{0:T(1024)S(1)} %pad_clamp_fusion), kind=kCustom, calls=%fused_computation | custom fusion | bytes 10490880 | tf_op jit(solution)/shard_map/jit(_take)/gather | solution.py:53
  9.8 5.9 %copy_select_fusion = bf16[16,8,160,128]{3,2,0,1:T(8,128)(2,1)} fusion(bf16[16,8,160,128]{3,0,2,1:T(8,128)(2,1)} %bitcast.72, pred[8,160]{1,0:T(8,128)(4,1)S(1)} %compare_and_fusion), kind=kLoop, calls=%fused_computation.2 | loop fusion | flops 2621440 | bytes 10487040 | tf_op jit(solution)/shard_map/jit(_take)/select_n | solution.py:53
  15.7 7.4 %all-to-all-start = ((bf16[16,8,160,128]{3,2,0,1:T(8,128)(2,1)}), bf16[16,8,160,128]{3,2,0,1:T(8,128)(2,1)}, u32[]{:S(2)}, u32[]{:S(2)}) async-start(bf16[16,8,160,128]{3,2,0,1:T(8,128)(2,1)} %copy_select_fusion), calls=%async_computation | async-start | bytes 10485760 | tf_op jit(solution)/shard_map/all_to_all | solution.py:55
  24.7 1.4 reduce-window.20
  27.0 1.4 reduce-window.24
  29.4 98.6 %pmax.7 = f32[64]{0:T(128)S(1)} all-reduce(bf16[64]{0:T(256)(128)(2,1)S(1)} %reduce_max.14), channel_id=1, replica_groups=mesh['grp'=2,'sv'=8,'tv'=2] {'sv'}, use_global_device_ids=true, to_apply=%region_17.18 | all-reduce | flops 64 | bytes 384 | tf_op jit(solution)/shard_map/pmax | solution.py:82
  128.2 0.4 convolution_convert_fusion.1
  128.6 0.5 convolution_convert_fusion
  129.1 41.4 %all_gather.3 = bf16[128,1920]{1,0:T(8,128)(2,1)} all-gather(bf16[8,1920]{1,0:T(8,128)(2,1)S(1)} %copy-done.3), channel_id=1, replica_groups=mesh['grp'=2,'sv'=8,'tv'=2] {'sv','tv'}, dimensions={0}, use_global_device_ids=true | all-gather | bytes 522240 | tf_op jit(solution)/shard_map/all_gather | solution.py:95
  170.5 9.4 %all_to_all.42 = bf16[16,8,160,128]{3,2,0,1:T(8,128)(2,1)S(1)} all-to-all(bf16[16,8,160,128]{3,2,0,1:T(8,128)(2,1)} %all-to-all-done), channel_id=1, replica_groups=mesh['grp'=2,'sv'=8,'tv'=2] {'tv'}, dimensions={1} | all-to-all | bytes 10485760 | tf_op jit(solution)/shard_map/all_to_all | solution.py:54
  179.9 0.8 copy.103
  180.6 2.1 fusion.2
  183.0 1.3 copy.105
  184.3 0.9 fusion.3
  185.2 17.1 %all-reduce = (f32[64]{0:T(128)S(1)}, f32[64]{0:T(128)S(1)}, f32[64]{0:T(128)S(1)}, f32[64]{0:T(128)S(1)}) all-reduce(f32[64]{0:T(128)S(1)} %get-tuple-element.21, f32[64]{0:T(128)S(1)} %reduce_sum.90, f32[64]{0:T(128)S(1)} %reduce_sum.87, f32[64]{0:T(128)S(1)} %get-tuple-element.20), channel_id=1, replica_groups=mesh['grp'=2,'sv'=8,'tv'=2] {'sv'}, use_global_device_ids=true, to_apply=%region_19.20 | all-reduce | flops 256 | bytes 2048 | tf_op jit(solution)/shard_map/psum | solution.py:84
  202.4 0.5 subtract_add_fusion
  202.9 0.9 fusion.9
  203.9 4.2 %all_to_all.43 = bf16[64,2,2048]{2,0,1:T(8,128)(2,1)S(1)} all-to-all(bf16[64,2,2048]{2,0,1:T(8,128)(2,1)S(1)} %bitcast.76), channel_id=1, replica_groups=mesh['grp'=2,'sv'=8,'tv'=2] {'tv'}, dimensions={1} | all-to-all | bytes 1048576 | tf_op jit(solution)/shard_map/all_to_all | solution.py:94
  208.0 6.3 %convert_bitcast_fusion = bf16[1920,2048]{0,1:T(8,128)(2,1)} fusion(bf16[128,2048]{1,0:T(8,128)(2,1)S(1)} %bitcast.75, bf16[128,1920]{1,0:T(8,128)(2,1)} %all_gather.3), kind=kOutput, calls=%fused_computation.1 | convolution fusion | flops 1010565120 | bytes 8880128 | tf_op jit(solution)/shard_map/dot_general | solution.py:96
  214.4 10.6 %copy.108 = bf16[1920,2048]{1,0:T(8,128)(2,1)} copy(bf16[1920,2048]{0,1:T(8,128)(2,1)} %convert_bitcast_fusion) | data formatting | bytes 15728640
  (62 shorter events, 5.0 us)
Async XLA Ops:
  0.6 3.9 %copy-start = (bf16[16,40960]{1,0:T(8,128)(2,1)S(1)}, bf16[16,40960]{1,0:T(8,128)(2,1)}, u32[]{:S(2)}) copy-start(bf16[16,40960]{1,0:T(8,128)(2,1)} %param.6) | copy-start | bytes 3932164
  15.7 8.3 %copy-start.5 = (bf16[640,2]{0,1:T(2,128)(2,1)S(1)}, bf16[640,2]{0,1:T(2,128)(2,1)}, u32[]{:S(2)}) copy-start(bf16[640,2]{0,1:T(2,128)(2,1)} %param.9) | copy-start | bytes 7684
  15.7 10.9 %copy-start.4 = (s32[640,2]{0,1:T(2,128)S(1)}, s32[640,2]{0,1:T(2,128)}, u32[]{:S(2)}) copy-start(s32[640,2]{0,1:T(2,128)} %param.8) | copy-start | bytes 15364
  15.7 13.5 %copy-start.1 = (bf16[64,4096]{1,0:T(8,128)(2,1)S(1)}, bf16[64,4096]{1,0:T(8,128)(2,1)}, u32[]{:S(2)}) copy-start(bf16[64,4096]{1,0:T(8,128)(2,1)} %param.10) | copy-start | bytes 1572868
  15.7 113.4 %copy-start.3 = (bf16[8,1920]{1,0:T(8,128)(2,1)S(1)}, bf16[8,1920]{1,0:T(8,128)(2,1)}, u32[]{:S(2)}) copy-start(bf16[8,1920]{1,0:T(8,128)(2,1)} %param.11) | copy-start | bytes 92164
  15.7 154.8 %all-to-all-start = ((bf16[16,8,160,128]{3,2,0,1:T(8,128)(2,1)}), bf16[16,8,160,128]{3,2,0,1:T(8,128)(2,1)}, u32[]{:S(2)}, u32[]{:S(2)}) async-start(bf16[16,8,160,128]{3,2,0,1:T(8,128)(2,1)} %copy_select_fusion), calls=%async_computation | async-start | bytes 10485760 | tf_op jit(solution)/shard_map/all_to_all | solution.py:55
  203.8 10.6 %copy-start.2 = (bf16[64,4096]{1,0:T(8,128)(2,1)}, bf16[64,4096]{1,0:T(8,128)(2,1)S(1)}, u32[]{:S(2)}) copy-start(bf16[64,4096]{1,0:T(8,128)(2,1)S(1)} %fusion.9) | copy-start | bytes 1572868
where the time goes:
time: 226 us; the launch traced here: 225 us
  blocking collectives  171 us (76%)
  local copies, waits for them, and re-layouts  22.7 us (10%)
  other arithmetic  13.9 us (6%)
  matrix products  9.33 us (4%)
  starting transfers between devices  7.42 us (3%)
    pmax x1, blocking collectives, body(): peak_value = lax.pmax(peak_local, 'sv')  98.6 us
    all_gather x1, blocking collectives, body(): hidden_all = lax.all_gather(hidden, ('sv', 'tv'), axis=0, tiled=True)  41.4 us
    psum x1, blocking collectives, body(): lax.psum((exp_local, mass_local, entropy_local, cross_local), 'sv')  17.1 us
    unnamed x13, local copies, waits for them, and re-layouts  10.6 us
    all_to_all x1, blocking collectives, body(): lax.all_to_all(lax.all_to_all(outgoing, 'sv', split_axis=1, concat_axis=1...  9.38 us
    all_to_all x1, starting transfers between devices, body(): lax.all_to_all(outgoing, 'sv', split_axis=1, concat_axis=1, tiled=True)  7.42 us
    dot_general x1, matrix products, body(): lax.dot_general(hidden_all, grad_columns, (((0,), (0,)), ((), ())), prefe...  6.35 us
    select_n x2, other arithmetic, body(): jnp.take(tile_view, source, axis=1)  5.96 us
  transfers between devices with their start and end apart: 1, of which 0 were waited for; matrix products, arithmetic and copies ran while one was open for 3% of the time, Pallas kernels for 0%

commit v1 on v0

v1 whole, which is shorter than its diff:
```python
import jax
import jax.numpy as jnp
from jax import lax
from jax.experimental import pallas as pl
from jax.experimental.pallas import tpu as pltpu
from jax.sharding import PartitionSpec as P

BLK = 128
TB = 640
MASS_ROWS = 16
VMEM_LIMIT = 48 * 1024 * 1024


def swap_halves(x):
    return lax.ppermute(x, "tv", [(0, 1), (1, 0)])


def block_weights(row_of, weight, rows):
    row_ids = lax.broadcasted_iota(jnp.int32, (rows + MASS_ROWS, row_of.shape[1]), 0)
    total = jnp.zeros(row_ids.shape, jnp.float32)
    for slot in range(row_of.shape[0]):
        hit = (row_ids == row_of[slot][None, :]) | (row_ids == rows + slot)
        total = total + jnp.where(hit, weight[slot].astype(jnp.float32)[None, :], 0.0)
    return total.astype(jnp.bfloat16)


def spread_tokens(t_ref, s_ref):
    tokens = t_ref.shape[0]
    count = t_ref.shape[1] // BLK
    step = 16

    def some(i, carry):
        for j in range(step):
            k = i * step + j
            tile = t_ref[:, pl.ds(pl.multiple_of(k * BLK, BLK), BLK)]
            s_ref[pl.ds(pl.multiple_of(k * tokens, tokens), tokens), :] = tile.astype(jnp.float32)
        return carry

    lax.fori_loop(0, count // step, some, 0)


def token_pair(s_ref, t, tokens):
    count = s_ref.shape[0] // tokens
    both = [s_ref[pl.ds(t + i, count, stride=tokens), :].astype(jnp.bfloat16) for i in range(2)]
    return jnp.concatenate(both, axis=1)


def map_own_kernel(w_ref, t_ref, o_ref, s_ref):
    tokens = t_ref.shape[0]
    spread_tokens(t_ref, s_ref)
    for t in range(0, tokens, 2):
        o_ref[:, t * BLK : (t + 2) * BLK] = jnp.dot(
            w_ref[...], token_pair(s_ref, t, tokens), preferred_element_type=jnp.float32
        )


def map_rest_kernel(w_ref, t_ref, p_ref, o_ref, s_ref, m_ref):
    tokens = t_ref.shape[0]
    owners, _, width = o_ref.shape
    rows = w_ref.shape[0] - MASS_ROWS
    spread_tokens(t_ref, s_ref)
    for t in range(0, tokens, 2):
        both = p_ref[:, t * BLK : (t + 2) * BLK] + jnp.dot(
            w_ref[...], token_pair(s_ref, t, tokens), preferred_element_type=jnp.float32
        )
        for i in range(2):
            one = both[:, i * BLK : (i + 1) * BLK]
            mass = jnp.sum(jnp.sum(one[rows : rows + 8], axis=0, keepdims=True), axis=1, keepdims=True)
            m_ref[pl.ds(t + i, rows, stride=tokens), :] = one[:rows] * (1.0 / mass)

    def owner(q, carry):
        for b in range(width // BLK):
            first = (q * (width // BLK) + b) * tokens
            tile = m_ref[pl.ds(pl.multiple_of(first, tokens), tokens), :]
            o_ref[q, :, b * BLK : (b + 1) * BLK] = tile.astype(jnp.bfloat16)
        return carry

    lax.fori_loop(0, owners, owner, 0)


def grad_kernel(scale, target_ref, logits_ref, norm_ref, grad_ref, part_ref):
    target = target_ref[...].astype(jnp.float32)
    log_probs = logits_ref[...].astype(jnp.float32) - norm_ref[...]
    grad_ref[...] = ((jnp.exp(log_probs) - target) * scale).astype(jnp.bfloat16)
    positive = target > 0
    terms = target * (jnp.log(jnp.where(positive, target, 1.0)) - log_probs)
    part_ref[...] = jnp.sum(jnp.where(positive, terms, 0.0), axis=1, keepdims=True)


def weight_kernel(hidden_ref, grad_ref, o_ref):
    o_ref[...] = jnp.dot(
        hidden_ref[...], grad_ref[...], preferred_element_type=jnp.float32
    ).astype(jnp.bfloat16)


def whole():
    return pl.BlockSpec(memory_space=pltpu.VMEM)


def params():
    return pltpu.CompilerParams(vmem_limit_bytes=VMEM_LIMIT)


def body(teacher_probs, align_owner, align_local, align_weight, student_logits, hidden):
    owners = lax.axis_size("sv")
    halves = lax.axis_size("tv")
    half_index = lax.axis_index("tv")
    tokens = teacher_probs.shape[0]
    columns = student_logits.shape[1]
    blocks = columns // BLK
    mine = blocks // halves
    width = mine * BLK
    rows = owners * mine
    per_half = TB // halves
    group_tokens = owners * tokens
    half_tokens = student_logits.shape[0]

    teacher_other = swap_halves(teacher_probs)

    logit_halves = student_logits.reshape(half_tokens, halves, width)
    keep = lax.dynamic_index_in_dim(logit_halves, half_index, 1, keepdims=False)
    give = lax.dynamic_index_in_dim(logit_halves, 1 - half_index, 1, keepdims=False)
    got = swap_halves(give)
    first = half_index == 0
    logits = jnp.concatenate([jnp.where(first, keep, got), jnp.where(first, got, keep)], axis=0)

    hidden_mine = lax.all_to_all(
        jnp.broadcast_to(hidden[None], (owners,) + hidden.shape), "sv", 0, 0, tiled=True
    )
    hidden_other = swap_halves(hidden_mine)
    hidden_pair = jnp.stack(
        [jnp.where(first, hidden_mine, hidden_other), jnp.where(first, hidden_other, hidden_mine)], axis=1
    )
    hidden_t = hidden_pair.reshape(group_tokens, hidden.shape[1]).T

    wide = student_logits.astype(jnp.float32)
    peak = jnp.max(wide, axis=1)
    sums = jnp.sum(jnp.exp(wide - peak[:, None]), axis=1)
    stats = jnp.broadcast_to(jnp.stack([peak, sums])[None], (owners * halves, 2, half_tokens))
    stats = lax.all_to_all(stats, ("sv", "tv"), 0, 0, tiled=True)
    stats = stats.reshape(owners, halves, 2, half_tokens)
    peaks, sums = stats[:, :, 0], stats[:, :, 1]
    top = jnp.max(peaks, axis=0)
    log_norm = top + jnp.log(jnp.sum(sums * jnp.exp(peaks - top[None]), axis=0))
    log_norm = log_norm.reshape(group_tokens, 1)

    local = align_local.T - half_index * mine
    row_of = jnp.where((local >= 0) & (local < mine), align_owner.T * mine + local, -1)
    weight = align_weight.T
    cut = lambda x, which: lax.dynamic_slice_in_dim(x, which * per_half, per_half, 1)
    w_own = block_weights(cut(row_of, half_index), cut(weight, half_index), rows)
    w_rest = block_weights(cut(row_of, 1 - half_index), cut(weight, 1 - half_index), rows)
    flops = 2 * (rows + MASS_ROWS) * per_half * tokens * BLK
    spread = pltpu.VMEM((per_half * tokens, BLK), jnp.float32)
    part = pl.pallas_call(
        map_own_kernel,
        out_shape=jax.ShapeDtypeStruct((rows + MASS_ROWS, tokens * BLK), jnp.float32),
        in_specs=[whole()] * 2,
        out_specs=whole(),
        scratch_shapes=[spread],
        compiler_params=params(),
        cost_estimate=pl.CostEstimate(flops=flops, bytes_accessed=3 << 20, transcendentals=0),
        name="map_own",
    )(w_own, teacher_probs)
    outgoing = pl.pallas_call(
        map_rest_kernel,
        out_shape=jax.ShapeDtypeStruct((owners, tokens, width), jnp.bfloat16),
        in_specs=[whole()] * 3,
        out_specs=whole(),
        scratch_shapes=[spread, pltpu.VMEM((rows * tokens, BLK), jnp.float32)],
        compiler_params=params(),
        cost_estimate=pl.CostEstimate(flops=flops, bytes_accessed=4 << 20, transcendentals=0),
        name="map_rest",
    )(w_rest, teacher_other, part)
    target = lax.all_to_all(outgoing, "sv", 0, 0, tiled=True).reshape(group_tokens, width)

    scale = float(columns * owners)
    grad, terms = pl.pallas_call(
        lambda *refs: grad_kernel(scale, *refs),
        out_shape=(
            jax.ShapeDtypeStruct((group_tokens, width), jnp.bfloat16),
            jax.ShapeDtypeStruct((group_tokens, 1), jnp.float32),
        ),
        in_specs=[whole()] * 3,
        out_specs=(whole(), whole()),
        compiler_params=params(),
        cost_estimate=pl.CostEstimate(
            flops=10 * group_tokens * width,
            bytes_accessed=6 * group_tokens * width,
            transcendentals=2 * group_tokens * width,
        ),
        name="logit_grad",
    )(target, logits, log_norm)

    grad_halves = grad.reshape(halves, half_tokens, width)
    keep = lax.dynamic_index_in_dim(grad_halves, half_index, 0, keepdims=False)
    give = lax.dynamic_index_in_dim(grad_halves, 1 - half_index, 0, keepdims=False)
    got = swap_halves(give)
    logit_grad = jnp.concatenate([jnp.where(first, keep, got), jnp.where(first, got, keep)], axis=1)

    terms = jnp.broadcast_to(terms.reshape(1, halves, half_tokens), (owners, halves, half_tokens))
    terms = lax.all_to_all(terms.reshape(owners * halves, half_tokens), ("sv", "tv"), 0, 0, tiled=True)
    divergence = jnp.sum(terms, axis=0)

    features = hidden.shape[1]
    tile = features // 8
    weight_grad = pl.pallas_call(
        weight_kernel,
        out_shape=jax.ShapeDtypeStruct((features, width), jnp.bfloat16),
        grid=(features // tile,),
        in_specs=[
            pl.BlockSpec((tile, group_tokens), lambda i: (i, 0)),
            pl.BlockSpec((group_tokens, width), lambda i: (0, 0)),
        ],
        out_specs=pl.BlockSpec((tile, width), lambda i: (i, 0)),
        compiler_params=params(),
        cost_estimate=pl.CostEstimate(
            flops=2 * features * group_tokens * width,
            bytes_accessed=2 * (features * width + group_tokens * (features + width)),
            transcendentals=0,
        ),
        name="weight_grad",
    )(hidden_t, grad)
    return (divergence, logit_grad, weight_grad)


def solution(mesh):
    return jax.shard_map(
        body,
        mesh=mesh,
        in_specs=(
            P(("grp", "sv"), "tv"),
            P(),
            P(),
            P(),
            P(("grp", "tv"), "sv"),
            P(("grp", "sv", "tv"), None),
        ),
        out_specs=(P(("grp", "tv")), P(("grp", "tv"), "sv"), P(None, ("grp", "sv", "tv"))),
        check_vma=False,
    )
```

time: 226 us -> 69.8 us (0.31)
  blocking collectives: 171 us -> 0 us
  waiting for transfers between devices: 0.01 us -> 25.5 us
  local copies, waits for them, and re-layouts: 22.7 us -> 6.79 us
  Pallas kernels: 0 us -> 12.1 us
  starting transfers between devices: 7.42 us -> 18.7 us
  matrix products: 9.33 us -> 0 us
  other arithmetic: 13.9 us -> 5.24 us
    pmax x1 -> x0, blocking collectives: 98.6 us -> none  [body(): peak_value = lax.pmax(peak_local, 'sv')]
    all_gather x1 -> x0, blocking collectives: 41.4 us -> none  [body(): hidden_all = lax.all_gather(hidden, ('sv', 'tv'), axis=0, tiled=True)]
    all_to_all x1 -> x4, waiting for transfers between devices: 0.01 us -> 25.5 us  [the longest x1 13.2 us: body(): lax.all_to_all(outgoing, 'sv', 0, 0, tiled=True)]
    psum x1 -> x0, blocking collectives: 17.1 us -> none  [body(): lax.psum((exp_local, mass_local, entropy_local, cross_local), 'sv')]
    all_to_all x2 -> x0, blocking collectives: 13.5 us -> none  [the longest x1 9.38 us: body(): lax.all_to_all(lax.all_to_all(outgoing, 'sv', split_axis=1, concat_axis=1...]
    pallas_call x0 -> x4, Pallas kernels: none -> 12.1 us  [the longest x1 5.82 us: body(): pl.pallas_call(weight_kernel, out_shape=jax.ShapeDtypeStruct((features, w...]
    all_to_all x1 -> x4, starting transfers between devices: 7.42 us -> 18.1 us  [the longest x1 7.39 us: body(): stats = lax.all_to_all(stats, ('sv', 'tv'), 0, 0, tiled=True)]
    dot_general x4 -> x0, matrix products: 9.33 us -> none  [the longest x1 6.35 us: body(): lax.dot_general(hidden_all, grad_columns, (((0,), (0,)), ((), ())), prefe...]
  transfers between devices with their start and end apart: 1 -> 8, of which waited for: 0 -> 4; matrix products, arithmetic and copies ran while one was open for 3% -> 11% of each run, Pallas kernels for 0% -> 17%
where the time goes in v1:
time: 69.8 us; the launch traced here: 69.2 us
  waiting for transfers between devices  25.5 us (37%)
  starting transfers between devices  18.7 us (27%)
  Pallas kernels  12.1 us (17%)
  local copies, waits for them, and re-layouts  6.79 us (10%)
  other arithmetic  5.24 us (8%)
  between operations  0.88 us (1%)
    all_to_all x1, waiting for transfers between devices, body(): lax.all_to_all(outgoing, 'sv', 0, 0, tiled=True)  13.2 us
    all_to_all x1, starting transfers between devices, body(): stats = lax.all_to_all(stats, ('sv', 'tv'), 0, 0, tiled=True)  7.39 us
    all_to_all x1, waiting for transfers between devices, body(): lax.all_to_all(jnp.broadcast_to(hidden[None], (owners,) + hidden.shape),...  7.36 us
    pallas_call x1, Pallas kernels, body(): pl.pallas_call(weight_kernel, out_shape=jax.ShapeDtypeStruct((features, w...  5.82 us
    all_to_all x1, waiting for transfers between devices, body(): stats = lax.all_to_all(stats, ('sv', 'tv'), 0, 0, tiled=True)  4.42 us
    pallas_call x1, Pallas kernels, body(): pl.pallas_call(map_rest_kernel, out_shape=jax.ShapeDtypeStruct((owners, t...  4.2 us
    all_to_all x1, starting transfers between devices, body(): lax.all_to_all(terms.reshape(owners * halves, half_tokens), ('sv', 'tv'),...  3.82 us
    all_to_all x1, starting transfers between devices, body(): lax.all_to_all(outgoing, 'sv', 0, 0, tiled=True)  3.49 us
  transfers between devices with their start and end apart: 8, of which 4 were waited for; matrix products, arithmetic and copies ran while one was open for 11% of the time, Pallas kernels for 17%

profile of v1, /device:TPU:0, one launch (start us, length us, event | category | flops | bytes accessed | tf_op | source)
XLA Modules:
  0.0 69.2 jit_solution(9045917716475711543)
XLA Ops:
  0.6 1.4 %reshape.66 = bf16[64,2,2048]{2,1,0:T(2,128)(2,1)S(1)} reshape(bf16[64,4096]{1,0:T(8,128)(2,1)} %param.10) | data formatting | bytes 1048576 | tf_op jit(solution)/shard_map/reshape | solution.py:120
  2.1 1.1 %constant_dynamic-slice_fusion.1 = (bf16[64,1,2048]{2,1,0:T(2,128)(2,1)S(1)}, bf16[64,1,2048]{2,1,0:T(2,128)(2,1)S(1)}) fusion(bf16[64,2,2048]{2,1,0:T(2,128)(2,1)S(1)} %reshape.66, s32[]{:T(128)S(6)} %select_n.76, s32[]{:T(128)S(6)} %select_n.77), kind=kLoop, calls=%fused_computation.33 | loop fusion | bytes 1048584 | tf_op jit(solution)/shard_map/jit(dynamic_index_in_dim)/dynamic_slice | solution.py:121
  3.2 0.9 %copy.58 = bf16[64,1,2048]{2,0,1:T(8,128)(2,1)} copy(bf16[64,1,2048]{2,1,0:T(2,128)(2,1)S(1)} %get-tuple-element.20) | data formatting | bytes 524288
  5.2 0.7 reshape.84
  5.8 7.4 %all-to-all-start.1 = ((f32[16,1,128]{2,1,0:T(1,128)}), f32[16,1,128]{2,1,0:T(1,128)S(1)}, u32[]{:S(2)}, u32[]{:S(2)}) async-start(f32[16,1,128]{2,1,0:T(1,128)} %reshape.84), calls=%async_computation.1 | async-start | bytes 16384 | tf_op jit(solution)/shard_map/all_to_all | solution.py:140
  13.7 1.4 %map_own.1.p_ref = f32[144,2048]{1,0:T(8,128)S(1)} custom-call(bf16[144,320]{1,0:T(8,128)(2,1)S(1)} %get-tuple-element.27.w_ref, bf16[16,40960]{1,0:T(8,128)(2,1)S(1)} %copy-done), custom_call_target="tpu_custom_call" | custom-call | flops 188743680 | bytes 3145728 | tf_op jit(solution)/shard_map/map_own/pallas_call | solution.py:155
  15.1 4.4 %all-to-all-done.1 = f32[16,1,128]{2,1,0:T(1,128)S(1)} async-done(((f32[16,1,128]{2,1,0:T(1,128)}), f32[16,1,128]{2,1,0:T(1,128)S(1)}, u32[]{:S(2)}, u32[]{:S(2)}) %all-to-all-start.1) | async-done | bytes 8224 | tf_op jit(solution)/shard_map/all_to_all | solution.py:140
  19.6 0.7 %broadcast_in_dim.96 = bf16[8,8,1920]{2,1,0:T(8,128)(2,1)} broadcast(bf16[8,1920]{1,0:T(8,128)(2,1)S(1)} %copy-done.2), dimensions={1,2} | broadcast | bytes 276480 | tf_op jit(solution)/shard_map/broadcast_in_dim | solution.py:128
  20.3 3.4 %all-to-all-start.3 = ((bf16[8,8,1920]{2,1,0:T(8,128)(2,1)}), bf16[8,8,1920]{2,1,0:T(8,128)(2,1)S(1)}, u32[]{:S(2)}, u32[]{:S(2)}) async-start(bf16[8,8,1920]{2,1,0:T(8,128)(2,1)} %broadcast_in_dim.96), calls=%async_computation.3 | async-start | bytes 491520 | tf_op jit(solution)/shard_map/all_to_all | solution.py:127
  23.7 0.5 broadcast.41
  24.2 0.7 reduce.20
  25.2 7.4 %all-to-all-done.3 = bf16[8,8,1920]{2,1,0:T(8,128)(2,1)S(1)} async-done(((bf16[8,8,1920]{2,1,0:T(8,128)(2,1)}), bf16[8,8,1920]{2,1,0:T(8,128)(2,1)S(1)}, u32[]{:S(2)}, u32[]{:S(2)}) %all-to-all-start.3) | async-done | bytes 245792 | tf_op jit(solution)/shard_map/all_to_all | solution.py:127
  32.5 4.2 %map_rest.1 = bf16[8,16,2048]{2,1,0:T(8,128)(2,1)} custom-call(bf16[144,320]{1,0:T(8,128)(2,1)S(1)} %get-tuple-element.28.w_ref, bf16[16,40960]{1,0:T(8,128)(2,1)} %collective-permute-done.t_ref, f32[144,2048]{1,0:T(8,128)S(1)} %map_own.1.p_ref), custom_call_target="tpu_custom_call" | custom-call | flops 188743680 | bytes 4194304 | tf_op jit(solution)/shard_map/map_rest/pallas_call | solution.py:165
  36.8 3.5 %all-to-all-start = ((bf16[8,16,2048]{2,1,0:T(8,128)(2,1)}), bf16[8,16,2048]{2,1,0:T(8,128)(2,1)S(1)}, u32[]{:S(2)}, u32[]{:S(2)}) async-start(bf16[8,16,2048]{2,1,0:T(8,128)(2,1)} %map_rest.1), calls=%async_computation | async-start | bytes 1048576 | tf_op jit(solution)/shard_map/all_to_all | solution.py:175
  40.3 1.1 %broadcast_select_fusion.1 = (bf16[64,2048]{1,0:T(8,128)(2,1)S(1)}, bf16[64,2048]{1,0:T(8,128)(2,1)S(1)}) fusion(bf16[64,2048]{1,0:T(8,128)(2,1)} %collective-permute-done.1, pred[]{:T(512)S(6)} %eq.71, bf16[64,1,2048]{2,1,0:T(2,128)(2,1)S(1)} %get-tuple-element.19), kind=kLoop, calls=%fused_computation.10 | loop fusion | flops 262144 | bytes 1048577 | tf_op jit(solution)/shard_map/jit(_where)/select_n | solution.py:125
  41.4 1.0 %select_bitcast_fusion.1 = (bf16[8,1,8,1920]{3,2,0,1:T(8,128)(2,1)S(1)}, bf16[8,1,8,1920]{3,2,0,1:T(8,128)(2,1)S(1)}) fusion(bf16[8,8,1920]{2,1,0:T(8,128)(2,1)S(1)} %all-to-all-done.3, bf16[8,8,1920]{2,1,0:T(8,128)(2,1)} %collective-permute-done.3, pred[]{:T(512)S(6)} %eq.71), kind=kLoop, calls=%fused_computation.12 | loop fusion | flops 245760 | bytes 983041 | tf_op jit(solution)/shard_map/stack | solution.py:131
  42.4 13.2 %all-to-all-done = bf16[8,16,2048]{2,1,0:T(8,128)(2,1)S(1)} async-done(((bf16[8,16,2048]{2,1,0:T(8,128)(2,1)}), bf16[8,16,2048]{2,1,0:T(8,128)(2,1)S(1)}, u32[]{:S(2)}, u32[]{:S(2)}) %all-to-all-start) | async-done | bytes 524320 | tf_op jit(solution)/shard_map/all_to_all | solution.py:175
  55.7 0.7 logit_grad.1
  57.0 0.6 broadcast_in_dim.95
  57.7 3.8 %all-to-all-start.2 = ((f32[16,1,64]{2,1,0:T(1,128)}), f32[16,1,64]{2,1,0:T(1,128)S(1)}, u32[]{:S(2)}, u32[]{:S(2)}) async-start(f32[16,1,64]{2,1,0:T(1,128)} %bitcast.12), calls=%async_computation.2 | async-start | bytes 16384 | tf_op jit(solution)/shard_map/all_to_all | solution.py:202
  61.5 5.8 %weight_grad.1 = bf16[1920,2048]{1,0:T(8,128)(2,1)} custom-call(bf16[1920,128]{1,0:T(8,128)(2,1)S(1)} %bitcast.50, bf16[128,2048]{1,0:T(8,128)(2,1)S(1)} %get-tuple-element.6.grad_ref), custom_call_target="tpu_custom_call" | custom-call | flops 1006632960 | bytes 8880128 | tf_op jit(solution)/shard_map/weight_grad/pallas_call | solution.py:207
  67.3 0.5 all-to-all-done.2
  67.8 0.5 reduce_sum.29
  68.4 0.8 %pad_maximum_fusion.1 = bf16[64,4096]{1,0:T(8,128)(2,1)} fusion(bf16[64,2048]{1,0:T(8,128)(2,1)S(1)} %get-tuple-element.16, bf16[64,2048]{1,0:T(8,128)(2,1)S(1)} %get-tuple-element.15), kind=kLoop, calls=%fused_computation.2 | loop fusion | flops 1048576 | bytes 1048576 | tf_op jit(solution)/shard_map/concatenate | solution.py:199
  (46 shorter events, 2.6 us)
Async XLA Ops:
  2.1 2.5 %copy-start = (bf16[16,40960]{1,0:T(8,128)(2,1)S(1)}, bf16[16,40960]{1,0:T(8,128)(2,1)}, u32[]{:S(2)}) copy-start(bf16[16,40960]{1,0:T(8,128)(2,1)} %t_ref.1) | copy-start | bytes 3932164
  2.1 2.5 %copy-start.1 = (bf16[64,4096]{1,0:T(8,128)(2,1)S(1)}, bf16[64,4096]{1,0:T(8,128)(2,1)}, u32[]{:S(2)}) copy-start(bf16[64,4096]{1,0:T(8,128)(2,1)} %param.10) | copy-start | bytes 1572868
  3.2 10.1 %copy-start.5 = (bf16[640,2]{0,1:T(2,128)(2,1)S(1)}, bf16[640,2]{0,1:T(2,128)(2,1)}, u32[]{:S(2)}) copy-start(bf16[640,2]{0,1:T(2,128)(2,1)} %param.9) | copy-start | bytes 7684
  3.2 10.1 %copy-start.3 = (s32[640,2]{0,1:T(2,128)S(1)}, s32[640,2]{0,1:T(2,128)}, u32[]{:S(2)}) copy-start(s32[640,2]{0,1:T(2,128)} %param.7) | copy-start | bytes 15364
  3.2 10.1 %copy-start.4 = (s32[640,2]{0,1:T(2,128)S(1)}, s32[640,2]{0,1:T(2,128)}, u32[]{:S(2)}) copy-start(s32[640,2]{0,1:T(2,128)} %param.8) | copy-start | bytes 15364
  4.1 36.2 %collective-permute-start.1 = (bf16[64,2048]{1,0:T(8,128)(2,1)}, bf16[64,2048]{1,0:T(8,128)(2,1)}, u32[]{:S(2)}, u32[]{:S(2)}) collective-permute-start(bf16[64,2048]{1,0:T(8,128)(2,1)} %bitcast.46), channel_id=1, source_target_pairs={{0,1},{1,0},{2,3},{3,2},{4,5},{5,4},{6,7},{7,6},{8,9},{9,8},{10,11... | collective-permute-start | bytes 786440 | tf_op jit(solution)/shard_map/ppermute | solution.py:15
  4.5 28.0 %collective-permute-start = (bf16[16,40960]{1,0:T(8,128)(2,1)S(1)}, bf16[16,40960]{1,0:T(8,128)(2,1)}, u32[]{:S(2)}, u32[]{:S(2)}) collective-permute-start(bf16[16,40960]{1,0:T(8,128)(2,1)S(1)} %copy-done), channel_id=1, source_target_pairs={{0,1},{1,0},{2,3},{3,2},{4,5},{5,4},{6,7},{7,6},{8,9},{9,8},{10,11... | collective-permute-start | bytes 3932168 | tf_op jit(solution)/shard_map/ppermute | solution.py:15
  5.8 13.7 %all-to-all-start.1 = ((f32[16,1,128]{2,1,0:T(1,128)}), f32[16,1,128]{2,1,0:T(1,128)S(1)}, u32[]{:S(2)}, u32[]{:S(2)}) async-start(f32[16,1,128]{2,1,0:T(1,128)} %reshape.84), calls=%async_computation.1 | async-start | bytes 16384 | tf_op jit(solution)/shard_map/all_to_all | solution.py:140
  13.7 5.8 %copy-start.2 = (bf16[8,1920]{1,0:T(8,128)(2,1)S(1)}, bf16[8,1920]{1,0:T(8,128)(2,1)}, u32[]{:S(2)}) copy-start(bf16[8,1920]{1,0:T(8,128)(2,1)} %param.11) | copy-start | bytes 92164
  20.3 12.3 %all-to-all-start.3 = ((bf16[8,8,1920]{2,1,0:T(8,128)(2,1)}), bf16[8,8,1920]{2,1,0:T(8,128)(2,1)S(1)}, u32[]{:S(2)}, u32[]{:S(2)}) async-start(bf16[8,8,1920]{2,1,0:T(8,128)(2,1)} %broadcast_in_dim.96), calls=%async_computation.3 | async-start | bytes 491520 | tf_op jit(solution)/shard_map/all_to_all | solution.py:127
  32.5 8.9 %collective-permute-start.3 = (bf16[8,8,1920]{2,1,0:T(8,128)(2,1)S(1)}, bf16[8,8,1920]{2,1,0:T(8,128)(2,1)}, u32[]{:S(2)}, u32[]{:S(2)}) collective-permute-start(bf16[8,8,1920]{2,1,0:T(8,128)(2,1)S(1)} %all-to-all-done.3), channel_id=1, source_target_pairs={{0,1},{1,0},{2,3},{3,2},{4,5},{5,4},{6,7},{7,6},{8,9},{9,8},{10,11... | collective-permute-start | bytes 737288 | tf_op jit(solution)/shard_map/ppermute | solution.py:15
  36.8 18.9 %all-to-all-start = ((bf16[8,16,2048]{2,1,0:T(8,128)(2,1)}), bf16[8,16,2048]{2,1,0:T(8,128)(2,1)S(1)}, u32[]{:S(2)}, u32[]{:S(2)}) async-start(bf16[8,16,2048]{2,1,0:T(8,128)(2,1)} %map_rest.1), calls=%async_computation | async-start | bytes 1048576 | tf_op jit(solution)/shard_map/all_to_all | solution.py:175
  56.4 12.0 %collective-permute-start.2 = (bf16[64,2048]{1,0:T(8,128)(2,1)S(1)}, bf16[64,2048]{1,0:T(8,128)(2,1)S(1)}, u32[]{:S(2)}, u32[]{:S(2)}) collective-permute-start(bf16[64,2048]{1,0:T(8,128)(2,1)S(1)} %dynamic-slice_bitcast_fusion), channel_id=1, source_target_pairs={{0,1},{1,0},{2,3},{3,2},{4,5},{5,4},{6,7},{7,6},{8,9},{9,8},{10,11... | collective-permute-start | bytes 786440 | tf_op jit(solution)/shard_map/ppermute | solution.py:15
  57.7 10.2 %all-to-all-start.2 = ((f32[16,1,64]{2,1,0:T(1,128)}), f32[16,1,64]{2,1,0:T(1,128)S(1)}, u32[]{:S(2)}, u32[]{:S(2)}) async-start(f32[16,1,64]{2,1,0:T(1,128)} %bitcast.12), calls=%async_computation.2 | async-start | bytes 16384 | tf_op jit(solution)/shard_map/all_to_all | solution.py:202

commit v2 on v1

--- a/solution.py
+++ b/solution.py
@@ -54,9 +54,10 @@
         )
 
 
-def map_rest_kernel(w_ref, t_ref, p_ref, o_ref, s_ref, m_ref):
+def map_rest_kernel(place_ref, w_ref, t_ref, p_ref, *refs):
+    o_refs, (s_ref, m_ref) = refs[:-2], refs[-2:]
     tokens = t_ref.shape[0]
-    owners, _, width = o_ref.shape
+    mine = o_refs[0].shape[1] // BLK
     rows = w_ref.shape[0] - MASS_ROWS
     spread_tokens(t_ref, s_ref)
     for t in range(0, tokens, 2):
@@ -67,24 +68,42 @@
             one = both[:, i * BLK : (i + 1) * BLK]
             mass = jnp.sum(jnp.sum(one[rows : rows + 8], axis=0, keepdims=True), axis=1, keepdims=True)
             m_ref[pl.ds(t + i, rows, stride=tokens), :] = one[:rows] * (1.0 / mass)
-
-    def owner(q, carry):
-        for b in range(width // BLK):
-            first = (q * (width // BLK) + b) * tokens
-            tile = m_ref[pl.ds(pl.multiple_of(first, tokens), tokens), :]
-            o_ref[q, :, b * BLK : (b + 1) * BLK] = tile.astype(jnp.bfloat16)
-        return carry
-
-    lax.fori_loop(0, owners, owner, 0)
-
-
-def grad_kernel(scale, target_ref, logits_ref, norm_ref, grad_ref, part_ref):
-    target = target_ref[...].astype(jnp.float32)
-    log_probs = logits_ref[...].astype(jnp.float32) - norm_ref[...]
-    grad_ref[...] = ((jnp.exp(log_probs) - target) * scale).astype(jnp.bfloat16)
-    positive = target > 0
-    terms = target * (jnp.log(jnp.where(positive, target, 1.0)) - log_probs)
-    part_ref[...] = jnp.sum(jnp.where(positive, terms, 0.0), axis=1, keepdims=True)
+    for offset, o_ref in enumerate(o_refs):
+        owner = place_ref[0] ^ offset
+        for b in range(mine):
+            first = pl.multiple_of((owner * mine + b) * tokens, tokens)
+            o_ref[:, b * BLK : (b + 1) * BLK] = m_ref[pl.ds(first, tokens), :].astype(jnp.bfloat16)
+
+
+def grad_kernel(scale, place_ref, logits_ref, norm_ref, *refs):
+    target_refs, (grad_ref, part_ref, sum_ref) = refs[:-3], refs[-3:]
+    tokens = target_refs[0].shape[0]
+    for offset, target_ref in enumerate(target_refs):
+        rows = pl.ds(pl.multiple_of((place_ref[0] ^ offset) * tokens, tokens), tokens)
+        target = target_ref[...].astype(jnp.float32)
+        log_probs = logits_ref[rows, :].astype(jnp.float32) - norm_ref[rows, :]
+        grad_ref[rows, :] = ((jnp.exp(log_probs) - target) * scale).astype(jnp.bfloat16)
+        positive = target > 0
+        terms = target * (jnp.log(jnp.where(positive, target, 1.0)) - log_probs)
+        total = jnp.sum(jnp.where(positive, terms, 0.0), axis=1, keepdims=True)
+        sum_ref[rows, :] = jnp.broadcast_to(total, (tokens, BLK))
+    for i in range(sum_ref.shape[0] // BLK):
+        part_ref[:, i * BLK : (i + 1) * BLK] = sum_ref[i * BLK : (i + 1) * BLK, :].T[:1]
+
+
+def hidden_kernel(place_ref, other_ref, *refs):
+    own_refs, (o_ref, s_ref) = refs[:-2], refs[-2:]
+    held = own_refs[0].shape[0]
+    for offset, own_ref in enumerate(own_refs):
+        first = (place_ref[0] ^ offset) * 2
+        own = pl.ds(pl.multiple_of((first + place_ref[1]) * held, held), held)
+        other = pl.ds(pl.multiple_of((first + 1 - place_ref[1]) * held, held), held)
+        s_ref[own, :] = own_ref[...].astype(jnp.float32)
+        s_ref[other, :] = other_ref[offset].astype(jnp.float32)
+    for i in range(s_ref.shape[0] // BLK):
+        for j in range(s_ref.shape[1] // BLK):
+            tile = s_ref[i * BLK : (i + 1) * BLK, j * BLK : (j + 1) * BLK].T
+            o_ref[j * BLK : (j + 1) * BLK, i * BLK : (i + 1) * BLK] = tile.astype(jnp.bfloat16)
 
 
 def weight_kernel(hidden_ref, grad_ref, o_ref):
@@ -101,10 +120,24 @@
     return pltpu.CompilerParams(vmem_limit_bytes=VMEM_LIMIT)
 
 
+def scalars():
+    return pl.BlockSpec(memory_space=pltpu.SMEM)
+
+
+def to_partner(x, offset, flip=False):
+    owners = lax.axis_size("sv")
+    pairs = [
+        (s * 2 + h, (s ^ offset) * 2 + (h ^ int(flip))) for s in range(owners) for h in range(2)
+    ]
+    return lax.ppermute(x, ("sv", "tv"), pairs)
+
+
 def body(teacher_probs, align_owner, align_local, align_weight, student_logits, hidden):
     owners = lax.axis_size("sv")
     halves = lax.axis_size("tv")
+    owner_index = lax.axis_index("sv")
     half_index = lax.axis_index("tv")
+    place = jnp.stack([owner_index, half_index]).astype(jnp.int32)
     tokens = teacher_probs.shape[0]
     columns = student_logits.shape[1]
     blocks = columns // BLK
@@ -114,31 +147,36 @@
     per_half = TB // halves
     group_tokens = owners * tokens
     half_tokens = student_logits.shape[0]
+    features = hidden.shape[1]
+    first = half_index == 0
 
     teacher_other = swap_halves(teacher_probs)
 
-    logit_halves = student_logits.reshape(half_tokens, halves, width)
-    keep = lax.dynamic_index_in_dim(logit_halves, half_index, 1, keepdims=False)
-    give = lax.dynamic_index_in_dim(logit_halves, 1 - half_index, 1, keepdims=False)
+    hidden_own = [hidden] + [to_partner(hidden, a) for a in range(1, owners)]
+    hidden_other = swap_halves(jnp.stack(hidden_own))
+    hidden_t = pl.pallas_call(
+        hidden_kernel,
+        out_shape=jax.ShapeDtypeStruct((features, group_tokens), jnp.bfloat16),
+        in_specs=[scalars()] + [whole()] * (owners + 1),
+        out_specs=whole(),
+        scratch_shapes=[pltpu.VMEM((group_tokens, features), jnp.float32)],
+        compiler_params=params(),
+        cost_estimate=pl.CostEstimate(flops=0, bytes_accessed=4 * features * group_tokens, transcendentals=0),
+        name="hidden_t",
+    )(place, hidden_other, *hidden_own)
+
+    keep = lax.dynamic_slice_in_dim(student_logits, half_index * width, width, 1)
+    give = lax.dynamic_slice_in_dim(student_logits, (1 - half_index) * width, width, 1)
     got = swap_halves(give)
-    first = half_index == 0
     logits = jnp.concatenate([jnp.where(first, keep, got), jnp.where(first, got, keep)], axis=0)
-
-    hidden_mine = lax.all_to_all(
-        jnp.broadcast_to(hidden[None], (owners,) + hidden.shape), "sv", 0, 0, tiled=True
-    )
-    hidden_other = swap_halves(hidden_mine)
-    hidden_pair = jnp.stack(
-        [jnp.where(first, hidden_mine, hidden_other), jnp.where(first, hidden_other, hidden_mine)], axis=1
-    )
-    hidden_t = hidden_pair.reshape(group_tokens, hidden.shape[1]).T
 
     wide = student_logits.astype(jnp.float32)
     peak = jnp.max(wide, axis=1)
     sums = jnp.sum(jnp.exp(wide - peak[:, None]), axis=1)
-    stats = jnp.broadcast_to(jnp.stack([peak, sums])[None], (owners * halves, 2, half_tokens))
-    stats = lax.all_to_all(stats, ("sv", "tv"), 0, 0, tiled=True)
-    stats = stats.reshape(owners, halves, 2, half_tokens)
+    stats = jnp.stack([peak, sums])
+    stats_other = swap_halves(stats)
+    stats = jnp.stack([jnp.where(first, stats, stats_other), jnp.where(first, stats_other, stats)])
+    stats = jnp.stack([stats] + [to_partner(stats, a) for a in range(1, owners)])
     peaks, sums = stats[:, :, 0], stats[:, :, 1]
     top = jnp.max(peaks, axis=0)
     log_norm = top + jnp.log(jnp.sum(sums * jnp.exp(peaks - top[None]), axis=0))
@@ -164,25 +202,26 @@
     )(w_own, teacher_probs)
     outgoing = pl.pallas_call(
         map_rest_kernel,
-        out_shape=jax.ShapeDtypeStruct((owners, tokens, width), jnp.bfloat16),
-        in_specs=[whole()] * 3,
-        out_specs=whole(),
+        out_shape=[jax.ShapeDtypeStruct((tokens, width), jnp.bfloat16)] * owners,
+        in_specs=[scalars()] + [whole()] * 3,
+        out_specs=[whole()] * owners,
         scratch_shapes=[spread, pltpu.VMEM((rows * tokens, BLK), jnp.float32)],
         compiler_params=params(),
         cost_estimate=pl.CostEstimate(flops=flops, bytes_accessed=4 << 20, transcendentals=0),
         name="map_rest",
-    )(w_rest, teacher_other, part)
-    target = lax.all_to_all(outgoing, "sv", 0, 0, tiled=True).reshape(group_tokens, width)
+    )(place, w_rest, teacher_other, part)
+    targets = [outgoing[0]] + [to_partner(outgoing[a], a) for a in range(1, owners)]
 
     scale = float(columns * owners)
     grad, terms = pl.pallas_call(
         lambda *refs: grad_kernel(scale, *refs),
         out_shape=(
             jax.ShapeDtypeStruct((group_tokens, width), jnp.bfloat16),
-            jax.ShapeDtypeStruct((group_tokens, 1), jnp.float32),
-        ),
-        in_specs=[whole()] * 3,
+            jax.ShapeDtypeStruct((1, group_tokens), jnp.float32),
+        ),
+        in_specs=[scalars()] + [whole()] * (owners + 2),
         out_specs=(whole(), whole()),
+        scratch_shapes=[pltpu.VMEM((group_tokens, BLK), jnp.float32)],
         compiler_params=params(),
         cost_estimate=pl.CostEstimate(
             flops=10 * group_tokens * width,
@@ -190,29 +229,29 @@
             transcendentals=2 * group_tokens * width,
         ),
         name="logit_grad",
-    )(target, logits, log_norm)
-
-    grad_halves = grad.reshape(halves, half_tokens, width)
-    keep = lax.dynamic_index_in_dim(grad_halves, half_index, 0, keepdims=False)
-    give = lax.dynamic_index_in_dim(grad_halves, 1 - half_index, 0, keepdims=False)
+    )(place, logits, log_norm, *targets)
+
+    keep = lax.dynamic_slice_in_dim(grad, half_index * half_tokens, half_tokens, 0)
+    give = lax.dynamic_slice_in_dim(grad, (1 - half_index) * half_tokens, half_tokens, 0)
     got = swap_halves(give)
     logit_grad = jnp.concatenate([jnp.where(first, keep, got), jnp.where(first, got, keep)], axis=1)
 
-    terms = jnp.broadcast_to(terms.reshape(1, halves, half_tokens), (owners, halves, half_tokens))
-    terms = lax.all_to_all(terms.reshape(owners * halves, half_tokens), ("sv", "tv"), 0, 0, tiled=True)
-    divergence = jnp.sum(terms, axis=0)
-
-    features = hidden.shape[1]
-    tile = features // 8
+    terms_keep = lax.dynamic_slice_in_dim(terms, half_index * half_tokens, half_tokens, 1)
+    terms_give = lax.dynamic_slice_in_dim(terms, (1 - half_index) * half_tokens, half_tokens, 1)
+    pieces = [terms_keep] + [to_partner(terms_keep, a) for a in range(1, owners)]
+    pieces += [to_partner(terms_give, a, True) for a in range(owners)]
+    divergence = sum(pieces[1:], pieces[0]).reshape(half_tokens)
+
+    tile = 256
     weight_grad = pl.pallas_call(
         weight_kernel,
         out_shape=jax.ShapeDtypeStruct((features, width), jnp.bfloat16),
-        grid=(features // tile,),
+        grid=(width // tile,),
         in_specs=[
-            pl.BlockSpec((tile, group_tokens), lambda i: (i, 0)),
-            pl.BlockSpec((group_tokens, width), lambda i: (0, 0)),
+            pl.BlockSpec((features, group_tokens), lambda i: (0, 0)),
+            pl.BlockSpec((group_tokens, tile), lambda i: (0, i)),
         ],
-        out_specs=pl.BlockSpec((tile, width), lambda i: (i, 0)),
+        out_specs=pl.BlockSpec((features, tile), lambda i: (0, i)),
         compiler_params=params(),
         cost_estimate=pl.CostEstimate(
             flops=2 * features * group_tokens * width,

time: 69.8 us -> 112 us (1.60)
  starting transfers between devices: 18.7 us -> 69.4 us
  local copies, waits for them, and re-layouts: 6.79 us -> 2.1 us
  waiting for transfers between devices: 25.5 us -> 21.2 us
    ppermute x0 -> x36, starting transfers between devices: none -> 68.7 us  [to_partner(): return lax.ppermute(x, ('sv', 'tv'), pairs)]
    all_to_all x4 -> x0, waiting for transfers between devices: 25.5 us -> none  [the longest x1 13.2 us: body(): lax.all_to_all(outgoing, 'sv', 0, 0, tiled=True)]
    ppermute x0 -> x36, waiting for transfers between devices: none -> 21.1 us  [to_partner(): return lax.ppermute(x, ('sv', 'tv'), pairs)]
    all_to_all x4 -> x0, starting transfers between devices: 18.1 us -> none  [the longest x1 7.39 us: body(): stats = lax.all_to_all(stats, ('sv', 'tv'), 0, 0, tiled=True)]
    reshape x2 -> x0, local copies, waits for them, and re-layouts: 1.7 us -> none  [the longest x1 1.43 us: body(): logit_halves = student_logits.reshape(half_tokens, halves, width)]
    broadcast_in_dim x4 -> x0, local copies, waits for them, and re-layouts: 1.42 us -> none  [the longest x1 0.71 us: body(): jnp.broadcast_to(hidden[None], (owners,) + hidden.shape)]
    pallas_call x1 -> x2, Pallas kernels: 4.2 us -> 4.19 us  [the longest x1 3.37 us: body(): pl.pallas_call(map_rest_kernel, out_shape=[jax.ShapeDtypeStruct((tokens,...]
  transfers between devices with their start and end apart: 8 -> 41, of which waited for: 4 -> 12; matrix products, arithmetic and copies ran while one was open for 11% -> 6% of each run, Pallas kernels for 17% -> 10%
where the time goes in v2:
time: 112 us
  starting transfers between devices  69.4 us (62%)
  waiting for transfers between devices  21.2 us (19%)
  Pallas kernels  12.6 us (11%)
  other arithmetic  5.33 us (5%)
  local copies, waits for them, and re-layouts  2.1 us (2%)
    ppermute x36, starting transfers between devices, to_partner(): return lax.ppermute(x, ('sv', 'tv'), pairs)  68.7 us
    ppermute x36, waiting for transfers between devices, to_partner(): return lax.ppermute(x, ('sv', 'tv'), pairs)  21.1 us
    pallas_call x1, Pallas kernels, body(): pl.pallas_call(weight_kernel, out_shape=jax.ShapeDtypeStruct((features, w...  5.83 us
    pallas_call x1, Pallas kernels, body(): pl.pallas_call(map_rest_kernel, out_shape=[jax.ShapeDtypeStruct((tokens,...  3.37 us
  transfers between devices with their start and end apart: 41, of which 12 were waited for; matrix products, arithmetic and copies ran while one was open for 6% of the time, Pallas kernels for 10%

profile of v2, /device:TPU:0, one launch (start us, length us, event | category | flops | bytes accessed | tf_op | source)
XLA Modules:
  0.0 111.6 jit_solution(12132356872862794525)
XLA Ops:
  0.6 3.0 %collective-permute-start.33 = (bf16[8,1920]{1,0:T(8,128)(2,1)}, bf16[8,1920]{1,0:T(8,128)(2,1)S(1)}, u32[]{:S(2)}, u32[]{:S(2)}) collective-permute-start(bf16[8,1920]{1,0:T(8,128)(2,1)} %refs_0_.1), channel_id=1, source_target_pairs={{0,2},{1,3},{2,0},{3,1},{4,6},{5,7},{6,4},{7,5},{8,10},{9,11},{10,... | collective-permute-start | bytes 92168 | tf_op jit(solution)/shard_map/ppermute | solution.py:132
  12.7 2.0 %collective-permute-start.2 = (f32[2,2,64]{2,1,0:T(2,128)S(1)}, f32[2,2,64]{2,1,0:T(2,128)S(1)}, u32[]{:S(2)}, u32[]{:S(2)}) collective-permute-start(f32[2,2,64]{2,1,0:T(2,128)S(1)} %pad_maximum_fusion.2), channel_id=1, source_target_pairs={{0,2},{1,3},{2,0},{3,1},{4,6},{5,7},{6,4},{7,5},{8,10},{9,11},{10,... | collective-permute-start | bytes 3080 | tf_op jit(solution)/shard_map/ppermute | solution.py:132
  16.4 2.0 %collective-permute-start.3 = (f32[2,2,64]{2,1,0:T(2,128)S(1)}, f32[2,2,64]{2,1,0:T(2,128)S(1)}, u32[]{:S(2)}, u32[]{:S(2)}) collective-permute-start(f32[2,2,64]{2,1,0:T(2,128)S(1)} %pad_maximum_fusion.2), channel_id=1, source_target_pairs={{0,4},{1,5},{2,6},{3,7},{4,0},{5,1},{6,2},{7,3},{8,12},{9,13},{10,... | collective-permute-start | bytes 3080 | tf_op jit(solution)/shard_map/ppermute | solution.py:132
  19.9 2.9 %collective-permute-start.4 = (f32[2,2,64]{2,1,0:T(2,128)S(1)}, f32[2,2,64]{2,1,0:T(2,128)S(1)}, u32[]{:S(2)}, u32[]{:S(2)}) collective-permute-start(f32[2,2,64]{2,1,0:T(2,128)S(1)} %pad_maximum_fusion.2), channel_id=1, source_target_pairs={{0,6},{1,7},{2,4},{3,5},{4,2},{5,3},{6,0},{7,1},{8,14},{9,15},{10,... | collective-permute-start | bytes 3080 | tf_op jit(solution)/shard_map/ppermute | solution.py:132
  24.4 3.0 %collective-permute-start.5 = (f32[2,2,64]{2,1,0:T(2,128)S(1)}, f32[2,2,64]{2,1,0:T(2,128)S(1)}, u32[]{:S(2)}, u32[]{:S(2)}) collective-permute-start(f32[2,2,64]{2,1,0:T(2,128)S(1)} %pad_maximum_fusion.2), channel_id=1, source_target_pairs={{0,8},{1,9},{2,10},{3,11},{4,12},{5,13},{6,14},{7,15},{8,0},{9,1},... | collective-permute-start | bytes 3080 | tf_op jit(solution)/shard_map/ppermute | solution.py:132
  29.0 3.9 %collective-permute-start.6 = (f32[2,2,64]{2,1,0:T(2,128)S(1)}, f32[2,2,64]{2,1,0:T(2,128)S(1)}, u32[]{:S(2)}, u32[]{:S(2)}) collective-permute-start(f32[2,2,64]{2,1,0:T(2,128)S(1)} %pad_maximum_fusion.2), channel_id=1, source_target_pairs={{0,10},{1,11},{2,8},{3,9},{4,14},{5,15},{6,12},{7,13},{8,2},{9,3},... | collective-permute-start | bytes 3080 | tf_op jit(solution)/shard_map/ppermute | solution.py:132
  34.4 3.9 %collective-permute-start.7 = (f32[2,2,64]{2,1,0:T(2,128)S(1)}, f32[2,2,64]{2,1,0:T(2,128)S(1)}, u32[]{:S(2)}, u32[]{:S(2)}) collective-permute-start(f32[2,2,64]{2,1,0:T(2,128)S(1)} %pad_maximum_fusion.2), channel_id=1, source_target_pairs={{0,12},{1,13},{2,14},{3,15},{4,8},{5,9},{6,10},{7,11},{8,4},{9,5},... | collective-permute-start | bytes 3080 | tf_op jit(solution)/shard_map/ppermute | solution.py:132
  39.9 4.8 %collective-permute-start.8 = (f32[2,2,64]{2,1,0:T(2,128)S(1)}, f32[2,2,64]{2,1,0:T(2,128)S(1)}, u32[]{:S(2)}, u32[]{:S(2)}) collective-permute-start(f32[2,2,64]{2,1,0:T(2,128)S(1)} %pad_maximum_fusion.2), channel_id=1, source_target_pairs={{0,14},{1,15},{2,12},{3,13},{4,10},{5,11},{6,8},{7,9},{8,6},{9,7},... | collective-permute-start | bytes 3080 | tf_op jit(solution)/shard_map/ppermute | solution.py:132
  46.4 4.2 %collective-permute-start.37 = (bf16[8,1920]{1,0:T(8,128)(2,1)S(1)}, bf16[8,1920]{1,0:T(8,128)(2,1)S(1)}, u32[]{:S(2)}, u32[]{:S(2)}) collective-permute-start(bf16[8,1920]{1,0:T(8,128)(2,1)S(1)} %copy-done.1), channel_id=1, source_target_pairs={{0,10},{1,11},{2,8},{3,9},{4,14},{5,15},{6,12},{7,13},{8,2},{9,3},... | collective-permute-start | bytes 92168 | tf_op jit(solution)/shard_map/ppermute | solution.py:132
  50.6 3.6 %collective-permute-start.38 = (bf16[8,1920]{1,0:T(8,128)(2,1)S(1)}, bf16[8,1920]{1,0:T(8,128)(2,1)S(1)}, u32[]{:S(2)}, u32[]{:S(2)}) collective-permute-start(bf16[8,1920]{1,0:T(8,128)(2,1)S(1)} %copy-done.1), channel_id=1, source_target_pairs={{0,12},{1,13},{2,14},{3,15},{4,8},{5,9},{6,10},{7,11},{8,4},{9,5},... | collective-permute-start | bytes 92168 | tf_op jit(solution)/shard_map/ppermute | solution.py:132
  54.4 1.9 %collective-permute-done.38.refs_6_ = bf16[8,1920]{1,0:T(8,128)(2,1)S(1)} collective-permute-done((bf16[8,1920]{1,0:T(8,128)(2,1)S(1)}, bf16[8,1920]{1,0:T(8,128)(2,1)S(1)}, u32[]{:S(2)}, u32[]{:S(2)}) %collective-permute-start.38) | collective-permute-done | bytes 30752 | tf_op jit(solution)/shard_map/ppermute | solution.py:132
  56.4 4.5 %collective-permute-done.39.refs_7_ = bf16[8,1920]{1,0:T(8,128)(2,1)S(1)} collective-permute-done((bf16[8,1920]{1,0:T(8,128)(2,1)S(1)}, bf16[8,1920]{1,0:T(8,128)(2,1)S(1)}, u32[]{:S(2)}, u32[]{:S(2)}) %collective-permute-start.39) | collective-permute-done | bytes 30752 | tf_op jit(solution)/shard_map/ppermute | solution.py:132
  60.9 3.4 %map_rest.1 = (bf16[16,2048]{1,0:T(8,128)(2,1)S(1)}, bf16[16,2048]{1,0:T(8,128)(2,1)S(1)}, bf16[16,2048]{1,0:T(8,128)(2,1)S(1)}, bf16[16,2048]{1,0:T(8,128)(2,1)...) custom-call(s32[2]{0:T(128)S(1)} %pad_add_fusion.place_ref.refs_0_, ...), custom_call_target="tpu_custom_call" | custom-call | flops 188743680 | bytes 4194304 | tf_op jit(solution)/shard_map/map_rest/pallas_call | solution.py:203
  65.0 3.0 %collective-permute-start.12 = (bf16[16,2048]{1,0:T(8,128)(2,1)S(1)}, bf16[16,2048]{1,0:T(8,128)(2,1)S(1)}, u32[]{:S(2)}, u32[]{:S(2)}) collective-permute-start(bf16[16,2048]{1,0:T(8,128)(2,1)S(1)} %get-tuple-element.16), channel_id=1, source_target_pairs={{0,6},{1,7},{2,4},{3,5},{4,2},{5,3},{6,0},{7,1},{8,14},{9,15},{10,... | collective-permute-start | bytes 196616 | tf_op jit(solution)/shard_map/ppermute | solution.py:132
  68.0 2.9 %collective-permute-start.14 = (bf16[16,2048]{1,0:T(8,128)(2,1)S(1)}, bf16[16,2048]{1,0:T(8,128)(2,1)S(1)}, u32[]{:S(2)}, u32[]{:S(2)}) collective-permute-start(bf16[16,2048]{1,0:T(8,128)(2,1)S(1)} %get-tuple-element.18), channel_id=1, source_target_pairs={{0,10},{1,11},{2,8},{3,9},{4,14},{5,15},{6,12},{7,13},{8,2},{9,3},... | collective-permute-start | bytes 196616 | tf_op jit(solution)/shard_map/ppermute | solution.py:132
  71.2 4.5 %collective-permute-start.16 = (bf16[16,2048]{1,0:T(8,128)(2,1)S(1)}, bf16[16,2048]{1,0:T(8,128)(2,1)S(1)}, u32[]{:S(2)}, u32[]{:S(2)}) collective-permute-start(bf16[16,2048]{1,0:T(8,128)(2,1)S(1)} %get-tuple-element.20), channel_id=1, source_target_pairs={{0,14},{1,15},{2,12},{3,13},{4,10},{5,11},{6,8},{7,9},{8,6},{9,7},... | collective-permute-start | bytes 196616 | tf_op jit(solution)/shard_map/ppermute | solution.py:132
  77.3 2.4 %collective-permute-done.14.refs_8_ = bf16[16,2048]{1,0:T(8,128)(2,1)S(1)} collective-permute-done((bf16[16,2048]{1,0:T(8,128)(2,1)S(1)}, bf16[16,2048]{1,0:T(8,128)(2,1)S(1)}, u32[]{:S(2)}, u32[]{:S(2)}) %collective-permute-start.14) | collective-permute-done | bytes 65568 | tf_op jit(solution)/shard_map/ppermute | solution.py:132
  82.2 3.3 %collective-permute-start.18 = (f32[1,64]{1,0:T(1,128)S(1)}, f32[1,64]{1,0:T(1,128)S(1)}, u32[]{:S(2)}, u32[]{:S(2)}) collective-permute-start(f32[1,64]{1,0:T(1,128)S(1)} %get-tuple-element.45), channel_id=1, source_target_pairs={{0,4},{1,5},{2,6},{3,7},{4,0},{5,1},{6,2},{7,3},{8,12},{9,13},{10,... | collective-permute-start | bytes 776 | tf_op jit(solution)/shard_map/ppermute | solution.py:132
  85.6 1.9 %collective-permute-start.20 = (f32[1,64]{1,0:T(1,128)S(1)}, f32[1,64]{1,0:T(1,128)S(1)}, u32[]{:S(2)}, u32[]{:S(2)}) collective-permute-start(f32[1,64]{1,0:T(1,128)S(1)} %get-tuple-element.45), channel_id=1, source_target_pairs={{0,8},{1,9},{2,10},{3,11},{4,12},{5,13},{6,14},{7,15},{8,0},{9,1},... | collective-permute-start | bytes 776 | tf_op jit(solution)/shard_map/ppermute | solution.py:132
  87.5 1.8 %collective-permute-start.21 = (f32[1,64]{1,0:T(1,128)S(1)}, f32[1,64]{1,0:T(1,128)S(1)}, u32[]{:S(2)}, u32[]{:S(2)}) collective-permute-start(f32[1,64]{1,0:T(1,128)S(1)} %get-tuple-element.45), channel_id=1, source_target_pairs={{0,10},{1,11},{2,8},{3,9},{4,14},{5,15},{6,12},{7,13},{8,2},{9,3},... | collective-permute-start | bytes 776 | tf_op jit(solution)/shard_map/ppermute | solution.py:132
  90.9 2.4 %collective-permute-start.23 = (f32[1,64]{1,0:T(1,128)S(1)}, f32[1,64]{1,0:T(1,128)S(1)}, u32[]{:S(2)}, u32[]{:S(2)}) collective-permute-start(f32[1,64]{1,0:T(1,128)S(1)} %get-tuple-element.45), channel_id=1, source_target_pairs={{0,14},{1,15},{2,12},{3,13},{4,10},{5,11},{6,8},{7,9},{8,6},{9,7},... | collective-permute-start | bytes 776 | tf_op jit(solution)/shard_map/ppermute | solution.py:132
  97.1 3.0 %collective-permute-start.29 = (f32[1,64]{1,0:T(1,128)S(1)}, f32[1,64]{1,0:T(1,128)S(1)}, u32[]{:S(2)}, u32[]{:S(2)}) collective-permute-start(f32[1,64]{1,0:T(1,128)S(1)} %get-tuple-element.46), channel_id=1, source_target_pairs={{0,11},{1,10},{2,9},{3,8},{4,15},{5,14},{6,13},{7,12},{8,3},{9,2},... | collective-permute-start | bytes 776 | tf_op jit(solution)/shard_map/ppermute | solution.py:132
  101.3 2.9 %collective-permute-start.31 = (f32[1,64]{1,0:T(1,128)S(1)}, f32[1,64]{1,0:T(1,128)S(1)}, u32[]{:S(2)}, u32[]{:S(2)}) collective-permute-start(f32[1,64]{1,0:T(1,128)S(1)} %get-tuple-element.46), channel_id=1, source_target_pairs={{0,15},{1,14},{2,13},{3,12},{4,11},{5,10},{6,9},{7,8},{8,7},{9,6},... | collective-permute-start | bytes 776 | tf_op jit(solution)/shard_map/ppermute | solution.py:132
  104.2 5.8 %weight_grad.1 = bf16[1920,2048]{1,0:T(8,128)(2,1)} custom-call(bf16[1920,128]{1,0:T(8,128)(2,1)S(1)} %hidden_t.1.hidden_ref, bf16[128,2048]{1,0:T(8,128)(2,1)S(1)} %get-tuple-element.22.grad_ref), custom_call_target="tpu_custom_call" | custom-call | flops 1006632960 | bytes 8880128 | tf_op jit(solution)/shard_map/weight_grad/pallas_call | solution.py:246
  (112 shorter events, 33.7 us)
Async XLA Ops:
  0.6 45.8 %collective-permute-start.33 = (bf16[8,1920]{1,0:T(8,128)(2,1)}, bf16[8,1920]{1,0:T(8,128)(2,1)S(1)}, u32[]{:S(2)}, u32[]{:S(2)}) collective-permute-start(bf16[8,1920]{1,0:T(8,128)(2,1)} %refs_0_.1), channel_id=1, source_target_pairs={{0,2},{1,3},{2,0},{3,1},{4,6},{5,7},{6,4},{7,5},{8,10},{9,11},{10,... | collective-permute-start | bytes 92168 | tf_op jit(solution)/shard_map/ppermute | solution.py:132
  3.7 47.0 %collective-permute-start.34 = (bf16[8,1920]{1,0:T(8,128)(2,1)}, bf16[8,1920]{1,0:T(8,128)(2,1)S(1)}, u32[]{:S(2)}, u32[]{:S(2)}) collective-permute-start(bf16[8,1920]{1,0:T(8,128)(2,1)} %refs_0_.1), channel_id=1, source_target_pairs={{0,4},{1,5},{2,6},{3,7},{4,0},{5,1},{6,2},{7,3},{8,12},{9,13},{10,... | collective-permute-start | bytes 92168 | tf_op jit(solution)/shard_map/ppermute | solution.py:132
  5.2 49.0 %collective-permute-start.35 = (bf16[8,1920]{1,0:T(8,128)(2,1)}, bf16[8,1920]{1,0:T(8,128)(2,1)S(1)}, u32[]{:S(2)}, u32[]{:S(2)}) collective-permute-start(bf16[8,1920]{1,0:T(8,128)(2,1)} %refs_0_.1), channel_id=1, source_target_pairs={{0,6},{1,7},{2,4},{3,5},{4,2},{5,3},{6,0},{7,1},{8,14},{9,15},{10,... | collective-permute-start | bytes 92168 | tf_op jit(solution)/shard_map/ppermute | solution.py:132
  5.3 55.6 %collective-permute-start.9 = (bf16[16,40960]{1,0:T(8,128)(2,1)}, bf16[16,40960]{1,0:T(8,128)(2,1)}, u32[]{:S(2)}, u32[]{:S(2)}) collective-permute-start(bf16[16,40960]{1,0:T(8,128)(2,1)} %t_ref.1), channel_id=1, source_target_pairs={{0,1},{1,0},{2,3},{3,2},{4,5},{5,4},{6,7},{7,6},{8,9},{9,8},{10,11... | collective-permute-start | bytes 3932168 | tf_op jit(solution)/shard_map/ppermute | solution.py:15
  46.2 8.1 %collective-permute-start.36 = (bf16[8,1920]{1,0:T(8,128)(2,1)S(1)}, bf16[8,1920]{1,0:T(8,128)(2,1)S(1)}, u32[]{:S(2)}, u32[]{:S(2)}) collective-permute-start(bf16[8,1920]{1,0:T(8,128)(2,1)S(1)} %copy-done.1), channel_id=1, source_target_pairs={{0,8},{1,9},{2,10},{3,11},{4,12},{5,13},{6,14},{7,15},{8,0},{9,1},... | collective-permute-start | bytes 92168 | tf_op jit(solution)/shard_map/ppermute | solution.py:132
  46.4 8.0 %collective-permute-start.37 = (bf16[8,1920]{1,0:T(8,128)(2,1)S(1)}, bf16[8,1920]{1,0:T(8,128)(2,1)S(1)}, u32[]{:S(2)}, u32[]{:S(2)}) collective-permute-start(bf16[8,1920]{1,0:T(8,128)(2,1)S(1)} %copy-done.1), channel_id=1, source_target_pairs={{0,10},{1,11},{2,8},{3,9},{4,14},{5,15},{6,12},{7,13},{8,2},{9,3},... | collective-permute-start | bytes 92168 | tf_op jit(solution)/shard_map/ppermute | solution.py:132
  54.3 10.5 %collective-permute-start = (bf16[64,2048]{1,0:T(8,128)(2,1)S(1)}, bf16[64,2048]{1,0:T(8,128)(2,1)S(1)}, u32[]{:S(2)}, u32[]{:S(2)}) collective-permute-start(bf16[64,2048]{1,0:T(8,128)(2,1)S(1)} %constant_dynamic-slice_fusion.5), channel_id=1, source_target_pairs={{0,1},{1,0},{2,3},{3,2},{4,5},{5,4},{6,7},{7,6},{8,9},{9,8},{10,11... | collective-permute-start | bytes 786440 | tf_op jit(solution)/shard_map/ppermute | solution.py:15
  60.9 7.1 %collective-permute-start.40 = (bf16[8,8,1920]{2,1,0:T(8,128)(2,1)S(1)}, bf16[8,8,1920]{2,1,0:T(8,128)(2,1)S(1)}, u32[]{:S(2)}, u32[]{:S(2)}) collective-permute-start(bf16[8,8,1920]{2,1,0:T(8,128)(2,1)S(1)} %constant_dynamic-update-slice_fusion.8), channel_id=1, source_target_pairs={{0,1},{1,0},{2,3},{3,2},{4,5},{5,4},{6,7},{7,6},{8,9},{9,8},{10,11... | collective-permute-start | bytes 737288 | tf_op jit(solution)/shard_map/ppermute | solution.py:15
  65.0 11.6 %collective-permute-start.12 = (bf16[16,2048]{1,0:T(8,128)(2,1)S(1)}, bf16[16,2048]{1,0:T(8,128)(2,1)S(1)}, u32[]{:S(2)}, u32[]{:S(2)}) collective-permute-start(bf16[16,2048]{1,0:T(8,128)(2,1)S(1)} %get-tuple-element.16), channel_id=1, source_target_pairs={{0,6},{1,7},{2,4},{3,5},{4,2},{5,3},{6,0},{7,1},{8,14},{9,15},{10,... | collective-permute-start | bytes 196616 | tf_op jit(solution)/shard_map/ppermute | solution.py:132
  68.0 9.3 %collective-permute-start.13 = (bf16[16,2048]{1,0:T(8,128)(2,1)S(1)}, bf16[16,2048]{1,0:T(8,128)(2,1)S(1)}, u32[]{:S(2)}, u32[]{:S(2)}) collective-permute-start(bf16[16,2048]{1,0:T(8,128)(2,1)S(1)} %get-tuple-element.17), channel_id=1, source_target_pairs={{0,8},{1,9},{2,10},{3,11},{4,12},{5,13},{6,14},{7,15},{8,0},{9,1},... | collective-permute-start | bytes 196616 | tf_op jit(solution)/shard_map/ppermute | solution.py:132
  68.0 11.7 %collective-permute-start.14 = (bf16[16,2048]{1,0:T(8,128)(2,1)S(1)}, bf16[16,2048]{1,0:T(8,128)(2,1)S(1)}, u32[]{:S(2)}, u32[]{:S(2)}) collective-permute-start(bf16[16,2048]{1,0:T(8,128)(2,1)S(1)} %get-tuple-element.18), channel_id=1, source_target_pairs={{0,10},{1,11},{2,8},{3,9},{4,14},{5,15},{6,12},{7,13},{8,2},{9,3},... | collective-permute-start | bytes 196616 | tf_op jit(solution)/shard_map/ppermute | solution.py:132
  70.9 8.8 %collective-permute-start.15 = (bf16[16,2048]{1,0:T(8,128)(2,1)S(1)}, bf16[16,2048]{1,0:T(8,128)(2,1)S(1)}, u32[]{:S(2)}, u32[]{:S(2)}) collective-permute-start(bf16[16,2048]{1,0:T(8,128)(2,1)S(1)} %get-tuple-element.19), channel_id=1, source_target_pairs={{0,12},{1,13},{2,14},{3,15},{4,8},{5,9},{6,10},{7,11},{8,4},{9,5},... | collective-permute-start | bytes 196616 | tf_op jit(solution)/shard_map/ppermute | solution.py:132
  71.2 8.5 %collective-permute-start.16 = (bf16[16,2048]{1,0:T(8,128)(2,1)S(1)}, bf16[16,2048]{1,0:T(8,128)(2,1)S(1)}, u32[]{:S(2)}, u32[]{:S(2)}) collective-permute-start(bf16[16,2048]{1,0:T(8,128)(2,1)S(1)} %get-tuple-element.20), channel_id=1, source_target_pairs={{0,14},{1,15},{2,12},{3,13},{4,10},{5,11},{6,8},{7,9},{8,6},{9,7},... | collective-permute-start | bytes 196616 | tf_op jit(solution)/shard_map/ppermute | solution.py:132
  81.0 8.3 %collective-permute-start.17 = (f32[1,64]{1,0:T(1,128)S(1)}, f32[1,64]{1,0:T(1,128)S(1)}, u32[]{:S(2)}, u32[]{:S(2)}) collective-permute-start(f32[1,64]{1,0:T(1,128)S(1)} %get-tuple-element.45), channel_id=1, source_target_pairs={{0,2},{1,3},{2,0},{3,1},{4,6},{5,7},{6,4},{7,5},{8,10},{9,11},{10,... | collective-permute-start | bytes 776 | tf_op jit(solution)/shard_map/ppermute | solution.py:132
  82.2 8.7 %collective-permute-start.18 = (f32[1,64]{1,0:T(1,128)S(1)}, f32[1,64]{1,0:T(1,128)S(1)}, u32[]{:S(2)}, u32[]{:S(2)}) collective-permute-start(f32[1,64]{1,0:T(1,128)S(1)} %get-tuple-element.45), channel_id=1, source_target_pairs={{0,4},{1,5},{2,6},{3,7},{4,0},{5,1},{6,2},{7,3},{8,12},{9,13},{10,... | collective-permute-start | bytes 776 | tf_op jit(solution)/shard_map/ppermute | solution.py:132
  85.5 7.8 %collective-permute-start.19 = (f32[1,64]{1,0:T(1,128)S(1)}, f32[1,64]{1,0:T(1,128)S(1)}, u32[]{:S(2)}, u32[]{:S(2)}) collective-permute-start(f32[1,64]{1,0:T(1,128)S(1)} %get-tuple-element.45), channel_id=1, source_target_pairs={{0,6},{1,7},{2,4},{3,5},{4,2},{5,3},{6,0},{7,1},{8,14},{9,15},{10,... | collective-permute-start | bytes 776 | tf_op jit(solution)/shard_map/ppermute | solution.py:132
  85.6 7.8 %collective-permute-start.20 = (f32[1,64]{1,0:T(1,128)S(1)}, f32[1,64]{1,0:T(1,128)S(1)}, u32[]{:S(2)}, u32[]{:S(2)}) collective-permute-start(f32[1,64]{1,0:T(1,128)S(1)} %get-tuple-element.45), channel_id=1, source_target_pairs={{0,8},{1,9},{2,10},{3,11},{4,12},{5,13},{6,14},{7,15},{8,0},{9,1},... | collective-permute-start | bytes 776 | tf_op jit(solution)/shard_map/ppermute | solution.py:132
  87.5 7.4 %collective-permute-start.21 = (f32[1,64]{1,0:T(1,128)S(1)}, f32[1,64]{1,0:T(1,128)S(1)}, u32[]{:S(2)}, u32[]{:S(2)}) collective-permute-start(f32[1,64]{1,0:T(1,128)S(1)} %get-tuple-element.45), channel_id=1, source_target_pairs={{0,10},{1,11},{2,8},{3,9},{4,14},{5,15},{6,12},{7,13},{8,2},{9,3},... | collective-permute-start | bytes 776 | tf_op jit(solution)/shard_map/ppermute | solution.py:132
  93.3 6.8 %collective-permute-start.25 = (f32[1,64]{1,0:T(1,128)S(1)}, f32[1,64]{1,0:T(1,128)S(1)}, u32[]{:S(2)}, u32[]{:S(2)}) collective-permute-start(f32[1,64]{1,0:T(1,128)S(1)} %get-tuple-element.46), channel_id=1, source_target_pairs={{0,3},{1,2},{2,1},{3,0},{4,7},{5,6},{6,5},{7,4},{8,11},{9,10},{10,... | collective-permute-start | bytes 776 | tf_op jit(solution)/shard_map/ppermute | solution.py:132
  94.8 9.4 %collective-permute-start.27 = (f32[1,64]{1,0:T(1,128)S(1)}, f32[1,64]{1,0:T(1,128)S(1)}, u32[]{:S(2)}, u32[]{:S(2)}) collective-permute-start(f32[1,64]{1,0:T(1,128)S(1)} %get-tuple-element.46), channel_id=1, source_target_pairs={{0,7},{1,6},{2,5},{3,4},{4,3},{5,2},{6,1},{7,0},{8,15},{9,14},{10,... | collective-permute-start | bytes 776 | tf_op jit(solution)/shard_map/ppermute | solution.py:132
  97.1 12.9 %collective-permute-start.28 = (f32[1,64]{1,0:T(1,128)S(1)}, f32[1,64]{1,0:T(1,128)S(1)}, u32[]{:S(2)}, u32[]{:S(2)}) collective-permute-start(f32[1,64]{1,0:T(1,128)S(1)} %get-tuple-element.46), channel_id=1, source_target_pairs={{0,9},{1,8},{2,11},{3,10},{4,13},{5,12},{6,15},{7,14},{8,1},{9,0},... | collective-permute-start | bytes 776 | tf_op jit(solution)/shard_map/ppermute | solution.py:132
  97.1 12.9 %collective-permute-start.29 = (f32[1,64]{1,0:T(1,128)S(1)}, f32[1,64]{1,0:T(1,128)S(1)}, u32[]{:S(2)}, u32[]{:S(2)}) collective-permute-start(f32[1,64]{1,0:T(1,128)S(1)} %get-tuple-element.46), channel_id=1, source_target_pairs={{0,11},{1,10},{2,9},{3,8},{4,15},{5,14},{6,13},{7,12},{8,3},{9,2},... | collective-permute-start | bytes 776 | tf_op jit(solution)/shard_map/ppermute | solution.py:132
  100.1 9.9 %collective-permute-start.30 = (f32[1,64]{1,0:T(1,128)S(1)}, f32[1,64]{1,0:T(1,128)S(1)}, u32[]{:S(2)}, u32[]{:S(2)}) collective-permute-start(f32[1,64]{1,0:T(1,128)S(1)} %get-tuple-element.46), channel_id=1, source_target_pairs={{0,13},{1,12},{2,15},{3,14},{4,9},{5,8},{6,11},{7,10},{8,5},{9,4},... | collective-permute-start | bytes 776 | tf_op jit(solution)/shard_map/ppermute | solution.py:132
  101.3 8.8 %collective-permute-start.31 = (f32[1,64]{1,0:T(1,128)S(1)}, f32[1,64]{1,0:T(1,128)S(1)}, u32[]{:S(2)}, u32[]{:S(2)}) collective-permute-start(f32[1,64]{1,0:T(1,128)S(1)} %get-tuple-element.46), channel_id=1, source_target_pairs={{0,15},{1,14},{2,13},{3,12},{4,11},{5,10},{6,9},{7,8},{8,7},{9,6},... | collective-permute-start | bytes 776 | tf_op jit(solution)/shard_map/ppermute | solution.py:132
  (20 other events, 139.0 us)

commit v3 on v1

v3 whole, which is shorter than its diff:
```python
import jax
import jax.numpy as jnp
from jax import lax
from jax.experimental import pallas as pl
from jax.experimental.pallas import tpu as pltpu
from jax.sharding import PartitionSpec as P

BLK = 128
TB = 640
MASS_ROWS = 16
VMEM_LIMIT = 48 * 1024 * 1024


def swap_halves(x):
    return lax.ppermute(x, "tv", [(0, 1), (1, 0)])


def block_weights(row_of, weight, rows):
    row_ids = lax.broadcasted_iota(jnp.int32, (rows + MASS_ROWS, row_of.shape[1]), 0)
    total = jnp.zeros(row_ids.shape, jnp.float32)
    for slot in range(row_of.shape[0]):
        hit = (row_ids == row_of[slot][None, :]) | (row_ids == rows + slot)
        total = total + jnp.where(hit, weight[slot].astype(jnp.float32)[None, :], 0.0)
    return total.astype(jnp.bfloat16)


def spread_tokens(t_ref, s_ref):
    tokens = t_ref.shape[0]
    count = t_ref.shape[1] // BLK
    step = 16

    def some(i, carry):
        for j in range(step):
            k = i * step + j
            tile = t_ref[:, pl.ds(pl.multiple_of(k * BLK, BLK), BLK)]
            s_ref[pl.ds(pl.multiple_of(k * tokens, tokens), tokens), :] = tile.astype(jnp.float32)
        return carry

    lax.fori_loop(0, count // step, some, 0)


def token_pair(s_ref, t, tokens):
    count = s_ref.shape[0] // tokens
    both = [s_ref[pl.ds(t + i, count, stride=tokens), :].astype(jnp.bfloat16) for i in range(2)]
    return jnp.concatenate(both, axis=1)


def map_own_kernel(w_ref, t_ref, o_ref, s_ref):
    tokens = t_ref.shape[0]
    spread_tokens(t_ref, s_ref)
    for t in range(0, tokens, 2):
        o_ref[:, t * BLK : (t + 2) * BLK] = jnp.dot(
            w_ref[...], token_pair(s_ref, t, tokens), preferred_element_type=jnp.float32
        )


def three_parts(x):
    parts = []
    for _ in range(3):
        parts.append(x.astype(jnp.bfloat16).astype(jnp.float32))
        x = x - parts[-1]
    return parts


def map_rest_kernel(w_ref, t_ref, p_ref, stats_ref, o_ref, s_ref, m_ref):
    tokens = t_ref.shape[0]
    owners = o_ref.shape[0]
    rows = w_ref.shape[0] - MASS_ROWS
    mine = rows // owners
    spread_tokens(t_ref, s_ref)
    for t in range(0, tokens, 2):
        both = p_ref[:, t * BLK : (t + 2) * BLK] + jnp.dot(
            w_ref[...], token_pair(s_ref, t, tokens), preferred_element_type=jnp.float32
        )
        for i in range(2):
            m_ref[pl.ds(t + i, rows + 8, stride=tokens), :] = both[: rows + 8, i * BLK : (i + 1) * BLK]
    mass = m_ref[rows * tokens : (rows + 1) * tokens, :]
    for slot in range(1, 2):
        mass = mass + m_ref[(rows + slot) * tokens : (rows + slot + 1) * tokens, :]
    inverse = jnp.broadcast_to(1.0 / jnp.sum(mass, axis=1, keepdims=True), (tokens, BLK))
    stats = [stats_ref[0:1, :]] + three_parts(stats_ref[1:2, :])
    extra = jnp.zeros((tokens, stats_ref.shape[1]), jnp.float32)
    row_ids = lax.broadcasted_iota(jnp.int32, extra.shape, 0)
    for i, row in enumerate(stats):
        extra = jnp.where(row_ids == i, row, extra)
    extra = extra.astype(jnp.bfloat16)

    def owner(q, carry):
        for b in range(mine):
            first = pl.multiple_of((q * mine + b) * tokens, tokens)
            tile = m_ref[pl.ds(first, tokens), :] * inverse
            o_ref[q, :, b * BLK : (b + 1) * BLK] = tile.astype(jnp.bfloat16)
        o_ref[q, :, mine * BLK :] = extra
        return carry

    lax.fori_loop(0, owners, owner, 0)


def grad_kernel(scale, target_ref, logits_ref, grad_ref, part_ref):
    owners, tokens, _ = target_ref.shape
    group_tokens, width = logits_ref.shape
    stats = [target_ref[q, :, width:].astype(jnp.float32) for q in range(owners)]
    top = stats[0][0:1]
    for one in stats[1:]:
        top = jnp.maximum(top, one[0:1])
    total = jnp.zeros_like(top)
    for one in stats:
        total = total + (one[1:2] + one[2:3] + one[3:4]) * jnp.exp(one[0:1] - top)
    log_norm = top + jnp.log(total)
    for i in range(group_tokens // BLK):
        rows = slice(i * BLK, (i + 1) * BLK)
        group = slice(i * BLK // tokens, (i + 1) * BLK // tokens)
        norm = jnp.broadcast_to(log_norm[:, rows], (BLK, BLK)).T
        terms = jnp.zeros((BLK, BLK), jnp.float32)
        for b in range(width // BLK):
            lanes = slice(b * BLK, (b + 1) * BLK)
            target = target_ref[group, :, lanes].reshape(BLK, BLK).astype(jnp.float32)
            log_probs = logits_ref[rows, lanes].astype(jnp.float32) - norm
            grad_ref[rows, lanes] = ((jnp.exp(log_probs) - target) * scale).astype(jnp.bfloat16)
            positive = target > 0
            one = target * (jnp.log(jnp.where(positive, target, 1.0)) - log_probs)
            terms = terms + jnp.where(positive, one, 0.0)
        part_ref[:, rows] = jnp.sum(terms.T, axis=0, keepdims=True)


def weight_kernel(hidden_ref, grad_ref, o_ref, block_ref, sem):
    steps, tile, _ = block_ref.shape
    copies = []
    for i in range(steps):
        rows = slice(i * tile, (i + 1) * tile)
        block_ref[i] = jnp.dot(
            hidden_ref[rows, :], grad_ref[...], preferred_element_type=jnp.float32
        ).astype(jnp.bfloat16)
        copies.append(pltpu.make_async_copy(block_ref.at[i], o_ref.at[pl.ds(i * tile, tile), :], sem.at[i]))
        copies[-1].start()
    for copy in copies:
        copy.wait()


def whole():
    return pl.BlockSpec(memory_space=pltpu.VMEM)


def params():
    return pltpu.CompilerParams(vmem_limit_bytes=VMEM_LIMIT)


def body(teacher_probs, align_owner, align_local, align_weight, student_logits, hidden):
    owners = lax.axis_size("sv")
    halves = lax.axis_size("tv")
    half_index = lax.axis_index("tv")
    tokens = teacher_probs.shape[0]
    columns = student_logits.shape[1]
    blocks = columns // BLK
    mine = blocks // halves
    width = mine * BLK
    rows = owners * mine
    per_half = TB // halves
    group_tokens = owners * tokens
    half_tokens = student_logits.shape[0]
    features = hidden.shape[1]
    first = half_index == 0

    def in_order(own, other, axis):
        return jnp.concatenate([jnp.where(first, own, other), jnp.where(first, other, own)], axis=axis)

    teacher_other = swap_halves(teacher_probs)

    keep = lax.dynamic_slice_in_dim(student_logits, half_index * width, width, 1)
    give = lax.dynamic_slice_in_dim(student_logits, (1 - half_index) * width, width, 1)
    logits = in_order(keep, swap_halves(give), 0)

    wide = student_logits.astype(jnp.float32)
    peak = jnp.max(wide, axis=1)
    sums = jnp.sum(jnp.exp(wide - peak[:, None]), axis=1)
    stats = jnp.stack([peak, sums])
    stats = in_order(stats, swap_halves(stats), 1)

    local = align_local.T - half_index * mine
    row_of = jnp.where((local >= 0) & (local < mine), align_owner.T * mine + local, -1)
    weight = align_weight.T
    cut = lambda x, which: lax.dynamic_slice_in_dim(x, which * per_half, per_half, 1)
    w_own = block_weights(cut(row_of, half_index), cut(weight, half_index), rows)
    w_rest = block_weights(cut(row_of, 1 - half_index), cut(weight, 1 - half_index), rows)
    flops = 2 * (rows + MASS_ROWS) * per_half * tokens * BLK
    spread = pltpu.VMEM((per_half * tokens, BLK), jnp.float32)
    part = pl.pallas_call(
        map_own_kernel,
        out_shape=jax.ShapeDtypeStruct((rows + MASS_ROWS, tokens * BLK), jnp.float32),
        in_specs=[whole()] * 2,
        out_specs=whole(),
        scratch_shapes=[spread],
        compiler_params=params(),
        cost_estimate=pl.CostEstimate(flops=flops, bytes_accessed=3 << 20, transcendentals=0),
        name="map_own",
    )(w_own, teacher_probs)
    outgoing = pl.pallas_call(
        map_rest_kernel,
        out_shape=jax.ShapeDtypeStruct((owners, tokens, width + group_tokens), jnp.bfloat16),
        in_specs=[whole()] * 4,
        out_specs=whole(),
        scratch_shapes=[spread, pltpu.VMEM(((rows + 8) * tokens, BLK), jnp.float32)],
        compiler_params=params(),
        cost_estimate=pl.CostEstimate(flops=flops, bytes_accessed=4 << 20, transcendentals=0),
        name="map_rest",
    )(w_rest, teacher_other, part, stats)
    target = lax.all_to_all(outgoing, "sv", 0, 0, tiled=True)

    hidden, outgoing = lax.optimization_barrier((hidden, outgoing))
    hidden_own = lax.all_gather(hidden, "sv")
    hidden_other = swap_halves(hidden_own)
    hidden_t = in_order(hidden_own, hidden_other, 1).reshape(group_tokens, features).T

    scale = float(columns * owners)
    grad, terms = pl.pallas_call(
        lambda *refs: grad_kernel(scale, *refs),
        out_shape=(
            jax.ShapeDtypeStruct((group_tokens, width), jnp.bfloat16),
            jax.ShapeDtypeStruct((1, group_tokens), jnp.float32),
        ),
        in_specs=[whole()] * 2,
        out_specs=(whole(), whole()),
        compiler_params=params(),
        cost_estimate=pl.CostEstimate(
            flops=10 * group_tokens * width,
            bytes_accessed=6 * group_tokens * width,
            transcendentals=2 * group_tokens * width,
        ),
        name="logit_grad",
    )(target, logits)

    keep = lax.dynamic_slice_in_dim(grad, half_index * half_tokens, half_tokens, 0)
    give = lax.dynamic_slice_in_dim(grad, (1 - half_index) * half_tokens, half_tokens, 0)
    logit_grad = in_order(keep, swap_halves(give), 1)

    terms = jnp.broadcast_to(terms.reshape(1, halves, half_tokens), (owners, halves, half_tokens))
    terms = lax.all_to_all(terms.reshape(owners * halves, half_tokens), ("sv", "tv"), 0, 0, tiled=True)
    divergence = jnp.sum(terms, axis=0)

    steps = 8
    weight_grad = pl.pallas_call(
        weight_kernel,
        out_shape=jax.ShapeDtypeStruct((features, width), jnp.bfloat16),
        in_specs=[whole()] * 2,
        out_specs=pl.BlockSpec(memory_space=pl.ANY),
        scratch_shapes=[
            pltpu.VMEM((steps, features // steps, width), jnp.bfloat16),
            pltpu.SemaphoreType.DMA((steps,)),
        ],
        compiler_params=params(),
        cost_estimate=pl.CostEstimate(
            flops=2 * features * group_tokens * width,
            bytes_accessed=2 * (features * width + group_tokens * (features + width)),
            transcendentals=0,
        ),
        name="weight_grad",
    )(hidden_t, grad)
    return (divergence, logit_grad, weight_grad)


def solution(mesh):
    return jax.shard_map(
        body,
        mesh=mesh,
        in_specs=(
            P(("grp", "sv"), "tv"),
            P(),
            P(),
            P(),
            P(("grp", "tv"), "sv"),
            P(("grp", "sv", "tv"), None),
        ),
        out_specs=(P(("grp", "tv")), P(("grp", "tv"), "sv"), P(None, ("grp", "sv", "tv"))),
        check_vma=False,
    )
```

time: 69.8 us -> 73.4 us (1.052)
  blocking collectives: 0 us -> 38.7 us
  waiting for transfers between devices: 25.5 us -> 4.01 us
  starting transfers between devices: 18.7 us -> 11.8 us
  local copies, waits for them, and re-layouts: 6.79 us -> 2.69 us
  Pallas kernels: 12.1 us -> 9.58 us
    all_gather x0 -> x1, blocking collectives: none -> 38.7 us  [body(): hidden_own = lax.all_gather(hidden, 'sv')]
    all_to_all x3 -> x1, waiting for transfers between devices: 25 us -> 0.01 us  [body(): target = lax.all_to_all(outgoing, 'sv', 0, 0, tiled=True)]
    all_to_all x3 -> x1, starting transfers between devices: 14.3 us -> 7.04 us  [body(): target = lax.all_to_all(outgoing, 'sv', 0, 0, tiled=True)]
    pallas_call x1, Pallas kernels: 5.82 us -> 3.63 us  [body(): pl.pallas_call(weight_kernel, out_shape=jax.ShapeDtypeStruct((features, w...]
    all_to_all x1, waiting for transfers between devices: 0.51 us -> 2.66 us  [body(): lax.all_to_all(terms.reshape(owners * halves, half_tokens), ('sv', 'tv'),...]
    unnamed x15 -> x12, local copies, waits for them, and re-layouts: 1.66 us -> 0.03 us
    reshape x2 -> x1, local copies, waits for them, and re-layouts: 1.7 us -> 0.27 us  [body(): in_order(hidden_own, hidden_other, 1).reshape(group_tokens, features)]
    ppermute x4 -> x5, waiting for transfers between devices: 0.01 us -> 1.35 us  [swap_halves(): return lax.ppermute(x, 'tv', [(0, 1), (1, 0)])]
  transfers between devices with their start and end apart: 8 -> 7, of which waited for: 4 -> 2; matrix products, arithmetic and copies ran while one was open for 11% -> 6% of each run, Pallas kernels for 17% -> 12%
where the time goes in v3:
time: 73.4 us; the launch traced here: 73.1 us
  blocking collectives  38.7 us (53%)
  starting transfers between devices  11.8 us (16%)
  Pallas kernels  9.58 us (13%)
  other arithmetic  5.43 us (7%)
  waiting for transfers between devices  4.01 us (5%)
  local copies, waits for them, and re-layouts  2.69 us (4%)
  between operations  0.82 us (1%)
    all_gather x1, blocking collectives, body(): hidden_own = lax.all_gather(hidden, 'sv')  38.7 us
    all_to_all x1, starting transfers between devices, body(): target = lax.all_to_all(outgoing, 'sv', 0, 0, tiled=True)  7.04 us
    pallas_call x1, Pallas kernels, body(): pl.pallas_call(map_rest_kernel, out_shape=jax.ShapeDtypeStruct((owners, t...  3.93 us
    pallas_call x1, Pallas kernels, body(): pl.pallas_call(weight_kernel, out_shape=jax.ShapeDtypeStruct((features, w...  3.63 us
    all_to_all x1, starting transfers between devices, body(): lax.all_to_all(terms.reshape(owners * halves, half_tokens), ('sv', 'tv'),...  3.47 us
    all_to_all x1, waiting for transfers between devices, body(): lax.all_to_all(terms.reshape(owners * halves, half_tokens), ('sv', 'tv'),...  2.66 us
  transfers between devices with their start and end apart: 7, of which 2 were waited for; matrix products, arithmetic and copies ran while one was open for 6% of the time, Pallas kernels for 12%

profile of v3, /device:TPU:0, one launch (start us, length us, event | category | flops | bytes accessed | tf_op | source)
XLA Modules:
  0.0 73.1 jit_solution(12929607272022321308)
XLA Ops:
  0.7 1.3 %reduce_max.18 = bf16[64]{0:T(256)(128)(2,1)S(1)} reduce(bf16[64,4096]{1,0:T(8,128)(2,1)} %param.10, bf16[]{:T(256)} %constant.8.clone.1), dimensions={1}, to_apply=%region_0.1 | reduce | flops 262080 | bytes 524418 | tf_op jit(solution)/shard_map/reduce_max | solution.py:174
  2.0 1.4 %exponential_reduce_fusion = f32[64]{0:T(128)S(1)} fusion(bf16[64,4096]{1,0:T(8,128)(2,1)} %param.10, f32[64]{0:T(128)S(1)} %get-tuple-element.32), kind=kLoop, calls=%fused_computation | loop fusion | flops 786368 | bytes 524800 | tf_op jit(solution)/shard_map/reduce_sum | solution.py:175
  3.4 0.5 collective-permute-start.1
  4.0 1.0 %constant_dynamic-slice_fusion.1 = bf16[64,2048]{1,0:T(8,128)(2,1)S(1)} fusion(bf16[64,4096]{1,0:T(8,128)(2,1)} %param.10, s32[]{:T(128)S(6)} %select_n.94), kind=kLoop, calls=%fused_computation.24 | loop fusion | bytes 524292 | tf_op jit(solution)/shard_map/dynamic_slice | solution.py:170
  5.0 0.5 collective-permute-start.2
  5.7 0.2 add_convert_fusion
  6.0 1.4 %map_own.1.p_ref = f32[144,2048]{1,0:T(8,128)S(1)} custom-call(bf16[144,320]{1,0:T(8,128)(2,1)S(1)} %get-tuple-element.29.w_ref, bf16[16,40960]{1,0:T(8,128)(2,1)S(1)} %copy-done), custom_call_target="tpu_custom_call" | custom-call | flops 188743680 | bytes 3145728 | tf_op jit(solution)/shard_map/map_own/pallas_call | solution.py:187
  7.5 3.9 %map_rest.1 = bf16[8,16,2176]{2,1,0:T(8,128)(2,1)} custom-call(bf16[144,320]{1,0:T(8,128)(2,1)S(1)} %get-tuple-element.30.w_ref, bf16[16,40960]{1,0:T(8,128)(2,1)} %collective-permute-done.t_ref, f32[144,2048]{1,0:T(8,128)S(1)} %map_own.1.p_ref, f32[2,128]{1,0:T(2,128)S(1)} %pad_maximum_fusion.4.stats_ref), custom_call_target="tpu_custom_call" | custom-call | flops 188743680 | bytes 4194304 | tf_op jit(solution)/shard_map/map_rest/pallas_call | solution.py:197
  11.4 7.0 %all-to-all-start = ((bf16[8,16,2176]{2,1,0:T(8,128)(2,1)}), bf16[8,16,2176]{2,1,0:T(8,128)(2,1)S(1)}, u32[]{:S(2)}, u32[]{:S(2)}) async-start(bf16[8,16,2176]{2,1,0:T(8,128)(2,1)} %map_rest.1), calls=%async_computation | async-start | bytes 1114112 | tf_op jit(solution)/shard_map/all_to_all | solution.py:207
  18.4 38.7 %all-gather = bf16[64,1920]{1,0:T(8,128)(2,1)S(1)} all-gather(bf16[8,1920]{1,0:T(8,128)(2,1)S(1)} %copy-done.2), channel_id=2, replica_groups=mesh['grp'=2,'sv'=8,'tv'=2] {'sv'}, dimensions={0}, use_global_device_ids=true | all-gather | bytes 276480 | tf_op jit(solution)/shard_map/all_gather | solution.py:210
  57.2 0.1 broadcast_select_fusion.3
  57.3 1.3 %collective-permute-done.4 = bf16[8,8,1920]{2,1,0:T(8,128)(2,1)S(1)} collective-permute-done((bf16[8,8,1920]{2,1,0:T(8,128)(2,1)S(1)}, bf16[8,8,1920]{2,1,0:T(8,128)(2,1)S(1)}, u32[]{:S(2)}, u32[]{:S(2)}) %collective-permute-start.4) | collective-permute-done | bytes 245792 | tf_op jit(solution)/shard_map/ppermute | solution.py:15
  58.7 0.6 logit_grad.1
  59.4 0.2 collective-permute-start.3
  59.6 0.3 copy.13
  59.9 0.5 broadcast.40
  60.4 0.7 reduce.21
  61.2 0.6 broadcast_in_dim.81
  61.8 3.5 %all-to-all-start.1 = ((f32[16,1,64]{2,1,0:T(1,128)}), f32[16,1,64]{2,1,0:T(1,128)S(1)}, u32[]{:S(2)}, u32[]{:S(2)}) async-start(f32[16,1,64]{2,1,0:T(1,128)} %bitcast.6), calls=%async_computation.1 | async-start | bytes 16384 | tf_op jit(solution)/shard_map/all_to_all | solution.py:237
  65.3 3.6 %weight_grad.1 = bf16[1920,2048]{1,0:T(8,128)(2,1)} custom-call(bf16[1920,128]{1,0:T(8,128)(2,1)S(1)} %bitcast.17, bf16[128,2048]{1,0:T(8,128)(2,1)S(1)} %get-tuple-element.7.grad_ref), custom_call_target="tpu_custom_call" | custom-call | flops 1006632960 | bytes 8880128 | tf_op jit(solution)/shard_map/weight_grad/pallas_call | solution.py:241
  68.9 2.7 %all-to-all-done.1 = f32[16,1,64]{2,1,0:T(1,128)S(1)} async-done(((f32[16,1,64]{2,1,0:T(1,128)}), f32[16,1,64]{2,1,0:T(1,128)S(1)}, u32[]{:S(2)}, u32[]{:S(2)}) %all-to-all-start.1) | async-done | bytes 4128 | tf_op jit(solution)/shard_map/all_to_all | solution.py:237
  71.6 0.5 reduce_sum.19
  72.1 0.1 broadcast_select_fusion.1
  72.2 0.8 %pad_maximum_fusion.1 = bf16[64,4096]{1,0:T(8,128)(2,1)} fusion(bf16[64,2048]{1,0:T(8,128)(2,1)S(1)} %get-tuple-element.18, bf16[64,2048]{1,0:T(8,128)(2,1)S(1)} %get-tuple-element.17), kind=kLoop, calls=%fused_computation.2 | loop fusion | flops 1048576 | bytes 1048576 | tf_op jit(solution)/shard_map/concatenate | solution.py:165
  (34 shorter events, 0.7 us)
Async XLA Ops:
  0.6 5.3 %copy-start = (bf16[16,40960]{1,0:T(8,128)(2,1)S(1)}, bf16[16,40960]{1,0:T(8,128)(2,1)}, u32[]{:S(2)}) copy-start(bf16[16,40960]{1,0:T(8,128)(2,1)} %t_ref.1) | copy-start | bytes 3932164
  0.6 4.8 %copy-start.5 = (bf16[640,2]{0,1:T(2,128)(2,1)S(1)}, bf16[640,2]{0,1:T(2,128)(2,1)}, u32[]{:S(2)}) copy-start(bf16[640,2]{0,1:T(2,128)(2,1)} %param.9) | copy-start | bytes 7684
  0.7 4.9 %copy-start.3 = (s32[640,2]{0,1:T(2,128)S(1)}, s32[640,2]{0,1:T(2,128)}, u32[]{:S(2)}) copy-start(s32[640,2]{0,1:T(2,128)} %param.7) | copy-start | bytes 15364
  0.7 4.9 %copy-start.4 = (s32[640,2]{0,1:T(2,128)S(1)}, s32[640,2]{0,1:T(2,128)}, u32[]{:S(2)}) copy-start(s32[640,2]{0,1:T(2,128)} %param.8) | copy-start | bytes 15364
  3.4 4.0 %collective-permute-start.1 = (f32[2,64]{1,0:T(2,128)S(1)}, f32[2,64]{1,0:T(2,128)S(1)}, u32[]{:S(2)}, u32[]{:S(2)}) collective-permute-start(f32[2,64]{1,0:T(2,128)S(1)} %pad_maximum_fusion.3), channel_id=1, source_target_pairs={{0,1},{1,0},{2,3},{3,2},{4,5},{5,4},{6,7},{7,6},{8,9},{9,8},{10,11... | collective-permute-start | bytes 1544 | tf_op jit(solution)/shard_map/ppermute | solution.py:15
  3.9 3.5 %collective-permute-start = (bf16[16,40960]{1,0:T(8,128)(2,1)}, bf16[16,40960]{1,0:T(8,128)(2,1)}, u32[]{:S(2)}, u32[]{:S(2)}) collective-permute-start(bf16[16,40960]{1,0:T(8,128)(2,1)} %t_ref.1), channel_id=1, source_target_pairs={{0,1},{1,0},{2,3},{3,2},{4,5},{5,4},{6,7},{7,6},{8,9},{9,8},{10,11... | collective-permute-start | bytes 3932168 | tf_op jit(solution)/shard_map/ppermute | solution.py:15
  5.0 52.2 %collective-permute-start.2 = (bf16[64,2048]{1,0:T(8,128)(2,1)S(1)}, bf16[64,2048]{1,0:T(8,128)(2,1)S(1)}, u32[]{:S(2)}, u32[]{:S(2)}) collective-permute-start(bf16[64,2048]{1,0:T(8,128)(2,1)S(1)} %constant_dynamic-slice_fusion.1), channel_id=1, source_target_pairs={{0,1},{1,0},{2,3},{3,2},{4,5},{5,4},{6,7},{7,6},{8,9},{9,8},{10,11... | collective-permute-start | bytes 786440 | tf_op jit(solution)/shard_map/ppermute | solution.py:15
  7.5 11.0 %copy-start.2 = (bf16[8,1920]{1,0:T(8,128)(2,1)S(1)}, bf16[8,1920]{1,0:T(8,128)(2,1)}, u32[]{:S(2)}) copy-start(bf16[8,1920]{1,0:T(8,128)(2,1)} %param.11) | copy-start | bytes 92164
  11.4 45.8 %copy-start.1 = (bf16[64,4096]{1,0:T(8,128)(2,1)S(1)}, bf16[64,4096]{1,0:T(8,128)(2,1)}, u32[]{:S(2)}) copy-start(bf16[64,4096]{1,0:T(8,128)(2,1)} %param.10) | copy-start | bytes 1572868
  11.4 47.3 %all-to-all-start = ((bf16[8,16,2176]{2,1,0:T(8,128)(2,1)}), bf16[8,16,2176]{2,1,0:T(8,128)(2,1)S(1)}, u32[]{:S(2)}, u32[]{:S(2)}) async-start(bf16[8,16,2176]{2,1,0:T(8,128)(2,1)} %map_rest.1), calls=%async_computation | async-start | bytes 1114112 | tf_op jit(solution)/shard_map/all_to_all | solution.py:207
  57.2 1.5 %collective-permute-start.4 = (bf16[8,8,1920]{2,1,0:T(8,128)(2,1)S(1)}, bf16[8,8,1920]{2,1,0:T(8,128)(2,1)S(1)}, u32[]{:S(2)}, u32[]{:S(2)}) collective-permute-start(bf16[8,8,1920]{2,1,0:T(8,128)(2,1)S(1)} %bitcast.19), channel_id=1, source_target_pairs={{0,1},{1,0},{2,3},{3,2},{4,5},{5,4},{6,7},{7,6},{8,9},{9,8},{10,11... | collective-permute-start | bytes 737288 | tf_op jit(solution)/shard_map/ppermute | solution.py:15
  59.4 12.7 %collective-permute-start.3 = (bf16[64,2048]{1,0:T(8,128)(2,1)S(1)}, bf16[64,2048]{1,0:T(8,128)(2,1)S(1)}, u32[]{:S(2)}, u32[]{:S(2)}) collective-permute-start(bf16[64,2048]{1,0:T(8,128)(2,1)S(1)} %constant_dynamic-slice_fusion), channel_id=1, source_target_pairs={{0,1},{1,0},{2,3},{3,2},{4,5},{5,4},{6,7},{7,6},{8,9},{9,8},{10,11... | collective-permute-start | bytes 786440 | tf_op jit(solution)/shard_map/ppermute | solution.py:15
  61.8 9.8 %all-to-all-start.1 = ((f32[16,1,64]{2,1,0:T(1,128)}), f32[16,1,64]{2,1,0:T(1,128)S(1)}, u32[]{:S(2)}, u32[]{:S(2)}) async-start(f32[16,1,64]{2,1,0:T(1,128)} %bitcast.6), calls=%async_computation.1 | async-start | bytes 16384 | tf_op jit(solution)/shard_map/all_to_all | solution.py:237

commit v4 on v3

--- a/solution.py
+++ b/solution.py
@@ -24,14 +24,13 @@
     return total.astype(jnp.bfloat16)
 
 
-def spread_tokens(t_ref, s_ref):
+def spread_tokens(t_ref, s_ref, start, count):
     tokens = t_ref.shape[0]
-    count = t_ref.shape[1] // BLK
     step = 16
 
     def some(i, carry):
         for j in range(step):
-            k = i * step + j
+            k = start + i * step + j
             tile = t_ref[:, pl.ds(pl.multiple_of(k * BLK, BLK), BLK)]
             s_ref[pl.ds(pl.multiple_of(k * tokens, tokens), tokens), :] = tile.astype(jnp.float32)
         return carry
@@ -47,7 +46,7 @@
 
 def map_own_kernel(w_ref, t_ref, o_ref, s_ref):
     tokens = t_ref.shape[0]
-    spread_tokens(t_ref, s_ref)
+    spread_tokens(t_ref, s_ref, 0, t_ref.shape[1] // BLK)
     for t in range(0, tokens, 2):
         o_ref[:, t * BLK : (t + 2) * BLK] = jnp.dot(
             w_ref[...], token_pair(s_ref, t, tokens), preferred_element_type=jnp.float32
@@ -62,12 +61,30 @@
     return parts
 
 
-def map_rest_kernel(w_ref, t_ref, p_ref, stats_ref, o_ref, s_ref, m_ref):
+def map_rest_kernel(w_ref, t_ref, p_ref, stats_ref, o_ref, t_buf, s_ref, m_ref, o_buf, in_sem, out_sem):
     tokens = t_ref.shape[0]
     owners = o_ref.shape[0]
     rows = w_ref.shape[0] - MASS_ROWS
     mine = rows // owners
-    spread_tokens(t_ref, s_ref)
+    cuts = in_sem.shape[0]
+    part = t_ref.shape[1] // cuts
+    arriving = [
+        pltpu.make_async_copy(
+            t_ref.at[:, pl.ds(i * part, part)], t_buf.at[:, pl.ds(i * part, part)], in_sem.at[i]
+        )
+        for i in range(cuts)
+    ]
+    for copy in arriving:
+        copy.start()
+    stats = [stats_ref[0:1, :]] + three_parts(stats_ref[1:2, :])
+    extra = jnp.zeros((tokens, stats_ref.shape[1]), jnp.float32)
+    row_ids = lax.broadcasted_iota(jnp.int32, extra.shape, 0)
+    for i, row in enumerate(stats):
+        extra = jnp.where(row_ids == i, row, extra)
+    extra = extra.astype(jnp.bfloat16)
+    for i, copy in enumerate(arriving):
+        copy.wait()
+        spread_tokens(t_buf, s_ref, i * (part // BLK), part // BLK)
     for t in range(0, tokens, 2):
         both = p_ref[:, t * BLK : (t + 2) * BLK] + jnp.dot(
             w_ref[...], token_pair(s_ref, t, tokens), preferred_element_type=jnp.float32
@@ -78,22 +95,40 @@
     for slot in range(1, 2):
         mass = mass + m_ref[(rows + slot) * tokens : (rows + slot + 1) * tokens, :]
     inverse = jnp.broadcast_to(1.0 / jnp.sum(mass, axis=1, keepdims=True), (tokens, BLK))
-    stats = [stats_ref[0:1, :]] + three_parts(stats_ref[1:2, :])
-    extra = jnp.zeros((tokens, stats_ref.shape[1]), jnp.float32)
-    row_ids = lax.broadcasted_iota(jnp.int32, extra.shape, 0)
-    for i, row in enumerate(stats):
-        extra = jnp.where(row_ids == i, row, extra)
-    extra = extra.astype(jnp.bfloat16)
+
+    def leaving(q):
+        return pltpu.make_async_copy(o_buf.at[q], o_ref.at[q], out_sem.at[q])
 
     def owner(q, carry):
         for b in range(mine):
             first = pl.multiple_of((q * mine + b) * tokens, tokens)
             tile = m_ref[pl.ds(first, tokens), :] * inverse
-            o_ref[q, :, b * BLK : (b + 1) * BLK] = tile.astype(jnp.bfloat16)
-        o_ref[q, :, mine * BLK :] = extra
+            o_buf[q, :, b * BLK : (b + 1) * BLK] = tile.astype(jnp.bfloat16)
+        o_buf[q, :, mine * BLK :] = extra
+        leaving(q).start()
         return carry
 
+    def left(q, carry):
+        leaving(q).wait()
+        return carry
+
     lax.fori_loop(0, owners, owner, 0)
+    lax.fori_loop(0, owners, left, 0)
+
+
+def stats_kernel(logits_ref, o_ref):
+    half_tokens, columns = logits_ref.shape
+    for i in range(0, half_tokens, 64):
+        rows = slice(i, i + 64)
+        peak = logits_ref[rows, :BLK].astype(jnp.float32)
+        for b in range(1, columns // BLK):
+            peak = jnp.maximum(peak, logits_ref[rows, b * BLK : (b + 1) * BLK].astype(jnp.float32))
+        peak = jnp.broadcast_to(jnp.max(peak, axis=1, keepdims=True), peak.shape)
+        total = jnp.zeros_like(peak)
+        for b in range(columns // BLK):
+            total = total + jnp.exp(logits_ref[rows, b * BLK : (b + 1) * BLK].astype(jnp.float32) - peak)
+        o_ref[0:1, rows] = peak.T[0:1]
+        o_ref[1:2, rows] = jnp.sum(total.T, axis=0, keepdims=True)
 
 
 def grad_kernel(scale, target_ref, logits_ref, grad_ref, part_ref):
@@ -120,7 +155,44 @@
             positive = target > 0
             one = target * (jnp.log(jnp.where(positive, target, 1.0)) - log_probs)
             terms = terms + jnp.where(positive, one, 0.0)
-        part_ref[:, rows] = jnp.sum(terms.T, axis=0, keepdims=True)
+        row = jnp.sum(terms.T, axis=0, keepdims=True)
+        for q in range(part_ref.shape[0]):
+            part_ref[q, :, rows] = jnp.broadcast_to(row, (part_ref.shape[1], BLK))
+
+
+def hidden_kernel(place_ref, own_ref, other_ref, o_ref, s_ref):
+    owners, held, features = own_ref.shape
+    for i in range(owners):
+        offset = sum(((i >> j) & 1) * (owners >> (j + 1)) for j in range(owners.bit_length() - 1))
+        first = (place_ref[0] ^ offset) * 2
+        own = pl.ds(pl.multiple_of((first + place_ref[1]) * held, held), held)
+        other = pl.ds(pl.multiple_of((first + 1 - place_ref[1]) * held, held), held)
+        s_ref[own, :] = own_ref[i].astype(jnp.float32)
+        s_ref[other, :] = other_ref[i].astype(jnp.float32)
+    for i in range(s_ref.shape[0] // BLK):
+        for j in range(features // BLK):
+            tile = s_ref[i * BLK : (i + 1) * BLK, j * BLK : (j + 1) * BLK].T
+            o_ref[j * BLK : (j + 1) * BLK, i * BLK : (i + 1) * BLK] = tile.astype(jnp.bfloat16)
+
+
+def finish_kernel(place_ref, grad_ref, got_ref, terms_ref, o_ref, d_ref, sem):
+    half_tokens, width = got_ref.shape
+    half = place_ref[1]
+    kept_at = pl.ds(pl.multiple_of(half * width, width), width)
+    got_at = pl.ds(pl.multiple_of((1 - half) * width, width), width)
+    rows = pl.ds(pl.multiple_of(half * half_tokens, half_tokens), half_tokens)
+    copies = [
+        pltpu.make_async_copy(grad_ref.at[rows, :], o_ref.at[:, kept_at], sem.at[0]),
+        pltpu.make_async_copy(got_ref, o_ref.at[:, got_at], sem.at[1]),
+    ]
+    for copy in copies:
+        copy.start()
+    total = terms_ref[0, 0:1, :]
+    for q in range(1, terms_ref.shape[0]):
+        total = total + terms_ref[q, 0:1, :]
+    d_ref[...] = jnp.where(half == 0, total[:, :half_tokens], total[:, half_tokens:])
+    for copy in copies:
+        copy.wait()
 
 
 def weight_kernel(hidden_ref, grad_ref, o_ref, block_ref, sem):
@@ -145,10 +217,23 @@
     return pltpu.CompilerParams(vmem_limit_bytes=VMEM_LIMIT)
 
 
+def scalars():
+    return pl.BlockSpec(memory_space=pltpu.SMEM)
+
+
+def anywhere():
+    return pl.BlockSpec(memory_space=pl.ANY)
+
+
+def to_partner(x, offset):
+    return lax.ppermute(x, "sv", [(s, s ^ offset) for s in range(lax.axis_size("sv"))])
+
+
 def body(teacher_probs, align_owner, align_local, align_weight, student_logits, hidden):
     owners = lax.axis_size("sv")
     halves = lax.axis_size("tv")
     half_index = lax.axis_index("tv")
+    place = jnp.stack([lax.axis_index("sv"), half_index]).astype(jnp.int32)
     tokens = teacher_probs.shape[0]
     columns = student_logits.shape[1]
     blocks = columns // BLK
@@ -166,14 +251,15 @@
 
     teacher_other = swap_halves(teacher_probs)
 
-    keep = lax.dynamic_slice_in_dim(student_logits, half_index * width, width, 1)
-    give = lax.dynamic_slice_in_dim(student_logits, (1 - half_index) * width, width, 1)
-    logits = in_order(keep, swap_halves(give), 0)
-
-    wide = student_logits.astype(jnp.float32)
-    peak = jnp.max(wide, axis=1)
-    sums = jnp.sum(jnp.exp(wide - peak[:, None]), axis=1)
-    stats = jnp.stack([peak, sums])
+    stats = pl.pallas_call(
+        stats_kernel,
+        out_shape=jax.ShapeDtypeStruct((2, half_tokens), jnp.float32),
+        in_specs=[whole()],
+        out_specs=whole(),
+        compiler_params=params(),
+        cost_estimate=pl.CostEstimate(flops=0, bytes_accessed=0, transcendentals=0),
+        name="stats",
+    )(student_logits)
     stats = in_order(stats, swap_halves(stats), 1)
 
     local = align_local.T - half_index * mine
@@ -182,7 +268,6 @@
     cut = lambda x, which: lax.dynamic_slice_in_dim(x, which * per_half, per_half, 1)
     w_own = block_weights(cut(row_of, half_index), cut(weight, half_index), rows)
     w_rest = block_weights(cut(row_of, 1 - half_index), cut(weight, 1 - half_index), rows)
-    flops = 2 * (rows + MASS_ROWS) * per_half * tokens * BLK
     spread = pltpu.VMEM((per_half * tokens, BLK), jnp.float32)
     part = pl.pallas_call(
         map_own_kernel,
@@ -191,32 +276,60 @@
         out_specs=whole(),
         scratch_shapes=[spread],
         compiler_params=params(),
-        cost_estimate=pl.CostEstimate(flops=flops, bytes_accessed=3 << 20, transcendentals=0),
+        cost_estimate=pl.CostEstimate(flops=0, bytes_accessed=0, transcendentals=0),
         name="map_own",
     )(w_own, teacher_probs)
+    chunk = (owners, tokens, width + group_tokens)
+    cuts = 4
     outgoing = pl.pallas_call(
         map_rest_kernel,
-        out_shape=jax.ShapeDtypeStruct((owners, tokens, width + group_tokens), jnp.bfloat16),
-        in_specs=[whole()] * 4,
-        out_specs=whole(),
-        scratch_shapes=[spread, pltpu.VMEM(((rows + 8) * tokens, BLK), jnp.float32)],
-        compiler_params=params(),
-        cost_estimate=pl.CostEstimate(flops=flops, bytes_accessed=4 << 20, transcendentals=0),
+        out_shape=jax.ShapeDtypeStruct(chunk, jnp.bfloat16),
+        in_specs=[whole(), anywhere(), whole(), whole()],
+        out_specs=anywhere(),
+        scratch_shapes=[
+            pltpu.VMEM((tokens, per_half * BLK), jnp.bfloat16),
+            spread,
+            pltpu.VMEM(((rows + 8) * tokens, BLK), jnp.float32),
+            pltpu.VMEM(chunk, jnp.bfloat16),
+            pltpu.SemaphoreType.DMA((cuts,)),
+            pltpu.SemaphoreType.DMA((owners,)),
+        ],
+        compiler_params=params(),
+        cost_estimate=pl.CostEstimate(
+            flops=2 * (rows + MASS_ROWS) * per_half * tokens * BLK, bytes_accessed=4 << 20, transcendentals=0
+        ),
         name="map_rest",
     )(w_rest, teacher_other, part, stats)
     target = lax.all_to_all(outgoing, "sv", 0, 0, tiled=True)
 
-    hidden, outgoing = lax.optimization_barrier((hidden, outgoing))
-    hidden_own = lax.all_gather(hidden, "sv")
-    hidden_other = swap_halves(hidden_own)
-    hidden_t = in_order(hidden_own, hidden_other, 1).reshape(group_tokens, features).T
+    hidden, late_logits, outgoing = lax.optimization_barrier((hidden, student_logits, outgoing))
+
+    keep = lax.dynamic_slice_in_dim(late_logits, half_index * width, width, 1)
+    give = lax.dynamic_slice_in_dim(late_logits, (1 - half_index) * width, width, 1)
+    logits = in_order(keep, swap_halves(give), 0)
+
+    hidden_own = hidden[None]
+    offset = owners // 2
+    while offset:
+        hidden_own = jnp.concatenate([hidden_own, to_partner(hidden_own, offset)])
+        offset //= 2
+    hidden_t = pl.pallas_call(
+        hidden_kernel,
+        out_shape=jax.ShapeDtypeStruct((features, group_tokens), jnp.bfloat16),
+        in_specs=[scalars(), whole(), whole()],
+        out_specs=whole(),
+        scratch_shapes=[pltpu.VMEM((group_tokens, features), jnp.float32)],
+        compiler_params=params(),
+        cost_estimate=pl.CostEstimate(flops=0, bytes_accessed=4 * features * group_tokens, transcendentals=0),
+        name="hidden_t",
+    )(place, hidden_own, swap_halves(hidden_own))
 
     scale = float(columns * owners)
     grad, terms = pl.pallas_call(
         lambda *refs: grad_kernel(scale, *refs),
         out_shape=(
             jax.ShapeDtypeStruct((group_tokens, width), jnp.bfloat16),
-            jax.ShapeDtypeStruct((1, group_tokens), jnp.float32),
+            jax.ShapeDtypeStruct((owners * halves, 8, group_tokens), jnp.float32),
         ),
         in_specs=[whole()] * 2,
         out_specs=(whole(), whole()),
@@ -229,20 +342,16 @@
         name="logit_grad",
     )(target, logits)
 
-    keep = lax.dynamic_slice_in_dim(grad, half_index * half_tokens, half_tokens, 0)
+    terms = lax.all_to_all(terms, ("sv", "tv"), 0, 0, tiled=True)
     give = lax.dynamic_slice_in_dim(grad, (1 - half_index) * half_tokens, half_tokens, 0)
-    logit_grad = in_order(keep, swap_halves(give), 1)
-
-    terms = jnp.broadcast_to(terms.reshape(1, halves, half_tokens), (owners, halves, half_tokens))
-    terms = lax.all_to_all(terms.reshape(owners * halves, half_tokens), ("sv", "tv"), 0, 0, tiled=True)
-    divergence = jnp.sum(terms, axis=0)
+    got = swap_halves(give)
 
     steps = 8
     weight_grad = pl.pallas_call(
         weight_kernel,
         out_shape=jax.ShapeDtypeStruct((features, width), jnp.bfloat16),
         in_specs=[whole()] * 2,
-        out_specs=pl.BlockSpec(memory_space=pl.ANY),
+        out_specs=anywhere(),
         scratch_shapes=[
             pltpu.VMEM((steps, features // steps, width), jnp.bfloat16),
             pltpu.SemaphoreType.DMA((steps,)),
@@ -255,7 +364,21 @@
         ),
         name="weight_grad",
     )(hidden_t, grad)
-    return (divergence, logit_grad, weight_grad)
+
+    logit_grad, divergence = pl.pallas_call(
+        finish_kernel,
+        out_shape=(
+            jax.ShapeDtypeStruct((half_tokens, columns), jnp.bfloat16),
+            jax.ShapeDtypeStruct((1, half_tokens), jnp.float32),
+        ),
+        in_specs=[scalars(), anywhere(), anywhere(), whole()],
+        out_specs=(anywhere(), whole()),
+        scratch_shapes=[pltpu.SemaphoreType.DMA((2,))],
+        compiler_params=params(),
+        cost_estimate=pl.CostEstimate(flops=0, bytes_accessed=4 * half_tokens * columns, transcendentals=0),
+        name="finish",
+    )(place, grad, got, terms)
+    return (divergence.reshape(half_tokens), logit_grad, weight_grad)
 
 
 def solution(mesh):

time: 73.4 us -> 51.7 us (0.70)
  blocking collectives: 38.7 us -> 0 us
  waiting for transfers between devices: 4.01 us -> 15.7 us
  starting transfers between devices: 11.8 us -> 17.9 us
  other arithmetic: 5.43 us -> 1.33 us
  Pallas kernels: 9.58 us -> 12.2 us
    all_gather x1 -> x0, blocking collectives: 38.7 us -> none  [body(): hidden_own = lax.all_gather(hidden, 'sv')]
    ppermute x0 -> x3, waiting for transfers between devices: none -> 8.41 us  [to_partner(): lax.ppermute(x, 'sv', [(s, s ^ offset) for s in range(lax.axis_size('sv'))])]
    ppermute x0 -> x3, starting transfers between devices: none -> 8.13 us  [to_partner(): lax.ppermute(x, 'sv', [(s, s ^ offset) for s in range(lax.axis_size('sv'))])]
    all_to_all x1, waiting for transfers between devices: 0.01 us -> 4.96 us  [body(): target = lax.all_to_all(outgoing, 'sv', 0, 0, tiled=True)]
    unnamed x12 -> x8, local copies, waits for them, and re-layouts: 0.03 us -> 2.36 us
    all_to_all x1, starting transfers between devices: 7.04 us -> 5.04 us  [body(): target = lax.all_to_all(outgoing, 'sv', 0, 0, tiled=True)]
    pallas_call x1 -> x4, Pallas kernels: 3.93 us -> 5.92 us  [the longest x1 2.85 us: body(): pl.pallas_call(map_rest_kernel, out_shape=jax.ShapeDtypeStruct(chunk, jnp...]
    reduce_sum x2 -> x0, other arithmetic: 1.93 us -> none  [the longest x1 1.38 us: body(): sums = jnp.sum(jnp.exp(wide - peak[:, None]), axis=1)]
  transfers between devices with their start and end apart: 7 -> 10, of which waited for: 2 -> 4; matrix products, arithmetic and copies ran while one was open for 6% -> 4% of each run, Pallas kernels for 12% -> 14%
where the time goes in v4:
time: 51.7 us; the launch traced here: 51.3 us
  starting transfers between devices  17.9 us (35%)
  waiting for transfers between devices  15.7 us (30%)
  Pallas kernels  12.2 us (24%)
  local copies, waits for them, and re-layouts  3.33 us (6%)
  other arithmetic  1.33 us (3%)
  between operations  0.82 us (2%)
    ppermute x3, waiting for transfers between devices, to_partner(): lax.ppermute(x, 'sv', [(s, s ^ offset) for s in range(lax.axis_size('sv'))])  8.41 us
    ppermute x3, starting transfers between devices, to_partner(): lax.ppermute(x, 'sv', [(s, s ^ offset) for s in range(lax.axis_size('sv'))])  8.13 us
    all_to_all x1, starting transfers between devices, body(): target = lax.all_to_all(outgoing, 'sv', 0, 0, tiled=True)  5.04 us
    all_to_all x1, waiting for transfers between devices, body(): target = lax.all_to_all(outgoing, 'sv', 0, 0, tiled=True)  4.96 us
    all_to_all x1, starting transfers between devices, body(): terms = lax.all_to_all(terms, ('sv', 'tv'), 0, 0, tiled=True)  3.88 us
    pallas_call x1, Pallas kernels, body(): pl.pallas_call(weight_kernel, out_shape=jax.ShapeDtypeStruct((features, w...  3.63 us
    pallas_call x1, Pallas kernels, body(): pl.pallas_call(map_rest_kernel, out_shape=jax.ShapeDtypeStruct(chunk, jnp...  2.85 us
    unnamed x8, local copies, waits for them, and re-layouts  2.36 us
  transfers between devices with their start and end apart: 10, of which 4 were waited for; matrix products, arithmetic and copies ran while one was open for 4% of the time, Pallas kernels for 14%

profile of v4, /device:TPU:0, one launch (start us, length us, event | category | flops | bytes accessed | tf_op | source)
XLA Modules:
  0.0 51.3 jit_solution(17520786323363022092)
XLA Ops:
  0.6 1.0 %copy-done = bf16[64,4096]{1,0:T(8,128)(2,1)S(1)} copy-done((bf16[64,4096]{1,0:T(8,128)(2,1)S(1)}, bf16[64,4096]{1,0:T(8,128)(2,1)}, u32[]{:S(2)}) %copy-start) | copy-done | bytes 524312
  1.7 0.4 stats.1
  2.1 0.5 %collective-permute-start.1 = (f32[2,64]{1,0:T(2,128)S(1)}, f32[2,64]{1,0:T(2,128)S(1)}, u32[]{:S(2)}, u32[]{:S(2)}) collective-permute-start(f32[2,64]{1,0:T(2,128)S(1)} %stats.1), channel_id=1, source_target_pairs={{0,1},{1,0},{2,3},{3,2},{4,5},{5,4},{6,7},{7,6},{8,9},{9,8},{10,11... | collective-permute-start | bytes 1544 | tf_op jit(solution)/shard_map/ppermute | solution.py:15
  2.6 0.1 collective-permute-start
  2.7 0.8 %fusion.5 = (bf16[2,320]{1,0:T(2,128)(2,1)S(1)}, bf16[2,320]{1,0:T(2,128)(2,1)S(1)}) fusion(bf16[640,2]{0,1:T(2,128)(2,1)} %param.9, s32[]{:T(128)S(6)} %select_n.63, s32[]{:T(128)S(6)} %select_n.60), kind=kLoop, calls=%fused_computation.24 | loop fusion | bytes 5128 | tf_op jit(solution)/shard_map/dynamic_slice | solution.py:268
  3.5 0.7 %and_select_fusion = s32[640,2]{0,1:T(2,128)S(1)} fusion(s32[640,2]{0,1:T(2,128)} %param.7, s32[640,2]{0,1:T(2,128)} %param.8, s32[]{:T(128)S(6)} %mul.24), kind=kLoop, calls=%fused_computation.16 | loop fusion | flops 8960 | bytes 15364 | tf_op jit(solution)/shard_map/jit(_where)/select_n | solution.py:266
  4.4 0.2 add_convert_fusion
  4.6 1.3 %copy-done.2 = bf16[16,40960]{1,0:T(8,128)(2,1)S(1)} copy-done((bf16[16,40960]{1,0:T(8,128)(2,1)S(1)}, bf16[16,40960]{1,0:T(8,128)(2,1)}, u32[]{:S(2)}) %copy-start.2) | copy-done | bytes 1310744
  5.9 1.4 %map_own.1.p_ref = f32[144,2048]{1,0:T(8,128)S(1)} custom-call(bf16[144,320]{1,0:T(8,128)(2,1)S(1)} %get-tuple-element.31.w_ref, bf16[16,40960]{1,0:T(8,128)(2,1)S(1)} %copy-done.2), custom_call_target="tpu_custom_call" | custom-call | tf_op jit(solution)/shard_map/map_own/pallas_call | solution.py:272
  7.4 2.9 %map_rest.1 = bf16[8,16,2176]{2,1,0:T(8,128)(2,1)} custom-call(bf16[144,320]{1,0:T(8,128)(2,1)S(1)} %get-tuple-element.32.w_ref, bf16[16,40960]{1,0:T(8,128)(2,1)S(1)} %collective-permute-done.t_ref, f32[144,2048]{1,0:T(8,128)S(1)} %map_own.1.p_ref, f32[2,128]{1,0:T(2,128)S(1)} %pad_maximum_fusion.4.stats_ref), custom_call_target="tpu_custom_call" | custom-call | flops 188743680 | bytes 4194304 | tf_op jit(solution)/shard_map/map_rest/pallas_call | solution.py:284
  10.3 4.1 %collective-permute-start.4 = (bf16[1,8,1920]{2,1,0:T(8,128)(2,1)S(1)}, bf16[1,8,1920]{2,1,0:T(8,128)(2,1)S(1)}, u32[]{:S(2)}, u32[]{:S(2)}) collective-permute-start(bf16[1,8,1920]{2,1,0:T(8,128)(2,1)S(1)} %bitcast.12), channel_id=1, source_target_pairs={{0,8},{2,10},{4,12},{6,14},{8,0},{10,2},{12,4},{14,6},{1,9},{3,11}... | collective-permute-start | bytes 92168 | tf_op jit(solution)/shard_map/ppermute | solution.py:229
  14.4 1.9 %collective-permute-done.4 = bf16[1,8,1920]{2,1,0:T(8,128)(2,1)S(1)} collective-permute-done((bf16[1,8,1920]{2,1,0:T(8,128)(2,1)S(1)}, bf16[1,8,1920]{2,1,0:T(8,128)(2,1)S(1)}, u32[]{:S(2)}, u32[]{:S(2)}) %collective-permute-start.4) | collective-permute-done | bytes 30752 | tf_op jit(solution)/shard_map/ppermute | solution.py:229
  16.3 2.0 %collective-permute-start.5 = (bf16[2,8,1920]{2,1,0:T(8,128)(2,1)S(1)}, bf16[2,8,1920]{2,1,0:T(8,128)(2,1)S(1)}, u32[]{:S(2)}, u32[]{:S(2)}) collective-permute-start(bf16[2,8,1920]{2,1,0:T(8,128)(2,1)S(1)} %pad_maximum_fusion.3), channel_id=1, source_target_pairs={{0,4},{2,6},{4,0},{6,2},{8,12},{10,14},{12,8},{14,10},{1,5},{3,7},... | collective-permute-start | bytes 184328 | tf_op jit(solution)/shard_map/ppermute | solution.py:229
  18.2 5.0 %all-to-all-start = ((bf16[8,16,2176]{2,1,0:T(8,128)(2,1)}), bf16[8,16,2176]{2,1,0:T(8,128)(2,1)S(1)}, u32[]{:S(2)}, u32[]{:S(2)}) async-start(bf16[8,16,2176]{2,1,0:T(8,128)(2,1)} %map_rest.1), calls=%async_computation | async-start | bytes 1114112 | tf_op jit(solution)/shard_map/all_to_all | solution.py:303
  23.3 2.1 %collective-permute-start.6 = (bf16[4,8,1920]{2,1,0:T(8,128)(2,1)S(1)}, bf16[4,8,1920]{2,1,0:T(8,128)(2,1)S(1)}, u32[]{:S(2)}, u32[]{:S(2)}) collective-permute-start(bf16[4,8,1920]{2,1,0:T(8,128)(2,1)S(1)} %pad_maximum_fusion.2), channel_id=1, source_target_pairs={{0,2},{2,0},{4,6},{6,4},{8,10},{10,8},{12,14},{14,12},{1,3},{3,1},... | collective-permute-start | bytes 368648 | tf_op jit(solution)/shard_map/ppermute | solution.py:229
  25.5 6.5 %collective-permute-done.6 = bf16[4,8,1920]{2,1,0:T(8,128)(2,1)S(1)} collective-permute-done((bf16[4,8,1920]{2,1,0:T(8,128)(2,1)S(1)}, bf16[4,8,1920]{2,1,0:T(8,128)(2,1)S(1)}, u32[]{:S(2)}, u32[]{:S(2)}) %collective-permute-start.6) | collective-permute-done | bytes 122912 | tf_op jit(solution)/shard_map/ppermute | solution.py:229
  32.1 0.1 broadcast_select_fusion.1
  32.3 5.0 %all-to-all-done.refs_0_ = bf16[8,16,2176]{2,1,0:T(8,128)(2,1)S(1)} async-done(((bf16[8,16,2176]{2,1,0:T(8,128)(2,1)}), bf16[8,16,2176]{2,1,0:T(8,128)(2,1)S(1)}, u32[]{:S(2)}, u32[]{:S(2)}) %all-to-all-start) | async-done | bytes 557088 | tf_op jit(solution)/shard_map/all_to_all | solution.py:303
  37.3 1.3 %logit_grad.1 = (bf16[128,2048]{1,0:T(8,128)(2,1)S(1)}, f32[16,8,128]{2,1,0:T(8,128)}) custom-call(bf16[8,16,2176]{2,1,0:T(8,128)(2,1)S(1)} %all-to-all-done.refs_0_, bf16[128,2048]{1,0:T(8,128)(2,1)S(1)} %pad_maximum_fusion.refs_1_), custom_call_target="tpu_custom_call" | custom-call | flops 2621440 | bytes 1572864 | tf_op jit(solution)/shard_map/logit_grad/pallas_call | solution.py:328
  38.6 3.9 %all-to-all-start.1 = ((f32[16,8,128]{2,1,0:T(8,128)}), f32[16,8,128]{2,1,0:T(8,128)S(1)}, u32[]{:S(2)}, u32[]{:S(2)}) async-start(f32[16,8,128]{2,1,0:T(8,128)} %get-tuple-element.11), calls=%async_computation.1 | async-start | bytes 131072 | tf_op jit(solution)/shard_map/all_to_all | solution.py:345
  42.6 0.8 %hidden_t.1.hidden_ref = bf16[1920,128]{1,0:T(8,128)(2,1)S(1)} custom-call(s32[2]{0:T(128)S(1)} %pad_add_fusion.place_ref, bf16[8,8,1920]{2,1,0:T(8,128)(2,1)S(1)} %pad_maximum_fusion.1.own_ref, bf16[8,8,1920]{2,1,0:T(8,128)(2,1)S(1)} %collective-permute-done.7.other_ref), custom_call_target="tpu_custom_call" | custom-call | bytes 983040 | tf_op jit(solution)/shard_map/hidden_t/pallas_call | solution.py:316
  43.4 3.6 %weight_grad.1 = bf16[1920,2048]{1,0:T(8,128)(2,1)} custom-call(bf16[1920,128]{1,0:T(8,128)(2,1)S(1)} %hidden_t.1.hidden_ref, bf16[128,2048]{1,0:T(8,128)(2,1)S(1)} %get-tuple-element.10.grad_ref), custom_call_target="tpu_custom_call" | custom-call | flops 1006632960 | bytes 8880128 | tf_op jit(solution)/shard_map/weight_grad/pallas_call | solution.py:350
  47.1 2.4 %all-to-all-done.1.terms_ref = f32[16,8,128]{2,1,0:T(8,128)S(1)} async-done(((f32[16,8,128]{2,1,0:T(8,128)}), f32[16,8,128]{2,1,0:T(8,128)S(1)}, u32[]{:S(2)}, u32[]{:S(2)}) %all-to-all-start.1) | async-done | bytes 65568 | tf_op jit(solution)/shard_map/all_to_all | solution.py:345
  49.4 1.9 %finish.1 = (bf16[64,4096]{1,0:T(8,128)(2,1)}, f32[1,64]{1,0:T(1,128)}) custom-call(s32[2]{0:T(128)S(1)} %pad_add_fusion.place_ref, bf16[128,2048]{1,0:T(8,128)(2,1)S(1)} %get-tuple-element.10.grad_ref, bf16[64,2048]{1,0:T(8,128)(2,1)S(1)} %collective-permute-done.3.got_ref, f32[16,8,128]{2,1,0:T(8,128)S(1)} %all-to-all-done.1.terms_ref), custom_call_target="tpu_custom_call" | custom-call | bytes 1048576 | tf_op jit(solution)/shard_map/finish/pallas_call | solution.py:368
  (28 shorter events, 0.7 us)
Async XLA Ops:
  0.6 1.0 %copy-start = (bf16[64,4096]{1,0:T(8,128)(2,1)S(1)}, bf16[64,4096]{1,0:T(8,128)(2,1)}, u32[]{:S(2)}) copy-start(bf16[64,4096]{1,0:T(8,128)(2,1)} %logits_ref.1) | copy-start | bytes 1572868
  2.1 5.2 %collective-permute-start.1 = (f32[2,64]{1,0:T(2,128)S(1)}, f32[2,64]{1,0:T(2,128)S(1)}, u32[]{:S(2)}, u32[]{:S(2)}) collective-permute-start(f32[2,64]{1,0:T(2,128)S(1)} %stats.1), channel_id=1, source_target_pairs={{0,1},{1,0},{2,3},{3,2},{4,5},{5,4},{6,7},{7,6},{8,9},{9,8},{10,11... | collective-permute-start | bytes 1544 | tf_op jit(solution)/shard_map/ppermute | solution.py:15
  2.6 4.8 %collective-permute-start = (bf16[16,40960]{1,0:T(8,128)(2,1)}, bf16[16,40960]{1,0:T(8,128)(2,1)S(1)}, u32[]{:S(2)}, u32[]{:S(2)}) collective-permute-start(bf16[16,40960]{1,0:T(8,128)(2,1)} %t_ref.1), channel_id=1, source_target_pairs={{0,1},{1,0},{2,3},{3,2},{4,5},{5,4},{6,7},{7,6},{8,9},{9,8},{10,11... | collective-permute-start | bytes 3932168 | tf_op jit(solution)/shard_map/ppermute | solution.py:15
  4.6 1.3 %copy-start.2 = (bf16[16,40960]{1,0:T(8,128)(2,1)S(1)}, bf16[16,40960]{1,0:T(8,128)(2,1)}, u32[]{:S(2)}) copy-start(bf16[16,40960]{1,0:T(8,128)(2,1)} %t_ref.1) | copy-start | bytes 3932164
  7.4 2.9 %copy-start.3 = (bf16[8,1920]{1,0:T(8,128)(2,1)S(1)}, bf16[8,1920]{1,0:T(8,128)(2,1)}, u32[]{:S(2)}) copy-start(bf16[8,1920]{1,0:T(8,128)(2,1)} %param.11) | copy-start | bytes 92164
  10.3 15.1 %copy-start.1 = (bf16[64,4096]{1,0:T(8,128)(2,1)S(1)}, bf16[64,4096]{1,0:T(8,128)(2,1)}, u32[]{:S(2)}) copy-start(bf16[64,4096]{1,0:T(8,128)(2,1)} %logits_ref.1) | copy-start | bytes 1572868
  10.3 6.0 %collective-permute-start.4 = (bf16[1,8,1920]{2,1,0:T(8,128)(2,1)S(1)}, bf16[1,8,1920]{2,1,0:T(8,128)(2,1)S(1)}, u32[]{:S(2)}, u32[]{:S(2)}) collective-permute-start(bf16[1,8,1920]{2,1,0:T(8,128)(2,1)S(1)} %bitcast.12), channel_id=1, source_target_pairs={{0,8},{2,10},{4,12},{6,14},{8,0},{10,2},{12,4},{14,6},{1,9},{3,11}... | collective-permute-start | bytes 92168 | tf_op jit(solution)/shard_map/ppermute | solution.py:229
  16.3 7.0 %collective-permute-start.5 = (bf16[2,8,1920]{2,1,0:T(8,128)(2,1)S(1)}, bf16[2,8,1920]{2,1,0:T(8,128)(2,1)S(1)}, u32[]{:S(2)}, u32[]{:S(2)}) collective-permute-start(bf16[2,8,1920]{2,1,0:T(8,128)(2,1)S(1)} %pad_maximum_fusion.3), channel_id=1, source_target_pairs={{0,4},{2,6},{4,0},{6,2},{8,12},{10,14},{12,8},{14,10},{1,5},{3,7},... | collective-permute-start | bytes 184328 | tf_op jit(solution)/shard_map/ppermute | solution.py:229
  18.2 19.0 %all-to-all-start = ((bf16[8,16,2176]{2,1,0:T(8,128)(2,1)}), bf16[8,16,2176]{2,1,0:T(8,128)(2,1)S(1)}, u32[]{:S(2)}, u32[]{:S(2)}) async-start(bf16[8,16,2176]{2,1,0:T(8,128)(2,1)} %map_rest.1), calls=%async_computation | async-start | bytes 1114112 | tf_op jit(solution)/shard_map/all_to_all | solution.py:303
  23.3 8.7 %collective-permute-start.6 = (bf16[4,8,1920]{2,1,0:T(8,128)(2,1)S(1)}, bf16[4,8,1920]{2,1,0:T(8,128)(2,1)S(1)}, u32[]{:S(2)}, u32[]{:S(2)}) collective-permute-start(bf16[4,8,1920]{2,1,0:T(8,128)(2,1)S(1)} %pad_maximum_fusion.2), channel_id=1, source_target_pairs={{0,2},{2,0},{4,6},{6,4},{8,10},{10,8},{12,14},{14,12},{1,3},{3,1},... | collective-permute-start | bytes 368648 | tf_op jit(solution)/shard_map/ppermute | solution.py:229
  25.4 6.7 %collective-permute-start.2 = (bf16[64,2048]{1,0:T(8,128)(2,1)S(1)}, bf16[64,2048]{1,0:T(8,128)(2,1)S(1)}, u32[]{:S(2)}, u32[]{:S(2)}) collective-permute-start(bf16[64,2048]{1,0:T(8,128)(2,1)S(1)} %constant_dynamic-slice_fusion.1), channel_id=1, source_target_pairs={{0,1},{1,0},{2,3},{3,2},{4,5},{5,4},{6,7},{7,6},{8,9},{9,8},{10,11... | collective-permute-start | bytes 786440 | tf_op jit(solution)/shard_map/ppermute | solution.py:15
  32.0 10.6 %collective-permute-start.7 = (bf16[8,8,1920]{2,1,0:T(8,128)(2,1)S(1)}, bf16[8,8,1920]{2,1,0:T(8,128)(2,1)S(1)}, u32[]{:S(2)}, u32[]{:S(2)}) collective-permute-start(bf16[8,8,1920]{2,1,0:T(8,128)(2,1)S(1)} %pad_maximum_fusion.1.own_ref), channel_id=1, source_target_pairs={{0,1},{1,0},{2,3},{3,2},{4,5},{5,4},{6,7},{7,6},{8,9},{9,8},{10,11... | collective-permute-start | bytes 737288 | tf_op jit(solution)/shard_map/ppermute | solution.py:15
  38.5 10.9 %collective-permute-start.3 = (bf16[64,2048]{1,0:T(8,128)(2,1)S(1)}, bf16[64,2048]{1,0:T(8,128)(2,1)S(1)}, u32[]{:S(2)}, u32[]{:S(2)}) collective-permute-start(bf16[64,2048]{1,0:T(8,128)(2,1)S(1)} %constant_dynamic-slice_fusion), channel_id=1, source_target_pairs={{0,1},{1,0},{2,3},{3,2},{4,5},{5,4},{6,7},{7,6},{8,9},{9,8},{10,11... | collective-permute-start | bytes 786440 | tf_op jit(solution)/shard_map/ppermute | solution.py:15
  38.6 10.8 %all-to-all-start.1 = ((f32[16,8,128]{2,1,0:T(8,128)}), f32[16,8,128]{2,1,0:T(8,128)S(1)}, u32[]{:S(2)}, u32[]{:S(2)}) async-start(f32[16,8,128]{2,1,0:T(8,128)} %get-tuple-element.11), calls=%async_computation.1 | async-start | bytes 131072 | tf_op jit(solution)/shard_map/all_to_all | solution.py:345

commit v5 on v4

--- a/solution.py
+++ b/solution.py
@@ -15,12 +15,18 @@
     return lax.ppermute(x, "tv", [(0, 1), (1, 0)])
 
 
-def block_weights(row_of, weight, rows):
-    row_ids = lax.broadcasted_iota(jnp.int32, (rows + MASS_ROWS, row_of.shape[1]), 0)
+def block_weights(place_ref, owner_ref, local_ref, weight_ref, which, rows, mine):
+    count = owner_ref.shape[1] // 2
+    halved = lambda x: jnp.where(which == 0, x[:, :count], x[:, count:])
+    local = local_ref[...] - place_ref[1] * mine
+    inside = (local >= 0) & (local < mine)
+    row_of = halved(jnp.where(inside, owner_ref[...] * mine + local, -1))
+    weight = halved(weight_ref[...].astype(jnp.float32))
+    row_ids = lax.broadcasted_iota(jnp.int32, (rows + MASS_ROWS, count), 0)
     total = jnp.zeros(row_ids.shape, jnp.float32)
     for slot in range(row_of.shape[0]):
-        hit = (row_ids == row_of[slot][None, :]) | (row_ids == rows + slot)
-        total = total + jnp.where(hit, weight[slot].astype(jnp.float32)[None, :], 0.0)
+        hit = (row_ids == row_of[slot : slot + 1]) | (row_ids == rows + slot)
+        total = total + jnp.where(hit, weight[slot : slot + 1], 0.0)
     return total.astype(jnp.bfloat16)
 
 
@@ -116,19 +122,51 @@
     lax.fori_loop(0, owners, left, 0)
 
 
-def stats_kernel(logits_ref, o_ref):
+def prepare_kernel(
+    place_ref, owner_ref, local_ref, weight_ref, logits_ref, t_ref, stats_ref, own_ref, rest_ref, held_ref, l_buf, sems
+):
     half_tokens, columns = logits_ref.shape
+    rows = own_ref.shape[0] - MASS_ROWS
+    mine = columns // BLK // 2
+    cuts = sems.shape[0] // 2
+    wide, deep = columns // cuts, t_ref.shape[1] // cuts
+    for_stats = [
+        pltpu.make_async_copy(
+            logits_ref.at[:, pl.ds(i * wide, wide)], l_buf.at[:, pl.ds(i * wide, wide)], sems.at[i]
+        )
+        for i in range(cuts)
+    ]
+    for_mapping = [
+        pltpu.make_async_copy(
+            t_ref.at[:, pl.ds(i * deep, deep)], held_ref.at[:, pl.ds(i * deep, deep)], sems.at[cuts + i]
+        )
+        for i in range(cuts)
+    ]
+    for copy in for_stats + for_mapping:
+        copy.start()
+    own_ref[...] = block_weights(place_ref, owner_ref, local_ref, weight_ref, place_ref[1], rows, mine)
+    rest_ref[...] = block_weights(place_ref, owner_ref, local_ref, weight_ref, 1 - place_ref[1], rows, mine)
+    for copy in for_stats:
+        copy.wait()
     for i in range(0, half_tokens, 64):
-        rows = slice(i, i + 64)
-        peak = logits_ref[rows, :BLK].astype(jnp.float32)
+        some = slice(i, i + 64)
+        peak = l_buf[some, :BLK].astype(jnp.float32)
         for b in range(1, columns // BLK):
-            peak = jnp.maximum(peak, logits_ref[rows, b * BLK : (b + 1) * BLK].astype(jnp.float32))
+            peak = jnp.maximum(peak, l_buf[some, b * BLK : (b + 1) * BLK].astype(jnp.float32))
         peak = jnp.broadcast_to(jnp.max(peak, axis=1, keepdims=True), peak.shape)
         total = jnp.zeros_like(peak)
         for b in range(columns // BLK):
-            total = total + jnp.exp(logits_ref[rows, b * BLK : (b + 1) * BLK].astype(jnp.float32) - peak)
-        o_ref[0:1, rows] = peak.T[0:1]
-        o_ref[1:2, rows] = jnp.sum(total.T, axis=0, keepdims=True)
+            total = total + jnp.exp(l_buf[some, b * BLK : (b + 1) * BLK].astype(jnp.float32) - peak)
+        stats_ref[0:1, some] = peak.T[0:1]
+        stats_ref[1:2, some] = jnp.sum(total.T, axis=0, keepdims=True)
+    for copy in for_mapping:
+        copy.wait()
+
+
+def later_kernel(place_ref, sent_ref, hidden_ref, logits_ref, h_ref, give_ref):
+    width = give_ref.shape[1]
+    h_ref[...] = hidden_ref[...]
+    give_ref[...] = jnp.where(place_ref[1] == 0, logits_ref[:, width:], logits_ref[:, :width])
 
 
 def grad_kernel(scale, target_ref, logits_ref, grad_ref, part_ref):
@@ -160,22 +198,28 @@
             part_ref[q, :, rows] = jnp.broadcast_to(row, (part_ref.shape[1], BLK))
 
 
-def hidden_kernel(place_ref, own_ref, other_ref, o_ref, s_ref):
-    owners, held, features = own_ref.shape
-    for i in range(owners):
-        offset = sum(((i >> j) & 1) * (owners >> (j + 1)) for j in range(owners.bit_length() - 1))
-        first = (place_ref[0] ^ offset) * 2
-        own = pl.ds(pl.multiple_of((first + place_ref[1]) * held, held), held)
-        other = pl.ds(pl.multiple_of((first + 1 - place_ref[1]) * held, held), held)
-        s_ref[own, :] = own_ref[i].astype(jnp.float32)
-        s_ref[other, :] = other_ref[i].astype(jnp.float32)
+def hidden_kernel(place_ref, *refs):
+    pieces, (o_ref, s_ref) = refs[:-2], refs[-2:]
+    count = len(pieces) // 2
+    _, held, features = pieces[0].shape
+    owners = s_ref.shape[0] // (2 * held)
+    i = 0
+    for own_ref, other_ref in zip(pieces[:count], pieces[count:]):
+        for j in range(own_ref.shape[0]):
+            offset = sum(((i >> bit) & 1) * (owners >> (bit + 1)) for bit in range(owners.bit_length() - 1))
+            first = (place_ref[0] ^ offset) * 2
+            own = pl.ds(pl.multiple_of((first + place_ref[1]) * held, held), held)
+            other = pl.ds(pl.multiple_of((first + 1 - place_ref[1]) * held, held), held)
+            s_ref[own, :] = own_ref[j].astype(jnp.float32)
+            s_ref[other, :] = other_ref[j].astype(jnp.float32)
+            i += 1
     for i in range(s_ref.shape[0] // BLK):
         for j in range(features // BLK):
             tile = s_ref[i * BLK : (i + 1) * BLK, j * BLK : (j + 1) * BLK].T
             o_ref[j * BLK : (j + 1) * BLK, i * BLK : (i + 1) * BLK] = tile.astype(jnp.bfloat16)
 
 
-def finish_kernel(place_ref, grad_ref, got_ref, terms_ref, o_ref, d_ref, sem):
+def join_kernel(place_ref, grad_ref, got_ref, o_ref, sem):
     half_tokens, width = got_ref.shape
     half = place_ref[1]
     kept_at = pl.ds(pl.multiple_of(half * width, width), width)
@@ -187,12 +231,16 @@
     ]
     for copy in copies:
         copy.start()
+    for copy in copies:
+        copy.wait()
+
+
+def sum_kernel(place_ref, terms_ref, joined_ref, d_ref):
+    half_tokens = d_ref.shape[1]
     total = terms_ref[0, 0:1, :]
     for q in range(1, terms_ref.shape[0]):
         total = total + terms_ref[q, 0:1, :]
-    d_ref[...] = jnp.where(half == 0, total[:, :half_tokens], total[:, half_tokens:])
-    for copy in copies:
-        copy.wait()
+    d_ref[...] = jnp.where(place_ref[1] == 0, total[:, :half_tokens], total[:, half_tokens:])
 
 
 def weight_kernel(hidden_ref, grad_ref, o_ref, block_ref, sem):
@@ -251,23 +299,24 @@
 
     teacher_other = swap_halves(teacher_probs)
 
-    stats = pl.pallas_call(
-        stats_kernel,
-        out_shape=jax.ShapeDtypeStruct((2, half_tokens), jnp.float32),
-        in_specs=[whole()],
-        out_specs=whole(),
+    weights = jax.ShapeDtypeStruct((rows + MASS_ROWS, per_half), jnp.bfloat16)
+    cuts = 4
+    stats, w_own, w_rest, teacher_own = pl.pallas_call(
+        prepare_kernel,
+        out_shape=(
+            jax.ShapeDtypeStruct((2, half_tokens), jnp.float32),
+            weights,
+            weights,
+            jax.ShapeDtypeStruct(teacher_probs.shape, jnp.bfloat16),
+        ),
+        in_specs=[scalars()] + [whole()] * 3 + [anywhere()] * 2,
+        out_specs=[whole()] * 4,
+        scratch_shapes=[pltpu.VMEM(student_logits.shape, jnp.bfloat16), pltpu.SemaphoreType.DMA((2 * cuts,))],
         compiler_params=params(),
         cost_estimate=pl.CostEstimate(flops=0, bytes_accessed=0, transcendentals=0),
-        name="stats",
-    )(student_logits)
+        name="prepare",
+    )(place, align_owner.T, align_local.T, align_weight.T, student_logits, teacher_probs)
     stats = in_order(stats, swap_halves(stats), 1)
-
-    local = align_local.T - half_index * mine
-    row_of = jnp.where((local >= 0) & (local < mine), align_owner.T * mine + local, -1)
-    weight = align_weight.T
-    cut = lambda x, which: lax.dynamic_slice_in_dim(x, which * per_half, per_half, 1)
-    w_own = block_weights(cut(row_of, half_index), cut(weight, half_index), rows)
-    w_rest = block_weights(cut(row_of, 1 - half_index), cut(weight, 1 - half_index), rows)
     spread = pltpu.VMEM((per_half * tokens, BLK), jnp.float32)
     part = pl.pallas_call(
         map_own_kernel,
@@ -278,9 +327,8 @@
         compiler_params=params(),
         cost_estimate=pl.CostEstimate(flops=0, bytes_accessed=0, transcendentals=0),
         name="map_own",
-    )(w_own, teacher_probs)
+    )(w_own, teacher_own)
     chunk = (owners, tokens, width + group_tokens)
-    cuts = 4
     outgoing = pl.pallas_call(
         map_rest_kernel,
         out_shape=jax.ShapeDtypeStruct(chunk, jnp.bfloat16),
@@ -302,27 +350,37 @@
     )(w_rest, teacher_other, part, stats)
     target = lax.all_to_all(outgoing, "sv", 0, 0, tiled=True)
 
-    hidden, late_logits, outgoing = lax.optimization_barrier((hidden, student_logits, outgoing))
-
-    keep = lax.dynamic_slice_in_dim(late_logits, half_index * width, width, 1)
-    give = lax.dynamic_slice_in_dim(late_logits, (1 - half_index) * width, width, 1)
+    hidden, give = pl.pallas_call(
+        later_kernel,
+        out_shape=(
+            jax.ShapeDtypeStruct(hidden.shape, jnp.bfloat16),
+            jax.ShapeDtypeStruct((half_tokens, width), jnp.bfloat16),
+        ),
+        in_specs=[scalars(), anywhere(), whole(), whole()],
+        out_specs=(whole(), whole()),
+        compiler_params=params(),
+        cost_estimate=pl.CostEstimate(flops=0, bytes_accessed=48 << 20, transcendentals=0),
+        name="later",
+    )(place, outgoing, hidden, student_logits)
+
+    keep = lax.dynamic_slice_in_dim(student_logits, half_index * width, width, 1)
     logits = in_order(keep, swap_halves(give), 0)
 
-    hidden_own = hidden[None]
+    pieces = [hidden[None]]
     offset = owners // 2
     while offset:
-        hidden_own = jnp.concatenate([hidden_own, to_partner(hidden_own, offset)])
+        pieces.append(to_partner(jnp.concatenate(pieces), offset))
         offset //= 2
     hidden_t = pl.pallas_call(
         hidden_kernel,
         out_shape=jax.ShapeDtypeStruct((features, group_tokens), jnp.bfloat16),
-        in_specs=[scalars(), whole(), whole()],
+        in_specs=[scalars()] + [whole()] * (2 * len(pieces)),
         out_specs=whole(),
         scratch_shapes=[pltpu.VMEM((group_tokens, features), jnp.float32)],
         compiler_params=params(),
         cost_estimate=pl.CostEstimate(flops=0, bytes_accessed=4 * features * group_tokens, transcendentals=0),
         name="hidden_t",
-    )(place, hidden_own, swap_halves(hidden_own))
+    )(place, *pieces, *[swap_halves(piece) for piece in pieces])
 
     scale = float(columns * owners)
     grad, terms = pl.pallas_call(
@@ -365,19 +423,25 @@
         name="weight_grad",
     )(hidden_t, grad)
 
-    logit_grad, divergence = pl.pallas_call(
-        finish_kernel,
-        out_shape=(
-            jax.ShapeDtypeStruct((half_tokens, columns), jnp.bfloat16),
-            jax.ShapeDtypeStruct((1, half_tokens), jnp.float32),
-        ),
-        in_specs=[scalars(), anywhere(), anywhere(), whole()],
-        out_specs=(anywhere(), whole()),
+    logit_grad = pl.pallas_call(
+        join_kernel,
+        out_shape=jax.ShapeDtypeStruct((half_tokens, columns), jnp.bfloat16),
+        in_specs=[scalars(), anywhere(), anywhere()],
+        out_specs=anywhere(),
         scratch_shapes=[pltpu.SemaphoreType.DMA((2,))],
         compiler_params=params(),
         cost_estimate=pl.CostEstimate(flops=0, bytes_accessed=4 * half_tokens * columns, transcendentals=0),
-        name="finish",
-    )(place, grad, got, terms)
+        name="join",
+    )(place, grad, got)
+    divergence = pl.pallas_call(
+        sum_kernel,
+        out_shape=jax.ShapeDtypeStruct((1, half_tokens), jnp.float32),
+        in_specs=[scalars(), whole(), anywhere()],
+        out_specs=whole(),
+        compiler_params=params(),
+        cost_estimate=pl.CostEstimate(flops=0, bytes_accessed=0, transcendentals=0),
+        name="divergence",
+    )(place, terms, logit_grad)
     return (divergence.reshape(half_tokens), logit_grad, weight_grad)
 
 

time: 51.7 us -> 55.1 us (1.066)
  Pallas kernels: 12.2 us -> 14.6 us
  local copies, waits for them, and re-layouts: 3.33 us -> 5.48 us
  waiting for transfers between devices: 15.7 us -> 14.6 us
  other arithmetic: 1.33 us -> 0.33 us
  starting transfers between devices: 17.9 us -> 18.8 us
    all_to_all x1, waiting for transfers between devices: 4.96 us -> 11.7 us  [body(): target = lax.all_to_all(outgoing, 'sv', 0, 0, tiled=True)]
    ppermute x3, waiting for transfers between devices: 8.41 us -> 1.88 us  [to_partner(): lax.ppermute(x, 'sv', [(s, s ^ offset) for s in range(lax.axis_size('sv'))])]
    unnamed x8 -> x16, local copies, waits for them, and re-layouts: 2.36 us -> 5.47 us
    pallas_call x2 -> x4, Pallas kernels: 2.25 us -> 4.65 us  [the longest x1 1.59 us: body(): pl.pallas_call(prepare_kernel, out_shape=(jax.ShapeDtypeStruct((2, half_t...]
    all_to_all x1, waiting for transfers between devices: 2.36 us -> 1.02 us  [body(): terms = lax.all_to_all(terms, ('sv', 'tv'), 0, 0, tiled=True)]
    ppermute x5 -> x8, starting transfers between devices: 0.81 us -> 1.8 us  [swap_halves(): return lax.ppermute(x, 'tv', [(0, 1), (1, 0)])]
    dynamic_slice x3 -> x0, local copies, waits for them, and re-layouts: 0.93 us -> none  [the longest x2 0.91 us: body(): lax.dynamic_slice_in_dim(x, which * per_half, per_half, 1)]
    select_n x1 -> x0, other arithmetic: 0.71 us -> none  [body(): jnp.where((local >= 0) & (local < mine), align_owner.T * mine + local, -1)]
  transfers between devices with their start and end apart: 10 -> 13, of which waited for: 4 -> 3; matrix products, arithmetic and copies ran while one was open for 4% -> 1% of each run, Pallas kernels for 14% -> 18%
where the time goes in v5:
time: 55.1 us; the launch traced here: 54.6 us
  starting transfers between devices  18.8 us (34%)
  Pallas kernels  14.6 us (26%)
  waiting for transfers between devices  14.6 us (26%)
  local copies, waits for them, and re-layouts  5.48 us (10%)
  between operations  0.84 us (2%)
    all_to_all x1, waiting for transfers between devices, body(): target = lax.all_to_all(outgoing, 'sv', 0, 0, tiled=True)  11.7 us
    ppermute x3, starting transfers between devices, to_partner(): lax.ppermute(x, 'sv', [(s, s ^ offset) for s in range(lax.axis_size('sv'))])  8.15 us
    unnamed x16, local copies, waits for them, and re-layouts  5.47 us
    all_to_all x1, starting transfers between devices, body(): target = lax.all_to_all(outgoing, 'sv', 0, 0, tiled=True)  5.04 us
    all_to_all x1, starting transfers between devices, body(): terms = lax.all_to_all(terms, ('sv', 'tv'), 0, 0, tiled=True)  3.83 us
    pallas_call x1, Pallas kernels, body(): pl.pallas_call(weight_kernel, out_shape=jax.ShapeDtypeStruct((features, w...  3.63 us
    pallas_call x1, Pallas kernels, body(): pl.pallas_call(map_rest_kernel, out_shape=jax.ShapeDtypeStruct(chunk, jnp...  2.85 us
    ppermute x3, waiting for transfers between devices, to_partner(): lax.ppermute(x, 'sv', [(s, s ^ offset) for s in range(lax.axis_size('sv'))])  1.88 us
  transfers between devices with their start and end apart: 13, of which 3 were waited for; matrix products, arithmetic and copies ran while one was open for 1% of the time, Pallas kernels for 18%

profile of v5, /device:TPU:0, one launch (start us, length us, event | category | flops | bytes accessed | tf_op | source)
XLA Modules:
  0.0 54.6 jit_solution(18000370816512254158)
XLA Ops:
  0.6 0.5 collective-permute-start
  1.2 1.0 %copy-done = bf16[64,4096]{1,0:T(8,128)(2,1)S(1)} copy-done((bf16[64,4096]{1,0:T(8,128)(2,1)S(1)}, bf16[64,4096]{1,0:T(8,128)(2,1)}, u32[]{:S(2)}) %copy-start) | copy-done | bytes 524312
  2.3 1.3 %copy-done.3 = bf16[16,40960]{1,0:T(8,128)(2,1)S(1)} copy-done((bf16[16,40960]{1,0:T(8,128)(2,1)S(1)}, bf16[16,40960]{1,0:T(8,128)(2,1)}, u32[]{:S(2)}) %copy-start.3) | copy-done | bytes 1310744
  3.6 0.7 %copy-done.5 = s32[640,2]{0,1:T(2,128)S(1)} copy-done((s32[640,2]{0,1:T(2,128)S(1)}, s32[640,2]{0,1:T(2,128)}, u32[]{:S(2)}) %copy-start.5) | copy-done | bytes 5144
  4.3 0.7 %copy-done.6 = s32[640,2]{0,1:T(2,128)S(1)} copy-done((s32[640,2]{0,1:T(2,128)S(1)}, s32[640,2]{0,1:T(2,128)}, u32[]{:S(2)}) %copy-start.6) | copy-done | bytes 5144
  5.0 0.7 %copy-done.7 = bf16[640,2]{0,1:T(2,128)(2,1)S(1)} copy-done((bf16[640,2]{0,1:T(2,128)(2,1)S(1)}, bf16[640,2]{0,1:T(2,128)(2,1)}, u32[]{:S(2)}) %copy-start.7) | copy-done | bytes 2584
  5.6 1.6 %prepare.1 = (f32[2,64]{1,0:T(2,128)S(1)}, bf16[144,320]{1,0:T(8,128)(2,1)S(1)}, bf16[144,320]{1,0:T(8,128)(2,1)S(1)}, bf16[16,40960]{1,0:T(8,128)(2,1)S(1)}) custom-call(s32[2]{0:T(128)S(1)} %pad_add_fusion.place_ref, s32[2,640]{1,0:T(2,128)S(1)} %bitcast.12, s32[2,640]{1,0:T(2,128)S(1)} %bitcast.13, bf16[2,640]{1,0:T(2,128)(2,1)S(1)} %bitcast.14, ...), custom_call_target="tpu_custom_call" | custom-call | tf_op jit(solution)/shard_map/prepare/pallas_call | solution.py:304
  7.4 1.4 %map_own.1.p_ref = f32[144,2048]{1,0:T(8,128)S(1)} custom-call(bf16[144,320]{1,0:T(8,128)(2,1)S(1)} %get-tuple-element.12.w_ref, bf16[16,40960]{1,0:T(8,128)(2,1)S(1)} %get-tuple-element.13.t_ref), custom_call_target="tpu_custom_call" | custom-call | tf_op jit(solution)/shard_map/map_own/pallas_call | solution.py:321
  8.9 2.8 %map_rest.1.sent_ref = bf16[8,16,2176]{2,1,0:T(8,128)(2,1)} custom-call(bf16[144,320]{1,0:T(8,128)(2,1)S(1)} %get-tuple-element.11.w_ref, bf16[16,40960]{1,0:T(8,128)(2,1)S(1)} %collective-permute-done.t_ref, f32[144,2048]{1,0:T(8,128)S(1)} %map_own.1.p_ref, f32[2,128]{1,0:T(2,128)S(1)} %pad_maximum_fusion.3.stats_ref), custom_call_target="tpu_custom_call" | custom-call | flops 188743680 | bytes 4194304 | tf_op jit(solution)/shard_map/map_rest/pallas_call | solution.py:332
  11.7 0.6 %later.1 = (bf16[8,1920]{1,0:T(8,128)(2,1)S(1)}, bf16[64,2048]{1,0:T(8,128)(2,1)S(1)}) custom-call(s32[2]{0:T(128)S(1)} %pad_add_fusion.place_ref, bf16[8,16,2176]{2,1,0:T(8,128)(2,1)} %map_rest.1.sent_ref, bf16[8,1920]{1,0:T(8,128)(2,1)S(1)} %copy-done.4, bf16[64,4096]{1,0:T(8,128)(2,1)S(1)} %copy-done.1), custom_call_target="tpu_custom_call" | custom-call | bytes 50331648 | tf_op jit(solution)/shard_map/later/pallas_call | solution.py:353
  12.3 4.1 %collective-permute-start.4 = (bf16[1,8,1920]{2,1,0:T(8,128)(2,1)S(1)}, bf16[1,8,1920]{2,1,0:T(8,128)(2,1)S(1)}, u32[]{:S(2)}, u32[]{:S(2)}) collective-permute-start(bf16[1,8,1920]{2,1,0:T(8,128)(2,1)S(1)} %bitcast.7), channel_id=1, source_target_pairs={{0,8},{2,10},{4,12},{6,14},{8,0},{10,2},{12,4},{14,6},{1,9},{3,11}... | collective-permute-start | bytes 92168 | tf_op jit(solution)/shard_map/ppermute | solution.py:277
  16.4 1.9 %collective-permute-done.4.refs_1_ = bf16[1,8,1920]{2,1,0:T(8,128)(2,1)S(1)} collective-permute-done((bf16[1,8,1920]{2,1,0:T(8,128)(2,1)S(1)}, bf16[1,8,1920]{2,1,0:T(8,128)(2,1)S(1)}, u32[]{:S(2)}, u32[]{:S(2)}) %collective-permute-start.4) | collective-permute-done | bytes 30752 | tf_op jit(solution)/shard_map/ppermute | solution.py:277
  18.3 2.0 %collective-permute-start.5 = (bf16[2,8,1920]{2,1,0:T(8,128)(2,1)S(1)}, bf16[2,8,1920]{2,1,0:T(8,128)(2,1)S(1)}, u32[]{:S(2)}, u32[]{:S(2)}) collective-permute-start(bf16[2,8,1920]{2,1,0:T(8,128)(2,1)S(1)} %pad_maximum_fusion.2), channel_id=1, source_target_pairs={{0,4},{2,6},{4,0},{6,2},{8,12},{10,14},{12,8},{14,10},{1,5},{3,7},... | collective-permute-start | bytes 184328 | tf_op jit(solution)/shard_map/ppermute | solution.py:277
  20.3 5.0 %all-to-all-start = ((bf16[8,16,2176]{2,1,0:T(8,128)(2,1)}), bf16[8,16,2176]{2,1,0:T(8,128)(2,1)S(1)}, u32[]{:S(2)}, u32[]{:S(2)}) async-start(bf16[8,16,2176]{2,1,0:T(8,128)(2,1)} %map_rest.1.sent_ref), calls=%async_computation | async-start | bytes 1114112 | tf_op jit(solution)/shard_map/all_to_all | solution.py:351
  25.4 2.1 %collective-permute-start.6 = (bf16[4,8,1920]{2,1,0:T(8,128)(2,1)S(1)}, bf16[4,8,1920]{2,1,0:T(8,128)(2,1)S(1)}, u32[]{:S(2)}, u32[]{:S(2)}) collective-permute-start(bf16[4,8,1920]{2,1,0:T(8,128)(2,1)S(1)} %pad_maximum_fusion.1), channel_id=1, source_target_pairs={{0,2},{2,0},{4,6},{6,4},{8,10},{10,8},{12,14},{14,12},{1,3},{3,1},... | collective-permute-start | bytes 368648 | tf_op jit(solution)/shard_map/ppermute | solution.py:277
  27.6 11.7 %all-to-all-done.refs_0_ = bf16[8,16,2176]{2,1,0:T(8,128)(2,1)S(1)} async-done(((bf16[8,16,2176]{2,1,0:T(8,128)(2,1)}), bf16[8,16,2176]{2,1,0:T(8,128)(2,1)S(1)}, u32[]{:S(2)}, u32[]{:S(2)}) %all-to-all-start) | async-done | bytes 557088 | tf_op jit(solution)/shard_map/all_to_all | solution.py:351
  39.3 1.2 %logit_grad.1 = (bf16[128,2048]{1,0:T(8,128)(2,1)S(1)}, f32[16,8,128]{2,1,0:T(8,128)}) custom-call(bf16[8,16,2176]{2,1,0:T(8,128)(2,1)S(1)} %all-to-all-done.refs_0_, bf16[128,2048]{1,0:T(8,128)(2,1)S(1)} %pad_maximum_fusion.refs_1_), custom_call_target="tpu_custom_call" | custom-call | flops 2621440 | bytes 1572864 | tf_op jit(solution)/shard_map/logit_grad/pallas_call | solution.py:386
  41.7 3.8 %all-to-all-start.1 = ((f32[16,8,128]{2,1,0:T(8,128)}), f32[16,8,128]{2,1,0:T(8,128)S(1)}, u32[]{:S(2)}, u32[]{:S(2)}) async-start(f32[16,8,128]{2,1,0:T(8,128)} %get-tuple-element.16), calls=%async_computation.1 | async-start | bytes 131072 | tf_op jit(solution)/shard_map/all_to_all | solution.py:403
  45.6 0.8 %hidden_t.1.hidden_ref = bf16[1920,128]{1,0:T(8,128)(2,1)S(1)} custom-call(s32[2]{0:T(128)S(1)} %pad_add_fusion.place_ref, bf16[1,8,1920]{2,1,0:T(8,128)(2,1)S(1)} %bitcast.11, bf16[1,8,1920]{2,1,0:T(8,128)(2,1)S(1)} %collective-permute-done.4.refs_1_, bf16[2,8,1920]{2,1,0:T(8,128)(2,1)S(1)} %collective-permute-done.5.refs_2_, ...), custom_call_target="tpu_custom_call" | custom-call | bytes 983040 | tf_op jit(solution)/shard_map/hidden_t/pallas_call | solution.py:374
  46.4 3.6 %weight_grad.1 = bf16[1920,2048]{1,0:T(8,128)(2,1)} custom-call(bf16[1920,128]{1,0:T(8,128)(2,1)S(1)} %hidden_t.1.hidden_ref, bf16[128,2048]{1,0:T(8,128)(2,1)S(1)} %get-tuple-element.17.grad_ref), custom_call_target="tpu_custom_call" | custom-call | flops 1006632960 | bytes 8880128 | tf_op jit(solution)/shard_map/weight_grad/pallas_call | solution.py:408
  50.1 1.4 %join.1.joined_ref = bf16[64,4096]{1,0:T(8,128)(2,1)} custom-call(s32[2]{0:T(128)S(1)} %pad_add_fusion.place_ref, bf16[128,2048]{1,0:T(8,128)(2,1)S(1)} %get-tuple-element.17.grad_ref, bf16[64,2048]{1,0:T(8,128)(2,1)S(1)} %collective-permute-done.3.got_ref), custom_call_target="tpu_custom_call" | custom-call | bytes 1048576 | tf_op jit(solution)/shard_map/join/pallas_call | solution.py:426
  51.4 1.0 %all-to-all-done.1.terms_ref = f32[16,8,128]{2,1,0:T(8,128)S(1)} async-done(((f32[16,8,128]{2,1,0:T(8,128)}), f32[16,8,128]{2,1,0:T(8,128)S(1)}, u32[]{:S(2)}, u32[]{:S(2)}) %all-to-all-start.1) | async-done | bytes 65568 | tf_op jit(solution)/shard_map/all_to_all | solution.py:403
  52.5 1.0 %copy-done.2 = bf16[64,4096]{1,0:T(8,128)(2,1)S(1)} copy-done((bf16[64,4096]{1,0:T(8,128)(2,1)S(1)}, bf16[64,4096]{1,0:T(8,128)(2,1)}, u32[]{:S(2)}) %copy-start.2) | copy-done | bytes 524312
  53.5 1.1 %divergence.1 = f32[1,64]{1,0:T(1,128)} custom-call(s32[2]{0:T(128)S(1)} %pad_add_fusion.place_ref, f32[16,8,128]{2,1,0:T(8,128)S(1)} %all-to-all-done.1.terms_ref, bf16[64,4096]{1,0:T(8,128)(2,1)S(1)} %copy-done.2), custom_call_target="tpu_custom_call" | custom-call | tf_op jit(solution)/shard_map/divergence/pallas_call | solution.py:436
  (35 shorter events, 1.7 us)
Async XLA Ops:
  0.6 8.2 %collective-permute-start = (bf16[16,40960]{1,0:T(8,128)(2,1)}, bf16[16,40960]{1,0:T(8,128)(2,1)S(1)}, u32[]{:S(2)}, u32[]{:S(2)}) collective-permute-start(bf16[16,40960]{1,0:T(8,128)(2,1)} %t_ref.1), channel_id=1, source_target_pairs={{0,1},{1,0},{2,3},{3,2},{4,5},{5,4},{6,7},{7,6},{8,9},{9,8},{10,11... | collective-permute-start | bytes 3932168 | tf_op jit(solution)/shard_map/ppermute | solution.py:15
  1.2 1.0 %copy-start = (bf16[64,4096]{1,0:T(8,128)(2,1)S(1)}, bf16[64,4096]{1,0:T(8,128)(2,1)}, u32[]{:S(2)}) copy-start(bf16[64,4096]{1,0:T(8,128)(2,1)} %logits_ref.3) | copy-start | bytes 1572868
  2.3 1.3 %copy-start.3 = (bf16[16,40960]{1,0:T(8,128)(2,1)S(1)}, bf16[16,40960]{1,0:T(8,128)(2,1)}, u32[]{:S(2)}) copy-start(bf16[16,40960]{1,0:T(8,128)(2,1)} %t_ref.1) | copy-start | bytes 3932164
  3.6 0.7 %copy-start.5 = (s32[640,2]{0,1:T(2,128)S(1)}, s32[640,2]{0,1:T(2,128)}, u32[]{:S(2)}) copy-start(s32[640,2]{0,1:T(2,128)} %param.7) | copy-start | bytes 15364
  4.3 0.7 %copy-start.6 = (s32[640,2]{0,1:T(2,128)S(1)}, s32[640,2]{0,1:T(2,128)}, u32[]{:S(2)}) copy-start(s32[640,2]{0,1:T(2,128)} %param.8) | copy-start | bytes 15364
  5.0 0.7 %copy-start.7 = (bf16[640,2]{0,1:T(2,128)(2,1)S(1)}, bf16[640,2]{0,1:T(2,128)(2,1)}, u32[]{:S(2)}) copy-start(bf16[640,2]{0,1:T(2,128)(2,1)} %param.9) | copy-start | bytes 7684
  7.2 1.5 %collective-permute-start.1 = (f32[2,64]{1,0:T(2,128)S(1)}, f32[2,64]{1,0:T(2,128)S(1)}, u32[]{:S(2)}, u32[]{:S(2)}) collective-permute-start(f32[2,64]{1,0:T(2,128)S(1)} %get-tuple-element.14), channel_id=1, source_target_pairs={{0,1},{1,0},{2,3},{3,2},{4,5},{5,4},{6,7},{7,6},{8,9},{9,8},{10,11... | collective-permute-start | bytes 1544 | tf_op jit(solution)/shard_map/ppermute | solution.py:15
  8.9 2.9 %copy-start.1 = (bf16[64,4096]{1,0:T(8,128)(2,1)S(1)}, bf16[64,4096]{1,0:T(8,128)(2,1)}, u32[]{:S(2)}) copy-start(bf16[64,4096]{1,0:T(8,128)(2,1)} %logits_ref.3) | copy-start | bytes 1572868
  8.9 2.9 %copy-start.4 = (bf16[8,1920]{1,0:T(8,128)(2,1)S(1)}, bf16[8,1920]{1,0:T(8,128)(2,1)}, u32[]{:S(2)}) copy-start(bf16[8,1920]{1,0:T(8,128)(2,1)} %hidden_ref.1) | copy-start | bytes 92164
  12.3 6.0 %collective-permute-start.4 = (bf16[1,8,1920]{2,1,0:T(8,128)(2,1)S(1)}, bf16[1,8,1920]{2,1,0:T(8,128)(2,1)S(1)}, u32[]{:S(2)}, u32[]{:S(2)}) collective-permute-start(bf16[1,8,1920]{2,1,0:T(8,128)(2,1)S(1)} %bitcast.7), channel_id=1, source_target_pairs={{0,8},{2,10},{4,12},{6,14},{8,0},{10,2},{12,4},{14,6},{1,9},{3,11}... | collective-permute-start | bytes 92168 | tf_op jit(solution)/shard_map/ppermute | solution.py:277
  18.3 7.0 %collective-permute-start.5 = (bf16[2,8,1920]{2,1,0:T(8,128)(2,1)S(1)}, bf16[2,8,1920]{2,1,0:T(8,128)(2,1)S(1)}, u32[]{:S(2)}, u32[]{:S(2)}) collective-permute-start(bf16[2,8,1920]{2,1,0:T(8,128)(2,1)S(1)} %pad_maximum_fusion.2), channel_id=1, source_target_pairs={{0,4},{2,6},{4,0},{6,2},{8,12},{10,14},{12,8},{14,10},{1,5},{3,7},... | collective-permute-start | bytes 184328 | tf_op jit(solution)/shard_map/ppermute | solution.py:277
  20.3 19.0 %all-to-all-start = ((bf16[8,16,2176]{2,1,0:T(8,128)(2,1)}), bf16[8,16,2176]{2,1,0:T(8,128)(2,1)S(1)}, u32[]{:S(2)}, u32[]{:S(2)}) async-start(bf16[8,16,2176]{2,1,0:T(8,128)(2,1)} %map_rest.1.sent_ref), calls=%async_computation | async-start | bytes 1114112 | tf_op jit(solution)/shard_map/all_to_all | solution.py:351
  25.3 2.1 %collective-permute-start.2 = (bf16[64,2048]{1,0:T(8,128)(2,1)S(1)}, bf16[64,2048]{1,0:T(8,128)(2,1)S(1)}, u32[]{:S(2)}, u32[]{:S(2)}) collective-permute-start(bf16[64,2048]{1,0:T(8,128)(2,1)S(1)} %get-tuple-element.15), channel_id=1, source_target_pairs={{0,1},{1,0},{2,3},{3,2},{4,5},{5,4},{6,7},{7,6},{8,9},{9,8},{10,11... | collective-permute-start | bytes 786440 | tf_op jit(solution)/shard_map/ppermute | solution.py:15
  25.4 15.2 %collective-permute-start.6 = (bf16[4,8,1920]{2,1,0:T(8,128)(2,1)S(1)}, bf16[4,8,1920]{2,1,0:T(8,128)(2,1)S(1)}, u32[]{:S(2)}, u32[]{:S(2)}) collective-permute-start(bf16[4,8,1920]{2,1,0:T(8,128)(2,1)S(1)} %pad_maximum_fusion.1), channel_id=1, source_target_pairs={{0,2},{2,0},{4,6},{6,4},{8,10},{10,8},{12,14},{14,12},{1,3},{3,1},... | collective-permute-start | bytes 368648 | tf_op jit(solution)/shard_map/ppermute | solution.py:277
  40.5 9.5 %collective-permute-start.3 = (bf16[64,2048]{1,0:T(8,128)(2,1)S(1)}, bf16[64,2048]{1,0:T(8,128)(2,1)S(1)}, u32[]{:S(2)}, u32[]{:S(2)}) collective-permute-start(bf16[64,2048]{1,0:T(8,128)(2,1)S(1)} %constant_dynamic-slice_fusion), channel_id=1, source_target_pairs={{0,1},{1,0},{2,3},{3,2},{4,5},{5,4},{6,7},{7,6},{8,9},{9,8},{10,11... | collective-permute-start | bytes 786440 | tf_op jit(solution)/shard_map/ppermute | solution.py:15
  40.6 5.0 %collective-permute-start.10 = (bf16[4,8,1920]{2,1,0:T(8,128)(2,1)S(1)}, bf16[4,8,1920]{2,1,0:T(8,128)(2,1)S(1)}, u32[]{:S(2)}, u32[]{:S(2)}) collective-permute-start(bf16[4,8,1920]{2,1,0:T(8,128)(2,1)S(1)} %collective-permute-done.6.refs_3_), channel_id=1, source_target_pairs={{0,1},{1,0},{2,3},{3,2},{4,5},{5,4},{6,7},{7,6},{8,9},{9,8},{10,11... | collective-permute-start | bytes 368648 | tf_op jit(solution)/shard_map/ppermute | solution.py:15
  41.1 4.5 %collective-permute-start.9 = (bf16[2,8,1920]{2,1,0:T(8,128)(2,1)S(1)}, bf16[2,8,1920]{2,1,0:T(8,128)(2,1)S(1)}, u32[]{:S(2)}, u32[]{:S(2)}) collective-permute-start(bf16[2,8,1920]{2,1,0:T(8,128)(2,1)S(1)} %collective-permute-done.5.refs_2_), channel_id=1, source_target_pairs={{0,1},{1,0},{2,3},{3,2},{4,5},{5,4},{6,7},{7,6},{8,9},{9,8},{10,11... | collective-permute-start | bytes 184328 | tf_op jit(solution)/shard_map/ppermute | solution.py:15
  41.2 4.4 %collective-permute-start.7 = (bf16[1,8,1920]{2,1,0:T(8,128)(2,1)S(1)}, bf16[1,8,1920]{2,1,0:T(8,128)(2,1)S(1)}, u32[]{:S(2)}, u32[]{:S(2)}) collective-permute-start(bf16[1,8,1920]{2,1,0:T(8,128)(2,1)S(1)} %bitcast.10), channel_id=1, source_target_pairs={{0,1},{1,0},{2,3},{3,2},{4,5},{5,4},{6,7},{7,6},{8,9},{9,8},{10,11... | collective-permute-start | bytes 92168 | tf_op jit(solution)/shard_map/ppermute | solution.py:15
  41.6 3.9 %collective-permute-start.8 = (bf16[1,8,1920]{2,1,0:T(8,128)(2,1)S(1)}, bf16[1,8,1920]{2,1,0:T(8,128)(2,1)S(1)}, u32[]{:S(2)}, u32[]{:S(2)}) collective-permute-start(bf16[1,8,1920]{2,1,0:T(8,128)(2,1)S(1)} %collective-permute-done.4.refs_1_), channel_id=1, source_target_pairs={{0,1},{1,0},{2,3},{3,2},{4,5},{5,4},{6,7},{7,6},{8,9},{9,8},{10,11... | collective-permute-start | bytes 92168 | tf_op jit(solution)/shard_map/ppermute | solution.py:15
  41.7 10.7 %all-to-all-start.1 = ((f32[16,8,128]{2,1,0:T(8,128)}), f32[16,8,128]{2,1,0:T(8,128)S(1)}, u32[]{:S(2)}, u32[]{:S(2)}) async-start(f32[16,8,128]{2,1,0:T(8,128)} %get-tuple-element.16), calls=%async_computation.1 | async-start | bytes 131072 | tf_op jit(solution)/shard_map/all_to_all | solution.py:403
  52.5 1.0 %copy-start.2 = (bf16[64,4096]{1,0:T(8,128)(2,1)S(1)}, bf16[64,4096]{1,0:T(8,128)(2,1)}, u32[]{:S(2)}) copy-start(bf16[64,4096]{1,0:T(8,128)(2,1)} %join.1.joined_ref) | copy-start | bytes 1572868

commit v6 on v4

--- a/solution.py
+++ b/solution.py
@@ -7,6 +7,7 @@
 
 BLK = 128
 TB = 640
+TOPA = 2
 MASS_ROWS = 16
 VMEM_LIMIT = 48 * 1024 * 1024
 
@@ -92,7 +93,7 @@
         for i in range(2):
             m_ref[pl.ds(t + i, rows + 8, stride=tokens), :] = both[: rows + 8, i * BLK : (i + 1) * BLK]
     mass = m_ref[rows * tokens : (rows + 1) * tokens, :]
-    for slot in range(1, 2):
+    for slot in range(1, TOPA):
         mass = mass + m_ref[(rows + slot) * tokens : (rows + slot + 1) * tokens, :]
     inverse = jnp.broadcast_to(1.0 / jnp.sum(mass, axis=1, keepdims=True), (tokens, BLK))
 
@@ -116,8 +117,9 @@
     lax.fori_loop(0, owners, left, 0)
 
 
-def stats_kernel(logits_ref, o_ref):
+def stats_kernel(place_ref, logits_ref, o_ref, give_ref):
     half_tokens, columns = logits_ref.shape
+    width = give_ref.shape[1]
     for i in range(0, half_tokens, 64):
         rows = slice(i, i + 64)
         peak = logits_ref[rows, :BLK].astype(jnp.float32)
@@ -129,9 +131,14 @@
             total = total + jnp.exp(logits_ref[rows, b * BLK : (b + 1) * BLK].astype(jnp.float32) - peak)
         o_ref[0:1, rows] = peak.T[0:1]
         o_ref[1:2, rows] = jnp.sum(total.T, axis=0, keepdims=True)
-
-
-def grad_kernel(scale, target_ref, logits_ref, grad_ref, part_ref):
+    give_ref[...] = jnp.where(place_ref[1] == 0, logits_ref[:, width:], logits_ref[:, :width])
+
+
+def later_kernel(sent_ref, hidden_ref, h_ref):
+    h_ref[...] = hidden_ref[...]
+
+
+def grad_kernel(scale, target_ref, logits_ref, grad_ref, part_ref, row_ref):
     owners, tokens, _ = target_ref.shape
     group_tokens, width = logits_ref.shape
     stats = [target_ref[q, :, width:].astype(jnp.float32) for q in range(owners)]
@@ -155,27 +162,36 @@
             positive = target > 0
             one = target * (jnp.log(jnp.where(positive, target, 1.0)) - log_probs)
             terms = terms + jnp.where(positive, one, 0.0)
-        row = jnp.sum(terms.T, axis=0, keepdims=True)
-        for q in range(part_ref.shape[0]):
-            part_ref[q, :, rows] = jnp.broadcast_to(row, (part_ref.shape[1], BLK))
-
-
-def hidden_kernel(place_ref, own_ref, other_ref, o_ref, s_ref):
-    owners, held, features = own_ref.shape
-    for i in range(owners):
-        offset = sum(((i >> j) & 1) * (owners >> (j + 1)) for j in range(owners.bit_length() - 1))
-        first = (place_ref[0] ^ offset) * 2
-        own = pl.ds(pl.multiple_of((first + place_ref[1]) * held, held), held)
-        other = pl.ds(pl.multiple_of((first + 1 - place_ref[1]) * held, held), held)
-        s_ref[own, :] = own_ref[i].astype(jnp.float32)
-        s_ref[other, :] = other_ref[i].astype(jnp.float32)
+        row_ref[:, rows] = jnp.sum(terms.T, axis=0, keepdims=True)
+    half_tokens = part_ref.shape[2]
+    for half in range(group_tokens // half_tokens):
+        row = row_ref[:, half * half_tokens : (half + 1) * half_tokens]
+        for q in range(owners):
+            part_ref[2 * q + half] = jnp.broadcast_to(row, part_ref.shape[1:])
+
+
+def hidden_kernel(place_ref, *refs):
+    pieces, (o_ref, s_ref) = refs[:-2], refs[-2:]
+    count = len(pieces) // 2
+    _, held, features = pieces[0].shape
+    owners = s_ref.shape[0] // (2 * held)
+    i = 0
+    for own_ref, other_ref in zip(pieces[:count], pieces[count:]):
+        for j in range(own_ref.shape[0]):
+            offset = sum(((i >> bit) & 1) * (owners >> (bit + 1)) for bit in range(owners.bit_length() - 1))
+            first = (place_ref[0] ^ offset) * 2
+            own = pl.ds(pl.multiple_of((first + place_ref[1]) * held, held), held)
+            other = pl.ds(pl.multiple_of((first + 1 - place_ref[1]) * held, held), held)
+            s_ref[own, :] = own_ref[j].astype(jnp.float32)
+            s_ref[other, :] = other_ref[j].astype(jnp.float32)
+            i += 1
     for i in range(s_ref.shape[0] // BLK):
         for j in range(features // BLK):
             tile = s_ref[i * BLK : (i + 1) * BLK, j * BLK : (j + 1) * BLK].T
             o_ref[j * BLK : (j + 1) * BLK, i * BLK : (i + 1) * BLK] = tile.astype(jnp.bfloat16)
 
 
-def finish_kernel(place_ref, grad_ref, got_ref, terms_ref, o_ref, d_ref, sem):
+def join_kernel(place_ref, grad_ref, got_ref, o_ref, sem):
     half_tokens, width = got_ref.shape
     half = place_ref[1]
     kept_at = pl.ds(pl.multiple_of(half * width, width), width)
@@ -187,10 +203,6 @@
     ]
     for copy in copies:
         copy.start()
-    total = terms_ref[0, 0:1, :]
-    for q in range(1, terms_ref.shape[0]):
-        total = total + terms_ref[q, 0:1, :]
-    d_ref[...] = jnp.where(half == 0, total[:, :half_tokens], total[:, half_tokens:])
     for copy in copies:
         copy.wait()
 
@@ -223,6 +235,10 @@
 
 def anywhere():
     return pl.BlockSpec(memory_space=pl.ANY)
+
+
+def in_hbm():
+    return pl.BlockSpec(memory_space=pltpu.HBM)
 
 
 def to_partner(x, offset):
@@ -251,16 +267,22 @@
 
     teacher_other = swap_halves(teacher_probs)
 
-    stats = pl.pallas_call(
+    stats, give = pl.pallas_call(
         stats_kernel,
-        out_shape=jax.ShapeDtypeStruct((2, half_tokens), jnp.float32),
-        in_specs=[whole()],
-        out_specs=whole(),
-        compiler_params=params(),
-        cost_estimate=pl.CostEstimate(flops=0, bytes_accessed=0, transcendentals=0),
+        out_shape=(
+            jax.ShapeDtypeStruct((2, half_tokens), jnp.float32),
+            jax.ShapeDtypeStruct((half_tokens, width), jnp.bfloat16),
+        ),
+        in_specs=[scalars(), whole()],
+        out_specs=(whole(), whole()),
+        compiler_params=params(),
+        cost_estimate=pl.CostEstimate(flops=0, bytes_accessed=8 << 20, transcendentals=0),
         name="stats",
-    )(student_logits)
+    )(place, student_logits)
     stats = in_order(stats, swap_halves(stats), 1)
+
+    keep = lax.dynamic_slice_in_dim(student_logits, half_index * width, width, 1)
+    logits = in_order(keep, swap_halves(give), 0)
 
     local = align_local.T - half_index * mine
     row_of = jnp.where((local >= 0) & (local < mine), align_owner.T * mine + local, -1)
@@ -276,11 +298,13 @@
         out_specs=whole(),
         scratch_shapes=[spread],
         compiler_params=params(),
-        cost_estimate=pl.CostEstimate(flops=0, bytes_accessed=0, transcendentals=0),
+        cost_estimate=pl.CostEstimate(
+            flops=2 * (rows + MASS_ROWS) * per_half * tokens * BLK, bytes_accessed=3 << 20, transcendentals=0
+        ),
         name="map_own",
     )(w_own, teacher_probs)
+    cuts = 4
     chunk = (owners, tokens, width + group_tokens)
-    cuts = 4
     outgoing = pl.pallas_call(
         map_rest_kernel,
         out_shape=jax.ShapeDtypeStruct(chunk, jnp.bfloat16),
@@ -302,37 +326,42 @@
     )(w_rest, teacher_other, part, stats)
     target = lax.all_to_all(outgoing, "sv", 0, 0, tiled=True)
 
-    hidden, late_logits, outgoing = lax.optimization_barrier((hidden, student_logits, outgoing))
-
-    keep = lax.dynamic_slice_in_dim(late_logits, half_index * width, width, 1)
-    give = lax.dynamic_slice_in_dim(late_logits, (1 - half_index) * width, width, 1)
-    logits = in_order(keep, swap_halves(give), 0)
-
-    hidden_own = hidden[None]
+    hidden = pl.pallas_call(
+        later_kernel,
+        out_shape=jax.ShapeDtypeStruct(hidden.shape, jnp.bfloat16),
+        in_specs=[in_hbm(), whole()],
+        out_specs=whole(),
+        compiler_params=params(),
+        cost_estimate=pl.CostEstimate(flops=0, bytes_accessed=0, transcendentals=0),
+        name="later",
+    )(outgoing, hidden)
+
+    pieces = [hidden[None]]
     offset = owners // 2
     while offset:
-        hidden_own = jnp.concatenate([hidden_own, to_partner(hidden_own, offset)])
+        pieces.append(to_partner(jnp.concatenate(pieces), offset))
         offset //= 2
     hidden_t = pl.pallas_call(
         hidden_kernel,
         out_shape=jax.ShapeDtypeStruct((features, group_tokens), jnp.bfloat16),
-        in_specs=[scalars(), whole(), whole()],
+        in_specs=[scalars()] + [whole()] * (2 * len(pieces)),
         out_specs=whole(),
         scratch_shapes=[pltpu.VMEM((group_tokens, features), jnp.float32)],
         compiler_params=params(),
         cost_estimate=pl.CostEstimate(flops=0, bytes_accessed=4 * features * group_tokens, transcendentals=0),
         name="hidden_t",
-    )(place, hidden_own, swap_halves(hidden_own))
+    )(place, *pieces, *[swap_halves(piece) for piece in pieces])
 
     scale = float(columns * owners)
     grad, terms = pl.pallas_call(
         lambda *refs: grad_kernel(scale, *refs),
         out_shape=(
             jax.ShapeDtypeStruct((group_tokens, width), jnp.bfloat16),
-            jax.ShapeDtypeStruct((owners * halves, 8, group_tokens), jnp.float32),
+            jax.ShapeDtypeStruct((owners * halves, 8, half_tokens), jnp.float32),
         ),
         in_specs=[whole()] * 2,
         out_specs=(whole(), whole()),
+        scratch_shapes=[pltpu.VMEM((1, group_tokens), jnp.float32)],
         compiler_params=params(),
         cost_estimate=pl.CostEstimate(
             flops=10 * group_tokens * width,
@@ -365,20 +394,19 @@
         name="weight_grad",
     )(hidden_t, grad)
 
-    logit_grad, divergence = pl.pallas_call(
-        finish_kernel,
-        out_shape=(
-            jax.ShapeDtypeStruct((half_tokens, columns), jnp.bfloat16),
-            jax.ShapeDtypeStruct((1, half_tokens), jnp.float32),
-        ),
-        in_specs=[scalars(), anywhere(), anywhere(), whole()],
-        out_specs=(anywhere(), whole()),
+    logit_grad = pl.pallas_call(
+        join_kernel,
+        out_shape=jax.ShapeDtypeStruct((half_tokens, columns), jnp.bfloat16),
+        in_specs=[scalars(), anywhere(), anywhere()],
+        out_specs=anywhere(),
         scratch_shapes=[pltpu.SemaphoreType.DMA((2,))],
         compiler_params=params(),
         cost_estimate=pl.CostEstimate(flops=0, bytes_accessed=4 * half_tokens * columns, transcendentals=0),
-        name="finish",
-    )(place, grad, got, terms)
-    return (divergence.reshape(half_tokens), logit_grad, weight_grad)
+        name="join",
+    )(place, grad, got)
+    terms, logit_grad = lax.optimization_barrier((terms, logit_grad))
+    divergence = jnp.sum(terms[:, 0], axis=0)
+    return (divergence, logit_grad, weight_grad)
 
 
 def solution(mesh):

time: 51.7 us -> 62.2 us (1.20)
  waiting for transfers between devices: 15.7 us -> 24.7 us
  local copies, waits for them, and re-layouts: 3.33 us -> 4.63 us
  other arithmetic: 1.33 us -> 2.55 us
    ppermute x3, waiting for transfers between devices: 8.41 us -> 20.8 us  [to_partner(): lax.ppermute(x, 'sv', [(s, s ^ offset) for s in range(lax.axis_size('sv'))])]
    all_to_all x1, waiting for transfers between devices: 4.96 us -> 0.01 us  [body(): target = lax.all_to_all(outgoing, 'sv', 0, 0, tiled=True)]
    ppermute x3, starting transfers between devices: 8.13 us -> 4.58 us  [to_partner(): lax.ppermute(x, 'sv', [(s, s ^ offset) for s in range(lax.axis_size('sv'))])]
    all_to_all x1, starting transfers between devices: 5.04 us -> 7.05 us  [body(): target = lax.all_to_all(outgoing, 'sv', 0, 0, tiled=True)]
    ppermute x5 -> x8, starting transfers between devices: 0.81 us -> 2.12 us  [swap_halves(): return lax.ppermute(x, 'tv', [(0, 1), (1, 0)])]
    ppermute x5 -> x8, waiting for transfers between devices: 0.01 us -> 0.87 us  [swap_halves(): return lax.ppermute(x, 'tv', [(0, 1), (1, 0)])]
    all_to_all x0 -> x1, other arithmetic: none -> 0.72 us  [body(): terms = lax.all_to_all(terms, ('sv', 'tv'), 0, 0, tiled=True)]
    unnamed x8 -> x9, local copies, waits for them, and re-layouts: 2.36 us -> 3.08 us
  transfers between devices with their start and end apart: 10 -> 13, of which waited for: 4 -> 6; matrix products, arithmetic and copies ran while one was open for 4% -> 7% of each run, Pallas kernels for 14% -> 15%
where the time goes in v6:
time: 62.2 us; the launch traced here: 61.8 us
  waiting for transfers between devices  24.7 us (40%)
  starting transfers between devices  17.5 us (28%)
  Pallas kernels  11.6 us (19%)
  local copies, waits for them, and re-layouts  4.63 us (7%)
  other arithmetic  2.55 us (4%)
  between operations  0.82 us (1%)
    ppermute x3, waiting for transfers between devices, to_partner(): lax.ppermute(x, 'sv', [(s, s ^ offset) for s in range(lax.axis_size('sv'))])  20.8 us
    all_to_all x1, starting transfers between devices, body(): target = lax.all_to_all(outgoing, 'sv', 0, 0, tiled=True)  7.05 us
    ppermute x3, starting transfers between devices, to_partner(): lax.ppermute(x, 'sv', [(s, s ^ offset) for s in range(lax.axis_size('sv'))])  4.58 us
    all_to_all x1, starting transfers between devices, body(): terms = lax.all_to_all(terms, ('sv', 'tv'), 0, 0, tiled=True)  3.74 us
    pallas_call x1, Pallas kernels, body(): pl.pallas_call(weight_kernel, out_shape=jax.ShapeDtypeStruct((features, w...  3.62 us
    unnamed x9, local copies, waits for them, and re-layouts  3.08 us
    all_to_all x1, waiting for transfers between devices, body(): terms = lax.all_to_all(terms, ('sv', 'tv'), 0, 0, tiled=True)  3 us
    pallas_call x1, Pallas kernels, body(): pl.pallas_call(map_rest_kernel, out_shape=jax.ShapeDtypeStruct(chunk, jnp...  2.85 us
  transfers between devices with their start and end apart: 13, of which 6 were waited for; matrix products, arithmetic and copies ran while one was open for 7% of the time, Pallas kernels for 15%

profile of v6, /device:TPU:0, one launch (start us, length us, event | category | flops | bytes accessed | tf_op | source)
XLA Modules:
  0.0 61.8 jit_solution(14765715626212161001)
XLA Ops:
  0.7 1.0 %copy-done.1 = bf16[64,4096]{1,0:T(8,128)(2,1)S(1)} copy-done((bf16[64,4096]{1,0:T(8,128)(2,1)S(1)}, bf16[64,4096]{1,0:T(8,128)(2,1)}, u32[]{:S(2)}) %copy-start.1) | copy-done | bytes 524312
  1.8 0.9 %stats.1 = (f32[2,64]{1,0:T(2,128)S(1)}, bf16[64,2048]{1,0:T(8,128)(2,1)S(1)}) custom-call(s32[2]{0:T(128)S(1)} %pad_add_fusion.place_ref, bf16[64,4096]{1,0:T(8,128)(2,1)S(1)} %copy-done.1), custom_call_target="tpu_custom_call" | custom-call | bytes 8388608 | tf_op jit(solution)/shard_map/stats/pallas_call | solution.py:270
  2.7 0.5 collective-permute-start.1
  3.7 0.8 %dynamic-slice_bitcast_fusion.2 = (bf16[2,320]{1,0:T(2,128)(2,1)S(1)}, bf16[2,320]{1,0:T(2,128)(2,1)S(1)}) fusion(bf16[640,2]{0,1:T(2,128)(2,1)} %param.9, s32[]{:T(128)S(6)} %select_n.60, s32[]{:T(128)S(6)} %select_n.57), kind=kLoop, calls=%fused_computation.31 | loop fusion | bytes 5128 | tf_op jit(solution)/shard_map/dynamic_slice | solution.py:290
  4.5 0.7 %and_select_fusion = s32[640,2]{0,1:T(2,128)S(1)} fusion(s32[640,2]{0,1:T(2,128)} %param.7, s32[640,2]{0,1:T(2,128)} %param.8, s32[]{:T(128)S(6)} %mul.21), kind=kLoop, calls=%fused_computation.15 | loop fusion | flops 8960 | bytes 15364 | tf_op jit(solution)/shard_map/jit(_where)/select_n | solution.py:288
  5.6 1.3 %copy-done = bf16[16,40960]{1,0:T(8,128)(2,1)S(1)} copy-done((bf16[16,40960]{1,0:T(8,128)(2,1)S(1)}, bf16[16,40960]{1,0:T(8,128)(2,1)}, u32[]{:S(2)}) %copy-start) | copy-done | bytes 1310744
  6.9 1.4 %map_own.1.p_ref = f32[144,2048]{1,0:T(8,128)S(1)} custom-call(bf16[144,320]{1,0:T(8,128)(2,1)S(1)} %get-tuple-element.31.w_ref, bf16[16,40960]{1,0:T(8,128)(2,1)S(1)} %copy-done), custom_call_target="tpu_custom_call" | custom-call | flops 188743680 | bytes 3145728 | tf_op jit(solution)/shard_map/map_own/pallas_call | solution.py:294
  8.4 2.8 %map_rest.1.sent_ref = bf16[8,16,2176]{2,1,0:T(8,128)(2,1)} custom-call(bf16[144,320]{1,0:T(8,128)(2,1)S(1)} %get-tuple-element.32.w_ref, bf16[16,40960]{1,0:T(8,128)(2,1)S(1)} %collective-permute-done.t_ref, f32[144,2048]{1,0:T(8,128)S(1)} %map_own.1.p_ref, f32[2,128]{1,0:T(2,128)S(1)} %pad_maximum_fusion.3.stats_ref), custom_call_target="tpu_custom_call" | custom-call | flops 188743680 | bytes 4194304 | tf_op jit(solution)/shard_map/map_rest/pallas_call | solution.py:308
  11.3 7.0 %all-to-all-start = ((bf16[8,16,2176]{2,1,0:T(8,128)(2,1)}), bf16[8,16,2176]{2,1,0:T(8,128)(2,1)S(1)}, u32[]{:S(2)}, u32[]{:S(2)}) async-start(bf16[8,16,2176]{2,1,0:T(8,128)(2,1)} %map_rest.1.sent_ref), calls=%async_computation | async-start | bytes 1114112 | tf_op jit(solution)/shard_map/all_to_all | solution.py:327
  18.4 3.0 %collective-permute-start.4 = (bf16[1,8,1920]{2,1,0:T(8,128)(2,1)S(1)}, bf16[1,8,1920]{2,1,0:T(8,128)(2,1)S(1)}, u32[]{:S(2)}, u32[]{:S(2)}) collective-permute-start(bf16[1,8,1920]{2,1,0:T(8,128)(2,1)S(1)} %bitcast.11), channel_id=1, source_target_pairs={{0,8},{2,10},{4,12},{6,14},{8,0},{10,2},{12,4},{14,6},{1,9},{3,11}... | collective-permute-start | bytes 92168 | tf_op jit(solution)/shard_map/ppermute | solution.py:245
  21.5 14.0 %collective-permute-done.4.refs_1_ = bf16[1,8,1920]{2,1,0:T(8,128)(2,1)S(1)} collective-permute-done((bf16[1,8,1920]{2,1,0:T(8,128)(2,1)S(1)}, bf16[1,8,1920]{2,1,0:T(8,128)(2,1)S(1)}, u32[]{:S(2)}, u32[]{:S(2)}) %collective-permute-start.4) | collective-permute-done | bytes 30752 | tf_op jit(solution)/shard_map/ppermute | solution.py:245
  35.6 4.2 %collective-permute-done.5.refs_2_ = bf16[2,8,1920]{2,1,0:T(8,128)(2,1)S(1)} collective-permute-done((bf16[2,8,1920]{2,1,0:T(8,128)(2,1)S(1)}, bf16[2,8,1920]{2,1,0:T(8,128)(2,1)S(1)}, u32[]{:S(2)}, u32[]{:S(2)}) %collective-permute-start.5) | collective-permute-done | bytes 61472 | tf_op jit(solution)/shard_map/ppermute | solution.py:245
  39.8 1.5 %collective-permute-start.6 = (bf16[4,8,1920]{2,1,0:T(8,128)(2,1)S(1)}, bf16[4,8,1920]{2,1,0:T(8,128)(2,1)S(1)}, u32[]{:S(2)}, u32[]{:S(2)}) collective-permute-start(bf16[4,8,1920]{2,1,0:T(8,128)(2,1)S(1)} %pad_maximum_fusion.1), channel_id=1, source_target_pairs={{0,2},{2,0},{4,6},{6,4},{8,10},{10,8},{12,14},{14,12},{1,3},{3,1},... | collective-permute-start | bytes 368648 | tf_op jit(solution)/shard_map/ppermute | solution.py:245
  41.3 0.6 %logit_grad.1 = (bf16[128,2048]{1,0:T(8,128)(2,1)S(1)}, f32[16,8,64]{2,1,0:T(8,128)S(1)}) custom-call(bf16[8,16,2176]{2,1,0:T(8,128)(2,1)S(1)} %all-to-all-done.refs_0_, bf16[128,2048]{1,0:T(8,128)(2,1)S(1)} %pad_maximum_fusion.refs_1_), custom_call_target="tpu_custom_call" | custom-call | flops 2621440 | bytes 1572864 | tf_op jit(solution)/shard_map/logit_grad/pallas_call | solution.py:356
  42.1 2.7 %collective-permute-done.6.refs_3_ = bf16[4,8,1920]{2,1,0:T(8,128)(2,1)S(1)} collective-permute-done((bf16[4,8,1920]{2,1,0:T(8,128)(2,1)S(1)}, bf16[4,8,1920]{2,1,0:T(8,128)(2,1)S(1)}, u32[]{:S(2)}, u32[]{:S(2)}) %collective-permute-start.6) | collective-permute-done | bytes 122912 | tf_op jit(solution)/shard_map/ppermute | solution.py:245
  45.8 0.7 %collective-permute-done.7.refs_4_ = bf16[1,8,1920]{2,1,0:T(8,128)(2,1)S(1)} collective-permute-done((bf16[1,8,1920]{2,1,0:T(8,128)(2,1)S(1)}, bf16[1,8,1920]{2,1,0:T(8,128)(2,1)S(1)}, u32[]{:S(2)}, u32[]{:S(2)}) %collective-permute-start.7) | collective-permute-done | bytes 30752 | tf_op jit(solution)/shard_map/ppermute | solution.py:16
  46.6 0.8 %hidden_t.1.hidden_ref = bf16[1920,128]{1,0:T(8,128)(2,1)S(1)} custom-call(s32[2]{0:T(128)S(1)} %pad_add_fusion.place_ref, bf16[1,8,1920]{2,1,0:T(8,128)(2,1)S(1)} %bitcast.15, bf16[1,8,1920]{2,1,0:T(8,128)(2,1)S(1)} %collective-permute-done.4.refs_1_, bf16[2,8,1920]{2,1,0:T(8,128)(2,1)S(1)} %collective-permute-done.5.refs_2_, ...), custom_call_target="tpu_custom_call" | custom-call | bytes 983040 | tf_op jit(solution)/shard_map/hidden_t/pallas_call | solution.py:344
  47.5 0.7 %reshape.18 = f32[16,1,512]{2,1,0:T(1,128)} reshape(f32[16,8,64]{2,1,0:T(8,128)S(1)} %get-tuple-element.11) | data formatting | bytes 65536
  48.2 3.7 %all-to-all-start.1 = ((f32[16,1,512]{2,1,0:T(1,128)}), f32[16,1,512]{2,1,0:T(1,128)S(1)}, u32[]{:S(2)}, u32[]{:S(2)}) async-start(f32[16,1,512]{2,1,0:T(1,128)} %reshape.18), calls=%async_computation.1 | async-start | bytes 65536 | tf_op jit(solution)/shard_map/all_to_all | solution.py:374
  51.9 3.6 %weight_grad.1 = bf16[1920,2048]{1,0:T(8,128)(2,1)} custom-call(bf16[1920,128]{1,0:T(8,128)(2,1)S(1)} %hidden_t.1.hidden_ref, bf16[128,2048]{1,0:T(8,128)(2,1)S(1)} %get-tuple-element.12.grad_ref), custom_call_target="tpu_custom_call" | custom-call | flops 1006632960 | bytes 8880128 | tf_op jit(solution)/shard_map/weight_grad/pallas_call | solution.py:379
  55.6 3.0 %all-to-all-done.1 = f32[16,1,512]{2,1,0:T(1,128)S(1)} async-done(((f32[16,1,512]{2,1,0:T(1,128)}), f32[16,1,512]{2,1,0:T(1,128)S(1)}, u32[]{:S(2)}, u32[]{:S(2)}) %all-to-all-start.1) | async-done | bytes 32800 | tf_op jit(solution)/shard_map/all_to_all | solution.py:374
  59.1 0.7 %reduce.17 = f32[16,512]{1,0:T(8,128)S(1)} reduce(f32[16,1,512]{2,1,0:T(1,128)S(1)} %all-to-all-done.1, f32[]{:T(128)} %broadcast.37), dimensions={1}, to_apply=%all_to_all.7.reduce_sub_computation | reduce | bytes 65540 | tf_op jit(solution)/shard_map/all_to_all | solution.py:374
  59.9 1.4 %join.1 = bf16[64,4096]{1,0:T(8,128)(2,1)} custom-call(s32[2]{0:T(128)S(1)} %pad_add_fusion.place_ref, bf16[128,2048]{1,0:T(8,128)(2,1)S(1)} %get-tuple-element.12.grad_ref, bf16[64,2048]{1,0:T(8,128)(2,1)S(1)} %collective-permute-done.3.got_ref), custom_call_target="tpu_custom_call" | custom-call | bytes 1048576 | tf_op jit(solution)/shard_map/join/pallas_call | solution.py:397
  61.2 0.5 slice_reduce_fusion
  (38 shorter events, 3.2 us)
Async XLA Ops:
  0.7 1.0 %copy-start.1 = (bf16[64,4096]{1,0:T(8,128)(2,1)S(1)}, bf16[64,4096]{1,0:T(8,128)(2,1)}, u32[]{:S(2)}) copy-start(bf16[64,4096]{1,0:T(8,128)(2,1)} %logits_ref.1) | copy-start | bytes 1572868
  2.7 5.7 %collective-permute-start.1 = (f32[2,64]{1,0:T(2,128)S(1)}, f32[2,64]{1,0:T(2,128)S(1)}, u32[]{:S(2)}, u32[]{:S(2)}) collective-permute-start(f32[2,64]{1,0:T(2,128)S(1)} %get-tuple-element.9), channel_id=1, source_target_pairs={{0,1},{1,0},{2,3},{3,2},{4,5},{5,4},{6,7},{7,6},{8,9},{9,8},{10,11... | collective-permute-start | bytes 1544 | tf_op jit(solution)/shard_map/ppermute | solution.py:16
  3.2 5.2 %collective-permute-start = (bf16[16,40960]{1,0:T(8,128)(2,1)}, bf16[16,40960]{1,0:T(8,128)(2,1)S(1)}, u32[]{:S(2)}, u32[]{:S(2)}) collective-permute-start(bf16[16,40960]{1,0:T(8,128)(2,1)} %t_ref.1), channel_id=1, source_target_pairs={{0,1},{1,0},{2,3},{3,2},{4,5},{5,4},{6,7},{7,6},{8,9},{9,8},{10,11... | collective-permute-start | bytes 3932168 | tf_op jit(solution)/shard_map/ppermute | solution.py:16
  3.3 18.1 %collective-permute-start.2 = (bf16[64,2048]{1,0:T(8,128)(2,1)S(1)}, bf16[64,2048]{1,0:T(8,128)(2,1)S(1)}, u32[]{:S(2)}, u32[]{:S(2)}) collective-permute-start(bf16[64,2048]{1,0:T(8,128)(2,1)S(1)} %get-tuple-element.10), channel_id=1, source_target_pairs={{0,1},{1,0},{2,3},{3,2},{4,5},{5,4},{6,7},{7,6},{8,9},{9,8},{10,11... | collective-permute-start | bytes 786440 | tf_op jit(solution)/shard_map/ppermute | solution.py:16
  5.6 1.3 %copy-start = (bf16[16,40960]{1,0:T(8,128)(2,1)S(1)}, bf16[16,40960]{1,0:T(8,128)(2,1)}, u32[]{:S(2)}) copy-start(bf16[16,40960]{1,0:T(8,128)(2,1)} %t_ref.1) | copy-start | bytes 3932164
  8.4 9.9 %copy-start.3 = (bf16[8,1920]{1,0:T(8,128)(2,1)S(1)}, bf16[8,1920]{1,0:T(8,128)(2,1)}, u32[]{:S(2)}) copy-start(bf16[8,1920]{1,0:T(8,128)(2,1)} %hidden_ref.1) | copy-start | bytes 92164
  11.3 10.1 %copy-start.2 = (bf16[64,4096]{1,0:T(8,128)(2,1)S(1)}, bf16[64,4096]{1,0:T(8,128)(2,1)}, u32[]{:S(2)}) copy-start(bf16[64,4096]{1,0:T(8,128)(2,1)} %logits_ref.1) | copy-start | bytes 1572868
  11.3 30.0 %all-to-all-start = ((bf16[8,16,2176]{2,1,0:T(8,128)(2,1)}), bf16[8,16,2176]{2,1,0:T(8,128)(2,1)S(1)}, u32[]{:S(2)}, u32[]{:S(2)}) async-start(bf16[8,16,2176]{2,1,0:T(8,128)(2,1)} %map_rest.1.sent_ref), calls=%async_computation | async-start | bytes 1114112 | tf_op jit(solution)/shard_map/all_to_all | solution.py:327
  18.4 17.1 %collective-permute-start.4 = (bf16[1,8,1920]{2,1,0:T(8,128)(2,1)S(1)}, bf16[1,8,1920]{2,1,0:T(8,128)(2,1)S(1)}, u32[]{:S(2)}, u32[]{:S(2)}) collective-permute-start(bf16[1,8,1920]{2,1,0:T(8,128)(2,1)S(1)} %bitcast.11), channel_id=1, source_target_pairs={{0,8},{2,10},{4,12},{6,14},{8,0},{10,2},{12,4},{14,6},{1,9},{3,11}... | collective-permute-start | bytes 92168 | tf_op jit(solution)/shard_map/ppermute | solution.py:245
  35.5 4.3 %collective-permute-start.5 = (bf16[2,8,1920]{2,1,0:T(8,128)(2,1)S(1)}, bf16[2,8,1920]{2,1,0:T(8,128)(2,1)S(1)}, u32[]{:S(2)}, u32[]{:S(2)}) collective-permute-start(bf16[2,8,1920]{2,1,0:T(8,128)(2,1)S(1)} %pad_maximum_fusion.2), channel_id=1, source_target_pairs={{0,4},{2,6},{4,0},{6,2},{8,12},{10,14},{12,8},{14,10},{1,5},{3,7},... | collective-permute-start | bytes 184328 | tf_op jit(solution)/shard_map/ppermute | solution.py:245
  39.8 4.9 %collective-permute-start.6 = (bf16[4,8,1920]{2,1,0:T(8,128)(2,1)S(1)}, bf16[4,8,1920]{2,1,0:T(8,128)(2,1)S(1)}, u32[]{:S(2)}, u32[]{:S(2)}) collective-permute-start(bf16[4,8,1920]{2,1,0:T(8,128)(2,1)S(1)} %pad_maximum_fusion.1), channel_id=1, source_target_pairs={{0,2},{2,0},{4,6},{6,4},{8,10},{10,8},{12,14},{14,12},{1,3},{3,1},... | collective-permute-start | bytes 368648 | tf_op jit(solution)/shard_map/ppermute | solution.py:245
  42.0 17.9 %collective-permute-start.3 = (bf16[64,2048]{1,0:T(8,128)(2,1)S(1)}, bf16[64,2048]{1,0:T(8,128)(2,1)S(1)}, u32[]{:S(2)}, u32[]{:S(2)}) collective-permute-start(bf16[64,2048]{1,0:T(8,128)(2,1)S(1)} %constant_dynamic-slice_fusion), channel_id=1, source_target_pairs={{0,1},{1,0},{2,3},{3,2},{4,5},{5,4},{6,7},{7,6},{8,9},{9,8},{10,11... | collective-permute-start | bytes 786440 | tf_op jit(solution)/shard_map/ppermute | solution.py:16
  44.7 1.9 %collective-permute-start.10 = (bf16[4,8,1920]{2,1,0:T(8,128)(2,1)S(1)}, bf16[4,8,1920]{2,1,0:T(8,128)(2,1)S(1)}, u32[]{:S(2)}, u32[]{:S(2)}) collective-permute-start(bf16[4,8,1920]{2,1,0:T(8,128)(2,1)S(1)} %collective-permute-done.6.refs_3_), channel_id=1, source_target_pairs={{0,1},{1,0},{2,3},{3,2},{4,5},{5,4},{6,7},{7,6},{8,9},{9,8},{10,11... | collective-permute-start | bytes 368648 | tf_op jit(solution)/shard_map/ppermute | solution.py:16
  44.8 1.9 %collective-permute-start.9 = (bf16[2,8,1920]{2,1,0:T(8,128)(2,1)S(1)}, bf16[2,8,1920]{2,1,0:T(8,128)(2,1)S(1)}, u32[]{:S(2)}, u32[]{:S(2)}) collective-permute-start(bf16[2,8,1920]{2,1,0:T(8,128)(2,1)S(1)} %collective-permute-done.5.refs_2_), channel_id=1, source_target_pairs={{0,1},{1,0},{2,3},{3,2},{4,5},{5,4},{6,7},{7,6},{8,9},{9,8},{10,11... | collective-permute-start | bytes 184328 | tf_op jit(solution)/shard_map/ppermute | solution.py:16
  45.3 1.2 %collective-permute-start.7 = (bf16[1,8,1920]{2,1,0:T(8,128)(2,1)S(1)}, bf16[1,8,1920]{2,1,0:T(8,128)(2,1)S(1)}, u32[]{:S(2)}, u32[]{:S(2)}) collective-permute-start(bf16[1,8,1920]{2,1,0:T(8,128)(2,1)S(1)} %bitcast.14), channel_id=1, source_target_pairs={{0,1},{1,0},{2,3},{3,2},{4,5},{5,4},{6,7},{7,6},{8,9},{9,8},{10,11... | collective-permute-start | bytes 92168 | tf_op jit(solution)/shard_map/ppermute | solution.py:16
  45.3 1.4 %collective-permute-start.8 = (bf16[1,8,1920]{2,1,0:T(8,128)(2,1)S(1)}, bf16[1,8,1920]{2,1,0:T(8,128)(2,1)S(1)}, u32[]{:S(2)}, u32[]{:S(2)}) collective-permute-start(bf16[1,8,1920]{2,1,0:T(8,128)(2,1)S(1)} %collective-permute-done.4.refs_1_), channel_id=1, source_target_pairs={{0,1},{1,0},{2,3},{3,2},{4,5},{5,4},{6,7},{7,6},{8,9},{9,8},{10,11... | collective-permute-start | bytes 92168 | tf_op jit(solution)/shard_map/ppermute | solution.py:16
  48.2 10.4 %all-to-all-start.1 = ((f32[16,1,512]{2,1,0:T(1,128)}), f32[16,1,512]{2,1,0:T(1,128)S(1)}, u32[]{:S(2)}, u32[]{:S(2)}) async-start(f32[16,1,512]{2,1,0:T(1,128)} %reshape.18), calls=%async_computation.1 | async-start | bytes 65536 | tf_op jit(solution)/shard_map/all_to_all | solution.py:374

commit v7 on v3

v7 whole, which is shorter than its diff:
```python
import jax
import jax.numpy as jnp
from jax import lax
from jax.experimental import pallas as pl
from jax.experimental.pallas import tpu as pltpu
from jax.sharding import PartitionSpec as P

BLK = 128
TB = 640
TOPA = 2
MASS_ROWS = 16
STEP = 16


def block_weights(place_ref, owner_ref, local_ref, weight_ref, which, rows, mine):
    count = owner_ref.shape[1] // 2
    halved = lambda x: jnp.where(which == 0, x[:, :count], x[:, count:])
    local = local_ref[...] - place_ref[1] * mine
    inside = (local >= 0) & (local < mine)
    row_of = halved(jnp.where(inside, owner_ref[...] * mine + local, -1))
    weight = halved(weight_ref[...].astype(jnp.float32))
    row_ids = lax.broadcasted_iota(jnp.int32, (rows + MASS_ROWS, count), 0)
    total = jnp.zeros(row_ids.shape, jnp.float32)
    for slot in range(row_of.shape[0]):
        hit = (row_ids == row_of[slot : slot + 1]) | (row_ids == rows + slot)
        total = total + jnp.where(hit, weight[slot : slot + 1], 0.0)
    return total.astype(jnp.bfloat16)


def column_copies(source, target, sems, first=0):
    cuts = sems.shape[0] - first
    wide = source.shape[1] // cuts
    at = [pl.ds(i * wide, wide) for i in range(cuts)]
    return [pltpu.make_async_copy(source.at[:, at[i]], target.at[:, at[i]], sems.at[first + i]) for i in range(cuts)]


def spread_tokens(t_ref, s_ref, start, count):
    tokens = t_ref.shape[0]

    def some(i, carry):
        for j in range(STEP):
            k = start + i * STEP + j
            tile = t_ref[:, pl.ds(pl.multiple_of(k * BLK, BLK), BLK)]
            s_ref[pl.ds(pl.multiple_of(k * tokens, tokens), tokens), :] = tile.astype(jnp.float32)
        return carry

    lax.fori_loop(0, count // STEP, some, 0)


def spread_arriving(copies, t_buf, s_ref):
    blocks = t_buf.shape[1] // BLK // len(copies)
    for i, copy in enumerate(copies):
        copy.wait()
        spread_tokens(t_buf, s_ref, i * blocks, blocks)


def token_pair(s_ref, t, tokens):
    count = s_ref.shape[0] // tokens
    both = [s_ref[pl.ds(t + i, count, stride=tokens), :].astype(jnp.bfloat16) for i in range(2)]
    return jnp.concatenate(both, axis=1)


def stats_kernel(place_ref, logits_ref, o_ref, give_ref, l_buf, sems, give_sem):
    half_tokens, columns = logits_ref.shape
    width = give_ref.shape[1]
    arriving = column_copies(logits_ref, l_buf, sems)
    for copy in arriving:
        copy.start()
    for copy in arriving:
        copy.wait()
    given = pl.ds(pl.multiple_of((1 - place_ref[1]) * width, width), width)
    give = pltpu.make_async_copy(l_buf.at[:, given], give_ref, give_sem)
    give.start()
    for i in range(0, half_tokens, 64):
        rows = slice(i, i + 64)
        peak = l_buf[rows, :BLK].astype(jnp.float32)
        for b in range(1, columns // BLK):
            peak = jnp.maximum(peak, l_buf[rows, b * BLK : (b + 1) * BLK].astype(jnp.float32))
        peak = jnp.broadcast_to(jnp.max(peak, axis=1, keepdims=True), peak.shape)
        total = jnp.zeros_like(peak)
        for b in range(columns // BLK):
            total = total + jnp.exp(l_buf[rows, b * BLK : (b + 1) * BLK].astype(jnp.float32) - peak)
        o_ref[0:1, rows] = peak.T[0:1]
        o_ref[1:2, rows] = jnp.sum(total.T, axis=0, keepdims=True)
    give.wait()


def map_own_kernel(mine, place_ref, *refs):
    tables, (t_ref, rest_ref, o_ref), scratch = refs[:3], refs[3:6], refs[6:]
    held, (t_buf, s_ref, o_buf, table_sems, in_sems, out_sems) = scratch[:3], scratch[3:]
    tokens = t_ref.shape[0]
    rows = rest_ref.shape[0] - MASS_ROWS
    for_weights = [pltpu.make_async_copy(x, y, table_sems.at[i]) for i, (x, y) in enumerate(zip(tables, held))]
    arriving = column_copies(t_ref, t_buf, in_sems)
    for copy in for_weights + arriving:
        copy.start()
    for copy in for_weights:
        copy.wait()
    own = block_weights(place_ref, *held, place_ref[1], rows, mine)
    rest_ref[...] = block_weights(place_ref, *held, 1 - place_ref[1], rows, mine)
    spread_arriving(arriving, t_buf, s_ref)
    leaving = column_copies(o_buf, o_ref, out_sems)
    for i, copy in enumerate(leaving):
        o_buf[:, 2 * i * BLK : 2 * (i + 1) * BLK] = jnp.dot(
            own, token_pair(s_ref, 2 * i, tokens), preferred_element_type=jnp.float32
        )
        copy.start()
    for copy in leaving:
        copy.wait()


def three_parts(x):
    parts = []
    for _ in range(3):
        parts.append(x.astype(jnp.bfloat16).astype(jnp.float32))
        x = x - parts[-1]
    return parts


def riding_tile(hidden, stats, lanes):
    held, features = hidden.shape
    wide = stats.shape[1]
    rows = [stats[0:1]] + three_parts(stats[1:2])
    corner = jnp.concatenate(rows + [jnp.zeros((held - len(rows), wide), jnp.float32)], axis=0)
    rest = features - lanes
    gap = lanes - rest - wide
    parts = [hidden[:, lanes:]] + ([jnp.zeros((held, gap), jnp.float32)] if gap else []) + [corner]
    return jnp.concatenate([hidden[:, :lanes], jnp.concatenate(parts, axis=1)], axis=0)


def map_rest_kernel(
    w_ref, t_ref, p_ref, stats_ref, hidden_ref, o_ref,
    w_buf, t_buf, p_buf, stats_buf, hidden_buf, s_ref, m_ref, o_buf, sems, in_sems, p_sems, out_sems,
):
    tokens = t_ref.shape[0]
    owners, _, chunk = o_ref.shape
    rows = w_ref.shape[0] - MASS_ROWS
    mine = rows // owners
    width = mine * BLK
    arriving = column_copies(t_ref, t_buf, in_sems)
    partial = column_copies(p_ref, p_buf, p_sems)
    small = [
        pltpu.make_async_copy(x, y, sems.at[i])
        for i, (x, y) in enumerate([(w_ref, w_buf), (stats_ref, stats_buf), (hidden_ref, hidden_buf)])
    ]
    for copy in arriving + small + partial:
        copy.start()
    spread_arriving(arriving, t_buf, s_ref)
    for copy in small:
        copy.wait()
    for i, copy in enumerate(partial):
        copy.wait()
        t = 2 * i
        both = p_buf[:, t * BLK : (t + 2) * BLK] + jnp.dot(
            w_buf[...], token_pair(s_ref, t, tokens), preferred_element_type=jnp.float32
        )
        for j in range(2):
            m_ref[pl.ds(t + j, rows + 8, stride=tokens), :] = both[: rows + 8, j * BLK : (j + 1) * BLK]
    mass = m_ref[rows * tokens : (rows + 1) * tokens, :]
    for slot in range(1, TOPA):
        mass = mass + m_ref[(rows + slot) * tokens : (rows + slot + 1) * tokens, :]
    inverse = jnp.broadcast_to(1.0 / jnp.sum(mass, axis=1, keepdims=True), (tokens, BLK))
    riding = riding_tile(hidden_buf[...].astype(jnp.float32), stats_buf[...], chunk - width).astype(jnp.bfloat16)

    def leaving(q):
        return pltpu.make_async_copy(o_buf.at[q], o_ref.at[q], out_sems.at[q])

    def owner(q, carry):
        for b in range(mine):
            first = pl.multiple_of((q * mine + b) * tokens, tokens)
            tile = m_ref[pl.ds(first, tokens), :] * inverse
            o_buf[q, :, b * BLK : (b + 1) * BLK] = tile.astype(jnp.bfloat16)
        o_buf[q, :, width:] = riding
        leaving(q).start()
        return carry

    def left(q, carry):
        leaving(q).wait()
        return carry

    lax.fori_loop(0, owners, owner, 0)
    lax.fori_loop(0, owners, left, 0)


def grad_kernel(scale, target_ref, logits_ref, grad_ref, terms_ref, hidden_ref, row_ref):
    owners, tokens, chunk = target_ref.shape
    group_tokens, width = logits_ref.shape
    stats = [target_ref[q, :, chunk - group_tokens :].astype(jnp.float32)[8:] for q in range(owners)]
    top = stats[0][0:1]
    for one in stats[1:]:
        top = jnp.maximum(top, one[0:1])
    total = jnp.zeros_like(top)
    for one in stats:
        total = total + (one[1:2] + one[2:3] + one[3:4]) * jnp.exp(one[0:1] - top)
    log_norm = top + jnp.log(total)
    for q in range(owners):
        hidden_ref[q] = target_ref[q, :, width:]
    for i in range(group_tokens // BLK):
        rows = slice(i * BLK, (i + 1) * BLK)
        group = slice(i * BLK // tokens, (i + 1) * BLK // tokens)
        norm = jnp.broadcast_to(log_norm[:, rows], (BLK, BLK)).T
        terms = jnp.zeros((BLK, BLK), jnp.float32)
        for b in range(width // BLK):
            lanes = slice(b * BLK, (b + 1) * BLK)
            target = target_ref[group, :, lanes].reshape(BLK, BLK).astype(jnp.float32)
            log_probs = logits_ref[rows, lanes].astype(jnp.float32) - norm
            grad_ref[rows, lanes] = ((jnp.exp(log_probs) - target) * scale).astype(jnp.bfloat16)
            positive = target > 0
            one = target * (jnp.log(jnp.where(positive, target, 1.0)) - log_probs)
            terms = terms + jnp.where(positive, one, 0.0)
        row_ref[:, rows] = jnp.sum(terms.T, axis=0, keepdims=True)
    half_tokens = group_tokens // 2
    for half in range(2):
        row = row_ref[:, half * half_tokens : (half + 1) * half_tokens]
        tile = jnp.concatenate([row] * (terms_ref.shape[2] // half_tokens), axis=1)
        for q in range(owners):
            terms_ref[2 * q + half] = jnp.broadcast_to(tile, terms_ref.shape[1:])


def join_kernel(place_ref, grad_ref, got_ref, o_ref, sem):
    half_tokens, width = got_ref.shape
    half = place_ref[1]
    kept_at = pl.ds(pl.multiple_of(half * width, width), width)
    got_at = pl.ds(pl.multiple_of((1 - half) * width, width), width)
    rows = pl.ds(pl.multiple_of(half * half_tokens, half_tokens), half_tokens)
    copies = [
        pltpu.make_async_copy(grad_ref.at[rows, :], o_ref.at[:, kept_at], sem.at[0]),
        pltpu.make_async_copy(got_ref, o_ref.at[:, got_at], sem.at[1]),
    ]
    for copy in copies:
        copy.start()
    for copy in copies:
        copy.wait()


def weight_kernel(place_ref, own_ref, other_ref, grad_ref, o_ref, s_ref, h_ref, block_ref, sem):
    owners, tokens, lanes = own_ref.shape
    held = tokens // 2
    features = s_ref.shape[1]
    for q in range(owners):
        for ref, half in ((own_ref, place_ref[1]), (other_ref, 1 - place_ref[1])):
            rows = pl.ds(pl.multiple_of((2 * q + half) * held, held), held)
            tile = ref[q].astype(jnp.float32)
            s_ref[rows, :lanes] = tile[:held]
            s_ref[rows, lanes:] = tile[held:, : features - lanes]
    for i in range(s_ref.shape[0] // BLK):
        for j in range(features // BLK):
            tile = s_ref[i * BLK : (i + 1) * BLK, j * BLK : (j + 1) * BLK].T
            h_ref[j * BLK : (j + 1) * BLK, i * BLK : (i + 1) * BLK] = tile.astype(jnp.bfloat16)
    steps, tile, _ = block_ref.shape
    copies = []
    for i in range(steps):
        rows = slice(i * tile, (i + 1) * tile)
        block_ref[i] = jnp.dot(
            h_ref[rows, :], grad_ref[...], preferred_element_type=jnp.float32
        ).astype(jnp.bfloat16)
        copies.append(pltpu.make_async_copy(block_ref.at[i], o_ref.at[pl.ds(i * tile, tile), :], sem.at[i]))
        copies[-1].start()
    for copy in copies:
        copy.wait()


def in_vmem():
    return pl.BlockSpec(memory_space=pltpu.VMEM)


def scalars():
    return pl.BlockSpec(memory_space=pltpu.SMEM)


def anywhere():
    return pl.BlockSpec(memory_space=pl.ANY)


def params(mib=48):
    return pltpu.CompilerParams(vmem_limit_bytes=mib << 20)


def cost(flops=0, bytes_accessed=0, transcendentals=0):
    return pl.CostEstimate(flops=flops, bytes_accessed=bytes_accessed, transcendentals=transcendentals)


def swap_halves(x):
    return lax.ppermute(x, "tv", [(0, 1), (1, 0)])


def body(teacher_probs, align_owner, align_local, align_weight, student_logits, hidden):
    owners = lax.axis_size("sv")
    halves = lax.axis_size("tv")
    half_index = lax.axis_index("tv")
    place = jnp.stack([lax.axis_index("sv"), half_index]).astype(jnp.int32)
    tokens = teacher_probs.shape[0]
    columns = student_logits.shape[1]
    blocks = columns // BLK
    mine = blocks // halves
    width = mine * BLK
    rows = owners * mine
    per_half = TB // halves
    group_tokens = owners * tokens
    half_tokens = student_logits.shape[0]
    features = hidden.shape[1]
    first = half_index == 0
    bf16, f32 = jnp.bfloat16, jnp.float32
    shape = jax.ShapeDtypeStruct
    dma = lambda count: pltpu.SemaphoreType.DMA((count,))

    def in_order(own, other, axis):
        return jnp.concatenate([jnp.where(first, own, other), jnp.where(first, other, own)], axis=axis)

    teacher_other = swap_halves(teacher_probs)

    cuts = 4
    stats, give = pl.pallas_call(
        stats_kernel,
        out_shape=(shape((2, half_tokens), f32), shape((half_tokens, width), bf16)),
        in_specs=[scalars(), anywhere()],
        out_specs=(in_vmem(), anywhere()),
        scratch_shapes=[pltpu.VMEM(student_logits.shape, bf16), dma(cuts), pltpu.SemaphoreType.DMA],
        compiler_params=params(60),
        cost_estimate=cost(),
        name="stats",
    )(place, student_logits)
    stats = in_order(stats, swap_halves(stats), 1)

    keep = lax.dynamic_slice_in_dim(student_logits, half_index * width, width, 1)
    logits = in_order(keep, swap_halves(give), 0)

    pairs = tokens // 2
    weights = shape((rows + MASS_ROWS, per_half), bf16)
    partial = shape((rows + MASS_ROWS, tokens * BLK), f32)
    spread = pltpu.VMEM((per_half * tokens, BLK), f32)
    teacher = pltpu.VMEM((tokens, per_half * BLK), bf16)
    tables = [align_owner.T, align_local.T, align_weight.T]
    w_rest, part = pl.pallas_call(
        lambda *refs: map_own_kernel(mine, *refs),
        out_shape=(weights, partial),
        in_specs=[scalars()] + [anywhere()] * 4,
        out_specs=(in_vmem(), anywhere()),
        scratch_shapes=[
            *[pltpu.VMEM(x.shape, x.dtype) for x in tables],
            teacher,
            spread,
            pltpu.VMEM(partial.shape, f32),
            dma(len(tables)),
            dma(cuts),
            dma(pairs),
        ],
        compiler_params=params(60),
        cost_estimate=cost(),
        name="map_own",
    )(place, *tables, teacher_probs)
    riding = -(-(features + group_tokens) // (2 * BLK)) * BLK
    chunk = (owners, tokens, width + riding)
    outgoing = pl.pallas_call(
        map_rest_kernel,
        out_shape=shape(chunk, bf16),
        in_specs=[anywhere()] * 5,
        out_specs=anywhere(),
        scratch_shapes=[
            pltpu.VMEM(weights.shape, bf16),
            teacher,
            pltpu.VMEM(partial.shape, f32),
            pltpu.VMEM(stats.shape, f32),
            pltpu.VMEM(hidden.shape, bf16),
            spread,
            pltpu.VMEM(((rows + 8) * tokens, BLK), f32),
            pltpu.VMEM(chunk, bf16),
            dma(3),
            dma(cuts),
            dma(pairs),
            dma(owners),
        ],
        compiler_params=params(48),
        cost_estimate=cost(2 * (rows + MASS_ROWS) * per_half * tokens * BLK, 4 << 20),
        name="map_rest",
    )(w_rest, teacher_other, part, stats, hidden)
    target = lax.all_to_all(outgoing, "sv", 0, 0, tiled=True)

    scale = float(columns * owners)
    lanes = -(-half_tokens // BLK) * BLK
    grad, terms, hidden_own = pl.pallas_call(
        lambda *refs: grad_kernel(scale, *refs),
        out_shape=(
            shape((group_tokens, width), bf16),
            shape((owners * halves, 8, lanes), f32),
            shape((owners, tokens, riding), bf16),
        ),
        in_specs=[in_vmem()] * 2,
        out_specs=[in_vmem()] * 3,
        scratch_shapes=[pltpu.VMEM((1, group_tokens), f32)],
        compiler_params=params(),
        cost_estimate=cost(
            10 * group_tokens * width, 6 * group_tokens * width, 2 * group_tokens * width
        ),
        name="logit_grad",
    )(target, logits)

    terms = lax.all_to_all(terms, ("sv", "tv"), 0, 0, tiled=True)
    give = lax.dynamic_slice_in_dim(grad, (1 - half_index) * half_tokens, half_tokens, 0)
    got = swap_halves(give)

    steps = 8
    weight_grad = pl.pallas_call(
        weight_kernel,
        out_shape=shape((features, width), bf16),
        in_specs=[scalars()] + [in_vmem()] * 3,
        out_specs=anywhere(),
        scratch_shapes=[
            pltpu.VMEM((group_tokens, features), f32),
            pltpu.VMEM((features, group_tokens), bf16),
            pltpu.VMEM((steps, features // steps, width), bf16),
            dma(steps),
        ],
        compiler_params=params(),
        cost_estimate=cost(
            2 * features * group_tokens * width,
            2 * (features * width + group_tokens * (features + width)),
        ),
        name="weight_grad",
    )(place, hidden_own, swap_halves(hidden_own), grad)

    logit_grad = pl.pallas_call(
        join_kernel,
        out_shape=shape((half_tokens, columns), bf16),
        in_specs=[scalars(), anywhere(), anywhere()],
        out_specs=anywhere(),
        scratch_shapes=[dma(2)],
        compiler_params=params(),
        cost_estimate=cost(0, 4 * half_tokens * columns),
        name="join",
    )(place, grad, got)
    terms, logit_grad = lax.optimization_barrier((terms, logit_grad))
    divergence = jnp.sum(terms[:, 0, :half_tokens], axis=0)
    return (divergence, logit_grad, weight_grad)


def solution(mesh):
    return jax.shard_map(
        body,
        mesh=mesh,
        in_specs=(
            P(("grp", "sv"), "tv"),
            P(),
            P(),
            P(),
            P(("grp", "tv"), "sv"),
            P(("grp", "sv", "tv"), None),
        ),
        out_specs=(P(("grp", "tv")), P(("grp", "tv"), "sv"), P(None, ("grp", "sv", "tv"))),
        check_vma=False,
    )
```

time: 73.4 us -> 62.2 us (0.85)
  blocking collectives: 38.7 us -> 0 us
  waiting for transfers between devices: 4.01 us -> 25.6 us
  Pallas kernels: 9.58 us -> 19.4 us
  other arithmetic: 5.43 us -> 1.35 us
    all_gather x1 -> x0, blocking collectives: 38.7 us -> none  [body(): hidden_own = lax.all_gather(hidden, 'sv')]
    all_to_all x1, waiting for transfers between devices: 0.01 us -> 18.6 us  [body(): target = lax.all_to_all(outgoing, 'sv', 0, 0, tiled=True)]
    pallas_call x4 -> x6, Pallas kernels: 9.58 us -> 19.4 us  [the longest x1 4.89 us: body(): pl.pallas_call(lambda *refs: map_own_kernel(mine, *refs), out_shape=(weig...]
    all_to_all x1, waiting for transfers between devices: 2.66 us -> 5.52 us  [body(): terms = lax.all_to_all(terms, ('sv', 'tv'), 0, 0, tiled=True)]
    unnamed x12 -> x14, local copies, waits for them, and re-layouts: 0.03 us -> 2.19 us
    reduce_sum x2 -> x1, other arithmetic: 1.93 us -> 0.54 us  [body(): divergence = jnp.sum(terms[:, 0, :half_tokens], axis=0)]
    reduce_max x2 -> x0, other arithmetic: 1.32 us -> none  [body(): peak = jnp.max(wide, axis=1)]
    dynamic_slice x3 -> x0, local copies, waits for them, and re-layouts: 1.13 us -> none  [the longest x1 0.97 us: body(): lax.dynamic_slice_in_dim(student_logits, (1 - half_index) * width, width, 1)]
  transfers between devices with their start and end apart: 7 -> 7, of which waited for: 2 -> 3; matrix products, arithmetic and copies ran while one was open for 6% -> 2% of each run, Pallas kernels for 12% -> 15%
where the time goes in v7:
time: 62.2 us; the launch traced here: 61.8 us
  waiting for transfers between devices  25.6 us (41%)
  Pallas kernels  19.4 us (31%)
  starting transfers between devices  12.4 us (20%)
  local copies, waits for them, and re-layouts  2.21 us (4%)
  other arithmetic  1.35 us (2%)
  between operations  0.8 us (1%)
    all_to_all x1, waiting for transfers between devices, body(): target = lax.all_to_all(outgoing, 'sv', 0, 0, tiled=True)  18.6 us
    all_to_all x1, starting transfers between devices, body(): target = lax.all_to_all(outgoing, 'sv', 0, 0, tiled=True)  7.43 us
    all_to_all x1, waiting for transfers between devices, body(): terms = lax.all_to_all(terms, ('sv', 'tv'), 0, 0, tiled=True)  5.52 us
    pallas_call x1, Pallas kernels, body(): pl.pallas_call(lambda *refs: map_own_kernel(mine, *refs), out_shape=(weig...  4.89 us
    pallas_call x1, Pallas kernels, body(): pl.pallas_call(map_rest_kernel, out_shape=shape(chunk, bf16), in_specs=[a...  4.55 us
    pallas_call x1, Pallas kernels, body(): pl.pallas_call(weight_kernel, out_shape=shape((features, width), bf16), i...  4.3 us
    all_to_all x1, starting transfers between devices, body(): terms = lax.all_to_all(terms, ('sv', 'tv'), 0, 0, tiled=True)  3.65 us
    pallas_call x1, Pallas kernels, body(): pl.pallas_call(stats_kernel, out_shape=(shape((2, half_tokens), f32), sha...  3.1 us
  transfers between devices with their start and end apart: 7, of which 3 were waited for; matrix products, arithmetic and copies ran while one was open for 2% of the time, Pallas kernels for 15%

profile of v7, /device:TPU:0, one launch (start us, length us, event | category | flops | bytes accessed | tf_op | source)
XLA Modules:
  0.0 61.8 jit_solution(366289656948921298)
XLA Ops:
  0.6 0.5 collective-permute-start
  1.2 0.6 pad_add_fusion.refs_0_.place_ref
  1.7 3.1 %stats.1 = (f32[2,64]{1,0:T(2,128)}, bf16[64,2048]{1,0:T(8,128)(2,1)}) custom-call(s32[2]{0:T(128)} %pad_add_fusion.refs_0_.place_ref, bf16[64,4096]{1,0:T(8,128)(2,1)} %logits_ref.1), custom_call_target="tpu_custom_call" | custom-call | tf_op jit(solution)/shard_map/stats/pallas_call | solution.py:313
  4.9 0.1 collective-permute-start.1
  5.0 4.9 %map_own.1 = (bf16[144,320]{1,0:T(8,128)(2,1)}, f32[144,2048]{1,0:T(8,128)}) custom-call(s32[2]{0:T(128)} %pad_add_fusion.refs_0_.place_ref, s32[2,640]{1,0:T(2,128)} %bitcast.5, s32[2,640]{1,0:T(2,128)} %bitcast.6, bf16[2,640]{1,0:T(2,128)(2,1)} %bitcast.7, bf16[16,40960]{1,0:T(8,128)(2,1)} %refs_4_.1), custom_call_target="tpu_custom_call" | custom-call | tf_op jit(solution)/shard_map/map_own/pallas_call | solution.py:334
  9.9 0.1 pad_maximum_fusion.1.stats_ref
  10.0 1.3 %copy-done = f32[144,2048]{1,0:T(8,128)S(1)} copy-done((f32[144,2048]{1,0:T(8,128)S(1)}, f32[144,2048]{1,0:T(8,128)}, u32[]{:S(2)}) %copy-start) | copy-done | bytes 1179672
  11.3 0.9 %copy-done.1 = bf16[144,320]{1,0:T(8,128)(2,1)S(1)} copy-done((bf16[144,320]{1,0:T(8,128)(2,1)S(1)}, bf16[144,320]{1,0:T(8,128)(2,1)}, u32[]{:S(2)}) %copy-start.1) | copy-done | bytes 92184
  12.2 4.5 %map_rest.1 = bf16[8,16,3072]{2,1,0:T(8,128)(2,1)} custom-call(bf16[144,320]{1,0:T(8,128)(2,1)S(1)} %copy-done.1, bf16[16,40960]{1,0:T(8,128)(2,1)S(1)} %collective-permute-done.t_ref, f32[144,2048]{1,0:T(8,128)S(1)} %copy-done, f32[2,128]{1,0:T(2,128)S(1)} %pad_maximum_fusion.1.stats_ref, bf16[8,1920]{1,0:T(8,128)(2,1)S(1)} %copy-done.2), custom_call_target="tpu_custom_call" | custom-call | flops 188743680 | bytes 4194304 | tf_op jit(solution)/shard_map/map_rest/pallas_call | solution.py:354
  16.7 0.0 copy-start.6
  16.7 0.0 copy-start.4
  16.7 7.4 %all-to-all-start = ((bf16[8,16,3072]{2,1,0:T(8,128)(2,1)}), bf16[8,16,3072]{2,1,0:T(8,128)(2,1)S(1)}, u32[]{:S(2)}, u32[]{:S(2)}) async-start(bf16[8,16,3072]{2,1,0:T(8,128)(2,1)} %map_rest.1), calls=%async_computation | async-start | bytes 1572864 | tf_op jit(solution)/shard_map/all_to_all | solution.py:377
  24.2 0.1 collective-permute-start.2
  24.3 1.5 %collective-permute-done.2 = bf16[64,2048]{1,0:T(8,128)(2,1)S(1)} collective-permute-done((bf16[64,2048]{1,0:T(8,128)(2,1)S(1)}, bf16[64,2048]{1,0:T(8,128)(2,1)S(1)}, u32[]{:S(2)}, u32[]{:S(2)}) %collective-permute-start.2) | collective-permute-done | bytes 262176 | tf_op jit(solution)/shard_map/ppermute | solution.py:284
  25.8 0.1 broadcast_select_fusion.1
  26.0 18.6 %all-to-all-done.refs_0_ = bf16[8,16,3072]{2,1,0:T(8,128)(2,1)S(1)} async-done(((bf16[8,16,3072]{2,1,0:T(8,128)(2,1)}), bf16[8,16,3072]{2,1,0:T(8,128)(2,1)S(1)}, u32[]{:S(2)}, u32[]{:S(2)}) %all-to-all-start) | async-done | bytes 786464 | tf_op jit(solution)/shard_map/all_to_all | solution.py:377
  44.6 1.3 %logit_grad.1 = (bf16[128,2048]{1,0:T(8,128)(2,1)S(1)}, f32[16,8,128]{2,1,0:T(8,128)}, bf16[8,16,1024]{2,1,0:T(8,128)(2,1)S(1)}) custom-call(bf16[8,16,3072]{2,1,0:T(8,128)(2,1)S(1)} %all-to-all-done.refs_0_, bf16[128,2048]{1,0:T(8,128)(2,1)S(1)} %pad_maximum_fusion.refs_1_), custom_call_target="tpu_custom_call" | custom-call | flops 2621440 | bytes 1572864 | tf_op jit(solution)/shard_map/logit_grad/pallas_call | solution.py:381
  45.8 0.1 collective-permute-start.3
  45.9 0.5 collective-permute-start.4
  46.4 3.7 %all-to-all-start.1 = ((f32[16,8,128]{2,1,0:T(8,128)}), f32[16,8,128]{2,1,0:T(8,128)S(1)}, u32[]{:S(2)}, u32[]{:S(2)}) async-start(f32[16,8,128]{2,1,0:T(8,128)} %get-tuple-element.16), calls=%async_computation.1 | async-start | bytes 131072 | tf_op jit(solution)/shard_map/all_to_all | solution.py:398
  50.1 1.4 %join.1 = bf16[64,4096]{1,0:T(8,128)(2,1)} custom-call(s32[2]{0:T(128)S(1)} %copy-done.3, bf16[128,2048]{1,0:T(8,128)(2,1)S(1)} %get-tuple-element.17.grad_ref, bf16[64,2048]{1,0:T(8,128)(2,1)S(1)} %collective-permute-done.3.got_ref), custom_call_target="tpu_custom_call" | custom-call | bytes 1048576 | tf_op jit(solution)/shard_map/join/pallas_call | solution.py:422
  51.4 5.5 %all-to-all-done.1 = f32[16,8,128]{2,1,0:T(8,128)S(1)} async-done(((f32[16,8,128]{2,1,0:T(8,128)}), f32[16,8,128]{2,1,0:T(8,128)S(1)}, u32[]{:S(2)}, u32[]{:S(2)}) %all-to-all-start.1) | async-done | bytes 65568 | tf_op jit(solution)/shard_map/all_to_all | solution.py:398
  57.0 0.5 slice_reduce_fusion
  57.5 4.3 %weight_grad.1 = bf16[1920,2048]{1,0:T(8,128)(2,1)} custom-call(s32[2]{0:T(128)S(1)} %copy-done.3, bf16[8,16,1024]{2,1,0:T(8,128)(2,1)S(1)} %get-tuple-element.20.own_ref, bf16[8,16,1024]{2,1,0:T(8,128)(2,1)S(1)} %collective-permute-done.4.other_ref, bf16[128,2048]{1,0:T(8,128)(2,1)S(1)} %get-tuple-element.17.grad_ref), custom_call_target="tpu_custom_call" | custom-call | flops 1006632960 | bytes 8880128 | tf_op jit(solution)/shard_map/weight_grad/pallas_call | solution.py:403
  (17 shorter events, 0.1 us)
Async XLA Ops:
  0.6 9.4 %copy-start.2 = (bf16[8,1920]{1,0:T(8,128)(2,1)S(1)}, bf16[8,1920]{1,0:T(8,128)(2,1)}, u32[]{:S(2)}) copy-start(bf16[8,1920]{1,0:T(8,128)(2,1)} %hidden_ref.1) | copy-start | bytes 92164
  0.6 9.4 %collective-permute-start = (bf16[16,40960]{1,0:T(8,128)(2,1)}, bf16[16,40960]{1,0:T(8,128)(2,1)S(1)}, u32[]{:S(2)}, u32[]{:S(2)}) collective-permute-start(bf16[16,40960]{1,0:T(8,128)(2,1)} %refs_4_.1), channel_id=1, source_target_pairs={{0,1},{1,0},{2,3},{3,2},{4,5},{5,4},{6,7},{7,6},{8,9},{9,8},{10,11... | collective-permute-start | bytes 3932168 | tf_op jit(solution)/shard_map/ppermute | solution.py:284
  4.9 5.0 %copy-start.5 = (f32[2,64]{1,0:T(2,128)S(1)}, f32[2,64]{1,0:T(2,128)}, u32[]{:S(2)}) copy-start(f32[2,64]{1,0:T(2,128)} %get-tuple-element.14) | copy-start | bytes 1540
  4.9 5.0 %collective-permute-start.1 = (f32[2,64]{1,0:T(2,128)}, f32[2,64]{1,0:T(2,128)S(1)}, u32[]{:S(2)}, u32[]{:S(2)}) collective-permute-start(f32[2,64]{1,0:T(2,128)} %get-tuple-element.14), channel_id=1, source_target_pairs={{0,1},{1,0},{2,3},{3,2},{4,5},{5,4},{6,7},{7,6},{8,9},{9,8},{10,11... | collective-permute-start | bytes 1544 | tf_op jit(solution)/shard_map/ppermute | solution.py:284
  10.0 1.3 %copy-start = (f32[144,2048]{1,0:T(8,128)S(1)}, f32[144,2048]{1,0:T(8,128)}, u32[]{:S(2)}) copy-start(f32[144,2048]{1,0:T(8,128)} %get-tuple-element.13.p_ref) | copy-start | bytes 3538948
  11.3 0.9 %copy-start.1 = (bf16[144,320]{1,0:T(8,128)(2,1)S(1)}, bf16[144,320]{1,0:T(8,128)(2,1)}, u32[]{:S(2)}) copy-start(bf16[144,320]{1,0:T(8,128)(2,1)} %get-tuple-element.12.w_ref) | copy-start | bytes 276484
  16.7 7.5 %copy-start.6 = (bf16[64,2048]{1,0:T(8,128)(2,1)S(1)}, bf16[64,2048]{1,0:T(8,128)(2,1)}, u32[]{:S(2)}) copy-start(bf16[64,2048]{1,0:T(8,128)(2,1)} %get-tuple-element.15) | copy-start | bytes 786436
  16.7 9.0 %copy-start.4 = (bf16[64,4096]{1,0:T(8,128)(2,1)S(1)}, bf16[64,4096]{1,0:T(8,128)(2,1)}, u32[]{:S(2)}) copy-start(bf16[64,4096]{1,0:T(8,128)(2,1)} %logits_ref.1) | copy-start | bytes 1572868
  16.7 27.8 %all-to-all-start = ((bf16[8,16,3072]{2,1,0:T(8,128)(2,1)}), bf16[8,16,3072]{2,1,0:T(8,128)(2,1)S(1)}, u32[]{:S(2)}, u32[]{:S(2)}) async-start(bf16[8,16,3072]{2,1,0:T(8,128)(2,1)} %map_rest.1), calls=%async_computation | async-start | bytes 1572864 | tf_op jit(solution)/shard_map/all_to_all | solution.py:377
  24.2 1.6 %collective-permute-start.2 = (bf16[64,2048]{1,0:T(8,128)(2,1)S(1)}, bf16[64,2048]{1,0:T(8,128)(2,1)S(1)}, u32[]{:S(2)}, u32[]{:S(2)}) collective-permute-start(bf16[64,2048]{1,0:T(8,128)(2,1)S(1)} %copy-done.6), channel_id=1, source_target_pairs={{0,1},{1,0},{2,3},{3,2},{4,5},{5,4},{6,7},{7,6},{8,9},{9,8},{10,11... | collective-permute-start | bytes 786440 | tf_op jit(solution)/shard_map/ppermute | solution.py:284
  25.9 24.2 %copy-start.3 = (s32[2]{0:T(128)S(1)}, s32[2]{0:T(128)}, u32[]{:S(2)}) copy-start(s32[2]{0:T(128)} %pad_add_fusion.refs_0_.place_ref) | copy-start | bytes 28
  45.8 4.2 %collective-permute-start.3 = (bf16[64,2048]{1,0:T(8,128)(2,1)S(1)}, bf16[64,2048]{1,0:T(8,128)(2,1)S(1)}, u32[]{:S(2)}, u32[]{:S(2)}) collective-permute-start(bf16[64,2048]{1,0:T(8,128)(2,1)S(1)} %constant_dynamic-slice_fusion), channel_id=1, source_target_pairs={{0,1},{1,0},{2,3},{3,2},{4,5},{5,4},{6,7},{7,6},{8,9},{9,8},{10,11... | collective-permute-start | bytes 786440 | tf_op jit(solution)/shard_map/ppermute | solution.py:284
  45.9 11.6 %collective-permute-start.4 = (bf16[8,16,1024]{2,1,0:T(8,128)(2,1)S(1)}, bf16[8,16,1024]{2,1,0:T(8,128)(2,1)S(1)}, u32[]{:S(2)}, u32[]{:S(2)}) collective-permute-start(bf16[8,16,1024]{2,1,0:T(8,128)(2,1)S(1)} %get-tuple-element.20.own_ref), channel_id=1, source_target_pairs={{0,1},{1,0},{2,3},{3,2},{4,5},{5,4},{6,7},{7,6},{8,9},{9,8},{10,11... | collective-permute-start | bytes 786440 | tf_op jit(solution)/shard_map/ppermute | solution.py:284
  46.4 10.6 %all-to-all-start.1 = ((f32[16,8,128]{2,1,0:T(8,128)}), f32[16,8,128]{2,1,0:T(8,128)S(1)}, u32[]{:S(2)}, u32[]{:S(2)}) async-start(f32[16,8,128]{2,1,0:T(8,128)} %get-tuple-element.16), calls=%async_computation.1 | async-start | bytes 131072 | tf_op jit(solution)/shard_map/all_to_all | solution.py:398

commit v8 on v3

v8 whole, which is shorter than its diff:
```python
import jax
import jax.numpy as jnp
from jax import lax
from jax.experimental import pallas as pl
from jax.experimental.pallas import tpu as pltpu
from jax.sharding import PartitionSpec as P

BLK = 128
TB = 640
TOPA = 2
MASS_ROWS = 16
STEP = 16


def block_weights(row_of, weight, rows):
    row_ids = lax.broadcasted_iota(jnp.int32, (rows + MASS_ROWS, row_of.shape[1]), 0)
    total = jnp.zeros(row_ids.shape, jnp.float32)
    for slot in range(row_of.shape[0]):
        hit = (row_ids == row_of[slot][None, :]) | (row_ids == rows + slot)
        total = total + jnp.where(hit, weight[slot].astype(jnp.float32)[None, :], 0.0)
    return total.astype(jnp.bfloat16)


def column_copies(source, target, sems, first=0):
    cuts = sems.shape[0] - first
    wide = source.shape[1] // cuts
    at = [pl.ds(i * wide, wide) for i in range(cuts)]
    return [pltpu.make_async_copy(source.at[:, at[i]], target.at[:, at[i]], sems.at[first + i]) for i in range(cuts)]


def spread_tokens(t_ref, s_ref, start, count):
    tokens = t_ref.shape[0]

    def some(i, carry):
        for j in range(STEP):
            k = start + i * STEP + j
            tile = t_ref[:, pl.ds(pl.multiple_of(k * BLK, BLK), BLK)]
            s_ref[pl.ds(pl.multiple_of(k * tokens, tokens), tokens), :] = tile.astype(jnp.float32)
        return carry

    lax.fori_loop(0, count // STEP, some, 0)


def spread_arriving(copies, t_buf, s_ref):
    blocks = t_buf.shape[1] // BLK // len(copies)
    for i, copy in enumerate(copies):
        copy.wait()
        spread_tokens(t_buf, s_ref, i * blocks, blocks)


def token_pair(s_ref, t, tokens):
    count = s_ref.shape[0] // tokens
    both = [s_ref[pl.ds(t + i, count, stride=tokens), :].astype(jnp.bfloat16) for i in range(2)]
    return jnp.concatenate(both, axis=1)


def map_own_kernel(w_ref, t_ref, first_ref, o_ref, s_ref):
    tokens = t_ref.shape[0]
    spread_tokens(t_ref, s_ref, 0, t_ref.shape[1] // BLK)
    for t in range(0, tokens, 2):
        o_ref[:, t * BLK : (t + 2) * BLK] = jnp.dot(
            w_ref[...], token_pair(s_ref, t, tokens), preferred_element_type=jnp.float32
        )


def three_parts(x):
    parts = []
    for _ in range(3):
        parts.append(x.astype(jnp.bfloat16).astype(jnp.float32))
        x = x - parts[-1]
    return parts


def map_rest_kernel(w_ref, t_ref, p_ref, stats_ref, o_ref, t_buf, s_ref, m_ref, o_buf, in_sem, out_sem):
    tokens = t_ref.shape[0]
    owners = o_ref.shape[0]
    rows = w_ref.shape[0] - MASS_ROWS
    mine = rows // owners
    arriving = column_copies(t_ref, t_buf, in_sem)
    for copy in arriving:
        copy.start()
    stats = [stats_ref[0:1, :]] + three_parts(stats_ref[1:2, :])
    extra = jnp.zeros((tokens, stats_ref.shape[1]), jnp.float32)
    row_ids = lax.broadcasted_iota(jnp.int32, extra.shape, 0)
    for i, row in enumerate(stats):
        extra = jnp.where(row_ids == i, row, extra)
    extra = extra.astype(jnp.bfloat16)
    spread_arriving(arriving, t_buf, s_ref)
    for t in range(0, tokens, 2):
        both = p_ref[:, t * BLK : (t + 2) * BLK] + jnp.dot(
            w_ref[...], token_pair(s_ref, t, tokens), preferred_element_type=jnp.float32
        )
        for i in range(2):
            m_ref[pl.ds(t + i, rows + 8, stride=tokens), :] = both[: rows + 8, i * BLK : (i + 1) * BLK]
    mass = m_ref[rows * tokens : (rows + 1) * tokens, :]
    for slot in range(1, TOPA):
        mass = mass + m_ref[(rows + slot) * tokens : (rows + slot + 1) * tokens, :]
    inverse = jnp.broadcast_to(1.0 / jnp.sum(mass, axis=1, keepdims=True), (tokens, BLK))

    def leaving(q):
        return pltpu.make_async_copy(o_buf.at[q], o_ref.at[q], out_sem.at[q])

    def owner(q, carry):
        for b in range(mine):
            first = pl.multiple_of((q * mine + b) * tokens, tokens)
            tile = m_ref[pl.ds(first, tokens), :] * inverse
            o_buf[q, :, b * BLK : (b + 1) * BLK] = tile.astype(jnp.bfloat16)
        o_buf[q, :, mine * BLK :] = extra
        leaving(q).start()
        return carry

    def left(q, carry):
        leaving(q).wait()
        return carry

    lax.fori_loop(0, owners, owner, 0)
    lax.fori_loop(0, owners, left, 0)


def grad_kernel(scale, target_ref, logits_ref, grad_ref, terms_ref, row_ref):
    owners, tokens, _ = target_ref.shape
    group_tokens, width = logits_ref.shape
    stats = [target_ref[q, :, width:].astype(jnp.float32) for q in range(owners)]
    top = stats[0][0:1]
    for one in stats[1:]:
        top = jnp.maximum(top, one[0:1])
    total = jnp.zeros_like(top)
    for one in stats:
        total = total + (one[1:2] + one[2:3] + one[3:4]) * jnp.exp(one[0:1] - top)
    log_norm = top + jnp.log(total)
    for i in range(group_tokens // BLK):
        rows = slice(i * BLK, (i + 1) * BLK)
        group = slice(i * BLK // tokens, (i + 1) * BLK // tokens)
        norm = jnp.broadcast_to(log_norm[:, rows], (BLK, BLK)).T
        terms = jnp.zeros((BLK, BLK), jnp.float32)
        for b in range(width // BLK):
            lanes = slice(b * BLK, (b + 1) * BLK)
            target = target_ref[group, :, lanes].reshape(BLK, BLK).astype(jnp.float32)
            log_probs = logits_ref[rows, lanes].astype(jnp.float32) - norm
            grad_ref[rows, lanes] = ((jnp.exp(log_probs) - target) * scale).astype(jnp.bfloat16)
            positive = target > 0
            one = target * (jnp.log(jnp.where(positive, target, 1.0)) - log_probs)
            terms = terms + jnp.where(positive, one, 0.0)
        row_ref[:, rows] = jnp.sum(terms.T, axis=0, keepdims=True)
    half_tokens = group_tokens // 2
    for half in range(2):
        row = row_ref[:, half * half_tokens : (half + 1) * half_tokens]
        tile = jnp.concatenate([row] * (terms_ref.shape[2] // half_tokens), axis=1)
        for q in range(owners):
            terms_ref[2 * q + half] = jnp.broadcast_to(tile, terms_ref.shape[1:])


def join_kernel(place_ref, grad_ref, got_ref, o_ref, sem):
    half_tokens, width = got_ref.shape
    half = place_ref[1]
    kept_at = pl.ds(pl.multiple_of(half * width, width), width)
    got_at = pl.ds(pl.multiple_of((1 - half) * width, width), width)
    rows = pl.ds(pl.multiple_of(half * half_tokens, half_tokens), half_tokens)
    copies = [
        pltpu.make_async_copy(grad_ref.at[rows, :], o_ref.at[:, kept_at], sem.at[0]),
        pltpu.make_async_copy(got_ref, o_ref.at[:, got_at], sem.at[1]),
    ]
    for copy in copies:
        copy.start()
    for copy in copies:
        copy.wait()


def weight_kernel(place_ref, *refs):
    pieces, (grad_ref, o_ref, s_ref, h_ref, block_ref, sem) = refs[:-6], refs[-6:]
    count = len(pieces) // 2
    _, held, features = pieces[0].shape
    owners = s_ref.shape[0] // (2 * held)
    i = 0
    for own_ref, other_ref in zip(pieces[:count], pieces[count:]):
        for j in range(own_ref.shape[0]):
            offset = sum(((i >> bit) & 1) * (owners >> (bit + 1)) for bit in range(owners.bit_length() - 1))
            first = (place_ref[0] ^ offset) * 2
            own = pl.ds(pl.multiple_of((first + place_ref[1]) * held, held), held)
            other = pl.ds(pl.multiple_of((first + 1 - place_ref[1]) * held, held), held)
            s_ref[own, :] = own_ref[j].astype(jnp.float32)
            s_ref[other, :] = other_ref[j].astype(jnp.float32)
            i += 1
    for i in range(s_ref.shape[0] // BLK):
        for j in range(features // BLK):
            tile = s_ref[i * BLK : (i + 1) * BLK, j * BLK : (j + 1) * BLK].T
            h_ref[j * BLK : (j + 1) * BLK, i * BLK : (i + 1) * BLK] = tile.astype(jnp.bfloat16)
    steps, tile, _ = block_ref.shape
    copies = []
    for i in range(steps):
        rows = slice(i * tile, (i + 1) * tile)
        block_ref[i] = jnp.dot(
            h_ref[rows, :], grad_ref[...], preferred_element_type=jnp.float32
        ).astype(jnp.bfloat16)
        copies.append(pltpu.make_async_copy(block_ref.at[i], o_ref.at[pl.ds(i * tile, tile), :], sem.at[i]))
        copies[-1].start()
    for copy in copies:
        copy.wait()


def in_vmem():
    return pl.BlockSpec(memory_space=pltpu.VMEM)


def scalars():
    return pl.BlockSpec(memory_space=pltpu.SMEM)


def anywhere():
    return pl.BlockSpec(memory_space=pl.ANY)


def params(mib=48):
    return pltpu.CompilerParams(vmem_limit_bytes=mib << 20)


def cost(flops=0, bytes_accessed=0, transcendentals=0):
    return pl.CostEstimate(flops=flops, bytes_accessed=bytes_accessed, transcendentals=transcendentals)


def swap_halves(x):
    return lax.ppermute(x, "tv", [(0, 1), (1, 0)])


def to_partner(x, offset):
    return lax.ppermute(x, "sv", [(s, s ^ offset) for s in range(lax.axis_size("sv"))])


def body(teacher_probs, align_owner, align_local, align_weight, student_logits, hidden):
    owners = lax.axis_size("sv")
    halves = lax.axis_size("tv")
    half_index = lax.axis_index("tv")
    place = jnp.stack([lax.axis_index("sv"), half_index]).astype(jnp.int32)
    tokens = teacher_probs.shape[0]
    columns = student_logits.shape[1]
    blocks = columns // BLK
    mine = blocks // halves
    width = mine * BLK
    rows = owners * mine
    per_half = TB // halves
    group_tokens = owners * tokens
    half_tokens = student_logits.shape[0]
    features = hidden.shape[1]
    first = half_index == 0
    bf16, f32 = jnp.bfloat16, jnp.float32
    shape = jax.ShapeDtypeStruct
    dma = lambda count: pltpu.SemaphoreType.DMA((count,))

    def in_order(own, other, axis):
        return jnp.concatenate([jnp.where(first, own, other), jnp.where(first, other, own)], axis=axis)

    teacher_other = swap_halves(teacher_probs)

    hidden = hidden[None]
    offset = owners // 2
    first_piece = to_partner(hidden, offset)

    wide = student_logits.astype(f32)
    peak = jnp.max(wide, axis=1)
    sums = jnp.sum(jnp.exp(wide - peak[:, None]), axis=1)
    stats = jnp.stack([peak, sums])
    stats = in_order(stats, swap_halves(stats), 1)

    local = align_local.T - half_index * mine
    row_of = jnp.where((local >= 0) & (local < mine), align_owner.T * mine + local, -1)
    weight = align_weight.T
    cut = lambda x, which: lax.dynamic_slice_in_dim(x, which * per_half, per_half, 1)
    w_own = block_weights(cut(row_of, half_index), cut(weight, half_index), rows)
    w_rest = block_weights(cut(row_of, 1 - half_index), cut(weight, 1 - half_index), rows)
    spread = pltpu.VMEM((per_half * tokens, BLK), f32)
    flops = 2 * (rows + MASS_ROWS) * per_half * tokens * BLK
    part = pl.pallas_call(
        map_own_kernel,
        out_shape=shape((rows + MASS_ROWS, tokens * BLK), f32),
        in_specs=[in_vmem(), in_vmem(), anywhere()],
        out_specs=in_vmem(),
        scratch_shapes=[spread],
        compiler_params=params(),
        cost_estimate=cost(flops, 3 << 20),
        name="map_own",
    )(w_own, teacher_probs, first_piece)
    cuts = 4
    chunk = (owners, tokens, width + group_tokens)
    outgoing = pl.pallas_call(
        map_rest_kernel,
        out_shape=shape(chunk, bf16),
        in_specs=[in_vmem(), anywhere(), in_vmem(), in_vmem()],
        out_specs=anywhere(),
        scratch_shapes=[
            pltpu.VMEM((tokens, per_half * BLK), bf16),
            spread,
            pltpu.VMEM(((rows + 8) * tokens, BLK), f32),
            pltpu.VMEM(chunk, bf16),
            dma(cuts),
            dma(owners),
        ],
        compiler_params=params(),
        cost_estimate=cost(flops, 4 << 20),
        name="map_rest",
    )(w_rest, teacher_other, part, stats)
    target = lax.all_to_all(outgoing, "sv", 0, 0, tiled=True)

    hidden, late_logits, outgoing = lax.optimization_barrier((hidden, student_logits, outgoing))

    keep = lax.dynamic_slice_in_dim(late_logits, half_index * width, width, 1)
    give = lax.dynamic_slice_in_dim(late_logits, (1 - half_index) * width, width, 1)
    logits = in_order(keep, swap_halves(give), 0)

    pieces = [hidden, first_piece]
    while offset > 1:
        offset //= 2
        pieces.append(to_partner(jnp.concatenate(pieces), offset))

    scale = float(columns * owners)
    lanes = -(-half_tokens // BLK) * BLK
    grad, terms = pl.pallas_call(
        lambda *refs: grad_kernel(scale, *refs),
        out_shape=(
            shape((group_tokens, width), bf16),
            shape((owners * halves, 8, lanes), f32),
        ),
        in_specs=[in_vmem()] * 2,
        out_specs=[in_vmem()] * 2,
        scratch_shapes=[pltpu.VMEM((1, group_tokens), f32)],
        compiler_params=params(),
        cost_estimate=cost(
            10 * group_tokens * width, 6 * group_tokens * width, 2 * group_tokens * width
        ),
        name="logit_grad",
    )(target, logits)

    terms = lax.all_to_all(terms, ("sv", "tv"), 0, 0, tiled=True)
    give = lax.dynamic_slice_in_dim(grad, (1 - half_index) * half_tokens, half_tokens, 0)
    got = swap_halves(give)

    steps = 8
    weight_grad = pl.pallas_call(
        weight_kernel,
        out_shape=shape((features, width), bf16),
        in_specs=[scalars()] + [in_vmem()] * (2 * len(pieces) + 1),
        out_specs=anywhere(),
        scratch_shapes=[
            pltpu.VMEM((group_tokens, features), f32),
            pltpu.VMEM((features, group_tokens), bf16),
            pltpu.VMEM((steps, features // steps, width), bf16),
            dma(steps),
        ],
        compiler_params=params(),
        cost_estimate=cost(
            2 * features * group_tokens * width,
            2 * (features * width + group_tokens * (features + width)),
        ),
        name="weight_grad",
    )(place, *pieces, *[swap_halves(piece) for piece in pieces], grad)

    logit_grad = pl.pallas_call(
        join_kernel,
        out_shape=shape((half_tokens, columns), bf16),
        in_specs=[scalars(), anywhere(), anywhere()],
        out_specs=anywhere(),
        scratch_shapes=[dma(2)],
        compiler_params=params(),
        cost_estimate=cost(0, 4 * half_tokens * columns),
        name="join",
    )(place, grad, got)
    terms, logit_grad, weight_grad = lax.optimization_barrier((terms, logit_grad, weight_grad))
    divergence = jnp.sum(terms[:, 0, :half_tokens], axis=0)
    return (divergence, logit_grad, weight_grad)


def solution(mesh):
    return jax.shard_map(
        body,
        mesh=mesh,
        in_specs=(
            P(("grp", "sv"), "tv"),
            P(),
            P(),
            P(),
            P(("grp", "tv"), "sv"),
            P(("grp", "sv", "tv"), None),
        ),
        out_specs=(P(("grp", "tv")), P(("grp", "tv"), "sv"), P(None, ("grp", "sv", "tv"))),
        check_vma=False,
    )
```

time: 73.4 us -> 49.6 us (0.68)
  blocking collectives: 38.7 us -> 0 us
  waiting for transfers between devices: 4.01 us -> 12.4 us
  starting transfers between devices: 11.8 us -> 19.4 us
  local copies, waits for them, and re-layouts: 2.69 us -> 0.99 us
  Pallas kernels: 9.58 us -> 11.2 us
  other arithmetic: 5.43 us -> 4.44 us
    all_gather x1 -> x0, blocking collectives: 38.7 us -> none  [body(): hidden_own = lax.all_gather(hidden, 'sv')]
    ppermute x0 -> x3, waiting for transfers between devices: none -> 8.47 us  [to_partner(): lax.ppermute(x, 'sv', [(s, s ^ offset) for s in range(lax.axis_size('sv'))])]
    ppermute x0 -> x3, starting transfers between devices: none -> 8.02 us  [to_partner(): lax.ppermute(x, 'sv', [(s, s ^ offset) for s in range(lax.axis_size('sv'))])]
    all_to_all x1, starting transfers between devices: 7.04 us -> 3.95 us  [body(): target = lax.all_to_all(outgoing, 'sv', 0, 0, tiled=True)]
    all_to_all x1, waiting for transfers between devices: 0.01 us -> 2.76 us  [body(): target = lax.all_to_all(outgoing, 'sv', 0, 0, tiled=True)]
    all_to_all x1, starting transfers between devices: 3.47 us -> 5.64 us  [body(): terms = lax.all_to_all(terms, ('sv', 'tv'), 0, 0, tiled=True)]
    pallas_call x4 -> x5, Pallas kernels: 9.58 us -> 11.2 us  [the longest x1 4.31 us: body(): pl.pallas_call(weight_kernel, out_shape=shape((features, width), bf16), i...]
    all_to_all x1, waiting for transfers between devices: 2.66 us -> 1.11 us  [body(): terms = lax.all_to_all(terms, ('sv', 'tv'), 0, 0, tiled=True)]
  transfers between devices with their start and end apart: 7 -> 13, of which waited for: 2 -> 3; matrix products, arithmetic and copies ran while one was open for 6% -> 10% of each run, Pallas kernels for 12% -> 17%
where the time goes in v8:
time: 49.6 us; the launch traced here: 49.2 us
  starting transfers between devices  19.4 us (39%)
  waiting for transfers between devices  12.4 us (25%)
  Pallas kernels  11.2 us (23%)
  other arithmetic  4.44 us (9%)
  local copies, waits for them, and re-layouts  0.99 us (2%)
  between operations  0.84 us (2%)
    ppermute x3, waiting for transfers between devices, to_partner(): lax.ppermute(x, 'sv', [(s, s ^ offset) for s in range(lax.axis_size('sv'))])  8.47 us
    ppermute x3, starting transfers between devices, to_partner(): lax.ppermute(x, 'sv', [(s, s ^ offset) for s in range(lax.axis_size('sv'))])  8.02 us
    all_to_all x1, starting transfers between devices, body(): terms = lax.all_to_all(terms, ('sv', 'tv'), 0, 0, tiled=True)  5.64 us
    pallas_call x1, Pallas kernels, body(): pl.pallas_call(weight_kernel, out_shape=shape((features, width), bf16), i...  4.31 us
    all_to_all x1, starting transfers between devices, body(): target = lax.all_to_all(outgoing, 'sv', 0, 0, tiled=True)  3.95 us
    pallas_call x1, Pallas kernels, body(): pl.pallas_call(map_rest_kernel, out_shape=shape(chunk, bf16), in_specs=[i...  2.86 us
    all_to_all x1, waiting for transfers between devices, body(): target = lax.all_to_all(outgoing, 'sv', 0, 0, tiled=True)  2.76 us
    ppermute x8, starting transfers between devices, swap_halves(): return lax.ppermute(x, 'tv', [(0, 1), (1, 0)])  1.8 us
  transfers between devices with their start and end apart: 13, of which 3 were waited for; matrix products, arithmetic and copies ran while one was open for 10% of the time, Pallas kernels for 17%

profile of v8, /device:TPU:0, one launch (start us, length us, event | category | flops | bytes accessed | tf_op | source)
XLA Modules:
  0.0 49.2 jit_solution(7359559742570385427)
XLA Ops:
  0.6 4.1 %collective-permute-start.1 = (bf16[1,8,1920]{2,1,0:T(8,128)(2,1)}, bf16[1,8,1920]{2,1,0:T(8,128)(2,1)S(1)}, u32[]{:S(2)}, u32[]{:S(2)}) collective-permute-start(bf16[1,8,1920]{2,1,0:T(8,128)(2,1)} %bitcast.14), channel_id=1, source_target_pairs={{0,8},{2,10},{4,12},{6,14},{8,0},{10,2},{12,4},{14,6},{1,9},{3,11}... | collective-permute-start | bytes 92168 | tf_op jit(solution)/shard_map/ppermute | solution.py:226
  4.7 1.2 %reduce_max.18 = bf16[64]{0:T(256)(128)(2,1)S(1)} reduce(bf16[64,4096]{1,0:T(8,128)(2,1)} %param.10, bf16[]{:T(256)} %constant.10.clone.1), dimensions={1}, to_apply=%region_0.0 | reduce | flops 262080 | bytes 524418 | tf_op jit(solution)/shard_map/reduce_max | solution.py:259
  6.0 1.4 %exponential_reduce_fusion = f32[64]{0:T(128)S(1)} fusion(bf16[64,4096]{1,0:T(8,128)(2,1)} %param.10, f32[64]{0:T(128)S(1)} %get-tuple-element.36), kind=kLoop, calls=%fused_computation | loop fusion | flops 786368 | bytes 524800 | tf_op jit(solution)/shard_map/reduce_sum | solution.py:260
  7.5 0.5 %collective-permute-start = (bf16[16,40960]{1,0:T(8,128)(2,1)}, bf16[16,40960]{1,0:T(8,128)(2,1)S(1)}, u32[]{:S(2)}, u32[]{:S(2)}) collective-permute-start(bf16[16,40960]{1,0:T(8,128)(2,1)} %t_ref.1), channel_id=1, source_target_pairs={{0,1},{1,0},{2,3},{3,2},{4,5},{5,4},{6,7},{7,6},{8,9},{9,8},{10,11... | collective-permute-start | bytes 3932168 | tf_op jit(solution)/shard_map/ppermute | solution.py:222
  8.0 0.8 %fusion.5 = (bf16[2,320]{1,0:T(2,128)(2,1)S(1)}, bf16[2,320]{1,0:T(2,128)(2,1)S(1)}) fusion(bf16[640,2]{0,1:T(2,128)(2,1)} %param.9, s32[]{:T(128)S(6)} %select_n.63, s32[]{:T(128)S(6)} %select_n.60), kind=kLoop, calls=%fused_computation.25 | loop fusion | bytes 5128 | tf_op jit(solution)/shard_map/dynamic_slice | solution.py:267
  8.8 0.7 %and_select_fusion = s32[640,2]{0,1:T(2,128)S(1)} fusion(s32[640,2]{0,1:T(2,128)} %param.7, s32[640,2]{0,1:T(2,128)} %param.8, s32[]{:T(128)S(6)} %mul.24), kind=kLoop, calls=%fused_computation.16 | loop fusion | flops 8960 | bytes 15364 | tf_op jit(solution)/shard_map/jit(_where)/select_n | solution.py:265
  9.6 0.2 add_convert_fusion
  10.0 1.4 %map_own.1.p_ref = f32[144,2048]{1,0:T(8,128)S(1)} custom-call(bf16[144,320]{1,0:T(8,128)(2,1)S(1)} %get-tuple-element.33.w_ref, bf16[16,40960]{1,0:T(8,128)(2,1)S(1)} %copy-done, bf16[1,8,1920]{2,1,0:T(8,128)(2,1)S(1)} %collective-permute-done.1.first_ref.refs_1_), custom_call_target="tpu_custom_call" | custom-call | flops 188743680 | bytes 3145728 | tf_op jit(solution)/shard_map/map_own/pallas_call | solution.py:272
  11.4 2.9 %map_rest.1 = bf16[8,16,2176]{2,1,0:T(8,128)(2,1)} custom-call(bf16[144,320]{1,0:T(8,128)(2,1)S(1)} %get-tuple-element.34.w_ref, bf16[16,40960]{1,0:T(8,128)(2,1)S(1)} %collective-permute-done.t_ref, f32[144,2048]{1,0:T(8,128)S(1)} %map_own.1.p_ref, f32[2,128]{1,0:T(2,128)S(1)} %pad_maximum_fusion.4.stats_ref), custom_call_target="tpu_custom_call" | custom-call | flops 188743680 | bytes 4194304 | tf_op jit(solution)/shard_map/map_rest/pallas_call | solution.py:284
  14.3 4.0 %all-to-all-start = ((bf16[8,16,2176]{2,1,0:T(8,128)(2,1)}), bf16[8,16,2176]{2,1,0:T(8,128)(2,1)S(1)}, u32[]{:S(2)}, u32[]{:S(2)}) async-start(bf16[8,16,2176]{2,1,0:T(8,128)(2,1)} %map_rest.1), calls=%async_computation | async-start | bytes 1114112 | tf_op jit(solution)/shard_map/all_to_all | solution.py:301
  18.3 2.1 %collective-permute-start.5 = (bf16[2,8,1920]{2,1,0:T(8,128)(2,1)S(1)}, bf16[2,8,1920]{2,1,0:T(8,128)(2,1)S(1)}, u32[]{:S(2)}, u32[]{:S(2)}) collective-permute-start(bf16[2,8,1920]{2,1,0:T(8,128)(2,1)S(1)} %pad_maximum_fusion.2), channel_id=1, source_target_pairs={{0,4},{2,6},{4,0},{6,2},{8,12},{10,14},{12,8},{14,10},{1,5},{3,7},... | collective-permute-start | bytes 184328 | tf_op jit(solution)/shard_map/ppermute | solution.py:226
  20.4 8.5 %collective-permute-done.5.refs_2_ = bf16[2,8,1920]{2,1,0:T(8,128)(2,1)S(1)} collective-permute-done((bf16[2,8,1920]{2,1,0:T(8,128)(2,1)S(1)}, bf16[2,8,1920]{2,1,0:T(8,128)(2,1)S(1)}, u32[]{:S(2)}, u32[]{:S(2)}) %collective-permute-start.5) | collective-permute-done | bytes 61472 | tf_op jit(solution)/shard_map/ppermute | solution.py:226
  28.9 1.8 %collective-permute-start.6 = (bf16[4,8,1920]{2,1,0:T(8,128)(2,1)S(1)}, bf16[4,8,1920]{2,1,0:T(8,128)(2,1)S(1)}, u32[]{:S(2)}, u32[]{:S(2)}) collective-permute-start(bf16[4,8,1920]{2,1,0:T(8,128)(2,1)S(1)} %pad_maximum_fusion.1), channel_id=1, source_target_pairs={{0,2},{2,0},{4,6},{6,4},{8,10},{10,8},{12,14},{14,12},{1,3},{3,1},... | collective-permute-start | bytes 368648 | tf_op jit(solution)/shard_map/ppermute | solution.py:226
  30.8 0.1 broadcast_select_fusion.1
  30.9 2.8 %all-to-all-done.refs_0_ = bf16[8,16,2176]{2,1,0:T(8,128)(2,1)S(1)} async-done(((bf16[8,16,2176]{2,1,0:T(8,128)(2,1)}), bf16[8,16,2176]{2,1,0:T(8,128)(2,1)S(1)}, u32[]{:S(2)}, u32[]{:S(2)}) %all-to-all-start) | async-done | bytes 557088 | tf_op jit(solution)/shard_map/all_to_all | solution.py:301
  33.7 1.2 %logit_grad.1 = (bf16[128,2048]{1,0:T(8,128)(2,1)S(1)}, f32[16,8,128]{2,1,0:T(8,128)}) custom-call(bf16[8,16,2176]{2,1,0:T(8,128)(2,1)S(1)} %all-to-all-done.refs_0_, bf16[128,2048]{1,0:T(8,128)(2,1)S(1)} %pad_maximum_fusion.refs_1_), custom_call_target="tpu_custom_call" | custom-call | flops 2621440 | bytes 1572864 | tf_op jit(solution)/shard_map/logit_grad/pallas_call | solution.py:316
  35.0 0.5 collective-permute-start.10
  35.5 0.1 collective-permute-start.8
  35.6 0.4 collective-permute-start.7
  36.1 5.6 %all-to-all-start.1 = ((f32[16,8,128]{2,1,0:T(8,128)}), f32[16,8,128]{2,1,0:T(8,128)S(1)}, u32[]{:S(2)}, u32[]{:S(2)}) async-start(f32[16,8,128]{2,1,0:T(8,128)} %get-tuple-element.11), calls=%async_computation.1 | async-start | bytes 131072 | tf_op jit(solution)/shard_map/all_to_all | solution.py:332
  41.8 4.3 %weight_grad.1 = bf16[1920,2048]{1,0:T(8,128)(2,1)} custom-call(s32[2]{0:T(128)S(1)} %pad_add_fusion.place_ref, bf16[1,8,1920]{2,1,0:T(8,128)(2,1)S(1)} %bitcast.18, bf16[1,8,1920]{2,1,0:T(8,128)(2,1)S(1)} %collective-permute-done.1.first_ref.refs_1_, bf16[2,8,1920]{2,1,0:T(8,128)(2,1)S(1)} %collective-permute-done.5.refs_2_, ...), custom_call_target="tpu_custom_call" | custom-call | flops 1006632960 | bytes 8880128 | tf_op jit(solution)/shard_map/weight_grad/pallas_call | solution.py:337
  46.2 1.4 %join.1 = bf16[64,4096]{1,0:T(8,128)(2,1)} custom-call(s32[2]{0:T(128)S(1)} %pad_add_fusion.place_ref, bf16[128,2048]{1,0:T(8,128)(2,1)S(1)} %get-tuple-element.12.grad_ref.refs_8_, bf16[64,2048]{1,0:T(8,128)(2,1)S(1)} %collective-permute-done.4.got_ref), custom_call_target="tpu_custom_call" | custom-call | bytes 1048576 | tf_op jit(solution)/shard_map/join/pallas_call | solution.py:356
  47.5 1.1 %all-to-all-done.1 = f32[16,8,128]{2,1,0:T(8,128)S(1)} async-done(((f32[16,8,128]{2,1,0:T(8,128)}), f32[16,8,128]{2,1,0:T(8,128)S(1)}, u32[]{:S(2)}, u32[]{:S(2)}) %all-to-all-start.1) | async-done | bytes 65568 | tf_op jit(solution)/shard_map/all_to_all | solution.py:332
  48.6 0.5 %slice_reduce_fusion = f32[64]{0:T(128)} fusion(f32[16,8,128]{2,1,0:T(8,128)S(1)} %all-to-all-done.1), kind=kLoop, calls=%fused_computation.17 | loop fusion | flops 960 | bytes 4352 | tf_op jit(solution)/shard_map/reduce_sum | solution.py:367
  (34 shorter events, 0.8 us)
Async XLA Ops:
  0.6 9.3 %copy-start = (bf16[16,40960]{1,0:T(8,128)(2,1)S(1)}, bf16[16,40960]{1,0:T(8,128)(2,1)}, u32[]{:S(2)}) copy-start(bf16[16,40960]{1,0:T(8,128)(2,1)} %t_ref.1) | copy-start | bytes 3932164
  0.6 9.3 %collective-permute-start.1 = (bf16[1,8,1920]{2,1,0:T(8,128)(2,1)}, bf16[1,8,1920]{2,1,0:T(8,128)(2,1)S(1)}, u32[]{:S(2)}, u32[]{:S(2)}) collective-permute-start(bf16[1,8,1920]{2,1,0:T(8,128)(2,1)} %bitcast.14), channel_id=1, source_target_pairs={{0,8},{2,10},{4,12},{6,14},{8,0},{10,2},{12,4},{14,6},{1,9},{3,11}... | collective-permute-start | bytes 92168 | tf_op jit(solution)/shard_map/ppermute | solution.py:226
  7.4 2.5 %collective-permute-start.2 = (f32[2,64]{1,0:T(2,128)S(1)}, f32[2,64]{1,0:T(2,128)S(1)}, u32[]{:S(2)}, u32[]{:S(2)}) collective-permute-start(f32[2,64]{1,0:T(2,128)S(1)} %pad_maximum_fusion.3), channel_id=1, source_target_pairs={{0,1},{1,0},{2,3},{3,2},{4,5},{5,4},{6,7},{7,6},{8,9},{9,8},{10,11... | collective-permute-start | bytes 1544 | tf_op jit(solution)/shard_map/ppermute | solution.py:222
  7.5 3.9 %collective-permute-start = (bf16[16,40960]{1,0:T(8,128)(2,1)}, bf16[16,40960]{1,0:T(8,128)(2,1)S(1)}, u32[]{:S(2)}, u32[]{:S(2)}) collective-permute-start(bf16[16,40960]{1,0:T(8,128)(2,1)} %t_ref.1), channel_id=1, source_target_pairs={{0,1},{1,0},{2,3},{3,2},{4,5},{5,4},{6,7},{7,6},{8,9},{9,8},{10,11... | collective-permute-start | bytes 3932168 | tf_op jit(solution)/shard_map/ppermute | solution.py:222
  11.4 6.8 %copy-start.1 = (bf16[8,1920]{1,0:T(8,128)(2,1)S(1)}, bf16[8,1920]{1,0:T(8,128)(2,1)}, u32[]{:S(2)}) copy-start(bf16[8,1920]{1,0:T(8,128)(2,1)} %param.11) | copy-start | bytes 92164
  14.3 6.1 %copy-start.2 = (bf16[64,4096]{1,0:T(8,128)(2,1)S(1)}, bf16[64,4096]{1,0:T(8,128)(2,1)}, u32[]{:S(2)}) copy-start(bf16[64,4096]{1,0:T(8,128)(2,1)} %param.10) | copy-start | bytes 1572868
  14.3 19.4 %all-to-all-start = ((bf16[8,16,2176]{2,1,0:T(8,128)(2,1)}), bf16[8,16,2176]{2,1,0:T(8,128)(2,1)S(1)}, u32[]{:S(2)}, u32[]{:S(2)}) async-start(bf16[8,16,2176]{2,1,0:T(8,128)(2,1)} %map_rest.1), calls=%async_computation | async-start | bytes 1114112 | tf_op jit(solution)/shard_map/all_to_all | solution.py:301
  18.3 10.6 %collective-permute-start.5 = (bf16[2,8,1920]{2,1,0:T(8,128)(2,1)S(1)}, bf16[2,8,1920]{2,1,0:T(8,128)(2,1)S(1)}, u32[]{:S(2)}, u32[]{:S(2)}) collective-permute-start(bf16[2,8,1920]{2,1,0:T(8,128)(2,1)S(1)} %pad_maximum_fusion.2), channel_id=1, source_target_pairs={{0,4},{2,6},{4,0},{6,2},{8,12},{10,14},{12,8},{14,10},{1,5},{3,7},... | collective-permute-start | bytes 184328 | tf_op jit(solution)/shard_map/ppermute | solution.py:226
  20.4 10.4 %collective-permute-start.3 = (bf16[64,2048]{1,0:T(8,128)(2,1)S(1)}, bf16[64,2048]{1,0:T(8,128)(2,1)S(1)}, u32[]{:S(2)}, u32[]{:S(2)}) collective-permute-start(bf16[64,2048]{1,0:T(8,128)(2,1)S(1)} %constant_dynamic-slice_fusion.1), channel_id=1, source_target_pairs={{0,1},{1,0},{2,3},{3,2},{4,5},{5,4},{6,7},{7,6},{8,9},{9,8},{10,11... | collective-permute-start | bytes 786440 | tf_op jit(solution)/shard_map/ppermute | solution.py:222
  28.9 6.1 %collective-permute-start.6 = (bf16[4,8,1920]{2,1,0:T(8,128)(2,1)S(1)}, bf16[4,8,1920]{2,1,0:T(8,128)(2,1)S(1)}, u32[]{:S(2)}, u32[]{:S(2)}) collective-permute-start(bf16[4,8,1920]{2,1,0:T(8,128)(2,1)S(1)} %pad_maximum_fusion.1), channel_id=1, source_target_pairs={{0,2},{2,0},{4,6},{6,4},{8,10},{10,8},{12,14},{14,12},{1,3},{3,1},... | collective-permute-start | bytes 368648 | tf_op jit(solution)/shard_map/ppermute | solution.py:226
  34.9 11.2 %collective-permute-start.4 = (bf16[64,2048]{1,0:T(8,128)(2,1)S(1)}, bf16[64,2048]{1,0:T(8,128)(2,1)S(1)}, u32[]{:S(2)}, u32[]{:S(2)}) collective-permute-start(bf16[64,2048]{1,0:T(8,128)(2,1)S(1)} %constant_dynamic-slice_fusion), channel_id=1, source_target_pairs={{0,1},{1,0},{2,3},{3,2},{4,5},{5,4},{6,7},{7,6},{8,9},{9,8},{10,11... | collective-permute-start | bytes 786440 | tf_op jit(solution)/shard_map/ppermute | solution.py:222
  35.0 6.8 %collective-permute-start.10 = (bf16[4,8,1920]{2,1,0:T(8,128)(2,1)S(1)}, bf16[4,8,1920]{2,1,0:T(8,128)(2,1)S(1)}, u32[]{:S(2)}, u32[]{:S(2)}) collective-permute-start(bf16[4,8,1920]{2,1,0:T(8,128)(2,1)S(1)} %collective-permute-done.6.refs_3_), channel_id=1, source_target_pairs={{0,1},{1,0},{2,3},{3,2},{4,5},{5,4},{6,7},{7,6},{8,9},{9,8},{10,11... | collective-permute-start | bytes 368648 | tf_op jit(solution)/shard_map/ppermute | solution.py:222
  35.5 6.3 %collective-permute-start.8 = (bf16[1,8,1920]{2,1,0:T(8,128)(2,1)S(1)}, bf16[1,8,1920]{2,1,0:T(8,128)(2,1)S(1)}, u32[]{:S(2)}, u32[]{:S(2)}) collective-permute-start(bf16[1,8,1920]{2,1,0:T(8,128)(2,1)S(1)} %collective-permute-done.1.first_ref.refs_1_), channel_id=1, source_target_pairs={{0,1},{1,0},{2,3},{3,2},{4,5},{5,4},{6,7},{7,6},{8,9},{9,8},{10,11... | collective-permute-start | bytes 92168 | tf_op jit(solution)/shard_map/ppermute | solution.py:222
  35.6 6.2 %collective-permute-start.7 = (bf16[1,8,1920]{2,1,0:T(8,128)(2,1)S(1)}, bf16[1,8,1920]{2,1,0:T(8,128)(2,1)S(1)}, u32[]{:S(2)}, u32[]{:S(2)}) collective-permute-start(bf16[1,8,1920]{2,1,0:T(8,128)(2,1)S(1)} %bitcast.17), channel_id=1, source_target_pairs={{0,1},{1,0},{2,3},{3,2},{4,5},{5,4},{6,7},{7,6},{8,9},{9,8},{10,11... | collective-permute-start | bytes 92168 | tf_op jit(solution)/shard_map/ppermute | solution.py:222
  36.0 5.8 %collective-permute-start.9 = (bf16[2,8,1920]{2,1,0:T(8,128)(2,1)S(1)}, bf16[2,8,1920]{2,1,0:T(8,128)(2,1)S(1)}, u32[]{:S(2)}, u32[]{:S(2)}) collective-permute-start(bf16[2,8,1920]{2,1,0:T(8,128)(2,1)S(1)} %collective-permute-done.5.refs_2_), channel_id=1, source_target_pairs={{0,1},{1,0},{2,3},{3,2},{4,5},{5,4},{6,7},{7,6},{8,9},{9,8},{10,11... | collective-permute-start | bytes 184328 | tf_op jit(solution)/shard_map/ppermute | solution.py:222
  36.1 12.5 %all-to-all-start.1 = ((f32[16,8,128]{2,1,0:T(8,128)}), f32[16,8,128]{2,1,0:T(8,128)S(1)}, u32[]{:S(2)}, u32[]{:S(2)}) async-start(f32[16,8,128]{2,1,0:T(8,128)} %get-tuple-element.11), calls=%async_computation.1 | async-start | bytes 131072 | tf_op jit(solution)/shard_map/all_to_all | solution.py:332

commit v9 on v8

v9 whole, which is shorter than its diff:
```python
import jax
import jax.numpy as jnp
from jax import lax
from jax.experimental import pallas as pl
from jax.experimental.pallas import tpu as pltpu
from jax.sharding import PartitionSpec as P

BLK = 128
TB = 640
TOPA = 2
MASS_ROWS = 16
STEP = 16


def block_weights(place_ref, table_ref, which, rows, mine):
    count = table_ref.shape[1] // 2
    table = jnp.where(which == 0, table_ref[:, :count], table_ref[:, count:])
    owner, local, weight = (table[i * TOPA : (i + 1) * TOPA] for i in range(3))
    local = local.astype(jnp.int32) - place_ref[1] * mine
    row_of = jnp.where((local >= 0) & (local < mine), owner.astype(jnp.int32) * mine + local, -1)
    row_ids = lax.broadcasted_iota(jnp.int32, (rows + MASS_ROWS, count), 0)
    total = jnp.zeros(row_ids.shape, jnp.float32)
    for slot in range(TOPA):
        hit = (row_ids == row_of[slot : slot + 1]) | (row_ids == rows + slot)
        total = total + jnp.where(hit, weight[slot : slot + 1], 0.0)
    return total.astype(jnp.bfloat16)


def column_copies(source, target, sems, first=0):
    cuts = sems.shape[0] - first
    wide = source.shape[1] // cuts
    at = [pl.ds(i * wide, wide) for i in range(cuts)]
    return [pltpu.make_async_copy(source.at[:, at[i]], target.at[:, at[i]], sems.at[first + i]) for i in range(cuts)]


def spread_tokens(t_ref, s_ref, start, count):
    tokens = t_ref.shape[0]

    def some(i, carry):
        for j in range(STEP):
            k = start + i * STEP + j
            tile = t_ref[:, pl.ds(pl.multiple_of(k * BLK, BLK), BLK)]
            s_ref[pl.ds(pl.multiple_of(k * tokens, tokens), tokens), :] = tile.astype(jnp.float32)
        return carry

    lax.fori_loop(0, count // STEP, some, 0)


def spread_arriving(copies, t_buf, s_ref):
    blocks = t_buf.shape[1] // BLK // len(copies)
    for i, copy in enumerate(copies):
        copy.wait()
        spread_tokens(t_buf, s_ref, i * blocks, blocks)


def token_pair(s_ref, t, tokens):
    count = s_ref.shape[0] // tokens
    both = [s_ref[pl.ds(t + i, count, stride=tokens), :].astype(jnp.bfloat16) for i in range(2)]
    return jnp.concatenate(both, axis=1)


def map_own_kernel(mine, place_ref, table_ref, t_ref, first_ref, o_ref, s_ref):
    tokens = t_ref.shape[0]
    weights = block_weights(place_ref, table_ref, place_ref[1], o_ref.shape[0] - MASS_ROWS, mine)
    spread_tokens(t_ref, s_ref, 0, t_ref.shape[1] // BLK)
    for t in range(0, tokens, 2):
        o_ref[:, t * BLK : (t + 2) * BLK] = jnp.dot(
            weights, token_pair(s_ref, t, tokens), preferred_element_type=jnp.float32
        )


def three_parts(x):
    parts = []
    for _ in range(3):
        parts.append(x.astype(jnp.bfloat16).astype(jnp.float32))
        x = x - parts[-1]
    return parts


def map_rest_kernel(mine, place_ref, table_ref, t_ref, p_ref, stats_ref, *refs):
    o_refs, (t_buf, s_ref, m_ref, in_sem) = refs[:-4], refs[-4:]
    tokens = t_ref.shape[0]
    rows = p_ref.shape[0] - MASS_ROWS
    arriving = column_copies(t_ref, t_buf, in_sem)
    for copy in arriving:
        copy.start()
    weights = block_weights(place_ref, table_ref, 1 - place_ref[1], rows, mine)
    stats = [stats_ref[0:1, :]] + three_parts(stats_ref[1:2, :])
    extra = jnp.zeros((tokens, stats_ref.shape[1]), jnp.float32)
    row_ids = lax.broadcasted_iota(jnp.int32, extra.shape, 0)
    for i, row in enumerate(stats):
        extra = jnp.where(row_ids == i, row, extra)
    extra = extra.astype(jnp.bfloat16)
    spread_arriving(arriving, t_buf, s_ref)
    for t in range(0, tokens, 2):
        both = p_ref[:, t * BLK : (t + 2) * BLK] + jnp.dot(
            weights, token_pair(s_ref, t, tokens), preferred_element_type=jnp.float32
        )
        for i in range(2):
            m_ref[pl.ds(t + i, rows + 8, stride=tokens), :] = both[: rows + 8, i * BLK : (i + 1) * BLK]
    mass = m_ref[rows * tokens : (rows + 1) * tokens, :]
    for slot in range(1, TOPA):
        mass = mass + m_ref[(rows + slot) * tokens : (rows + slot + 1) * tokens, :]
    inverse = jnp.broadcast_to(1.0 / jnp.sum(mass, axis=1, keepdims=True), (tokens, BLK))
    for offset, o_ref in enumerate(o_refs):
        owner = place_ref[0] ^ offset
        for b in range(mine):
            first = pl.multiple_of((owner * mine + b) * tokens, tokens)
            tile = m_ref[pl.ds(first, tokens), :] * inverse
            o_ref[:, b * BLK : (b + 1) * BLK] = tile.astype(jnp.bfloat16)
        o_ref[:, mine * BLK :] = extra


def grad_kernel(scale, place_ref, logits_ref, *refs):
    target_refs, (grad_ref, terms_ref, norm_ref, sum_ref, t_buf, sem) = refs[:-6], refs[-6:]
    tokens = target_refs[0].shape[0]
    group_tokens, width = logits_ref.shape
    stats = [ref[:, width:].astype(jnp.float32) for ref in target_refs]
    top = stats[0][0:1]
    for one in stats[1:]:
        top = jnp.maximum(top, one[0:1])
    total = jnp.zeros_like(top)
    for one in stats:
        total = total + (one[1:2] + one[2:3] + one[3:4]) * jnp.exp(one[0:1] - top)
    log_norm = top + jnp.log(total)
    for i in range(0, group_tokens, BLK):
        norm_ref[i : i + BLK, :] = jnp.broadcast_to(log_norm[:, i : i + BLK], (BLK, BLK)).T
    per = BLK // tokens
    at = [pl.ds(pl.multiple_of((place_ref[0] ^ a) * tokens, tokens), tokens) for a in range(len(target_refs))]

    def block(i, b):
        lanes = slice(b * BLK, (b + 1) * BLK)
        some = range(i * per, (i + 1) * per)
        target = jnp.concatenate([target_refs[a][:, lanes] for a in some], axis=0).astype(jnp.float32)
        logits = jnp.concatenate([logits_ref[at[a], lanes] for a in some], axis=0).astype(jnp.float32)
        return target, logits

    norms = []
    for i in range(group_tokens // BLK):
        norms.append(jnp.concatenate([norm_ref[at[a], :] for a in range(i * per, (i + 1) * per)], axis=0))
        terms = jnp.zeros((BLK, BLK), jnp.float32)
        for b in range(width // BLK):
            target, logits = block(i, b)
            positive = target > 0
            one = target * (jnp.log(jnp.where(positive, target, 1.0)) - (logits - norms[i]))
            terms = terms + jnp.where(positive, one, 0.0)
        for j in range(per):
            sum_ref[at[i * per + j], :] = terms[j * tokens : (j + 1) * tokens]
    owners, half_tokens = len(target_refs), group_tokens // 2
    row = jnp.concatenate(
        [jnp.sum(sum_ref[i : i + BLK, :].T, axis=0, keepdims=True) for i in range(0, group_tokens, BLK)], axis=1
    )
    for half in range(2):
        mine = row[:, half * half_tokens : (half + 1) * half_tokens]
        tile = jnp.concatenate([mine] * (t_buf.shape[2] // half_tokens), axis=1)
        for q in range(owners):
            t_buf[2 * q + half] = jnp.broadcast_to(tile, t_buf.shape[1:])
    leaving = pltpu.make_async_copy(t_buf, terms_ref, sem)
    leaving.start()
    for i in range(group_tokens // BLK):
        for b in range(width // BLK):
            target, logits = block(i, b)
            grad = (jnp.exp(logits - norms[i]) - target) * scale
            grad_ref[i * BLK : (i + 1) * BLK, b * BLK : (b + 1) * BLK] = grad.astype(jnp.bfloat16)
    leaving.wait()


def join_kernel(place_ref, grad_ref, got_ref, o_ref, sem):
    half_tokens, width = got_ref.shape
    count = sem.shape[0] // 2
    tokens = half_tokens // count
    owner, half = place_ref[0], place_ref[1]
    kept_at = pl.ds(pl.multiple_of(half * width, width), width)
    got_at = pl.ds(pl.multiple_of((1 - half) * width, width), width)
    kept = ((owner // count) ^ half) * half_tokens
    copies = []
    for j in range(count):
        to = pl.ds(pl.multiple_of(((owner % count) ^ j) * tokens, tokens), tokens)
        here = pl.ds(pl.multiple_of(kept + j * tokens, tokens), tokens)
        there = pl.ds(j * tokens, tokens)
        copies.append(pltpu.make_async_copy(grad_ref.at[here, :], o_ref.at[to, kept_at], sem.at[2 * j]))
        copies.append(pltpu.make_async_copy(got_ref.at[there, :], o_ref.at[to, got_at], sem.at[2 * j + 1]))
    for copy in copies:
        copy.start()
    for copy in copies:
        copy.wait()


def arrival_order(owners):
    bits = owners.bit_length() - 1
    return [sum(((i >> bit) & 1) * (owners >> (bit + 1)) for bit in range(bits)) for i in range(owners)]


def weight_kernel(place_ref, own_ref, other_ref, grad_ref, o_ref, s_ref, h_ref, block_ref, sem):
    owners, held, features = own_ref.shape
    for i, offset in enumerate(arrival_order(owners)):
        own = pl.ds(pl.multiple_of((offset * 2 + place_ref[1]) * held, held), held)
        other = pl.ds(pl.multiple_of((offset * 2 + 1 - place_ref[1]) * held, held), held)
        s_ref[own, :] = own_ref[i].astype(jnp.float32)
        s_ref[other, :] = other_ref[i].astype(jnp.float32)
    for i in range(s_ref.shape[0] // BLK):
        for j in range(features // BLK):
            tile = s_ref[i * BLK : (i + 1) * BLK, j * BLK : (j + 1) * BLK].T
            h_ref[j * BLK : (j + 1) * BLK, i * BLK : (i + 1) * BLK] = tile.astype(jnp.bfloat16)
    steps, tile, _ = block_ref.shape
    copies = []
    for i in range(steps):
        rows = slice(i * tile, (i + 1) * tile)
        block_ref[i] = jnp.dot(
            h_ref[rows, :], grad_ref[...], preferred_element_type=jnp.float32
        ).astype(jnp.bfloat16)
        copies.append(pltpu.make_async_copy(block_ref.at[i], o_ref.at[pl.ds(i * tile, tile), :], sem.at[i]))
        copies[-1].start()
    for copy in copies:
        copy.wait()


def in_vmem():
    return pl.BlockSpec(memory_space=pltpu.VMEM)


def scalars():
    return pl.BlockSpec(memory_space=pltpu.SMEM)


def anywhere():
    return pl.BlockSpec(memory_space=pl.ANY)


def params(mib=48):
    return pltpu.CompilerParams(vmem_limit_bytes=mib << 20)


def cost(flops=0, bytes_accessed=0, transcendentals=0):
    return pl.CostEstimate(flops=flops, bytes_accessed=bytes_accessed, transcendentals=transcendentals)


def swap_halves(x):
    return lax.ppermute(x, "tv", [(0, 1), (1, 0)])


def to_partner(x, offset):
    return lax.ppermute(x, "sv", [(s, s ^ offset) for s in range(lax.axis_size("sv"))])


def body(teacher_probs, align_owner, align_local, align_weight, student_logits, hidden):
    owners = lax.axis_size("sv")
    halves = lax.axis_size("tv")
    half_index = lax.axis_index("tv")
    place = jnp.stack([lax.axis_index("sv"), half_index]).astype(jnp.int32)
    tokens = teacher_probs.shape[0]
    columns = student_logits.shape[1]
    blocks = columns // BLK
    mine = blocks // halves
    width = mine * BLK
    rows = owners * mine
    per_half = TB // halves
    group_tokens = owners * tokens
    half_tokens = student_logits.shape[0]
    features = hidden.shape[1]
    first = half_index == 0
    bf16, f32 = jnp.bfloat16, jnp.float32
    shape = jax.ShapeDtypeStruct
    dma = lambda count: pltpu.SemaphoreType.DMA((count,))

    def in_order(own, other, axis):
        return jnp.concatenate([jnp.where(first, own, other), jnp.where(first, other, own)], axis=axis)

    teacher_other = swap_halves(teacher_probs)

    hidden = hidden[None]
    offset = owners // 2
    first_piece = to_partner(hidden, offset)

    def merge(one, two):
        top = jnp.maximum(one[0], two[0])
        return top, one[1] * jnp.exp(one[0] - top) + two[1] * jnp.exp(two[0] - top)

    wide = student_logits.astype(f32)
    low = jnp.float32(-1e38)
    stats = jnp.stack(lax.reduce((wide, jnp.ones_like(wide)), (low, jnp.float32(0)), merge, (1,)))
    stats = in_order(stats, swap_halves(stats), 1)

    tables = jnp.concatenate([x.T.astype(f32) for x in (align_owner, align_local, align_weight)])
    spread = pltpu.VMEM((per_half * tokens, BLK), f32)
    flops = 2 * (rows + MASS_ROWS) * per_half * tokens * BLK
    part = pl.pallas_call(
        lambda *refs: map_own_kernel(mine, *refs),
        out_shape=shape((rows + MASS_ROWS, tokens * BLK), f32),
        in_specs=[scalars(), in_vmem(), in_vmem(), anywhere()],
        out_specs=in_vmem(),
        scratch_shapes=[spread],
        compiler_params=params(),
        cost_estimate=cost(flops, 3 << 20),
        name="map_own",
    )(place, tables, teacher_probs, first_piece)
    cuts = 4
    outgoing = pl.pallas_call(
        lambda *refs: map_rest_kernel(mine, *refs),
        out_shape=[shape((tokens, width + group_tokens), bf16)] * owners,
        in_specs=[scalars(), in_vmem(), anywhere(), in_vmem(), in_vmem()],
        out_specs=[in_vmem()] * owners,
        scratch_shapes=[
            pltpu.VMEM((tokens, per_half * BLK), bf16),
            spread,
            pltpu.VMEM(((rows + 8) * tokens, BLK), f32),
            dma(cuts),
        ],
        compiler_params=params(),
        cost_estimate=cost(flops, 4 << 20),
        name="map_rest",
    )(place, tables, teacher_other, part, stats)
    targets = dict(enumerate(outgoing))
    for a in [*range(owners // 2, owners), *range(1, owners // 2)]:
        targets[a] = to_partner(outgoing[a], a)

    late_logits, _ = lax.optimization_barrier((student_logits, outgoing[0]))
    hidden, _ = lax.optimization_barrier((hidden, targets[owners // 2]))

    keep = lax.dynamic_slice_in_dim(late_logits, half_index * width, width, 1)
    give = lax.dynamic_slice_in_dim(late_logits, (1 - half_index) * width, width, 1)
    logits = in_order(keep, swap_halves(give), 0)

    hidden_own = jnp.concatenate([hidden, first_piece])
    while offset > 1:
        offset //= 2
        hidden_own = jnp.concatenate([hidden_own, to_partner(hidden_own, offset)])

    scale = float(columns * owners)
    lanes = -(-half_tokens // BLK) * BLK
    grad, terms = pl.pallas_call(
        lambda *refs: grad_kernel(scale, *refs),
        out_shape=(shape((group_tokens, width), bf16), shape((owners * halves, 8, lanes), f32)),
        in_specs=[scalars()] + [in_vmem()] * (owners + 1),
        out_specs=(in_vmem(), anywhere()),
        scratch_shapes=[
            pltpu.VMEM((group_tokens, BLK), f32),
            pltpu.VMEM((group_tokens, BLK), f32),
            pltpu.VMEM((owners * halves, 8, lanes), f32),
            pltpu.SemaphoreType.DMA,
        ],
        compiler_params=params(),
        cost_estimate=cost(
            10 * group_tokens * width, 6 * group_tokens * width, 2 * group_tokens * width
        ),
        name="logit_grad",
    )(place, logits, *[targets[a] for a in range(owners)])

    terms = lax.all_to_all(terms, ("sv", "tv"), 0, 0, tiled=True)
    count = half_tokens // tokens
    given = (lax.axis_index("sv") // count) ^ (1 - half_index)
    give = lax.dynamic_slice_in_dim(grad, given * half_tokens, half_tokens, 0)
    got = swap_halves(give)

    steps = 8
    weight_grad = pl.pallas_call(
        weight_kernel,
        out_shape=shape((features, width), bf16),
        in_specs=[scalars()] + [in_vmem()] * 3,
        out_specs=anywhere(),
        scratch_shapes=[
            pltpu.VMEM((group_tokens, features), f32),
            pltpu.VMEM((features, group_tokens), bf16),
            pltpu.VMEM((steps, features // steps, width), bf16),
            dma(steps),
        ],
        compiler_params=params(),
        cost_estimate=cost(
            2 * features * group_tokens * width,
            2 * (features * width + group_tokens * (features + width)),
        ),
        name="weight_grad",
    )(place, hidden_own, swap_halves(hidden_own), grad)

    logit_grad = pl.pallas_call(
        join_kernel,
        out_shape=shape((half_tokens, columns), bf16),
        in_specs=[scalars(), anywhere(), anywhere()],
        out_specs=anywhere(),
        scratch_shapes=[dma(2 * count)],
        compiler_params=params(),
        cost_estimate=cost(0, 4 * half_tokens * columns),
        name="join",
    )(place, grad, got)
    terms, logit_grad, weight_grad = lax.optimization_barrier((terms, logit_grad, weight_grad))
    divergence = jnp.sum(terms[:, 0, :half_tokens], axis=0)
    return (divergence, logit_grad, weight_grad)


def solution(mesh):
    return jax.shard_map(
        body,
        mesh=mesh,
        in_specs=(
            P(("grp", "sv"), "tv"),
            P(),
            P(),
            P(),
            P(("grp", "tv"), "sv"),
            P(("grp", "sv", "tv"), None),
        ),
        out_specs=(P(("grp", "tv")), P(("grp", "tv"), "sv"), P(None, ("grp", "sv", "tv"))),
        check_vma=False,
    )
```

time: 49.6 us -> 58 us (1.17)
  starting transfers between devices: 19.4 us -> 23.4 us
  waiting for transfers between devices: 12.4 us -> 15.7 us
  Pallas kernels: 11.2 us -> 12.5 us
  other arithmetic: 4.44 us -> 3.85 us
    ppermute x3 -> x10, starting transfers between devices: 8.02 us -> 18.6 us  [to_partner(): lax.ppermute(x, 'sv', [(s, s ^ offset) for s in range(lax.axis_size('sv'))])]
    ppermute x3 -> x10, waiting for transfers between devices: 8.47 us -> 14.5 us  [to_partner(): lax.ppermute(x, 'sv', [(s, s ^ offset) for s in range(lax.axis_size('sv'))])]
    all_to_all x1 -> x0, starting transfers between devices: 3.95 us -> none  [body(): target = lax.all_to_all(outgoing, 'sv', 0, 0, tiled=True)]
    all_to_all x1 -> x0, waiting for transfers between devices: 2.76 us -> none  [body(): target = lax.all_to_all(outgoing, 'sv', 0, 0, tiled=True)]
    all_to_all x1, starting transfers between devices: 5.64 us -> 3.94 us  [body(): terms = lax.all_to_all(terms, ('sv', 'tv'), 0, 0, tiled=True)]
    another operation x1 -> x2, other arithmetic: 0.01 us -> 1.58 us  [the longest x1 1.57 us: body(): lax.reduce((wide, jnp.ones_like(wide)), (low, jnp.float32(0)), merge, (1,))]
    reduce_sum x1 -> x0, other arithmetic: 1.39 us -> none  [body(): sums = jnp.sum(jnp.exp(wide - peak[:, None]), axis=1)]
    unnamed x6 -> x9, local copies, waits for them, and re-layouts: 0.02 us -> 1.35 us
  transfers between devices with their start and end apart: 13 -> 16, of which waited for: 3 -> 6; matrix products, arithmetic and copies ran while one was open for 10% -> 6% of each run, Pallas kernels for 17% -> 17%
where the time goes in v9:
time: 58 us; the launch traced here: 57.6 us
  starting transfers between devices  23.4 us (40%)
  waiting for transfers between devices  15.7 us (27%)
  Pallas kernels  12.5 us (22%)
  other arithmetic  3.85 us (7%)
  local copies, waits for them, and re-layouts  1.41 us (2%)
  between operations  0.86 us (1%)
    ppermute x10, starting transfers between devices, to_partner(): lax.ppermute(x, 'sv', [(s, s ^ offset) for s in range(lax.axis_size('sv'))])  18.6 us
    ppermute x10, waiting for transfers between devices, to_partner(): lax.ppermute(x, 'sv', [(s, s ^ offset) for s in range(lax.axis_size('sv'))])  14.5 us
    pallas_call x1, Pallas kernels, body(): pl.pallas_call(weight_kernel, out_shape=shape((features, width), bf16), i...  4.3 us
    all_to_all x1, starting transfers between devices, body(): terms = lax.all_to_all(terms, ('sv', 'tv'), 0, 0, tiled=True)  3.94 us
    pallas_call x1, Pallas kernels, body(): pl.pallas_call(lambda *refs: map_rest_kernel(mine, *refs), out_shape=[sha...  2.78 us
    pallas_call x1, Pallas kernels, body(): pl.pallas_call(lambda *refs: map_own_kernel(mine, *refs), out_shape=shape...  2.11 us
    pallas_call x1, Pallas kernels, body(): pl.pallas_call(lambda *refs: grad_kernel(scale, *refs), out_shape=(shape(...  1.88 us
    another operation x1, other arithmetic, body(): lax.reduce((wide, jnp.ones_like(wide)), (low, jnp.float32(0)), merge, (1,))  1.57 us
  transfers between devices with their start and end apart: 16, of which 6 were waited for; matrix products, arithmetic and copies ran while one was open for 6% of the time, Pallas kernels for 17%

profile of v9, /device:TPU:0, one launch (start us, length us, event | category | flops | bytes accessed | tf_op | source)
XLA Modules:
  0.0 57.6 jit_solution(2608197657632012508)
XLA Ops:
  1.1 1.6 %convert_reduce_fusion = (f32[64]{0:T(128)S(1)}, f32[64]{0:T(128)S(1)}) fusion(bf16[64,4096]{1,0:T(8,128)(2,1)} %param.10), kind=kLoop, calls=%fused_computation | loop fusion | flops 1834624 | bytes 524800 | tf_op jit(solution)/shard_map/reduce | solution.py:281
  2.8 4.0 %collective-permute-start.1 = (bf16[1,8,1920]{2,1,0:T(8,128)(2,1)}, bf16[1,8,1920]{2,1,0:T(8,128)(2,1)S(1)}, u32[]{:S(2)}, u32[]{:S(2)}) collective-permute-start(bf16[1,8,1920]{2,1,0:T(8,128)(2,1)} %bitcast.11), channel_id=1, source_target_pairs={{0,8},{2,10},{4,12},{6,14},{8,0},{10,2},{12,4},{14,6},{1,9},{3,11}... | collective-permute-start | bytes 92168 | tf_op jit(solution)/shard_map/ppermute | solution.py:243
  7.0 0.7 %convert_bitcast_fusion = f32[2,640]{1,0:T(2,128)S(1)} fusion(bf16[640,2]{0,1:T(2,128)(2,1)} %param.9), kind=kLoop, calls=%fused_computation.12 | loop fusion | flops 1280 | bytes 7680 | tf_op jit(solution)/shard_map/convert_element_type | solution.py:284
  7.6 0.7 %convert_bitcast_fusion.1 = (f32[2,640]{1,0:T(2,128)S(1)}, f32[2,640]{1,0:T(2,128)S(1)}) fusion(s32[640,2]{0,1:T(2,128)} %param.8, s32[640,2]{0,1:T(2,128)} %param.7), kind=kLoop, calls=%fused_computation.13 | loop fusion | flops 2560 | bytes 20480 | tf_op jit(solution)/shard_map/convert_element_type | solution.py:284
  9.0 1.3 %copy-done = bf16[16,40960]{1,0:T(8,128)(2,1)S(1)} copy-done((bf16[16,40960]{1,0:T(8,128)(2,1)S(1)}, bf16[16,40960]{1,0:T(8,128)(2,1)}, u32[]{:S(2)}) %copy-start) | copy-done | bytes 1310744
  10.3 2.1 %map_own.1.refs_3_ = f32[144,2048]{1,0:T(8,128)S(1)} custom-call(s32[2]{0:T(128)S(1)} %pad_add_fusion.refs_0_.place_ref, f32[6,640]{1,0:T(8,128)S(1)} %pad_maximum_fusion.3.refs_1_, bf16[16,40960]{1,0:T(8,128)(2,1)S(1)} %copy-done, bf16[1,8,1920]{2,1,0:T(8,128)(2,1)S(1)} %collective-permute-done.1.refs_3_), custom_call_target="tpu_custom_call" | custom-call | flops 188743680 | bytes 3145728 | tf_op jit(solution)/shard_map/map_own/pallas_call | solution.py:287
  12.4 2.8 %map_rest.1 = (bf16[16,2176]{1,0:T(8,128)(2,1)S(1)}, bf16[16,2176]{1,0:T(8,128)(2,1)S(1)}, bf16[16,2176]{1,0:T(8,128)(2,1)S(1)}, bf16[16,2176]{1,0:T(8,128)(2,1)...) custom-call(s32[2]{0:T(128)S(1)} %pad_add_fusion.refs_0_.place_ref, ...), custom_call_target="tpu_custom_call" | custom-call | flops 188743680 | bytes 4194304 | tf_op jit(solution)/shard_map/map_rest/pallas_call | solution.py:298
  15.2 3.0 %collective-permute-start.7 = (bf16[16,2176]{1,0:T(8,128)(2,1)S(1)}, bf16[16,2176]{1,0:T(8,128)(2,1)S(1)}, u32[]{:S(2)}, u32[]{:S(2)}) collective-permute-start(bf16[16,2176]{1,0:T(8,128)(2,1)S(1)} %get-tuple-element.27), channel_id=1, source_target_pairs={{0,8},{2,10},{4,12},{6,14},{8,0},{10,2},{12,4},{14,6},{1,9},{3,11}... | collective-permute-start | bytes 208904 | tf_op jit(solution)/shard_map/ppermute | solution.py:243
  18.3 2.3 %collective-permute-start.10 = (bf16[16,2176]{1,0:T(8,128)(2,1)S(1)}, bf16[16,2176]{1,0:T(8,128)(2,1)S(1)}, u32[]{:S(2)}, u32[]{:S(2)}) collective-permute-start(bf16[16,2176]{1,0:T(8,128)(2,1)S(1)} %get-tuple-element.30), channel_id=1, source_target_pairs={{0,14},{2,12},{4,10},{6,8},{8,6},{10,4},{12,2},{14,0},{1,15},{3,13... | collective-permute-start | bytes 208904 | tf_op jit(solution)/shard_map/ppermute | solution.py:243
  21.2 0.6 %collective-permute-start.5 = (bf16[16,2176]{1,0:T(8,128)(2,1)S(1)}, bf16[16,2176]{1,0:T(8,128)(2,1)S(1)}, u32[]{:S(2)}, u32[]{:S(2)}) collective-permute-start(bf16[16,2176]{1,0:T(8,128)(2,1)S(1)} %get-tuple-element.25), channel_id=1, source_target_pairs={{0,4},{2,6},{4,0},{6,2},{8,12},{10,14},{12,8},{14,10},{1,5},{3,7},... | collective-permute-start | bytes 208904 | tf_op jit(solution)/shard_map/ppermute | solution.py:243
  21.8 1.5 %collective-permute-start.12 = (bf16[2,8,1920]{2,1,0:T(8,128)(2,1)S(1)}, bf16[2,8,1920]{2,1,0:T(8,128)(2,1)S(1)}, u32[]{:S(2)}, u32[]{:S(2)}) collective-permute-start(bf16[2,8,1920]{2,1,0:T(8,128)(2,1)S(1)} %pad_maximum_fusion.2), channel_id=1, source_target_pairs={{0,4},{2,6},{4,0},{6,2},{8,12},{10,14},{12,8},{14,10},{1,5},{3,7},... | collective-permute-start | bytes 184328 | tf_op jit(solution)/shard_map/ppermute | solution.py:243
  23.3 4.6 %collective-permute-done.12 = bf16[2,8,1920]{2,1,0:T(8,128)(2,1)S(1)} collective-permute-done((bf16[2,8,1920]{2,1,0:T(8,128)(2,1)S(1)}, bf16[2,8,1920]{2,1,0:T(8,128)(2,1)S(1)}, u32[]{:S(2)}, u32[]{:S(2)}) %collective-permute-start.12) | collective-permute-done | bytes 61472 | tf_op jit(solution)/shard_map/ppermute | solution.py:243
  28.0 1.2 %collective-permute-start.13 = (bf16[4,8,1920]{2,1,0:T(8,128)(2,1)S(1)}, bf16[4,8,1920]{2,1,0:T(8,128)(2,1)S(1)}, u32[]{:S(2)}, u32[]{:S(2)}) collective-permute-start(bf16[4,8,1920]{2,1,0:T(8,128)(2,1)S(1)} %pad_maximum_fusion.1), channel_id=1, source_target_pairs={{0,2},{2,0},{4,6},{6,4},{8,10},{10,8},{12,14},{14,12},{1,3},{3,1},... | collective-permute-start | bytes 368648 | tf_op jit(solution)/shard_map/ppermute | solution.py:243
  29.2 3.7 %collective-permute-done.13 = bf16[4,8,1920]{2,1,0:T(8,128)(2,1)S(1)} collective-permute-done((bf16[4,8,1920]{2,1,0:T(8,128)(2,1)S(1)}, bf16[4,8,1920]{2,1,0:T(8,128)(2,1)S(1)}, u32[]{:S(2)}, u32[]{:S(2)}) %collective-permute-start.13) | collective-permute-done | bytes 122912 | tf_op jit(solution)/shard_map/ppermute | solution.py:243
  32.9 1.8 %collective-permute-start.6 = (bf16[16,2176]{1,0:T(8,128)(2,1)S(1)}, bf16[16,2176]{1,0:T(8,128)(2,1)S(1)}, u32[]{:S(2)}, u32[]{:S(2)}) collective-permute-start(bf16[16,2176]{1,0:T(8,128)(2,1)S(1)} %get-tuple-element.26), channel_id=1, source_target_pairs={{0,6},{2,4},{4,2},{6,0},{8,14},{10,12},{12,10},{14,8},{1,7},{3,5},... | collective-permute-start | bytes 208904 | tf_op jit(solution)/shard_map/ppermute | solution.py:243
  34.8 3.2 %collective-permute-start.8 = (bf16[16,2176]{1,0:T(8,128)(2,1)S(1)}, bf16[16,2176]{1,0:T(8,128)(2,1)S(1)}, u32[]{:S(2)}, u32[]{:S(2)}) collective-permute-start(bf16[16,2176]{1,0:T(8,128)(2,1)S(1)} %get-tuple-element.28), channel_id=1, source_target_pairs={{0,10},{2,8},{4,14},{6,12},{8,2},{10,0},{12,6},{14,4},{1,11},{3,9}... | collective-permute-start | bytes 208904 | tf_op jit(solution)/shard_map/ppermute | solution.py:243
  38.6 3.2 %collective-permute-done.8.refs_7_ = bf16[16,2176]{1,0:T(8,128)(2,1)S(1)} collective-permute-done((bf16[16,2176]{1,0:T(8,128)(2,1)S(1)}, bf16[16,2176]{1,0:T(8,128)(2,1)S(1)}, u32[]{:S(2)}, u32[]{:S(2)}) %collective-permute-start.8) | collective-permute-done | bytes 69664 | tf_op jit(solution)/shard_map/ppermute | solution.py:243
  41.9 2.4 %collective-permute-done.9.refs_8_ = bf16[16,2176]{1,0:T(8,128)(2,1)S(1)} collective-permute-done((bf16[16,2176]{1,0:T(8,128)(2,1)S(1)}, bf16[16,2176]{1,0:T(8,128)(2,1)S(1)}, u32[]{:S(2)}, u32[]{:S(2)}) %collective-permute-start.9) | collective-permute-done | bytes 69664 | tf_op jit(solution)/shard_map/ppermute | solution.py:243
  44.3 1.9 %logit_grad.1 = (bf16[128,2048]{1,0:T(8,128)(2,1)S(1)}, f32[16,8,128]{2,1,0:T(8,128)}) custom-call(s32[2]{0:T(128)S(1)} %pad_add_fusion.refs_0_.place_ref, bf16[128,2048]{1,0:T(8,128)(2,1)S(1)} %pad_maximum_fusion.refs_1_, bf16[16,2176]{1,0:T(8,128)(2,1)S(1)} %get-tuple-element.22.refs_2_, bf16[16,2176]{1,0:T(8,128)(2,1)S(1)} %collective-permute-done.4.refs_3_, ...), custom_call_target="tpu_custom_call" | custom-call | flops 2621440 | bytes 1572864 | tf_op jit(solution)/shard_map/logit_grad/pallas_call | solution.py:331
  46.3 3.9 %all-to-all-start = ((f32[16,8,128]{2,1,0:T(8,128)}), f32[16,8,128]{2,1,0:T(8,128)S(1)}, u32[]{:S(2)}, u32[]{:S(2)}) async-start(f32[16,8,128]{2,1,0:T(8,128)} %get-tuple-element.31), calls=%async_computation | async-start | bytes 131072 | tf_op jit(solution)/shard_map/all_to_all | solution.py:349
  50.2 4.3 %weight_grad.1 = bf16[1920,2048]{1,0:T(8,128)(2,1)} custom-call(s32[2]{0:T(128)S(1)} %pad_add_fusion.refs_0_.place_ref, bf16[8,8,1920]{2,1,0:T(8,128)(2,1)S(1)} %constant_dynamic-update-slice_fusion.own_ref, bf16[8,8,1920]{2,1,0:T(8,128)(2,1)S(1)} %collective-permute-done.14.other_ref, bf16[128,2048]{1,0:T(8,128)(2,1)S(1)} %get-tuple-element.32.grad_ref), custom_call_target="tpu_custom_call" | custom-call | flops 1006632960 | bytes 8880128 | tf_op jit(solution)/shard_map/weight_grad/pallas_call | solution.py:356
  54.5 1.4 %join.1 = bf16[64,4096]{1,0:T(8,128)(2,1)} custom-call(s32[2]{0:T(128)S(1)} %pad_add_fusion.refs_0_.place_ref, bf16[128,2048]{1,0:T(8,128)(2,1)S(1)} %get-tuple-element.32.grad_ref, bf16[64,2048]{1,0:T(8,128)(2,1)S(1)} %collective-permute-done.11.got_ref), custom_call_target="tpu_custom_call" | custom-call | bytes 1048576 | tf_op jit(solution)/shard_map/join/pallas_call | solution.py:375
  55.9 1.2 %all-to-all-done = f32[16,8,128]{2,1,0:T(8,128)S(1)} async-done(((f32[16,8,128]{2,1,0:T(8,128)}), f32[16,8,128]{2,1,0:T(8,128)S(1)}, u32[]{:S(2)}, u32[]{:S(2)}) %all-to-all-start) | async-done | bytes 65568 | tf_op jit(solution)/shard_map/all_to_all | solution.py:349
  57.1 0.5 slice_reduce_fusion
  (38 shorter events, 2.7 us)
Async XLA Ops:
  0.6 11.8 %collective-permute-start = (bf16[16,40960]{1,0:T(8,128)(2,1)}, bf16[16,40960]{1,0:T(8,128)(2,1)S(1)}, u32[]{:S(2)}, u32[]{:S(2)}) collective-permute-start(bf16[16,40960]{1,0:T(8,128)(2,1)} %refs_2_.1), channel_id=1, source_target_pairs={{0,1},{1,0},{2,3},{3,2},{4,5},{5,4},{6,7},{7,6},{8,9},{9,8},{10,11... | collective-permute-start | bytes 3932168 | tf_op jit(solution)/shard_map/ppermute | solution.py:239
  2.7 5.7 %collective-permute-start.2 = (f32[2,64]{1,0:T(2,128)S(1)}, f32[2,64]{1,0:T(2,128)S(1)}, u32[]{:S(2)}, u32[]{:S(2)}) collective-permute-start(f32[2,64]{1,0:T(2,128)S(1)} %pad_maximum_fusion.4), channel_id=1, source_target_pairs={{0,1},{1,0},{2,3},{3,2},{4,5},{5,4},{6,7},{7,6},{8,9},{9,8},{10,11... | collective-permute-start | bytes 1544 | tf_op jit(solution)/shard_map/ppermute | solution.py:239
  2.8 6.1 %collective-permute-start.1 = (bf16[1,8,1920]{2,1,0:T(8,128)(2,1)}, bf16[1,8,1920]{2,1,0:T(8,128)(2,1)S(1)}, u32[]{:S(2)}, u32[]{:S(2)}) collective-permute-start(bf16[1,8,1920]{2,1,0:T(8,128)(2,1)} %bitcast.11), channel_id=1, source_target_pairs={{0,8},{2,10},{4,12},{6,14},{8,0},{10,2},{12,4},{14,6},{1,9},{3,11}... | collective-permute-start | bytes 92168 | tf_op jit(solution)/shard_map/ppermute | solution.py:243
  9.0 1.3 %copy-start = (bf16[16,40960]{1,0:T(8,128)(2,1)S(1)}, bf16[16,40960]{1,0:T(8,128)(2,1)}, u32[]{:S(2)}) copy-start(bf16[16,40960]{1,0:T(8,128)(2,1)} %refs_2_.1) | copy-start | bytes 3932164
  12.4 5.8 %copy-start.1 = (bf16[64,4096]{1,0:T(8,128)(2,1)S(1)}, bf16[64,4096]{1,0:T(8,128)(2,1)}, u32[]{:S(2)}) copy-start(bf16[64,4096]{1,0:T(8,128)(2,1)} %param.10) | copy-start | bytes 1572868
  12.4 9.4 %copy-start.2 = (bf16[8,1920]{1,0:T(8,128)(2,1)S(1)}, bf16[8,1920]{1,0:T(8,128)(2,1)}, u32[]{:S(2)}) copy-start(bf16[8,1920]{1,0:T(8,128)(2,1)} %param.11) | copy-start | bytes 92164
  15.2 6.6 %collective-permute-start.7 = (bf16[16,2176]{1,0:T(8,128)(2,1)S(1)}, bf16[16,2176]{1,0:T(8,128)(2,1)S(1)}, u32[]{:S(2)}, u32[]{:S(2)}) collective-permute-start(bf16[16,2176]{1,0:T(8,128)(2,1)S(1)} %get-tuple-element.27), channel_id=1, source_target_pairs={{0,8},{2,10},{4,12},{6,14},{8,0},{10,2},{12,4},{14,6},{1,9},{3,11}... | collective-permute-start | bytes 208904 | tf_op jit(solution)/shard_map/ppermute | solution.py:243
  18.3 16.5 %collective-permute-start.3 = (bf16[64,2048]{1,0:T(8,128)(2,1)S(1)}, bf16[64,2048]{1,0:T(8,128)(2,1)S(1)}, u32[]{:S(2)}, u32[]{:S(2)}) collective-permute-start(bf16[64,2048]{1,0:T(8,128)(2,1)S(1)} %constant_dynamic-slice_fusion.1), channel_id=1, source_target_pairs={{0,1},{1,0},{2,3},{3,2},{4,5},{5,4},{6,7},{7,6},{8,9},{9,8},{10,11... | collective-permute-start | bytes 786440 | tf_op jit(solution)/shard_map/ppermute | solution.py:239
  18.3 19.7 %collective-permute-start.10 = (bf16[16,2176]{1,0:T(8,128)(2,1)S(1)}, bf16[16,2176]{1,0:T(8,128)(2,1)S(1)}, u32[]{:S(2)}, u32[]{:S(2)}) collective-permute-start(bf16[16,2176]{1,0:T(8,128)(2,1)S(1)} %get-tuple-element.30), channel_id=1, source_target_pairs={{0,14},{2,12},{4,10},{6,8},{8,6},{10,4},{12,2},{14,0},{1,15},{3,13... | collective-permute-start | bytes 208904 | tf_op jit(solution)/shard_map/ppermute | solution.py:243
  20.7 17.8 %collective-permute-start.4 = (bf16[16,2176]{1,0:T(8,128)(2,1)S(1)}, bf16[16,2176]{1,0:T(8,128)(2,1)S(1)}, u32[]{:S(2)}, u32[]{:S(2)}) collective-permute-start(bf16[16,2176]{1,0:T(8,128)(2,1)S(1)} %get-tuple-element.24), channel_id=1, source_target_pairs={{0,2},{2,0},{4,6},{6,4},{8,10},{10,8},{12,14},{14,12},{1,3},{3,1},... | collective-permute-start | bytes 208904 | tf_op jit(solution)/shard_map/ppermute | solution.py:243
  21.2 17.4 %collective-permute-start.5 = (bf16[16,2176]{1,0:T(8,128)(2,1)S(1)}, bf16[16,2176]{1,0:T(8,128)(2,1)S(1)}, u32[]{:S(2)}, u32[]{:S(2)}) collective-permute-start(bf16[16,2176]{1,0:T(8,128)(2,1)S(1)} %get-tuple-element.25), channel_id=1, source_target_pairs={{0,4},{2,6},{4,0},{6,2},{8,12},{10,14},{12,8},{14,10},{1,5},{3,7},... | collective-permute-start | bytes 208904 | tf_op jit(solution)/shard_map/ppermute | solution.py:243
  21.8 6.2 %collective-permute-start.12 = (bf16[2,8,1920]{2,1,0:T(8,128)(2,1)S(1)}, bf16[2,8,1920]{2,1,0:T(8,128)(2,1)S(1)}, u32[]{:S(2)}, u32[]{:S(2)}) collective-permute-start(bf16[2,8,1920]{2,1,0:T(8,128)(2,1)S(1)} %pad_maximum_fusion.2), channel_id=1, source_target_pairs={{0,4},{2,6},{4,0},{6,2},{8,12},{10,14},{12,8},{14,10},{1,5},{3,7},... | collective-permute-start | bytes 184328 | tf_op jit(solution)/shard_map/ppermute | solution.py:243
  28.0 4.9 %collective-permute-start.13 = (bf16[4,8,1920]{2,1,0:T(8,128)(2,1)S(1)}, bf16[4,8,1920]{2,1,0:T(8,128)(2,1)S(1)}, u32[]{:S(2)}, u32[]{:S(2)}) collective-permute-start(bf16[4,8,1920]{2,1,0:T(8,128)(2,1)S(1)} %pad_maximum_fusion.1), channel_id=1, source_target_pairs={{0,2},{2,0},{4,6},{6,4},{8,10},{10,8},{12,14},{14,12},{1,3},{3,1},... | collective-permute-start | bytes 368648 | tf_op jit(solution)/shard_map/ppermute | solution.py:243
  32.9 5.7 %collective-permute-start.6 = (bf16[16,2176]{1,0:T(8,128)(2,1)S(1)}, bf16[16,2176]{1,0:T(8,128)(2,1)S(1)}, u32[]{:S(2)}, u32[]{:S(2)}) collective-permute-start(bf16[16,2176]{1,0:T(8,128)(2,1)S(1)} %get-tuple-element.26), channel_id=1, source_target_pairs={{0,6},{2,4},{4,2},{6,0},{8,14},{10,12},{12,10},{14,8},{1,7},{3,5},... | collective-permute-start | bytes 208904 | tf_op jit(solution)/shard_map/ppermute | solution.py:243
  34.8 7.1 %collective-permute-start.8 = (bf16[16,2176]{1,0:T(8,128)(2,1)S(1)}, bf16[16,2176]{1,0:T(8,128)(2,1)S(1)}, u32[]{:S(2)}, u32[]{:S(2)}) collective-permute-start(bf16[16,2176]{1,0:T(8,128)(2,1)S(1)} %get-tuple-element.28), channel_id=1, source_target_pairs={{0,10},{2,8},{4,14},{6,12},{8,2},{10,0},{12,6},{14,4},{1,11},{3,9}... | collective-permute-start | bytes 208904 | tf_op jit(solution)/shard_map/ppermute | solution.py:243
  38.1 6.2 %collective-permute-start.9 = (bf16[16,2176]{1,0:T(8,128)(2,1)S(1)}, bf16[16,2176]{1,0:T(8,128)(2,1)S(1)}, u32[]{:S(2)}, u32[]{:S(2)}) collective-permute-start(bf16[16,2176]{1,0:T(8,128)(2,1)S(1)} %get-tuple-element.29), channel_id=1, source_target_pairs={{0,12},{2,14},{4,8},{6,10},{8,4},{10,6},{12,0},{14,2},{1,13},{3,15... | collective-permute-start | bytes 208904 | tf_op jit(solution)/shard_map/ppermute | solution.py:243
  38.5 11.7 %collective-permute-start.14 = (bf16[8,8,1920]{2,1,0:T(8,128)(2,1)S(1)}, bf16[8,8,1920]{2,1,0:T(8,128)(2,1)S(1)}, u32[]{:S(2)}, u32[]{:S(2)}) collective-permute-start(bf16[8,8,1920]{2,1,0:T(8,128)(2,1)S(1)} %constant_dynamic-update-slice_fusion.own_ref), channel_id=1, source_target_pairs={{0,1},{1,0},{2,3},{3,2},{4,5},{5,4},{6,7},{7,6},{8,9},{9,8},{10,11... | collective-permute-start | bytes 737288 | tf_op jit(solution)/shard_map/ppermute | solution.py:239
  46.2 8.4 %collective-permute-start.11 = (bf16[64,2048]{1,0:T(8,128)(2,1)S(1)}, bf16[64,2048]{1,0:T(8,128)(2,1)S(1)}, u32[]{:S(2)}, u32[]{:S(2)}) collective-permute-start(bf16[64,2048]{1,0:T(8,128)(2,1)S(1)} %constant_dynamic-slice_fusion), channel_id=1, source_target_pairs={{0,1},{1,0},{2,3},{3,2},{4,5},{5,4},{6,7},{7,6},{8,9},{9,8},{10,11... | collective-permute-start | bytes 786440 | tf_op jit(solution)/shard_map/ppermute | solution.py:239
  46.3 10.8 %all-to-all-start = ((f32[16,8,128]{2,1,0:T(8,128)}), f32[16,8,128]{2,1,0:T(8,128)S(1)}, u32[]{:S(2)}, u32[]{:S(2)}) async-start(f32[16,8,128]{2,1,0:T(8,128)} %get-tuple-element.31), calls=%async_computation | async-start | bytes 131072 | tf_op jit(solution)/shard_map/all_to_all | solution.py:349

commit v10 on v8

--- a/solution.py
+++ b/solution.py
@@ -17,7 +17,7 @@
     total = jnp.zeros(row_ids.shape, jnp.float32)
     for slot in range(row_of.shape[0]):
         hit = (row_ids == row_of[slot][None, :]) | (row_ids == rows + slot)
-        total = total + jnp.where(hit, weight[slot].astype(jnp.float32)[None, :], 0.0)
+        total = total + jnp.where(hit, weight[slot][None, :], 0.0)
     return total.astype(jnp.bfloat16)
 
 
@@ -117,7 +117,7 @@
     lax.fori_loop(0, owners, left, 0)
 
 
-def grad_kernel(scale, target_ref, logits_ref, grad_ref, terms_ref, row_ref):
+def grad_kernel(scale, target_ref, logits_ref, grad_ref, terms_ref, norm_ref, t_buf, sem):
     owners, tokens, _ = target_ref.shape
     group_tokens, width = logits_ref.shape
     stats = [target_ref[q, :, width:].astype(jnp.float32) for q in range(owners)]
@@ -128,26 +128,41 @@
     for one in stats:
         total = total + (one[1:2] + one[2:3] + one[3:4]) * jnp.exp(one[0:1] - top)
     log_norm = top + jnp.log(total)
+
+    def block(i, b):
+        lanes = slice(b * BLK, (b + 1) * BLK)
+        group = slice(i * BLK // tokens, (i + 1) * BLK // tokens)
+        target = target_ref[group, :, lanes].reshape(BLK, BLK).astype(jnp.float32)
+        return target, logits_ref[i * BLK : (i + 1) * BLK, lanes].astype(jnp.float32)
+
+    sums = []
     for i in range(group_tokens // BLK):
         rows = slice(i * BLK, (i + 1) * BLK)
-        group = slice(i * BLK // tokens, (i + 1) * BLK // tokens)
         norm = jnp.broadcast_to(log_norm[:, rows], (BLK, BLK)).T
+        norm_ref[rows, :] = norm
         terms = jnp.zeros((BLK, BLK), jnp.float32)
         for b in range(width // BLK):
-            lanes = slice(b * BLK, (b + 1) * BLK)
-            target = target_ref[group, :, lanes].reshape(BLK, BLK).astype(jnp.float32)
-            log_probs = logits_ref[rows, lanes].astype(jnp.float32) - norm
-            grad_ref[rows, lanes] = ((jnp.exp(log_probs) - target) * scale).astype(jnp.bfloat16)
+            target, logits = block(i, b)
             positive = target > 0
-            one = target * (jnp.log(jnp.where(positive, target, 1.0)) - log_probs)
+            one = target * (jnp.log(jnp.where(positive, target, 1.0)) - (logits - norm))
             terms = terms + jnp.where(positive, one, 0.0)
-        row_ref[:, rows] = jnp.sum(terms.T, axis=0, keepdims=True)
+        sums.append(jnp.sum(terms.T, axis=0, keepdims=True))
+    row = jnp.concatenate(sums, axis=1)
     half_tokens = group_tokens // 2
     for half in range(2):
-        row = row_ref[:, half * half_tokens : (half + 1) * half_tokens]
-        tile = jnp.concatenate([row] * (terms_ref.shape[2] // half_tokens), axis=1)
+        mine = row[:, half * half_tokens : (half + 1) * half_tokens]
+        tile = jnp.concatenate([mine] * (t_buf.shape[2] // half_tokens), axis=1)
         for q in range(owners):
-            terms_ref[2 * q + half] = jnp.broadcast_to(tile, terms_ref.shape[1:])
+            t_buf[2 * q + half] = jnp.broadcast_to(tile, t_buf.shape[1:])
+    leaving = pltpu.make_async_copy(t_buf, terms_ref, sem)
+    leaving.start()
+    for i in range(group_tokens // BLK):
+        rows = slice(i * BLK, (i + 1) * BLK)
+        for b in range(width // BLK):
+            target, logits = block(i, b)
+            grad = (jnp.exp(logits - norm_ref[rows, :]) - target) * scale
+            grad_ref[rows, b * BLK : (b + 1) * BLK] = grad.astype(jnp.bfloat16)
+    leaving.wait()
 
 
 def join_kernel(place_ref, grad_ref, got_ref, o_ref, sem):
@@ -166,21 +181,19 @@
         copy.wait()
 
 
-def weight_kernel(place_ref, *refs):
-    pieces, (grad_ref, o_ref, s_ref, h_ref, block_ref, sem) = refs[:-6], refs[-6:]
-    count = len(pieces) // 2
-    _, held, features = pieces[0].shape
-    owners = s_ref.shape[0] // (2 * held)
-    i = 0
-    for own_ref, other_ref in zip(pieces[:count], pieces[count:]):
-        for j in range(own_ref.shape[0]):
-            offset = sum(((i >> bit) & 1) * (owners >> (bit + 1)) for bit in range(owners.bit_length() - 1))
-            first = (place_ref[0] ^ offset) * 2
-            own = pl.ds(pl.multiple_of((first + place_ref[1]) * held, held), held)
-            other = pl.ds(pl.multiple_of((first + 1 - place_ref[1]) * held, held), held)
-            s_ref[own, :] = own_ref[j].astype(jnp.float32)
-            s_ref[other, :] = other_ref[j].astype(jnp.float32)
-            i += 1
+def arrival_order(owners):
+    bits = owners.bit_length() - 1
+    return [sum(((i >> bit) & 1) * (owners >> (bit + 1)) for bit in range(bits)) for i in range(owners)]
+
+
+def weight_kernel(place_ref, own_ref, other_ref, grad_ref, o_ref, s_ref, h_ref, block_ref, sem):
+    owners, held, features = own_ref.shape
+    for i, offset in enumerate(arrival_order(owners)):
+        first = (place_ref[0] ^ offset) * 2
+        own = pl.ds(pl.multiple_of((first + place_ref[1]) * held, held), held)
+        other = pl.ds(pl.multiple_of((first + 1 - place_ref[1]) * held, held), held)
+        s_ref[own, :] = own_ref[i].astype(jnp.float32)
+        s_ref[other, :] = other_ref[i].astype(jnp.float32)
     for i in range(s_ref.shape[0] // BLK):
         for j in range(features // BLK):
             tile = s_ref[i * BLK : (i + 1) * BLK, j * BLK : (j + 1) * BLK].T
@@ -249,21 +262,24 @@
     def in_order(own, other, axis):
         return jnp.concatenate([jnp.where(first, own, other), jnp.where(first, other, own)], axis=axis)
 
-    teacher_other = swap_halves(teacher_probs)
-
     hidden = hidden[None]
     offset = owners // 2
     first_piece = to_partner(hidden, offset)
 
+    def merge(one, two):
+        top = jnp.maximum(one[0], two[0])
+        return top, one[1] * jnp.exp(one[0] - top) + two[1] * jnp.exp(two[0] - top)
+
     wide = student_logits.astype(f32)
-    peak = jnp.max(wide, axis=1)
-    sums = jnp.sum(jnp.exp(wide - peak[:, None]), axis=1)
-    stats = jnp.stack([peak, sums])
+    low = jnp.float32(-1e38)
+    stats = jnp.stack(lax.reduce((wide, jnp.ones_like(wide)), (low, jnp.float32(0)), merge, (1,)))
+    teacher_given, stats = lax.optimization_barrier((teacher_probs, stats))
+    teacher_other = swap_halves(teacher_given)
     stats = in_order(stats, swap_halves(stats), 1)
 
     local = align_local.T - half_index * mine
     row_of = jnp.where((local >= 0) & (local < mine), align_owner.T * mine + local, -1)
-    weight = align_weight.T
+    weight = jnp.where(align_owner.T >= 0, align_weight.T.astype(f32), 0.0)
     cut = lambda x, which: lax.dynamic_slice_in_dim(x, which * per_half, per_half, 1)
     w_own = block_weights(cut(row_of, half_index), cut(weight, half_index), rows)
     w_rest = block_weights(cut(row_of, 1 - half_index), cut(weight, 1 - half_index), rows)
@@ -306,22 +322,23 @@
     give = lax.dynamic_slice_in_dim(late_logits, (1 - half_index) * width, width, 1)
     logits = in_order(keep, swap_halves(give), 0)
 
-    pieces = [hidden, first_piece]
+    hidden_own = jnp.concatenate([hidden, first_piece])
     while offset > 1:
         offset //= 2
-        pieces.append(to_partner(jnp.concatenate(pieces), offset))
+        hidden_own = jnp.concatenate([hidden_own, to_partner(hidden_own, offset)])
 
     scale = float(columns * owners)
     lanes = -(-half_tokens // BLK) * BLK
     grad, terms = pl.pallas_call(
         lambda *refs: grad_kernel(scale, *refs),
-        out_shape=(
-            shape((group_tokens, width), bf16),
-            shape((owners * halves, 8, lanes), f32),
-        ),
+        out_shape=(shape((group_tokens, width), bf16), shape((owners * halves, 8, lanes), f32)),
         in_specs=[in_vmem()] * 2,
-        out_specs=[in_vmem()] * 2,
-        scratch_shapes=[pltpu.VMEM((1, group_tokens), f32)],
+        out_specs=(in_vmem(), anywhere()),
+        scratch_shapes=[
+            pltpu.VMEM((group_tokens, BLK), f32),
+            pltpu.VMEM((owners * halves, 8, lanes), f32),
+            pltpu.SemaphoreType.DMA,
+        ],
         compiler_params=params(),
         cost_estimate=cost(
             10 * group_tokens * width, 6 * group_tokens * width, 2 * group_tokens * width
@@ -337,7 +354,7 @@
     weight_grad = pl.pallas_call(
         weight_kernel,
         out_shape=shape((features, width), bf16),
-        in_specs=[scalars()] + [in_vmem()] * (2 * len(pieces) + 1),
+        in_specs=[scalars()] + [in_vmem()] * 3,
         out_specs=anywhere(),
         scratch_shapes=[
             pltpu.VMEM((group_tokens, features), f32),
@@ -351,7 +368,7 @@
             2 * (features * width + group_tokens * (features + width)),
         ),
         name="weight_grad",
-    )(place, *pieces, *[swap_halves(piece) for piece in pieces], grad)
+    )(place, hidden_own, swap_halves(hidden_own), grad)
 
     logit_grad = pl.pallas_call(
         join_kernel,

time: 49.6 us -> 49.7 us (level)
  starting transfers between devices: 19.4 us -> 20.5 us
  local copies, waits for them, and re-layouts: 0.99 us -> 0.33 us
    all_to_all x1, waiting for transfers between devices: 2.76 us -> 0.01 us  [body(): target = lax.all_to_all(outgoing, 'sv', 0, 0, tiled=True)]
    ppermute x3, waiting for transfers between devices: 8.47 us -> 11.2 us  [to_partner(): lax.ppermute(x, 'sv', [(s, s ^ offset) for s in range(lax.axis_size('sv'))])]
    another operation x1 -> x2, other arithmetic: 0.01 us -> 1.58 us  [the longest x1 1.57 us: body(): lax.reduce((wide, jnp.ones_like(wide)), (low, jnp.float32(0)), merge, (1,))]
    reduce_sum x1 -> x0, other arithmetic: 1.39 us -> none  [body(): sums = jnp.sum(jnp.exp(wide - peak[:, None]), axis=1)]
    all_to_all x1, starting transfers between devices: 5.64 us -> 6.89 us  [body(): terms = lax.all_to_all(terms, ('sv', 'tv'), 0, 0, tiled=True)]
    reduce_max x2 -> x0, other arithmetic: 1.22 us -> none  [body(): peak = jnp.max(wide, axis=1)]
    dynamic_slice x2, local copies, waits for them, and re-layouts: 0.91 us -> 0.16 us  [body(): lax.dynamic_slice_in_dim(x, which * per_half, per_half, 1)]
    select_n x0 -> x1, other arithmetic: none -> 0.71 us  [body(): weight = jnp.where(align_owner.T >= 0, align_weight.T.astype(f32), 0.0)]
  transfers between devices with their start and end apart: 13 -> 10, of which waited for: 3 -> 3; matrix products, arithmetic and copies ran while one was open for 10% -> 8% of each run, Pallas kernels for 17% -> 17%
where the time goes in v10:
time: 49.7 us; the launch traced here: 49.3 us
  starting transfers between devices  20.5 us (41%)
  waiting for transfers between devices  12.3 us (25%)
  Pallas kernels  11.1 us (22%)
  other arithmetic  4.09 us (8%)
  between operations  0.85 us (2%)
    ppermute x3, waiting for transfers between devices, to_partner(): lax.ppermute(x, 'sv', [(s, s ^ offset) for s in range(lax.axis_size('sv'))])  11.2 us
    ppermute x3, starting transfers between devices, to_partner(): lax.ppermute(x, 'sv', [(s, s ^ offset) for s in range(lax.axis_size('sv'))])  7.93 us
    all_to_all x1, starting transfers between devices, body(): terms = lax.all_to_all(terms, ('sv', 'tv'), 0, 0, tiled=True)  6.89 us
    all_to_all x1, starting transfers between devices, body(): target = lax.all_to_all(outgoing, 'sv', 0, 0, tiled=True)  4.48 us
    pallas_call x1, Pallas kernels, body(): pl.pallas_call(weight_kernel, out_shape=shape((features, width), bf16), i...  4.31 us
    pallas_call x1, Pallas kernels, body(): pl.pallas_call(map_rest_kernel, out_shape=shape(chunk, bf16), in_specs=[i...  2.86 us
    another operation x1, other arithmetic, body(): lax.reduce((wide, jnp.ones_like(wide)), (low, jnp.float32(0)), merge, (1,))  1.57 us
    pallas_call x1, Pallas kernels, body(): pl.pallas_call(map_own_kernel, out_shape=shape((rows + MASS_ROWS, tokens...  1.41 us
  transfers between devices with their start and end apart: 10, of which 3 were waited for; matrix products, arithmetic and copies ran while one was open for 8% of the time, Pallas kernels for 17%

profile of v10, /device:TPU:0, one launch (start us, length us, event | category | flops | bytes accessed | tf_op | source)
XLA Modules:
  0.0 49.3 jit_solution(3950154360584574129)
XLA Ops:
  0.6 4.1 %collective-permute-start.1 = (bf16[1,8,1920]{2,1,0:T(8,128)(2,1)}, bf16[1,8,1920]{2,1,0:T(8,128)(2,1)S(1)}, u32[]{:S(2)}, u32[]{:S(2)}) collective-permute-start(bf16[1,8,1920]{2,1,0:T(8,128)(2,1)} %bitcast.13), channel_id=1, source_target_pairs={{0,8},{2,10},{4,12},{6,14},{8,0},{10,2},{12,4},{14,6},{1,9},{3,11}... | collective-permute-start | bytes 92168 | tf_op jit(solution)/shard_map/ppermute | solution.py:239
  4.7 1.6 %convert_reduce_fusion = (f32[64]{0:T(128)S(1)}, f32[64]{0:T(128)S(1)}) fusion(bf16[64,4096]{1,0:T(8,128)(2,1)} %param.10), kind=kLoop, calls=%fused_computation | loop fusion | flops 1834624 | bytes 524800 | tf_op jit(solution)/shard_map/reduce | solution.py:275
  6.4 0.5 %collective-permute-start = (bf16[16,40960]{1,0:T(8,128)(2,1)}, bf16[16,40960]{1,0:T(8,128)(2,1)S(1)}, u32[]{:S(2)}, u32[]{:S(2)}) collective-permute-start(bf16[16,40960]{1,0:T(8,128)(2,1)} %t_ref.1), channel_id=1, source_target_pairs={{0,1},{1,0},{2,3},{3,2},{4,5},{5,4},{6,7},{7,6},{8,9},{9,8},{10,11... | collective-permute-start | bytes 3932168 | tf_op jit(solution)/shard_map/ppermute | solution.py:235
  6.9 0.7 %and_select_fusion = s32[640,2]{0,1:T(2,128)S(1)} fusion(s32[640,2]{0,1:T(2,128)} %param.7, s32[640,2]{0,1:T(2,128)} %param.8, s32[]{:T(128)S(6)} %mul.28), kind=kLoop, calls=%fused_computation.21 | loop fusion | flops 8960 | bytes 15364 | tf_op jit(solution)/shard_map/jit(_where)/select_n | solution.py:281
  7.6 0.1 dynamic-slice_bitcast_fusion.1
  7.7 0.7 %compare_select_fusion = f32[640,2]{0,1:T(2,128)S(1)} fusion(s32[640,2]{0,1:T(2,128)} %param.7, bf16[640,2]{0,1:T(2,128)(2,1)} %param.9), kind=kLoop, calls=%fused_computation.20 | loop fusion | flops 3840 | bytes 12800 | tf_op jit(solution)/shard_map/jit(_where)/select_n | solution.py:282
  8.4 0.1 dynamic-slice_bitcast_fusion
  8.6 0.2 add_convert_fusion
  8.9 1.4 %map_own.1.p_ref = f32[144,2048]{1,0:T(8,128)S(1)} custom-call(bf16[144,320]{1,0:T(8,128)(2,1)S(1)} %get-tuple-element.41.w_ref, bf16[16,40960]{1,0:T(8,128)(2,1)S(1)} %copy-done, bf16[1,8,1920]{2,1,0:T(8,128)(2,1)S(1)} %collective-permute-done.1.first_ref), custom_call_target="tpu_custom_call" | custom-call | flops 188743680 | bytes 3145728 | tf_op jit(solution)/shard_map/map_own/pallas_call | solution.py:288
  10.3 2.9 %map_rest.1 = bf16[8,16,2176]{2,1,0:T(8,128)(2,1)} custom-call(bf16[144,320]{1,0:T(8,128)(2,1)S(1)} %get-tuple-element.42.w_ref, bf16[16,40960]{1,0:T(8,128)(2,1)S(1)} %collective-permute-done.t_ref, f32[144,2048]{1,0:T(8,128)S(1)} %map_own.1.p_ref, f32[2,128]{1,0:T(2,128)S(1)} %pad_maximum_fusion.4.stats_ref), custom_call_target="tpu_custom_call" | custom-call | flops 188743680 | bytes 4194304 | tf_op jit(solution)/shard_map/map_rest/pallas_call | solution.py:300
  13.2 4.5 %all-to-all-start = ((bf16[8,16,2176]{2,1,0:T(8,128)(2,1)}), bf16[8,16,2176]{2,1,0:T(8,128)(2,1)S(1)}, u32[]{:S(2)}, u32[]{:S(2)}) async-start(bf16[8,16,2176]{2,1,0:T(8,128)(2,1)} %map_rest.1), calls=%async_computation | async-start | bytes 1114112 | tf_op jit(solution)/shard_map/all_to_all | solution.py:317
  17.7 2.1 %collective-permute-start.5 = (bf16[2,8,1920]{2,1,0:T(8,128)(2,1)S(1)}, bf16[2,8,1920]{2,1,0:T(8,128)(2,1)S(1)}, u32[]{:S(2)}, u32[]{:S(2)}) collective-permute-start(bf16[2,8,1920]{2,1,0:T(8,128)(2,1)S(1)} %pad_maximum_fusion.2), channel_id=1, source_target_pairs={{0,4},{2,6},{4,0},{6,2},{8,12},{10,14},{12,8},{14,10},{1,5},{3,7},... | collective-permute-start | bytes 184328 | tf_op jit(solution)/shard_map/ppermute | solution.py:239
  19.9 8.0 %collective-permute-done.5 = bf16[2,8,1920]{2,1,0:T(8,128)(2,1)S(1)} collective-permute-done((bf16[2,8,1920]{2,1,0:T(8,128)(2,1)S(1)}, bf16[2,8,1920]{2,1,0:T(8,128)(2,1)S(1)}, u32[]{:S(2)}, u32[]{:S(2)}) %collective-permute-start.5) | collective-permute-done | bytes 61472 | tf_op jit(solution)/shard_map/ppermute | solution.py:239
  27.9 1.7 %collective-permute-start.6 = (bf16[4,8,1920]{2,1,0:T(8,128)(2,1)S(1)}, bf16[4,8,1920]{2,1,0:T(8,128)(2,1)S(1)}, u32[]{:S(2)}, u32[]{:S(2)}) collective-permute-start(bf16[4,8,1920]{2,1,0:T(8,128)(2,1)S(1)} %pad_maximum_fusion.1), channel_id=1, source_target_pairs={{0,2},{2,0},{4,6},{6,4},{8,10},{10,8},{12,14},{14,12},{1,3},{3,1},... | collective-permute-start | bytes 368648 | tf_op jit(solution)/shard_map/ppermute | solution.py:239
  29.7 3.2 %collective-permute-done.6 = bf16[4,8,1920]{2,1,0:T(8,128)(2,1)S(1)} collective-permute-done((bf16[4,8,1920]{2,1,0:T(8,128)(2,1)S(1)}, bf16[4,8,1920]{2,1,0:T(8,128)(2,1)S(1)}, u32[]{:S(2)}, u32[]{:S(2)}) %collective-permute-start.6) | collective-permute-done | bytes 122912 | tf_op jit(solution)/shard_map/ppermute | solution.py:239
  33.0 0.1 broadcast_select_fusion.1
  33.1 1.2 %logit_grad.1 = (bf16[128,2048]{1,0:T(8,128)(2,1)S(1)}, f32[16,8,128]{2,1,0:T(8,128)}) custom-call(bf16[8,16,2176]{2,1,0:T(8,128)(2,1)S(1)} %all-to-all-done.refs_0_, bf16[128,2048]{1,0:T(8,128)(2,1)S(1)} %pad_maximum_fusion.refs_1_), custom_call_target="tpu_custom_call" | custom-call | flops 2621440 | bytes 1572864 | tf_op jit(solution)/shard_map/logit_grad/pallas_call | solution.py:332
  34.4 0.5 %collective-permute-start.4 = (bf16[64,2048]{1,0:T(8,128)(2,1)S(1)}, bf16[64,2048]{1,0:T(8,128)(2,1)S(1)}, u32[]{:S(2)}, u32[]{:S(2)}) collective-permute-start(bf16[64,2048]{1,0:T(8,128)(2,1)S(1)} %constant_dynamic-slice_fusion), channel_id=1, source_target_pairs={{0,1},{1,0},{2,3},{3,2},{4,5},{5,4},{6,7},{7,6},{8,9},{9,8},{10,11... | collective-permute-start | bytes 786440 | tf_op jit(solution)/shard_map/ppermute | solution.py:235
  34.9 6.9 %all-to-all-start.1 = ((f32[16,8,128]{2,1,0:T(8,128)}), f32[16,8,128]{2,1,0:T(8,128)S(1)}, u32[]{:S(2)}, u32[]{:S(2)}) async-start(f32[16,8,128]{2,1,0:T(8,128)} %get-tuple-element.19), calls=%async_computation.1 | async-start | bytes 131072 | tf_op jit(solution)/shard_map/all_to_all | solution.py:349
  41.8 0.1 pad_add_fusion.place_ref
  41.9 4.3 %weight_grad.1 = bf16[1920,2048]{1,0:T(8,128)(2,1)} custom-call(s32[2]{0:T(128)S(1)} %pad_add_fusion.place_ref, bf16[8,8,1920]{2,1,0:T(8,128)(2,1)S(1)} %constant_dynamic-update-slice_fusion.own_ref, bf16[8,8,1920]{2,1,0:T(8,128)(2,1)S(1)} %collective-permute-done.7.other_ref, bf16[128,2048]{1,0:T(8,128)(2,1)S(1)} %get-tuple-element.20.grad_ref), custom_call_target="tpu_custom_call" | custom-call | flops 1006632960 | bytes 8880128 | tf_op jit(solution)/shard_map/weight_grad/pallas_call | solution.py:354
  46.3 1.4 %join.1 = bf16[64,4096]{1,0:T(8,128)(2,1)} custom-call(s32[2]{0:T(128)S(1)} %pad_add_fusion.place_ref, bf16[128,2048]{1,0:T(8,128)(2,1)S(1)} %get-tuple-element.20.grad_ref, bf16[64,2048]{1,0:T(8,128)(2,1)S(1)} %collective-permute-done.4.got_ref), custom_call_target="tpu_custom_call" | custom-call | bytes 1048576 | tf_op jit(solution)/shard_map/join/pallas_call | solution.py:373
  47.6 1.1 %all-to-all-done.1 = f32[16,8,128]{2,1,0:T(8,128)S(1)} async-done(((f32[16,8,128]{2,1,0:T(8,128)}), f32[16,8,128]{2,1,0:T(8,128)S(1)}, u32[]{:S(2)}, u32[]{:S(2)}) %all-to-all-start.1) | async-done | bytes 65568 | tf_op jit(solution)/shard_map/all_to_all | solution.py:349
  48.7 0.5 %slice_reduce_fusion = f32[64]{0:T(128)} fusion(f32[16,8,128]{2,1,0:T(8,128)S(1)} %all-to-all-done.1), kind=kLoop, calls=%fused_computation.22 | loop fusion | flops 960 | bytes 4352 | tf_op jit(solution)/shard_map/reduce_sum | solution.py:384
  (31 shorter events, 0.6 us)
Async XLA Ops:
  0.6 8.2 %copy-start = (bf16[16,40960]{1,0:T(8,128)(2,1)S(1)}, bf16[16,40960]{1,0:T(8,128)(2,1)}, u32[]{:S(2)}) copy-start(bf16[16,40960]{1,0:T(8,128)(2,1)} %t_ref.1) | copy-start | bytes 3932164
  0.6 8.2 %collective-permute-start.1 = (bf16[1,8,1920]{2,1,0:T(8,128)(2,1)}, bf16[1,8,1920]{2,1,0:T(8,128)(2,1)S(1)}, u32[]{:S(2)}, u32[]{:S(2)}) collective-permute-start(bf16[1,8,1920]{2,1,0:T(8,128)(2,1)} %bitcast.13), channel_id=1, source_target_pairs={{0,8},{2,10},{4,12},{6,14},{8,0},{10,2},{12,4},{14,6},{1,9},{3,11}... | collective-permute-start | bytes 92168 | tf_op jit(solution)/shard_map/ppermute | solution.py:239
  6.3 2.4 %collective-permute-start.2 = (f32[2,64]{1,0:T(2,128)S(1)}, f32[2,64]{1,0:T(2,128)S(1)}, u32[]{:S(2)}, u32[]{:S(2)}) collective-permute-start(f32[2,64]{1,0:T(2,128)S(1)} %pad_maximum_fusion.3), channel_id=1, source_target_pairs={{0,1},{1,0},{2,3},{3,2},{4,5},{5,4},{6,7},{7,6},{8,9},{9,8},{10,11... | collective-permute-start | bytes 1544 | tf_op jit(solution)/shard_map/ppermute | solution.py:235
  6.4 3.9 %collective-permute-start = (bf16[16,40960]{1,0:T(8,128)(2,1)}, bf16[16,40960]{1,0:T(8,128)(2,1)S(1)}, u32[]{:S(2)}, u32[]{:S(2)}) collective-permute-start(bf16[16,40960]{1,0:T(8,128)(2,1)} %t_ref.1), channel_id=1, source_target_pairs={{0,1},{1,0},{2,3},{3,2},{4,5},{5,4},{6,7},{7,6},{8,9},{9,8},{10,11... | collective-permute-start | bytes 3932168 | tf_op jit(solution)/shard_map/ppermute | solution.py:235
  10.3 7.4 %copy-start.2 = (bf16[8,1920]{1,0:T(8,128)(2,1)S(1)}, bf16[8,1920]{1,0:T(8,128)(2,1)}, u32[]{:S(2)}) copy-start(bf16[8,1920]{1,0:T(8,128)(2,1)} %param.11) | copy-start | bytes 92164
  13.2 6.6 %copy-start.1 = (bf16[64,4096]{1,0:T(8,128)(2,1)S(1)}, bf16[64,4096]{1,0:T(8,128)(2,1)}, u32[]{:S(2)}) copy-start(bf16[64,4096]{1,0:T(8,128)(2,1)} %param.10) | copy-start | bytes 1572868
  13.2 19.9 %all-to-all-start = ((bf16[8,16,2176]{2,1,0:T(8,128)(2,1)}), bf16[8,16,2176]{2,1,0:T(8,128)(2,1)S(1)}, u32[]{:S(2)}, u32[]{:S(2)}) async-start(bf16[8,16,2176]{2,1,0:T(8,128)(2,1)} %map_rest.1), calls=%async_computation | async-start | bytes 1114112 | tf_op jit(solution)/shard_map/all_to_all | solution.py:317
  17.7 10.2 %collective-permute-start.5 = (bf16[2,8,1920]{2,1,0:T(8,128)(2,1)S(1)}, bf16[2,8,1920]{2,1,0:T(8,128)(2,1)S(1)}, u32[]{:S(2)}, u32[]{:S(2)}) collective-permute-start(bf16[2,8,1920]{2,1,0:T(8,128)(2,1)S(1)} %pad_maximum_fusion.2), channel_id=1, source_target_pairs={{0,4},{2,6},{4,0},{6,2},{8,12},{10,14},{12,8},{14,10},{1,5},{3,7},... | collective-permute-start | bytes 184328 | tf_op jit(solution)/shard_map/ppermute | solution.py:239
  19.8 13.2 %collective-permute-start.3 = (bf16[64,2048]{1,0:T(8,128)(2,1)S(1)}, bf16[64,2048]{1,0:T(8,128)(2,1)S(1)}, u32[]{:S(2)}, u32[]{:S(2)}) collective-permute-start(bf16[64,2048]{1,0:T(8,128)(2,1)S(1)} %constant_dynamic-slice_fusion.1), channel_id=1, source_target_pairs={{0,1},{1,0},{2,3},{3,2},{4,5},{5,4},{6,7},{7,6},{8,9},{9,8},{10,11... | collective-permute-start | bytes 786440 | tf_op jit(solution)/shard_map/ppermute | solution.py:235
  27.9 4.9 %collective-permute-start.6 = (bf16[4,8,1920]{2,1,0:T(8,128)(2,1)S(1)}, bf16[4,8,1920]{2,1,0:T(8,128)(2,1)S(1)}, u32[]{:S(2)}, u32[]{:S(2)}) collective-permute-start(bf16[4,8,1920]{2,1,0:T(8,128)(2,1)S(1)} %pad_maximum_fusion.1), channel_id=1, source_target_pairs={{0,2},{2,0},{4,6},{6,4},{8,10},{10,8},{12,14},{14,12},{1,3},{3,1},... | collective-permute-start | bytes 368648 | tf_op jit(solution)/shard_map/ppermute | solution.py:239
  32.9 9.1 %collective-permute-start.7 = (bf16[8,8,1920]{2,1,0:T(8,128)(2,1)S(1)}, bf16[8,8,1920]{2,1,0:T(8,128)(2,1)S(1)}, u32[]{:S(2)}, u32[]{:S(2)}) collective-permute-start(bf16[8,8,1920]{2,1,0:T(8,128)(2,1)S(1)} %constant_dynamic-update-slice_fusion.own_ref), channel_id=1, source_target_pairs={{0,1},{1,0},{2,3},{3,2},{4,5},{5,4},{6,7},{7,6},{8,9},{9,8},{10,11... | collective-permute-start | bytes 737288 | tf_op jit(solution)/shard_map/ppermute | solution.py:235
  34.4 11.8 %collective-permute-start.4 = (bf16[64,2048]{1,0:T(8,128)(2,1)S(1)}, bf16[64,2048]{1,0:T(8,128)(2,1)S(1)}, u32[]{:S(2)}, u32[]{:S(2)}) collective-permute-start(bf16[64,2048]{1,0:T(8,128)(2,1)S(1)} %constant_dynamic-slice_fusion), channel_id=1, source_target_pairs={{0,1},{1,0},{2,3},{3,2},{4,5},{5,4},{6,7},{7,6},{8,9},{9,8},{10,11... | collective-permute-start | bytes 786440 | tf_op jit(solution)/shard_map/ppermute | solution.py:235
  34.9 13.8 %all-to-all-start.1 = ((f32[16,8,128]{2,1,0:T(8,128)}), f32[16,8,128]{2,1,0:T(8,128)S(1)}, u32[]{:S(2)}, u32[]{:S(2)}) async-start(f32[16,8,128]{2,1,0:T(8,128)} %get-tuple-element.19), calls=%async_computation.1 | async-start | bytes 131072 | tf_op jit(solution)/shard_map/all_to_all | solution.py:349

commit v11 on v10

--- a/solution.py
+++ b/solution.py
@@ -12,12 +12,14 @@
 STEP = 16
 
 
-def block_weights(row_of, weight, rows):
-    row_ids = lax.broadcasted_iota(jnp.int32, (rows + MASS_ROWS, row_of.shape[1]), 0)
+def block_weights(code, rows):
+    row_ids = lax.broadcasted_iota(jnp.int32, (rows + MASS_ROWS, code.shape[1]), 0)
     total = jnp.zeros(row_ids.shape, jnp.float32)
-    for slot in range(row_of.shape[0]):
-        hit = (row_ids == row_of[slot][None, :]) | (row_ids == rows + slot)
-        total = total + jnp.where(hit, weight[slot][None, :], 0.0)
+    for slot in range(TOPA):
+        row = jnp.floor(code[slot])
+        weight = (code[slot] - row) * 2.0
+        hit = (row_ids == row.astype(jnp.int32)[None, :]) | (row_ids == rows + slot)
+        total = total + jnp.where(hit, weight[None, :], 0.0)
     return total.astype(jnp.bfloat16)
 
 
@@ -148,12 +150,8 @@
             terms = terms + jnp.where(positive, one, 0.0)
         sums.append(jnp.sum(terms.T, axis=0, keepdims=True))
     row = jnp.concatenate(sums, axis=1)
-    half_tokens = group_tokens // 2
-    for half in range(2):
-        mine = row[:, half * half_tokens : (half + 1) * half_tokens]
-        tile = jnp.concatenate([mine] * (t_buf.shape[2] // half_tokens), axis=1)
-        for q in range(owners):
-            t_buf[2 * q + half] = jnp.broadcast_to(tile, t_buf.shape[1:])
+    for q in range(owners):
+        t_buf[q] = jnp.broadcast_to(row, t_buf.shape[1:])
     leaving = pltpu.make_async_copy(t_buf, terms_ref, sem)
     leaving.start()
     for i in range(group_tokens // BLK):
@@ -165,28 +163,24 @@
     leaving.wait()
 
 
-def join_kernel(place_ref, grad_ref, got_ref, o_ref, sem):
-    half_tokens, width = got_ref.shape
-    half = place_ref[1]
-    kept_at = pl.ds(pl.multiple_of(half * width, width), width)
-    got_at = pl.ds(pl.multiple_of((1 - half) * width, width), width)
-    rows = pl.ds(pl.multiple_of(half * half_tokens, half_tokens), half_tokens)
-    copies = [
-        pltpu.make_async_copy(grad_ref.at[rows, :], o_ref.at[:, kept_at], sem.at[0]),
-        pltpu.make_async_copy(got_ref, o_ref.at[:, got_at], sem.at[1]),
-    ]
-    for copy in copies:
-        copy.start()
-    for copy in copies:
-        copy.wait()
-
-
 def arrival_order(owners):
-    bits = owners.bit_length() - 1
-    return [sum(((i >> bit) & 1) * (owners >> (bit + 1)) for bit in range(bits)) for i in range(owners)]
-
-
-def weight_kernel(place_ref, own_ref, other_ref, grad_ref, o_ref, s_ref, h_ref, block_ref, sem):
+    return [a for b in range(owners // 2) for a in (b, b + owners // 2)]
+
+
+def weight_blocks(h_ref, grad_ref, o_ref, block_ref, sems, first):
+    steps, tile, _ = block_ref.shape
+    copies = []
+    for i in range(steps):
+        block_ref[i] = jnp.dot(
+            h_ref[i * tile : (i + 1) * tile, :], grad_ref[...], preferred_element_type=jnp.float32
+        ).astype(jnp.bfloat16)
+        rows = pl.ds(first + i * tile, tile)
+        copies.append(pltpu.make_async_copy(block_ref.at[i], o_ref.at[rows, :], sems.at[i]))
+        copies[-1].start()
+    return copies
+
+
+def first_weight_kernel(place_ref, own_ref, other_ref, grad_ref, o_ref, later_ref, s_ref, h_ref, block_ref, sems):
     owners, held, features = own_ref.shape
     for i, offset in enumerate(arrival_order(owners)):
         first = (place_ref[0] ^ offset) * 2
@@ -198,16 +192,27 @@
         for j in range(features // BLK):
             tile = s_ref[i * BLK : (i + 1) * BLK, j * BLK : (j + 1) * BLK].T
             h_ref[j * BLK : (j + 1) * BLK, i * BLK : (i + 1) * BLK] = tile.astype(jnp.bfloat16)
-    steps, tile, _ = block_ref.shape
-    copies = []
-    for i in range(steps):
-        rows = slice(i * tile, (i + 1) * tile)
-        block_ref[i] = jnp.dot(
-            h_ref[rows, :], grad_ref[...], preferred_element_type=jnp.float32
-        ).astype(jnp.bfloat16)
-        copies.append(pltpu.make_async_copy(block_ref.at[i], o_ref.at[pl.ds(i * tile, tile), :], sem.at[i]))
-        copies[-1].start()
+    copies = weight_blocks(h_ref, grad_ref, o_ref, block_ref, sems, 0)
+    later_ref[...] = h_ref[features // 2 :, :]
     for copy in copies:
+        copy.wait()
+
+
+def second_weight_kernel(
+    place_ref, h_ref, grad_ref, got_ref, sums_ref, half_ref, o_ref, joined_ref, block_ref, sems, join_sems
+):
+    half_tokens, width = got_ref.shape
+    half = place_ref[1]
+    kept_at = pl.ds(pl.multiple_of(half * width, width), width)
+    got_at = pl.ds(pl.multiple_of((1 - half) * width, width), width)
+    rows = pl.ds(pl.multiple_of(half * half_tokens, half_tokens), half_tokens)
+    copies = [
+        pltpu.make_async_copy(grad_ref.at[rows, :], joined_ref.at[:, kept_at], join_sems.at[0]),
+        pltpu.make_async_copy(got_ref, joined_ref.at[:, got_at], join_sems.at[1]),
+    ]
+    for copy in copies:
+        copy.start()
+    for copy in copies + weight_blocks(h_ref, grad_ref, o_ref, block_ref, sems, h_ref.shape[0]):
         copy.wait()
 
 
@@ -279,10 +284,10 @@
 
     local = align_local.T - half_index * mine
     row_of = jnp.where((local >= 0) & (local < mine), align_owner.T * mine + local, -1)
-    weight = jnp.where(align_owner.T >= 0, align_weight.T.astype(f32), 0.0)
-    cut = lambda x, which: lax.dynamic_slice_in_dim(x, which * per_half, per_half, 1)
-    w_own = block_weights(cut(row_of, half_index), cut(weight, half_index), rows)
-    w_rest = block_weights(cut(row_of, 1 - half_index), cut(weight, 1 - half_index), rows)
+    code = row_of.astype(f32) + 0.5 * align_weight.T.astype(f32)
+    cut = lambda which: lax.dynamic_slice_in_dim(code, which * per_half, per_half, 1)
+    w_own = block_weights(cut(half_index), rows)
+    w_rest = block_weights(cut(1 - half_index), rows)
     spread = pltpu.VMEM((per_half * tokens, BLK), f32)
     flops = 2 * (rows + MASS_ROWS) * per_half * tokens * BLK
     part = pl.pallas_call(
@@ -322,21 +327,19 @@
     give = lax.dynamic_slice_in_dim(late_logits, (1 - half_index) * width, width, 1)
     logits = in_order(keep, swap_halves(give), 0)
 
-    hidden_own = jnp.concatenate([hidden, first_piece])
-    while offset > 1:
-        offset //= 2
-        hidden_own = jnp.concatenate([hidden_own, to_partner(hidden_own, offset)])
+    pieces = [jnp.concatenate([hidden, first_piece])]
+    pieces += [to_partner(pieces[0], a) for a in range(1, offset)]
+    hidden_own = jnp.concatenate(pieces)
 
     scale = float(columns * owners)
-    lanes = -(-half_tokens // BLK) * BLK
     grad, terms = pl.pallas_call(
         lambda *refs: grad_kernel(scale, *refs),
-        out_shape=(shape((group_tokens, width), bf16), shape((owners * halves, 8, lanes), f32)),
+        out_shape=(shape((group_tokens, width), bf16), shape((owners, 8, group_tokens), f32)),
         in_specs=[in_vmem()] * 2,
         out_specs=(in_vmem(), anywhere()),
         scratch_shapes=[
             pltpu.VMEM((group_tokens, BLK), f32),
-            pltpu.VMEM((owners * halves, 8, lanes), f32),
+            pltpu.VMEM((owners, 8, group_tokens), f32),
             pltpu.SemaphoreType.DMA,
         ],
         compiler_params=params(),
@@ -346,42 +349,47 @@
         name="logit_grad",
     )(target, logits)
 
-    terms = lax.all_to_all(terms, ("sv", "tv"), 0, 0, tiled=True)
+    terms = lax.all_to_all(terms, "sv", 0, 0, tiled=True)
     give = lax.dynamic_slice_in_dim(grad, (1 - half_index) * half_tokens, half_tokens, 0)
     got = swap_halves(give)
 
-    steps = 8
-    weight_grad = pl.pallas_call(
-        weight_kernel,
-        out_shape=shape((features, width), bf16),
+    steps = 4
+    part_rows = features // 2
+    blocks = pltpu.VMEM((steps, part_rows // steps, width), bf16)
+    weight_cost = cost(
+        features * group_tokens * width, features * width + group_tokens * (features + 2 * width)
+    )
+    weight_grad, hidden_t = pl.pallas_call(
+        first_weight_kernel,
+        out_shape=(shape((features, width), bf16), shape((part_rows, group_tokens), bf16)),
         in_specs=[scalars()] + [in_vmem()] * 3,
-        out_specs=anywhere(),
+        out_specs=(anywhere(), in_vmem()),
         scratch_shapes=[
             pltpu.VMEM((group_tokens, features), f32),
             pltpu.VMEM((features, group_tokens), bf16),
-            pltpu.VMEM((steps, features // steps, width), bf16),
+            blocks,
             dma(steps),
         ],
         compiler_params=params(),
-        cost_estimate=cost(
-            2 * features * group_tokens * width,
-            2 * (features * width + group_tokens * (features + width)),
-        ),
-        name="weight_grad",
+        cost_estimate=weight_cost,
+        name="weight_grad_first",
     )(place, hidden_own, swap_halves(hidden_own), grad)
 
-    logit_grad = pl.pallas_call(
-        join_kernel,
-        out_shape=shape((half_tokens, columns), bf16),
-        in_specs=[scalars(), anywhere(), anywhere()],
-        out_specs=anywhere(),
-        scratch_shapes=[dma(2)],
+    sums = jnp.sum(terms[:, 0], axis=0)
+    sums_other = swap_halves(sums)
+    weight_grad, logit_grad = pl.pallas_call(
+        second_weight_kernel,
+        out_shape=(shape((features, width), bf16), shape((half_tokens, columns), bf16)),
+        in_specs=[scalars(), in_vmem(), in_vmem(), anywhere(), anywhere(), anywhere()],
+        out_specs=(anywhere(), anywhere()),
+        scratch_shapes=[blocks, dma(steps), dma(2)],
+        input_output_aliases={5: 0},
         compiler_params=params(),
-        cost_estimate=cost(0, 4 * half_tokens * columns),
-        name="join",
-    )(place, grad, got)
-    terms, logit_grad, weight_grad = lax.optimization_barrier((terms, logit_grad, weight_grad))
-    divergence = jnp.sum(terms[:, 0, :half_tokens], axis=0)
+        cost_estimate=weight_cost,
+        name="weight_grad_second",
+    )(place, hidden_t, grad, got, sums, weight_grad)
+    sums_other, weight_grad, logit_grad = lax.optimization_barrier((sums_other, weight_grad, logit_grad))
+    divergence = lax.dynamic_slice_in_dim(sums + sums_other, half_index * half_tokens, half_tokens, 0)
     return (divergence, logit_grad, weight_grad)
 
 

time: 49.7 us -> 53.3 us (1.072)
  waiting for transfers between devices: 12.3 us -> 17.9 us
  starting transfers between devices: 20.5 us -> 18.7 us
  other arithmetic: 4.09 us -> 3.03 us
    all_to_all x1, waiting for transfers between devices: 0.01 us -> 12.7 us  [body(): target = lax.all_to_all(outgoing, 'sv', 0, 0, tiled=True)]
    ppermute x3 -> x4, waiting for transfers between devices: 11.2 us -> 0.78 us  [to_partner(): lax.ppermute(x, 'sv', [(s, s ^ offset) for s in range(lax.axis_size('sv'))])]
    all_to_all x1, starting transfers between devices: 6.89 us -> 3.65 us  [body(): terms = lax.all_to_all(terms, 'sv', 0, 0, tiled=True)]
    all_to_all x1, waiting for transfers between devices: 1.13 us -> 3.57 us  [body(): terms = lax.all_to_all(terms, 'sv', 0, 0, tiled=True)]
    all_to_all x1, starting transfers between devices: 4.48 us -> 6.44 us  [body(): target = lax.all_to_all(outgoing, 'sv', 0, 0, tiled=True)]
    select_n x2 -> x0, other arithmetic: 1.42 us -> none  [the longest x1 0.71 us: body(): jnp.where((local >= 0) & (local < mine), align_owner.T * mine + local, -1)]
    ppermute x5 -> x6, waiting for transfers between devices: 0.01 us -> 0.91 us  [swap_halves(): return lax.ppermute(x, 'tv', [(0, 1), (1, 0)])]
    add x0 -> x2, other arithmetic: none -> 0.74 us  [the longest x1 0.73 us: body(): code = row_of.astype(f32) + 0.5 * align_weight.T.astype(f32)]
  transfers between devices with their start and end apart: 10 -> 12, of which waited for: 3 -> 4; matrix products, arithmetic and copies ran while one was open for 8% -> 3% of each run, Pallas kernels for 17% -> 16%
where the time goes in v11:
time: 53.3 us; the launch traced here: 52.9 us
  starting transfers between devices  18.7 us (35%)
  waiting for transfers between devices  17.9 us (34%)
  Pallas kernels  11.5 us (22%)
  other arithmetic  3.03 us (6%)
  between operations  0.87 us (2%)
  local copies, waits for them, and re-layouts  0.81 us (2%)
    all_to_all x1, waiting for transfers between devices, body(): target = lax.all_to_all(outgoing, 'sv', 0, 0, tiled=True)  12.7 us
    ppermute x4, starting transfers between devices, to_partner(): lax.ppermute(x, 'sv', [(s, s ^ offset) for s in range(lax.axis_size('sv'))])  7.22 us
    all_to_all x1, starting transfers between devices, body(): target = lax.all_to_all(outgoing, 'sv', 0, 0, tiled=True)  6.44 us
    all_to_all x1, starting transfers between devices, body(): terms = lax.all_to_all(terms, 'sv', 0, 0, tiled=True)  3.65 us
    all_to_all x1, waiting for transfers between devices, body(): terms = lax.all_to_all(terms, 'sv', 0, 0, tiled=True)  3.57 us
    pallas_call x1, Pallas kernels, body(): pl.pallas_call(second_weight_kernel, out_shape=(shape((features, width),...  3.08 us
    pallas_call x1, Pallas kernels, body(): pl.pallas_call(first_weight_kernel, out_shape=(shape((features, width), b...  3.03 us
    pallas_call x1, Pallas kernels, body(): pl.pallas_call(map_rest_kernel, out_shape=shape(chunk, bf16), in_specs=[i...  2.86 us
  transfers between devices with their start and end apart: 12, of which 4 were waited for; matrix products, arithmetic and copies ran while one was open for 3% of the time, Pallas kernels for 16%

profile of v11, /device:TPU:0, one launch (start us, length us, event | category | flops | bytes accessed | tf_op | source)
XLA Modules:
  0.0 52.9 jit_solution(9788838376107440638)
XLA Ops:
  0.6 1.7 %convert_reduce_fusion = (f32[64]{0:T(128)S(1)}, f32[64]{0:T(128)S(1)}) fusion(bf16[64,4096]{1,0:T(8,128)(2,1)} %param.10), kind=kLoop, calls=%fused_computation | loop fusion | flops 1834624 | bytes 524800 | tf_op jit(solution)/shard_map/reduce | solution.py:280
  2.3 0.5 collective-permute-start
  2.8 3.7 %collective-permute-start.1 = (bf16[1,8,1920]{2,1,0:T(8,128)(2,1)}, bf16[1,8,1920]{2,1,0:T(8,128)(2,1)S(1)}, u32[]{:S(2)}, u32[]{:S(2)}) collective-permute-start(bf16[1,8,1920]{2,1,0:T(8,128)(2,1)} %bitcast.9), channel_id=1, source_target_pairs={{0,8},{2,10},{4,12},{6,14},{8,0},{10,2},{12,4},{14,6},{1,9},{3,11}... | collective-permute-start | bytes 92168 | tf_op jit(solution)/shard_map/ppermute | solution.py:244
  6.5 0.2 collective-permute-start.2
  6.7 0.7 %fusion.5 = f32[640,2]{0,1:T(2,128)S(1)} fusion(bf16[640,2]{0,1:T(2,128)(2,1)} %param.9, s32[640,2]{0,1:T(2,128)} %param.7, s32[640,2]{0,1:T(2,128)} %param.8, s32[]{:T(128)S(6)} %mul.54), kind=kLoop, calls=%fused_computation.23 | loop fusion | flops 14080 | bytes 17924 | tf_op jit(solution)/shard_map/add | solution.py:287
  7.4 0.1 dynamic-slice_bitcast_fusion
  7.6 0.2 add_convert_fusion
  7.9 0.8 %collective-permute-done.1.first_ref = bf16[1,8,1920]{2,1,0:T(8,128)(2,1)S(1)} collective-permute-done((bf16[1,8,1920]{2,1,0:T(8,128)(2,1)}, bf16[1,8,1920]{2,1,0:T(8,128)(2,1)S(1)}, u32[]{:S(2)}, u32[]{:S(2)}) %collective-permute-start.1) | collective-permute-done | bytes 30752 | tf_op jit(solution)/shard_map/ppermute | solution.py:244
  8.7 1.4 %map_own.1.p_ref = f32[144,2048]{1,0:T(8,128)S(1)} custom-call(bf16[144,320]{1,0:T(8,128)(2,1)S(1)} %get-tuple-element.51.w_ref, bf16[16,40960]{1,0:T(8,128)(2,1)S(1)} %copy-done, bf16[1,8,1920]{2,1,0:T(8,128)(2,1)S(1)} %collective-permute-done.1.first_ref), custom_call_target="tpu_custom_call" | custom-call | flops 188743680 | bytes 3145728 | tf_op jit(solution)/shard_map/map_own/pallas_call | solution.py:293
  10.1 2.9 %map_rest.1 = bf16[8,16,2176]{2,1,0:T(8,128)(2,1)} custom-call(bf16[144,320]{1,0:T(8,128)(2,1)S(1)} %get-tuple-element.52.w_ref, bf16[16,40960]{1,0:T(8,128)(2,1)S(1)} %collective-permute-done.t_ref, f32[144,2048]{1,0:T(8,128)S(1)} %map_own.1.p_ref, f32[2,128]{1,0:T(2,128)S(1)} %pad_maximum_fusion.2.stats_ref), custom_call_target="tpu_custom_call" | custom-call | flops 188743680 | bytes 4194304 | tf_op jit(solution)/shard_map/map_rest/pallas_call | solution.py:305
  13.0 1.8 %collective-permute-start.5 = (bf16[2,8,1920]{2,1,0:T(8,128)(2,1)S(1)}, bf16[2,8,1920]{2,1,0:T(8,128)(2,1)S(1)}, u32[]{:S(2)}, u32[]{:S(2)}) collective-permute-start(bf16[2,8,1920]{2,1,0:T(8,128)(2,1)S(1)} %get-tuple-element.43), channel_id=1, source_target_pairs={{0,2},{2,0},{4,6},{6,4},{8,10},{10,8},{12,14},{14,12},{1,3},{3,1},... | collective-permute-start | bytes 184328 | tf_op jit(solution)/shard_map/ppermute | solution.py:244
  14.9 1.6 %collective-permute-start.6 = (bf16[2,8,1920]{2,1,0:T(8,128)(2,1)S(1)}, bf16[2,8,1920]{2,1,0:T(8,128)(2,1)S(1)}, u32[]{:S(2)}, u32[]{:S(2)}) collective-permute-start(bf16[2,8,1920]{2,1,0:T(8,128)(2,1)S(1)} %get-tuple-element.43), channel_id=1, source_target_pairs={{0,4},{2,6},{4,0},{6,2},{8,12},{10,14},{12,8},{14,10},{1,5},{3,7},... | collective-permute-start | bytes 184328 | tf_op jit(solution)/shard_map/ppermute | solution.py:244
  16.4 0.1 collective-permute-start.7
  16.6 6.4 %all-to-all-start = ((bf16[8,16,2176]{2,1,0:T(8,128)(2,1)}), bf16[8,16,2176]{2,1,0:T(8,128)(2,1)S(1)}, u32[]{:S(2)}, u32[]{:S(2)}) async-start(bf16[8,16,2176]{2,1,0:T(8,128)(2,1)} %map_rest.1), calls=%async_computation | async-start | bytes 1114112 | tf_op jit(solution)/shard_map/all_to_all | solution.py:322
  23.2 0.5 %collective-permute-start.8 = (bf16[8,8,1920]{2,1,0:T(8,128)(2,1)S(1)}, bf16[8,8,1920]{2,1,0:T(8,128)(2,1)S(1)}, u32[]{:S(2)}, u32[]{:S(2)}) collective-permute-start(bf16[8,8,1920]{2,1,0:T(8,128)(2,1)S(1)} %constant_dynamic-update-slice_fusion.2.own_ref), channel_id=1, source_target_pairs={{0,1},{1,0},{2,3},{3,2},{4,5},{5,4},{6,7},{7,6},{8,9},{9,8},{10,11... | collective-permute-start | bytes 737288 | tf_op jit(solution)/shard_map/ppermute | solution.py:240
  23.8 0.9 %collective-permute-done.3 = bf16[64,2048]{1,0:T(8,128)(2,1)S(1)} collective-permute-done((bf16[64,2048]{1,0:T(8,128)(2,1)S(1)}, bf16[64,2048]{1,0:T(8,128)(2,1)S(1)}, u32[]{:S(2)}, u32[]{:S(2)}) %collective-permute-start.3) | collective-permute-done | bytes 262176 | tf_op jit(solution)/shard_map/ppermute | solution.py:240
  24.7 0.1 broadcast_select_fusion.1
  24.8 12.7 %all-to-all-done.refs_0_ = bf16[8,16,2176]{2,1,0:T(8,128)(2,1)S(1)} async-done(((bf16[8,16,2176]{2,1,0:T(8,128)(2,1)}), bf16[8,16,2176]{2,1,0:T(8,128)(2,1)S(1)}, u32[]{:S(2)}, u32[]{:S(2)}) %all-to-all-start) | async-done | bytes 557088 | tf_op jit(solution)/shard_map/all_to_all | solution.py:322
  37.5 1.1 %logit_grad.1 = (bf16[128,2048]{1,0:T(8,128)(2,1)S(1)}, f32[8,8,128]{2,1,0:T(8,128)}) custom-call(bf16[8,16,2176]{2,1,0:T(8,128)(2,1)S(1)} %all-to-all-done.refs_0_, bf16[128,2048]{1,0:T(8,128)(2,1)S(1)} %pad_maximum_fusion.refs_1_), custom_call_target="tpu_custom_call" | custom-call | flops 2621440 | bytes 1572864 | tf_op jit(solution)/shard_map/logit_grad/pallas_call | solution.py:335
  38.8 3.6 %all-to-all-start.1 = ((f32[8,8,128]{2,1,0:T(8,128)}), f32[8,8,128]{2,1,0:T(8,128)S(1)}, u32[]{:S(2)}, u32[]{:S(2)}) async-start(f32[8,8,128]{2,1,0:T(8,128)} %get-tuple-element.23), calls=%async_computation.1 | async-start | bytes 65536 | tf_op jit(solution)/shard_map/all_to_all | solution.py:352
  42.5 3.0 %weight_grad_first.1 = (bf16[1920,2048]{1,0:T(8,128)(2,1)}, bf16[960,128]{1,0:T(8,128)(2,1)S(1)}) custom-call(s32[2]{0:T(128)S(1)} %pad_add_fusion.place_ref, bf16[8,8,1920]{2,1,0:T(8,128)(2,1)S(1)} %constant_dynamic-update-slice_fusion.2.own_ref, bf16[8,8,1920]{2,1,0:T(8,128)(2,1)S(1)} %collective-permute-done.8.other_ref, ...), custom_call_target="tpu_custom_call" | custom-call | flops 503316480 | bytes 4702208 | tf_op jit(solution)/shard_map/weight_grad_first/pallas_call | solution.py:362
  45.5 3.6 %all-to-all-done.1 = f32[8,8,128]{2,1,0:T(8,128)S(1)} async-done(((f32[8,8,128]{2,1,0:T(8,128)}), f32[8,8,128]{2,1,0:T(8,128)S(1)}, u32[]{:S(2)}, u32[]{:S(2)}) %all-to-all-start.1) | async-done | bytes 32800 | tf_op jit(solution)/shard_map/all_to_all | solution.py:352
  49.2 3.1 %weight_grad_second.1 = (bf16[1920,2048]{1,0:T(8,128)(2,1)}, bf16[64,4096]{1,0:T(8,128)(2,1)}) custom-call(s32[2]{0:T(128)S(1)} %pad_add_fusion.place_ref, bf16[960,128]{1,0:T(8,128)(2,1)S(1)} %get-tuple-element.26.h_ref, bf16[128,2048]{1,0:T(8,128)(2,1)S(1)} %get-tuple-element.25.grad_ref, ...), custom_call_target="tpu_custom_call", output_to_operand_aliasing={{0}: (5, {})} | custom-call | flops 503316480 | bytes 4702208 | tf_op jit(solution)/shard_map/weight_grad_second/pallas_call | solution.py:380
  52.3 0.6 %dynamic_slice.23 = f32[64]{0:T(128)} dynamic-slice(f32[128]{0:T(128)S(1)} %add.45, s32[]{:T(128)S(6)} %select_n.79), dynamic_slice_sizes={64} | dynamic-slice | bytes 516 | tf_op jit(solution)/shard_map/dynamic_slice | solution.py:392
  (34 shorter events, 0.7 us)
Async XLA Ops:
  0.6 8.0 %copy-start = (bf16[16,40960]{1,0:T(8,128)(2,1)S(1)}, bf16[16,40960]{1,0:T(8,128)(2,1)}, u32[]{:S(2)}) copy-start(bf16[16,40960]{1,0:T(8,128)(2,1)} %t_ref.1) | copy-start | bytes 3932164
  2.3 7.7 %collective-permute-start = (bf16[16,40960]{1,0:T(8,128)(2,1)}, bf16[16,40960]{1,0:T(8,128)(2,1)S(1)}, u32[]{:S(2)}, u32[]{:S(2)}) collective-permute-start(bf16[16,40960]{1,0:T(8,128)(2,1)} %t_ref.1), channel_id=1, source_target_pairs={{0,1},{1,0},{2,3},{3,2},{4,5},{5,4},{6,7},{7,6},{8,9},{9,8},{10,11... | collective-permute-start | bytes 3932168 | tf_op jit(solution)/shard_map/ppermute | solution.py:240
  2.8 5.8 %collective-permute-start.1 = (bf16[1,8,1920]{2,1,0:T(8,128)(2,1)}, bf16[1,8,1920]{2,1,0:T(8,128)(2,1)S(1)}, u32[]{:S(2)}, u32[]{:S(2)}) collective-permute-start(bf16[1,8,1920]{2,1,0:T(8,128)(2,1)} %bitcast.9), channel_id=1, source_target_pairs={{0,8},{2,10},{4,12},{6,14},{8,0},{10,2},{12,4},{14,6},{1,9},{3,11}... | collective-permute-start | bytes 92168 | tf_op jit(solution)/shard_map/ppermute | solution.py:244
  6.5 1.3 %collective-permute-start.2 = (f32[2,64]{1,0:T(2,128)S(1)}, f32[2,64]{1,0:T(2,128)S(1)}, u32[]{:S(2)}, u32[]{:S(2)}) collective-permute-start(f32[2,64]{1,0:T(2,128)S(1)} %pad_maximum_fusion.1), channel_id=1, source_target_pairs={{0,1},{1,0},{2,3},{3,2},{4,5},{5,4},{6,7},{7,6},{8,9},{9,8},{10,11... | collective-permute-start | bytes 1544 | tf_op jit(solution)/shard_map/ppermute | solution.py:240
  10.1 2.9 %copy-start.2 = (bf16[8,1920]{1,0:T(8,128)(2,1)S(1)}, bf16[8,1920]{1,0:T(8,128)(2,1)}, u32[]{:S(2)}) copy-start(bf16[8,1920]{1,0:T(8,128)(2,1)} %param.11) | copy-start | bytes 92164
  13.0 10.0 %copy-start.1 = (bf16[64,4096]{1,0:T(8,128)(2,1)S(1)}, bf16[64,4096]{1,0:T(8,128)(2,1)}, u32[]{:S(2)}) copy-start(bf16[64,4096]{1,0:T(8,128)(2,1)} %param.10) | copy-start | bytes 1572868
  13.0 10.1 %collective-permute-start.5 = (bf16[2,8,1920]{2,1,0:T(8,128)(2,1)S(1)}, bf16[2,8,1920]{2,1,0:T(8,128)(2,1)S(1)}, u32[]{:S(2)}, u32[]{:S(2)}) collective-permute-start(bf16[2,8,1920]{2,1,0:T(8,128)(2,1)S(1)} %get-tuple-element.43), channel_id=1, source_target_pairs={{0,2},{2,0},{4,6},{6,4},{8,10},{10,8},{12,14},{14,12},{1,3},{3,1},... | collective-permute-start | bytes 184328 | tf_op jit(solution)/shard_map/ppermute | solution.py:244
  14.9 8.3 %collective-permute-start.6 = (bf16[2,8,1920]{2,1,0:T(8,128)(2,1)S(1)}, bf16[2,8,1920]{2,1,0:T(8,128)(2,1)S(1)}, u32[]{:S(2)}, u32[]{:S(2)}) collective-permute-start(bf16[2,8,1920]{2,1,0:T(8,128)(2,1)S(1)} %get-tuple-element.43), channel_id=1, source_target_pairs={{0,4},{2,6},{4,0},{6,2},{8,12},{10,14},{12,8},{14,10},{1,5},{3,7},... | collective-permute-start | bytes 184328 | tf_op jit(solution)/shard_map/ppermute | solution.py:244
  16.4 6.8 %collective-permute-start.7 = (bf16[2,8,1920]{2,1,0:T(8,128)(2,1)S(1)}, bf16[2,8,1920]{2,1,0:T(8,128)(2,1)S(1)}, u32[]{:S(2)}, u32[]{:S(2)}) collective-permute-start(bf16[2,8,1920]{2,1,0:T(8,128)(2,1)S(1)} %get-tuple-element.43), channel_id=1, source_target_pairs={{0,6},{2,4},{4,2},{6,0},{8,14},{10,12},{12,10},{14,8},{1,7},{3,5},... | collective-permute-start | bytes 184328 | tf_op jit(solution)/shard_map/ppermute | solution.py:244
  16.6 20.9 %all-to-all-start = ((bf16[8,16,2176]{2,1,0:T(8,128)(2,1)}), bf16[8,16,2176]{2,1,0:T(8,128)(2,1)S(1)}, u32[]{:S(2)}, u32[]{:S(2)}) async-start(bf16[8,16,2176]{2,1,0:T(8,128)(2,1)} %map_rest.1), calls=%async_computation | async-start | bytes 1114112 | tf_op jit(solution)/shard_map/all_to_all | solution.py:322
  23.1 1.6 %collective-permute-start.3 = (bf16[64,2048]{1,0:T(8,128)(2,1)S(1)}, bf16[64,2048]{1,0:T(8,128)(2,1)S(1)}, u32[]{:S(2)}, u32[]{:S(2)}) collective-permute-start(bf16[64,2048]{1,0:T(8,128)(2,1)S(1)} %constant_dynamic-slice_fusion.1), channel_id=1, source_target_pairs={{0,1},{1,0},{2,3},{3,2},{4,5},{5,4},{6,7},{7,6},{8,9},{9,8},{10,11... | collective-permute-start | bytes 786440 | tf_op jit(solution)/shard_map/ppermute | solution.py:240
  23.2 19.3 %collective-permute-start.8 = (bf16[8,8,1920]{2,1,0:T(8,128)(2,1)S(1)}, bf16[8,8,1920]{2,1,0:T(8,128)(2,1)S(1)}, u32[]{:S(2)}, u32[]{:S(2)}) collective-permute-start(bf16[8,8,1920]{2,1,0:T(8,128)(2,1)S(1)} %constant_dynamic-update-slice_fusion.2.own_ref), channel_id=1, source_target_pairs={{0,1},{1,0},{2,3},{3,2},{4,5},{5,4},{6,7},{7,6},{8,9},{9,8},{10,11... | collective-permute-start | bytes 737288 | tf_op jit(solution)/shard_map/ppermute | solution.py:240
  38.7 10.5 %collective-permute-start.9 = (bf16[64,2048]{1,0:T(8,128)(2,1)S(1)}, bf16[64,2048]{1,0:T(8,128)(2,1)S(1)}, u32[]{:S(2)}, u32[]{:S(2)}) collective-permute-start(bf16[64,2048]{1,0:T(8,128)(2,1)S(1)} %constant_dynamic-slice_fusion), channel_id=1, source_target_pairs={{0,1},{1,0},{2,3},{3,2},{4,5},{5,4},{6,7},{7,6},{8,9},{9,8},{10,11... | collective-permute-start | bytes 786440 | tf_op jit(solution)/shard_map/ppermute | solution.py:240
  38.8 10.3 %all-to-all-start.1 = ((f32[8,8,128]{2,1,0:T(8,128)}), f32[8,8,128]{2,1,0:T(8,128)S(1)}, u32[]{:S(2)}, u32[]{:S(2)}) async-start(f32[8,8,128]{2,1,0:T(8,128)} %get-tuple-element.23), calls=%async_computation.1 | async-start | bytes 65536 | tf_op jit(solution)/shard_map/all_to_all | solution.py:352
  49.1 3.2 %collective-permute-start.4 = (f32[128]{0:T(128)S(1)}, f32[128]{0:T(128)S(1)}, u32[]{:S(2)}, u32[]{:S(2)}) collective-permute-start(f32[128]{0:T(128)S(1)} %slice_reduce_fusion.sums_ref), channel_id=1, source_target_pairs={{0,1},{1,0},{2,3},{3,2},{4,5},{5,4},{6,7},{7,6},{8,9},{9,8},{10,11... | collective-permute-start | bytes 1544 | tf_op jit(solution)/shard_map/ppermute | solution.py:240

commit v12 on v10

--- a/solution.py
+++ b/solution.py
@@ -12,20 +12,15 @@
 STEP = 16
 
 
-def block_weights(row_of, weight, rows):
-    row_ids = lax.broadcasted_iota(jnp.int32, (rows + MASS_ROWS, row_of.shape[1]), 0)
+def block_weights(code, rows):
+    row_ids = lax.broadcasted_iota(jnp.int32, (rows + MASS_ROWS, code.shape[1]), 0)
     total = jnp.zeros(row_ids.shape, jnp.float32)
-    for slot in range(row_of.shape[0]):
-        hit = (row_ids == row_of[slot][None, :]) | (row_ids == rows + slot)
-        total = total + jnp.where(hit, weight[slot][None, :], 0.0)
+    for slot in range(TOPA):
+        row = jnp.floor(code[slot])
+        weight = (code[slot] - row) * 2.0
+        hit = (row_ids == row.astype(jnp.int32)[None, :]) | (row_ids == rows + slot)
+        total = total + jnp.where(hit, weight[None, :], 0.0)
     return total.astype(jnp.bfloat16)
-
-
-def column_copies(source, target, sems, first=0):
-    cuts = sems.shape[0] - first
-    wide = source.shape[1] // cuts
-    at = [pl.ds(i * wide, wide) for i in range(cuts)]
-    return [pltpu.make_async_copy(source.at[:, at[i]], target.at[:, at[i]], sems.at[first + i]) for i in range(cuts)]
 
 
 def spread_tokens(t_ref, s_ref, start, count):
@@ -39,13 +34,6 @@
         return carry
 
     lax.fori_loop(0, count // STEP, some, 0)
-
-
-def spread_arriving(copies, t_buf, s_ref):
-    blocks = t_buf.shape[1] // BLK // len(copies)
-    for i, copy in enumerate(copies):
-        copy.wait()
-        spread_tokens(t_buf, s_ref, i * blocks, blocks)
 
 
 def token_pair(s_ref, t, tokens):
@@ -71,21 +59,18 @@
     return parts
 
 
-def map_rest_kernel(w_ref, t_ref, p_ref, stats_ref, o_ref, t_buf, s_ref, m_ref, o_buf, in_sem, out_sem):
+def map_rest_kernel(w_ref, t_ref, p_ref, stats_ref, o_ref, s_ref, m_ref, o_buf, out_sem):
     tokens = t_ref.shape[0]
     owners = o_ref.shape[0]
     rows = w_ref.shape[0] - MASS_ROWS
     mine = rows // owners
-    arriving = column_copies(t_ref, t_buf, in_sem)
-    for copy in arriving:
-        copy.start()
     stats = [stats_ref[0:1, :]] + three_parts(stats_ref[1:2, :])
     extra = jnp.zeros((tokens, stats_ref.shape[1]), jnp.float32)
     row_ids = lax.broadcasted_iota(jnp.int32, extra.shape, 0)
     for i, row in enumerate(stats):
         extra = jnp.where(row_ids == i, row, extra)
     extra = extra.astype(jnp.bfloat16)
-    spread_arriving(arriving, t_buf, s_ref)
+    spread_tokens(t_ref, s_ref, 0, t_ref.shape[1] // BLK)
     for t in range(0, tokens, 2):
         both = p_ref[:, t * BLK : (t + 2) * BLK] + jnp.dot(
             w_ref[...], token_pair(s_ref, t, tokens), preferred_element_type=jnp.float32
@@ -165,33 +150,29 @@
     leaving.wait()
 
 
-def join_kernel(place_ref, grad_ref, got_ref, o_ref, sem):
+def arrival_order(owners):
+    return [a for b in range(owners // 2) for a in (b, b + owners // 2)]
+
+
+def weight_kernel(
+    place_ref, own_ref, other_ref, grad_ref, got_ref, o_ref, joined_ref, s_ref, h_ref, block_ref, sems, join_sems
+):
     half_tokens, width = got_ref.shape
     half = place_ref[1]
     kept_at = pl.ds(pl.multiple_of(half * width, width), width)
     got_at = pl.ds(pl.multiple_of((1 - half) * width, width), width)
-    rows = pl.ds(pl.multiple_of(half * half_tokens, half_tokens), half_tokens)
+    kept = pl.ds(pl.multiple_of(half * half_tokens, half_tokens), half_tokens)
     copies = [
-        pltpu.make_async_copy(grad_ref.at[rows, :], o_ref.at[:, kept_at], sem.at[0]),
-        pltpu.make_async_copy(got_ref, o_ref.at[:, got_at], sem.at[1]),
+        pltpu.make_async_copy(grad_ref.at[kept, :], joined_ref.at[:, kept_at], join_sems.at[0]),
+        pltpu.make_async_copy(got_ref, joined_ref.at[:, got_at], join_sems.at[1]),
     ]
     for copy in copies:
         copy.start()
-    for copy in copies:
-        copy.wait()
-
-
-def arrival_order(owners):
-    bits = owners.bit_length() - 1
-    return [sum(((i >> bit) & 1) * (owners >> (bit + 1)) for bit in range(bits)) for i in range(owners)]
-
-
-def weight_kernel(place_ref, own_ref, other_ref, grad_ref, o_ref, s_ref, h_ref, block_ref, sem):
     owners, held, features = own_ref.shape
     for i, offset in enumerate(arrival_order(owners)):
         first = (place_ref[0] ^ offset) * 2
-        own = pl.ds(pl.multiple_of((first + place_ref[1]) * held, held), held)
-        other = pl.ds(pl.multiple_of((first + 1 - place_ref[1]) * held, held), held)
+        own = pl.ds(pl.multiple_of((first + half) * held, held), held)
+        other = pl.ds(pl.multiple_of((first + 1 - half) * held, held), held)
         s_ref[own, :] = own_ref[i].astype(jnp.float32)
         s_ref[other, :] = other_ref[i].astype(jnp.float32)
     for i in range(s_ref.shape[0] // BLK):
@@ -199,13 +180,12 @@
             tile = s_ref[i * BLK : (i + 1) * BLK, j * BLK : (j + 1) * BLK].T
             h_ref[j * BLK : (j + 1) * BLK, i * BLK : (i + 1) * BLK] = tile.astype(jnp.bfloat16)
     steps, tile, _ = block_ref.shape
-    copies = []
     for i in range(steps):
         rows = slice(i * tile, (i + 1) * tile)
         block_ref[i] = jnp.dot(
             h_ref[rows, :], grad_ref[...], preferred_element_type=jnp.float32
         ).astype(jnp.bfloat16)
-        copies.append(pltpu.make_async_copy(block_ref.at[i], o_ref.at[pl.ds(i * tile, tile), :], sem.at[i]))
+        copies.append(pltpu.make_async_copy(block_ref.at[i], o_ref.at[pl.ds(i * tile, tile), :], sems.at[i]))
         copies[-1].start()
     for copy in copies:
         copy.wait()
@@ -279,10 +259,10 @@
 
     local = align_local.T - half_index * mine
     row_of = jnp.where((local >= 0) & (local < mine), align_owner.T * mine + local, -1)
-    weight = jnp.where(align_owner.T >= 0, align_weight.T.astype(f32), 0.0)
-    cut = lambda x, which: lax.dynamic_slice_in_dim(x, which * per_half, per_half, 1)
-    w_own = block_weights(cut(row_of, half_index), cut(weight, half_index), rows)
-    w_rest = block_weights(cut(row_of, 1 - half_index), cut(weight, 1 - half_index), rows)
+    code = row_of.astype(f32) + 0.5 * align_weight.T.astype(f32)
+    cut = lambda which: lax.dynamic_slice_in_dim(code, which * per_half, per_half, 1)
+    w_own = block_weights(cut(half_index), rows)
+    w_rest = block_weights(cut(1 - half_index), rows)
     spread = pltpu.VMEM((per_half * tokens, BLK), f32)
     flops = 2 * (rows + MASS_ROWS) * per_half * tokens * BLK
     part = pl.pallas_call(
@@ -295,19 +275,16 @@
         cost_estimate=cost(flops, 3 << 20),
         name="map_own",
     )(w_own, teacher_probs, first_piece)
-    cuts = 4
     chunk = (owners, tokens, width + group_tokens)
     outgoing = pl.pallas_call(
         map_rest_kernel,
         out_shape=shape(chunk, bf16),
-        in_specs=[in_vmem(), anywhere(), in_vmem(), in_vmem()],
+        in_specs=[in_vmem()] * 4,
         out_specs=anywhere(),
         scratch_shapes=[
-            pltpu.VMEM((tokens, per_half * BLK), bf16),
             spread,
             pltpu.VMEM(((rows + 8) * tokens, BLK), f32),
             pltpu.VMEM(chunk, bf16),
-            dma(cuts),
             dma(owners),
         ],
         compiler_params=params(),
@@ -322,10 +299,8 @@
     give = lax.dynamic_slice_in_dim(late_logits, (1 - half_index) * width, width, 1)
     logits = in_order(keep, swap_halves(give), 0)
 
-    hidden_own = jnp.concatenate([hidden, first_piece])
-    while offset > 1:
-        offset //= 2
-        hidden_own = jnp.concatenate([hidden_own, to_partner(hidden_own, offset)])
+    pieces = [jnp.concatenate([hidden, first_piece])]
+    pieces += [to_partner(pieces[0], a) for a in range(1, offset)]
 
     scale = float(columns * owners)
     lanes = -(-half_tokens // BLK) * BLK
@@ -350,17 +325,20 @@
     give = lax.dynamic_slice_in_dim(grad, (1 - half_index) * half_tokens, half_tokens, 0)
     got = swap_halves(give)
 
+    *pieces, grad = lax.optimization_barrier((*pieces, grad))
+    hidden_own = jnp.concatenate(pieces)
     steps = 8
-    weight_grad = pl.pallas_call(
+    weight_grad, logit_grad = pl.pallas_call(
         weight_kernel,
-        out_shape=shape((features, width), bf16),
-        in_specs=[scalars()] + [in_vmem()] * 3,
-        out_specs=anywhere(),
+        out_shape=(shape((features, width), bf16), shape((half_tokens, columns), bf16)),
+        in_specs=[scalars()] + [in_vmem()] * 4,
+        out_specs=(anywhere(), anywhere()),
         scratch_shapes=[
             pltpu.VMEM((group_tokens, features), f32),
             pltpu.VMEM((features, group_tokens), bf16),
             pltpu.VMEM((steps, features // steps, width), bf16),
             dma(steps),
+            dma(2),
         ],
         compiler_params=params(),
         cost_estimate=cost(
@@ -368,18 +346,7 @@
             2 * (features * width + group_tokens * (features + width)),
         ),
         name="weight_grad",
-    )(place, hidden_own, swap_halves(hidden_own), grad)
-
-    logit_grad = pl.pallas_call(
-        join_kernel,
-        out_shape=shape((half_tokens, columns), bf16),
-        in_specs=[scalars(), anywhere(), anywhere()],
-        out_specs=anywhere(),
-        scratch_shapes=[dma(2)],
-        compiler_params=params(),
-        cost_estimate=cost(0, 4 * half_tokens * columns),
-        name="join",
-    )(place, grad, got)
+    )(place, hidden_own, swap_halves(hidden_own), grad, got)
     terms, logit_grad, weight_grad = lax.optimization_barrier((terms, logit_grad, weight_grad))
     divergence = jnp.sum(terms[:, 0, :half_tokens], axis=0)
     return (divergence, logit_grad, weight_grad)

time: 49.7 us -> 47.3 us (0.952)
  starting transfers between devices: 20.5 us -> 19 us
  Pallas kernels: 11.1 us -> 9.68 us
  waiting for transfers between devices: 12.3 us -> 13.6 us
  other arithmetic: 4.09 us -> 3.54 us
    all_to_all x1, waiting for transfers between devices: 0.01 us -> 10.4 us  [body(): target = lax.all_to_all(outgoing, 'sv', 0, 0, tiled=True)]
    ppermute x3 -> x4, waiting for transfers between devices: 11.2 us -> 0.88 us  [to_partner(): lax.ppermute(x, 'sv', [(s, s ^ offset) for s in range(lax.axis_size('sv'))])]
    all_to_all x1, starting transfers between devices: 6.89 us -> 3.74 us  [body(): terms = lax.all_to_all(terms, ('sv', 'tv'), 0, 0, tiled=True)]
    all_to_all x1, starting transfers between devices: 4.48 us -> 6.39 us  [body(): target = lax.all_to_all(outgoing, 'sv', 0, 0, tiled=True)]
    select_n x2 -> x0, other arithmetic: 1.42 us -> none  [the longest x1 0.71 us: body(): jnp.where((local >= 0) & (local < mine), align_owner.T * mine + local, -1)]
    all_to_all x1, waiting for transfers between devices: 1.13 us -> 2.32 us  [body(): terms = lax.all_to_all(terms, ('sv', 'tv'), 0, 0, tiled=True)]
    pallas_call x2 -> x1, Pallas kernels: 5.66 us -> 4.48 us  [body(): pl.pallas_call(weight_kernel, out_shape=(shape((features, width), bf16),...]
    add x0 -> x1, other arithmetic: none -> 0.73 us  [body(): code = row_of.astype(f32) + 0.5 * align_weight.T.astype(f32)]
  transfers between devices with their start and end apart: 10 -> 11, of which waited for: 3 -> 3; matrix products, arithmetic and copies ran while one was open for 8% -> 3% of each run, Pallas kernels for 17% -> 15%
where the time goes in v12:
time: 47.3 us; the launch traced here: 46.9 us
  starting transfers between devices  19 us (40%)
  waiting for transfers between devices  13.6 us (29%)
  Pallas kernels  9.68 us (20%)
  other arithmetic  3.54 us (7%)
  between operations  0.85 us (2%)
    all_to_all x1, waiting for transfers between devices, body(): target = lax.all_to_all(outgoing, 'sv', 0, 0, tiled=True)  10.4 us
    ppermute x4, starting transfers between devices, to_partner(): lax.ppermute(x, 'sv', [(s, s ^ offset) for s in range(lax.axis_size('sv'))])  7.62 us
    all_to_all x1, starting transfers between devices, body(): target = lax.all_to_all(outgoing, 'sv', 0, 0, tiled=True)  6.39 us
    pallas_call x1, Pallas kernels, body(): pl.pallas_call(weight_kernel, out_shape=(shape((features, width), bf16),...  4.48 us
    all_to_all x1, starting transfers between devices, body(): terms = lax.all_to_all(terms, ('sv', 'tv'), 0, 0, tiled=True)  3.74 us
    pallas_call x1, Pallas kernels, body(): pl.pallas_call(map_rest_kernel, out_shape=shape(chunk, bf16), in_specs=[i...  2.57 us
    all_to_all x1, waiting for transfers between devices, body(): terms = lax.all_to_all(terms, ('sv', 'tv'), 0, 0, tiled=True)  2.32 us
    another operation x1, other arithmetic, body(): lax.reduce((wide, jnp.ones_like(wide)), (low, jnp.float32(0)), merge, (1,))  1.68 us
  transfers between devices with their start and end apart: 11, of which 3 were waited for; matrix products, arithmetic and copies ran while one was open for 3% of the time, Pallas kernels for 15%

profile of v12, /device:TPU:0, one launch (start us, length us, event | category | flops | bytes accessed | tf_op | source)
XLA Modules:
  0.0 46.9 jit_solution(12612049693050091904)
XLA Ops:
  0.6 1.7 %convert_reduce_fusion = (f32[64]{0:T(128)S(1)}, f32[64]{0:T(128)S(1)}) fusion(bf16[64,4096]{1,0:T(8,128)(2,1)} %param.10), kind=kLoop, calls=%fused_computation | loop fusion | flops 1834624 | bytes 524800 | tf_op jit(solution)/shard_map/reduce | solution.py:255
  2.3 0.5 %collective-permute-start = (bf16[16,40960]{1,0:T(8,128)(2,1)}, bf16[16,40960]{1,0:T(8,128)(2,1)S(1)}, u32[]{:S(2)}, u32[]{:S(2)}) collective-permute-start(bf16[16,40960]{1,0:T(8,128)(2,1)} %t_ref.1), channel_id=1, source_target_pairs={{0,1},{1,0},{2,3},{3,2},{4,5},{5,4},{6,7},{7,6},{8,9},{9,8},{10,11... | collective-permute-start | bytes 3932168 | tf_op jit(solution)/shard_map/ppermute | solution.py:215
  2.8 0.1 collective-permute-start.2
  2.9 4.0 %collective-permute-start.1 = (bf16[1,8,1920]{2,1,0:T(8,128)(2,1)}, bf16[1,8,1920]{2,1,0:T(8,128)(2,1)S(1)}, u32[]{:S(2)}, u32[]{:S(2)}) collective-permute-start(bf16[1,8,1920]{2,1,0:T(8,128)(2,1)} %bitcast.9), channel_id=1, source_target_pairs={{0,8},{2,10},{4,12},{6,14},{8,0},{10,2},{12,4},{14,6},{1,9},{3,11}... | collective-permute-start | bytes 92168 | tf_op jit(solution)/shard_map/ppermute | solution.py:219
  6.9 0.7 %fusion.5 = f32[640,2]{0,1:T(2,128)S(1)} fusion(bf16[640,2]{0,1:T(2,128)(2,1)} %param.9, s32[640,2]{0,1:T(2,128)} %param.7, s32[640,2]{0,1:T(2,128)} %param.8, s32[]{:T(128)S(6)} %mul.51), kind=kLoop, calls=%fused_computation.23 | loop fusion | flops 14080 | bytes 17924 | tf_op jit(solution)/shard_map/add | solution.py:262
  7.7 0.1 dynamic-slice_bitcast_fusion
  7.8 0.2 add_convert_fusion
  8.1 0.1 pad_maximum_fusion.2.stats_ref
  8.1 0.9 %collective-permute-done.1.first_ref = bf16[1,8,1920]{2,1,0:T(8,128)(2,1)S(1)} collective-permute-done((bf16[1,8,1920]{2,1,0:T(8,128)(2,1)}, bf16[1,8,1920]{2,1,0:T(8,128)(2,1)S(1)}, u32[]{:S(2)}, u32[]{:S(2)}) %collective-permute-start.1) | collective-permute-done | bytes 30752 | tf_op jit(solution)/shard_map/ppermute | solution.py:219
  9.0 1.4 %map_own.1.p_ref = f32[144,2048]{1,0:T(8,128)S(1)} custom-call(bf16[144,320]{1,0:T(8,128)(2,1)S(1)} %get-tuple-element.53.w_ref, bf16[16,40960]{1,0:T(8,128)(2,1)S(1)} %copy-done, bf16[1,8,1920]{2,1,0:T(8,128)(2,1)S(1)} %collective-permute-done.1.first_ref), custom_call_target="tpu_custom_call" | custom-call | flops 188743680 | bytes 3145728 | tf_op jit(solution)/shard_map/map_own/pallas_call | solution.py:268
  10.5 2.6 %map_rest.1 = bf16[8,16,2176]{2,1,0:T(8,128)(2,1)} custom-call(bf16[144,320]{1,0:T(8,128)(2,1)S(1)} %get-tuple-element.54.w_ref, bf16[16,40960]{1,0:T(8,128)(2,1)S(1)} %collective-permute-done.t_ref, f32[144,2048]{1,0:T(8,128)S(1)} %map_own.1.p_ref, f32[2,128]{1,0:T(2,128)S(1)} %pad_maximum_fusion.2.stats_ref), custom_call_target="tpu_custom_call" | custom-call | flops 188743680 | bytes 4194304 | tf_op jit(solution)/shard_map/map_rest/pallas_call | solution.py:279
  13.0 6.4 %all-to-all-start = ((bf16[8,16,2176]{2,1,0:T(8,128)(2,1)}), bf16[8,16,2176]{2,1,0:T(8,128)(2,1)S(1)}, u32[]{:S(2)}, u32[]{:S(2)}) async-start(bf16[8,16,2176]{2,1,0:T(8,128)(2,1)} %map_rest.1), calls=%async_computation | async-start | bytes 1114112 | tf_op jit(solution)/shard_map/all_to_all | solution.py:294
  19.6 3.0 %collective-permute-start.6 = (bf16[2,8,1920]{2,1,0:T(8,128)(2,1)S(1)}, bf16[2,8,1920]{2,1,0:T(8,128)(2,1)S(1)}, u32[]{:S(2)}, u32[]{:S(2)}) collective-permute-start(bf16[2,8,1920]{2,1,0:T(8,128)(2,1)S(1)} %constant_dynamic-update-slice_fusion), channel_id=1, source_target_pairs={{0,6},{2,4},{4,2},{6,0},{8,14},{10,12},{12,10},{14,8},{1,7},{3,5},... | collective-permute-start | bytes 184328 | tf_op jit(solution)/shard_map/ppermute | solution.py:219
  22.6 0.6 %collective-permute-start.5 = (bf16[2,8,1920]{2,1,0:T(8,128)(2,1)S(1)}, bf16[2,8,1920]{2,1,0:T(8,128)(2,1)S(1)}, u32[]{:S(2)}, u32[]{:S(2)}) collective-permute-start(bf16[2,8,1920]{2,1,0:T(8,128)(2,1)S(1)} %constant_dynamic-update-slice_fusion), channel_id=1, source_target_pairs={{0,4},{2,6},{4,0},{6,2},{8,12},{10,14},{12,8},{14,10},{1,5},{3,7},... | collective-permute-start | bytes 184328 | tf_op jit(solution)/shard_map/ppermute | solution.py:219
  23.1 0.1 collective-permute-start.4
  23.2 0.1 broadcast_select_fusion.1
  23.4 10.4 %all-to-all-done.refs_0_ = bf16[8,16,2176]{2,1,0:T(8,128)(2,1)S(1)} async-done(((bf16[8,16,2176]{2,1,0:T(8,128)(2,1)}), bf16[8,16,2176]{2,1,0:T(8,128)(2,1)S(1)}, u32[]{:S(2)}, u32[]{:S(2)}) %all-to-all-start) | async-done | bytes 557088 | tf_op jit(solution)/shard_map/all_to_all | solution.py:294
  33.8 1.2 %logit_grad.1 = (bf16[128,2048]{1,0:T(8,128)(2,1)S(1)}, f32[16,8,128]{2,1,0:T(8,128)}) custom-call(bf16[8,16,2176]{2,1,0:T(8,128)(2,1)S(1)} %all-to-all-done.refs_0_, bf16[128,2048]{1,0:T(8,128)(2,1)S(1)} %pad_maximum_fusion.refs_1_), custom_call_target="tpu_custom_call" | custom-call | flops 2621440 | bytes 1572864 | tf_op jit(solution)/shard_map/logit_grad/pallas_call | solution.py:307
  35.2 0.5 %collective-permute-start.7 = (bf16[8,8,1920]{2,1,0:T(8,128)(2,1)S(1)}, bf16[8,8,1920]{2,1,0:T(8,128)(2,1)S(1)}, u32[]{:S(2)}, u32[]{:S(2)}) collective-permute-start(bf16[8,8,1920]{2,1,0:T(8,128)(2,1)S(1)} %constant_dynamic-update-slice_fusion.2.own_ref), channel_id=1, source_target_pairs={{0,1},{1,0},{2,3},{3,2},{4,5},{5,4},{6,7},{7,6},{8,9},{9,8},{10,11... | collective-permute-start | bytes 737288 | tf_op jit(solution)/shard_map/ppermute | solution.py:215
  35.8 3.7 %all-to-all-start.1 = ((f32[16,8,128]{2,1,0:T(8,128)}), f32[16,8,128]{2,1,0:T(8,128)S(1)}, u32[]{:S(2)}, u32[]{:S(2)}) async-start(f32[16,8,128]{2,1,0:T(8,128)} %get-tuple-element.26), calls=%async_computation.1 | async-start | bytes 131072 | tf_op jit(solution)/shard_map/all_to_all | solution.py:324
  39.5 0.1 pad_add_fusion.place_ref
  39.6 4.5 %weight_grad.1 = (bf16[1920,2048]{1,0:T(8,128)(2,1)}, bf16[64,4096]{1,0:T(8,128)(2,1)}) custom-call(s32[2]{0:T(128)S(1)} %pad_add_fusion.place_ref, bf16[8,8,1920]{2,1,0:T(8,128)(2,1)S(1)} %constant_dynamic-update-slice_fusion.2.own_ref, bf16[8,8,1920]{2,1,0:T(8,128)(2,1)S(1)} %collective-permute-done.7.other_ref, ...), custom_call_target="tpu_custom_call" | custom-call | flops 1006632960 | bytes 8880128 | tf_op jit(solution)/shard_map/weight_grad/pallas_call | solution.py:331
  44.1 2.3 %all-to-all-done.1 = f32[16,8,128]{2,1,0:T(8,128)S(1)} async-done(((f32[16,8,128]{2,1,0:T(8,128)}), f32[16,8,128]{2,1,0:T(8,128)S(1)}, u32[]{:S(2)}, u32[]{:S(2)}) %all-to-all-start.1) | async-done | bytes 65568 | tf_op jit(solution)/shard_map/all_to_all | solution.py:324
  46.4 0.5 %slice_reduce_fusion = f32[64]{0:T(128)} fusion(f32[16,8,128]{2,1,0:T(8,128)S(1)} %all-to-all-done.1), kind=kLoop, calls=%fused_computation.21 | loop fusion | flops 960 | bytes 4352 | tf_op jit(solution)/shard_map/reduce_sum | solution.py:351
  (30 shorter events, 0.4 us)
Async XLA Ops:
  0.6 8.4 %copy-start = (bf16[16,40960]{1,0:T(8,128)(2,1)S(1)}, bf16[16,40960]{1,0:T(8,128)(2,1)}, u32[]{:S(2)}) copy-start(bf16[16,40960]{1,0:T(8,128)(2,1)} %t_ref.1) | copy-start | bytes 3932164
  2.3 8.1 %collective-permute-start = (bf16[16,40960]{1,0:T(8,128)(2,1)}, bf16[16,40960]{1,0:T(8,128)(2,1)S(1)}, u32[]{:S(2)}, u32[]{:S(2)}) collective-permute-start(bf16[16,40960]{1,0:T(8,128)(2,1)} %t_ref.1), channel_id=1, source_target_pairs={{0,1},{1,0},{2,3},{3,2},{4,5},{5,4},{6,7},{7,6},{8,9},{9,8},{10,11... | collective-permute-start | bytes 3932168 | tf_op jit(solution)/shard_map/ppermute | solution.py:215
  2.8 5.2 %collective-permute-start.2 = (f32[2,64]{1,0:T(2,128)S(1)}, f32[2,64]{1,0:T(2,128)S(1)}, u32[]{:S(2)}, u32[]{:S(2)}) collective-permute-start(f32[2,64]{1,0:T(2,128)S(1)} %pad_maximum_fusion.1), channel_id=1, source_target_pairs={{0,1},{1,0},{2,3},{3,2},{4,5},{5,4},{6,7},{7,6},{8,9},{9,8},{10,11... | collective-permute-start | bytes 1544 | tf_op jit(solution)/shard_map/ppermute | solution.py:215
  2.9 6.1 %collective-permute-start.1 = (bf16[1,8,1920]{2,1,0:T(8,128)(2,1)}, bf16[1,8,1920]{2,1,0:T(8,128)(2,1)S(1)}, u32[]{:S(2)}, u32[]{:S(2)}) collective-permute-start(bf16[1,8,1920]{2,1,0:T(8,128)(2,1)} %bitcast.9), channel_id=1, source_target_pairs={{0,8},{2,10},{4,12},{6,14},{8,0},{10,2},{12,4},{14,6},{1,9},{3,11}... | collective-permute-start | bytes 92168 | tf_op jit(solution)/shard_map/ppermute | solution.py:219
  10.4 9.0 %copy-start.1 = (bf16[64,4096]{1,0:T(8,128)(2,1)S(1)}, bf16[64,4096]{1,0:T(8,128)(2,1)}, u32[]{:S(2)}) copy-start(bf16[64,4096]{1,0:T(8,128)(2,1)} %param.10) | copy-start | bytes 1572868
  13.0 6.5 %copy-start.2 = (bf16[8,1920]{1,0:T(8,128)(2,1)S(1)}, bf16[8,1920]{1,0:T(8,128)(2,1)}, u32[]{:S(2)}) copy-start(bf16[8,1920]{1,0:T(8,128)(2,1)} %param.11) | copy-start | bytes 92164
  13.0 20.7 %all-to-all-start = ((bf16[8,16,2176]{2,1,0:T(8,128)(2,1)}), bf16[8,16,2176]{2,1,0:T(8,128)(2,1)S(1)}, u32[]{:S(2)}, u32[]{:S(2)}) async-start(bf16[8,16,2176]{2,1,0:T(8,128)(2,1)} %map_rest.1), calls=%async_computation | async-start | bytes 1114112 | tf_op jit(solution)/shard_map/all_to_all | solution.py:294
  19.5 3.7 %collective-permute-start.3 = (bf16[64,2048]{1,0:T(8,128)(2,1)S(1)}, bf16[64,2048]{1,0:T(8,128)(2,1)S(1)}, u32[]{:S(2)}, u32[]{:S(2)}) collective-permute-start(bf16[64,2048]{1,0:T(8,128)(2,1)S(1)} %constant_dynamic-slice_fusion.1), channel_id=1, source_target_pairs={{0,1},{1,0},{2,3},{3,2},{4,5},{5,4},{6,7},{7,6},{8,9},{9,8},{10,11... | collective-permute-start | bytes 786440 | tf_op jit(solution)/shard_map/ppermute | solution.py:215
  19.6 15.4 %collective-permute-start.6 = (bf16[2,8,1920]{2,1,0:T(8,128)(2,1)S(1)}, bf16[2,8,1920]{2,1,0:T(8,128)(2,1)S(1)}, u32[]{:S(2)}, u32[]{:S(2)}) collective-permute-start(bf16[2,8,1920]{2,1,0:T(8,128)(2,1)S(1)} %constant_dynamic-update-slice_fusion), channel_id=1, source_target_pairs={{0,6},{2,4},{4,2},{6,0},{8,14},{10,12},{12,10},{14,8},{1,7},{3,5},... | collective-permute-start | bytes 184328 | tf_op jit(solution)/shard_map/ppermute | solution.py:219
  22.6 12.4 %collective-permute-start.5 = (bf16[2,8,1920]{2,1,0:T(8,128)(2,1)S(1)}, bf16[2,8,1920]{2,1,0:T(8,128)(2,1)S(1)}, u32[]{:S(2)}, u32[]{:S(2)}) collective-permute-start(bf16[2,8,1920]{2,1,0:T(8,128)(2,1)S(1)} %constant_dynamic-update-slice_fusion), channel_id=1, source_target_pairs={{0,4},{2,6},{4,0},{6,2},{8,12},{10,14},{12,8},{14,10},{1,5},{3,7},... | collective-permute-start | bytes 184328 | tf_op jit(solution)/shard_map/ppermute | solution.py:219
  23.1 11.9 %collective-permute-start.4 = (bf16[2,8,1920]{2,1,0:T(8,128)(2,1)S(1)}, bf16[2,8,1920]{2,1,0:T(8,128)(2,1)S(1)}, u32[]{:S(2)}, u32[]{:S(2)}) collective-permute-start(bf16[2,8,1920]{2,1,0:T(8,128)(2,1)S(1)} %constant_dynamic-update-slice_fusion), channel_id=1, source_target_pairs={{0,2},{2,0},{4,6},{6,4},{8,10},{10,8},{12,14},{14,12},{1,3},{3,1},... | collective-permute-start | bytes 184328 | tf_op jit(solution)/shard_map/ppermute | solution.py:219
  35.1 4.5 %collective-permute-start.8 = (bf16[64,2048]{1,0:T(8,128)(2,1)S(1)}, bf16[64,2048]{1,0:T(8,128)(2,1)S(1)}, u32[]{:S(2)}, u32[]{:S(2)}) collective-permute-start(bf16[64,2048]{1,0:T(8,128)(2,1)S(1)} %constant_dynamic-slice_fusion), channel_id=1, source_target_pairs={{0,1},{1,0},{2,3},{3,2},{4,5},{5,4},{6,7},{7,6},{8,9},{9,8},{10,11... | collective-permute-start | bytes 786440 | tf_op jit(solution)/shard_map/ppermute | solution.py:215
  35.2 4.4 %collective-permute-start.7 = (bf16[8,8,1920]{2,1,0:T(8,128)(2,1)S(1)}, bf16[8,8,1920]{2,1,0:T(8,128)(2,1)S(1)}, u32[]{:S(2)}, u32[]{:S(2)}) collective-permute-start(bf16[8,8,1920]{2,1,0:T(8,128)(2,1)S(1)} %constant_dynamic-update-slice_fusion.2.own_ref), channel_id=1, source_target_pairs={{0,1},{1,0},{2,3},{3,2},{4,5},{5,4},{6,7},{7,6},{8,9},{9,8},{10,11... | collective-permute-start | bytes 737288 | tf_op jit(solution)/shard_map/ppermute | solution.py:215
  35.8 10.6 %all-to-all-start.1 = ((f32[16,8,128]{2,1,0:T(8,128)}), f32[16,8,128]{2,1,0:T(8,128)S(1)}, u32[]{:S(2)}, u32[]{:S(2)}) async-start(f32[16,8,128]{2,1,0:T(8,128)} %get-tuple-element.26), calls=%async_computation.1 | async-start | bytes 131072 | tf_op jit(solution)/shard_map/all_to_all | solution.py:324

commit v13 on v12

--- a/solution.py
+++ b/solution.py
@@ -42,7 +42,7 @@
     return jnp.concatenate(both, axis=1)
 
 
-def map_own_kernel(w_ref, t_ref, first_ref, o_ref, s_ref):
+def map_own_kernel(w_ref, t_ref, o_ref, s_ref):
     tokens = t_ref.shape[0]
     spread_tokens(t_ref, s_ref, 0, t_ref.shape[1] // BLK)
     for t in range(0, tokens, 2):
@@ -268,13 +268,13 @@
     part = pl.pallas_call(
         map_own_kernel,
         out_shape=shape((rows + MASS_ROWS, tokens * BLK), f32),
-        in_specs=[in_vmem(), in_vmem(), anywhere()],
+        in_specs=[in_vmem()] * 2,
         out_specs=in_vmem(),
         scratch_shapes=[spread],
         compiler_params=params(),
         cost_estimate=cost(flops, 3 << 20),
         name="map_own",
-    )(w_own, teacher_probs, first_piece)
+    )(w_own, teacher_probs)
     chunk = (owners, tokens, width + group_tokens)
     outgoing = pl.pallas_call(
         map_rest_kernel,
@@ -291,6 +291,7 @@
         cost_estimate=cost(flops, 4 << 20),
         name="map_rest",
     )(w_rest, teacher_other, part, stats)
+    outgoing, first_piece = lax.optimization_barrier((outgoing, first_piece))
     target = lax.all_to_all(outgoing, "sv", 0, 0, tiled=True)
 
     hidden, late_logits, outgoing = lax.optimization_barrier((hidden, student_logits, outgoing))

time: 47.3 us -> 46.1 us (0.975)
  starting transfers between devices: 19 us -> 16.5 us
  Pallas kernels: 9.68 us -> 11 us
    all_to_all x1, starting transfers between devices: 6.39 us -> 3.82 us  [body(): target = lax.all_to_all(outgoing, 'sv', 0, 0, tiled=True)]
    pallas_call x1, Pallas kernels: 2.57 us -> 3.94 us  [body(): pl.pallas_call(map_rest_kernel, out_shape=shape(chunk, bf16), in_specs=[i...]
    ppermute x4, waiting for transfers between devices: 0.88 us -> 0.01 us  [to_partner(): lax.ppermute(x, 'sv', [(s, s ^ offset) for s in range(lax.axis_size('sv'))])]
    all_to_all x1, waiting for transfers between devices: 10.4 us -> 11.2 us  [body(): target = lax.all_to_all(outgoing, 'sv', 0, 0, tiled=True)]
  transfers between devices with their start and end apart: 11 -> 11, of which waited for: 3 -> 2; matrix products, arithmetic and copies ran while one was open for 3% -> 3% of each run, Pallas kernels for 15% -> 24%
where the time goes in v13:
time: 46.1 us; the launch traced here: 45.7 us
  starting transfers between devices  16.5 us (36%)
  waiting for transfers between devices  13.6 us (30%)
  Pallas kernels  11 us (24%)
  other arithmetic  3.54 us (8%)
  between operations  0.85 us (2%)
    all_to_all x1, waiting for transfers between devices, body(): target = lax.all_to_all(outgoing, 'sv', 0, 0, tiled=True)  11.2 us
    ppermute x4, starting transfers between devices, to_partner(): lax.ppermute(x, 'sv', [(s, s ^ offset) for s in range(lax.axis_size('sv'))])  7.62 us
    pallas_call x1, Pallas kernels, body(): pl.pallas_call(weight_kernel, out_shape=(shape((features, width), bf16),...  4.48 us
    pallas_call x1, Pallas kernels, body(): pl.pallas_call(map_rest_kernel, out_shape=shape(chunk, bf16), in_specs=[i...  3.94 us
    all_to_all x1, starting transfers between devices, body(): target = lax.all_to_all(outgoing, 'sv', 0, 0, tiled=True)  3.82 us
    all_to_all x1, starting transfers between devices, body(): terms = lax.all_to_all(terms, ('sv', 'tv'), 0, 0, tiled=True)  3.74 us
    all_to_all x1, waiting for transfers between devices, body(): terms = lax.all_to_all(terms, ('sv', 'tv'), 0, 0, tiled=True)  2.32 us
    another operation x1, other arithmetic, body(): lax.reduce((wide, jnp.ones_like(wide)), (low, jnp.float32(0)), merge, (1,))  1.68 us
  transfers between devices with their start and end apart: 11, of which 2 were waited for; matrix products, arithmetic and copies ran while one was open for 3% of the time, Pallas kernels for 24%

profile of v13, /device:TPU:0, one launch (start us, length us, event | category | flops | bytes accessed | tf_op | source)
XLA Modules:
  0.0 45.7 jit_solution(17398609859242776989)
XLA Ops:
  0.6 1.7 %convert_reduce_fusion = (f32[64]{0:T(128)S(1)}, f32[64]{0:T(128)S(1)}) fusion(bf16[64,4096]{1,0:T(8,128)(2,1)} %param.10), kind=kLoop, calls=%fused_computation | loop fusion | flops 1834624 | bytes 524800 | tf_op jit(solution)/shard_map/reduce | solution.py:255
  2.3 0.5 %collective-permute-start = (bf16[16,40960]{1,0:T(8,128)(2,1)}, bf16[16,40960]{1,0:T(8,128)(2,1)}, u32[]{:S(2)}, u32[]{:S(2)}) collective-permute-start(bf16[16,40960]{1,0:T(8,128)(2,1)} %t_ref.1), channel_id=1, source_target_pairs={{0,1},{1,0},{2,3},{3,2},{4,5},{5,4},{6,7},{7,6},{8,9},{9,8},{10,11... | collective-permute-start | bytes 3932168 | tf_op jit(solution)/shard_map/ppermute | solution.py:215
  2.8 0.1 collective-permute-start.1
  2.9 4.0 %collective-permute-start.2 = (bf16[1,8,1920]{2,1,0:T(8,128)(2,1)}, bf16[1,8,1920]{2,1,0:T(8,128)(2,1)S(1)}, u32[]{:S(2)}, u32[]{:S(2)}) collective-permute-start(bf16[1,8,1920]{2,1,0:T(8,128)(2,1)} %bitcast.9), channel_id=1, source_target_pairs={{0,8},{2,10},{4,12},{6,14},{8,0},{10,2},{12,4},{14,6},{1,9},{3,11}... | collective-permute-start | bytes 92168 | tf_op jit(solution)/shard_map/ppermute | solution.py:219
  6.9 0.7 %fusion.5 = f32[640,2]{0,1:T(2,128)S(1)} fusion(bf16[640,2]{0,1:T(2,128)(2,1)} %param.9, s32[640,2]{0,1:T(2,128)} %param.7, s32[640,2]{0,1:T(2,128)} %param.8, s32[]{:T(128)S(6)} %mul.51), kind=kLoop, calls=%fused_computation.23 | loop fusion | flops 14080 | bytes 17924 | tf_op jit(solution)/shard_map/add | solution.py:262
  7.7 0.1 dynamic-slice_bitcast_fusion
  7.8 0.2 add_convert_fusion
  8.1 1.4 %map_own.1.p_ref = f32[144,2048]{1,0:T(8,128)S(1)} custom-call(bf16[144,320]{1,0:T(8,128)(2,1)S(1)} %get-tuple-element.57.w_ref, bf16[16,40960]{1,0:T(8,128)(2,1)S(1)} %copy-done), custom_call_target="tpu_custom_call" | custom-call | flops 188743680 | bytes 3145728 | tf_op jit(solution)/shard_map/map_own/pallas_call | solution.py:268
  9.5 0.1 pad_maximum_fusion.2.stats_ref
  9.6 3.9 %map_rest.1 = bf16[8,16,2176]{2,1,0:T(8,128)(2,1)} custom-call(bf16[144,320]{1,0:T(8,128)(2,1)S(1)} %get-tuple-element.58.w_ref, bf16[16,40960]{1,0:T(8,128)(2,1)} %collective-permute-done.t_ref, f32[144,2048]{1,0:T(8,128)S(1)} %map_own.1.p_ref, f32[2,128]{1,0:T(2,128)S(1)} %pad_maximum_fusion.2.stats_ref), custom_call_target="tpu_custom_call" | custom-call | flops 188743680 | bytes 4194304 | tf_op jit(solution)/shard_map/map_rest/pallas_call | solution.py:279
  13.5 3.8 %all-to-all-start = ((bf16[8,16,2176]{2,1,0:T(8,128)(2,1)}), bf16[8,16,2176]{2,1,0:T(8,128)(2,1)S(1)}, u32[]{:S(2)}, u32[]{:S(2)}) async-start(bf16[8,16,2176]{2,1,0:T(8,128)(2,1)} %map_rest.1), calls=%async_computation | async-start | bytes 1114112 | tf_op jit(solution)/shard_map/all_to_all | solution.py:295
  17.4 0.1 collective-permute-start.3
  17.5 3.0 %collective-permute-start.6 = (bf16[2,8,1920]{2,1,0:T(8,128)(2,1)S(1)}, bf16[2,8,1920]{2,1,0:T(8,128)(2,1)S(1)}, u32[]{:S(2)}, u32[]{:S(2)}) collective-permute-start(bf16[2,8,1920]{2,1,0:T(8,128)(2,1)S(1)} %constant_dynamic-update-slice_fusion), channel_id=1, source_target_pairs={{0,6},{2,4},{4,2},{6,0},{8,14},{10,12},{12,10},{14,8},{1,7},{3,5},... | collective-permute-start | bytes 184328 | tf_op jit(solution)/shard_map/ppermute | solution.py:219
  20.5 0.6 %collective-permute-start.5 = (bf16[2,8,1920]{2,1,0:T(8,128)(2,1)S(1)}, bf16[2,8,1920]{2,1,0:T(8,128)(2,1)S(1)}, u32[]{:S(2)}, u32[]{:S(2)}) collective-permute-start(bf16[2,8,1920]{2,1,0:T(8,128)(2,1)S(1)} %constant_dynamic-update-slice_fusion), channel_id=1, source_target_pairs={{0,4},{2,6},{4,0},{6,2},{8,12},{10,14},{12,8},{14,10},{1,5},{3,7},... | collective-permute-start | bytes 184328 | tf_op jit(solution)/shard_map/ppermute | solution.py:219
  21.1 0.1 collective-permute-start.4
  21.1 0.1 broadcast_select_fusion.1
  21.3 11.2 %all-to-all-done.refs_0_ = bf16[8,16,2176]{2,1,0:T(8,128)(2,1)S(1)} async-done(((bf16[8,16,2176]{2,1,0:T(8,128)(2,1)}), bf16[8,16,2176]{2,1,0:T(8,128)(2,1)S(1)}, u32[]{:S(2)}, u32[]{:S(2)}) %all-to-all-start) | async-done | bytes 557088 | tf_op jit(solution)/shard_map/all_to_all | solution.py:295
  32.5 1.2 %logit_grad.1 = (bf16[128,2048]{1,0:T(8,128)(2,1)S(1)}, f32[16,8,128]{2,1,0:T(8,128)}) custom-call(bf16[8,16,2176]{2,1,0:T(8,128)(2,1)S(1)} %all-to-all-done.refs_0_, bf16[128,2048]{1,0:T(8,128)(2,1)S(1)} %pad_maximum_fusion.refs_1_), custom_call_target="tpu_custom_call" | custom-call | flops 2621440 | bytes 1572864 | tf_op jit(solution)/shard_map/logit_grad/pallas_call | solution.py:308
  34.0 0.5 %collective-permute-start.7 = (bf16[8,8,1920]{2,1,0:T(8,128)(2,1)S(1)}, bf16[8,8,1920]{2,1,0:T(8,128)(2,1)S(1)}, u32[]{:S(2)}, u32[]{:S(2)}) collective-permute-start(bf16[8,8,1920]{2,1,0:T(8,128)(2,1)S(1)} %constant_dynamic-update-slice_fusion.2.own_ref), channel_id=1, source_target_pairs={{0,1},{1,0},{2,3},{3,2},{4,5},{5,4},{6,7},{7,6},{8,9},{9,8},{10,11... | collective-permute-start | bytes 737288 | tf_op jit(solution)/shard_map/ppermute | solution.py:215
  34.5 3.7 %all-to-all-start.1 = ((f32[16,8,128]{2,1,0:T(8,128)}), f32[16,8,128]{2,1,0:T(8,128)S(1)}, u32[]{:S(2)}, u32[]{:S(2)}) async-start(f32[16,8,128]{2,1,0:T(8,128)} %get-tuple-element.29), calls=%async_computation.1 | async-start | bytes 131072 | tf_op jit(solution)/shard_map/all_to_all | solution.py:325
  38.3 0.1 pad_add_fusion.place_ref
  38.3 4.5 %weight_grad.1 = (bf16[1920,2048]{1,0:T(8,128)(2,1)}, bf16[64,4096]{1,0:T(8,128)(2,1)}) custom-call(s32[2]{0:T(128)S(1)} %pad_add_fusion.place_ref, bf16[8,8,1920]{2,1,0:T(8,128)(2,1)S(1)} %constant_dynamic-update-slice_fusion.2.own_ref, bf16[8,8,1920]{2,1,0:T(8,128)(2,1)S(1)} %collective-permute-done.7.other_ref, ...), custom_call_target="tpu_custom_call" | custom-call | flops 1006632960 | bytes 8880128 | tf_op jit(solution)/shard_map/weight_grad/pallas_call | solution.py:332
  42.8 2.3 %all-to-all-done.1 = f32[16,8,128]{2,1,0:T(8,128)S(1)} async-done(((f32[16,8,128]{2,1,0:T(8,128)}), f32[16,8,128]{2,1,0:T(8,128)S(1)}, u32[]{:S(2)}, u32[]{:S(2)}) %all-to-all-start.1) | async-done | bytes 65568 | tf_op jit(solution)/shard_map/all_to_all | solution.py:325
  45.1 0.5 %slice_reduce_fusion = f32[64]{0:T(128)} fusion(f32[16,8,128]{2,1,0:T(8,128)S(1)} %all-to-all-done.1), kind=kLoop, calls=%fused_computation.21 | loop fusion | flops 960 | bytes 4352 | tf_op jit(solution)/shard_map/reduce_sum | solution.py:352
  (30 shorter events, 0.4 us)
Async XLA Ops:
  0.6 7.4 %copy-start = (bf16[16,40960]{1,0:T(8,128)(2,1)S(1)}, bf16[16,40960]{1,0:T(8,128)(2,1)}, u32[]{:S(2)}) copy-start(bf16[16,40960]{1,0:T(8,128)(2,1)} %t_ref.1) | copy-start | bytes 3932164
  2.3 7.2 %collective-permute-start = (bf16[16,40960]{1,0:T(8,128)(2,1)}, bf16[16,40960]{1,0:T(8,128)(2,1)}, u32[]{:S(2)}, u32[]{:S(2)}) collective-permute-start(bf16[16,40960]{1,0:T(8,128)(2,1)} %t_ref.1), channel_id=1, source_target_pairs={{0,1},{1,0},{2,3},{3,2},{4,5},{5,4},{6,7},{7,6},{8,9},{9,8},{10,11... | collective-permute-start | bytes 3932168 | tf_op jit(solution)/shard_map/ppermute | solution.py:215
  2.8 6.6 %collective-permute-start.1 = (f32[2,64]{1,0:T(2,128)S(1)}, f32[2,64]{1,0:T(2,128)S(1)}, u32[]{:S(2)}, u32[]{:S(2)}) collective-permute-start(f32[2,64]{1,0:T(2,128)S(1)} %pad_maximum_fusion.1), channel_id=1, source_target_pairs={{0,1},{1,0},{2,3},{3,2},{4,5},{5,4},{6,7},{7,6},{8,9},{9,8},{10,11... | collective-permute-start | bytes 1544 | tf_op jit(solution)/shard_map/ppermute | solution.py:215
  2.9 10.6 %collective-permute-start.2 = (bf16[1,8,1920]{2,1,0:T(8,128)(2,1)}, bf16[1,8,1920]{2,1,0:T(8,128)(2,1)S(1)}, u32[]{:S(2)}, u32[]{:S(2)}) collective-permute-start(bf16[1,8,1920]{2,1,0:T(8,128)(2,1)} %bitcast.9), channel_id=1, source_target_pairs={{0,8},{2,10},{4,12},{6,14},{8,0},{10,2},{12,4},{14,6},{1,9},{3,11}... | collective-permute-start | bytes 92168 | tf_op jit(solution)/shard_map/ppermute | solution.py:219
  9.6 7.8 %copy-start.1 = (bf16[64,4096]{1,0:T(8,128)(2,1)S(1)}, bf16[64,4096]{1,0:T(8,128)(2,1)}, u32[]{:S(2)}) copy-start(bf16[64,4096]{1,0:T(8,128)(2,1)} %param.10) | copy-start | bytes 1572868
  13.5 4.0 %copy-start.2 = (bf16[8,1920]{1,0:T(8,128)(2,1)S(1)}, bf16[8,1920]{1,0:T(8,128)(2,1)}, u32[]{:S(2)}) copy-start(bf16[8,1920]{1,0:T(8,128)(2,1)} %param.11) | copy-start | bytes 92164
  13.5 19.0 %all-to-all-start = ((bf16[8,16,2176]{2,1,0:T(8,128)(2,1)}), bf16[8,16,2176]{2,1,0:T(8,128)(2,1)S(1)}, u32[]{:S(2)}, u32[]{:S(2)}) async-start(bf16[8,16,2176]{2,1,0:T(8,128)(2,1)} %map_rest.1), calls=%async_computation | async-start | bytes 1114112 | tf_op jit(solution)/shard_map/all_to_all | solution.py:295
  17.4 3.7 %collective-permute-start.3 = (bf16[64,2048]{1,0:T(8,128)(2,1)S(1)}, bf16[64,2048]{1,0:T(8,128)(2,1)S(1)}, u32[]{:S(2)}, u32[]{:S(2)}) collective-permute-start(bf16[64,2048]{1,0:T(8,128)(2,1)S(1)} %constant_dynamic-slice_fusion.1), channel_id=1, source_target_pairs={{0,1},{1,0},{2,3},{3,2},{4,5},{5,4},{6,7},{7,6},{8,9},{9,8},{10,11... | collective-permute-start | bytes 786440 | tf_op jit(solution)/shard_map/ppermute | solution.py:215
  17.5 16.2 %collective-permute-start.6 = (bf16[2,8,1920]{2,1,0:T(8,128)(2,1)S(1)}, bf16[2,8,1920]{2,1,0:T(8,128)(2,1)S(1)}, u32[]{:S(2)}, u32[]{:S(2)}) collective-permute-start(bf16[2,8,1920]{2,1,0:T(8,128)(2,1)S(1)} %constant_dynamic-update-slice_fusion), channel_id=1, source_target_pairs={{0,6},{2,4},{4,2},{6,0},{8,14},{10,12},{12,10},{14,8},{1,7},{3,5},... | collective-permute-start | bytes 184328 | tf_op jit(solution)/shard_map/ppermute | solution.py:219
  20.5 13.3 %collective-permute-start.5 = (bf16[2,8,1920]{2,1,0:T(8,128)(2,1)S(1)}, bf16[2,8,1920]{2,1,0:T(8,128)(2,1)S(1)}, u32[]{:S(2)}, u32[]{:S(2)}) collective-permute-start(bf16[2,8,1920]{2,1,0:T(8,128)(2,1)S(1)} %constant_dynamic-update-slice_fusion), channel_id=1, source_target_pairs={{0,4},{2,6},{4,0},{6,2},{8,12},{10,14},{12,8},{14,10},{1,5},{3,7},... | collective-permute-start | bytes 184328 | tf_op jit(solution)/shard_map/ppermute | solution.py:219
  21.1 12.7 %collective-permute-start.4 = (bf16[2,8,1920]{2,1,0:T(8,128)(2,1)S(1)}, bf16[2,8,1920]{2,1,0:T(8,128)(2,1)S(1)}, u32[]{:S(2)}, u32[]{:S(2)}) collective-permute-start(bf16[2,8,1920]{2,1,0:T(8,128)(2,1)S(1)} %constant_dynamic-update-slice_fusion), channel_id=1, source_target_pairs={{0,2},{2,0},{4,6},{6,4},{8,10},{10,8},{12,14},{14,12},{1,3},{3,1},... | collective-permute-start | bytes 184328 | tf_op jit(solution)/shard_map/ppermute | solution.py:219
  33.8 4.5 %collective-permute-start.8 = (bf16[64,2048]{1,0:T(8,128)(2,1)S(1)}, bf16[64,2048]{1,0:T(8,128)(2,1)S(1)}, u32[]{:S(2)}, u32[]{:S(2)}) collective-permute-start(bf16[64,2048]{1,0:T(8,128)(2,1)S(1)} %constant_dynamic-slice_fusion), channel_id=1, source_target_pairs={{0,1},{1,0},{2,3},{3,2},{4,5},{5,4},{6,7},{7,6},{8,9},{9,8},{10,11... | collective-permute-start | bytes 786440 | tf_op jit(solution)/shard_map/ppermute | solution.py:215
  34.0 4.4 %collective-permute-start.7 = (bf16[8,8,1920]{2,1,0:T(8,128)(2,1)S(1)}, bf16[8,8,1920]{2,1,0:T(8,128)(2,1)S(1)}, u32[]{:S(2)}, u32[]{:S(2)}) collective-permute-start(bf16[8,8,1920]{2,1,0:T(8,128)(2,1)S(1)} %constant_dynamic-update-slice_fusion.2.own_ref), channel_id=1, source_target_pairs={{0,1},{1,0},{2,3},{3,2},{4,5},{5,4},{6,7},{7,6},{8,9},{9,8},{10,11... | collective-permute-start | bytes 737288 | tf_op jit(solution)/shard_map/ppermute | solution.py:215
  34.5 10.6 %all-to-all-start.1 = ((f32[16,8,128]{2,1,0:T(8,128)}), f32[16,8,128]{2,1,0:T(8,128)S(1)}, u32[]{:S(2)}, u32[]{:S(2)}) async-start(f32[16,8,128]{2,1,0:T(8,128)} %get-tuple-element.29), calls=%async_computation.1 | async-start | bytes 131072 | tf_op jit(solution)/shard_map/all_to_all | solution.py:325

commit v14 on v13

--- a/solution.py
+++ b/solution.py
@@ -59,7 +59,7 @@
     return parts
 
 
-def map_rest_kernel(w_ref, t_ref, p_ref, stats_ref, o_ref, s_ref, m_ref, o_buf, out_sem):
+def map_rest_kernel(w_ref, t_ref, p_ref, stats_ref, first_ref, o_ref, s_ref, m_ref, o_buf, out_sem):
     tokens = t_ref.shape[0]
     owners = o_ref.shape[0]
     rows = w_ref.shape[0] - MASS_ROWS
@@ -203,7 +203,7 @@
     return pl.BlockSpec(memory_space=pl.ANY)
 
 
-def params(mib=48):
+def params(mib=24):
     return pltpu.CompilerParams(vmem_limit_bytes=mib << 20)
 
 
@@ -279,7 +279,7 @@
     outgoing = pl.pallas_call(
         map_rest_kernel,
         out_shape=shape(chunk, bf16),
-        in_specs=[in_vmem()] * 4,
+        in_specs=[in_vmem()] * 4 + [anywhere()],
         out_specs=anywhere(),
         scratch_shapes=[
             spread,
@@ -290,8 +290,7 @@
         compiler_params=params(),
         cost_estimate=cost(flops, 4 << 20),
         name="map_rest",
-    )(w_rest, teacher_other, part, stats)
-    outgoing, first_piece = lax.optimization_barrier((outgoing, first_piece))
+    )(w_rest, teacher_other, part, stats, first_piece)
     target = lax.all_to_all(outgoing, "sv", 0, 0, tiled=True)
 
     hidden, late_logits, outgoing = lax.optimization_barrier((hidden, student_logits, outgoing))
@@ -341,7 +340,7 @@
             dma(steps),
             dma(2),
         ],
-        compiler_params=params(),
+        compiler_params=params(32),
         cost_estimate=cost(
             2 * features * group_tokens * width,
             2 * (features * width + group_tokens * (features + width)),

time: 46.1 us -> 46 us (level)
  Pallas kernels: 11 us -> 9.65 us
  local copies, waits for them, and re-layouts: 0.22 us -> 1.52 us
  starting transfers between devices: 16.5 us -> 17.2 us
  waiting for transfers between devices: 13.6 us -> 12.9 us
    pallas_call x1, Pallas kernels: 3.94 us -> 2.57 us  [body(): pl.pallas_call(map_rest_kernel, out_shape=shape(chunk, bf16), in_specs=[i...]
    unnamed x10, local copies, waits for them, and re-layouts: 0.05 us -> 1.36 us
    all_to_all x1, starting transfers between devices: 3.82 us -> 4.54 us  [body(): target = lax.all_to_all(outgoing, 'sv', 0, 0, tiled=True)]
    all_to_all x1, waiting for transfers between devices: 11.2 us -> 10.5 us  [body(): target = lax.all_to_all(outgoing, 'sv', 0, 0, tiled=True)]
  transfers between devices with their start and end apart: 11 -> 11, of which waited for: 2 -> 2; matrix products, arithmetic and copies ran while one was open for 3% -> 3% of each run, Pallas kernels for 24% -> 16%
where the time goes in v14:
time: 46 us; the launch traced here: 45.5 us
  starting transfers between devices  17.2 us (37%)
  waiting for transfers between devices  12.9 us (28%)
  Pallas kernels  9.65 us (21%)
  other arithmetic  3.44 us (7%)
  local copies, waits for them, and re-layouts  1.52 us (3%)
  between operations  0.84 us (2%)
    all_to_all x1, waiting for transfers between devices, body(): target = lax.all_to_all(outgoing, 'sv', 0, 0, tiled=True)  10.5 us
    ppermute x4, starting transfers between devices, to_partner(): lax.ppermute(x, 'sv', [(s, s ^ offset) for s in range(lax.axis_size('sv'))])  7.63 us
    all_to_all x1, starting transfers between devices, body(): target = lax.all_to_all(outgoing, 'sv', 0, 0, tiled=True)  4.54 us
    pallas_call x1, Pallas kernels, body(): pl.pallas_call(weight_kernel, out_shape=(shape((features, width), bf16),...  4.48 us
    all_to_all x1, starting transfers between devices, body(): terms = lax.all_to_all(terms, ('sv', 'tv'), 0, 0, tiled=True)  3.74 us
    pallas_call x1, Pallas kernels, body(): pl.pallas_call(map_rest_kernel, out_shape=shape(chunk, bf16), in_specs=[i...  2.57 us
    all_to_all x1, waiting for transfers between devices, body(): terms = lax.all_to_all(terms, ('sv', 'tv'), 0, 0, tiled=True)  2.32 us
    another operation x1, other arithmetic, body(): lax.reduce((wide, jnp.ones_like(wide)), (low, jnp.float32(0)), merge, (1,))  1.57 us
  transfers between devices with their start and end apart: 11, of which 2 were waited for; matrix products, arithmetic and copies ran while one was open for 3% of the time, Pallas kernels for 16%

profile of v14, /device:TPU:0, one launch (start us, length us, event | category | flops | bytes accessed | tf_op | source)
XLA Modules:
  0.0 45.5 jit_solution(4763455284293122679)
XLA Ops:
  0.6 1.6 %convert_reduce_fusion = (f32[64]{0:T(128)S(1)}, f32[64]{0:T(128)S(1)}) fusion(bf16[64,4096]{1,0:T(8,128)(2,1)} %param.10), kind=kLoop, calls=%fused_computation | loop fusion | flops 1834624 | bytes 524800 | tf_op jit(solution)/shard_map/reduce | solution.py:255
  2.2 0.5 %collective-permute-start = (bf16[16,40960]{1,0:T(8,128)(2,1)}, bf16[16,40960]{1,0:T(8,128)(2,1)S(1)}, u32[]{:S(2)}, u32[]{:S(2)}) collective-permute-start(bf16[16,40960]{1,0:T(8,128)(2,1)} %t_ref.1), channel_id=1, source_target_pairs={{0,1},{1,0},{2,3},{3,2},{4,5},{5,4},{6,7},{7,6},{8,9},{9,8},{10,11... | collective-permute-start | bytes 3932168 | tf_op jit(solution)/shard_map/ppermute | solution.py:215
  2.7 0.1 collective-permute-start.1
  2.8 4.0 %collective-permute-start.2 = (bf16[1,8,1920]{2,1,0:T(8,128)(2,1)}, bf16[1,8,1920]{2,1,0:T(8,128)(2,1)S(1)}, u32[]{:S(2)}, u32[]{:S(2)}) collective-permute-start(bf16[1,8,1920]{2,1,0:T(8,128)(2,1)} %bitcast.9), channel_id=1, source_target_pairs={{0,8},{2,10},{4,12},{6,14},{8,0},{10,2},{12,4},{14,6},{1,9},{3,11}... | collective-permute-start | bytes 92168 | tf_op jit(solution)/shard_map/ppermute | solution.py:219
  6.8 0.7 %fusion.5 = f32[640,2]{0,1:T(2,128)S(1)} fusion(bf16[640,2]{0,1:T(2,128)(2,1)} %param.9, s32[640,2]{0,1:T(2,128)} %param.7, s32[640,2]{0,1:T(2,128)} %param.8, s32[]{:T(128)S(6)} %mul.51), kind=kLoop, calls=%fused_computation.23 | loop fusion | flops 14080 | bytes 17924 | tf_op jit(solution)/shard_map/add | solution.py:262
  7.6 0.1 dynamic-slice_bitcast_fusion
  7.7 0.2 add_convert_fusion
  7.9 1.3 %copy-done = bf16[16,40960]{1,0:T(8,128)(2,1)S(1)} copy-done((bf16[16,40960]{1,0:T(8,128)(2,1)S(1)}, bf16[16,40960]{1,0:T(8,128)(2,1)}, u32[]{:S(2)}) %copy-start) | copy-done | bytes 1310744
  9.3 1.4 %map_own.1.p_ref = f32[144,2048]{1,0:T(8,128)S(1)} custom-call(bf16[144,320]{1,0:T(8,128)(2,1)S(1)} %get-tuple-element.53.w_ref, bf16[16,40960]{1,0:T(8,128)(2,1)S(1)} %copy-done), custom_call_target="tpu_custom_call" | custom-call | flops 188743680 | bytes 3145728 | tf_op jit(solution)/shard_map/map_own/pallas_call | solution.py:268
  10.7 0.1 pad_maximum_fusion.2.stats_ref
  10.8 2.6 %map_rest.1 = bf16[8,16,2176]{2,1,0:T(8,128)(2,1)} custom-call(bf16[144,320]{1,0:T(8,128)(2,1)S(1)} %get-tuple-element.54.w_ref, bf16[16,40960]{1,0:T(8,128)(2,1)S(1)} %collective-permute-done.t_ref, f32[144,2048]{1,0:T(8,128)S(1)} %map_own.1.p_ref, f32[2,128]{1,0:T(2,128)S(1)} %pad_maximum_fusion.2.stats_ref, ...), custom_call_target="tpu_custom_call" | custom-call | flops 188743680 | bytes 4194304 | tf_op jit(solution)/shard_map/map_rest/pallas_call | solution.py:279
  13.4 4.5 %all-to-all-start = ((bf16[8,16,2176]{2,1,0:T(8,128)(2,1)}), bf16[8,16,2176]{2,1,0:T(8,128)(2,1)S(1)}, u32[]{:S(2)}, u32[]{:S(2)}) async-start(bf16[8,16,2176]{2,1,0:T(8,128)(2,1)} %map_rest.1), calls=%async_computation | async-start | bytes 1114112 | tf_op jit(solution)/shard_map/all_to_all | solution.py:294
  18.0 3.0 %collective-permute-start.6 = (bf16[2,8,1920]{2,1,0:T(8,128)(2,1)S(1)}, bf16[2,8,1920]{2,1,0:T(8,128)(2,1)S(1)}, u32[]{:S(2)}, u32[]{:S(2)}) collective-permute-start(bf16[2,8,1920]{2,1,0:T(8,128)(2,1)S(1)} %constant_dynamic-update-slice_fusion), channel_id=1, source_target_pairs={{0,6},{2,4},{4,2},{6,0},{8,14},{10,12},{12,10},{14,8},{1,7},{3,5},... | collective-permute-start | bytes 184328 | tf_op jit(solution)/shard_map/ppermute | solution.py:219
  21.0 0.6 %collective-permute-start.5 = (bf16[2,8,1920]{2,1,0:T(8,128)(2,1)S(1)}, bf16[2,8,1920]{2,1,0:T(8,128)(2,1)S(1)}, u32[]{:S(2)}, u32[]{:S(2)}) collective-permute-start(bf16[2,8,1920]{2,1,0:T(8,128)(2,1)S(1)} %constant_dynamic-update-slice_fusion), channel_id=1, source_target_pairs={{0,4},{2,6},{4,0},{6,2},{8,12},{10,14},{12,8},{14,10},{1,5},{3,7},... | collective-permute-start | bytes 184328 | tf_op jit(solution)/shard_map/ppermute | solution.py:219
  21.6 0.1 collective-permute-start.4
  21.7 0.1 broadcast_select_fusion.1
  21.8 10.5 %all-to-all-done.refs_0_ = bf16[8,16,2176]{2,1,0:T(8,128)(2,1)S(1)} async-done(((bf16[8,16,2176]{2,1,0:T(8,128)(2,1)}), bf16[8,16,2176]{2,1,0:T(8,128)(2,1)S(1)}, u32[]{:S(2)}, u32[]{:S(2)}) %all-to-all-start) | async-done | bytes 557088 | tf_op jit(solution)/shard_map/all_to_all | solution.py:294
  32.4 1.2 %logit_grad.1 = (bf16[128,2048]{1,0:T(8,128)(2,1)S(1)}, f32[16,8,128]{2,1,0:T(8,128)}) custom-call(bf16[8,16,2176]{2,1,0:T(8,128)(2,1)S(1)} %all-to-all-done.refs_0_, bf16[128,2048]{1,0:T(8,128)(2,1)S(1)} %pad_maximum_fusion.refs_1_), custom_call_target="tpu_custom_call" | custom-call | flops 2621440 | bytes 1572864 | tf_op jit(solution)/shard_map/logit_grad/pallas_call | solution.py:307
  33.8 0.5 %collective-permute-start.7 = (bf16[8,8,1920]{2,1,0:T(8,128)(2,1)S(1)}, bf16[8,8,1920]{2,1,0:T(8,128)(2,1)S(1)}, u32[]{:S(2)}, u32[]{:S(2)}) collective-permute-start(bf16[8,8,1920]{2,1,0:T(8,128)(2,1)S(1)} %constant_dynamic-update-slice_fusion.2.own_ref), channel_id=1, source_target_pairs={{0,1},{1,0},{2,3},{3,2},{4,5},{5,4},{6,7},{7,6},{8,9},{9,8},{10,11... | collective-permute-start | bytes 737288 | tf_op jit(solution)/shard_map/ppermute | solution.py:215
  34.3 3.7 %all-to-all-start.1 = ((f32[16,8,128]{2,1,0:T(8,128)}), f32[16,8,128]{2,1,0:T(8,128)S(1)}, u32[]{:S(2)}, u32[]{:S(2)}) async-start(f32[16,8,128]{2,1,0:T(8,128)} %get-tuple-element.26), calls=%async_computation.1 | async-start | bytes 131072 | tf_op jit(solution)/shard_map/all_to_all | solution.py:324
  38.1 0.1 pad_add_fusion.place_ref
  38.2 4.5 %weight_grad.1 = (bf16[1920,2048]{1,0:T(8,128)(2,1)}, bf16[64,4096]{1,0:T(8,128)(2,1)}) custom-call(s32[2]{0:T(128)S(1)} %pad_add_fusion.place_ref, bf16[8,8,1920]{2,1,0:T(8,128)(2,1)S(1)} %constant_dynamic-update-slice_fusion.2.own_ref, bf16[8,8,1920]{2,1,0:T(8,128)(2,1)S(1)} %collective-permute-done.7.other_ref, ...), custom_call_target="tpu_custom_call" | custom-call | flops 1006632960 | bytes 8880128 | tf_op jit(solution)/shard_map/weight_grad/pallas_call | solution.py:331
  42.7 2.3 %all-to-all-done.1 = f32[16,8,128]{2,1,0:T(8,128)S(1)} async-done(((f32[16,8,128]{2,1,0:T(8,128)}), f32[16,8,128]{2,1,0:T(8,128)S(1)}, u32[]{:S(2)}, u32[]{:S(2)}) %all-to-all-start.1) | async-done | bytes 65568 | tf_op jit(solution)/shard_map/all_to_all | solution.py:324
  45.0 0.5 %slice_reduce_fusion = f32[64]{0:T(128)} fusion(f32[16,8,128]{2,1,0:T(8,128)S(1)} %all-to-all-done.1), kind=kLoop, calls=%fused_computation.21 | loop fusion | flops 960 | bytes 4352 | tf_op jit(solution)/shard_map/reduce_sum | solution.py:351
  (30 shorter events, 0.4 us)
Async XLA Ops:
  2.2 8.5 %collective-permute-start = (bf16[16,40960]{1,0:T(8,128)(2,1)}, bf16[16,40960]{1,0:T(8,128)(2,1)S(1)}, u32[]{:S(2)}, u32[]{:S(2)}) collective-permute-start(bf16[16,40960]{1,0:T(8,128)(2,1)} %t_ref.1), channel_id=1, source_target_pairs={{0,1},{1,0},{2,3},{3,2},{4,5},{5,4},{6,7},{7,6},{8,9},{9,8},{10,11... | collective-permute-start | bytes 3932168 | tf_op jit(solution)/shard_map/ppermute | solution.py:215
  2.7 7.9 %collective-permute-start.1 = (f32[2,64]{1,0:T(2,128)S(1)}, f32[2,64]{1,0:T(2,128)S(1)}, u32[]{:S(2)}, u32[]{:S(2)}) collective-permute-start(f32[2,64]{1,0:T(2,128)S(1)} %pad_maximum_fusion.1), channel_id=1, source_target_pairs={{0,1},{1,0},{2,3},{3,2},{4,5},{5,4},{6,7},{7,6},{8,9},{9,8},{10,11... | collective-permute-start | bytes 1544 | tf_op jit(solution)/shard_map/ppermute | solution.py:215
  2.8 7.9 %collective-permute-start.2 = (bf16[1,8,1920]{2,1,0:T(8,128)(2,1)}, bf16[1,8,1920]{2,1,0:T(8,128)(2,1)S(1)}, u32[]{:S(2)}, u32[]{:S(2)}) collective-permute-start(bf16[1,8,1920]{2,1,0:T(8,128)(2,1)} %bitcast.9), channel_id=1, source_target_pairs={{0,8},{2,10},{4,12},{6,14},{8,0},{10,2},{12,4},{14,6},{1,9},{3,11}... | collective-permute-start | bytes 92168 | tf_op jit(solution)/shard_map/ppermute | solution.py:219
  7.9 1.3 %copy-start = (bf16[16,40960]{1,0:T(8,128)(2,1)S(1)}, bf16[16,40960]{1,0:T(8,128)(2,1)}, u32[]{:S(2)}) copy-start(bf16[16,40960]{1,0:T(8,128)(2,1)} %t_ref.1) | copy-start | bytes 3932164
  10.8 7.1 %copy-start.1 = (bf16[64,4096]{1,0:T(8,128)(2,1)S(1)}, bf16[64,4096]{1,0:T(8,128)(2,1)}, u32[]{:S(2)}) copy-start(bf16[64,4096]{1,0:T(8,128)(2,1)} %param.10) | copy-start | bytes 1572868
  13.3 4.7 %copy-start.2 = (bf16[8,1920]{1,0:T(8,128)(2,1)S(1)}, bf16[8,1920]{1,0:T(8,128)(2,1)}, u32[]{:S(2)}) copy-start(bf16[8,1920]{1,0:T(8,128)(2,1)} %param.11) | copy-start | bytes 92164
  13.4 19.0 %all-to-all-start = ((bf16[8,16,2176]{2,1,0:T(8,128)(2,1)}), bf16[8,16,2176]{2,1,0:T(8,128)(2,1)S(1)}, u32[]{:S(2)}, u32[]{:S(2)}) async-start(bf16[8,16,2176]{2,1,0:T(8,128)(2,1)} %map_rest.1), calls=%async_computation | async-start | bytes 1114112 | tf_op jit(solution)/shard_map/all_to_all | solution.py:294
  17.9 3.7 %collective-permute-start.3 = (bf16[64,2048]{1,0:T(8,128)(2,1)S(1)}, bf16[64,2048]{1,0:T(8,128)(2,1)S(1)}, u32[]{:S(2)}, u32[]{:S(2)}) collective-permute-start(bf16[64,2048]{1,0:T(8,128)(2,1)S(1)} %constant_dynamic-slice_fusion.1), channel_id=1, source_target_pairs={{0,1},{1,0},{2,3},{3,2},{4,5},{5,4},{6,7},{7,6},{8,9},{9,8},{10,11... | collective-permute-start | bytes 786440 | tf_op jit(solution)/shard_map/ppermute | solution.py:215
  18.0 15.5 %collective-permute-start.6 = (bf16[2,8,1920]{2,1,0:T(8,128)(2,1)S(1)}, bf16[2,8,1920]{2,1,0:T(8,128)(2,1)S(1)}, u32[]{:S(2)}, u32[]{:S(2)}) collective-permute-start(bf16[2,8,1920]{2,1,0:T(8,128)(2,1)S(1)} %constant_dynamic-update-slice_fusion), channel_id=1, source_target_pairs={{0,6},{2,4},{4,2},{6,0},{8,14},{10,12},{12,10},{14,8},{1,7},{3,5},... | collective-permute-start | bytes 184328 | tf_op jit(solution)/shard_map/ppermute | solution.py:219
  21.0 12.6 %collective-permute-start.5 = (bf16[2,8,1920]{2,1,0:T(8,128)(2,1)S(1)}, bf16[2,8,1920]{2,1,0:T(8,128)(2,1)S(1)}, u32[]{:S(2)}, u32[]{:S(2)}) collective-permute-start(bf16[2,8,1920]{2,1,0:T(8,128)(2,1)S(1)} %constant_dynamic-update-slice_fusion), channel_id=1, source_target_pairs={{0,4},{2,6},{4,0},{6,2},{8,12},{10,14},{12,8},{14,10},{1,5},{3,7},... | collective-permute-start | bytes 184328 | tf_op jit(solution)/shard_map/ppermute | solution.py:219
  21.6 12.0 %collective-permute-start.4 = (bf16[2,8,1920]{2,1,0:T(8,128)(2,1)S(1)}, bf16[2,8,1920]{2,1,0:T(8,128)(2,1)S(1)}, u32[]{:S(2)}, u32[]{:S(2)}) collective-permute-start(bf16[2,8,1920]{2,1,0:T(8,128)(2,1)S(1)} %constant_dynamic-update-slice_fusion), channel_id=1, source_target_pairs={{0,2},{2,0},{4,6},{6,4},{8,10},{10,8},{12,14},{14,12},{1,3},{3,1},... | collective-permute-start | bytes 184328 | tf_op jit(solution)/shard_map/ppermute | solution.py:219
  33.7 4.5 %collective-permute-start.8 = (bf16[64,2048]{1,0:T(8,128)(2,1)S(1)}, bf16[64,2048]{1,0:T(8,128)(2,1)S(1)}, u32[]{:S(2)}, u32[]{:S(2)}) collective-permute-start(bf16[64,2048]{1,0:T(8,128)(2,1)S(1)} %constant_dynamic-slice_fusion), channel_id=1, source_target_pairs={{0,1},{1,0},{2,3},{3,2},{4,5},{5,4},{6,7},{7,6},{8,9},{9,8},{10,11... | collective-permute-start | bytes 786440 | tf_op jit(solution)/shard_map/ppermute | solution.py:215
  33.8 4.4 %collective-permute-start.7 = (bf16[8,8,1920]{2,1,0:T(8,128)(2,1)S(1)}, bf16[8,8,1920]{2,1,0:T(8,128)(2,1)S(1)}, u32[]{:S(2)}, u32[]{:S(2)}) collective-permute-start(bf16[8,8,1920]{2,1,0:T(8,128)(2,1)S(1)} %constant_dynamic-update-slice_fusion.2.own_ref), channel_id=1, source_target_pairs={{0,1},{1,0},{2,3},{3,2},{4,5},{5,4},{6,7},{7,6},{8,9},{9,8},{10,11... | collective-permute-start | bytes 737288 | tf_op jit(solution)/shard_map/ppermute | solution.py:215
  34.3 10.6 %all-to-all-start.1 = ((f32[16,8,128]{2,1,0:T(8,128)}), f32[16,8,128]{2,1,0:T(8,128)S(1)}, u32[]{:S(2)}, u32[]{:S(2)}) async-start(f32[16,8,128]{2,1,0:T(8,128)} %get-tuple-element.26), calls=%async_computation.1 | async-start | bytes 131072 | tf_op jit(solution)/shard_map/all_to_all | solution.py:324

commit v15 on v14

--- a/solution.py
+++ b/solution.py
@@ -203,7 +203,7 @@
     return pl.BlockSpec(memory_space=pl.ANY)
 
 
-def params(mib=24):
+def params(mib=48):
     return pltpu.CompilerParams(vmem_limit_bytes=mib << 20)
 
 
@@ -340,7 +340,7 @@
             dma(steps),
             dma(2),
         ],
-        compiler_params=params(32),
+        compiler_params=params(),
         cost_estimate=cost(
             2 * features * group_tokens * width,
             2 * (features * width + group_tokens * (features + width)),

time: 46 us -> 46 us (level)
  no operation moved by 1% of the time
where the time goes in v15:
time: 46 us; the launch traced here: 45.5 us
  starting transfers between devices  17.2 us (37%)
  waiting for transfers between devices  12.9 us (28%)
  Pallas kernels  9.66 us (21%)
  other arithmetic  3.44 us (7%)
  local copies, waits for them, and re-layouts  1.52 us (3%)
  between operations  0.84 us (2%)
    all_to_all x1, waiting for transfers between devices, body(): target = lax.all_to_all(outgoing, 'sv', 0, 0, tiled=True)  10.6 us
    ppermute x4, starting transfers between devices, to_partner(): lax.ppermute(x, 'sv', [(s, s ^ offset) for s in range(lax.axis_size('sv'))])  7.63 us
    all_to_all x1, starting transfers between devices, body(): target = lax.all_to_all(outgoing, 'sv', 0, 0, tiled=True)  4.53 us
    pallas_call x1, Pallas kernels, body(): pl.pallas_call(weight_kernel, out_shape=(shape((features, width), bf16),...  4.48 us
    all_to_all x1, starting transfers between devices, body(): terms = lax.all_to_all(terms, ('sv', 'tv'), 0, 0, tiled=True)  3.74 us
    pallas_call x1, Pallas kernels, body(): pl.pallas_call(map_rest_kernel, out_shape=shape(chunk, bf16), in_specs=[i...  2.57 us
    all_to_all x1, waiting for transfers between devices, body(): terms = lax.all_to_all(terms, ('sv', 'tv'), 0, 0, tiled=True)  2.32 us
    another operation x1, other arithmetic, body(): lax.reduce((wide, jnp.ones_like(wide)), (low, jnp.float32(0)), merge, (1,))  1.57 us
  transfers between devices with their start and end apart: 11, of which 2 were waited for; matrix products, arithmetic and copies ran while one was open for 3% of the time, Pallas kernels for 16%

profile of v15, /device:TPU:0, one launch (start us, length us, event | category | flops | bytes accessed | tf_op | source)
XLA Modules:
  0.0 45.5 jit_solution(15407438508556814805)
XLA Ops:
  0.6 1.6 %convert_reduce_fusion = (f32[64]{0:T(128)S(1)}, f32[64]{0:T(128)S(1)}) fusion(bf16[64,4096]{1,0:T(8,128)(2,1)} %param.10), kind=kLoop, calls=%fused_computation | loop fusion | flops 1834624 | bytes 524800 | tf_op jit(solution)/shard_map/reduce | solution.py:255
  2.2 0.5 %collective-permute-start = (bf16[16,40960]{1,0:T(8,128)(2,1)}, bf16[16,40960]{1,0:T(8,128)(2,1)S(1)}, u32[]{:S(2)}, u32[]{:S(2)}) collective-permute-start(bf16[16,40960]{1,0:T(8,128)(2,1)} %t_ref.1), channel_id=1, source_target_pairs={{0,1},{1,0},{2,3},{3,2},{4,5},{5,4},{6,7},{7,6},{8,9},{9,8},{10,11... | collective-permute-start | bytes 3932168 | tf_op jit(solution)/shard_map/ppermute | solution.py:215
  2.7 0.1 collective-permute-start.1
  2.8 4.0 %collective-permute-start.2 = (bf16[1,8,1920]{2,1,0:T(8,128)(2,1)}, bf16[1,8,1920]{2,1,0:T(8,128)(2,1)S(1)}, u32[]{:S(2)}, u32[]{:S(2)}) collective-permute-start(bf16[1,8,1920]{2,1,0:T(8,128)(2,1)} %bitcast.9), channel_id=1, source_target_pairs={{0,8},{2,10},{4,12},{6,14},{8,0},{10,2},{12,4},{14,6},{1,9},{3,11}... | collective-permute-start | bytes 92168 | tf_op jit(solution)/shard_map/ppermute | solution.py:219
  6.8 0.7 %fusion.5 = f32[640,2]{0,1:T(2,128)S(1)} fusion(bf16[640,2]{0,1:T(2,128)(2,1)} %param.9, s32[640,2]{0,1:T(2,128)} %param.7, s32[640,2]{0,1:T(2,128)} %param.8, s32[]{:T(128)S(6)} %mul.51), kind=kLoop, calls=%fused_computation.23 | loop fusion | flops 14080 | bytes 17924 | tf_op jit(solution)/shard_map/add | solution.py:262
  7.6 0.1 dynamic-slice_bitcast_fusion
  7.7 0.2 add_convert_fusion
  7.9 1.3 %copy-done = bf16[16,40960]{1,0:T(8,128)(2,1)S(1)} copy-done((bf16[16,40960]{1,0:T(8,128)(2,1)S(1)}, bf16[16,40960]{1,0:T(8,128)(2,1)}, u32[]{:S(2)}) %copy-start) | copy-done | bytes 1310744
  9.3 1.4 %map_own.1.p_ref = f32[144,2048]{1,0:T(8,128)S(1)} custom-call(bf16[144,320]{1,0:T(8,128)(2,1)S(1)} %get-tuple-element.53.w_ref, bf16[16,40960]{1,0:T(8,128)(2,1)S(1)} %copy-done), custom_call_target="tpu_custom_call" | custom-call | flops 188743680 | bytes 3145728 | tf_op jit(solution)/shard_map/map_own/pallas_call | solution.py:268
  10.7 0.1 pad_maximum_fusion.2.stats_ref
  10.8 2.6 %map_rest.1 = bf16[8,16,2176]{2,1,0:T(8,128)(2,1)} custom-call(bf16[144,320]{1,0:T(8,128)(2,1)S(1)} %get-tuple-element.54.w_ref, bf16[16,40960]{1,0:T(8,128)(2,1)S(1)} %collective-permute-done.t_ref, f32[144,2048]{1,0:T(8,128)S(1)} %map_own.1.p_ref, f32[2,128]{1,0:T(2,128)S(1)} %pad_maximum_fusion.2.stats_ref, ...), custom_call_target="tpu_custom_call" | custom-call | flops 188743680 | bytes 4194304 | tf_op jit(solution)/shard_map/map_rest/pallas_call | solution.py:279
  13.4 4.5 %all-to-all-start = ((bf16[8,16,2176]{2,1,0:T(8,128)(2,1)}), bf16[8,16,2176]{2,1,0:T(8,128)(2,1)S(1)}, u32[]{:S(2)}, u32[]{:S(2)}) async-start(bf16[8,16,2176]{2,1,0:T(8,128)(2,1)} %map_rest.1), calls=%async_computation | async-start | bytes 1114112 | tf_op jit(solution)/shard_map/all_to_all | solution.py:294
  18.0 3.0 %collective-permute-start.6 = (bf16[2,8,1920]{2,1,0:T(8,128)(2,1)S(1)}, bf16[2,8,1920]{2,1,0:T(8,128)(2,1)S(1)}, u32[]{:S(2)}, u32[]{:S(2)}) collective-permute-start(bf16[2,8,1920]{2,1,0:T(8,128)(2,1)S(1)} %constant_dynamic-update-slice_fusion), channel_id=1, source_target_pairs={{0,6},{2,4},{4,2},{6,0},{8,14},{10,12},{12,10},{14,8},{1,7},{3,5},... | collective-permute-start | bytes 184328 | tf_op jit(solution)/shard_map/ppermute | solution.py:219
  21.0 0.6 %collective-permute-start.5 = (bf16[2,8,1920]{2,1,0:T(8,128)(2,1)S(1)}, bf16[2,8,1920]{2,1,0:T(8,128)(2,1)S(1)}, u32[]{:S(2)}, u32[]{:S(2)}) collective-permute-start(bf16[2,8,1920]{2,1,0:T(8,128)(2,1)S(1)} %constant_dynamic-update-slice_fusion), channel_id=1, source_target_pairs={{0,4},{2,6},{4,0},{6,2},{8,12},{10,14},{12,8},{14,10},{1,5},{3,7},... | collective-permute-start | bytes 184328 | tf_op jit(solution)/shard_map/ppermute | solution.py:219
  21.6 0.1 collective-permute-start.4
  21.7 0.1 broadcast_select_fusion.1
  21.8 10.6 %all-to-all-done.refs_0_ = bf16[8,16,2176]{2,1,0:T(8,128)(2,1)S(1)} async-done(((bf16[8,16,2176]{2,1,0:T(8,128)(2,1)}), bf16[8,16,2176]{2,1,0:T(8,128)(2,1)S(1)}, u32[]{:S(2)}, u32[]{:S(2)}) %all-to-all-start) | async-done | bytes 557088 | tf_op jit(solution)/shard_map/all_to_all | solution.py:294
  32.4 1.2 %logit_grad.1 = (bf16[128,2048]{1,0:T(8,128)(2,1)S(1)}, f32[16,8,128]{2,1,0:T(8,128)}) custom-call(bf16[8,16,2176]{2,1,0:T(8,128)(2,1)S(1)} %all-to-all-done.refs_0_, bf16[128,2048]{1,0:T(8,128)(2,1)S(1)} %pad_maximum_fusion.refs_1_), custom_call_target="tpu_custom_call" | custom-call | flops 2621440 | bytes 1572864 | tf_op jit(solution)/shard_map/logit_grad/pallas_call | solution.py:307
  33.8 0.5 %collective-permute-start.7 = (bf16[8,8,1920]{2,1,0:T(8,128)(2,1)S(1)}, bf16[8,8,1920]{2,1,0:T(8,128)(2,1)S(1)}, u32[]{:S(2)}, u32[]{:S(2)}) collective-permute-start(bf16[8,8,1920]{2,1,0:T(8,128)(2,1)S(1)} %constant_dynamic-update-slice_fusion.2.own_ref), channel_id=1, source_target_pairs={{0,1},{1,0},{2,3},{3,2},{4,5},{5,4},{6,7},{7,6},{8,9},{9,8},{10,11... | collective-permute-start | bytes 737288 | tf_op jit(solution)/shard_map/ppermute | solution.py:215
  34.4 3.7 %all-to-all-start.1 = ((f32[16,8,128]{2,1,0:T(8,128)}), f32[16,8,128]{2,1,0:T(8,128)S(1)}, u32[]{:S(2)}, u32[]{:S(2)}) async-start(f32[16,8,128]{2,1,0:T(8,128)} %get-tuple-element.26), calls=%async_computation.1 | async-start | bytes 131072 | tf_op jit(solution)/shard_map/all_to_all | solution.py:324
  38.1 0.1 pad_add_fusion.place_ref
  38.2 4.5 %weight_grad.1 = (bf16[1920,2048]{1,0:T(8,128)(2,1)}, bf16[64,4096]{1,0:T(8,128)(2,1)}) custom-call(s32[2]{0:T(128)S(1)} %pad_add_fusion.place_ref, bf16[8,8,1920]{2,1,0:T(8,128)(2,1)S(1)} %constant_dynamic-update-slice_fusion.2.own_ref, bf16[8,8,1920]{2,1,0:T(8,128)(2,1)S(1)} %collective-permute-done.7.other_ref, ...), custom_call_target="tpu_custom_call" | custom-call | flops 1006632960 | bytes 8880128 | tf_op jit(solution)/shard_map/weight_grad/pallas_call | solution.py:331
  42.7 2.3 %all-to-all-done.1 = f32[16,8,128]{2,1,0:T(8,128)S(1)} async-done(((f32[16,8,128]{2,1,0:T(8,128)}), f32[16,8,128]{2,1,0:T(8,128)S(1)}, u32[]{:S(2)}, u32[]{:S(2)}) %all-to-all-start.1) | async-done | bytes 65568 | tf_op jit(solution)/shard_map/all_to_all | solution.py:324
  45.0 0.5 %slice_reduce_fusion = f32[64]{0:T(128)} fusion(f32[16,8,128]{2,1,0:T(8,128)S(1)} %all-to-all-done.1), kind=kLoop, calls=%fused_computation.21 | loop fusion | flops 960 | bytes 4352 | tf_op jit(solution)/shard_map/reduce_sum | solution.py:351
  (30 shorter events, 0.4 us)
Async XLA Ops:
  2.2 8.5 %collective-permute-start = (bf16[16,40960]{1,0:T(8,128)(2,1)}, bf16[16,40960]{1,0:T(8,128)(2,1)S(1)}, u32[]{:S(2)}, u32[]{:S(2)}) collective-permute-start(bf16[16,40960]{1,0:T(8,128)(2,1)} %t_ref.1), channel_id=1, source_target_pairs={{0,1},{1,0},{2,3},{3,2},{4,5},{5,4},{6,7},{7,6},{8,9},{9,8},{10,11... | collective-permute-start | bytes 3932168 | tf_op jit(solution)/shard_map/ppermute | solution.py:215
  2.7 7.9 %collective-permute-start.1 = (f32[2,64]{1,0:T(2,128)S(1)}, f32[2,64]{1,0:T(2,128)S(1)}, u32[]{:S(2)}, u32[]{:S(2)}) collective-permute-start(f32[2,64]{1,0:T(2,128)S(1)} %pad_maximum_fusion.1), channel_id=1, source_target_pairs={{0,1},{1,0},{2,3},{3,2},{4,5},{5,4},{6,7},{7,6},{8,9},{9,8},{10,11... | collective-permute-start | bytes 1544 | tf_op jit(solution)/shard_map/ppermute | solution.py:215
  2.8 7.9 %collective-permute-start.2 = (bf16[1,8,1920]{2,1,0:T(8,128)(2,1)}, bf16[1,8,1920]{2,1,0:T(8,128)(2,1)S(1)}, u32[]{:S(2)}, u32[]{:S(2)}) collective-permute-start(bf16[1,8,1920]{2,1,0:T(8,128)(2,1)} %bitcast.9), channel_id=1, source_target_pairs={{0,8},{2,10},{4,12},{6,14},{8,0},{10,2},{12,4},{14,6},{1,9},{3,11}... | collective-permute-start | bytes 92168 | tf_op jit(solution)/shard_map/ppermute | solution.py:219
  7.9 1.3 %copy-start = (bf16[16,40960]{1,0:T(8,128)(2,1)S(1)}, bf16[16,40960]{1,0:T(8,128)(2,1)}, u32[]{:S(2)}) copy-start(bf16[16,40960]{1,0:T(8,128)(2,1)} %t_ref.1) | copy-start | bytes 3932164
  10.8 7.1 %copy-start.1 = (bf16[64,4096]{1,0:T(8,128)(2,1)S(1)}, bf16[64,4096]{1,0:T(8,128)(2,1)}, u32[]{:S(2)}) copy-start(bf16[64,4096]{1,0:T(8,128)(2,1)} %param.10) | copy-start | bytes 1572868
  13.3 4.7 %copy-start.2 = (bf16[8,1920]{1,0:T(8,128)(2,1)S(1)}, bf16[8,1920]{1,0:T(8,128)(2,1)}, u32[]{:S(2)}) copy-start(bf16[8,1920]{1,0:T(8,128)(2,1)} %param.11) | copy-start | bytes 92164
  13.4 19.0 %all-to-all-start = ((bf16[8,16,2176]{2,1,0:T(8,128)(2,1)}), bf16[8,16,2176]{2,1,0:T(8,128)(2,1)S(1)}, u32[]{:S(2)}, u32[]{:S(2)}) async-start(bf16[8,16,2176]{2,1,0:T(8,128)(2,1)} %map_rest.1), calls=%async_computation | async-start | bytes 1114112 | tf_op jit(solution)/shard_map/all_to_all | solution.py:294
  17.9 3.7 %collective-permute-start.3 = (bf16[64,2048]{1,0:T(8,128)(2,1)S(1)}, bf16[64,2048]{1,0:T(8,128)(2,1)S(1)}, u32[]{:S(2)}, u32[]{:S(2)}) collective-permute-start(bf16[64,2048]{1,0:T(8,128)(2,1)S(1)} %constant_dynamic-slice_fusion.1), channel_id=1, source_target_pairs={{0,1},{1,0},{2,3},{3,2},{4,5},{5,4},{6,7},{7,6},{8,9},{9,8},{10,11... | collective-permute-start | bytes 786440 | tf_op jit(solution)/shard_map/ppermute | solution.py:215
  18.0 15.6 %collective-permute-start.6 = (bf16[2,8,1920]{2,1,0:T(8,128)(2,1)S(1)}, bf16[2,8,1920]{2,1,0:T(8,128)(2,1)S(1)}, u32[]{:S(2)}, u32[]{:S(2)}) collective-permute-start(bf16[2,8,1920]{2,1,0:T(8,128)(2,1)S(1)} %constant_dynamic-update-slice_fusion), channel_id=1, source_target_pairs={{0,6},{2,4},{4,2},{6,0},{8,14},{10,12},{12,10},{14,8},{1,7},{3,5},... | collective-permute-start | bytes 184328 | tf_op jit(solution)/shard_map/ppermute | solution.py:219
  21.0 12.6 %collective-permute-start.5 = (bf16[2,8,1920]{2,1,0:T(8,128)(2,1)S(1)}, bf16[2,8,1920]{2,1,0:T(8,128)(2,1)S(1)}, u32[]{:S(2)}, u32[]{:S(2)}) collective-permute-start(bf16[2,8,1920]{2,1,0:T(8,128)(2,1)S(1)} %constant_dynamic-update-slice_fusion), channel_id=1, source_target_pairs={{0,4},{2,6},{4,0},{6,2},{8,12},{10,14},{12,8},{14,10},{1,5},{3,7},... | collective-permute-start | bytes 184328 | tf_op jit(solution)/shard_map/ppermute | solution.py:219
  21.6 12.0 %collective-permute-start.4 = (bf16[2,8,1920]{2,1,0:T(8,128)(2,1)S(1)}, bf16[2,8,1920]{2,1,0:T(8,128)(2,1)S(1)}, u32[]{:S(2)}, u32[]{:S(2)}) collective-permute-start(bf16[2,8,1920]{2,1,0:T(8,128)(2,1)S(1)} %constant_dynamic-update-slice_fusion), channel_id=1, source_target_pairs={{0,2},{2,0},{4,6},{6,4},{8,10},{10,8},{12,14},{14,12},{1,3},{3,1},... | collective-permute-start | bytes 184328 | tf_op jit(solution)/shard_map/ppermute | solution.py:219
  33.7 4.5 %collective-permute-start.8 = (bf16[64,2048]{1,0:T(8,128)(2,1)S(1)}, bf16[64,2048]{1,0:T(8,128)(2,1)S(1)}, u32[]{:S(2)}, u32[]{:S(2)}) collective-permute-start(bf16[64,2048]{1,0:T(8,128)(2,1)S(1)} %constant_dynamic-slice_fusion), channel_id=1, source_target_pairs={{0,1},{1,0},{2,3},{3,2},{4,5},{5,4},{6,7},{7,6},{8,9},{9,8},{10,11... | collective-permute-start | bytes 786440 | tf_op jit(solution)/shard_map/ppermute | solution.py:215
  33.8 4.4 %collective-permute-start.7 = (bf16[8,8,1920]{2,1,0:T(8,128)(2,1)S(1)}, bf16[8,8,1920]{2,1,0:T(8,128)(2,1)S(1)}, u32[]{:S(2)}, u32[]{:S(2)}) collective-permute-start(bf16[8,8,1920]{2,1,0:T(8,128)(2,1)S(1)} %constant_dynamic-update-slice_fusion.2.own_ref), channel_id=1, source_target_pairs={{0,1},{1,0},{2,3},{3,2},{4,5},{5,4},{6,7},{7,6},{8,9},{9,8},{10,11... | collective-permute-start | bytes 737288 | tf_op jit(solution)/shard_map/ppermute | solution.py:215
  34.4 10.6 %all-to-all-start.1 = ((f32[16,8,128]{2,1,0:T(8,128)}), f32[16,8,128]{2,1,0:T(8,128)S(1)}, u32[]{:S(2)}, u32[]{:S(2)}) async-start(f32[16,8,128]{2,1,0:T(8,128)} %get-tuple-element.26), calls=%async_computation.1 | async-start | bytes 131072 | tf_op jit(solution)/shard_map/all_to_all | solution.py:324

commit v16 on v15

--- a/solution.py
+++ b/solution.py
@@ -42,7 +42,7 @@
     return jnp.concatenate(both, axis=1)
 
 
-def map_own_kernel(w_ref, t_ref, o_ref, s_ref):
+def map_own_kernel(w_ref, t_ref, stats_ref, o_ref, s_ref):
     tokens = t_ref.shape[0]
     spread_tokens(t_ref, s_ref, 0, t_ref.shape[1] // BLK)
     for t in range(0, tokens, 2):
@@ -268,13 +268,13 @@
     part = pl.pallas_call(
         map_own_kernel,
         out_shape=shape((rows + MASS_ROWS, tokens * BLK), f32),
-        in_specs=[in_vmem()] * 2,
+        in_specs=[in_vmem()] * 2 + [anywhere()],
         out_specs=in_vmem(),
         scratch_shapes=[spread],
         compiler_params=params(),
         cost_estimate=cost(flops, 3 << 20),
         name="map_own",
-    )(w_own, teacher_probs)
+    )(w_own, teacher_probs, stats)
     chunk = (owners, tokens, width + group_tokens)
     outgoing = pl.pallas_call(
         map_rest_kernel,

time: 46 us -> 45.9 us (level)
  starting transfers between devices: 17.2 us -> 18.5 us
  local copies, waits for them, and re-layouts: 1.52 us -> 0.22 us
    unnamed x10, local copies, waits for them, and re-layouts: 1.36 us -> 0.05 us
    all_to_all x1, starting transfers between devices: 4.53 us -> 5.82 us  [body(): target = lax.all_to_all(outgoing, 'sv', 0, 0, tiled=True)]
where the time goes in v16:
time: 45.9 us; the launch traced here: 45.5 us
  starting transfers between devices  18.5 us (40%)
  waiting for transfers between devices  12.8 us (28%)
  Pallas kernels  9.67 us (21%)
  other arithmetic  3.54 us (8%)
  between operations  0.86 us (2%)
    all_to_all x1, waiting for transfers between devices, body(): target = lax.all_to_all(outgoing, 'sv', 0, 0, tiled=True)  10.4 us
    ppermute x4, starting transfers between devices, to_partner(): lax.ppermute(x, 'sv', [(s, s ^ offset) for s in range(lax.axis_size('sv'))])  7.62 us
    all_to_all x1, starting transfers between devices, body(): target = lax.all_to_all(outgoing, 'sv', 0, 0, tiled=True)  5.82 us
    pallas_call x1, Pallas kernels, body(): pl.pallas_call(weight_kernel, out_shape=(shape((features, width), bf16),...  4.48 us
    all_to_all x1, starting transfers between devices, body(): terms = lax.all_to_all(terms, ('sv', 'tv'), 0, 0, tiled=True)  3.74 us
    pallas_call x1, Pallas kernels, body(): pl.pallas_call(map_rest_kernel, out_shape=shape(chunk, bf16), in_specs=[i...  2.57 us
    all_to_all x1, waiting for transfers between devices, body(): terms = lax.all_to_all(terms, ('sv', 'tv'), 0, 0, tiled=True)  2.32 us
    another operation x1, other arithmetic, body(): lax.reduce((wide, jnp.ones_like(wide)), (low, jnp.float32(0)), merge, (1,))  1.68 us
  transfers between devices with their start and end apart: 11, of which 2 were waited for; matrix products, arithmetic and copies ran while one was open for 3% of the time, Pallas kernels for 16%

profile of v16, /device:TPU:0, one launch (start us, length us, event | category | flops | bytes accessed | tf_op | source)
XLA Modules:
  0.0 45.5 jit_solution(17922995875262751127)
XLA Ops:
  0.6 1.7 %convert_reduce_fusion = (f32[64]{0:T(128)S(1)}, f32[64]{0:T(128)S(1)}) fusion(bf16[64,4096]{1,0:T(8,128)(2,1)} %param.10), kind=kLoop, calls=%fused_computation | loop fusion | flops 1834624 | bytes 524800 | tf_op jit(solution)/shard_map/reduce | solution.py:255
  2.3 0.5 %collective-permute-start = (bf16[16,40960]{1,0:T(8,128)(2,1)}, bf16[16,40960]{1,0:T(8,128)(2,1)S(1)}, u32[]{:S(2)}, u32[]{:S(2)}) collective-permute-start(bf16[16,40960]{1,0:T(8,128)(2,1)} %t_ref.1), channel_id=1, source_target_pairs={{0,1},{1,0},{2,3},{3,2},{4,5},{5,4},{6,7},{7,6},{8,9},{9,8},{10,11... | collective-permute-start | bytes 3932168 | tf_op jit(solution)/shard_map/ppermute | solution.py:215
  2.8 0.1 collective-permute-start.1
  2.9 4.0 %collective-permute-start.2 = (bf16[1,8,1920]{2,1,0:T(8,128)(2,1)}, bf16[1,8,1920]{2,1,0:T(8,128)(2,1)S(1)}, u32[]{:S(2)}, u32[]{:S(2)}) collective-permute-start(bf16[1,8,1920]{2,1,0:T(8,128)(2,1)} %bitcast.9), channel_id=1, source_target_pairs={{0,8},{2,10},{4,12},{6,14},{8,0},{10,2},{12,4},{14,6},{1,9},{3,11}... | collective-permute-start | bytes 92168 | tf_op jit(solution)/shard_map/ppermute | solution.py:219
  6.9 0.7 %fusion.5 = f32[640,2]{0,1:T(2,128)S(1)} fusion(bf16[640,2]{0,1:T(2,128)(2,1)} %param.9, s32[640,2]{0,1:T(2,128)} %param.7, s32[640,2]{0,1:T(2,128)} %param.8, s32[]{:T(128)S(6)} %mul.51), kind=kLoop, calls=%fused_computation.23 | loop fusion | flops 14080 | bytes 17924 | tf_op jit(solution)/shard_map/add | solution.py:262
  7.7 0.1 dynamic-slice_bitcast_fusion
  7.8 0.2 add_convert_fusion
  8.1 0.1 pad_maximum_fusion.2.stats_ref
  8.2 1.4 %map_own.1.p_ref = f32[144,2048]{1,0:T(8,128)S(1)} custom-call(bf16[144,320]{1,0:T(8,128)(2,1)S(1)} %get-tuple-element.53.w_ref, bf16[16,40960]{1,0:T(8,128)(2,1)S(1)} %copy-done, f32[2,128]{1,0:T(2,128)S(1)} %pad_maximum_fusion.2.stats_ref), custom_call_target="tpu_custom_call" | custom-call | flops 188743680 | bytes 3145728 | tf_op jit(solution)/shard_map/map_own/pallas_call | solution.py:268
  9.6 2.6 %map_rest.1 = bf16[8,16,2176]{2,1,0:T(8,128)(2,1)} custom-call(bf16[144,320]{1,0:T(8,128)(2,1)S(1)} %get-tuple-element.54.w_ref, bf16[16,40960]{1,0:T(8,128)(2,1)S(1)} %collective-permute-done.t_ref, f32[144,2048]{1,0:T(8,128)S(1)} %map_own.1.p_ref, f32[2,128]{1,0:T(2,128)S(1)} %pad_maximum_fusion.2.stats_ref, ...), custom_call_target="tpu_custom_call" | custom-call | flops 188743680 | bytes 4194304 | tf_op jit(solution)/shard_map/map_rest/pallas_call | solution.py:279
  12.2 5.8 %all-to-all-start = ((bf16[8,16,2176]{2,1,0:T(8,128)(2,1)}), bf16[8,16,2176]{2,1,0:T(8,128)(2,1)S(1)}, u32[]{:S(2)}, u32[]{:S(2)}) async-start(bf16[8,16,2176]{2,1,0:T(8,128)(2,1)} %map_rest.1), calls=%async_computation | async-start | bytes 1114112 | tf_op jit(solution)/shard_map/all_to_all | solution.py:294
  18.0 0.1 collective-permute-start.3
  18.2 3.0 %collective-permute-start.6 = (bf16[2,8,1920]{2,1,0:T(8,128)(2,1)S(1)}, bf16[2,8,1920]{2,1,0:T(8,128)(2,1)S(1)}, u32[]{:S(2)}, u32[]{:S(2)}) collective-permute-start(bf16[2,8,1920]{2,1,0:T(8,128)(2,1)S(1)} %constant_dynamic-update-slice_fusion), channel_id=1, source_target_pairs={{0,6},{2,4},{4,2},{6,0},{8,14},{10,12},{12,10},{14,8},{1,7},{3,5},... | collective-permute-start | bytes 184328 | tf_op jit(solution)/shard_map/ppermute | solution.py:219
  21.1 0.6 %collective-permute-start.5 = (bf16[2,8,1920]{2,1,0:T(8,128)(2,1)S(1)}, bf16[2,8,1920]{2,1,0:T(8,128)(2,1)S(1)}, u32[]{:S(2)}, u32[]{:S(2)}) collective-permute-start(bf16[2,8,1920]{2,1,0:T(8,128)(2,1)S(1)} %constant_dynamic-update-slice_fusion), channel_id=1, source_target_pairs={{0,4},{2,6},{4,0},{6,2},{8,12},{10,14},{12,8},{14,10},{1,5},{3,7},... | collective-permute-start | bytes 184328 | tf_op jit(solution)/shard_map/ppermute | solution.py:219
  21.7 0.1 collective-permute-start.4
  21.8 0.1 broadcast_select_fusion.1
  21.9 10.4 %all-to-all-done.refs_0_ = bf16[8,16,2176]{2,1,0:T(8,128)(2,1)S(1)} async-done(((bf16[8,16,2176]{2,1,0:T(8,128)(2,1)}), bf16[8,16,2176]{2,1,0:T(8,128)(2,1)S(1)}, u32[]{:S(2)}, u32[]{:S(2)}) %all-to-all-start) | async-done | bytes 557088 | tf_op jit(solution)/shard_map/all_to_all | solution.py:294
  32.3 1.2 %logit_grad.1 = (bf16[128,2048]{1,0:T(8,128)(2,1)S(1)}, f32[16,8,128]{2,1,0:T(8,128)}) custom-call(bf16[8,16,2176]{2,1,0:T(8,128)(2,1)S(1)} %all-to-all-done.refs_0_, bf16[128,2048]{1,0:T(8,128)(2,1)S(1)} %pad_maximum_fusion.refs_1_), custom_call_target="tpu_custom_call" | custom-call | flops 2621440 | bytes 1572864 | tf_op jit(solution)/shard_map/logit_grad/pallas_call | solution.py:307
  33.8 0.5 %collective-permute-start.7 = (bf16[8,8,1920]{2,1,0:T(8,128)(2,1)S(1)}, bf16[8,8,1920]{2,1,0:T(8,128)(2,1)S(1)}, u32[]{:S(2)}, u32[]{:S(2)}) collective-permute-start(bf16[8,8,1920]{2,1,0:T(8,128)(2,1)S(1)} %constant_dynamic-update-slice_fusion.2.own_ref), channel_id=1, source_target_pairs={{0,1},{1,0},{2,3},{3,2},{4,5},{5,4},{6,7},{7,6},{8,9},{9,8},{10,11... | collective-permute-start | bytes 737288 | tf_op jit(solution)/shard_map/ppermute | solution.py:215
  34.3 3.7 %all-to-all-start.1 = ((f32[16,8,128]{2,1,0:T(8,128)}), f32[16,8,128]{2,1,0:T(8,128)S(1)}, u32[]{:S(2)}, u32[]{:S(2)}) async-start(f32[16,8,128]{2,1,0:T(8,128)} %get-tuple-element.26), calls=%async_computation.1 | async-start | bytes 131072 | tf_op jit(solution)/shard_map/all_to_all | solution.py:324
  38.1 0.1 pad_add_fusion.place_ref
  38.1 4.5 %weight_grad.1 = (bf16[1920,2048]{1,0:T(8,128)(2,1)}, bf16[64,4096]{1,0:T(8,128)(2,1)}) custom-call(s32[2]{0:T(128)S(1)} %pad_add_fusion.place_ref, bf16[8,8,1920]{2,1,0:T(8,128)(2,1)S(1)} %constant_dynamic-update-slice_fusion.2.own_ref, bf16[8,8,1920]{2,1,0:T(8,128)(2,1)S(1)} %collective-permute-done.7.other_ref, ...), custom_call_target="tpu_custom_call" | custom-call | flops 1006632960 | bytes 8880128 | tf_op jit(solution)/shard_map/weight_grad/pallas_call | solution.py:331
  42.6 2.3 %all-to-all-done.1 = f32[16,8,128]{2,1,0:T(8,128)S(1)} async-done(((f32[16,8,128]{2,1,0:T(8,128)}), f32[16,8,128]{2,1,0:T(8,128)S(1)}, u32[]{:S(2)}, u32[]{:S(2)}) %all-to-all-start.1) | async-done | bytes 65568 | tf_op jit(solution)/shard_map/all_to_all | solution.py:324
  45.0 0.5 %slice_reduce_fusion = f32[64]{0:T(128)} fusion(f32[16,8,128]{2,1,0:T(8,128)S(1)} %all-to-all-done.1), kind=kLoop, calls=%fused_computation.21 | loop fusion | flops 960 | bytes 4352 | tf_op jit(solution)/shard_map/reduce_sum | solution.py:351
  (30 shorter events, 0.4 us)
Async XLA Ops:
  0.6 7.5 %copy-start = (bf16[16,40960]{1,0:T(8,128)(2,1)S(1)}, bf16[16,40960]{1,0:T(8,128)(2,1)}, u32[]{:S(2)}) copy-start(bf16[16,40960]{1,0:T(8,128)(2,1)} %t_ref.1) | copy-start | bytes 3932164
  2.3 7.2 %collective-permute-start = (bf16[16,40960]{1,0:T(8,128)(2,1)}, bf16[16,40960]{1,0:T(8,128)(2,1)S(1)}, u32[]{:S(2)}, u32[]{:S(2)}) collective-permute-start(bf16[16,40960]{1,0:T(8,128)(2,1)} %t_ref.1), channel_id=1, source_target_pairs={{0,1},{1,0},{2,3},{3,2},{4,5},{5,4},{6,7},{7,6},{8,9},{9,8},{10,11... | collective-permute-start | bytes 3932168 | tf_op jit(solution)/shard_map/ppermute | solution.py:215
  2.8 5.2 %collective-permute-start.1 = (f32[2,64]{1,0:T(2,128)S(1)}, f32[2,64]{1,0:T(2,128)S(1)}, u32[]{:S(2)}, u32[]{:S(2)}) collective-permute-start(f32[2,64]{1,0:T(2,128)S(1)} %pad_maximum_fusion.1), channel_id=1, source_target_pairs={{0,1},{1,0},{2,3},{3,2},{4,5},{5,4},{6,7},{7,6},{8,9},{9,8},{10,11... | collective-permute-start | bytes 1544 | tf_op jit(solution)/shard_map/ppermute | solution.py:215
  2.9 6.6 %collective-permute-start.2 = (bf16[1,8,1920]{2,1,0:T(8,128)(2,1)}, bf16[1,8,1920]{2,1,0:T(8,128)(2,1)S(1)}, u32[]{:S(2)}, u32[]{:S(2)}) collective-permute-start(bf16[1,8,1920]{2,1,0:T(8,128)(2,1)} %bitcast.9), channel_id=1, source_target_pairs={{0,8},{2,10},{4,12},{6,14},{8,0},{10,2},{12,4},{14,6},{1,9},{3,11}... | collective-permute-start | bytes 92168 | tf_op jit(solution)/shard_map/ppermute | solution.py:219
  9.6 8.4 %copy-start.1 = (bf16[64,4096]{1,0:T(8,128)(2,1)S(1)}, bf16[64,4096]{1,0:T(8,128)(2,1)}, u32[]{:S(2)}) copy-start(bf16[64,4096]{1,0:T(8,128)(2,1)} %param.10) | copy-start | bytes 1572868
  12.2 6.0 %copy-start.2 = (bf16[8,1920]{1,0:T(8,128)(2,1)S(1)}, bf16[8,1920]{1,0:T(8,128)(2,1)}, u32[]{:S(2)}) copy-start(bf16[8,1920]{1,0:T(8,128)(2,1)} %param.11) | copy-start | bytes 92164
  12.2 20.2 %all-to-all-start = ((bf16[8,16,2176]{2,1,0:T(8,128)(2,1)}), bf16[8,16,2176]{2,1,0:T(8,128)(2,1)S(1)}, u32[]{:S(2)}, u32[]{:S(2)}) async-start(bf16[8,16,2176]{2,1,0:T(8,128)(2,1)} %map_rest.1), calls=%async_computation | async-start | bytes 1114112 | tf_op jit(solution)/shard_map/all_to_all | solution.py:294
  18.0 3.7 %collective-permute-start.3 = (bf16[64,2048]{1,0:T(8,128)(2,1)S(1)}, bf16[64,2048]{1,0:T(8,128)(2,1)S(1)}, u32[]{:S(2)}, u32[]{:S(2)}) collective-permute-start(bf16[64,2048]{1,0:T(8,128)(2,1)S(1)} %constant_dynamic-slice_fusion.1), channel_id=1, source_target_pairs={{0,1},{1,0},{2,3},{3,2},{4,5},{5,4},{6,7},{7,6},{8,9},{9,8},{10,11... | collective-permute-start | bytes 786440 | tf_op jit(solution)/shard_map/ppermute | solution.py:215
  18.2 15.4 %collective-permute-start.6 = (bf16[2,8,1920]{2,1,0:T(8,128)(2,1)S(1)}, bf16[2,8,1920]{2,1,0:T(8,128)(2,1)S(1)}, u32[]{:S(2)}, u32[]{:S(2)}) collective-permute-start(bf16[2,8,1920]{2,1,0:T(8,128)(2,1)S(1)} %constant_dynamic-update-slice_fusion), channel_id=1, source_target_pairs={{0,6},{2,4},{4,2},{6,0},{8,14},{10,12},{12,10},{14,8},{1,7},{3,5},... | collective-permute-start | bytes 184328 | tf_op jit(solution)/shard_map/ppermute | solution.py:219
  21.1 12.4 %collective-permute-start.5 = (bf16[2,8,1920]{2,1,0:T(8,128)(2,1)S(1)}, bf16[2,8,1920]{2,1,0:T(8,128)(2,1)S(1)}, u32[]{:S(2)}, u32[]{:S(2)}) collective-permute-start(bf16[2,8,1920]{2,1,0:T(8,128)(2,1)S(1)} %constant_dynamic-update-slice_fusion), channel_id=1, source_target_pairs={{0,4},{2,6},{4,0},{6,2},{8,12},{10,14},{12,8},{14,10},{1,5},{3,7},... | collective-permute-start | bytes 184328 | tf_op jit(solution)/shard_map/ppermute | solution.py:219
  21.7 11.9 %collective-permute-start.4 = (bf16[2,8,1920]{2,1,0:T(8,128)(2,1)S(1)}, bf16[2,8,1920]{2,1,0:T(8,128)(2,1)S(1)}, u32[]{:S(2)}, u32[]{:S(2)}) collective-permute-start(bf16[2,8,1920]{2,1,0:T(8,128)(2,1)S(1)} %constant_dynamic-update-slice_fusion), channel_id=1, source_target_pairs={{0,2},{2,0},{4,6},{6,4},{8,10},{10,8},{12,14},{14,12},{1,3},{3,1},... | collective-permute-start | bytes 184328 | tf_op jit(solution)/shard_map/ppermute | solution.py:219
  33.6 4.5 %collective-permute-start.8 = (bf16[64,2048]{1,0:T(8,128)(2,1)S(1)}, bf16[64,2048]{1,0:T(8,128)(2,1)S(1)}, u32[]{:S(2)}, u32[]{:S(2)}) collective-permute-start(bf16[64,2048]{1,0:T(8,128)(2,1)S(1)} %constant_dynamic-slice_fusion), channel_id=1, source_target_pairs={{0,1},{1,0},{2,3},{3,2},{4,5},{5,4},{6,7},{7,6},{8,9},{9,8},{10,11... | collective-permute-start | bytes 786440 | tf_op jit(solution)/shard_map/ppermute | solution.py:215
  33.8 4.4 %collective-permute-start.7 = (bf16[8,8,1920]{2,1,0:T(8,128)(2,1)S(1)}, bf16[8,8,1920]{2,1,0:T(8,128)(2,1)S(1)}, u32[]{:S(2)}, u32[]{:S(2)}) collective-permute-start(bf16[8,8,1920]{2,1,0:T(8,128)(2,1)S(1)} %constant_dynamic-update-slice_fusion.2.own_ref), channel_id=1, source_target_pairs={{0,1},{1,0},{2,3},{3,2},{4,5},{5,4},{6,7},{7,6},{8,9},{9,8},{10,11... | collective-permute-start | bytes 737288 | tf_op jit(solution)/shard_map/ppermute | solution.py:215
  34.3 10.6 %all-to-all-start.1 = ((f32[16,8,128]{2,1,0:T(8,128)}), f32[16,8,128]{2,1,0:T(8,128)S(1)}, u32[]{:S(2)}, u32[]{:S(2)}) async-start(f32[16,8,128]{2,1,0:T(8,128)} %get-tuple-element.26), calls=%async_computation.1 | async-start | bytes 131072 | tf_op jit(solution)/shard_map/all_to_all | solution.py:324

commit v17 on v13

--- a/solution.py
+++ b/solution.py
@@ -42,7 +42,7 @@
     return jnp.concatenate(both, axis=1)
 
 
-def map_own_kernel(w_ref, t_ref, o_ref, s_ref):
+def map_own_kernel(w_ref, t_ref, stats_ref, o_ref, s_ref):
     tokens = t_ref.shape[0]
     spread_tokens(t_ref, s_ref, 0, t_ref.shape[1] // BLK)
     for t in range(0, tokens, 2):
@@ -268,13 +268,13 @@
     part = pl.pallas_call(
         map_own_kernel,
         out_shape=shape((rows + MASS_ROWS, tokens * BLK), f32),
-        in_specs=[in_vmem()] * 2,
+        in_specs=[in_vmem()] * 2 + [anywhere()],
         out_specs=in_vmem(),
         scratch_shapes=[spread],
         compiler_params=params(),
         cost_estimate=cost(flops, 3 << 20),
         name="map_own",
-    )(w_own, teacher_probs)
+    )(w_own, teacher_probs, stats)
     chunk = (owners, tokens, width + group_tokens)
     outgoing = pl.pallas_call(
         map_rest_kernel,

time: 46.1 us -> 45.7 us (level)
  Pallas kernels: 11 us -> 9.67 us
  starting transfers between devices: 16.5 us -> 17 us
  waiting for transfers between devices: 13.6 us -> 14.1 us
    pallas_call x1, Pallas kernels: 3.94 us -> 2.57 us  [body(): pl.pallas_call(map_rest_kernel, out_shape=shape(chunk, bf16), in_specs=[i...]
    all_to_all x1, waiting for transfers between devices: 11.2 us -> 11.8 us  [body(): target = lax.all_to_all(outgoing, 'sv', 0, 0, tiled=True)]
    all_to_all x1, starting transfers between devices: 3.82 us -> 4.29 us  [body(): target = lax.all_to_all(outgoing, 'sv', 0, 0, tiled=True)]
  transfers between devices with their start and end apart: 11 -> 11, of which waited for: 2 -> 2; matrix products, arithmetic and copies ran while one was open for 3% -> 3% of each run, Pallas kernels for 24% -> 21%
where the time goes in v17:
time: 45.7 us; the launch traced here: 45.3 us
  starting transfers between devices  17 us (37%)
  waiting for transfers between devices  14.1 us (31%)
  Pallas kernels  9.67 us (21%)
  other arithmetic  3.54 us (8%)
  between operations  0.83 us (2%)
    all_to_all x1, waiting for transfers between devices, body(): target = lax.all_to_all(outgoing, 'sv', 0, 0, tiled=True)  11.8 us
    ppermute x4, starting transfers between devices, to_partner(): lax.ppermute(x, 'sv', [(s, s ^ offset) for s in range(lax.axis_size('sv'))])  7.59 us
    pallas_call x1, Pallas kernels, body(): pl.pallas_call(weight_kernel, out_shape=(shape((features, width), bf16),...  4.48 us
    all_to_all x1, starting transfers between devices, body(): target = lax.all_to_all(outgoing, 'sv', 0, 0, tiled=True)  4.29 us
    all_to_all x1, starting transfers between devices, body(): terms = lax.all_to_all(terms, ('sv', 'tv'), 0, 0, tiled=True)  3.74 us
    pallas_call x1, Pallas kernels, body(): pl.pallas_call(map_rest_kernel, out_shape=shape(chunk, bf16), in_specs=[i...  2.57 us
    all_to_all x1, waiting for transfers between devices, body(): terms = lax.all_to_all(terms, ('sv', 'tv'), 0, 0, tiled=True)  2.32 us
    another operation x1, other arithmetic, body(): lax.reduce((wide, jnp.ones_like(wide)), (low, jnp.float32(0)), merge, (1,))  1.68 us
  transfers between devices with their start and end apart: 11, of which 2 were waited for; matrix products, arithmetic and copies ran while one was open for 3% of the time, Pallas kernels for 21%

profile of v17, /device:TPU:0, one launch (start us, length us, event | category | flops | bytes accessed | tf_op | source)
XLA Modules:
  0.0 45.3 jit_solution(7809973910117664283)
XLA Ops:
  0.6 1.7 %convert_reduce_fusion = (f32[64]{0:T(128)S(1)}, f32[64]{0:T(128)S(1)}) fusion(bf16[64,4096]{1,0:T(8,128)(2,1)} %param.10), kind=kLoop, calls=%fused_computation | loop fusion | flops 1834624 | bytes 524800 | tf_op jit(solution)/shard_map/reduce | solution.py:255
  2.3 0.5 %collective-permute-start = (bf16[16,40960]{1,0:T(8,128)(2,1)}, bf16[16,40960]{1,0:T(8,128)(2,1)S(1)}, u32[]{:S(2)}, u32[]{:S(2)}) collective-permute-start(bf16[16,40960]{1,0:T(8,128)(2,1)} %t_ref.1), channel_id=1, source_target_pairs={{0,1},{1,0},{2,3},{3,2},{4,5},{5,4},{6,7},{7,6},{8,9},{9,8},{10,11... | collective-permute-start | bytes 3932168 | tf_op jit(solution)/shard_map/ppermute | solution.py:215
  2.8 0.1 collective-permute-start.1
  2.9 4.0 %collective-permute-start.2 = (bf16[1,8,1920]{2,1,0:T(8,128)(2,1)}, bf16[1,8,1920]{2,1,0:T(8,128)(2,1)S(1)}, u32[]{:S(2)}, u32[]{:S(2)}) collective-permute-start(bf16[1,8,1920]{2,1,0:T(8,128)(2,1)} %bitcast.9), channel_id=1, source_target_pairs={{0,8},{2,10},{4,12},{6,14},{8,0},{10,2},{12,4},{14,6},{1,9},{3,11}... | collective-permute-start | bytes 92168 | tf_op jit(solution)/shard_map/ppermute | solution.py:219
  6.9 0.7 %fusion.5 = f32[640,2]{0,1:T(2,128)S(1)} fusion(bf16[640,2]{0,1:T(2,128)(2,1)} %param.9, s32[640,2]{0,1:T(2,128)} %param.7, s32[640,2]{0,1:T(2,128)} %param.8, s32[]{:T(128)S(6)} %mul.51), kind=kLoop, calls=%fused_computation.23 | loop fusion | flops 14080 | bytes 17924 | tf_op jit(solution)/shard_map/add | solution.py:262
  7.7 0.1 dynamic-slice_bitcast_fusion
  7.8 0.2 add_convert_fusion
  8.1 0.1 pad_maximum_fusion.2.stats_ref
  8.2 1.4 %map_own.1.p_ref = f32[144,2048]{1,0:T(8,128)S(1)} custom-call(bf16[144,320]{1,0:T(8,128)(2,1)S(1)} %get-tuple-element.57.w_ref, bf16[16,40960]{1,0:T(8,128)(2,1)S(1)} %copy-done, f32[2,128]{1,0:T(2,128)S(1)} %pad_maximum_fusion.2.stats_ref), custom_call_target="tpu_custom_call" | custom-call | flops 188743680 | bytes 3145728 | tf_op jit(solution)/shard_map/map_own/pallas_call | solution.py:268
  9.6 2.6 %map_rest.1 = bf16[8,16,2176]{2,1,0:T(8,128)(2,1)} custom-call(bf16[144,320]{1,0:T(8,128)(2,1)S(1)} %get-tuple-element.58.w_ref, bf16[16,40960]{1,0:T(8,128)(2,1)S(1)} %collective-permute-done.t_ref, f32[144,2048]{1,0:T(8,128)S(1)} %map_own.1.p_ref, f32[2,128]{1,0:T(2,128)S(1)} %pad_maximum_fusion.2.stats_ref), custom_call_target="tpu_custom_call" | custom-call | flops 188743680 | bytes 4194304 | tf_op jit(solution)/shard_map/map_rest/pallas_call | solution.py:279
  12.2 4.3 %all-to-all-start = ((bf16[8,16,2176]{2,1,0:T(8,128)(2,1)}), bf16[8,16,2176]{2,1,0:T(8,128)(2,1)S(1)}, u32[]{:S(2)}, u32[]{:S(2)}) async-start(bf16[8,16,2176]{2,1,0:T(8,128)(2,1)} %map_rest.1), calls=%async_computation | async-start | bytes 1114112 | tf_op jit(solution)/shard_map/all_to_all | solution.py:295
  16.5 0.1 collective-permute-start.3
  16.7 2.9 %collective-permute-start.6 = (bf16[2,8,1920]{2,1,0:T(8,128)(2,1)S(1)}, bf16[2,8,1920]{2,1,0:T(8,128)(2,1)S(1)}, u32[]{:S(2)}, u32[]{:S(2)}) collective-permute-start(bf16[2,8,1920]{2,1,0:T(8,128)(2,1)S(1)} %constant_dynamic-update-slice_fusion), channel_id=1, source_target_pairs={{0,6},{2,4},{4,2},{6,0},{8,14},{10,12},{12,10},{14,8},{1,7},{3,5},... | collective-permute-start | bytes 184328 | tf_op jit(solution)/shard_map/ppermute | solution.py:219
  19.6 0.6 %collective-permute-start.5 = (bf16[2,8,1920]{2,1,0:T(8,128)(2,1)S(1)}, bf16[2,8,1920]{2,1,0:T(8,128)(2,1)S(1)}, u32[]{:S(2)}, u32[]{:S(2)}) collective-permute-start(bf16[2,8,1920]{2,1,0:T(8,128)(2,1)S(1)} %constant_dynamic-update-slice_fusion), channel_id=1, source_target_pairs={{0,4},{2,6},{4,0},{6,2},{8,12},{10,14},{12,8},{14,10},{1,5},{3,7},... | collective-permute-start | bytes 184328 | tf_op jit(solution)/shard_map/ppermute | solution.py:219
  20.2 0.1 collective-permute-start.4
  20.2 0.1 broadcast_select_fusion.1
  20.4 11.8 %all-to-all-done.refs_0_ = bf16[8,16,2176]{2,1,0:T(8,128)(2,1)S(1)} async-done(((bf16[8,16,2176]{2,1,0:T(8,128)(2,1)}), bf16[8,16,2176]{2,1,0:T(8,128)(2,1)S(1)}, u32[]{:S(2)}, u32[]{:S(2)}) %all-to-all-start) | async-done | bytes 557088 | tf_op jit(solution)/shard_map/all_to_all | solution.py:295
  32.2 1.2 %logit_grad.1 = (bf16[128,2048]{1,0:T(8,128)(2,1)S(1)}, f32[16,8,128]{2,1,0:T(8,128)}) custom-call(bf16[8,16,2176]{2,1,0:T(8,128)(2,1)S(1)} %all-to-all-done.refs_0_, bf16[128,2048]{1,0:T(8,128)(2,1)S(1)} %pad_maximum_fusion.refs_1_), custom_call_target="tpu_custom_call" | custom-call | flops 2621440 | bytes 1572864 | tf_op jit(solution)/shard_map/logit_grad/pallas_call | solution.py:308
  33.6 0.5 %collective-permute-start.7 = (bf16[8,8,1920]{2,1,0:T(8,128)(2,1)S(1)}, bf16[8,8,1920]{2,1,0:T(8,128)(2,1)S(1)}, u32[]{:S(2)}, u32[]{:S(2)}) collective-permute-start(bf16[8,8,1920]{2,1,0:T(8,128)(2,1)S(1)} %constant_dynamic-update-slice_fusion.2.own_ref), channel_id=1, source_target_pairs={{0,1},{1,0},{2,3},{3,2},{4,5},{5,4},{6,7},{7,6},{8,9},{9,8},{10,11... | collective-permute-start | bytes 737288 | tf_op jit(solution)/shard_map/ppermute | solution.py:215
  34.2 3.7 %all-to-all-start.1 = ((f32[16,8,128]{2,1,0:T(8,128)}), f32[16,8,128]{2,1,0:T(8,128)S(1)}, u32[]{:S(2)}, u32[]{:S(2)}) async-start(f32[16,8,128]{2,1,0:T(8,128)} %get-tuple-element.29), calls=%async_computation.1 | async-start | bytes 131072 | tf_op jit(solution)/shard_map/all_to_all | solution.py:325
  37.9 0.1 pad_add_fusion.place_ref
  38.0 4.5 %weight_grad.1 = (bf16[1920,2048]{1,0:T(8,128)(2,1)}, bf16[64,4096]{1,0:T(8,128)(2,1)}) custom-call(s32[2]{0:T(128)S(1)} %pad_add_fusion.place_ref, bf16[8,8,1920]{2,1,0:T(8,128)(2,1)S(1)} %constant_dynamic-update-slice_fusion.2.own_ref, bf16[8,8,1920]{2,1,0:T(8,128)(2,1)S(1)} %collective-permute-done.7.other_ref, ...), custom_call_target="tpu_custom_call" | custom-call | flops 1006632960 | bytes 8880128 | tf_op jit(solution)/shard_map/weight_grad/pallas_call | solution.py:332
  42.5 2.3 %all-to-all-done.1 = f32[16,8,128]{2,1,0:T(8,128)S(1)} async-done(((f32[16,8,128]{2,1,0:T(8,128)}), f32[16,8,128]{2,1,0:T(8,128)S(1)}, u32[]{:S(2)}, u32[]{:S(2)}) %all-to-all-start.1) | async-done | bytes 65568 | tf_op jit(solution)/shard_map/all_to_all | solution.py:325
  44.8 0.5 %slice_reduce_fusion = f32[64]{0:T(128)} fusion(f32[16,8,128]{2,1,0:T(8,128)S(1)} %all-to-all-done.1), kind=kLoop, calls=%fused_computation.21 | loop fusion | flops 960 | bytes 4352 | tf_op jit(solution)/shard_map/reduce_sum | solution.py:352
  (30 shorter events, 0.4 us)
Async XLA Ops:
  0.6 7.5 %copy-start = (bf16[16,40960]{1,0:T(8,128)(2,1)S(1)}, bf16[16,40960]{1,0:T(8,128)(2,1)}, u32[]{:S(2)}) copy-start(bf16[16,40960]{1,0:T(8,128)(2,1)} %t_ref.1) | copy-start | bytes 3932164
  2.3 7.2 %collective-permute-start = (bf16[16,40960]{1,0:T(8,128)(2,1)}, bf16[16,40960]{1,0:T(8,128)(2,1)S(1)}, u32[]{:S(2)}, u32[]{:S(2)}) collective-permute-start(bf16[16,40960]{1,0:T(8,128)(2,1)} %t_ref.1), channel_id=1, source_target_pairs={{0,1},{1,0},{2,3},{3,2},{4,5},{5,4},{6,7},{7,6},{8,9},{9,8},{10,11... | collective-permute-start | bytes 3932168 | tf_op jit(solution)/shard_map/ppermute | solution.py:215
  2.8 5.2 %collective-permute-start.1 = (f32[2,64]{1,0:T(2,128)S(1)}, f32[2,64]{1,0:T(2,128)S(1)}, u32[]{:S(2)}, u32[]{:S(2)}) collective-permute-start(f32[2,64]{1,0:T(2,128)S(1)} %pad_maximum_fusion.1), channel_id=1, source_target_pairs={{0,1},{1,0},{2,3},{3,2},{4,5},{5,4},{6,7},{7,6},{8,9},{9,8},{10,11... | collective-permute-start | bytes 1544 | tf_op jit(solution)/shard_map/ppermute | solution.py:215
  2.9 9.3 %collective-permute-start.2 = (bf16[1,8,1920]{2,1,0:T(8,128)(2,1)}, bf16[1,8,1920]{2,1,0:T(8,128)(2,1)S(1)}, u32[]{:S(2)}, u32[]{:S(2)}) collective-permute-start(bf16[1,8,1920]{2,1,0:T(8,128)(2,1)} %bitcast.9), channel_id=1, source_target_pairs={{0,8},{2,10},{4,12},{6,14},{8,0},{10,2},{12,4},{14,6},{1,9},{3,11}... | collective-permute-start | bytes 92168 | tf_op jit(solution)/shard_map/ppermute | solution.py:219
  9.6 6.9 %copy-start.1 = (bf16[64,4096]{1,0:T(8,128)(2,1)S(1)}, bf16[64,4096]{1,0:T(8,128)(2,1)}, u32[]{:S(2)}) copy-start(bf16[64,4096]{1,0:T(8,128)(2,1)} %param.10) | copy-start | bytes 1572868
  12.2 4.5 %copy-start.2 = (bf16[8,1920]{1,0:T(8,128)(2,1)S(1)}, bf16[8,1920]{1,0:T(8,128)(2,1)}, u32[]{:S(2)}) copy-start(bf16[8,1920]{1,0:T(8,128)(2,1)} %param.11) | copy-start | bytes 92164
  12.2 20.0 %all-to-all-start = ((bf16[8,16,2176]{2,1,0:T(8,128)(2,1)}), bf16[8,16,2176]{2,1,0:T(8,128)(2,1)S(1)}, u32[]{:S(2)}, u32[]{:S(2)}) async-start(bf16[8,16,2176]{2,1,0:T(8,128)(2,1)} %map_rest.1), calls=%async_computation | async-start | bytes 1114112 | tf_op jit(solution)/shard_map/all_to_all | solution.py:295
  16.5 3.7 %collective-permute-start.3 = (bf16[64,2048]{1,0:T(8,128)(2,1)S(1)}, bf16[64,2048]{1,0:T(8,128)(2,1)S(1)}, u32[]{:S(2)}, u32[]{:S(2)}) collective-permute-start(bf16[64,2048]{1,0:T(8,128)(2,1)S(1)} %constant_dynamic-slice_fusion.1), channel_id=1, source_target_pairs={{0,1},{1,0},{2,3},{3,2},{4,5},{5,4},{6,7},{7,6},{8,9},{9,8},{10,11... | collective-permute-start | bytes 786440 | tf_op jit(solution)/shard_map/ppermute | solution.py:215
  16.7 16.7 %collective-permute-start.6 = (bf16[2,8,1920]{2,1,0:T(8,128)(2,1)S(1)}, bf16[2,8,1920]{2,1,0:T(8,128)(2,1)S(1)}, u32[]{:S(2)}, u32[]{:S(2)}) collective-permute-start(bf16[2,8,1920]{2,1,0:T(8,128)(2,1)S(1)} %constant_dynamic-update-slice_fusion), channel_id=1, source_target_pairs={{0,6},{2,4},{4,2},{6,0},{8,14},{10,12},{12,10},{14,8},{1,7},{3,5},... | collective-permute-start | bytes 184328 | tf_op jit(solution)/shard_map/ppermute | solution.py:219
  19.6 13.8 %collective-permute-start.5 = (bf16[2,8,1920]{2,1,0:T(8,128)(2,1)S(1)}, bf16[2,8,1920]{2,1,0:T(8,128)(2,1)S(1)}, u32[]{:S(2)}, u32[]{:S(2)}) collective-permute-start(bf16[2,8,1920]{2,1,0:T(8,128)(2,1)S(1)} %constant_dynamic-update-slice_fusion), channel_id=1, source_target_pairs={{0,4},{2,6},{4,0},{6,2},{8,12},{10,14},{12,8},{14,10},{1,5},{3,7},... | collective-permute-start | bytes 184328 | tf_op jit(solution)/shard_map/ppermute | solution.py:219
  20.2 13.3 %collective-permute-start.4 = (bf16[2,8,1920]{2,1,0:T(8,128)(2,1)S(1)}, bf16[2,8,1920]{2,1,0:T(8,128)(2,1)S(1)}, u32[]{:S(2)}, u32[]{:S(2)}) collective-permute-start(bf16[2,8,1920]{2,1,0:T(8,128)(2,1)S(1)} %constant_dynamic-update-slice_fusion), channel_id=1, source_target_pairs={{0,2},{2,0},{4,6},{6,4},{8,10},{10,8},{12,14},{14,12},{1,3},{3,1},... | collective-permute-start | bytes 184328 | tf_op jit(solution)/shard_map/ppermute | solution.py:219
  33.5 4.5 %collective-permute-start.8 = (bf16[64,2048]{1,0:T(8,128)(2,1)S(1)}, bf16[64,2048]{1,0:T(8,128)(2,1)S(1)}, u32[]{:S(2)}, u32[]{:S(2)}) collective-permute-start(bf16[64,2048]{1,0:T(8,128)(2,1)S(1)} %constant_dynamic-slice_fusion), channel_id=1, source_target_pairs={{0,1},{1,0},{2,3},{3,2},{4,5},{5,4},{6,7},{7,6},{8,9},{9,8},{10,11... | collective-permute-start | bytes 786440 | tf_op jit(solution)/shard_map/ppermute | solution.py:215
  33.6 4.4 %collective-permute-start.7 = (bf16[8,8,1920]{2,1,0:T(8,128)(2,1)S(1)}, bf16[8,8,1920]{2,1,0:T(8,128)(2,1)S(1)}, u32[]{:S(2)}, u32[]{:S(2)}) collective-permute-start(bf16[8,8,1920]{2,1,0:T(8,128)(2,1)S(1)} %constant_dynamic-update-slice_fusion.2.own_ref), channel_id=1, source_target_pairs={{0,1},{1,0},{2,3},{3,2},{4,5},{5,4},{6,7},{7,6},{8,9},{9,8},{10,11... | collective-permute-start | bytes 737288 | tf_op jit(solution)/shard_map/ppermute | solution.py:215
  34.2 10.6 %all-to-all-start.1 = ((f32[16,8,128]{2,1,0:T(8,128)}), f32[16,8,128]{2,1,0:T(8,128)S(1)}, u32[]{:S(2)}, u32[]{:S(2)}) async-start(f32[16,8,128]{2,1,0:T(8,128)} %get-tuple-element.29), calls=%async_computation.1 | async-start | bytes 131072 | tf_op jit(solution)/shard_map/all_to_all | solution.py:325

commit v18 on v17

--- a/solution.py
+++ b/solution.py
@@ -59,11 +59,10 @@
     return parts
 
 
-def map_rest_kernel(w_ref, t_ref, p_ref, stats_ref, o_ref, s_ref, m_ref, o_buf, out_sem):
+def map_rest_kernel(mine, place_ref, w_ref, t_ref, p_ref, stats_ref, *refs):
+    o_refs, (s_ref, m_ref) = refs[:-2], refs[-2:]
     tokens = t_ref.shape[0]
-    owners = o_ref.shape[0]
     rows = w_ref.shape[0] - MASS_ROWS
-    mine = rows // owners
     stats = [stats_ref[0:1, :]] + three_parts(stats_ref[1:2, :])
     extra = jnp.zeros((tokens, stats_ref.shape[1]), jnp.float32)
     row_ids = lax.broadcasted_iota(jnp.int32, extra.shape, 0)
@@ -82,27 +81,26 @@
         mass = mass + m_ref[(rows + slot) * tokens : (rows + slot + 1) * tokens, :]
     inverse = jnp.broadcast_to(1.0 / jnp.sum(mass, axis=1, keepdims=True), (tokens, BLK))
 
-    def leaving(q):
-        return pltpu.make_async_copy(o_buf.at[q], o_ref.at[q], out_sem.at[q])
-
-    def owner(q, carry):
+    for offset, o_ref in enumerate(o_refs):
+        owner = place_ref[0] ^ offset
         for b in range(mine):
-            first = pl.multiple_of((q * mine + b) * tokens, tokens)
+            first = pl.multiple_of((owner * mine + b) * tokens, tokens)
             tile = m_ref[pl.ds(first, tokens), :] * inverse
-            o_buf[q, :, b * BLK : (b + 1) * BLK] = tile.astype(jnp.bfloat16)
-        o_buf[q, :, mine * BLK :] = extra
-        leaving(q).start()
-        return carry
-
-    def left(q, carry):
-        leaving(q).wait()
-        return carry
-
-    lax.fori_loop(0, owners, owner, 0)
-    lax.fori_loop(0, owners, left, 0)
-
-
-def grad_kernel(scale, target_ref, logits_ref, grad_ref, terms_ref, norm_ref, t_buf, sem):
+            o_ref[:, b * BLK : (b + 1) * BLK] = tile.astype(jnp.bfloat16)
+        o_ref[:, mine * BLK :] = extra
+
+
+def leaving_order(owners):
+    near = list(range(1, owners // 2))
+    return [*range(owners // 2, owners), *near[1:], *near[:1]]
+
+
+def grad_kernel(scale, place_ref, logits_ref, *refs):
+    own_ref, target_refs = refs[0], refs[1:-6]
+    grad_ref, terms_ref, target_ref, norm_ref, t_buf, sem = refs[-6:]
+    target_ref[place_ref[0]] = own_ref[...]
+    for offset, ref in zip(leaving_order(target_ref.shape[0]), target_refs):
+        target_ref[place_ref[0] ^ offset] = ref[...]
     owners, tokens, _ = target_ref.shape
     group_tokens, width = logits_ref.shape
     stats = [target_ref[q, :, width:].astype(jnp.float32) for q in range(owners)]
@@ -275,26 +273,21 @@
         cost_estimate=cost(flops, 3 << 20),
         name="map_own",
     )(w_own, teacher_probs, stats)
-    chunk = (owners, tokens, width + group_tokens)
+    chunk = (tokens, width + group_tokens)
     outgoing = pl.pallas_call(
-        map_rest_kernel,
-        out_shape=shape(chunk, bf16),
-        in_specs=[in_vmem()] * 4,
-        out_specs=anywhere(),
-        scratch_shapes=[
-            spread,
-            pltpu.VMEM(((rows + 8) * tokens, BLK), f32),
-            pltpu.VMEM(chunk, bf16),
-            dma(owners),
-        ],
+        lambda *refs: map_rest_kernel(mine, *refs),
+        out_shape=[shape(chunk, bf16)] * owners,
+        in_specs=[scalars()] + [in_vmem()] * 4,
+        out_specs=[in_vmem()] * owners,
+        scratch_shapes=[spread, pltpu.VMEM(((rows + 8) * tokens, BLK), f32)],
         compiler_params=params(),
         cost_estimate=cost(flops, 4 << 20),
         name="map_rest",
-    )(w_rest, teacher_other, part, stats)
+    )(place, w_rest, teacher_other, part, stats)
     outgoing, first_piece = lax.optimization_barrier((outgoing, first_piece))
-    target = lax.all_to_all(outgoing, "sv", 0, 0, tiled=True)
-
-    hidden, late_logits, outgoing = lax.optimization_barrier((hidden, student_logits, outgoing))
+    targets = [to_partner(outgoing[a], a) for a in leaving_order(owners)]
+
+    hidden, late_logits, _ = lax.optimization_barrier((hidden, student_logits, outgoing[0]))
 
     keep = lax.dynamic_slice_in_dim(late_logits, half_index * width, width, 1)
     give = lax.dynamic_slice_in_dim(late_logits, (1 - half_index) * width, width, 1)
@@ -308,9 +301,10 @@
     grad, terms = pl.pallas_call(
         lambda *refs: grad_kernel(scale, *refs),
         out_shape=(shape((group_tokens, width), bf16), shape((owners * halves, 8, lanes), f32)),
-        in_specs=[in_vmem()] * 2,
+        in_specs=[scalars()] + [in_vmem()] * (owners + 1),
         out_specs=(in_vmem(), anywhere()),
         scratch_shapes=[
+            pltpu.VMEM((owners, *chunk), bf16),
             pltpu.VMEM((group_tokens, BLK), f32),
             pltpu.VMEM((owners * halves, 8, lanes), f32),
             pltpu.SemaphoreType.DMA,
@@ -320,7 +314,7 @@
             10 * group_tokens * width, 6 * group_tokens * width, 2 * group_tokens * width
         ),
         name="logit_grad",
-    )(target, logits)
+    )(place, logits, outgoing[0], *targets)
 
     terms = lax.all_to_all(terms, ("sv", "tv"), 0, 0, tiled=True)
     give = lax.dynamic_slice_in_dim(grad, (1 - half_index) * half_tokens, half_tokens, 0)

time: 45.7 us -> 48.4 us (1.059)
  starting transfers between devices: 17 us -> 21.3 us
  waiting for transfers between devices: 14.1 us -> 12.1 us
    all_to_all x1 -> x0, waiting for transfers between devices: 11.8 us -> none  [body(): target = lax.all_to_all(outgoing, 'sv', 0, 0, tiled=True)]
    ppermute x4 -> x11, waiting for transfers between devices: 0.01 us -> 9.4 us  [to_partner(): lax.ppermute(x, 'sv', [(s, s ^ offset) for s in range(lax.axis_size('sv'))])]
    ppermute x4 -> x11, starting transfers between devices: 7.59 us -> 16.2 us  [to_partner(): lax.ppermute(x, 'sv', [(s, s ^ offset) for s in range(lax.axis_size('sv'))])]
    all_to_all x1 -> x0, starting transfers between devices: 4.29 us -> none  [body(): target = lax.all_to_all(outgoing, 'sv', 0, 0, tiled=True)]
    pallas_call x1, Pallas kernels: 1.21 us -> 1.81 us  [body(): pl.pallas_call(lambda *refs: grad_kernel(scale, *refs), out_shape=(shape(...]
  transfers between devices with their start and end apart: 11 -> 17, of which waited for: 2 -> 6; matrix products, arithmetic and copies ran while one was open for 3% -> 3% of each run, Pallas kernels for 21% -> 21%
where the time goes in v18:
time: 48.4 us; the launch traced here: 48.1 us
  starting transfers between devices  21.3 us (44%)
  waiting for transfers between devices  12.1 us (25%)
  Pallas kernels  10 us (21%)
  other arithmetic  3.55 us (7%)
  between operations  0.86 us (2%)
    ppermute x11, starting transfers between devices, to_partner(): lax.ppermute(x, 'sv', [(s, s ^ offset) for s in range(lax.axis_size('sv'))])  16.2 us
    ppermute x11, waiting for transfers between devices, to_partner(): lax.ppermute(x, 'sv', [(s, s ^ offset) for s in range(lax.axis_size('sv'))])  9.4 us
    pallas_call x1, Pallas kernels, body(): pl.pallas_call(weight_kernel, out_shape=(shape((features, width), bf16),...  4.48 us
    all_to_all x1, starting transfers between devices, body(): terms = lax.all_to_all(terms, ('sv', 'tv'), 0, 0, tiled=True)  3.5 us
    pallas_call x1, Pallas kernels, body(): pl.pallas_call(lambda *refs: map_rest_kernel(mine, *refs), out_shape=[sha...  2.37 us
    all_to_all x1, waiting for transfers between devices, body(): terms = lax.all_to_all(terms, ('sv', 'tv'), 0, 0, tiled=True)  2.35 us
    pallas_call x1, Pallas kernels, body(): pl.pallas_call(lambda *refs: grad_kernel(scale, *refs), out_shape=(shape(...  1.81 us
    another operation x1, other arithmetic, body(): lax.reduce((wide, jnp.ones_like(wide)), (low, jnp.float32(0)), merge, (1,))  1.68 us
  transfers between devices with their start and end apart: 17, of which 6 were waited for; matrix products, arithmetic and copies ran while one was open for 3% of the time, Pallas kernels for 21%

profile of v18, /device:TPU:0, one launch (start us, length us, event | category | flops | bytes accessed | tf_op | source)
XLA Modules:
  0.0 48.1 jit_solution(8547630578985760723)
XLA Ops:
  0.6 1.7 %convert_reduce_fusion = (f32[64]{0:T(128)S(1)}, f32[64]{0:T(128)S(1)}) fusion(bf16[64,4096]{1,0:T(8,128)(2,1)} %param.10), kind=kLoop, calls=%fused_computation | loop fusion | flops 1834624 | bytes 524800 | tf_op jit(solution)/shard_map/reduce | solution.py:253
  2.3 0.5 %collective-permute-start.1 = (f32[2,64]{1,0:T(2,128)S(1)}, f32[2,64]{1,0:T(2,128)S(1)}, u32[]{:S(2)}, u32[]{:S(2)}) collective-permute-start(f32[2,64]{1,0:T(2,128)S(1)} %pad_maximum_fusion.1), channel_id=1, source_target_pairs={{0,1},{1,0},{2,3},{3,2},{4,5},{5,4},{6,7},{7,6},{8,9},{9,8},{10,11... | collective-permute-start | bytes 1544 | tf_op jit(solution)/shard_map/ppermute | solution.py:213
  2.8 3.7 %collective-permute-start.2 = (bf16[1,8,1920]{2,1,0:T(8,128)(2,1)}, bf16[1,8,1920]{2,1,0:T(8,128)(2,1)S(1)}, u32[]{:S(2)}, u32[]{:S(2)}) collective-permute-start(bf16[1,8,1920]{2,1,0:T(8,128)(2,1)} %bitcast.9), channel_id=1, source_target_pairs={{0,8},{2,10},{4,12},{6,14},{8,0},{10,2},{12,4},{14,6},{1,9},{3,11}... | collective-permute-start | bytes 92168 | tf_op jit(solution)/shard_map/ppermute | solution.py:217
  6.8 0.7 %fusion.5 = f32[640,2]{0,1:T(2,128)S(1)} fusion(bf16[640,2]{0,1:T(2,128)(2,1)} %param.9, s32[640,2]{0,1:T(2,128)} %param.7, s32[640,2]{0,1:T(2,128)} %param.8, s32[]{:T(128)S(6)} %mul.51), kind=kLoop, calls=%fused_computation.23 | loop fusion | flops 14080 | bytes 17924 | tf_op jit(solution)/shard_map/add | solution.py:260
  8.0 1.4 %map_own.1.refs_3_ = f32[144,2048]{1,0:T(8,128)S(1)} custom-call(bf16[144,320]{1,0:T(8,128)(2,1)S(1)} %get-tuple-element.87.w_ref, bf16[16,40960]{1,0:T(8,128)(2,1)S(1)} %copy-done, f32[2,128]{1,0:T(2,128)S(1)} %pad_maximum_fusion.2.stats_ref.refs_4_), custom_call_target="tpu_custom_call" | custom-call | flops 188743680 | bytes 3145728 | tf_op jit(solution)/shard_map/map_own/pallas_call | solution.py:266
  9.4 0.4 collective-permute-done.refs_2_
  9.8 2.4 %map_rest.1 = (bf16[16,2176]{1,0:T(8,128)(2,1)S(1)}, bf16[16,2176]{1,0:T(8,128)(2,1)S(1)}, bf16[16,2176]{1,0:T(8,128)(2,1)S(1)}, bf16[16,2176]{1,0:T(8,128)(2,1)...) custom-call(s32[2]{0:T(128)S(1)} %pad_add_fusion.refs_0_.place_ref, ...), custom_call_target="tpu_custom_call" | custom-call | flops 188743680 | bytes 4194304 | tf_op jit(solution)/shard_map/map_rest/pallas_call | solution.py:277
  12.4 0.3 collective-permute-start.4
  12.7 3.6 %collective-permute-start.5 = (bf16[16,2176]{1,0:T(8,128)(2,1)S(1)}, bf16[16,2176]{1,0:T(8,128)(2,1)S(1)}, u32[]{:S(2)}, u32[]{:S(2)}) collective-permute-start(bf16[16,2176]{1,0:T(8,128)(2,1)S(1)} %get-tuple-element.53), channel_id=1, source_target_pairs={{0,10},{2,8},{4,14},{6,12},{8,2},{10,0},{12,6},{14,4},{1,11},{3,9}... | collective-permute-start | bytes 208904 | tf_op jit(solution)/shard_map/ppermute | solution.py:217
  16.3 1.3 %collective-permute-start.6 = (bf16[16,2176]{1,0:T(8,128)(2,1)S(1)}, bf16[16,2176]{1,0:T(8,128)(2,1)S(1)}, u32[]{:S(2)}, u32[]{:S(2)}) collective-permute-start(bf16[16,2176]{1,0:T(8,128)(2,1)S(1)} %get-tuple-element.54), channel_id=1, source_target_pairs={{0,12},{2,14},{4,8},{6,10},{8,4},{10,6},{12,0},{14,2},{1,13},{3,15... | collective-permute-start | bytes 208904 | tf_op jit(solution)/shard_map/ppermute | solution.py:217
  17.7 2.4 %collective-permute-start.7 = (bf16[16,2176]{1,0:T(8,128)(2,1)S(1)}, bf16[16,2176]{1,0:T(8,128)(2,1)S(1)}, u32[]{:S(2)}, u32[]{:S(2)}) collective-permute-start(bf16[16,2176]{1,0:T(8,128)(2,1)S(1)} %get-tuple-element.55), channel_id=1, source_target_pairs={{0,14},{2,12},{4,10},{6,8},{8,6},{10,4},{12,2},{14,0},{1,15},{3,13... | collective-permute-start | bytes 208904 | tf_op jit(solution)/shard_map/ppermute | solution.py:217
  20.3 3.6 %collective-permute-done.4.refs_3_ = bf16[16,2176]{1,0:T(8,128)(2,1)S(1)} collective-permute-done((bf16[16,2176]{1,0:T(8,128)(2,1)S(1)}, bf16[16,2176]{1,0:T(8,128)(2,1)S(1)}, u32[]{:S(2)}, u32[]{:S(2)}) %collective-permute-start.4) | collective-permute-done | bytes 69664 | tf_op jit(solution)/shard_map/ppermute | solution.py:217
  23.9 2.9 %collective-permute-done.5.refs_4_ = bf16[16,2176]{1,0:T(8,128)(2,1)S(1)} collective-permute-done((bf16[16,2176]{1,0:T(8,128)(2,1)S(1)}, bf16[16,2176]{1,0:T(8,128)(2,1)S(1)}, u32[]{:S(2)}, u32[]{:S(2)}) %collective-permute-start.5) | collective-permute-done | bytes 69664 | tf_op jit(solution)/shard_map/ppermute | solution.py:217
  26.8 0.6 %collective-permute-start.12 = (bf16[2,8,1920]{2,1,0:T(8,128)(2,1)S(1)}, bf16[2,8,1920]{2,1,0:T(8,128)(2,1)S(1)}, u32[]{:S(2)}, u32[]{:S(2)}) collective-permute-start(bf16[2,8,1920]{2,1,0:T(8,128)(2,1)S(1)} %constant_dynamic-update-slice_fusion), channel_id=1, source_target_pairs={{0,4},{2,6},{4,0},{6,2},{8,12},{10,14},{12,8},{14,10},{1,5},{3,7},... | collective-permute-start | bytes 184328 | tf_op jit(solution)/shard_map/ppermute | solution.py:217
  27.4 2.9 %collective-permute-start.9 = (bf16[16,2176]{1,0:T(8,128)(2,1)S(1)}, bf16[16,2176]{1,0:T(8,128)(2,1)S(1)}, u32[]{:S(2)}, u32[]{:S(2)}) collective-permute-start(bf16[16,2176]{1,0:T(8,128)(2,1)S(1)} %get-tuple-element.57), channel_id=1, source_target_pairs={{0,6},{2,4},{4,2},{6,0},{8,14},{10,12},{12,10},{14,8},{1,7},{3,5},... | collective-permute-start | bytes 208904 | tf_op jit(solution)/shard_map/ppermute | solution.py:217
  30.3 1.4 %collective-permute-start.10 = (bf16[16,2176]{1,0:T(8,128)(2,1)S(1)}, bf16[16,2176]{1,0:T(8,128)(2,1)S(1)}, u32[]{:S(2)}, u32[]{:S(2)}) collective-permute-start(bf16[16,2176]{1,0:T(8,128)(2,1)S(1)} %get-tuple-element.58), channel_id=1, source_target_pairs={{0,2},{2,0},{4,6},{6,4},{8,10},{10,8},{12,14},{14,12},{1,3},{3,1},... | collective-permute-start | bytes 208904 | tf_op jit(solution)/shard_map/ppermute | solution.py:217
  31.7 1.0 %collective-permute-done.9.refs_8_ = bf16[16,2176]{1,0:T(8,128)(2,1)S(1)} collective-permute-done((bf16[16,2176]{1,0:T(8,128)(2,1)S(1)}, bf16[16,2176]{1,0:T(8,128)(2,1)S(1)}, u32[]{:S(2)}, u32[]{:S(2)}) %collective-permute-start.9) | collective-permute-done | bytes 69664 | tf_op jit(solution)/shard_map/ppermute | solution.py:217
  32.7 1.9 %collective-permute-done.10.refs_9_ = bf16[16,2176]{1,0:T(8,128)(2,1)S(1)} collective-permute-done((bf16[16,2176]{1,0:T(8,128)(2,1)S(1)}, bf16[16,2176]{1,0:T(8,128)(2,1)S(1)}, u32[]{:S(2)}, u32[]{:S(2)}) %collective-permute-start.10) | collective-permute-done | bytes 69664 | tf_op jit(solution)/shard_map/ppermute | solution.py:217
  34.6 1.8 %logit_grad.1 = (bf16[128,2048]{1,0:T(8,128)(2,1)S(1)}, f32[16,8,128]{2,1,0:T(8,128)}) custom-call(s32[2]{0:T(128)S(1)} %pad_add_fusion.refs_0_.place_ref, bf16[128,2048]{1,0:T(8,128)(2,1)S(1)} %pad_maximum_fusion.refs_1_, bf16[16,2176]{1,0:T(8,128)(2,1)S(1)} %get-tuple-element.50.refs_2_, bf16[16,2176]{1,0:T(8,128)(2,1)S(1)} %collective-permute-done.4.refs_3_, ...), custom_call_target="tpu_custom_call" | custom-call | flops 2621440 | bytes 1572864 | tf_op jit(solution)/shard_map/logit_grad/pallas_call | solution.py:301
  36.6 0.5 %collective-permute-start.14 = (bf16[8,8,1920]{2,1,0:T(8,128)(2,1)S(1)}, bf16[8,8,1920]{2,1,0:T(8,128)(2,1)S(1)}, u32[]{:S(2)}, u32[]{:S(2)}) collective-permute-start(bf16[8,8,1920]{2,1,0:T(8,128)(2,1)S(1)} %constant_dynamic-update-slice_fusion.2.own_ref), channel_id=1, source_target_pairs={{0,1},{1,0},{2,3},{3,2},{4,5},{5,4},{6,7},{7,6},{8,9},{9,8},{10,11... | collective-permute-start | bytes 737288 | tf_op jit(solution)/shard_map/ppermute | solution.py:213
  37.2 3.5 %all-to-all-start = ((f32[16,8,128]{2,1,0:T(8,128)}), f32[16,8,128]{2,1,0:T(8,128)S(1)}, u32[]{:S(2)}, u32[]{:S(2)}) async-start(f32[16,8,128]{2,1,0:T(8,128)} %get-tuple-element.59), calls=%async_computation | async-start | bytes 131072 | tf_op jit(solution)/shard_map/all_to_all | solution.py:319
  40.7 4.5 %weight_grad.1 = (bf16[1920,2048]{1,0:T(8,128)(2,1)}, bf16[64,4096]{1,0:T(8,128)(2,1)}) custom-call(s32[2]{0:T(128)S(1)} %pad_add_fusion.refs_0_.place_ref, bf16[8,8,1920]{2,1,0:T(8,128)(2,1)S(1)} %constant_dynamic-update-slice_fusion.2.own_ref, bf16[8,8,1920]{2,1,0:T(8,128)(2,1)S(1)} %collective-permute-done.14.other_ref, ...), custom_call_target="tpu_custom_call" | custom-call | flops 1006632960 | bytes 8880128 | tf_op jit(solution)/shard_map/weight_grad/pallas_call | solution.py:326
  45.2 2.4 %all-to-all-done = f32[16,8,128]{2,1,0:T(8,128)S(1)} async-done(((f32[16,8,128]{2,1,0:T(8,128)}), f32[16,8,128]{2,1,0:T(8,128)S(1)}, u32[]{:S(2)}, u32[]{:S(2)}) %all-to-all-start) | async-done | bytes 65568 | tf_op jit(solution)/shard_map/all_to_all | solution.py:319
  47.5 0.5 %slice_reduce_fusion = f32[64]{0:T(128)} fusion(f32[16,8,128]{2,1,0:T(8,128)S(1)} %all-to-all-done), kind=kLoop, calls=%fused_computation.21 | loop fusion | flops 960 | bytes 4352 | tf_op jit(solution)/shard_map/reduce_sum | solution.py:346
  (42 shorter events, 1.4 us)
Async XLA Ops:
  0.6 7.3 %copy-start = (bf16[16,40960]{1,0:T(8,128)(2,1)S(1)}, bf16[16,40960]{1,0:T(8,128)(2,1)}, u32[]{:S(2)}) copy-start(bf16[16,40960]{1,0:T(8,128)(2,1)} %t_ref.1) | copy-start | bytes 3932164
  2.3 5.5 %collective-permute-start.1 = (f32[2,64]{1,0:T(2,128)S(1)}, f32[2,64]{1,0:T(2,128)S(1)}, u32[]{:S(2)}, u32[]{:S(2)}) collective-permute-start(f32[2,64]{1,0:T(2,128)S(1)} %pad_maximum_fusion.1), channel_id=1, source_target_pairs={{0,1},{1,0},{2,3},{3,2},{4,5},{5,4},{6,7},{7,6},{8,9},{9,8},{10,11... | collective-permute-start | bytes 1544 | tf_op jit(solution)/shard_map/ppermute | solution.py:213
  2.8 9.3 %collective-permute-start.2 = (bf16[1,8,1920]{2,1,0:T(8,128)(2,1)}, bf16[1,8,1920]{2,1,0:T(8,128)(2,1)S(1)}, u32[]{:S(2)}, u32[]{:S(2)}) collective-permute-start(bf16[1,8,1920]{2,1,0:T(8,128)(2,1)} %bitcast.9), channel_id=1, source_target_pairs={{0,8},{2,10},{4,12},{6,14},{8,0},{10,2},{12,4},{14,6},{1,9},{3,11}... | collective-permute-start | bytes 92168 | tf_op jit(solution)/shard_map/ppermute | solution.py:217
  6.5 3.2 %collective-permute-start = (bf16[16,40960]{1,0:T(8,128)(2,1)}, bf16[16,40960]{1,0:T(8,128)(2,1)S(1)}, u32[]{:S(2)}, u32[]{:S(2)}) collective-permute-start(bf16[16,40960]{1,0:T(8,128)(2,1)} %t_ref.1), channel_id=1, source_target_pairs={{0,1},{1,0},{2,3},{3,2},{4,5},{5,4},{6,7},{7,6},{8,9},{9,8},{10,11... | collective-permute-start | bytes 3932168 | tf_op jit(solution)/shard_map/ppermute | solution.py:213
  9.4 2.8 %copy-start.1 = (bf16[64,4096]{1,0:T(8,128)(2,1)S(1)}, bf16[64,4096]{1,0:T(8,128)(2,1)}, u32[]{:S(2)}) copy-start(bf16[64,4096]{1,0:T(8,128)(2,1)} %param.10) | copy-start | bytes 1572868
  9.8 2.7 %copy-start.2 = (bf16[8,1920]{1,0:T(8,128)(2,1)S(1)}, bf16[8,1920]{1,0:T(8,128)(2,1)}, u32[]{:S(2)}) copy-start(bf16[8,1920]{1,0:T(8,128)(2,1)} %param.11) | copy-start | bytes 92164
  12.2 7.9 %collective-permute-start.3 = (bf16[64,2048]{1,0:T(8,128)(2,1)S(1)}, bf16[64,2048]{1,0:T(8,128)(2,1)S(1)}, u32[]{:S(2)}, u32[]{:S(2)}) collective-permute-start(bf16[64,2048]{1,0:T(8,128)(2,1)S(1)} %constant_dynamic-slice_fusion.1), channel_id=1, source_target_pairs={{0,1},{1,0},{2,3},{3,2},{4,5},{5,4},{6,7},{7,6},{8,9},{9,8},{10,11... | collective-permute-start | bytes 786440 | tf_op jit(solution)/shard_map/ppermute | solution.py:213
  12.4 11.4 %collective-permute-start.4 = (bf16[16,2176]{1,0:T(8,128)(2,1)S(1)}, bf16[16,2176]{1,0:T(8,128)(2,1)S(1)}, u32[]{:S(2)}, u32[]{:S(2)}) collective-permute-start(bf16[16,2176]{1,0:T(8,128)(2,1)S(1)} %get-tuple-element.52), channel_id=1, source_target_pairs={{0,8},{2,10},{4,12},{6,14},{8,0},{10,2},{12,4},{14,6},{1,9},{3,11}... | collective-permute-start | bytes 208904 | tf_op jit(solution)/shard_map/ppermute | solution.py:217
  12.7 14.1 %collective-permute-start.5 = (bf16[16,2176]{1,0:T(8,128)(2,1)S(1)}, bf16[16,2176]{1,0:T(8,128)(2,1)S(1)}, u32[]{:S(2)}, u32[]{:S(2)}) collective-permute-start(bf16[16,2176]{1,0:T(8,128)(2,1)S(1)} %get-tuple-element.53), channel_id=1, source_target_pairs={{0,10},{2,8},{4,14},{6,12},{8,2},{10,0},{12,6},{14,4},{1,11},{3,9}... | collective-permute-start | bytes 208904 | tf_op jit(solution)/shard_map/ppermute | solution.py:217
  16.3 11.1 %collective-permute-start.6 = (bf16[16,2176]{1,0:T(8,128)(2,1)S(1)}, bf16[16,2176]{1,0:T(8,128)(2,1)S(1)}, u32[]{:S(2)}, u32[]{:S(2)}) collective-permute-start(bf16[16,2176]{1,0:T(8,128)(2,1)S(1)} %get-tuple-element.54), channel_id=1, source_target_pairs={{0,12},{2,14},{4,8},{6,10},{8,4},{10,6},{12,0},{14,2},{1,13},{3,15... | collective-permute-start | bytes 208904 | tf_op jit(solution)/shard_map/ppermute | solution.py:217
  17.7 9.7 %collective-permute-start.7 = (bf16[16,2176]{1,0:T(8,128)(2,1)S(1)}, bf16[16,2176]{1,0:T(8,128)(2,1)S(1)}, u32[]{:S(2)}, u32[]{:S(2)}) collective-permute-start(bf16[16,2176]{1,0:T(8,128)(2,1)S(1)} %get-tuple-element.55), channel_id=1, source_target_pairs={{0,14},{2,12},{4,10},{6,8},{8,6},{10,4},{12,2},{14,0},{1,15},{3,13... | collective-permute-start | bytes 208904 | tf_op jit(solution)/shard_map/ppermute | solution.py:217
  20.1 10.2 %collective-permute-start.8 = (bf16[16,2176]{1,0:T(8,128)(2,1)S(1)}, bf16[16,2176]{1,0:T(8,128)(2,1)S(1)}, u32[]{:S(2)}, u32[]{:S(2)}) collective-permute-start(bf16[16,2176]{1,0:T(8,128)(2,1)S(1)} %get-tuple-element.56), channel_id=1, source_target_pairs={{0,4},{2,6},{4,0},{6,2},{8,12},{10,14},{12,8},{14,10},{1,5},{3,7},... | collective-permute-start | bytes 208904 | tf_op jit(solution)/shard_map/ppermute | solution.py:217
  23.9 12.5 %collective-permute-start.13 = (bf16[2,8,1920]{2,1,0:T(8,128)(2,1)S(1)}, bf16[2,8,1920]{2,1,0:T(8,128)(2,1)S(1)}, u32[]{:S(2)}, u32[]{:S(2)}) collective-permute-start(bf16[2,8,1920]{2,1,0:T(8,128)(2,1)S(1)} %constant_dynamic-update-slice_fusion), channel_id=1, source_target_pairs={{0,6},{2,4},{4,2},{6,0},{8,14},{10,12},{12,10},{14,8},{1,7},{3,5},... | collective-permute-start | bytes 184328 | tf_op jit(solution)/shard_map/ppermute | solution.py:217
  26.8 9.6 %collective-permute-start.12 = (bf16[2,8,1920]{2,1,0:T(8,128)(2,1)S(1)}, bf16[2,8,1920]{2,1,0:T(8,128)(2,1)S(1)}, u32[]{:S(2)}, u32[]{:S(2)}) collective-permute-start(bf16[2,8,1920]{2,1,0:T(8,128)(2,1)S(1)} %constant_dynamic-update-slice_fusion), channel_id=1, source_target_pairs={{0,4},{2,6},{4,0},{6,2},{8,12},{10,14},{12,8},{14,10},{1,5},{3,7},... | collective-permute-start | bytes 184328 | tf_op jit(solution)/shard_map/ppermute | solution.py:217
  27.4 9.1 %collective-permute-start.11 = (bf16[2,8,1920]{2,1,0:T(8,128)(2,1)S(1)}, bf16[2,8,1920]{2,1,0:T(8,128)(2,1)S(1)}, u32[]{:S(2)}, u32[]{:S(2)}) collective-permute-start(bf16[2,8,1920]{2,1,0:T(8,128)(2,1)S(1)} %constant_dynamic-update-slice_fusion), channel_id=1, source_target_pairs={{0,2},{2,0},{4,6},{6,4},{8,10},{10,8},{12,14},{14,12},{1,3},{3,1},... | collective-permute-start | bytes 184328 | tf_op jit(solution)/shard_map/ppermute | solution.py:217
  27.4 5.3 %collective-permute-start.9 = (bf16[16,2176]{1,0:T(8,128)(2,1)S(1)}, bf16[16,2176]{1,0:T(8,128)(2,1)S(1)}, u32[]{:S(2)}, u32[]{:S(2)}) collective-permute-start(bf16[16,2176]{1,0:T(8,128)(2,1)S(1)} %get-tuple-element.57), channel_id=1, source_target_pairs={{0,6},{2,4},{4,2},{6,0},{8,14},{10,12},{12,10},{14,8},{1,7},{3,5},... | collective-permute-start | bytes 208904 | tf_op jit(solution)/shard_map/ppermute | solution.py:217
  30.3 4.3 %collective-permute-start.10 = (bf16[16,2176]{1,0:T(8,128)(2,1)S(1)}, bf16[16,2176]{1,0:T(8,128)(2,1)S(1)}, u32[]{:S(2)}, u32[]{:S(2)}) collective-permute-start(bf16[16,2176]{1,0:T(8,128)(2,1)S(1)} %get-tuple-element.58), channel_id=1, source_target_pairs={{0,2},{2,0},{4,6},{6,4},{8,10},{10,8},{12,14},{14,12},{1,3},{3,1},... | collective-permute-start | bytes 208904 | tf_op jit(solution)/shard_map/ppermute | solution.py:217
  36.5 4.2 %collective-permute-start.15 = (bf16[64,2048]{1,0:T(8,128)(2,1)S(1)}, bf16[64,2048]{1,0:T(8,128)(2,1)S(1)}, u32[]{:S(2)}, u32[]{:S(2)}) collective-permute-start(bf16[64,2048]{1,0:T(8,128)(2,1)S(1)} %constant_dynamic-slice_fusion), channel_id=1, source_target_pairs={{0,1},{1,0},{2,3},{3,2},{4,5},{5,4},{6,7},{7,6},{8,9},{9,8},{10,11... | collective-permute-start | bytes 786440 | tf_op jit(solution)/shard_map/ppermute | solution.py:213
  36.6 4.1 %collective-permute-start.14 = (bf16[8,8,1920]{2,1,0:T(8,128)(2,1)S(1)}, bf16[8,8,1920]{2,1,0:T(8,128)(2,1)S(1)}, u32[]{:S(2)}, u32[]{:S(2)}) collective-permute-start(bf16[8,8,1920]{2,1,0:T(8,128)(2,1)S(1)} %constant_dynamic-update-slice_fusion.2.own_ref), channel_id=1, source_target_pairs={{0,1},{1,0},{2,3},{3,2},{4,5},{5,4},{6,7},{7,6},{8,9},{9,8},{10,11... | collective-permute-start | bytes 737288 | tf_op jit(solution)/shard_map/ppermute | solution.py:213
  37.2 10.4 %all-to-all-start = ((f32[16,8,128]{2,1,0:T(8,128)}), f32[16,8,128]{2,1,0:T(8,128)S(1)}, u32[]{:S(2)}, u32[]{:S(2)}) async-start(f32[16,8,128]{2,1,0:T(8,128)} %get-tuple-element.59), calls=%async_computation | async-start | bytes 131072 | tf_op jit(solution)/shard_map/all_to_all | solution.py:319

commit v19 on v18

--- a/solution.py
+++ b/solution.py
@@ -95,15 +95,25 @@
     return [*range(owners // 2, owners), *near[1:], *near[:1]]
 
 
+def arrange_kernel(tokens, place_ref, keep_ref, got_ref, o_ref):
+    count = keep_ref.shape[0] // tokens
+    owner, half = place_ref[0], place_ref[1]
+    for a in range(o_ref.shape[0] // tokens):
+        rows = pl.ds(pl.multiple_of(((owner ^ a) % count) * tokens, tokens), tokens)
+        kept = (owner ^ a) // count == half
+        o_ref[a * tokens : (a + 1) * tokens, :] = jnp.where(kept, keep_ref[rows, :], got_ref[rows, :])
+
+
 def grad_kernel(scale, place_ref, logits_ref, *refs):
-    own_ref, target_refs = refs[0], refs[1:-6]
-    grad_ref, terms_ref, target_ref, norm_ref, t_buf, sem = refs[-6:]
-    target_ref[place_ref[0]] = own_ref[...]
-    for offset, ref in zip(leaving_order(target_ref.shape[0]), target_refs):
-        target_ref[place_ref[0] ^ offset] = ref[...]
-    owners, tokens, _ = target_ref.shape
+    own_ref, far_refs = refs[0], refs[1:-6]
+    grad_ref, terms_ref, norm_ref, sum_ref, t_buf, sem = refs[-6:]
+    owners = len(far_refs) + 1
+    tokens = own_ref.shape[0]
     group_tokens, width = logits_ref.shape
-    stats = [target_ref[q, :, width:].astype(jnp.float32) for q in range(owners)]
+    target_refs = [own_ref] + [None] * (owners - 1)
+    for offset, ref in zip(leaving_order(owners), far_refs):
+        target_refs[offset] = ref
+    stats = [ref[:, width:].astype(jnp.float32) for ref in target_refs]
     top = stats[0][0:1]
     for one in stats[1:]:
         top = jnp.maximum(top, one[0:1])
@@ -111,26 +121,31 @@
     for one in stats:
         total = total + (one[1:2] + one[2:3] + one[3:4]) * jnp.exp(one[0:1] - top)
     log_norm = top + jnp.log(total)
+    for i in range(0, group_tokens, BLK):
+        sum_ref[i : i + BLK, :] = jnp.broadcast_to(log_norm[:, i : i + BLK], (BLK, BLK)).T
+    at = [pl.ds(pl.multiple_of((place_ref[0] ^ a) * tokens, tokens), tokens) for a in range(owners)]
+    for a in range(owners):
+        norm_ref[a * tokens : (a + 1) * tokens, :] = sum_ref[at[a], :]
+    per = BLK // tokens
 
     def block(i, b):
         lanes = slice(b * BLK, (b + 1) * BLK)
-        group = slice(i * BLK // tokens, (i + 1) * BLK // tokens)
-        target = target_ref[group, :, lanes].reshape(BLK, BLK).astype(jnp.float32)
-        return target, logits_ref[i * BLK : (i + 1) * BLK, lanes].astype(jnp.float32)
-
-    sums = []
+        parts = [target_refs[a][:, lanes].astype(jnp.float32) for a in range(i * per, (i + 1) * per)]
+        logits = logits_ref[i * BLK : (i + 1) * BLK, lanes].astype(jnp.float32)
+        return jnp.concatenate(parts, axis=0), logits - norm_ref[i * BLK : (i + 1) * BLK, :]
+
     for i in range(group_tokens // BLK):
-        rows = slice(i * BLK, (i + 1) * BLK)
-        norm = jnp.broadcast_to(log_norm[:, rows], (BLK, BLK)).T
-        norm_ref[rows, :] = norm
         terms = jnp.zeros((BLK, BLK), jnp.float32)
         for b in range(width // BLK):
-            target, logits = block(i, b)
+            target, log_probs = block(i, b)
             positive = target > 0
-            one = target * (jnp.log(jnp.where(positive, target, 1.0)) - (logits - norm))
+            one = target * (jnp.log(jnp.where(positive, target, 1.0)) - log_probs)
             terms = terms + jnp.where(positive, one, 0.0)
-        sums.append(jnp.sum(terms.T, axis=0, keepdims=True))
-    row = jnp.concatenate(sums, axis=1)
+        for j in range(per):
+            sum_ref[at[i * per + j], :] = terms[j * tokens : (j + 1) * tokens]
+    row = jnp.concatenate(
+        [jnp.sum(sum_ref[i : i + BLK, :].T, axis=0, keepdims=True) for i in range(0, group_tokens, BLK)], axis=1
+    )
     half_tokens = group_tokens // 2
     for half in range(2):
         mine = row[:, half * half_tokens : (half + 1) * half_tokens]
@@ -140,11 +155,10 @@
     leaving = pltpu.make_async_copy(t_buf, terms_ref, sem)
     leaving.start()
     for i in range(group_tokens // BLK):
-        rows = slice(i * BLK, (i + 1) * BLK)
         for b in range(width // BLK):
-            target, logits = block(i, b)
-            grad = (jnp.exp(logits - norm_ref[rows, :]) - target) * scale
-            grad_ref[rows, b * BLK : (b + 1) * BLK] = grad.astype(jnp.bfloat16)
+            target, log_probs = block(i, b)
+            grad = (jnp.exp(log_probs) - target) * scale
+            grad_ref[i * BLK : (i + 1) * BLK, b * BLK : (b + 1) * BLK] = grad.astype(jnp.bfloat16)
     leaving.wait()
 
 
@@ -156,21 +170,25 @@
     place_ref, own_ref, other_ref, grad_ref, got_ref, o_ref, joined_ref, s_ref, h_ref, block_ref, sems, join_sems
 ):
     half_tokens, width = got_ref.shape
-    half = place_ref[1]
+    count = join_sems.shape[0] // 2
+    tokens = half_tokens // count
+    owner, half = place_ref[0], place_ref[1]
     kept_at = pl.ds(pl.multiple_of(half * width, width), width)
     got_at = pl.ds(pl.multiple_of((1 - half) * width, width), width)
-    kept = pl.ds(pl.multiple_of(half * half_tokens, half_tokens), half_tokens)
-    copies = [
-        pltpu.make_async_copy(grad_ref.at[kept, :], joined_ref.at[:, kept_at], join_sems.at[0]),
-        pltpu.make_async_copy(got_ref, joined_ref.at[:, got_at], join_sems.at[1]),
-    ]
+    kept = ((owner // count) ^ half) * half_tokens
+    copies = []
+    for j in range(count):
+        to = pl.ds(pl.multiple_of(((owner % count) ^ j) * tokens, tokens), tokens)
+        here = pl.ds(pl.multiple_of(kept + j * tokens, tokens), tokens)
+        there = pl.ds(j * tokens, tokens)
+        copies.append(pltpu.make_async_copy(grad_ref.at[here, :], joined_ref.at[to, kept_at], join_sems.at[2 * j]))
+        copies.append(pltpu.make_async_copy(got_ref.at[there, :], joined_ref.at[to, got_at], join_sems.at[2 * j + 1]))
     for copy in copies:
         copy.start()
     owners, held, features = own_ref.shape
     for i, offset in enumerate(arrival_order(owners)):
-        first = (place_ref[0] ^ offset) * 2
-        own = pl.ds(pl.multiple_of((first + half) * held, held), held)
-        other = pl.ds(pl.multiple_of((first + 1 - half) * held, held), held)
+        own = pl.ds(pl.multiple_of((2 * offset + half) * held, held), held)
+        other = pl.ds(pl.multiple_of((2 * offset + 1 - half) * held, held), held)
         s_ref[own, :] = own_ref[i].astype(jnp.float32)
         s_ref[other, :] = other_ref[i].astype(jnp.float32)
     for i in range(s_ref.shape[0] // BLK):
@@ -287,11 +305,20 @@
     outgoing, first_piece = lax.optimization_barrier((outgoing, first_piece))
     targets = [to_partner(outgoing[a], a) for a in leaving_order(owners)]
 
-    hidden, late_logits, _ = lax.optimization_barrier((hidden, student_logits, outgoing[0]))
+    late_logits, _ = lax.optimization_barrier((student_logits, outgoing[0]))
+    hidden, _ = lax.optimization_barrier((hidden, targets[owners // 2 - 1]))
 
     keep = lax.dynamic_slice_in_dim(late_logits, half_index * width, width, 1)
     give = lax.dynamic_slice_in_dim(late_logits, (1 - half_index) * width, width, 1)
-    logits = in_order(keep, swap_halves(give), 0)
+    logits = pl.pallas_call(
+        lambda *refs: arrange_kernel(tokens, *refs),
+        out_shape=shape((group_tokens, width), bf16),
+        in_specs=[scalars()] + [in_vmem()] * 2,
+        out_specs=in_vmem(),
+        compiler_params=params(),
+        cost_estimate=cost(0, 4 * group_tokens * width),
+        name="arrange",
+    )(place, keep, swap_halves(give))
 
     pieces = [jnp.concatenate([hidden, first_piece])]
     pieces += [to_partner(pieces[0], a) for a in range(1, offset)]
@@ -304,7 +331,7 @@
         in_specs=[scalars()] + [in_vmem()] * (owners + 1),
         out_specs=(in_vmem(), anywhere()),
         scratch_shapes=[
-            pltpu.VMEM((owners, *chunk), bf16),
+            pltpu.VMEM((group_tokens, BLK), f32),
             pltpu.VMEM((group_tokens, BLK), f32),
             pltpu.VMEM((owners * halves, 8, lanes), f32),
             pltpu.SemaphoreType.DMA,
@@ -317,7 +344,9 @@
     )(place, logits, outgoing[0], *targets)
 
     terms = lax.all_to_all(terms, ("sv", "tv"), 0, 0, tiled=True)
-    give = lax.dynamic_slice_in_dim(grad, (1 - half_index) * half_tokens, half_tokens, 0)
+    count = half_tokens // tokens
+    given = (lax.axis_index("sv") // count) ^ (1 - half_index)
+    give = lax.dynamic_slice_in_dim(grad, given * half_tokens, half_tokens, 0)
     got = swap_halves(give)
 
     *pieces, grad = lax.optimization_barrier((*pieces, grad))
@@ -333,7 +362,7 @@
             pltpu.VMEM((features, group_tokens), bf16),
             pltpu.VMEM((steps, features // steps, width), bf16),
             dma(steps),
-            dma(2),
+            dma(2 * count),
         ],
         compiler_params=params(),
         cost_estimate=cost(

time: 48.4 us -> 49.2 us (1.017)
  starting transfers between devices: 21.3 us -> 25.9 us
  waiting for transfers between devices: 12.1 us -> 7.85 us
  Pallas kernels: 10 us -> 10.8 us
    ppermute x11, starting transfers between devices: 16.2 us -> 21 us  [to_partner(): lax.ppermute(x, 'sv', [(s, s ^ offset) for s in range(lax.axis_size('sv'))])]
    ppermute x11, waiting for transfers between devices: 9.4 us -> 5.12 us  [to_partner(): lax.ppermute(x, 'sv', [(s, s ^ offset) for s in range(lax.axis_size('sv'))])]
    pallas_call x0 -> x1, Pallas kernels: none -> 0.61 us  [body(): pl.pallas_call(lambda *refs: arrange_kernel(tokens, *refs), out_shape=sha...]
  transfers between devices with their start and end apart: 17 -> 17, of which waited for: 6 -> 4; matrix products, arithmetic and copies ran while one was open for 3% -> 3% of each run, Pallas kernels for 21% -> 22%
where the time goes in v19:
time: 49.2 us; the launch traced here: 48.9 us
  starting transfers between devices  25.9 us (53%)
  Pallas kernels  10.8 us (22%)
  waiting for transfers between devices  7.85 us (16%)
  other arithmetic  3.4 us (7%)
  between operations  0.83 us (2%)
    ppermute x11, starting transfers between devices, to_partner(): lax.ppermute(x, 'sv', [(s, s ^ offset) for s in range(lax.axis_size('sv'))])  21 us
    ppermute x11, waiting for transfers between devices, to_partner(): lax.ppermute(x, 'sv', [(s, s ^ offset) for s in range(lax.axis_size('sv'))])  5.12 us
    pallas_call x1, Pallas kernels, body(): pl.pallas_call(weight_kernel, out_shape=(shape((features, width), bf16),...  4.53 us
    all_to_all x1, starting transfers between devices, body(): terms = lax.all_to_all(terms, ('sv', 'tv'), 0, 0, tiled=True)  3.54 us
    pallas_call x1, Pallas kernels, body(): pl.pallas_call(lambda *refs: map_rest_kernel(mine, *refs), out_shape=[sha...  2.37 us
    all_to_all x1, waiting for transfers between devices, body(): terms = lax.all_to_all(terms, ('sv', 'tv'), 0, 0, tiled=True)  2.34 us
    pallas_call x1, Pallas kernels, body(): pl.pallas_call(lambda *refs: grad_kernel(scale, *refs), out_shape=(shape(...  1.88 us
    another operation x1, other arithmetic, body(): lax.reduce((wide, jnp.ones_like(wide)), (low, jnp.float32(0)), merge, (1,))  1.68 us
  transfers between devices with their start and end apart: 17, of which 4 were waited for; matrix products, arithmetic and copies ran while one was open for 3% of the time, Pallas kernels for 22%

profile of v19, /device:TPU:0, one launch (start us, length us, event | category | flops | bytes accessed | tf_op | source)
XLA Modules:
  0.0 48.9 jit_solution(14396065753765190416)
XLA Ops:
  0.6 1.7 %convert_reduce_fusion = (f32[64]{0:T(128)S(1)}, f32[64]{0:T(128)S(1)}) fusion(bf16[64,4096]{1,0:T(8,128)(2,1)} %param.10), kind=kLoop, calls=%fused_computation | loop fusion | flops 1834624 | bytes 524800 | tf_op jit(solution)/shard_map/reduce | solution.py:271
  2.3 0.5 %collective-permute-start.1 = (f32[2,64]{1,0:T(2,128)S(1)}, f32[2,64]{1,0:T(2,128)S(1)}, u32[]{:S(2)}, u32[]{:S(2)}) collective-permute-start(f32[2,64]{1,0:T(2,128)S(1)} %pad_maximum_fusion), channel_id=1, source_target_pairs={{0,1},{1,0},{2,3},{3,2},{4,5},{5,4},{6,7},{7,6},{8,9},{9,8},{10,11... | collective-permute-start | bytes 1544 | tf_op jit(solution)/shard_map/ppermute | solution.py:231
  2.8 3.7 %collective-permute-start.2 = (bf16[1,8,1920]{2,1,0:T(8,128)(2,1)}, bf16[1,8,1920]{2,1,0:T(8,128)(2,1)S(1)}, u32[]{:S(2)}, u32[]{:S(2)}) collective-permute-start(bf16[1,8,1920]{2,1,0:T(8,128)(2,1)} %bitcast.9), channel_id=1, source_target_pairs={{0,8},{2,10},{4,12},{6,14},{8,0},{10,2},{12,4},{14,6},{1,9},{3,11}... | collective-permute-start | bytes 92168 | tf_op jit(solution)/shard_map/ppermute | solution.py:235
  6.8 0.7 %fusion.5 = f32[640,2]{0,1:T(2,128)S(1)} fusion(bf16[640,2]{0,1:T(2,128)(2,1)} %param.9, s32[640,2]{0,1:T(2,128)} %param.7, s32[640,2]{0,1:T(2,128)} %param.8, s32[]{:T(128)S(6)} %mul.51), kind=kLoop, calls=%fused_computation.20 | loop fusion | flops 14080 | bytes 17924 | tf_op jit(solution)/shard_map/add | solution.py:278
  7.6 0.2 add_convert_fusion
  8.0 1.4 %map_own.1.refs_3_ = f32[144,2048]{1,0:T(8,128)S(1)} custom-call(bf16[144,320]{1,0:T(8,128)(2,1)S(1)} %get-tuple-element.87.w_ref, bf16[16,40960]{1,0:T(8,128)(2,1)S(1)} %copy-done, f32[2,128]{1,0:T(2,128)S(1)} %pad_maximum_fusion.1.stats_ref.refs_4_), custom_call_target="tpu_custom_call" | custom-call | flops 188743680 | bytes 3145728 | tf_op jit(solution)/shard_map/map_own/pallas_call | solution.py:284
  9.4 0.4 collective-permute-done.refs_2_
  9.8 2.4 %map_rest.1 = (bf16[16,2176]{1,0:T(8,128)(2,1)S(1)}, bf16[16,2176]{1,0:T(8,128)(2,1)S(1)}, bf16[16,2176]{1,0:T(8,128)(2,1)S(1)}, bf16[16,2176]{1,0:T(8,128)(2,1)...) custom-call(s32[2]{0:T(128)S(1)} %pad_add_fusion.refs_0_.place_ref, ...), custom_call_target="tpu_custom_call" | custom-call | flops 188743680 | bytes 4194304 | tf_op jit(solution)/shard_map/map_rest/pallas_call | solution.py:295
  12.3 3.8 %collective-permute-start.5 = (bf16[16,2176]{1,0:T(8,128)(2,1)S(1)}, bf16[16,2176]{1,0:T(8,128)(2,1)S(1)}, u32[]{:S(2)}, u32[]{:S(2)}) collective-permute-start(bf16[16,2176]{1,0:T(8,128)(2,1)S(1)} %get-tuple-element.53), channel_id=1, source_target_pairs={{0,10},{2,8},{4,14},{6,12},{8,2},{10,0},{12,6},{14,4},{1,11},{3,9}... | collective-permute-start | bytes 208904 | tf_op jit(solution)/shard_map/ppermute | solution.py:235
  16.1 1.3 %collective-permute-start.6 = (bf16[16,2176]{1,0:T(8,128)(2,1)S(1)}, bf16[16,2176]{1,0:T(8,128)(2,1)S(1)}, u32[]{:S(2)}, u32[]{:S(2)}) collective-permute-start(bf16[16,2176]{1,0:T(8,128)(2,1)S(1)} %get-tuple-element.54), channel_id=1, source_target_pairs={{0,12},{2,14},{4,8},{6,10},{8,4},{10,6},{12,0},{14,2},{1,13},{3,15... | collective-permute-start | bytes 208904 | tf_op jit(solution)/shard_map/ppermute | solution.py:235
  17.4 2.4 %collective-permute-start.7 = (bf16[16,2176]{1,0:T(8,128)(2,1)S(1)}, bf16[16,2176]{1,0:T(8,128)(2,1)S(1)}, u32[]{:S(2)}, u32[]{:S(2)}) collective-permute-start(bf16[16,2176]{1,0:T(8,128)(2,1)S(1)} %get-tuple-element.55), channel_id=1, source_target_pairs={{0,14},{2,12},{4,10},{6,8},{8,6},{10,4},{12,2},{14,0},{1,15},{3,13... | collective-permute-start | bytes 208904 | tf_op jit(solution)/shard_map/ppermute | solution.py:235
  19.9 4.9 %collective-permute-done.7.refs_6_ = bf16[16,2176]{1,0:T(8,128)(2,1)S(1)} collective-permute-done((bf16[16,2176]{1,0:T(8,128)(2,1)S(1)}, bf16[16,2176]{1,0:T(8,128)(2,1)S(1)}, u32[]{:S(2)}, u32[]{:S(2)}) %collective-permute-start.7) | collective-permute-done | bytes 69664 | tf_op jit(solution)/shard_map/ppermute | solution.py:235
  24.8 4.6 %collective-permute-start.9 = (bf16[16,2176]{1,0:T(8,128)(2,1)S(1)}, bf16[16,2176]{1,0:T(8,128)(2,1)S(1)}, u32[]{:S(2)}, u32[]{:S(2)}) collective-permute-start(bf16[16,2176]{1,0:T(8,128)(2,1)S(1)} %get-tuple-element.57), channel_id=1, source_target_pairs={{0,6},{2,4},{4,2},{6,0},{8,14},{10,12},{12,10},{14,8},{1,7},{3,5},... | collective-permute-start | bytes 208904 | tf_op jit(solution)/shard_map/ppermute | solution.py:235
  29.5 1.5 %collective-permute-start.10 = (bf16[16,2176]{1,0:T(8,128)(2,1)S(1)}, bf16[16,2176]{1,0:T(8,128)(2,1)S(1)}, u32[]{:S(2)}, u32[]{:S(2)}) collective-permute-start(bf16[16,2176]{1,0:T(8,128)(2,1)S(1)} %get-tuple-element.58), channel_id=1, source_target_pairs={{0,2},{2,0},{4,6},{6,4},{8,10},{10,8},{12,14},{14,12},{1,3},{3,1},... | collective-permute-start | bytes 208904 | tf_op jit(solution)/shard_map/ppermute | solution.py:235
  31.1 1.9 %collective-permute-start.12 = (bf16[2,8,1920]{2,1,0:T(8,128)(2,1)S(1)}, bf16[2,8,1920]{2,1,0:T(8,128)(2,1)S(1)}, u32[]{:S(2)}, u32[]{:S(2)}) collective-permute-start(bf16[2,8,1920]{2,1,0:T(8,128)(2,1)S(1)} %constant_dynamic-update-slice_fusion), channel_id=1, source_target_pairs={{0,4},{2,6},{4,0},{6,2},{8,12},{10,14},{12,8},{14,10},{1,5},{3,7},... | collective-permute-start | bytes 184328 | tf_op jit(solution)/shard_map/ppermute | solution.py:235
  33.0 1.5 %collective-permute-start.11 = (bf16[2,8,1920]{2,1,0:T(8,128)(2,1)S(1)}, bf16[2,8,1920]{2,1,0:T(8,128)(2,1)S(1)}, u32[]{:S(2)}, u32[]{:S(2)}) collective-permute-start(bf16[2,8,1920]{2,1,0:T(8,128)(2,1)S(1)} %constant_dynamic-update-slice_fusion), channel_id=1, source_target_pairs={{0,2},{2,0},{4,6},{6,4},{8,10},{10,8},{12,14},{14,12},{1,3},{3,1},... | collective-permute-start | bytes 184328 | tf_op jit(solution)/shard_map/ppermute | solution.py:235
  34.5 0.6 %arrange.1.refs_1_ = bf16[128,2048]{1,0:T(8,128)(2,1)S(1)} custom-call(s32[2]{0:T(128)S(1)} %pad_add_fusion.refs_0_.place_ref, bf16[64,2048]{1,0:T(8,128)(2,1)S(1)} %get-tuple-element.82.refs_1_, bf16[64,2048]{1,0:T(8,128)(2,1)S(1)} %collective-permute-done.3.refs_2_), custom_call_target="tpu_custom_call" | custom-call | bytes 1048576 | tf_op jit(solution)/shard_map/arrange/pallas_call | solution.py:313
  35.1 1.9 %logit_grad.1 = (bf16[128,2048]{1,0:T(8,128)(2,1)S(1)}, f32[16,8,128]{2,1,0:T(8,128)}) custom-call(s32[2]{0:T(128)S(1)} %pad_add_fusion.refs_0_.place_ref, bf16[128,2048]{1,0:T(8,128)(2,1)S(1)} %arrange.1.refs_1_, bf16[16,2176]{1,0:T(8,128)(2,1)S(1)} %get-tuple-element.50.refs_2_, bf16[16,2176]{1,0:T(8,128)(2,1)S(1)} %collective-permute-done.4.refs_3_, ...), custom_call_target="tpu_custom_call" | custom-call | flops 2621440 | bytes 1572864 | tf_op jit(solution)/shard_map/logit_grad/pallas_call | solution.py:328
  37.0 0.2 collective-permute-done.11
  37.4 0.5 %collective-permute-start.14 = (bf16[8,8,1920]{2,1,0:T(8,128)(2,1)S(1)}, bf16[8,8,1920]{2,1,0:T(8,128)(2,1)S(1)}, u32[]{:S(2)}, u32[]{:S(2)}) collective-permute-start(bf16[8,8,1920]{2,1,0:T(8,128)(2,1)S(1)} %constant_dynamic-update-slice_fusion.2.own_ref), channel_id=1, source_target_pairs={{0,1},{1,0},{2,3},{3,2},{4,5},{5,4},{6,7},{7,6},{8,9},{9,8},{10,11... | collective-permute-start | bytes 737288 | tf_op jit(solution)/shard_map/ppermute | solution.py:231
  37.9 3.5 %all-to-all-start = ((f32[16,8,128]{2,1,0:T(8,128)}), f32[16,8,128]{2,1,0:T(8,128)S(1)}, u32[]{:S(2)}, u32[]{:S(2)}) async-start(f32[16,8,128]{2,1,0:T(8,128)} %get-tuple-element.59), calls=%async_computation | async-start | bytes 131072 | tf_op jit(solution)/shard_map/all_to_all | solution.py:346
  41.5 4.5 %weight_grad.1 = (bf16[1920,2048]{1,0:T(8,128)(2,1)}, bf16[64,4096]{1,0:T(8,128)(2,1)}) custom-call(s32[2]{0:T(128)S(1)} %pad_add_fusion.refs_0_.place_ref, bf16[8,8,1920]{2,1,0:T(8,128)(2,1)S(1)} %constant_dynamic-update-slice_fusion.2.own_ref, bf16[8,8,1920]{2,1,0:T(8,128)(2,1)S(1)} %collective-permute-done.14.other_ref, ...), custom_call_target="tpu_custom_call" | custom-call | flops 1006632960 | bytes 8880128 | tf_op jit(solution)/shard_map/weight_grad/pallas_call | solution.py:355
  46.1 2.3 %all-to-all-done = f32[16,8,128]{2,1,0:T(8,128)S(1)} async-done(((f32[16,8,128]{2,1,0:T(8,128)}), f32[16,8,128]{2,1,0:T(8,128)S(1)}, u32[]{:S(2)}, u32[]{:S(2)}) %all-to-all-start) | async-done | bytes 65568 | tf_op jit(solution)/shard_map/all_to_all | solution.py:346
  48.4 0.5 %slice_reduce_fusion = f32[64]{0:T(128)} fusion(f32[16,8,128]{2,1,0:T(8,128)S(1)} %all-to-all-done), kind=kLoop, calls=%fused_computation.18 | loop fusion | flops 960 | bytes 4352 | tf_op jit(solution)/shard_map/reduce_sum | solution.py:375
  (41 shorter events, 1.0 us)
Async XLA Ops:
  0.6 7.3 %copy-start = (bf16[16,40960]{1,0:T(8,128)(2,1)S(1)}, bf16[16,40960]{1,0:T(8,128)(2,1)}, u32[]{:S(2)}) copy-start(bf16[16,40960]{1,0:T(8,128)(2,1)} %t_ref.1) | copy-start | bytes 3932164
  2.3 5.5 %collective-permute-start.1 = (f32[2,64]{1,0:T(2,128)S(1)}, f32[2,64]{1,0:T(2,128)S(1)}, u32[]{:S(2)}, u32[]{:S(2)}) collective-permute-start(f32[2,64]{1,0:T(2,128)S(1)} %pad_maximum_fusion), channel_id=1, source_target_pairs={{0,1},{1,0},{2,3},{3,2},{4,5},{5,4},{6,7},{7,6},{8,9},{9,8},{10,11... | collective-permute-start | bytes 1544 | tf_op jit(solution)/shard_map/ppermute | solution.py:231
  2.8 9.3 %collective-permute-start.2 = (bf16[1,8,1920]{2,1,0:T(8,128)(2,1)}, bf16[1,8,1920]{2,1,0:T(8,128)(2,1)S(1)}, u32[]{:S(2)}, u32[]{:S(2)}) collective-permute-start(bf16[1,8,1920]{2,1,0:T(8,128)(2,1)} %bitcast.9), channel_id=1, source_target_pairs={{0,8},{2,10},{4,12},{6,14},{8,0},{10,2},{12,4},{14,6},{1,9},{3,11}... | collective-permute-start | bytes 92168 | tf_op jit(solution)/shard_map/ppermute | solution.py:235
  6.5 3.2 %collective-permute-start = (bf16[16,40960]{1,0:T(8,128)(2,1)}, bf16[16,40960]{1,0:T(8,128)(2,1)S(1)}, u32[]{:S(2)}, u32[]{:S(2)}) collective-permute-start(bf16[16,40960]{1,0:T(8,128)(2,1)} %t_ref.1), channel_id=1, source_target_pairs={{0,1},{1,0},{2,3},{3,2},{4,5},{5,4},{6,7},{7,6},{8,9},{9,8},{10,11... | collective-permute-start | bytes 3932168 | tf_op jit(solution)/shard_map/ppermute | solution.py:231
  9.4 10.5 %copy-start.1 = (bf16[64,4096]{1,0:T(8,128)(2,1)S(1)}, bf16[64,4096]{1,0:T(8,128)(2,1)}, u32[]{:S(2)}) copy-start(bf16[64,4096]{1,0:T(8,128)(2,1)} %param.10) | copy-start | bytes 1572868
  9.8 15.0 %copy-start.2 = (bf16[8,1920]{1,0:T(8,128)(2,1)S(1)}, bf16[8,1920]{1,0:T(8,128)(2,1)}, u32[]{:S(2)}) copy-start(bf16[8,1920]{1,0:T(8,128)(2,1)} %param.11) | copy-start | bytes 92164
  12.1 12.7 %collective-permute-start.4 = (bf16[16,2176]{1,0:T(8,128)(2,1)S(1)}, bf16[16,2176]{1,0:T(8,128)(2,1)S(1)}, u32[]{:S(2)}, u32[]{:S(2)}) collective-permute-start(bf16[16,2176]{1,0:T(8,128)(2,1)S(1)} %get-tuple-element.52), channel_id=1, source_target_pairs={{0,8},{2,10},{4,12},{6,14},{8,0},{10,2},{12,4},{14,6},{1,9},{3,11}... | collective-permute-start | bytes 208904 | tf_op jit(solution)/shard_map/ppermute | solution.py:235
  12.3 17.2 %collective-permute-start.5 = (bf16[16,2176]{1,0:T(8,128)(2,1)S(1)}, bf16[16,2176]{1,0:T(8,128)(2,1)S(1)}, u32[]{:S(2)}, u32[]{:S(2)}) collective-permute-start(bf16[16,2176]{1,0:T(8,128)(2,1)S(1)} %get-tuple-element.53), channel_id=1, source_target_pairs={{0,10},{2,8},{4,14},{6,12},{8,2},{10,0},{12,6},{14,4},{1,11},{3,9}... | collective-permute-start | bytes 208904 | tf_op jit(solution)/shard_map/ppermute | solution.py:235
  16.1 14.8 %collective-permute-start.6 = (bf16[16,2176]{1,0:T(8,128)(2,1)S(1)}, bf16[16,2176]{1,0:T(8,128)(2,1)S(1)}, u32[]{:S(2)}, u32[]{:S(2)}) collective-permute-start(bf16[16,2176]{1,0:T(8,128)(2,1)S(1)} %get-tuple-element.54), channel_id=1, source_target_pairs={{0,12},{2,14},{4,8},{6,10},{8,4},{10,6},{12,0},{14,2},{1,13},{3,15... | collective-permute-start | bytes 208904 | tf_op jit(solution)/shard_map/ppermute | solution.py:235
  17.4 7.4 %collective-permute-start.7 = (bf16[16,2176]{1,0:T(8,128)(2,1)S(1)}, bf16[16,2176]{1,0:T(8,128)(2,1)S(1)}, u32[]{:S(2)}, u32[]{:S(2)}) collective-permute-start(bf16[16,2176]{1,0:T(8,128)(2,1)S(1)} %get-tuple-element.55), channel_id=1, source_target_pairs={{0,14},{2,12},{4,10},{6,8},{8,6},{10,4},{12,2},{14,0},{1,15},{3,13... | collective-permute-start | bytes 208904 | tf_op jit(solution)/shard_map/ppermute | solution.py:235
  19.9 11.2 %collective-permute-start.8 = (bf16[16,2176]{1,0:T(8,128)(2,1)S(1)}, bf16[16,2176]{1,0:T(8,128)(2,1)S(1)}, u32[]{:S(2)}, u32[]{:S(2)}) collective-permute-start(bf16[16,2176]{1,0:T(8,128)(2,1)S(1)} %get-tuple-element.56), channel_id=1, source_target_pairs={{0,4},{2,6},{4,0},{6,2},{8,12},{10,14},{12,8},{14,10},{1,5},{3,7},... | collective-permute-start | bytes 208904 | tf_op jit(solution)/shard_map/ppermute | solution.py:235
  24.8 8.2 %collective-permute-start.3 = (bf16[64,2048]{1,0:T(8,128)(2,1)S(1)}, bf16[64,2048]{1,0:T(8,128)(2,1)S(1)}, u32[]{:S(2)}, u32[]{:S(2)}) collective-permute-start(bf16[64,2048]{1,0:T(8,128)(2,1)S(1)} %get-tuple-element.81), channel_id=1, source_target_pairs={{0,1},{1,0},{2,3},{3,2},{4,5},{5,4},{6,7},{7,6},{8,9},{9,8},{10,11... | collective-permute-start | bytes 786440 | tf_op jit(solution)/shard_map/ppermute | solution.py:231
  24.8 10.3 %collective-permute-start.9 = (bf16[16,2176]{1,0:T(8,128)(2,1)S(1)}, bf16[16,2176]{1,0:T(8,128)(2,1)S(1)}, u32[]{:S(2)}, u32[]{:S(2)}) collective-permute-start(bf16[16,2176]{1,0:T(8,128)(2,1)S(1)} %get-tuple-element.57), channel_id=1, source_target_pairs={{0,6},{2,4},{4,2},{6,0},{8,14},{10,12},{12,10},{14,8},{1,7},{3,5},... | collective-permute-start | bytes 208904 | tf_op jit(solution)/shard_map/ppermute | solution.py:235
  29.5 5.7 %collective-permute-start.10 = (bf16[16,2176]{1,0:T(8,128)(2,1)S(1)}, bf16[16,2176]{1,0:T(8,128)(2,1)S(1)}, u32[]{:S(2)}, u32[]{:S(2)}) collective-permute-start(bf16[16,2176]{1,0:T(8,128)(2,1)S(1)} %get-tuple-element.58), channel_id=1, source_target_pairs={{0,2},{2,0},{4,6},{6,4},{8,10},{10,8},{12,14},{14,12},{1,3},{3,1},... | collective-permute-start | bytes 208904 | tf_op jit(solution)/shard_map/ppermute | solution.py:235
  30.9 6.1 %collective-permute-start.13 = (bf16[2,8,1920]{2,1,0:T(8,128)(2,1)S(1)}, bf16[2,8,1920]{2,1,0:T(8,128)(2,1)S(1)}, u32[]{:S(2)}, u32[]{:S(2)}) collective-permute-start(bf16[2,8,1920]{2,1,0:T(8,128)(2,1)S(1)} %constant_dynamic-update-slice_fusion), channel_id=1, source_target_pairs={{0,6},{2,4},{4,2},{6,0},{8,14},{10,12},{12,10},{14,8},{1,7},{3,5},... | collective-permute-start | bytes 184328 | tf_op jit(solution)/shard_map/ppermute | solution.py:235
  31.1 6.0 %collective-permute-start.12 = (bf16[2,8,1920]{2,1,0:T(8,128)(2,1)S(1)}, bf16[2,8,1920]{2,1,0:T(8,128)(2,1)S(1)}, u32[]{:S(2)}, u32[]{:S(2)}) collective-permute-start(bf16[2,8,1920]{2,1,0:T(8,128)(2,1)S(1)} %constant_dynamic-update-slice_fusion), channel_id=1, source_target_pairs={{0,4},{2,6},{4,0},{6,2},{8,12},{10,14},{12,8},{14,10},{1,5},{3,7},... | collective-permute-start | bytes 184328 | tf_op jit(solution)/shard_map/ppermute | solution.py:235
  33.0 4.2 %collective-permute-start.11 = (bf16[2,8,1920]{2,1,0:T(8,128)(2,1)S(1)}, bf16[2,8,1920]{2,1,0:T(8,128)(2,1)S(1)}, u32[]{:S(2)}, u32[]{:S(2)}) collective-permute-start(bf16[2,8,1920]{2,1,0:T(8,128)(2,1)S(1)} %constant_dynamic-update-slice_fusion), channel_id=1, source_target_pairs={{0,2},{2,0},{4,6},{6,4},{8,10},{10,8},{12,14},{14,12},{1,3},{3,1},... | collective-permute-start | bytes 184328 | tf_op jit(solution)/shard_map/ppermute | solution.py:235
  37.3 4.2 %collective-permute-start.15 = (bf16[64,2048]{1,0:T(8,128)(2,1)S(1)}, bf16[64,2048]{1,0:T(8,128)(2,1)S(1)}, u32[]{:S(2)}, u32[]{:S(2)}) collective-permute-start(bf16[64,2048]{1,0:T(8,128)(2,1)S(1)} %constant_dynamic-slice_fusion), channel_id=1, source_target_pairs={{0,1},{1,0},{2,3},{3,2},{4,5},{5,4},{6,7},{7,6},{8,9},{9,8},{10,11... | collective-permute-start | bytes 786440 | tf_op jit(solution)/shard_map/ppermute | solution.py:231
  37.4 4.1 %collective-permute-start.14 = (bf16[8,8,1920]{2,1,0:T(8,128)(2,1)S(1)}, bf16[8,8,1920]{2,1,0:T(8,128)(2,1)S(1)}, u32[]{:S(2)}, u32[]{:S(2)}) collective-permute-start(bf16[8,8,1920]{2,1,0:T(8,128)(2,1)S(1)} %constant_dynamic-update-slice_fusion.2.own_ref), channel_id=1, source_target_pairs={{0,1},{1,0},{2,3},{3,2},{4,5},{5,4},{6,7},{7,6},{8,9},{9,8},{10,11... | collective-permute-start | bytes 737288 | tf_op jit(solution)/shard_map/ppermute | solution.py:231
  37.9 10.4 %all-to-all-start = ((f32[16,8,128]{2,1,0:T(8,128)}), f32[16,8,128]{2,1,0:T(8,128)S(1)}, u32[]{:S(2)}, u32[]{:S(2)}) async-start(f32[16,8,128]{2,1,0:T(8,128)} %get-tuple-element.59), calls=%async_computation | async-start | bytes 131072 | tf_op jit(solution)/shard_map/all_to_all | solution.py:346

commit v20 on v18

--- a/solution.py
+++ b/solution.py
@@ -59,10 +59,15 @@
     return parts
 
 
-def map_rest_kernel(mine, place_ref, w_ref, t_ref, p_ref, stats_ref, *refs):
-    o_refs, (s_ref, m_ref) = refs[:-2], refs[-2:]
+def map_rest_kernel(mine, place_ref, w_ref, t_ref, p_ref, stats_ref, hidden_ref, first_ref, near_ref, *refs):
+    far_refs, (s_ref, m_ref, o_buf, out_sem) = refs[:-4], refs[-4:]
     tokens = t_ref.shape[0]
     rows = w_ref.shape[0] - MASS_ROWS
+    near = near_ref.shape[0]
+    width = mine * BLK
+    wide = far_refs[0].shape[1]
+    riding = jnp.concatenate([hidden_ref[0].astype(jnp.float32), first_ref[0].astype(jnp.float32)], axis=0)
+    riding = riding.astype(jnp.bfloat16)
     stats = [stats_ref[0:1, :]] + three_parts(stats_ref[1:2, :])
     extra = jnp.zeros((tokens, stats_ref.shape[1]), jnp.float32)
     row_ids = lax.broadcasted_iota(jnp.int32, extra.shape, 0)
@@ -81,41 +86,55 @@
         mass = mass + m_ref[(rows + slot) * tokens : (rows + slot + 1) * tokens, :]
     inverse = jnp.broadcast_to(1.0 / jnp.sum(mass, axis=1, keepdims=True), (tokens, BLK))
 
-    for offset, o_ref in enumerate(o_refs):
-        owner = place_ref[0] ^ offset
+    def fill(o_ref, owner):
         for b in range(mine):
             first = pl.multiple_of((owner * mine + b) * tokens, tokens)
             tile = m_ref[pl.ds(first, tokens), :] * inverse
             o_ref[:, b * BLK : (b + 1) * BLK] = tile.astype(jnp.bfloat16)
-        o_ref[:, mine * BLK :] = extra
-
-
-def leaving_order(owners):
-    near = list(range(1, owners // 2))
-    return [*range(owners // 2, owners), *near[1:], *near[:1]]
-
-
-def grad_kernel(scale, place_ref, logits_ref, *refs):
-    own_ref, target_refs = refs[0], refs[1:-6]
-    grad_ref, terms_ref, target_ref, norm_ref, t_buf, sem = refs[-6:]
-    target_ref[place_ref[0]] = own_ref[...]
-    for offset, ref in zip(leaving_order(target_ref.shape[0]), target_refs):
-        target_ref[place_ref[0] ^ offset] = ref[...]
-    owners, tokens, _ = target_ref.shape
+        o_ref[:, width:wide] = extra
+
+    copies = []
+    for g in range(near):
+        o_buf[g, :, wide:] = riding
+        fill(o_buf.at[g], place_ref[0] // near * near + g)
+        copies.append(pltpu.make_async_copy(o_buf.at[g], near_ref.at[g], out_sem.at[g]))
+        copies[-1].start()
+    for g, far_ref in enumerate(far_refs):
+        fill(far_ref, place_ref[0] ^ (near + g))
+    for copy in copies:
+        copy.wait()
+
+
+def grad_kernel(scale, place_ref, logits_ref, near_ref, *refs):
+    far_refs, (grad_ref, terms_ref, far_buf, norm_ref, t_buf, sem) = refs[:-6], refs[-6:]
+    near, tokens, _ = near_ref.shape
+    owners = 2 * near
     group_tokens, width = logits_ref.shape
-    stats = [target_ref[q, :, width:].astype(jnp.float32) for q in range(owners)]
+    half_tokens = group_tokens // 2
+    for g, far_ref in enumerate(far_refs):
+        far_buf[(place_ref[0] ^ g) % near] = far_ref[...]
+    tiles = slice(width, width + group_tokens)
+    stats = [near_ref[g, :, tiles].astype(jnp.float32) for g in range(near)]
+    stats += [far_buf[g, :, tiles].astype(jnp.float32) for g in range(near)]
     top = stats[0][0:1]
     for one in stats[1:]:
         top = jnp.maximum(top, one[0:1])
     total = jnp.zeros_like(top)
     for one in stats:
         total = total + (one[1:2] + one[2:3] + one[3:4]) * jnp.exp(one[0:1] - top)
-    log_norm = top + jnp.log(total)
+
+    def turned(row):
+        other = jnp.concatenate([row[:, half_tokens:], row[:, :half_tokens]], axis=1)
+        return jnp.where(place_ref[0] < near, row, other)
+
+    log_norm = turned(top + jnp.log(total))
+    per = BLK // tokens
 
     def block(i, b):
         lanes = slice(b * BLK, (b + 1) * BLK)
-        group = slice(i * BLK // tokens, (i + 1) * BLK // tokens)
-        target = target_ref[group, :, lanes].reshape(BLK, BLK).astype(jnp.float32)
+        chunks = range(i * per, (i + 1) * per)
+        parts = [near_ref[c, :, lanes] if c < near else far_buf[c - near, :, lanes] for c in chunks]
+        target = jnp.concatenate(parts, axis=0).astype(jnp.float32)
         return target, logits_ref[i * BLK : (i + 1) * BLK, lanes].astype(jnp.float32)
 
     sums = []
@@ -130,8 +149,7 @@
             one = target * (jnp.log(jnp.where(positive, target, 1.0)) - (logits - norm))
             terms = terms + jnp.where(positive, one, 0.0)
         sums.append(jnp.sum(terms.T, axis=0, keepdims=True))
-    row = jnp.concatenate(sums, axis=1)
-    half_tokens = group_tokens // 2
+    row = turned(jnp.concatenate(sums, axis=1))
     for half in range(2):
         mine = row[:, half * half_tokens : (half + 1) * half_tokens]
         tile = jnp.concatenate([mine] * (t_buf.shape[2] // half_tokens), axis=1)
@@ -148,10 +166,6 @@
     leaving.wait()
 
 
-def arrival_order(owners):
-    return [a for b in range(owners // 2) for a in (b, b + owners // 2)]
-
-
 def weight_kernel(
     place_ref, own_ref, other_ref, grad_ref, got_ref, o_ref, joined_ref, s_ref, h_ref, block_ref, sems, join_sems
 ):
@@ -159,20 +173,22 @@
     half = place_ref[1]
     kept_at = pl.ds(pl.multiple_of(half * width, width), width)
     got_at = pl.ds(pl.multiple_of((1 - half) * width, width), width)
-    kept = pl.ds(pl.multiple_of(half * half_tokens, half_tokens), half_tokens)
+    near = own_ref.shape[0]
+    kept = pl.ds(pl.multiple_of((place_ref[0] // near ^ half) * half_tokens, half_tokens), half_tokens)
     copies = [
         pltpu.make_async_copy(grad_ref.at[kept, :], joined_ref.at[:, kept_at], join_sems.at[0]),
         pltpu.make_async_copy(got_ref, joined_ref.at[:, got_at], join_sems.at[1]),
     ]
     for copy in copies:
         copy.start()
-    owners, held, features = own_ref.shape
-    for i, offset in enumerate(arrival_order(owners)):
-        first = (place_ref[0] ^ offset) * 2
-        own = pl.ds(pl.multiple_of((first + half) * held, held), held)
-        other = pl.ds(pl.multiple_of((first + 1 - half) * held, held), held)
-        s_ref[own, :] = own_ref[i].astype(jnp.float32)
-        s_ref[other, :] = other_ref[i].astype(jnp.float32)
+    near, tokens, features = own_ref.shape
+    held = tokens // 2
+    for ref, side in ((own_ref, half), (other_ref, 1 - half)):
+        for g in range(near):
+            tile = ref[g].astype(jnp.float32)
+            for far in range(2):
+                rows = pl.ds(pl.multiple_of((far * near + g) * tokens + side * held, held), held)
+                s_ref[rows, :] = tile[far * held : (far + 1) * held]
     for i in range(s_ref.shape[0] // BLK):
         for j in range(features // BLK):
             tile = s_ref[i * BLK : (i + 1) * BLK, j * BLK : (j + 1) * BLK].T
@@ -273,38 +289,46 @@
         cost_estimate=cost(flops, 3 << 20),
         name="map_own",
     )(w_own, teacher_probs, stats)
-    chunk = (tokens, width + group_tokens)
-    outgoing = pl.pallas_call(
+    near = owners // 2
+    wide = width + group_tokens
+    chunk = (near, tokens, wide + features)
+    near_out, *far_out = pl.pallas_call(
         lambda *refs: map_rest_kernel(mine, *refs),
-        out_shape=[shape(chunk, bf16)] * owners,
-        in_specs=[scalars()] + [in_vmem()] * 4,
-        out_specs=[in_vmem()] * owners,
-        scratch_shapes=[spread, pltpu.VMEM(((rows + 8) * tokens, BLK), f32)],
+        out_shape=[shape(chunk, bf16)] + [shape((tokens, wide), bf16)] * near,
+        in_specs=[scalars()] + [in_vmem()] * 6,
+        out_specs=[anywhere()] + [in_vmem()] * near,
+        scratch_shapes=[
+            spread,
+            pltpu.VMEM(((rows + 8) * tokens, BLK), f32),
+            pltpu.VMEM(chunk, bf16),
+            dma(near),
+        ],
         compiler_params=params(),
         cost_estimate=cost(flops, 4 << 20),
         name="map_rest",
-    )(place, w_rest, teacher_other, part, stats)
-    outgoing, first_piece = lax.optimization_barrier((outgoing, first_piece))
-    targets = [to_partner(outgoing[a], a) for a in leaving_order(owners)]
-
-    hidden, late_logits, _ = lax.optimization_barrier((hidden, student_logits, outgoing[0]))
+    )(place, w_rest, teacher_other, part, stats, hidden, first_piece)
+    far_in = [to_partner(x, near + g) for g, x in enumerate(far_out)]
+    groups = [list(range(near)), list(range(near, owners))]
+    near_in = lax.all_to_all(near_out, "sv", 0, 0, axis_index_groups=groups, tiled=True)
+
+    late_logits, _ = lax.optimization_barrier((student_logits, near_out))
 
     keep = lax.dynamic_slice_in_dim(late_logits, half_index * width, width, 1)
     give = lax.dynamic_slice_in_dim(late_logits, (1 - half_index) * width, width, 1)
-    logits = in_order(keep, swap_halves(give), 0)
-
-    pieces = [jnp.concatenate([hidden, first_piece])]
-    pieces += [to_partner(pieces[0], a) for a in range(1, offset)]
+    got = swap_halves(give)
+    near_side = lax.axis_index("sv") // near
+    near_own = half_index == near_side
+    logits = jnp.concatenate([jnp.where(near_own, keep, got), jnp.where(near_own, got, keep)], axis=0)
 
     scale = float(columns * owners)
     lanes = -(-half_tokens // BLK) * BLK
     grad, terms = pl.pallas_call(
         lambda *refs: grad_kernel(scale, *refs),
         out_shape=(shape((group_tokens, width), bf16), shape((owners * halves, 8, lanes), f32)),
-        in_specs=[scalars()] + [in_vmem()] * (owners + 1),
+        in_specs=[scalars()] + [in_vmem()] * (near + 2),
         out_specs=(in_vmem(), anywhere()),
         scratch_shapes=[
-            pltpu.VMEM((owners, *chunk), bf16),
+            pltpu.VMEM((near, tokens, wide), bf16),
             pltpu.VMEM((group_tokens, BLK), f32),
             pltpu.VMEM((owners * halves, 8, lanes), f32),
             pltpu.SemaphoreType.DMA,
@@ -314,14 +338,14 @@
             10 * group_tokens * width, 6 * group_tokens * width, 2 * group_tokens * width
         ),
         name="logit_grad",
-    )(place, logits, outgoing[0], *targets)
+    )(place, logits, near_in, *far_in)
 
     terms = lax.all_to_all(terms, ("sv", "tv"), 0, 0, tiled=True)
-    give = lax.dynamic_slice_in_dim(grad, (1 - half_index) * half_tokens, half_tokens, 0)
+    given = near_side ^ (1 - half_index)
+    give = lax.dynamic_slice_in_dim(grad, given * half_tokens, half_tokens, 0)
     got = swap_halves(give)
 
-    *pieces, grad = lax.optimization_barrier((*pieces, grad))
-    hidden_own = jnp.concatenate(pieces)
+    hidden_own = near_in[:, :, wide:]
     steps = 8
     weight_grad, logit_grad = pl.pallas_call(
         weight_kernel,

time: 48.4 us -> 47.8 us (0.988)
  starting transfers between devices: 21.3 us -> 20.1 us
  Pallas kernels: 10 us -> 10.9 us
    ppermute x11 -> x5, starting transfers between devices: 16.2 us -> 11.3 us  [to_partner(): lax.ppermute(x, 'sv', [(s, s ^ offset) for s in range(lax.axis_size('sv'))])]
    all_to_all x0 -> x1, starting transfers between devices: none -> 3.8 us  [body(): lax.all_to_all(near_out, 'sv', 0, 0, axis_index_groups=groups, tiled=True)]
    pallas_call x1, Pallas kernels: 2.37 us -> 3.11 us  [body(): pl.pallas_call(lambda *refs: map_rest_kernel(mine, *refs), out_shape=[sha...]
    ppermute x11 -> x5, waiting for transfers between devices: 9.4 us -> 9.25 us  [to_partner(): lax.ppermute(x, 'sv', [(s, s ^ offset) for s in range(lax.axis_size('sv'))])]
  transfers between devices with their start and end apart: 17 -> 12, of which waited for: 6 -> 6; matrix products, arithmetic and copies ran while one was open for 3% -> 3% of each run, Pallas kernels for 21% -> 12%
where the time goes in v20:
time: 47.8 us; the launch traced here: 47.5 us
  starting transfers between devices  20.1 us (42%)
  waiting for transfers between devices  12 us (25%)
  Pallas kernels  10.9 us (23%)
  other arithmetic  3.53 us (7%)
  between operations  0.78 us (2%)
    ppermute x5, starting transfers between devices, to_partner(): lax.ppermute(x, 'sv', [(s, s ^ offset) for s in range(lax.axis_size('sv'))])  11.3 us
    ppermute x5, waiting for transfers between devices, to_partner(): lax.ppermute(x, 'sv', [(s, s ^ offset) for s in range(lax.axis_size('sv'))])  9.25 us
    pallas_call x1, Pallas kernels, body(): pl.pallas_call(weight_kernel, out_shape=(shape((features, width), bf16),...  4.48 us
    all_to_all x1, starting transfers between devices, body(): lax.all_to_all(near_out, 'sv', 0, 0, axis_index_groups=groups, tiled=True)  3.8 us
    all_to_all x1, starting transfers between devices, body(): terms = lax.all_to_all(terms, ('sv', 'tv'), 0, 0, tiled=True)  3.5 us
    pallas_call x1, Pallas kernels, body(): pl.pallas_call(lambda *refs: map_rest_kernel(mine, *refs), out_shape=[sha...  3.11 us
    all_to_all x1, waiting for transfers between devices, body(): terms = lax.all_to_all(terms, ('sv', 'tv'), 0, 0, tiled=True)  2.35 us
    pallas_call x1, Pallas kernels, body(): pl.pallas_call(lambda *refs: grad_kernel(scale, *refs), out_shape=(shape(...  1.92 us
  transfers between devices with their start and end apart: 12, of which 6 were waited for; matrix products, arithmetic and copies ran while one was open for 3% of the time, Pallas kernels for 12%

profile of v20, /device:TPU:0, one launch (start us, length us, event | category | flops | bytes accessed | tf_op | source)
XLA Modules:
  0.0 47.5 jit_solution(14625852255503911460)
XLA Ops:
  0.6 1.7 %convert_reduce_fusion = (f32[64]{0:T(128)S(1)}, f32[64]{0:T(128)S(1)}) fusion(bf16[64,4096]{1,0:T(8,128)(2,1)} %param.10), kind=kLoop, calls=%fused_computation | loop fusion | flops 1834624 | bytes 524800 | tf_op jit(solution)/shard_map/reduce | solution.py:269
  2.3 0.5 %collective-permute-start.1 = (f32[2,64]{1,0:T(2,128)S(1)}, f32[2,64]{1,0:T(2,128)S(1)}, u32[]{:S(2)}, u32[]{:S(2)}) collective-permute-start(f32[2,64]{1,0:T(2,128)S(1)} %pad_maximum_fusion.1), channel_id=1, source_target_pairs={{0,1},{1,0},{2,3},{3,2},{4,5},{5,4},{6,7},{7,6},{8,9},{9,8},{10,11... | collective-permute-start | bytes 1544 | tf_op jit(solution)/shard_map/ppermute | solution.py:229
  2.8 3.7 %collective-permute-start.2 = (bf16[1,8,1920]{2,1,0:T(8,128)(2,1)}, bf16[1,8,1920]{2,1,0:T(8,128)(2,1)S(1)}, u32[]{:S(2)}, u32[]{:S(2)}) collective-permute-start(bf16[1,8,1920]{2,1,0:T(8,128)(2,1)} %bitcast.9), channel_id=1, source_target_pairs={{0,8},{2,10},{4,12},{6,14},{8,0},{10,2},{12,4},{14,6},{1,9},{3,11}... | collective-permute-start | bytes 92168 | tf_op jit(solution)/shard_map/ppermute | solution.py:233
  6.7 0.7 %fusion.5 = f32[640,2]{0,1:T(2,128)S(1)} fusion(bf16[640,2]{0,1:T(2,128)(2,1)} %param.9, s32[640,2]{0,1:T(2,128)} %param.7, s32[640,2]{0,1:T(2,128)} %param.8, s32[]{:T(128)S(6)} %mul.51), kind=kLoop, calls=%fused_computation.17 | loop fusion | flops 14080 | bytes 17924 | tf_op jit(solution)/shard_map/add | solution.py:276
  7.6 0.2 add_convert_fusion
  8.0 1.4 %map_own.1.refs_3_ = f32[144,2048]{1,0:T(8,128)S(1)} custom-call(bf16[144,320]{1,0:T(8,128)(2,1)S(1)} %get-tuple-element.51.w_ref, bf16[16,40960]{1,0:T(8,128)(2,1)S(1)} %copy-done, f32[2,128]{1,0:T(2,128)S(1)} %pad_maximum_fusion.2.stats_ref.refs_4_), custom_call_target="tpu_custom_call" | custom-call | flops 188743680 | bytes 3145728 | tf_op jit(solution)/shard_map/map_own/pallas_call | solution.py:282
  9.4 0.4 collective-permute-done.refs_2_
  9.8 3.1 %map_rest.1 = (bf16[4,16,4096]{2,1,0:T(8,128)(2,1)}, bf16[16,2176]{1,0:T(8,128)(2,1)S(1)}, bf16[16,2176]{1,0:T(8,128)(2,1)S(1)}, bf16[16,2176]{1,0:T(8,128)(2,1)S(1)}, bf16[16,2176]{1,0:T(8,128)(2,1)S(1)}) custom-call(s32[2]{0:T(128)S(1)} %pad_add_fusion.refs_0_.place_ref, bf16[144,320]{1,0:T(8,128)(2,1)S(1)} %get-tuple-element.52.refs_1_, ...), custom_call_target="tpu_custom_call" | custom-call | flops 188743680 | bytes 4194304 | tf_op jit(solution)/shard_map/map_rest/pallas_call | solution.py:295
  12.9 0.2 collective-permute-start.3
  13.1 3.8 %all-to-all-start = ((bf16[4,16,4096]{2,1,0:T(8,128)(2,1)}), bf16[4,16,4096]{2,1,0:T(8,128)(2,1)S(1)}, u32[]{:S(2)}, u32[]{:S(2)}) async-start(bf16[4,16,4096]{2,1,0:T(8,128)(2,1)} %get-tuple-element.24), calls=%async_computation | async-start | bytes 1048576 | tf_op jit(solution)/shard_map/all_to_all | solution.py:312
  16.9 2.0 %collective-permute-start.4 = (bf16[16,2176]{1,0:T(8,128)(2,1)S(1)}, bf16[16,2176]{1,0:T(8,128)(2,1)S(1)}, u32[]{:S(2)}, u32[]{:S(2)}) collective-permute-start(bf16[16,2176]{1,0:T(8,128)(2,1)S(1)} %get-tuple-element.26), channel_id=1, source_target_pairs={{0,8},{2,10},{4,12},{6,14},{8,0},{10,2},{12,4},{14,6},{1,9},{3,11}... | collective-permute-start | bytes 208904 | tf_op jit(solution)/shard_map/ppermute | solution.py:233
  18.9 2.4 %collective-permute-start.5 = (bf16[16,2176]{1,0:T(8,128)(2,1)S(1)}, bf16[16,2176]{1,0:T(8,128)(2,1)S(1)}, u32[]{:S(2)}, u32[]{:S(2)}) collective-permute-start(bf16[16,2176]{1,0:T(8,128)(2,1)S(1)} %get-tuple-element.27), channel_id=1, source_target_pairs={{0,10},{2,8},{4,14},{6,12},{8,2},{10,0},{12,6},{14,4},{1,11},{3,9}... | collective-permute-start | bytes 208904 | tf_op jit(solution)/shard_map/ppermute | solution.py:233
  21.3 2.9 %collective-permute-start.6 = (bf16[16,2176]{1,0:T(8,128)(2,1)S(1)}, bf16[16,2176]{1,0:T(8,128)(2,1)S(1)}, u32[]{:S(2)}, u32[]{:S(2)}) collective-permute-start(bf16[16,2176]{1,0:T(8,128)(2,1)S(1)} %get-tuple-element.28), channel_id=1, source_target_pairs={{0,12},{2,14},{4,8},{6,10},{8,4},{10,6},{12,0},{14,2},{1,13},{3,15... | collective-permute-start | bytes 208904 | tf_op jit(solution)/shard_map/ppermute | solution.py:233
  24.2 0.4 collective-permute-start.7
  24.7 0.6 %collective-permute-done.4.refs_3_ = bf16[16,2176]{1,0:T(8,128)(2,1)S(1)} collective-permute-done((bf16[16,2176]{1,0:T(8,128)(2,1)S(1)}, bf16[16,2176]{1,0:T(8,128)(2,1)S(1)}, u32[]{:S(2)}, u32[]{:S(2)}) %collective-permute-start.4) | collective-permute-done | bytes 69664 | tf_op jit(solution)/shard_map/ppermute | solution.py:233
  25.4 1.5 %collective-permute-done.5.refs_4_ = bf16[16,2176]{1,0:T(8,128)(2,1)S(1)} collective-permute-done((bf16[16,2176]{1,0:T(8,128)(2,1)S(1)}, bf16[16,2176]{1,0:T(8,128)(2,1)S(1)}, u32[]{:S(2)}, u32[]{:S(2)}) %collective-permute-start.5) | collective-permute-done | bytes 69664 | tf_op jit(solution)/shard_map/ppermute | solution.py:233
  26.9 5.5 %collective-permute-done.6.refs_5_ = bf16[16,2176]{1,0:T(8,128)(2,1)S(1)} collective-permute-done((bf16[16,2176]{1,0:T(8,128)(2,1)S(1)}, bf16[16,2176]{1,0:T(8,128)(2,1)S(1)}, u32[]{:S(2)}, u32[]{:S(2)}) %collective-permute-start.6) | collective-permute-done | bytes 69664 | tf_op jit(solution)/shard_map/ppermute | solution.py:233
  32.3 1.7 %collective-permute-done.7.refs_6_ = bf16[16,2176]{1,0:T(8,128)(2,1)S(1)} collective-permute-done((bf16[16,2176]{1,0:T(8,128)(2,1)S(1)}, bf16[16,2176]{1,0:T(8,128)(2,1)S(1)}, u32[]{:S(2)}, u32[]{:S(2)}) %collective-permute-start.7) | collective-permute-done | bytes 69664 | tf_op jit(solution)/shard_map/ppermute | solution.py:233
  34.0 1.9 %logit_grad.1 = (bf16[128,2048]{1,0:T(8,128)(2,1)S(1)}, f32[16,8,128]{2,1,0:T(8,128)}) custom-call(s32[2]{0:T(128)S(1)} %pad_add_fusion.refs_0_.place_ref, bf16[128,2048]{1,0:T(8,128)(2,1)S(1)} %pad_maximum_fusion.refs_1_, bf16[4,16,4096]{2,1,0:T(8,128)(2,1)S(1)} %all-to-all-done.refs_2_, bf16[16,2176]{1,0:T(8,128)(2,1)S(1)} %collective-permute-done.4.refs_3_, ...), custom_call_target="tpu_custom_call" | custom-call | flops 2621440 | bytes 1572864 | tf_op jit(solution)/shard_map/logit_grad/pallas_call | solution.py:325
  36.1 0.6 %collective-permute-start.8 = (bf16[4,16,1920]{2,1,0:T(8,128)(2,1)S(1)}, bf16[4,16,1920]{2,1,0:T(8,128)(2,1)S(1)}, u32[]{:S(2)}, u32[]{:S(2)}) collective-permute-start(bf16[4,16,1920]{2,1,0:T(8,128)(2,1)S(1)} %slice.32.own_ref), channel_id=1, source_target_pairs={{0,1},{1,0},{2,3},{3,2},{4,5},{5,4},{6,7},{7,6},{8,9},{9,8},{10,11... | collective-permute-start | bytes 737288 | tf_op jit(solution)/shard_map/ppermute | solution.py:229
  36.6 3.5 %all-to-all-start.1 = ((f32[16,8,128]{2,1,0:T(8,128)}), f32[16,8,128]{2,1,0:T(8,128)S(1)}, u32[]{:S(2)}, u32[]{:S(2)}) async-start(f32[16,8,128]{2,1,0:T(8,128)} %get-tuple-element.30), calls=%async_computation.1 | async-start | bytes 131072 | tf_op jit(solution)/shard_map/all_to_all | solution.py:343
  40.1 4.5 %weight_grad.1 = (bf16[1920,2048]{1,0:T(8,128)(2,1)}, bf16[64,4096]{1,0:T(8,128)(2,1)}) custom-call(s32[2]{0:T(128)S(1)} %pad_add_fusion.refs_0_.place_ref, bf16[4,16,1920]{2,1,0:T(8,128)(2,1)S(1)} %slice.32.own_ref, bf16[4,16,1920]{2,1,0:T(8,128)(2,1)S(1)} %collective-permute-done.8.other_ref, bf16[128,2048]{1,0:T(8,128)(2,1)S(1)} %get-tuple-element.31.grad_ref, ...), custom_call_target="tpu_custom_call" | custom-call | flops 1006632960 | bytes 8880128 | tf_op jit(solution)/shard_map/weight_grad/pallas_call | solution.py:350
  44.6 2.3 %all-to-all-done.1 = f32[16,8,128]{2,1,0:T(8,128)S(1)} async-done(((f32[16,8,128]{2,1,0:T(8,128)}), f32[16,8,128]{2,1,0:T(8,128)S(1)}, u32[]{:S(2)}, u32[]{:S(2)}) %all-to-all-start.1) | async-done | bytes 65568 | tf_op jit(solution)/shard_map/all_to_all | solution.py:343
  47.0 0.5 %slice_reduce_fusion = f32[64]{0:T(128)} fusion(f32[16,8,128]{2,1,0:T(8,128)S(1)} %all-to-all-done.1), kind=kLoop, calls=%fused_computation.15 | loop fusion | flops 960 | bytes 4352 | tf_op jit(solution)/shard_map/reduce_sum | solution.py:370
  (27 shorter events, 0.8 us)
Async XLA Ops:
  0.6 7.3 %copy-start = (bf16[16,40960]{1,0:T(8,128)(2,1)S(1)}, bf16[16,40960]{1,0:T(8,128)(2,1)}, u32[]{:S(2)}) copy-start(bf16[16,40960]{1,0:T(8,128)(2,1)} %t_ref.1) | copy-start | bytes 3932164
  2.3 5.5 %collective-permute-start.1 = (f32[2,64]{1,0:T(2,128)S(1)}, f32[2,64]{1,0:T(2,128)S(1)}, u32[]{:S(2)}, u32[]{:S(2)}) collective-permute-start(f32[2,64]{1,0:T(2,128)S(1)} %pad_maximum_fusion.1), channel_id=1, source_target_pairs={{0,1},{1,0},{2,3},{3,2},{4,5},{5,4},{6,7},{7,6},{8,9},{9,8},{10,11... | collective-permute-start | bytes 1544 | tf_op jit(solution)/shard_map/ppermute | solution.py:229
  2.8 6.5 %collective-permute-start.2 = (bf16[1,8,1920]{2,1,0:T(8,128)(2,1)}, bf16[1,8,1920]{2,1,0:T(8,128)(2,1)S(1)}, u32[]{:S(2)}, u32[]{:S(2)}) collective-permute-start(bf16[1,8,1920]{2,1,0:T(8,128)(2,1)} %bitcast.9), channel_id=1, source_target_pairs={{0,8},{2,10},{4,12},{6,14},{8,0},{10,2},{12,4},{14,6},{1,9},{3,11}... | collective-permute-start | bytes 92168 | tf_op jit(solution)/shard_map/ppermute | solution.py:233
  6.5 3.2 %collective-permute-start = (bf16[16,40960]{1,0:T(8,128)(2,1)}, bf16[16,40960]{1,0:T(8,128)(2,1)S(1)}, u32[]{:S(2)}, u32[]{:S(2)}) collective-permute-start(bf16[16,40960]{1,0:T(8,128)(2,1)} %t_ref.1), channel_id=1, source_target_pairs={{0,1},{1,0},{2,3},{3,2},{4,5},{5,4},{6,7},{7,6},{8,9},{9,8},{10,11... | collective-permute-start | bytes 3932168 | tf_op jit(solution)/shard_map/ppermute | solution.py:229
  7.9 1.9 %copy-start.1 = (bf16[8,1920]{1,0:T(8,128)(2,1)S(1)}, bf16[8,1920]{1,0:T(8,128)(2,1)}, u32[]{:S(2)}) copy-start(bf16[8,1920]{1,0:T(8,128)(2,1)} %param.11) | copy-start | bytes 92164
  9.8 3.1 %copy-start.2 = (bf16[64,4096]{1,0:T(8,128)(2,1)S(1)}, bf16[64,4096]{1,0:T(8,128)(2,1)}, u32[]{:S(2)}) copy-start(bf16[64,4096]{1,0:T(8,128)(2,1)} %param.10) | copy-start | bytes 1572868
  12.9 11.7 %collective-permute-start.3 = (bf16[64,2048]{1,0:T(8,128)(2,1)S(1)}, bf16[64,2048]{1,0:T(8,128)(2,1)S(1)}, u32[]{:S(2)}, u32[]{:S(2)}) collective-permute-start(bf16[64,2048]{1,0:T(8,128)(2,1)S(1)} %constant_dynamic-slice_fusion.1), channel_id=1, source_target_pairs={{0,1},{1,0},{2,3},{3,2},{4,5},{5,4},{6,7},{7,6},{8,9},{9,8},{10,11... | collective-permute-start | bytes 786440 | tf_op jit(solution)/shard_map/ppermute | solution.py:229
  13.1 20.8 %all-to-all-start = ((bf16[4,16,4096]{2,1,0:T(8,128)(2,1)}), bf16[4,16,4096]{2,1,0:T(8,128)(2,1)S(1)}, u32[]{:S(2)}, u32[]{:S(2)}) async-start(bf16[4,16,4096]{2,1,0:T(8,128)(2,1)} %get-tuple-element.24), calls=%async_computation | async-start | bytes 1048576 | tf_op jit(solution)/shard_map/all_to_all | solution.py:312
  16.9 8.4 %collective-permute-start.4 = (bf16[16,2176]{1,0:T(8,128)(2,1)S(1)}, bf16[16,2176]{1,0:T(8,128)(2,1)S(1)}, u32[]{:S(2)}, u32[]{:S(2)}) collective-permute-start(bf16[16,2176]{1,0:T(8,128)(2,1)S(1)} %get-tuple-element.26), channel_id=1, source_target_pairs={{0,8},{2,10},{4,12},{6,14},{8,0},{10,2},{12,4},{14,6},{1,9},{3,11}... | collective-permute-start | bytes 208904 | tf_op jit(solution)/shard_map/ppermute | solution.py:233
  18.9 7.9 %collective-permute-start.5 = (bf16[16,2176]{1,0:T(8,128)(2,1)S(1)}, bf16[16,2176]{1,0:T(8,128)(2,1)S(1)}, u32[]{:S(2)}, u32[]{:S(2)}) collective-permute-start(bf16[16,2176]{1,0:T(8,128)(2,1)S(1)} %get-tuple-element.27), channel_id=1, source_target_pairs={{0,10},{2,8},{4,14},{6,12},{8,2},{10,0},{12,6},{14,4},{1,11},{3,9}... | collective-permute-start | bytes 208904 | tf_op jit(solution)/shard_map/ppermute | solution.py:233
  21.3 11.0 %collective-permute-start.6 = (bf16[16,2176]{1,0:T(8,128)(2,1)S(1)}, bf16[16,2176]{1,0:T(8,128)(2,1)S(1)}, u32[]{:S(2)}, u32[]{:S(2)}) collective-permute-start(bf16[16,2176]{1,0:T(8,128)(2,1)S(1)} %get-tuple-element.28), channel_id=1, source_target_pairs={{0,12},{2,14},{4,8},{6,10},{8,4},{10,6},{12,0},{14,2},{1,13},{3,15... | collective-permute-start | bytes 208904 | tf_op jit(solution)/shard_map/ppermute | solution.py:233
  24.2 9.8 %collective-permute-start.7 = (bf16[16,2176]{1,0:T(8,128)(2,1)S(1)}, bf16[16,2176]{1,0:T(8,128)(2,1)S(1)}, u32[]{:S(2)}, u32[]{:S(2)}) collective-permute-start(bf16[16,2176]{1,0:T(8,128)(2,1)S(1)} %get-tuple-element.29), channel_id=1, source_target_pairs={{0,14},{2,12},{4,10},{6,8},{8,6},{10,4},{12,2},{14,0},{1,15},{3,13... | collective-permute-start | bytes 208904 | tf_op jit(solution)/shard_map/ppermute | solution.py:233
  36.0 4.2 %collective-permute-start.9 = (bf16[64,2048]{1,0:T(8,128)(2,1)S(1)}, bf16[64,2048]{1,0:T(8,128)(2,1)S(1)}, u32[]{:S(2)}, u32[]{:S(2)}) collective-permute-start(bf16[64,2048]{1,0:T(8,128)(2,1)S(1)} %constant_dynamic-slice_fusion), channel_id=1, source_target_pairs={{0,1},{1,0},{2,3},{3,2},{4,5},{5,4},{6,7},{7,6},{8,9},{9,8},{10,11... | collective-permute-start | bytes 786440 | tf_op jit(solution)/shard_map/ppermute | solution.py:229
  36.1 4.1 %collective-permute-start.8 = (bf16[4,16,1920]{2,1,0:T(8,128)(2,1)S(1)}, bf16[4,16,1920]{2,1,0:T(8,128)(2,1)S(1)}, u32[]{:S(2)}, u32[]{:S(2)}) collective-permute-start(bf16[4,16,1920]{2,1,0:T(8,128)(2,1)S(1)} %slice.32.own_ref), channel_id=1, source_target_pairs={{0,1},{1,0},{2,3},{3,2},{4,5},{5,4},{6,7},{7,6},{8,9},{9,8},{10,11... | collective-permute-start | bytes 737288 | tf_op jit(solution)/shard_map/ppermute | solution.py:229
  36.6 10.4 %all-to-all-start.1 = ((f32[16,8,128]{2,1,0:T(8,128)}), f32[16,8,128]{2,1,0:T(8,128)S(1)}, u32[]{:S(2)}, u32[]{:S(2)}) async-start(f32[16,8,128]{2,1,0:T(8,128)} %get-tuple-element.30), calls=%async_computation.1 | async-start | bytes 131072 | tf_op jit(solution)/shard_map/all_to_all | solution.py:343

commit v21 on v17

--- a/solution.py
+++ b/solution.py
@@ -10,6 +10,7 @@
 TOPA = 2
 MASS_ROWS = 16
 STEP = 16
+GROUP = 8
 
 
 def block_weights(code, rows):
@@ -36,18 +37,18 @@
     lax.fori_loop(0, count // STEP, some, 0)
 
 
-def token_pair(s_ref, t, tokens):
+def token_columns(s_ref, t, tokens):
     count = s_ref.shape[0] // tokens
-    both = [s_ref[pl.ds(t + i, count, stride=tokens), :].astype(jnp.bfloat16) for i in range(2)]
-    return jnp.concatenate(both, axis=1)
+    some = [s_ref[pl.ds(t + i, count, stride=tokens), :].astype(jnp.bfloat16) for i in range(GROUP)]
+    return jnp.concatenate(some, axis=1)
 
 
 def map_own_kernel(w_ref, t_ref, stats_ref, o_ref, s_ref):
     tokens = t_ref.shape[0]
     spread_tokens(t_ref, s_ref, 0, t_ref.shape[1] // BLK)
-    for t in range(0, tokens, 2):
-        o_ref[:, t * BLK : (t + 2) * BLK] = jnp.dot(
-            w_ref[...], token_pair(s_ref, t, tokens), preferred_element_type=jnp.float32
+    for t in range(0, tokens, GROUP):
+        o_ref[:, t * BLK : (t + GROUP) * BLK] = jnp.dot(
+            w_ref[...], token_columns(s_ref, t, tokens), preferred_element_type=jnp.float32
         )
 
 
@@ -71,11 +72,11 @@
         extra = jnp.where(row_ids == i, row, extra)
     extra = extra.astype(jnp.bfloat16)
     spread_tokens(t_ref, s_ref, 0, t_ref.shape[1] // BLK)
-    for t in range(0, tokens, 2):
-        both = p_ref[:, t * BLK : (t + 2) * BLK] + jnp.dot(
-            w_ref[...], token_pair(s_ref, t, tokens), preferred_element_type=jnp.float32
+    for t in range(0, tokens, GROUP):
+        both = p_ref[:, t * BLK : (t + GROUP) * BLK] + jnp.dot(
+            w_ref[...], token_columns(s_ref, t, tokens), preferred_element_type=jnp.float32
         )
-        for i in range(2):
+        for i in range(GROUP):
             m_ref[pl.ds(t + i, rows + 8, stride=tokens), :] = both[: rows + 8, i * BLK : (i + 1) * BLK]
     mass = m_ref[rows * tokens : (rows + 1) * tokens, :]
     for slot in range(1, TOPA):

time: 45.7 us -> 45.7 us (level)
  no operation moved by 1% of the time
where the time goes in v21:
time: 45.7 us; the launch traced here: 45.4 us
  starting transfers between devices  17 us (37%)
  waiting for transfers between devices  14.1 us (31%)
  Pallas kernels  9.7 us (21%)
  other arithmetic  3.54 us (8%)
  between operations  0.83 us (2%)
    all_to_all x1, waiting for transfers between devices, body(): target = lax.all_to_all(outgoing, 'sv', 0, 0, tiled=True)  11.8 us
    ppermute x4, starting transfers between devices, to_partner(): lax.ppermute(x, 'sv', [(s, s ^ offset) for s in range(lax.axis_size('sv'))])  7.59 us
    pallas_call x1, Pallas kernels, body(): pl.pallas_call(weight_kernel, out_shape=(shape((features, width), bf16),...  4.48 us
    all_to_all x1, starting transfers between devices, body(): target = lax.all_to_all(outgoing, 'sv', 0, 0, tiled=True)  4.29 us
    all_to_all x1, starting transfers between devices, body(): terms = lax.all_to_all(terms, ('sv', 'tv'), 0, 0, tiled=True)  3.74 us
    pallas_call x1, Pallas kernels, body(): pl.pallas_call(map_rest_kernel, out_shape=shape(chunk, bf16), in_specs=[i...  2.59 us
    all_to_all x1, waiting for transfers between devices, body(): terms = lax.all_to_all(terms, ('sv', 'tv'), 0, 0, tiled=True)  2.32 us
    another operation x1, other arithmetic, body(): lax.reduce((wide, jnp.ones_like(wide)), (low, jnp.float32(0)), merge, (1,))  1.68 us
  transfers between devices with their start and end apart: 11, of which 2 were waited for; matrix products, arithmetic and copies ran while one was open for 3% of the time, Pallas kernels for 21%

profile of v21, /device:TPU:0, one launch (start us, length us, event | category | flops | bytes accessed | tf_op | source)
XLA Modules:
  0.0 45.4 jit_solution(1659270678814230383)
XLA Ops:
  0.6 1.7 %convert_reduce_fusion = (f32[64]{0:T(128)S(1)}, f32[64]{0:T(128)S(1)}) fusion(bf16[64,4096]{1,0:T(8,128)(2,1)} %param.10), kind=kLoop, calls=%fused_computation | loop fusion | flops 1834624 | bytes 524800 | tf_op jit(solution)/shard_map/reduce | solution.py:256
  2.3 0.5 %collective-permute-start = (bf16[16,40960]{1,0:T(8,128)(2,1)}, bf16[16,40960]{1,0:T(8,128)(2,1)S(1)}, u32[]{:S(2)}, u32[]{:S(2)}) collective-permute-start(bf16[16,40960]{1,0:T(8,128)(2,1)} %t_ref.1), channel_id=1, source_target_pairs={{0,1},{1,0},{2,3},{3,2},{4,5},{5,4},{6,7},{7,6},{8,9},{9,8},{10,11... | collective-permute-start | bytes 3932168 | tf_op jit(solution)/shard_map/ppermute | solution.py:216
  2.8 0.1 collective-permute-start.1
  2.9 4.0 %collective-permute-start.2 = (bf16[1,8,1920]{2,1,0:T(8,128)(2,1)}, bf16[1,8,1920]{2,1,0:T(8,128)(2,1)S(1)}, u32[]{:S(2)}, u32[]{:S(2)}) collective-permute-start(bf16[1,8,1920]{2,1,0:T(8,128)(2,1)} %bitcast.9), channel_id=1, source_target_pairs={{0,8},{2,10},{4,12},{6,14},{8,0},{10,2},{12,4},{14,6},{1,9},{3,11}... | collective-permute-start | bytes 92168 | tf_op jit(solution)/shard_map/ppermute | solution.py:220
  6.9 0.7 %fusion.5 = f32[640,2]{0,1:T(2,128)S(1)} fusion(bf16[640,2]{0,1:T(2,128)(2,1)} %param.9, s32[640,2]{0,1:T(2,128)} %param.7, s32[640,2]{0,1:T(2,128)} %param.8, s32[]{:T(128)S(6)} %mul.51), kind=kLoop, calls=%fused_computation.23 | loop fusion | flops 14080 | bytes 17924 | tf_op jit(solution)/shard_map/add | solution.py:263
  7.7 0.1 dynamic-slice_bitcast_fusion
  7.8 0.2 add_convert_fusion
  8.1 0.1 pad_maximum_fusion.2.stats_ref
  8.2 1.4 %map_own.1.p_ref = f32[144,2048]{1,0:T(8,128)S(1)} custom-call(bf16[144,320]{1,0:T(8,128)(2,1)S(1)} %get-tuple-element.57.w_ref, bf16[16,40960]{1,0:T(8,128)(2,1)S(1)} %copy-done, f32[2,128]{1,0:T(2,128)S(1)} %pad_maximum_fusion.2.stats_ref), custom_call_target="tpu_custom_call" | custom-call | flops 188743680 | bytes 3145728 | tf_op jit(solution)/shard_map/map_own/pallas_call | solution.py:269
  9.6 2.6 %map_rest.1 = bf16[8,16,2176]{2,1,0:T(8,128)(2,1)} custom-call(bf16[144,320]{1,0:T(8,128)(2,1)S(1)} %get-tuple-element.58.w_ref, bf16[16,40960]{1,0:T(8,128)(2,1)S(1)} %collective-permute-done.t_ref, f32[144,2048]{1,0:T(8,128)S(1)} %map_own.1.p_ref, f32[2,128]{1,0:T(2,128)S(1)} %pad_maximum_fusion.2.stats_ref), custom_call_target="tpu_custom_call" | custom-call | flops 188743680 | bytes 4194304 | tf_op jit(solution)/shard_map/map_rest/pallas_call | solution.py:280
  12.2 4.3 %all-to-all-start = ((bf16[8,16,2176]{2,1,0:T(8,128)(2,1)}), bf16[8,16,2176]{2,1,0:T(8,128)(2,1)S(1)}, u32[]{:S(2)}, u32[]{:S(2)}) async-start(bf16[8,16,2176]{2,1,0:T(8,128)(2,1)} %map_rest.1), calls=%async_computation | async-start | bytes 1114112 | tf_op jit(solution)/shard_map/all_to_all | solution.py:296
  16.5 0.1 collective-permute-start.3
  16.7 2.9 %collective-permute-start.6 = (bf16[2,8,1920]{2,1,0:T(8,128)(2,1)S(1)}, bf16[2,8,1920]{2,1,0:T(8,128)(2,1)S(1)}, u32[]{:S(2)}, u32[]{:S(2)}) collective-permute-start(bf16[2,8,1920]{2,1,0:T(8,128)(2,1)S(1)} %constant_dynamic-update-slice_fusion), channel_id=1, source_target_pairs={{0,6},{2,4},{4,2},{6,0},{8,14},{10,12},{12,10},{14,8},{1,7},{3,5},... | collective-permute-start | bytes 184328 | tf_op jit(solution)/shard_map/ppermute | solution.py:220
  19.6 0.6 %collective-permute-start.5 = (bf16[2,8,1920]{2,1,0:T(8,128)(2,1)S(1)}, bf16[2,8,1920]{2,1,0:T(8,128)(2,1)S(1)}, u32[]{:S(2)}, u32[]{:S(2)}) collective-permute-start(bf16[2,8,1920]{2,1,0:T(8,128)(2,1)S(1)} %constant_dynamic-update-slice_fusion), channel_id=1, source_target_pairs={{0,4},{2,6},{4,0},{6,2},{8,12},{10,14},{12,8},{14,10},{1,5},{3,7},... | collective-permute-start | bytes 184328 | tf_op jit(solution)/shard_map/ppermute | solution.py:220
  20.2 0.1 collective-permute-start.4
  20.3 0.1 broadcast_select_fusion.1
  20.4 11.8 %all-to-all-done.refs_0_ = bf16[8,16,2176]{2,1,0:T(8,128)(2,1)S(1)} async-done(((bf16[8,16,2176]{2,1,0:T(8,128)(2,1)}), bf16[8,16,2176]{2,1,0:T(8,128)(2,1)S(1)}, u32[]{:S(2)}, u32[]{:S(2)}) %all-to-all-start) | async-done | bytes 557088 | tf_op jit(solution)/shard_map/all_to_all | solution.py:296
  32.2 1.2 %logit_grad.1 = (bf16[128,2048]{1,0:T(8,128)(2,1)S(1)}, f32[16,8,128]{2,1,0:T(8,128)}) custom-call(bf16[8,16,2176]{2,1,0:T(8,128)(2,1)S(1)} %all-to-all-done.refs_0_, bf16[128,2048]{1,0:T(8,128)(2,1)S(1)} %pad_maximum_fusion.refs_1_), custom_call_target="tpu_custom_call" | custom-call | flops 2621440 | bytes 1572864 | tf_op jit(solution)/shard_map/logit_grad/pallas_call | solution.py:309
  33.6 0.5 %collective-permute-start.7 = (bf16[8,8,1920]{2,1,0:T(8,128)(2,1)S(1)}, bf16[8,8,1920]{2,1,0:T(8,128)(2,1)S(1)}, u32[]{:S(2)}, u32[]{:S(2)}) collective-permute-start(bf16[8,8,1920]{2,1,0:T(8,128)(2,1)S(1)} %constant_dynamic-update-slice_fusion.2.own_ref), channel_id=1, source_target_pairs={{0,1},{1,0},{2,3},{3,2},{4,5},{5,4},{6,7},{7,6},{8,9},{9,8},{10,11... | collective-permute-start | bytes 737288 | tf_op jit(solution)/shard_map/ppermute | solution.py:216
  34.2 3.7 %all-to-all-start.1 = ((f32[16,8,128]{2,1,0:T(8,128)}), f32[16,8,128]{2,1,0:T(8,128)S(1)}, u32[]{:S(2)}, u32[]{:S(2)}) async-start(f32[16,8,128]{2,1,0:T(8,128)} %get-tuple-element.29), calls=%async_computation.1 | async-start | bytes 131072 | tf_op jit(solution)/shard_map/all_to_all | solution.py:326
  37.9 0.1 pad_add_fusion.place_ref
  38.0 4.5 %weight_grad.1 = (bf16[1920,2048]{1,0:T(8,128)(2,1)}, bf16[64,4096]{1,0:T(8,128)(2,1)}) custom-call(s32[2]{0:T(128)S(1)} %pad_add_fusion.place_ref, bf16[8,8,1920]{2,1,0:T(8,128)(2,1)S(1)} %constant_dynamic-update-slice_fusion.2.own_ref, bf16[8,8,1920]{2,1,0:T(8,128)(2,1)S(1)} %collective-permute-done.7.other_ref, ...), custom_call_target="tpu_custom_call" | custom-call | flops 1006632960 | bytes 8880128 | tf_op jit(solution)/shard_map/weight_grad/pallas_call | solution.py:333
  42.5 2.3 %all-to-all-done.1 = f32[16,8,128]{2,1,0:T(8,128)S(1)} async-done(((f32[16,8,128]{2,1,0:T(8,128)}), f32[16,8,128]{2,1,0:T(8,128)S(1)}, u32[]{:S(2)}, u32[]{:S(2)}) %all-to-all-start.1) | async-done | bytes 65568 | tf_op jit(solution)/shard_map/all_to_all | solution.py:326
  44.8 0.5 %slice_reduce_fusion = f32[64]{0:T(128)} fusion(f32[16,8,128]{2,1,0:T(8,128)S(1)} %all-to-all-done.1), kind=kLoop, calls=%fused_computation.21 | loop fusion | flops 960 | bytes 4352 | tf_op jit(solution)/shard_map/reduce_sum | solution.py:353
  (30 shorter events, 0.4 us)
Async XLA Ops:
  0.6 7.5 %copy-start = (bf16[16,40960]{1,0:T(8,128)(2,1)S(1)}, bf16[16,40960]{1,0:T(8,128)(2,1)}, u32[]{:S(2)}) copy-start(bf16[16,40960]{1,0:T(8,128)(2,1)} %t_ref.1) | copy-start | bytes 3932164
  2.3 7.2 %collective-permute-start = (bf16[16,40960]{1,0:T(8,128)(2,1)}, bf16[16,40960]{1,0:T(8,128)(2,1)S(1)}, u32[]{:S(2)}, u32[]{:S(2)}) collective-permute-start(bf16[16,40960]{1,0:T(8,128)(2,1)} %t_ref.1), channel_id=1, source_target_pairs={{0,1},{1,0},{2,3},{3,2},{4,5},{5,4},{6,7},{7,6},{8,9},{9,8},{10,11... | collective-permute-start | bytes 3932168 | tf_op jit(solution)/shard_map/ppermute | solution.py:216
  2.8 5.2 %collective-permute-start.1 = (f32[2,64]{1,0:T(2,128)S(1)}, f32[2,64]{1,0:T(2,128)S(1)}, u32[]{:S(2)}, u32[]{:S(2)}) collective-permute-start(f32[2,64]{1,0:T(2,128)S(1)} %pad_maximum_fusion.1), channel_id=1, source_target_pairs={{0,1},{1,0},{2,3},{3,2},{4,5},{5,4},{6,7},{7,6},{8,9},{9,8},{10,11... | collective-permute-start | bytes 1544 | tf_op jit(solution)/shard_map/ppermute | solution.py:216
  2.9 9.3 %collective-permute-start.2 = (bf16[1,8,1920]{2,1,0:T(8,128)(2,1)}, bf16[1,8,1920]{2,1,0:T(8,128)(2,1)S(1)}, u32[]{:S(2)}, u32[]{:S(2)}) collective-permute-start(bf16[1,8,1920]{2,1,0:T(8,128)(2,1)} %bitcast.9), channel_id=1, source_target_pairs={{0,8},{2,10},{4,12},{6,14},{8,0},{10,2},{12,4},{14,6},{1,9},{3,11}... | collective-permute-start | bytes 92168 | tf_op jit(solution)/shard_map/ppermute | solution.py:220
  9.6 6.9 %copy-start.1 = (bf16[64,4096]{1,0:T(8,128)(2,1)S(1)}, bf16[64,4096]{1,0:T(8,128)(2,1)}, u32[]{:S(2)}) copy-start(bf16[64,4096]{1,0:T(8,128)(2,1)} %param.10) | copy-start | bytes 1572868
  12.2 4.5 %copy-start.2 = (bf16[8,1920]{1,0:T(8,128)(2,1)S(1)}, bf16[8,1920]{1,0:T(8,128)(2,1)}, u32[]{:S(2)}) copy-start(bf16[8,1920]{1,0:T(8,128)(2,1)} %param.11) | copy-start | bytes 92164
  12.2 20.0 %all-to-all-start = ((bf16[8,16,2176]{2,1,0:T(8,128)(2,1)}), bf16[8,16,2176]{2,1,0:T(8,128)(2,1)S(1)}, u32[]{:S(2)}, u32[]{:S(2)}) async-start(bf16[8,16,2176]{2,1,0:T(8,128)(2,1)} %map_rest.1), calls=%async_computation | async-start | bytes 1114112 | tf_op jit(solution)/shard_map/all_to_all | solution.py:296
  16.5 3.7 %collective-permute-start.3 = (bf16[64,2048]{1,0:T(8,128)(2,1)S(1)}, bf16[64,2048]{1,0:T(8,128)(2,1)S(1)}, u32[]{:S(2)}, u32[]{:S(2)}) collective-permute-start(bf16[64,2048]{1,0:T(8,128)(2,1)S(1)} %constant_dynamic-slice_fusion.1), channel_id=1, source_target_pairs={{0,1},{1,0},{2,3},{3,2},{4,5},{5,4},{6,7},{7,6},{8,9},{9,8},{10,11... | collective-permute-start | bytes 786440 | tf_op jit(solution)/shard_map/ppermute | solution.py:216
  16.7 16.7 %collective-permute-start.6 = (bf16[2,8,1920]{2,1,0:T(8,128)(2,1)S(1)}, bf16[2,8,1920]{2,1,0:T(8,128)(2,1)S(1)}, u32[]{:S(2)}, u32[]{:S(2)}) collective-permute-start(bf16[2,8,1920]{2,1,0:T(8,128)(2,1)S(1)} %constant_dynamic-update-slice_fusion), channel_id=1, source_target_pairs={{0,6},{2,4},{4,2},{6,0},{8,14},{10,12},{12,10},{14,8},{1,7},{3,5},... | collective-permute-start | bytes 184328 | tf_op jit(solution)/shard_map/ppermute | solution.py:220
  19.6 13.8 %collective-permute-start.5 = (bf16[2,8,1920]{2,1,0:T(8,128)(2,1)S(1)}, bf16[2,8,1920]{2,1,0:T(8,128)(2,1)S(1)}, u32[]{:S(2)}, u32[]{:S(2)}) collective-permute-start(bf16[2,8,1920]{2,1,0:T(8,128)(2,1)S(1)} %constant_dynamic-update-slice_fusion), channel_id=1, source_target_pairs={{0,4},{2,6},{4,0},{6,2},{8,12},{10,14},{12,8},{14,10},{1,5},{3,7},... | collective-permute-start | bytes 184328 | tf_op jit(solution)/shard_map/ppermute | solution.py:220
  20.2 13.3 %collective-permute-start.4 = (bf16[2,8,1920]{2,1,0:T(8,128)(2,1)S(1)}, bf16[2,8,1920]{2,1,0:T(8,128)(2,1)S(1)}, u32[]{:S(2)}, u32[]{:S(2)}) collective-permute-start(bf16[2,8,1920]{2,1,0:T(8,128)(2,1)S(1)} %constant_dynamic-update-slice_fusion), channel_id=1, source_target_pairs={{0,2},{2,0},{4,6},{6,4},{8,10},{10,8},{12,14},{14,12},{1,3},{3,1},... | collective-permute-start | bytes 184328 | tf_op jit(solution)/shard_map/ppermute | solution.py:220
  33.5 4.5 %collective-permute-start.8 = (bf16[64,2048]{1,0:T(8,128)(2,1)S(1)}, bf16[64,2048]{1,0:T(8,128)(2,1)S(1)}, u32[]{:S(2)}, u32[]{:S(2)}) collective-permute-start(bf16[64,2048]{1,0:T(8,128)(2,1)S(1)} %constant_dynamic-slice_fusion), channel_id=1, source_target_pairs={{0,1},{1,0},{2,3},{3,2},{4,5},{5,4},{6,7},{7,6},{8,9},{9,8},{10,11... | collective-permute-start | bytes 786440 | tf_op jit(solution)/shard_map/ppermute | solution.py:216
  33.6 4.4 %collective-permute-start.7 = (bf16[8,8,1920]{2,1,0:T(8,128)(2,1)S(1)}, bf16[8,8,1920]{2,1,0:T(8,128)(2,1)S(1)}, u32[]{:S(2)}, u32[]{:S(2)}) collective-permute-start(bf16[8,8,1920]{2,1,0:T(8,128)(2,1)S(1)} %constant_dynamic-update-slice_fusion.2.own_ref), channel_id=1, source_target_pairs={{0,1},{1,0},{2,3},{3,2},{4,5},{5,4},{6,7},{7,6},{8,9},{9,8},{10,11... | collective-permute-start | bytes 737288 | tf_op jit(solution)/shard_map/ppermute | solution.py:216
  34.2 10.6 %all-to-all-start.1 = ((f32[16,8,128]{2,1,0:T(8,128)}), f32[16,8,128]{2,1,0:T(8,128)S(1)}, u32[]{:S(2)}, u32[]{:S(2)}) async-start(f32[16,8,128]{2,1,0:T(8,128)} %get-tuple-element.29), calls=%async_computation.1 | async-start | bytes 131072 | tf_op jit(solution)/shard_map/all_to_all | solution.py:326

commit v22 on v17

--- a/solution.py
+++ b/solution.py
@@ -21,6 +21,10 @@
         hit = (row_ids == row.astype(jnp.int32)[None, :]) | (row_ids == rows + slot)
         total = total + jnp.where(hit, weight[None, :], 0.0)
     return total.astype(jnp.bfloat16)
+
+
+def turned_group(members):
+    return [(i + members // 4) % members for i in range(members)]
 
 
 def spread_tokens(t_ref, s_ref, start, count):
@@ -86,8 +90,9 @@
         return pltpu.make_async_copy(o_buf.at[q], o_ref.at[q], out_sem.at[q])
 
     def owner(q, carry):
+        member = lax.rem(q + owners // 4, owners)
         for b in range(mine):
-            first = pl.multiple_of((q * mine + b) * tokens, tokens)
+            first = pl.multiple_of((member * mine + b) * tokens, tokens)
             tile = m_ref[pl.ds(first, tokens), :] * inverse
             o_buf[q, :, b * BLK : (b + 1) * BLK] = tile.astype(jnp.bfloat16)
         o_buf[q, :, mine * BLK :] = extra
@@ -116,8 +121,14 @@
 
     def block(i, b):
         lanes = slice(b * BLK, (b + 1) * BLK)
-        group = slice(i * BLK // tokens, (i + 1) * BLK // tokens)
-        target = target_ref[group, :, lanes].reshape(BLK, BLK).astype(jnp.float32)
+        first, count = i * BLK // tokens, BLK // tokens
+        at = (first - owners // 4) % owners
+        cut = min(count, owners - at)
+        target = target_ref[at : at + cut, :, lanes].reshape(cut * tokens, BLK)
+        if cut < count:
+            rest = target_ref[: count - cut, :, lanes].reshape((count - cut) * tokens, BLK)
+            target = jnp.concatenate([target, rest], axis=0)
+        target = target.astype(jnp.float32)
         return target, logits_ref[i * BLK : (i + 1) * BLK, lanes].astype(jnp.float32)
 
     sums = []
@@ -292,7 +303,7 @@
         name="map_rest",
     )(w_rest, teacher_other, part, stats)
     outgoing, first_piece = lax.optimization_barrier((outgoing, first_piece))
-    target = lax.all_to_all(outgoing, "sv", 0, 0, tiled=True)
+    target = lax.all_to_all(outgoing, "sv", 0, 0, axis_index_groups=[turned_group(owners)], tiled=True)
 
     hidden, late_logits, outgoing = lax.optimization_barrier((hidden, student_logits, outgoing))
 
@@ -322,7 +333,8 @@
         name="logit_grad",
     )(target, logits)
 
-    terms = lax.all_to_all(terms, ("sv", "tv"), 0, 0, tiled=True)
+    everyone = [turned_group(owners * halves)]
+    terms = lax.all_to_all(terms, ("sv", "tv"), 0, 0, axis_index_groups=everyone, tiled=True)
     give = lax.dynamic_slice_in_dim(grad, (1 - half_index) * half_tokens, half_tokens, 0)
     got = swap_halves(give)
 

time: 45.7 us -> 43.9 us (0.961)
  waiting for transfers between devices: 14.1 us -> 11.2 us
  starting transfers between devices: 17 us -> 18.1 us
    all_to_all x2, waiting for transfers between devices: 14.1 us -> 11.1 us  [the longest x1 10.2 us: body(): lax.all_to_all(outgoing, 'sv', 0, 0, axis_index_groups=[turned_group(owne...]
    all_to_all x2, starting transfers between devices: 8.03 us -> 9.28 us  [the longest x1 5.06 us: body(): lax.all_to_all(outgoing, 'sv', 0, 0, axis_index_groups=[turned_group(owne...]
  transfers between devices with their start and end apart: 11 -> 11, of which waited for: 2 -> 2; matrix products, arithmetic and copies ran while one was open for 3% -> 3% of each run, Pallas kernels for 21% -> 22%
where the time goes in v22:
time: 43.9 us; the launch traced here: 43.5 us
  starting transfers between devices  18.1 us (41%)
  waiting for transfers between devices  11.2 us (26%)
  Pallas kernels  9.67 us (22%)
  other arithmetic  3.54 us (8%)
  between operations  0.84 us (2%)
    all_to_all x1, waiting for transfers between devices, body(): lax.all_to_all(outgoing, 'sv', 0, 0, axis_index_groups=[turned_group(owne...  10.2 us
    ppermute x4, starting transfers between devices, to_partner(): lax.ppermute(x, 'sv', [(s, s ^ offset) for s in range(lax.axis_size('sv'))])  7.57 us
    all_to_all x1, starting transfers between devices, body(): lax.all_to_all(outgoing, 'sv', 0, 0, axis_index_groups=[turned_group(owne...  5.06 us
    pallas_call x1, Pallas kernels, body(): pl.pallas_call(weight_kernel, out_shape=(shape((features, width), bf16),...  4.48 us
    all_to_all x1, starting transfers between devices, body(): lax.all_to_all(terms, ('sv', 'tv'), 0, 0, axis_index_groups=everyone, til...  4.22 us
    pallas_call x1, Pallas kernels, body(): pl.pallas_call(map_rest_kernel, out_shape=shape(chunk, bf16), in_specs=[i...  2.57 us
    another operation x1, other arithmetic, body(): lax.reduce((wide, jnp.ones_like(wide)), (low, jnp.float32(0)), merge, (1,))  1.68 us
    pallas_call x1, Pallas kernels, body(): pl.pallas_call(map_own_kernel, out_shape=shape((rows + MASS_ROWS, tokens...  1.4 us
  transfers between devices with their start and end apart: 11, of which 2 were waited for; matrix products, arithmetic and copies ran while one was open for 3% of the time, Pallas kernels for 22%

profile of v22, /device:TPU:0, one launch (start us, length us, event | category | flops | bytes accessed | tf_op | source)
XLA Modules:
  0.0 43.5 jit_solution(13802237954720059538)
XLA Ops:
  0.6 1.7 %convert_reduce_fusion = (f32[64]{0:T(128)S(1)}, f32[64]{0:T(128)S(1)}) fusion(bf16[64,4096]{1,0:T(8,128)(2,1)} %param.10), kind=kLoop, calls=%fused_computation | loop fusion | flops 1834624 | bytes 524800 | tf_op jit(solution)/shard_map/reduce | solution.py:266
  2.3 0.5 %collective-permute-start = (bf16[16,40960]{1,0:T(8,128)(2,1)}, bf16[16,40960]{1,0:T(8,128)(2,1)S(1)}, u32[]{:S(2)}, u32[]{:S(2)}) collective-permute-start(bf16[16,40960]{1,0:T(8,128)(2,1)} %t_ref.1), channel_id=1, source_target_pairs={{0,1},{1,0},{2,3},{3,2},{4,5},{5,4},{6,7},{7,6},{8,9},{9,8},{10,11... | collective-permute-start | bytes 3932168 | tf_op jit(solution)/shard_map/ppermute | solution.py:226
  2.8 0.1 collective-permute-start.1
  2.9 4.0 %collective-permute-start.2 = (bf16[1,8,1920]{2,1,0:T(8,128)(2,1)}, bf16[1,8,1920]{2,1,0:T(8,128)(2,1)S(1)}, u32[]{:S(2)}, u32[]{:S(2)}) collective-permute-start(bf16[1,8,1920]{2,1,0:T(8,128)(2,1)} %bitcast.9), channel_id=1, source_target_pairs={{0,8},{2,10},{4,12},{6,14},{8,0},{10,2},{12,4},{14,6},{1,9},{3,11}... | collective-permute-start | bytes 92168 | tf_op jit(solution)/shard_map/ppermute | solution.py:230
  6.9 0.7 %fusion.5 = f32[640,2]{0,1:T(2,128)S(1)} fusion(bf16[640,2]{0,1:T(2,128)(2,1)} %param.9, s32[640,2]{0,1:T(2,128)} %param.7, s32[640,2]{0,1:T(2,128)} %param.8, s32[]{:T(128)S(6)} %mul.51), kind=kLoop, calls=%fused_computation.23 | loop fusion | flops 14080 | bytes 17924 | tf_op jit(solution)/shard_map/add | solution.py:273
  7.7 0.1 dynamic-slice_bitcast_fusion
  7.8 0.2 add_convert_fusion
  8.1 0.1 pad_maximum_fusion.2.stats_ref
  8.2 1.4 %map_own.1.p_ref = f32[144,2048]{1,0:T(8,128)S(1)} custom-call(bf16[144,320]{1,0:T(8,128)(2,1)S(1)} %get-tuple-element.57.w_ref, bf16[16,40960]{1,0:T(8,128)(2,1)S(1)} %copy-done, f32[2,128]{1,0:T(2,128)S(1)} %pad_maximum_fusion.2.stats_ref), custom_call_target="tpu_custom_call" | custom-call | flops 188743680 | bytes 3145728 | tf_op jit(solution)/shard_map/map_own/pallas_call | solution.py:279
  9.6 2.6 %map_rest.1 = bf16[8,16,2176]{2,1,0:T(8,128)(2,1)} custom-call(bf16[144,320]{1,0:T(8,128)(2,1)S(1)} %get-tuple-element.58.w_ref, bf16[16,40960]{1,0:T(8,128)(2,1)S(1)} %collective-permute-done.t_ref, f32[144,2048]{1,0:T(8,128)S(1)} %map_own.1.p_ref, f32[2,128]{1,0:T(2,128)S(1)} %pad_maximum_fusion.2.stats_ref), custom_call_target="tpu_custom_call" | custom-call | flops 188743680 | bytes 4194304 | tf_op jit(solution)/shard_map/map_rest/pallas_call | solution.py:290
  12.2 5.1 %all-to-all-start = ((bf16[8,16,2176]{2,1,0:T(8,128)(2,1)}), bf16[8,16,2176]{2,1,0:T(8,128)(2,1)S(1)}, u32[]{:S(2)}, u32[]{:S(2)}) async-start(bf16[8,16,2176]{2,1,0:T(8,128)(2,1)} %map_rest.1), calls=%async_computation | async-start | bytes 1114112 | tf_op jit(solution)/shard_map/all_to_all | solution.py:306
  17.3 0.1 collective-permute-start.3
  17.4 1.5 %collective-permute-start.6 = (bf16[2,8,1920]{2,1,0:T(8,128)(2,1)S(1)}, bf16[2,8,1920]{2,1,0:T(8,128)(2,1)S(1)}, u32[]{:S(2)}, u32[]{:S(2)}) collective-permute-start(bf16[2,8,1920]{2,1,0:T(8,128)(2,1)S(1)} %constant_dynamic-update-slice_fusion), channel_id=1, source_target_pairs={{0,6},{2,4},{4,2},{6,0},{8,14},{10,12},{12,10},{14,8},{1,7},{3,5},... | collective-permute-start | bytes 184328 | tf_op jit(solution)/shard_map/ppermute | solution.py:230
  18.9 1.5 %collective-permute-start.5 = (bf16[2,8,1920]{2,1,0:T(8,128)(2,1)S(1)}, bf16[2,8,1920]{2,1,0:T(8,128)(2,1)S(1)}, u32[]{:S(2)}, u32[]{:S(2)}) collective-permute-start(bf16[2,8,1920]{2,1,0:T(8,128)(2,1)S(1)} %constant_dynamic-update-slice_fusion), channel_id=1, source_target_pairs={{0,4},{2,6},{4,0},{6,2},{8,12},{10,14},{12,8},{14,10},{1,5},{3,7},... | collective-permute-start | bytes 184328 | tf_op jit(solution)/shard_map/ppermute | solution.py:230
  20.4 0.6 %collective-permute-start.4 = (bf16[2,8,1920]{2,1,0:T(8,128)(2,1)S(1)}, bf16[2,8,1920]{2,1,0:T(8,128)(2,1)S(1)}, u32[]{:S(2)}, u32[]{:S(2)}) collective-permute-start(bf16[2,8,1920]{2,1,0:T(8,128)(2,1)S(1)} %constant_dynamic-update-slice_fusion), channel_id=1, source_target_pairs={{0,2},{2,0},{4,6},{6,4},{8,10},{10,8},{12,14},{14,12},{1,3},{3,1},... | collective-permute-start | bytes 184328 | tf_op jit(solution)/shard_map/ppermute | solution.py:230
  20.9 0.1 broadcast_select_fusion.1
  21.1 10.2 %all-to-all-done.refs_0_ = bf16[8,16,2176]{2,1,0:T(8,128)(2,1)S(1)} async-done(((bf16[8,16,2176]{2,1,0:T(8,128)(2,1)}), bf16[8,16,2176]{2,1,0:T(8,128)(2,1)S(1)}, u32[]{:S(2)}, u32[]{:S(2)}) %all-to-all-start) | async-done | bytes 557088 | tf_op jit(solution)/shard_map/all_to_all | solution.py:306
  31.3 1.2 %logit_grad.1 = (bf16[128,2048]{1,0:T(8,128)(2,1)S(1)}, f32[16,8,128]{2,1,0:T(8,128)}) custom-call(bf16[8,16,2176]{2,1,0:T(8,128)(2,1)S(1)} %all-to-all-done.refs_0_, bf16[128,2048]{1,0:T(8,128)(2,1)S(1)} %pad_maximum_fusion.refs_1_), custom_call_target="tpu_custom_call" | custom-call | flops 2621440 | bytes 1572864 | tf_op jit(solution)/shard_map/logit_grad/pallas_call | solution.py:319
  32.7 0.5 %collective-permute-start.7 = (bf16[8,8,1920]{2,1,0:T(8,128)(2,1)S(1)}, bf16[8,8,1920]{2,1,0:T(8,128)(2,1)S(1)}, u32[]{:S(2)}, u32[]{:S(2)}) collective-permute-start(bf16[8,8,1920]{2,1,0:T(8,128)(2,1)S(1)} %constant_dynamic-update-slice_fusion.2.own_ref), channel_id=1, source_target_pairs={{0,1},{1,0},{2,3},{3,2},{4,5},{5,4},{6,7},{7,6},{8,9},{9,8},{10,11... | collective-permute-start | bytes 737288 | tf_op jit(solution)/shard_map/ppermute | solution.py:226
  33.3 4.2 %all-to-all-start.1 = ((f32[16,8,128]{2,1,0:T(8,128)}), f32[16,8,128]{2,1,0:T(8,128)S(1)}, u32[]{:S(2)}, u32[]{:S(2)}) async-start(f32[16,8,128]{2,1,0:T(8,128)} %get-tuple-element.29), calls=%async_computation.1 | async-start | bytes 131072 | tf_op jit(solution)/shard_map/all_to_all | solution.py:337
  37.5 0.1 pad_add_fusion.place_ref
  37.6 4.5 %weight_grad.1 = (bf16[1920,2048]{1,0:T(8,128)(2,1)}, bf16[64,4096]{1,0:T(8,128)(2,1)}) custom-call(s32[2]{0:T(128)S(1)} %pad_add_fusion.place_ref, bf16[8,8,1920]{2,1,0:T(8,128)(2,1)S(1)} %constant_dynamic-update-slice_fusion.2.own_ref, bf16[8,8,1920]{2,1,0:T(8,128)(2,1)S(1)} %collective-permute-done.7.other_ref, ...), custom_call_target="tpu_custom_call" | custom-call | flops 1006632960 | bytes 8880128 | tf_op jit(solution)/shard_map/weight_grad/pallas_call | solution.py:344
  42.0 1.0 %all-to-all-done.1 = f32[16,8,128]{2,1,0:T(8,128)S(1)} async-done(((f32[16,8,128]{2,1,0:T(8,128)}), f32[16,8,128]{2,1,0:T(8,128)S(1)}, u32[]{:S(2)}, u32[]{:S(2)}) %all-to-all-start.1) | async-done | bytes 65568 | tf_op jit(solution)/shard_map/all_to_all | solution.py:337
  43.0 0.5 %slice_reduce_fusion = f32[64]{0:T(128)} fusion(f32[16,8,128]{2,1,0:T(8,128)S(1)} %all-to-all-done.1), kind=kLoop, calls=%fused_computation.21 | loop fusion | flops 960 | bytes 4352 | tf_op jit(solution)/shard_map/reduce_sum | solution.py:364
  (30 shorter events, 0.3 us)
Async XLA Ops:
  0.6 7.5 %copy-start = (bf16[16,40960]{1,0:T(8,128)(2,1)S(1)}, bf16[16,40960]{1,0:T(8,128)(2,1)}, u32[]{:S(2)}) copy-start(bf16[16,40960]{1,0:T(8,128)(2,1)} %t_ref.1) | copy-start | bytes 3932164
  2.3 7.2 %collective-permute-start = (bf16[16,40960]{1,0:T(8,128)(2,1)}, bf16[16,40960]{1,0:T(8,128)(2,1)S(1)}, u32[]{:S(2)}, u32[]{:S(2)}) collective-permute-start(bf16[16,40960]{1,0:T(8,128)(2,1)} %t_ref.1), channel_id=1, source_target_pairs={{0,1},{1,0},{2,3},{3,2},{4,5},{5,4},{6,7},{7,6},{8,9},{9,8},{10,11... | collective-permute-start | bytes 3932168 | tf_op jit(solution)/shard_map/ppermute | solution.py:226
  2.8 5.2 %collective-permute-start.1 = (f32[2,64]{1,0:T(2,128)S(1)}, f32[2,64]{1,0:T(2,128)S(1)}, u32[]{:S(2)}, u32[]{:S(2)}) collective-permute-start(f32[2,64]{1,0:T(2,128)S(1)} %pad_maximum_fusion.1), channel_id=1, source_target_pairs={{0,1},{1,0},{2,3},{3,2},{4,5},{5,4},{6,7},{7,6},{8,9},{9,8},{10,11... | collective-permute-start | bytes 1544 | tf_op jit(solution)/shard_map/ppermute | solution.py:226
  2.9 9.3 %collective-permute-start.2 = (bf16[1,8,1920]{2,1,0:T(8,128)(2,1)}, bf16[1,8,1920]{2,1,0:T(8,128)(2,1)S(1)}, u32[]{:S(2)}, u32[]{:S(2)}) collective-permute-start(bf16[1,8,1920]{2,1,0:T(8,128)(2,1)} %bitcast.9), channel_id=1, source_target_pairs={{0,8},{2,10},{4,12},{6,14},{8,0},{10,2},{12,4},{14,6},{1,9},{3,11}... | collective-permute-start | bytes 92168 | tf_op jit(solution)/shard_map/ppermute | solution.py:230
  9.6 7.7 %copy-start.1 = (bf16[64,4096]{1,0:T(8,128)(2,1)S(1)}, bf16[64,4096]{1,0:T(8,128)(2,1)}, u32[]{:S(2)}) copy-start(bf16[64,4096]{1,0:T(8,128)(2,1)} %param.10) | copy-start | bytes 1572868
  12.2 5.2 %copy-start.2 = (bf16[8,1920]{1,0:T(8,128)(2,1)S(1)}, bf16[8,1920]{1,0:T(8,128)(2,1)}, u32[]{:S(2)}) copy-start(bf16[8,1920]{1,0:T(8,128)(2,1)} %param.11) | copy-start | bytes 92164
  12.2 19.1 %all-to-all-start = ((bf16[8,16,2176]{2,1,0:T(8,128)(2,1)}), bf16[8,16,2176]{2,1,0:T(8,128)(2,1)S(1)}, u32[]{:S(2)}, u32[]{:S(2)}) async-start(bf16[8,16,2176]{2,1,0:T(8,128)(2,1)} %map_rest.1), calls=%async_computation | async-start | bytes 1114112 | tf_op jit(solution)/shard_map/all_to_all | solution.py:306
  17.3 3.7 %collective-permute-start.3 = (bf16[64,2048]{1,0:T(8,128)(2,1)S(1)}, bf16[64,2048]{1,0:T(8,128)(2,1)S(1)}, u32[]{:S(2)}, u32[]{:S(2)}) collective-permute-start(bf16[64,2048]{1,0:T(8,128)(2,1)S(1)} %constant_dynamic-slice_fusion.1), channel_id=1, source_target_pairs={{0,1},{1,0},{2,3},{3,2},{4,5},{5,4},{6,7},{7,6},{8,9},{9,8},{10,11... | collective-permute-start | bytes 786440 | tf_op jit(solution)/shard_map/ppermute | solution.py:226
  17.4 15.1 %collective-permute-start.6 = (bf16[2,8,1920]{2,1,0:T(8,128)(2,1)S(1)}, bf16[2,8,1920]{2,1,0:T(8,128)(2,1)S(1)}, u32[]{:S(2)}, u32[]{:S(2)}) collective-permute-start(bf16[2,8,1920]{2,1,0:T(8,128)(2,1)S(1)} %constant_dynamic-update-slice_fusion), channel_id=1, source_target_pairs={{0,6},{2,4},{4,2},{6,0},{8,14},{10,12},{12,10},{14,8},{1,7},{3,5},... | collective-permute-start | bytes 184328 | tf_op jit(solution)/shard_map/ppermute | solution.py:230
  18.9 13.6 %collective-permute-start.5 = (bf16[2,8,1920]{2,1,0:T(8,128)(2,1)S(1)}, bf16[2,8,1920]{2,1,0:T(8,128)(2,1)S(1)}, u32[]{:S(2)}, u32[]{:S(2)}) collective-permute-start(bf16[2,8,1920]{2,1,0:T(8,128)(2,1)S(1)} %constant_dynamic-update-slice_fusion), channel_id=1, source_target_pairs={{0,4},{2,6},{4,0},{6,2},{8,12},{10,14},{12,8},{14,10},{1,5},{3,7},... | collective-permute-start | bytes 184328 | tf_op jit(solution)/shard_map/ppermute | solution.py:230
  20.4 12.1 %collective-permute-start.4 = (bf16[2,8,1920]{2,1,0:T(8,128)(2,1)S(1)}, bf16[2,8,1920]{2,1,0:T(8,128)(2,1)S(1)}, u32[]{:S(2)}, u32[]{:S(2)}) collective-permute-start(bf16[2,8,1920]{2,1,0:T(8,128)(2,1)S(1)} %constant_dynamic-update-slice_fusion), channel_id=1, source_target_pairs={{0,2},{2,0},{4,6},{6,4},{8,10},{10,8},{12,14},{14,12},{1,3},{3,1},... | collective-permute-start | bytes 184328 | tf_op jit(solution)/shard_map/ppermute | solution.py:230
  32.6 5.0 %collective-permute-start.8 = (bf16[64,2048]{1,0:T(8,128)(2,1)S(1)}, bf16[64,2048]{1,0:T(8,128)(2,1)S(1)}, u32[]{:S(2)}, u32[]{:S(2)}) collective-permute-start(bf16[64,2048]{1,0:T(8,128)(2,1)S(1)} %constant_dynamic-slice_fusion), channel_id=1, source_target_pairs={{0,1},{1,0},{2,3},{3,2},{4,5},{5,4},{6,7},{7,6},{8,9},{9,8},{10,11... | collective-permute-start | bytes 786440 | tf_op jit(solution)/shard_map/ppermute | solution.py:226
  32.7 4.8 %collective-permute-start.7 = (bf16[8,8,1920]{2,1,0:T(8,128)(2,1)S(1)}, bf16[8,8,1920]{2,1,0:T(8,128)(2,1)S(1)}, u32[]{:S(2)}, u32[]{:S(2)}) collective-permute-start(bf16[8,8,1920]{2,1,0:T(8,128)(2,1)S(1)} %constant_dynamic-update-slice_fusion.2.own_ref), channel_id=1, source_target_pairs={{0,1},{1,0},{2,3},{3,2},{4,5},{5,4},{6,7},{7,6},{8,9},{9,8},{10,11... | collective-permute-start | bytes 737288 | tf_op jit(solution)/shard_map/ppermute | solution.py:226
  33.3 9.7 %all-to-all-start.1 = ((f32[16,8,128]{2,1,0:T(8,128)}), f32[16,8,128]{2,1,0:T(8,128)S(1)}, u32[]{:S(2)}, u32[]{:S(2)}) async-start(f32[16,8,128]{2,1,0:T(8,128)} %get-tuple-element.29), calls=%async_computation.1 | async-start | bytes 131072 | tf_op jit(solution)/shard_map/all_to_all | solution.py:337

commit v23 on v22

--- a/solution.py
+++ b/solution.py
@@ -23,8 +23,8 @@
     return total.astype(jnp.bfloat16)
 
 
-def turned_group(members):
-    return [(i + members // 4) % members for i in range(members)]
+def turned_group(members, first):
+    return [(i + first) % members for i in range(members)]
 
 
 def spread_tokens(t_ref, s_ref, start, count):
@@ -90,7 +90,7 @@
         return pltpu.make_async_copy(o_buf.at[q], o_ref.at[q], out_sem.at[q])
 
     def owner(q, carry):
-        member = lax.rem(q + owners // 4, owners)
+        member = lax.rem(q + owners // 2, owners)
         for b in range(mine):
             first = pl.multiple_of((member * mine + b) * tokens, tokens)
             tile = m_ref[pl.ds(first, tokens), :] * inverse
@@ -122,7 +122,7 @@
     def block(i, b):
         lanes = slice(b * BLK, (b + 1) * BLK)
         first, count = i * BLK // tokens, BLK // tokens
-        at = (first - owners // 4) % owners
+        at = (first - owners // 2) % owners
         cut = min(count, owners - at)
         target = target_ref[at : at + cut, :, lanes].reshape(cut * tokens, BLK)
         if cut < count:
@@ -303,7 +303,7 @@
         name="map_rest",
     )(w_rest, teacher_other, part, stats)
     outgoing, first_piece = lax.optimization_barrier((outgoing, first_piece))
-    target = lax.all_to_all(outgoing, "sv", 0, 0, axis_index_groups=[turned_group(owners)], tiled=True)
+    target = lax.all_to_all(outgoing, "sv", 0, 0, axis_index_groups=[turned_group(owners, owners // 2)], tiled=True)
 
     hidden, late_logits, outgoing = lax.optimization_barrier((hidden, student_logits, outgoing))
 
@@ -333,7 +333,7 @@
         name="logit_grad",
     )(target, logits)
 
-    everyone = [turned_group(owners * halves)]
+    everyone = [turned_group(owners * halves, owners // 4 * halves)]
     terms = lax.all_to_all(terms, ("sv", "tv"), 0, 0, axis_index_groups=everyone, tiled=True)
     give = lax.dynamic_slice_in_dim(grad, (1 - half_index) * half_tokens, half_tokens, 0)
     got = swap_halves(give)

time: 43.9 us -> 43.9 us (level)
  waiting for transfers between devices: 11.2 us -> 9.76 us
  starting transfers between devices: 18.1 us -> 19.5 us
    all_to_all x1, waiting for transfers between devices: 10.2 us -> 8.78 us  [body(): lax.all_to_all(outgoing, 'sv', 0, 0, axis_index_groups=[turned_group(owne...]
    all_to_all x1, starting transfers between devices: 4.22 us -> 5.4 us  [body(): lax.all_to_all(terms, ('sv', 'tv'), 0, 0, axis_index_groups=everyone, til...]
where the time goes in v23:
time: 43.9 us; the launch traced here: 43.5 us
  starting transfers between devices  19.5 us (44%)
  waiting for transfers between devices  9.76 us (22%)
  Pallas kernels  9.66 us (22%)
  other arithmetic  3.54 us (8%)
  between operations  0.84 us (2%)
    all_to_all x1, waiting for transfers between devices, body(): lax.all_to_all(outgoing, 'sv', 0, 0, axis_index_groups=[turned_group(owne...  8.78 us
    ppermute x4, starting transfers between devices, to_partner(): lax.ppermute(x, 'sv', [(s, s ^ offset) for s in range(lax.axis_size('sv'))])  7.57 us
    all_to_all x1, starting transfers between devices, body(): lax.all_to_all(terms, ('sv', 'tv'), 0, 0, axis_index_groups=everyone, til...  5.4 us
    all_to_all x1, starting transfers between devices, body(): lax.all_to_all(outgoing, 'sv', 0, 0, axis_index_groups=[turned_group(owne...  5.28 us
    pallas_call x1, Pallas kernels, body(): pl.pallas_call(weight_kernel, out_shape=(shape((features, width), bf16),...  4.48 us
    pallas_call x1, Pallas kernels, body(): pl.pallas_call(map_rest_kernel, out_shape=shape(chunk, bf16), in_specs=[i...  2.57 us
    another operation x1, other arithmetic, body(): lax.reduce((wide, jnp.ones_like(wide)), (low, jnp.float32(0)), merge, (1,))  1.68 us
    pallas_call x1, Pallas kernels, body(): pl.pallas_call(map_own_kernel, out_shape=shape((rows + MASS_ROWS, tokens...  1.4 us
  transfers between devices with their start and end apart: 11, of which 2 were waited for; matrix products, arithmetic and copies ran while one was open for 3% of the time, Pallas kernels for 22%

profile of v23, /device:TPU:0, one launch (start us, length us, event | category | flops | bytes accessed | tf_op | source)
XLA Modules:
  0.0 43.5 jit_solution(10668956887378856516)
XLA Ops:
  0.6 1.7 %convert_reduce_fusion = (f32[64]{0:T(128)S(1)}, f32[64]{0:T(128)S(1)}) fusion(bf16[64,4096]{1,0:T(8,128)(2,1)} %param.10), kind=kLoop, calls=%fused_computation | loop fusion | flops 1834624 | bytes 524800 | tf_op jit(solution)/shard_map/reduce | solution.py:266
  2.3 0.5 %collective-permute-start = (bf16[16,40960]{1,0:T(8,128)(2,1)}, bf16[16,40960]{1,0:T(8,128)(2,1)S(1)}, u32[]{:S(2)}, u32[]{:S(2)}) collective-permute-start(bf16[16,40960]{1,0:T(8,128)(2,1)} %t_ref.1), channel_id=1, source_target_pairs={{0,1},{1,0},{2,3},{3,2},{4,5},{5,4},{6,7},{7,6},{8,9},{9,8},{10,11... | collective-permute-start | bytes 3932168 | tf_op jit(solution)/shard_map/ppermute | solution.py:226
  2.8 0.1 collective-permute-start.1
  2.9 4.0 %collective-permute-start.2 = (bf16[1,8,1920]{2,1,0:T(8,128)(2,1)}, bf16[1,8,1920]{2,1,0:T(8,128)(2,1)S(1)}, u32[]{:S(2)}, u32[]{:S(2)}) collective-permute-start(bf16[1,8,1920]{2,1,0:T(8,128)(2,1)} %bitcast.9), channel_id=1, source_target_pairs={{0,8},{2,10},{4,12},{6,14},{8,0},{10,2},{12,4},{14,6},{1,9},{3,11}... | collective-permute-start | bytes 92168 | tf_op jit(solution)/shard_map/ppermute | solution.py:230
  6.9 0.7 %fusion.5 = f32[640,2]{0,1:T(2,128)S(1)} fusion(bf16[640,2]{0,1:T(2,128)(2,1)} %param.9, s32[640,2]{0,1:T(2,128)} %param.7, s32[640,2]{0,1:T(2,128)} %param.8, s32[]{:T(128)S(6)} %mul.51), kind=kLoop, calls=%fused_computation.23 | loop fusion | flops 14080 | bytes 17924 | tf_op jit(solution)/shard_map/add | solution.py:273
  7.7 0.1 dynamic-slice_bitcast_fusion
  7.8 0.2 add_convert_fusion
  8.1 0.1 pad_maximum_fusion.2.stats_ref
  8.2 1.4 %map_own.1.p_ref = f32[144,2048]{1,0:T(8,128)S(1)} custom-call(bf16[144,320]{1,0:T(8,128)(2,1)S(1)} %get-tuple-element.57.w_ref, bf16[16,40960]{1,0:T(8,128)(2,1)S(1)} %copy-done, f32[2,128]{1,0:T(2,128)S(1)} %pad_maximum_fusion.2.stats_ref), custom_call_target="tpu_custom_call" | custom-call | flops 188743680 | bytes 3145728 | tf_op jit(solution)/shard_map/map_own/pallas_call | solution.py:279
  9.6 2.6 %map_rest.1 = bf16[8,16,2176]{2,1,0:T(8,128)(2,1)} custom-call(bf16[144,320]{1,0:T(8,128)(2,1)S(1)} %get-tuple-element.58.w_ref, bf16[16,40960]{1,0:T(8,128)(2,1)S(1)} %collective-permute-done.t_ref, f32[144,2048]{1,0:T(8,128)S(1)} %map_own.1.p_ref, f32[2,128]{1,0:T(2,128)S(1)} %pad_maximum_fusion.2.stats_ref), custom_call_target="tpu_custom_call" | custom-call | flops 188743680 | bytes 4194304 | tf_op jit(solution)/shard_map/map_rest/pallas_call | solution.py:290
  12.2 5.3 %all-to-all-start = ((bf16[8,16,2176]{2,1,0:T(8,128)(2,1)}), bf16[8,16,2176]{2,1,0:T(8,128)(2,1)S(1)}, u32[]{:S(2)}, u32[]{:S(2)}) async-start(bf16[8,16,2176]{2,1,0:T(8,128)(2,1)} %map_rest.1), calls=%async_computation | async-start | bytes 1114112 | tf_op jit(solution)/shard_map/all_to_all | solution.py:306
  17.5 0.1 collective-permute-start.3
  17.6 1.5 %collective-permute-start.6 = (bf16[2,8,1920]{2,1,0:T(8,128)(2,1)S(1)}, bf16[2,8,1920]{2,1,0:T(8,128)(2,1)S(1)}, u32[]{:S(2)}, u32[]{:S(2)}) collective-permute-start(bf16[2,8,1920]{2,1,0:T(8,128)(2,1)S(1)} %constant_dynamic-update-slice_fusion), channel_id=1, source_target_pairs={{0,6},{2,4},{4,2},{6,0},{8,14},{10,12},{12,10},{14,8},{1,7},{3,5},... | collective-permute-start | bytes 184328 | tf_op jit(solution)/shard_map/ppermute | solution.py:230
  19.1 1.5 %collective-permute-start.5 = (bf16[2,8,1920]{2,1,0:T(8,128)(2,1)S(1)}, bf16[2,8,1920]{2,1,0:T(8,128)(2,1)S(1)}, u32[]{:S(2)}, u32[]{:S(2)}) collective-permute-start(bf16[2,8,1920]{2,1,0:T(8,128)(2,1)S(1)} %constant_dynamic-update-slice_fusion), channel_id=1, source_target_pairs={{0,4},{2,6},{4,0},{6,2},{8,12},{10,14},{12,8},{14,10},{1,5},{3,7},... | collective-permute-start | bytes 184328 | tf_op jit(solution)/shard_map/ppermute | solution.py:230
  20.6 0.6 %collective-permute-start.4 = (bf16[2,8,1920]{2,1,0:T(8,128)(2,1)S(1)}, bf16[2,8,1920]{2,1,0:T(8,128)(2,1)S(1)}, u32[]{:S(2)}, u32[]{:S(2)}) collective-permute-start(bf16[2,8,1920]{2,1,0:T(8,128)(2,1)S(1)} %constant_dynamic-update-slice_fusion), channel_id=1, source_target_pairs={{0,2},{2,0},{4,6},{6,4},{8,10},{10,8},{12,14},{14,12},{1,3},{3,1},... | collective-permute-start | bytes 184328 | tf_op jit(solution)/shard_map/ppermute | solution.py:230
  21.2 0.1 broadcast_select_fusion.1
  21.3 8.8 %all-to-all-done.refs_0_ = bf16[8,16,2176]{2,1,0:T(8,128)(2,1)S(1)} async-done(((bf16[8,16,2176]{2,1,0:T(8,128)(2,1)}), bf16[8,16,2176]{2,1,0:T(8,128)(2,1)S(1)}, u32[]{:S(2)}, u32[]{:S(2)}) %all-to-all-start) | async-done | bytes 557088 | tf_op jit(solution)/shard_map/all_to_all | solution.py:306
  30.1 1.2 %logit_grad.1 = (bf16[128,2048]{1,0:T(8,128)(2,1)S(1)}, f32[16,8,128]{2,1,0:T(8,128)}) custom-call(bf16[8,16,2176]{2,1,0:T(8,128)(2,1)S(1)} %all-to-all-done.refs_0_, bf16[128,2048]{1,0:T(8,128)(2,1)S(1)} %pad_maximum_fusion.refs_1_), custom_call_target="tpu_custom_call" | custom-call | flops 2621440 | bytes 1572864 | tf_op jit(solution)/shard_map/logit_grad/pallas_call | solution.py:319
  31.5 0.5 %collective-permute-start.7 = (bf16[8,8,1920]{2,1,0:T(8,128)(2,1)S(1)}, bf16[8,8,1920]{2,1,0:T(8,128)(2,1)S(1)}, u32[]{:S(2)}, u32[]{:S(2)}) collective-permute-start(bf16[8,8,1920]{2,1,0:T(8,128)(2,1)S(1)} %constant_dynamic-update-slice_fusion.2.own_ref), channel_id=1, source_target_pairs={{0,1},{1,0},{2,3},{3,2},{4,5},{5,4},{6,7},{7,6},{8,9},{9,8},{10,11... | collective-permute-start | bytes 737288 | tf_op jit(solution)/shard_map/ppermute | solution.py:226
  32.1 5.4 %all-to-all-start.1 = ((f32[16,8,128]{2,1,0:T(8,128)}), f32[16,8,128]{2,1,0:T(8,128)S(1)}, u32[]{:S(2)}, u32[]{:S(2)}) async-start(f32[16,8,128]{2,1,0:T(8,128)} %get-tuple-element.29), calls=%async_computation.1 | async-start | bytes 131072 | tf_op jit(solution)/shard_map/all_to_all | solution.py:337
  37.5 0.1 pad_add_fusion.place_ref
  37.6 4.5 %weight_grad.1 = (bf16[1920,2048]{1,0:T(8,128)(2,1)}, bf16[64,4096]{1,0:T(8,128)(2,1)}) custom-call(s32[2]{0:T(128)S(1)} %pad_add_fusion.place_ref, bf16[8,8,1920]{2,1,0:T(8,128)(2,1)S(1)} %constant_dynamic-update-slice_fusion.2.own_ref, bf16[8,8,1920]{2,1,0:T(8,128)(2,1)S(1)} %collective-permute-done.7.other_ref, ...), custom_call_target="tpu_custom_call" | custom-call | flops 1006632960 | bytes 8880128 | tf_op jit(solution)/shard_map/weight_grad/pallas_call | solution.py:344
  42.0 1.0 %all-to-all-done.1 = f32[16,8,128]{2,1,0:T(8,128)S(1)} async-done(((f32[16,8,128]{2,1,0:T(8,128)}), f32[16,8,128]{2,1,0:T(8,128)S(1)}, u32[]{:S(2)}, u32[]{:S(2)}) %all-to-all-start.1) | async-done | bytes 65568 | tf_op jit(solution)/shard_map/all_to_all | solution.py:337
  43.0 0.5 %slice_reduce_fusion = f32[64]{0:T(128)} fusion(f32[16,8,128]{2,1,0:T(8,128)S(1)} %all-to-all-done.1), kind=kLoop, calls=%fused_computation.21 | loop fusion | flops 960 | bytes 4352 | tf_op jit(solution)/shard_map/reduce_sum | solution.py:364
  (30 shorter events, 0.3 us)
Async XLA Ops:
  0.6 7.5 %copy-start = (bf16[16,40960]{1,0:T(8,128)(2,1)S(1)}, bf16[16,40960]{1,0:T(8,128)(2,1)}, u32[]{:S(2)}) copy-start(bf16[16,40960]{1,0:T(8,128)(2,1)} %t_ref.1) | copy-start | bytes 3932164
  2.3 7.2 %collective-permute-start = (bf16[16,40960]{1,0:T(8,128)(2,1)}, bf16[16,40960]{1,0:T(8,128)(2,1)S(1)}, u32[]{:S(2)}, u32[]{:S(2)}) collective-permute-start(bf16[16,40960]{1,0:T(8,128)(2,1)} %t_ref.1), channel_id=1, source_target_pairs={{0,1},{1,0},{2,3},{3,2},{4,5},{5,4},{6,7},{7,6},{8,9},{9,8},{10,11... | collective-permute-start | bytes 3932168 | tf_op jit(solution)/shard_map/ppermute | solution.py:226
  2.8 5.2 %collective-permute-start.1 = (f32[2,64]{1,0:T(2,128)S(1)}, f32[2,64]{1,0:T(2,128)S(1)}, u32[]{:S(2)}, u32[]{:S(2)}) collective-permute-start(f32[2,64]{1,0:T(2,128)S(1)} %pad_maximum_fusion.1), channel_id=1, source_target_pairs={{0,1},{1,0},{2,3},{3,2},{4,5},{5,4},{6,7},{7,6},{8,9},{9,8},{10,11... | collective-permute-start | bytes 1544 | tf_op jit(solution)/shard_map/ppermute | solution.py:226
  2.9 9.3 %collective-permute-start.2 = (bf16[1,8,1920]{2,1,0:T(8,128)(2,1)}, bf16[1,8,1920]{2,1,0:T(8,128)(2,1)S(1)}, u32[]{:S(2)}, u32[]{:S(2)}) collective-permute-start(bf16[1,8,1920]{2,1,0:T(8,128)(2,1)} %bitcast.9), channel_id=1, source_target_pairs={{0,8},{2,10},{4,12},{6,14},{8,0},{10,2},{12,4},{14,6},{1,9},{3,11}... | collective-permute-start | bytes 92168 | tf_op jit(solution)/shard_map/ppermute | solution.py:230
  9.6 7.9 %copy-start.1 = (bf16[64,4096]{1,0:T(8,128)(2,1)S(1)}, bf16[64,4096]{1,0:T(8,128)(2,1)}, u32[]{:S(2)}) copy-start(bf16[64,4096]{1,0:T(8,128)(2,1)} %param.10) | copy-start | bytes 1572868
  12.2 5.4 %copy-start.2 = (bf16[8,1920]{1,0:T(8,128)(2,1)S(1)}, bf16[8,1920]{1,0:T(8,128)(2,1)}, u32[]{:S(2)}) copy-start(bf16[8,1920]{1,0:T(8,128)(2,1)} %param.11) | copy-start | bytes 92164
  12.2 17.9 %all-to-all-start = ((bf16[8,16,2176]{2,1,0:T(8,128)(2,1)}), bf16[8,16,2176]{2,1,0:T(8,128)(2,1)S(1)}, u32[]{:S(2)}, u32[]{:S(2)}) async-start(bf16[8,16,2176]{2,1,0:T(8,128)(2,1)} %map_rest.1), calls=%async_computation | async-start | bytes 1114112 | tf_op jit(solution)/shard_map/all_to_all | solution.py:306
  17.5 3.7 %collective-permute-start.3 = (bf16[64,2048]{1,0:T(8,128)(2,1)S(1)}, bf16[64,2048]{1,0:T(8,128)(2,1)S(1)}, u32[]{:S(2)}, u32[]{:S(2)}) collective-permute-start(bf16[64,2048]{1,0:T(8,128)(2,1)S(1)} %constant_dynamic-slice_fusion.1), channel_id=1, source_target_pairs={{0,1},{1,0},{2,3},{3,2},{4,5},{5,4},{6,7},{7,6},{8,9},{9,8},{10,11... | collective-permute-start | bytes 786440 | tf_op jit(solution)/shard_map/ppermute | solution.py:226
  17.6 13.7 %collective-permute-start.6 = (bf16[2,8,1920]{2,1,0:T(8,128)(2,1)S(1)}, bf16[2,8,1920]{2,1,0:T(8,128)(2,1)S(1)}, u32[]{:S(2)}, u32[]{:S(2)}) collective-permute-start(bf16[2,8,1920]{2,1,0:T(8,128)(2,1)S(1)} %constant_dynamic-update-slice_fusion), channel_id=1, source_target_pairs={{0,6},{2,4},{4,2},{6,0},{8,14},{10,12},{12,10},{14,8},{1,7},{3,5},... | collective-permute-start | bytes 184328 | tf_op jit(solution)/shard_map/ppermute | solution.py:230
  19.1 12.2 %collective-permute-start.5 = (bf16[2,8,1920]{2,1,0:T(8,128)(2,1)S(1)}, bf16[2,8,1920]{2,1,0:T(8,128)(2,1)S(1)}, u32[]{:S(2)}, u32[]{:S(2)}) collective-permute-start(bf16[2,8,1920]{2,1,0:T(8,128)(2,1)S(1)} %constant_dynamic-update-slice_fusion), channel_id=1, source_target_pairs={{0,4},{2,6},{4,0},{6,2},{8,12},{10,14},{12,8},{14,10},{1,5},{3,7},... | collective-permute-start | bytes 184328 | tf_op jit(solution)/shard_map/ppermute | solution.py:230
  20.6 10.8 %collective-permute-start.4 = (bf16[2,8,1920]{2,1,0:T(8,128)(2,1)S(1)}, bf16[2,8,1920]{2,1,0:T(8,128)(2,1)S(1)}, u32[]{:S(2)}, u32[]{:S(2)}) collective-permute-start(bf16[2,8,1920]{2,1,0:T(8,128)(2,1)S(1)} %constant_dynamic-update-slice_fusion), channel_id=1, source_target_pairs={{0,2},{2,0},{4,6},{6,4},{8,10},{10,8},{12,14},{14,12},{1,3},{3,1},... | collective-permute-start | bytes 184328 | tf_op jit(solution)/shard_map/ppermute | solution.py:230
  31.4 6.2 %collective-permute-start.8 = (bf16[64,2048]{1,0:T(8,128)(2,1)S(1)}, bf16[64,2048]{1,0:T(8,128)(2,1)S(1)}, u32[]{:S(2)}, u32[]{:S(2)}) collective-permute-start(bf16[64,2048]{1,0:T(8,128)(2,1)S(1)} %constant_dynamic-slice_fusion), channel_id=1, source_target_pairs={{0,1},{1,0},{2,3},{3,2},{4,5},{5,4},{6,7},{7,6},{8,9},{9,8},{10,11... | collective-permute-start | bytes 786440 | tf_op jit(solution)/shard_map/ppermute | solution.py:226
  31.5 6.0 %collective-permute-start.7 = (bf16[8,8,1920]{2,1,0:T(8,128)(2,1)S(1)}, bf16[8,8,1920]{2,1,0:T(8,128)(2,1)S(1)}, u32[]{:S(2)}, u32[]{:S(2)}) collective-permute-start(bf16[8,8,1920]{2,1,0:T(8,128)(2,1)S(1)} %constant_dynamic-update-slice_fusion.2.own_ref), channel_id=1, source_target_pairs={{0,1},{1,0},{2,3},{3,2},{4,5},{5,4},{6,7},{7,6},{8,9},{9,8},{10,11... | collective-permute-start | bytes 737288 | tf_op jit(solution)/shard_map/ppermute | solution.py:226
  32.1 10.9 %all-to-all-start.1 = ((f32[16,8,128]{2,1,0:T(8,128)}), f32[16,8,128]{2,1,0:T(8,128)S(1)}, u32[]{:S(2)}, u32[]{:S(2)}) async-start(f32[16,8,128]{2,1,0:T(8,128)} %get-tuple-element.29), calls=%async_computation.1 | async-start | bytes 131072 | tf_op jit(solution)/shard_map/all_to_all | solution.py:337

commit v24 on v23

--- a/solution.py
+++ b/solution.py
@@ -166,16 +166,16 @@
 
 
 def weight_kernel(
-    place_ref, own_ref, other_ref, grad_ref, got_ref, o_ref, joined_ref, s_ref, h_ref, block_ref, sems, join_sems
+    place_ref, own_ref, got_ref, grad_ref, o_ref, joined_ref, s_ref, h_ref, block_ref, sems, join_sems
 ):
-    half_tokens, width = got_ref.shape
+    half_tokens, width = got_ref.shape[0], grad_ref.shape[1]
     half = place_ref[1]
     kept_at = pl.ds(pl.multiple_of(half * width, width), width)
     got_at = pl.ds(pl.multiple_of((1 - half) * width, width), width)
     kept = pl.ds(pl.multiple_of(half * half_tokens, half_tokens), half_tokens)
     copies = [
         pltpu.make_async_copy(grad_ref.at[kept, :], joined_ref.at[:, kept_at], join_sems.at[0]),
-        pltpu.make_async_copy(got_ref, joined_ref.at[:, got_at], join_sems.at[1]),
+        pltpu.make_async_copy(got_ref.at[:, pl.ds(0, width)], joined_ref.at[:, got_at], join_sems.at[1]),
     ]
     for copy in copies:
         copy.start()
@@ -185,7 +185,8 @@
         own = pl.ds(pl.multiple_of((first + half) * held, held), held)
         other = pl.ds(pl.multiple_of((first + 1 - half) * held, held), held)
         s_ref[own, :] = own_ref[i].astype(jnp.float32)
-        s_ref[other, :] = other_ref[i].astype(jnp.float32)
+        pair = got_ref[i // 2 * 2 * held : (i // 2 + 1) * 2 * held, width:].astype(jnp.float32)
+        s_ref[other, :] = pair[i % 2 * held : (i % 2 + 1) * held]
     for i in range(s_ref.shape[0] // BLK):
         for j in range(features // BLK):
             tile = s_ref[i * BLK : (i + 1) * BLK, j * BLK : (j + 1) * BLK].T
@@ -335,16 +336,15 @@
 
     everyone = [turned_group(owners * halves, owners // 4 * halves)]
     terms = lax.all_to_all(terms, ("sv", "tv"), 0, 0, axis_index_groups=everyone, tiled=True)
+    *pieces, grad = lax.optimization_barrier((*pieces, grad))
     give = lax.dynamic_slice_in_dim(grad, (1 - half_index) * half_tokens, half_tokens, 0)
-    got = swap_halves(give)
-
-    *pieces, grad = lax.optimization_barrier((*pieces, grad))
     hidden_own = jnp.concatenate(pieces)
+    got = swap_halves(jnp.concatenate([give, hidden_own.reshape(half_tokens, features)], axis=1))
     steps = 8
     weight_grad, logit_grad = pl.pallas_call(
         weight_kernel,
         out_shape=(shape((features, width), bf16), shape((half_tokens, columns), bf16)),
-        in_specs=[scalars()] + [in_vmem()] * 4,
+        in_specs=[scalars()] + [in_vmem()] * 3,
         out_specs=(anywhere(), anywhere()),
         scratch_shapes=[
             pltpu.VMEM((group_tokens, features), f32),
@@ -359,7 +359,7 @@
             2 * (features * width + group_tokens * (features + width)),
         ),
         name="weight_grad",
-    )(place, hidden_own, swap_halves(hidden_own), grad, got)
+    )(place, hidden_own, got, grad)
     terms, logit_grad, weight_grad = lax.optimization_barrier((terms, logit_grad, weight_grad))
     divergence = jnp.sum(terms[:, 0, :half_tokens], axis=0)
     return (divergence, logit_grad, weight_grad)

time: 43.9 us -> 43.5 us (level)
    ppermute x5 -> x4, starting transfers between devices: 1.28 us -> 0.73 us  [swap_halves(): return lax.ppermute(x, 'tv', [(0, 1), (1, 0)])]
  transfers between devices with their start and end apart: 11 -> 10, of which waited for: 2 -> 2; matrix products, arithmetic and copies ran while one was open for 3% -> 3% of each run, Pallas kernels for 22% -> 22%
where the time goes in v24:
time: 43.5 us; the launch traced here: 43.1 us
  starting transfers between devices  19.1 us (44%)
  waiting for transfers between devices  9.76 us (22%)
  Pallas kernels  9.66 us (22%)
  other arithmetic  3.58 us (8%)
  between operations  0.85 us (2%)
    all_to_all x1, waiting for transfers between devices, body(): lax.all_to_all(outgoing, 'sv', 0, 0, axis_index_groups=[turned_group(owne...  8.78 us
    ppermute x4, starting transfers between devices, to_partner(): lax.ppermute(x, 'sv', [(s, s ^ offset) for s in range(lax.axis_size('sv'))])  7.57 us
    all_to_all x1, starting transfers between devices, body(): lax.all_to_all(terms, ('sv', 'tv'), 0, 0, axis_index_groups=everyone, til...  5.5 us
    all_to_all x1, starting transfers between devices, body(): lax.all_to_all(outgoing, 'sv', 0, 0, axis_index_groups=[turned_group(owne...  5.28 us
    pallas_call x1, Pallas kernels, body(): pl.pallas_call(weight_kernel, out_shape=(shape((features, width), bf16),...  4.48 us
    pallas_call x1, Pallas kernels, body(): pl.pallas_call(map_rest_kernel, out_shape=shape(chunk, bf16), in_specs=[i...  2.57 us
    another operation x1, other arithmetic, body(): lax.reduce((wide, jnp.ones_like(wide)), (low, jnp.float32(0)), merge, (1,))  1.68 us
    pallas_call x1, Pallas kernels, body(): pl.pallas_call(map_own_kernel, out_shape=shape((rows + MASS_ROWS, tokens...  1.4 us
  transfers between devices with their start and end apart: 10, of which 2 were waited for; matrix products, arithmetic and copies ran while one was open for 3% of the time, Pallas kernels for 22%

profile of v24, /device:TPU:0, one launch (start us, length us, event | category | flops | bytes accessed | tf_op | source)
XLA Modules:
  0.0 43.1 jit_solution(1379641229401367566)
XLA Ops:
  0.6 1.7 %convert_reduce_fusion = (f32[64]{0:T(128)S(1)}, f32[64]{0:T(128)S(1)}) fusion(bf16[64,4096]{1,0:T(8,128)(2,1)} %param.10), kind=kLoop, calls=%fused_computation | loop fusion | flops 1834624 | bytes 524800 | tf_op jit(solution)/shard_map/reduce | solution.py:267
  2.3 0.5 %collective-permute-start = (bf16[16,40960]{1,0:T(8,128)(2,1)}, bf16[16,40960]{1,0:T(8,128)(2,1)S(1)}, u32[]{:S(2)}, u32[]{:S(2)}) collective-permute-start(bf16[16,40960]{1,0:T(8,128)(2,1)} %t_ref.1), channel_id=1, source_target_pairs={{0,1},{1,0},{2,3},{3,2},{4,5},{5,4},{6,7},{7,6},{8,9},{9,8},{10,11... | collective-permute-start | bytes 3932168 | tf_op jit(solution)/shard_map/ppermute | solution.py:227
  2.8 0.1 collective-permute-start.1
  2.9 4.0 %collective-permute-start.2 = (bf16[1,8,1920]{2,1,0:T(8,128)(2,1)}, bf16[1,8,1920]{2,1,0:T(8,128)(2,1)S(1)}, u32[]{:S(2)}, u32[]{:S(2)}) collective-permute-start(bf16[1,8,1920]{2,1,0:T(8,128)(2,1)} %bitcast.11), channel_id=1, source_target_pairs={{0,8},{2,10},{4,12},{6,14},{8,0},{10,2},{12,4},{14,6},{1,9},{3,11}... | collective-permute-start | bytes 92168 | tf_op jit(solution)/shard_map/ppermute | solution.py:231
  6.9 0.7 %fusion.5 = f32[640,2]{0,1:T(2,128)S(1)} fusion(bf16[640,2]{0,1:T(2,128)(2,1)} %param.9, s32[640,2]{0,1:T(2,128)} %param.7, s32[640,2]{0,1:T(2,128)} %param.8, s32[]{:T(128)S(6)} %mul.51), kind=kLoop, calls=%fused_computation.24 | loop fusion | flops 14080 | bytes 17924 | tf_op jit(solution)/shard_map/add | solution.py:274
  7.7 0.1 dynamic-slice_bitcast_fusion
  7.8 0.2 add_convert_fusion
  8.1 0.1 pad_maximum_fusion.3.stats_ref
  8.2 1.4 %map_own.1.p_ref = f32[144,2048]{1,0:T(8,128)S(1)} custom-call(bf16[144,320]{1,0:T(8,128)(2,1)S(1)} %get-tuple-element.57.w_ref, bf16[16,40960]{1,0:T(8,128)(2,1)S(1)} %copy-done, f32[2,128]{1,0:T(2,128)S(1)} %pad_maximum_fusion.3.stats_ref), custom_call_target="tpu_custom_call" | custom-call | flops 188743680 | bytes 3145728 | tf_op jit(solution)/shard_map/map_own/pallas_call | solution.py:280
  9.6 2.6 %map_rest.1 = bf16[8,16,2176]{2,1,0:T(8,128)(2,1)} custom-call(bf16[144,320]{1,0:T(8,128)(2,1)S(1)} %get-tuple-element.58.w_ref, bf16[16,40960]{1,0:T(8,128)(2,1)S(1)} %collective-permute-done.t_ref, f32[144,2048]{1,0:T(8,128)S(1)} %map_own.1.p_ref, f32[2,128]{1,0:T(2,128)S(1)} %pad_maximum_fusion.3.stats_ref), custom_call_target="tpu_custom_call" | custom-call | flops 188743680 | bytes 4194304 | tf_op jit(solution)/shard_map/map_rest/pallas_call | solution.py:291
  12.2 5.3 %all-to-all-start = ((bf16[8,16,2176]{2,1,0:T(8,128)(2,1)}), bf16[8,16,2176]{2,1,0:T(8,128)(2,1)S(1)}, u32[]{:S(2)}, u32[]{:S(2)}) async-start(bf16[8,16,2176]{2,1,0:T(8,128)(2,1)} %map_rest.1), calls=%async_computation | async-start | bytes 1114112 | tf_op jit(solution)/shard_map/all_to_all | solution.py:307
  17.5 0.1 collective-permute-start.3
  17.6 1.5 %collective-permute-start.6 = (bf16[2,8,1920]{2,1,0:T(8,128)(2,1)S(1)}, bf16[2,8,1920]{2,1,0:T(8,128)(2,1)S(1)}, u32[]{:S(2)}, u32[]{:S(2)}) collective-permute-start(bf16[2,8,1920]{2,1,0:T(8,128)(2,1)S(1)} %constant_dynamic-update-slice_fusion), channel_id=1, source_target_pairs={{0,6},{2,4},{4,2},{6,0},{8,14},{10,12},{12,10},{14,8},{1,7},{3,5},... | collective-permute-start | bytes 184328 | tf_op jit(solution)/shard_map/ppermute | solution.py:231
  19.1 1.5 %collective-permute-start.5 = (bf16[2,8,1920]{2,1,0:T(8,128)(2,1)S(1)}, bf16[2,8,1920]{2,1,0:T(8,128)(2,1)S(1)}, u32[]{:S(2)}, u32[]{:S(2)}) collective-permute-start(bf16[2,8,1920]{2,1,0:T(8,128)(2,1)S(1)} %constant_dynamic-update-slice_fusion), channel_id=1, source_target_pairs={{0,4},{2,6},{4,0},{6,2},{8,12},{10,14},{12,8},{14,10},{1,5},{3,7},... | collective-permute-start | bytes 184328 | tf_op jit(solution)/shard_map/ppermute | solution.py:231
  20.6 0.6 %collective-permute-start.4 = (bf16[2,8,1920]{2,1,0:T(8,128)(2,1)S(1)}, bf16[2,8,1920]{2,1,0:T(8,128)(2,1)S(1)}, u32[]{:S(2)}, u32[]{:S(2)}) collective-permute-start(bf16[2,8,1920]{2,1,0:T(8,128)(2,1)S(1)} %constant_dynamic-update-slice_fusion), channel_id=1, source_target_pairs={{0,2},{2,0},{4,6},{6,4},{8,10},{10,8},{12,14},{14,12},{1,3},{3,1},... | collective-permute-start | bytes 184328 | tf_op jit(solution)/shard_map/ppermute | solution.py:231
  21.2 0.1 broadcast_select_fusion.1
  21.3 8.8 %all-to-all-done.refs_0_ = bf16[8,16,2176]{2,1,0:T(8,128)(2,1)S(1)} async-done(((bf16[8,16,2176]{2,1,0:T(8,128)(2,1)}), bf16[8,16,2176]{2,1,0:T(8,128)(2,1)S(1)}, u32[]{:S(2)}, u32[]{:S(2)}) %all-to-all-start) | async-done | bytes 557088 | tf_op jit(solution)/shard_map/all_to_all | solution.py:307
  30.1 1.2 %logit_grad.1 = (bf16[128,2048]{1,0:T(8,128)(2,1)S(1)}, f32[16,8,128]{2,1,0:T(8,128)}) custom-call(bf16[8,16,2176]{2,1,0:T(8,128)(2,1)S(1)} %all-to-all-done.refs_0_, bf16[128,2048]{1,0:T(8,128)(2,1)S(1)} %pad_maximum_fusion.refs_1_), custom_call_target="tpu_custom_call" | custom-call | flops 2621440 | bytes 1572864 | tf_op jit(solution)/shard_map/logit_grad/pallas_call | solution.py:320
  31.5 0.1 collective-permute-start.7
  31.6 5.5 %all-to-all-start.1 = ((f32[16,8,128]{2,1,0:T(8,128)}), f32[16,8,128]{2,1,0:T(8,128)S(1)}, u32[]{:S(2)}, u32[]{:S(2)}) async-start(f32[16,8,128]{2,1,0:T(8,128)} %get-tuple-element.29), calls=%async_computation.1 | async-start | bytes 131072 | tf_op jit(solution)/shard_map/all_to_all | solution.py:338
  37.1 0.1 pad_add_fusion.place_ref
  37.2 4.5 %weight_grad.1 = (bf16[1920,2048]{1,0:T(8,128)(2,1)}, bf16[64,4096]{1,0:T(8,128)(2,1)}) custom-call(s32[2]{0:T(128)S(1)} %pad_add_fusion.place_ref, bf16[8,8,1920]{2,1,0:T(8,128)(2,1)S(1)} %constant_dynamic-update-slice_fusion.2.own_ref, bf16[64,3968]{1,0:T(8,128)(2,1)S(1)} %collective-permute-done.7.got_ref, bf16[128,2048]{1,0:T(8,128)(2,1)S(1)} %get-tuple-element.37.grad_ref), custom_call_target="tpu_custom_call" | custom-call | flops 1006632960 | bytes 8880128 | tf_op jit(solution)/shard_map/weight_grad/pallas_call | solution.py:344
  41.6 1.0 %all-to-all-done.1 = f32[16,8,128]{2,1,0:T(8,128)S(1)} async-done(((f32[16,8,128]{2,1,0:T(8,128)}), f32[16,8,128]{2,1,0:T(8,128)S(1)}, u32[]{:S(2)}, u32[]{:S(2)}) %all-to-all-start.1) | async-done | bytes 65568 | tf_op jit(solution)/shard_map/all_to_all | solution.py:338
  42.6 0.5 %slice_reduce_fusion = f32[64]{0:T(128)} fusion(f32[16,8,128]{2,1,0:T(8,128)S(1)} %all-to-all-done.1), kind=kLoop, calls=%fused_computation.22 | loop fusion | flops 960 | bytes 4352 | tf_op jit(solution)/shard_map/reduce_sum | solution.py:364
  (29 shorter events, 0.3 us)
Async XLA Ops:
  0.6 7.5 %copy-start = (bf16[16,40960]{1,0:T(8,128)(2,1)S(1)}, bf16[16,40960]{1,0:T(8,128)(2,1)}, u32[]{:S(2)}) copy-start(bf16[16,40960]{1,0:T(8,128)(2,1)} %t_ref.1) | copy-start | bytes 3932164
  2.3 7.2 %collective-permute-start = (bf16[16,40960]{1,0:T(8,128)(2,1)}, bf16[16,40960]{1,0:T(8,128)(2,1)S(1)}, u32[]{:S(2)}, u32[]{:S(2)}) collective-permute-start(bf16[16,40960]{1,0:T(8,128)(2,1)} %t_ref.1), channel_id=1, source_target_pairs={{0,1},{1,0},{2,3},{3,2},{4,5},{5,4},{6,7},{7,6},{8,9},{9,8},{10,11... | collective-permute-start | bytes 3932168 | tf_op jit(solution)/shard_map/ppermute | solution.py:227
  2.8 5.2 %collective-permute-start.1 = (f32[2,64]{1,0:T(2,128)S(1)}, f32[2,64]{1,0:T(2,128)S(1)}, u32[]{:S(2)}, u32[]{:S(2)}) collective-permute-start(f32[2,64]{1,0:T(2,128)S(1)} %pad_maximum_fusion.2), channel_id=1, source_target_pairs={{0,1},{1,0},{2,3},{3,2},{4,5},{5,4},{6,7},{7,6},{8,9},{9,8},{10,11... | collective-permute-start | bytes 1544 | tf_op jit(solution)/shard_map/ppermute | solution.py:227
  2.9 9.3 %collective-permute-start.2 = (bf16[1,8,1920]{2,1,0:T(8,128)(2,1)}, bf16[1,8,1920]{2,1,0:T(8,128)(2,1)S(1)}, u32[]{:S(2)}, u32[]{:S(2)}) collective-permute-start(bf16[1,8,1920]{2,1,0:T(8,128)(2,1)} %bitcast.11), channel_id=1, source_target_pairs={{0,8},{2,10},{4,12},{6,14},{8,0},{10,2},{12,4},{14,6},{1,9},{3,11}... | collective-permute-start | bytes 92168 | tf_op jit(solution)/shard_map/ppermute | solution.py:231
  9.6 7.9 %copy-start.1 = (bf16[64,4096]{1,0:T(8,128)(2,1)S(1)}, bf16[64,4096]{1,0:T(8,128)(2,1)}, u32[]{:S(2)}) copy-start(bf16[64,4096]{1,0:T(8,128)(2,1)} %param.10) | copy-start | bytes 1572868
  12.2 5.4 %copy-start.2 = (bf16[8,1920]{1,0:T(8,128)(2,1)S(1)}, bf16[8,1920]{1,0:T(8,128)(2,1)}, u32[]{:S(2)}) copy-start(bf16[8,1920]{1,0:T(8,128)(2,1)} %param.11) | copy-start | bytes 92164
  12.2 17.9 %all-to-all-start = ((bf16[8,16,2176]{2,1,0:T(8,128)(2,1)}), bf16[8,16,2176]{2,1,0:T(8,128)(2,1)S(1)}, u32[]{:S(2)}, u32[]{:S(2)}) async-start(bf16[8,16,2176]{2,1,0:T(8,128)(2,1)} %map_rest.1), calls=%async_computation | async-start | bytes 1114112 | tf_op jit(solution)/shard_map/all_to_all | solution.py:307
  17.5 3.7 %collective-permute-start.3 = (bf16[64,2048]{1,0:T(8,128)(2,1)S(1)}, bf16[64,2048]{1,0:T(8,128)(2,1)S(1)}, u32[]{:S(2)}, u32[]{:S(2)}) collective-permute-start(bf16[64,2048]{1,0:T(8,128)(2,1)S(1)} %constant_dynamic-slice_fusion.1), channel_id=1, source_target_pairs={{0,1},{1,0},{2,3},{3,2},{4,5},{5,4},{6,7},{7,6},{8,9},{9,8},{10,11... | collective-permute-start | bytes 786440 | tf_op jit(solution)/shard_map/ppermute | solution.py:227
  17.6 13.7 %collective-permute-start.6 = (bf16[2,8,1920]{2,1,0:T(8,128)(2,1)S(1)}, bf16[2,8,1920]{2,1,0:T(8,128)(2,1)S(1)}, u32[]{:S(2)}, u32[]{:S(2)}) collective-permute-start(bf16[2,8,1920]{2,1,0:T(8,128)(2,1)S(1)} %constant_dynamic-update-slice_fusion), channel_id=1, source_target_pairs={{0,6},{2,4},{4,2},{6,0},{8,14},{10,12},{12,10},{14,8},{1,7},{3,5},... | collective-permute-start | bytes 184328 | tf_op jit(solution)/shard_map/ppermute | solution.py:231
  19.1 12.2 %collective-permute-start.5 = (bf16[2,8,1920]{2,1,0:T(8,128)(2,1)S(1)}, bf16[2,8,1920]{2,1,0:T(8,128)(2,1)S(1)}, u32[]{:S(2)}, u32[]{:S(2)}) collective-permute-start(bf16[2,8,1920]{2,1,0:T(8,128)(2,1)S(1)} %constant_dynamic-update-slice_fusion), channel_id=1, source_target_pairs={{0,4},{2,6},{4,0},{6,2},{8,12},{10,14},{12,8},{14,10},{1,5},{3,7},... | collective-permute-start | bytes 184328 | tf_op jit(solution)/shard_map/ppermute | solution.py:231
  20.6 10.8 %collective-permute-start.4 = (bf16[2,8,1920]{2,1,0:T(8,128)(2,1)S(1)}, bf16[2,8,1920]{2,1,0:T(8,128)(2,1)S(1)}, u32[]{:S(2)}, u32[]{:S(2)}) collective-permute-start(bf16[2,8,1920]{2,1,0:T(8,128)(2,1)S(1)} %constant_dynamic-update-slice_fusion), channel_id=1, source_target_pairs={{0,2},{2,0},{4,6},{6,4},{8,10},{10,8},{12,14},{14,12},{1,3},{3,1},... | collective-permute-start | bytes 184328 | tf_op jit(solution)/shard_map/ppermute | solution.py:231
  31.5 5.7 %collective-permute-start.7 = (bf16[64,3968]{1,0:T(8,128)(2,1)S(1)}, bf16[64,3968]{1,0:T(8,128)(2,1)S(1)}, u32[]{:S(2)}, u32[]{:S(2)}) collective-permute-start(bf16[64,3968]{1,0:T(8,128)(2,1)S(1)} %pad_maximum_fusion.1), channel_id=1, source_target_pairs={{0,1},{1,0},{2,3},{3,2},{4,5},{5,4},{6,7},{7,6},{8,9},{9,8},{10,11... | collective-permute-start | bytes 1523720 | tf_op jit(solution)/shard_map/ppermute | solution.py:227
  31.6 11.0 %all-to-all-start.1 = ((f32[16,8,128]{2,1,0:T(8,128)}), f32[16,8,128]{2,1,0:T(8,128)S(1)}, u32[]{:S(2)}, u32[]{:S(2)}) async-start(f32[16,8,128]{2,1,0:T(8,128)} %get-tuple-element.29), calls=%async_computation.1 | async-start | bytes 131072 | tf_op jit(solution)/shard_map/all_to_all | solution.py:338

commit v25 on v24

--- a/solution.py
+++ b/solution.py
@@ -334,7 +334,7 @@
         name="logit_grad",
     )(target, logits)
 
-    everyone = [turned_group(owners * halves, owners // 4 * halves)]
+    everyone = [turned_group(owners * halves, owners // 2 * halves)]
     terms = lax.all_to_all(terms, ("sv", "tv"), 0, 0, axis_index_groups=everyone, tiled=True)
     *pieces, grad = lax.optimization_barrier((*pieces, grad))
     give = lax.dynamic_slice_in_dim(grad, (1 - half_index) * half_tokens, half_tokens, 0)

time: 43.5 us -> 42.6 us (0.979)
  waiting for transfers between devices: 9.76 us -> 8.86 us
    all_to_all x1, waiting for transfers between devices: 0.96 us -> 0.06 us  [body(): lax.all_to_all(terms, ('sv', 'tv'), 0, 0, axis_index_groups=everyone, til...]
  transfers between devices with their start and end apart: 10 -> 10, of which waited for: 2 -> 2; matrix products, arithmetic and copies ran while one was open for 3% -> 3% of each run, Pallas kernels for 22% -> 23%
where the time goes in v25:
time: 42.6 us; the launch traced here: 42.2 us
  starting transfers between devices  19.1 us (45%)
  Pallas kernels  9.67 us (23%)
  waiting for transfers between devices  8.86 us (21%)
  other arithmetic  3.58 us (8%)
  between operations  0.85 us (2%)
    all_to_all x1, waiting for transfers between devices, body(): lax.all_to_all(outgoing, 'sv', 0, 0, axis_index_groups=[turned_group(owne...  8.78 us
    ppermute x4, starting transfers between devices, to_partner(): lax.ppermute(x, 'sv', [(s, s ^ offset) for s in range(lax.axis_size('sv'))])  7.57 us
    all_to_all x1, starting transfers between devices, body(): lax.all_to_all(terms, ('sv', 'tv'), 0, 0, axis_index_groups=everyone, til...  5.49 us
    all_to_all x1, starting transfers between devices, body(): lax.all_to_all(outgoing, 'sv', 0, 0, axis_index_groups=[turned_group(owne...  5.28 us
    pallas_call x1, Pallas kernels, body(): pl.pallas_call(weight_kernel, out_shape=(shape((features, width), bf16),...  4.48 us
    pallas_call x1, Pallas kernels, body(): pl.pallas_call(map_rest_kernel, out_shape=shape(chunk, bf16), in_specs=[i...  2.57 us
    another operation x1, other arithmetic, body(): lax.reduce((wide, jnp.ones_like(wide)), (low, jnp.float32(0)), merge, (1,))  1.68 us
    pallas_call x1, Pallas kernels, body(): pl.pallas_call(map_own_kernel, out_shape=shape((rows + MASS_ROWS, tokens...  1.4 us
  transfers between devices with their start and end apart: 10, of which 2 were waited for; matrix products, arithmetic and copies ran while one was open for 3% of the time, Pallas kernels for 23%

profile of v25, /device:TPU:0, one launch (start us, length us, event | category | flops | bytes accessed | tf_op | source)
XLA Modules:
  0.0 42.2 jit_solution(5857442765450682608)
XLA Ops:
  0.6 1.7 %convert_reduce_fusion = (f32[64]{0:T(128)S(1)}, f32[64]{0:T(128)S(1)}) fusion(bf16[64,4096]{1,0:T(8,128)(2,1)} %param.10), kind=kLoop, calls=%fused_computation | loop fusion | flops 1834624 | bytes 524800 | tf_op jit(solution)/shard_map/reduce | solution.py:267
  2.3 0.5 %collective-permute-start = (bf16[16,40960]{1,0:T(8,128)(2,1)}, bf16[16,40960]{1,0:T(8,128)(2,1)S(1)}, u32[]{:S(2)}, u32[]{:S(2)}) collective-permute-start(bf16[16,40960]{1,0:T(8,128)(2,1)} %t_ref.1), channel_id=1, source_target_pairs={{0,1},{1,0},{2,3},{3,2},{4,5},{5,4},{6,7},{7,6},{8,9},{9,8},{10,11... | collective-permute-start | bytes 3932168 | tf_op jit(solution)/shard_map/ppermute | solution.py:227
  2.8 0.1 collective-permute-start.1
  2.9 4.0 %collective-permute-start.2 = (bf16[1,8,1920]{2,1,0:T(8,128)(2,1)}, bf16[1,8,1920]{2,1,0:T(8,128)(2,1)S(1)}, u32[]{:S(2)}, u32[]{:S(2)}) collective-permute-start(bf16[1,8,1920]{2,1,0:T(8,128)(2,1)} %bitcast.11), channel_id=1, source_target_pairs={{0,8},{2,10},{4,12},{6,14},{8,0},{10,2},{12,4},{14,6},{1,9},{3,11}... | collective-permute-start | bytes 92168 | tf_op jit(solution)/shard_map/ppermute | solution.py:231
  6.9 0.7 %fusion.5 = f32[640,2]{0,1:T(2,128)S(1)} fusion(bf16[640,2]{0,1:T(2,128)(2,1)} %param.9, s32[640,2]{0,1:T(2,128)} %param.7, s32[640,2]{0,1:T(2,128)} %param.8, s32[]{:T(128)S(6)} %mul.51), kind=kLoop, calls=%fused_computation.24 | loop fusion | flops 14080 | bytes 17924 | tf_op jit(solution)/shard_map/add | solution.py:274
  7.7 0.1 dynamic-slice_bitcast_fusion
  7.8 0.2 add_convert_fusion
  8.1 0.1 pad_maximum_fusion.3.stats_ref
  8.2 1.4 %map_own.1.p_ref = f32[144,2048]{1,0:T(8,128)S(1)} custom-call(bf16[144,320]{1,0:T(8,128)(2,1)S(1)} %get-tuple-element.57.w_ref, bf16[16,40960]{1,0:T(8,128)(2,1)S(1)} %copy-done, f32[2,128]{1,0:T(2,128)S(1)} %pad_maximum_fusion.3.stats_ref), custom_call_target="tpu_custom_call" | custom-call | flops 188743680 | bytes 3145728 | tf_op jit(solution)/shard_map/map_own/pallas_call | solution.py:280
  9.6 2.6 %map_rest.1 = bf16[8,16,2176]{2,1,0:T(8,128)(2,1)} custom-call(bf16[144,320]{1,0:T(8,128)(2,1)S(1)} %get-tuple-element.58.w_ref, bf16[16,40960]{1,0:T(8,128)(2,1)S(1)} %collective-permute-done.t_ref, f32[144,2048]{1,0:T(8,128)S(1)} %map_own.1.p_ref, f32[2,128]{1,0:T(2,128)S(1)} %pad_maximum_fusion.3.stats_ref), custom_call_target="tpu_custom_call" | custom-call | flops 188743680 | bytes 4194304 | tf_op jit(solution)/shard_map/map_rest/pallas_call | solution.py:291
  12.2 5.3 %all-to-all-start = ((bf16[8,16,2176]{2,1,0:T(8,128)(2,1)}), bf16[8,16,2176]{2,1,0:T(8,128)(2,1)S(1)}, u32[]{:S(2)}, u32[]{:S(2)}) async-start(bf16[8,16,2176]{2,1,0:T(8,128)(2,1)} %map_rest.1), calls=%async_computation | async-start | bytes 1114112 | tf_op jit(solution)/shard_map/all_to_all | solution.py:307
  17.5 0.1 collective-permute-start.3
  17.6 1.5 %collective-permute-start.6 = (bf16[2,8,1920]{2,1,0:T(8,128)(2,1)S(1)}, bf16[2,8,1920]{2,1,0:T(8,128)(2,1)S(1)}, u32[]{:S(2)}, u32[]{:S(2)}) collective-permute-start(bf16[2,8,1920]{2,1,0:T(8,128)(2,1)S(1)} %constant_dynamic-update-slice_fusion), channel_id=1, source_target_pairs={{0,6},{2,4},{4,2},{6,0},{8,14},{10,12},{12,10},{14,8},{1,7},{3,5},... | collective-permute-start | bytes 184328 | tf_op jit(solution)/shard_map/ppermute | solution.py:231
  19.1 1.5 %collective-permute-start.5 = (bf16[2,8,1920]{2,1,0:T(8,128)(2,1)S(1)}, bf16[2,8,1920]{2,1,0:T(8,128)(2,1)S(1)}, u32[]{:S(2)}, u32[]{:S(2)}) collective-permute-start(bf16[2,8,1920]{2,1,0:T(8,128)(2,1)S(1)} %constant_dynamic-update-slice_fusion), channel_id=1, source_target_pairs={{0,4},{2,6},{4,0},{6,2},{8,12},{10,14},{12,8},{14,10},{1,5},{3,7},... | collective-permute-start | bytes 184328 | tf_op jit(solution)/shard_map/ppermute | solution.py:231
  20.6 0.6 %collective-permute-start.4 = (bf16[2,8,1920]{2,1,0:T(8,128)(2,1)S(1)}, bf16[2,8,1920]{2,1,0:T(8,128)(2,1)S(1)}, u32[]{:S(2)}, u32[]{:S(2)}) collective-permute-start(bf16[2,8,1920]{2,1,0:T(8,128)(2,1)S(1)} %constant_dynamic-update-slice_fusion), channel_id=1, source_target_pairs={{0,2},{2,0},{4,6},{6,4},{8,10},{10,8},{12,14},{14,12},{1,3},{3,1},... | collective-permute-start | bytes 184328 | tf_op jit(solution)/shard_map/ppermute | solution.py:231
  21.2 0.1 broadcast_select_fusion.1
  21.3 8.8 %all-to-all-done.refs_0_ = bf16[8,16,2176]{2,1,0:T(8,128)(2,1)S(1)} async-done(((bf16[8,16,2176]{2,1,0:T(8,128)(2,1)}), bf16[8,16,2176]{2,1,0:T(8,128)(2,1)S(1)}, u32[]{:S(2)}, u32[]{:S(2)}) %all-to-all-start) | async-done | bytes 557088 | tf_op jit(solution)/shard_map/all_to_all | solution.py:307
  30.1 1.2 %logit_grad.1 = (bf16[128,2048]{1,0:T(8,128)(2,1)S(1)}, f32[16,8,128]{2,1,0:T(8,128)}) custom-call(bf16[8,16,2176]{2,1,0:T(8,128)(2,1)S(1)} %all-to-all-done.refs_0_, bf16[128,2048]{1,0:T(8,128)(2,1)S(1)} %pad_maximum_fusion.refs_1_), custom_call_target="tpu_custom_call" | custom-call | flops 2621440 | bytes 1572864 | tf_op jit(solution)/shard_map/logit_grad/pallas_call | solution.py:320
  31.5 0.1 collective-permute-start.7
  31.6 5.5 %all-to-all-start.1 = ((f32[16,8,128]{2,1,0:T(8,128)}), f32[16,8,128]{2,1,0:T(8,128)S(1)}, u32[]{:S(2)}, u32[]{:S(2)}) async-start(f32[16,8,128]{2,1,0:T(8,128)} %get-tuple-element.29), calls=%async_computation.1 | async-start | bytes 131072 | tf_op jit(solution)/shard_map/all_to_all | solution.py:338
  37.1 0.1 pad_add_fusion.place_ref
  37.2 4.5 %weight_grad.1 = (bf16[1920,2048]{1,0:T(8,128)(2,1)}, bf16[64,4096]{1,0:T(8,128)(2,1)}) custom-call(s32[2]{0:T(128)S(1)} %pad_add_fusion.place_ref, bf16[8,8,1920]{2,1,0:T(8,128)(2,1)S(1)} %constant_dynamic-update-slice_fusion.2.own_ref, bf16[64,3968]{1,0:T(8,128)(2,1)S(1)} %collective-permute-done.7.got_ref, bf16[128,2048]{1,0:T(8,128)(2,1)S(1)} %get-tuple-element.37.grad_ref), custom_call_target="tpu_custom_call" | custom-call | flops 1006632960 | bytes 8880128 | tf_op jit(solution)/shard_map/weight_grad/pallas_call | solution.py:344
  41.6 0.1 all-to-all-done.1
  41.7 0.5 %slice_reduce_fusion = f32[64]{0:T(128)} fusion(f32[16,8,128]{2,1,0:T(8,128)S(1)} %all-to-all-done.1), kind=kLoop, calls=%fused_computation.22 | loop fusion | flops 960 | bytes 4352 | tf_op jit(solution)/shard_map/reduce_sum | solution.py:364
  (29 shorter events, 0.3 us)
Async XLA Ops:
  0.6 7.5 %copy-start = (bf16[16,40960]{1,0:T(8,128)(2,1)S(1)}, bf16[16,40960]{1,0:T(8,128)(2,1)}, u32[]{:S(2)}) copy-start(bf16[16,40960]{1,0:T(8,128)(2,1)} %t_ref.1) | copy-start | bytes 3932164
  2.3 7.2 %collective-permute-start = (bf16[16,40960]{1,0:T(8,128)(2,1)}, bf16[16,40960]{1,0:T(8,128)(2,1)S(1)}, u32[]{:S(2)}, u32[]{:S(2)}) collective-permute-start(bf16[16,40960]{1,0:T(8,128)(2,1)} %t_ref.1), channel_id=1, source_target_pairs={{0,1},{1,0},{2,3},{3,2},{4,5},{5,4},{6,7},{7,6},{8,9},{9,8},{10,11... | collective-permute-start | bytes 3932168 | tf_op jit(solution)/shard_map/ppermute | solution.py:227
  2.8 5.2 %collective-permute-start.1 = (f32[2,64]{1,0:T(2,128)S(1)}, f32[2,64]{1,0:T(2,128)S(1)}, u32[]{:S(2)}, u32[]{:S(2)}) collective-permute-start(f32[2,64]{1,0:T(2,128)S(1)} %pad_maximum_fusion.2), channel_id=1, source_target_pairs={{0,1},{1,0},{2,3},{3,2},{4,5},{5,4},{6,7},{7,6},{8,9},{9,8},{10,11... | collective-permute-start | bytes 1544 | tf_op jit(solution)/shard_map/ppermute | solution.py:227
  2.9 9.3 %collective-permute-start.2 = (bf16[1,8,1920]{2,1,0:T(8,128)(2,1)}, bf16[1,8,1920]{2,1,0:T(8,128)(2,1)S(1)}, u32[]{:S(2)}, u32[]{:S(2)}) collective-permute-start(bf16[1,8,1920]{2,1,0:T(8,128)(2,1)} %bitcast.11), channel_id=1, source_target_pairs={{0,8},{2,10},{4,12},{6,14},{8,0},{10,2},{12,4},{14,6},{1,9},{3,11}... | collective-permute-start | bytes 92168 | tf_op jit(solution)/shard_map/ppermute | solution.py:231
  9.6 7.9 %copy-start.1 = (bf16[64,4096]{1,0:T(8,128)(2,1)S(1)}, bf16[64,4096]{1,0:T(8,128)(2,1)}, u32[]{:S(2)}) copy-start(bf16[64,4096]{1,0:T(8,128)(2,1)} %param.10) | copy-start | bytes 1572868
  12.2 5.4 %copy-start.2 = (bf16[8,1920]{1,0:T(8,128)(2,1)S(1)}, bf16[8,1920]{1,0:T(8,128)(2,1)}, u32[]{:S(2)}) copy-start(bf16[8,1920]{1,0:T(8,128)(2,1)} %param.11) | copy-start | bytes 92164
  12.2 17.9 %all-to-all-start = ((bf16[8,16,2176]{2,1,0:T(8,128)(2,1)}), bf16[8,16,2176]{2,1,0:T(8,128)(2,1)S(1)}, u32[]{:S(2)}, u32[]{:S(2)}) async-start(bf16[8,16,2176]{2,1,0:T(8,128)(2,1)} %map_rest.1), calls=%async_computation | async-start | bytes 1114112 | tf_op jit(solution)/shard_map/all_to_all | solution.py:307
  17.5 3.7 %collective-permute-start.3 = (bf16[64,2048]{1,0:T(8,128)(2,1)S(1)}, bf16[64,2048]{1,0:T(8,128)(2,1)S(1)}, u32[]{:S(2)}, u32[]{:S(2)}) collective-permute-start(bf16[64,2048]{1,0:T(8,128)(2,1)S(1)} %constant_dynamic-slice_fusion.1), channel_id=1, source_target_pairs={{0,1},{1,0},{2,3},{3,2},{4,5},{5,4},{6,7},{7,6},{8,9},{9,8},{10,11... | collective-permute-start | bytes 786440 | tf_op jit(solution)/shard_map/ppermute | solution.py:227
  17.6 13.7 %collective-permute-start.6 = (bf16[2,8,1920]{2,1,0:T(8,128)(2,1)S(1)}, bf16[2,8,1920]{2,1,0:T(8,128)(2,1)S(1)}, u32[]{:S(2)}, u32[]{:S(2)}) collective-permute-start(bf16[2,8,1920]{2,1,0:T(8,128)(2,1)S(1)} %constant_dynamic-update-slice_fusion), channel_id=1, source_target_pairs={{0,6},{2,4},{4,2},{6,0},{8,14},{10,12},{12,10},{14,8},{1,7},{3,5},... | collective-permute-start | bytes 184328 | tf_op jit(solution)/shard_map/ppermute | solution.py:231
  19.1 12.2 %collective-permute-start.5 = (bf16[2,8,1920]{2,1,0:T(8,128)(2,1)S(1)}, bf16[2,8,1920]{2,1,0:T(8,128)(2,1)S(1)}, u32[]{:S(2)}, u32[]{:S(2)}) collective-permute-start(bf16[2,8,1920]{2,1,0:T(8,128)(2,1)S(1)} %constant_dynamic-update-slice_fusion), channel_id=1, source_target_pairs={{0,4},{2,6},{4,0},{6,2},{8,12},{10,14},{12,8},{14,10},{1,5},{3,7},... | collective-permute-start | bytes 184328 | tf_op jit(solution)/shard_map/ppermute | solution.py:231
  20.6 10.8 %collective-permute-start.4 = (bf16[2,8,1920]{2,1,0:T(8,128)(2,1)S(1)}, bf16[2,8,1920]{2,1,0:T(8,128)(2,1)S(1)}, u32[]{:S(2)}, u32[]{:S(2)}) collective-permute-start(bf16[2,8,1920]{2,1,0:T(8,128)(2,1)S(1)} %constant_dynamic-update-slice_fusion), channel_id=1, source_target_pairs={{0,2},{2,0},{4,6},{6,4},{8,10},{10,8},{12,14},{14,12},{1,3},{3,1},... | collective-permute-start | bytes 184328 | tf_op jit(solution)/shard_map/ppermute | solution.py:231
  31.5 5.7 %collective-permute-start.7 = (bf16[64,3968]{1,0:T(8,128)(2,1)S(1)}, bf16[64,3968]{1,0:T(8,128)(2,1)S(1)}, u32[]{:S(2)}, u32[]{:S(2)}) collective-permute-start(bf16[64,3968]{1,0:T(8,128)(2,1)S(1)} %pad_maximum_fusion.1), channel_id=1, source_target_pairs={{0,1},{1,0},{2,3},{3,2},{4,5},{5,4},{6,7},{7,6},{8,9},{9,8},{10,11... | collective-permute-start | bytes 1523720 | tf_op jit(solution)/shard_map/ppermute | solution.py:227
  31.6 10.1 %all-to-all-start.1 = ((f32[16,8,128]{2,1,0:T(8,128)}), f32[16,8,128]{2,1,0:T(8,128)S(1)}, u32[]{:S(2)}, u32[]{:S(2)}) async-start(f32[16,8,128]{2,1,0:T(8,128)} %get-tuple-element.29), calls=%async_computation.1 | async-start | bytes 131072 | tf_op jit(solution)/shard_map/all_to_all | solution.py:338

commit v26 on v25

--- a/solution.py
+++ b/solution.py
@@ -165,6 +165,13 @@
     return [a for b in range(owners // 2) for a in (b, b + owners // 2)]
 
 
+def row_blocks(features):
+    tiles = features // BLK
+    sizes = [2] + [3] * ((tiles - 3) // 3)
+    sizes.append(tiles - sum(sizes))
+    return [size * BLK for size in sizes]
+
+
 def weight_kernel(
     place_ref, own_ref, got_ref, grad_ref, o_ref, joined_ref, s_ref, h_ref, block_ref, sems, join_sems
 ):
@@ -187,18 +194,19 @@
         s_ref[own, :] = own_ref[i].astype(jnp.float32)
         pair = got_ref[i // 2 * 2 * held : (i // 2 + 1) * 2 * held, width:].astype(jnp.float32)
         s_ref[other, :] = pair[i % 2 * held : (i % 2 + 1) * held]
-    for i in range(s_ref.shape[0] // BLK):
-        for j in range(features // BLK):
-            tile = s_ref[i * BLK : (i + 1) * BLK, j * BLK : (j + 1) * BLK].T
-            h_ref[j * BLK : (j + 1) * BLK, i * BLK : (i + 1) * BLK] = tile.astype(jnp.bfloat16)
-    steps, tile, _ = block_ref.shape
-    for i in range(steps):
-        rows = slice(i * tile, (i + 1) * tile)
-        block_ref[i] = jnp.dot(
+    first = 0
+    for i, size in enumerate(row_blocks(features)):
+        rows = slice(first, first + size)
+        for j in range(first, first + size, BLK):
+            for t in range(0, s_ref.shape[0], BLK):
+                h_ref[j : j + BLK, t : t + BLK] = s_ref[t : t + BLK, j : j + BLK].T.astype(jnp.bfloat16)
+        block_ref[rows, :] = jnp.dot(
             h_ref[rows, :], grad_ref[...], preferred_element_type=jnp.float32
         ).astype(jnp.bfloat16)
-        copies.append(pltpu.make_async_copy(block_ref.at[i], o_ref.at[pl.ds(i * tile, tile), :], sems.at[i]))
+        at = pl.ds(first, size)
+        copies.append(pltpu.make_async_copy(block_ref.at[at, :], o_ref.at[at, :], sems.at[i]))
         copies[-1].start()
+        first += size
     for copy in copies:
         copy.wait()
 
@@ -340,7 +348,6 @@
     give = lax.dynamic_slice_in_dim(grad, (1 - half_index) * half_tokens, half_tokens, 0)
     hidden_own = jnp.concatenate(pieces)
     got = swap_halves(jnp.concatenate([give, hidden_own.reshape(half_tokens, features)], axis=1))
-    steps = 8
     weight_grad, logit_grad = pl.pallas_call(
         weight_kernel,
         out_shape=(shape((features, width), bf16), shape((half_tokens, columns), bf16)),
@@ -349,8 +356,8 @@
         scratch_shapes=[
             pltpu.VMEM((group_tokens, features), f32),
             pltpu.VMEM((features, group_tokens), bf16),
-            pltpu.VMEM((steps, features // steps, width), bf16),
-            dma(steps),
+            pltpu.VMEM((features, width), bf16),
+            dma(len(row_blocks(features))),
             dma(2),
         ],
         compiler_params=params(),

time: 42.6 us -> 42.6 us (level)
  transfers between devices with their start and end apart: 10 -> 10, of which waited for: 2 -> 1; matrix products, arithmetic and copies ran while one was open for 3% -> 3% of each run, Pallas kernels for 23% -> 23%
where the time goes in v26:
time: 42.6 us; the launch traced here: 42.2 us
  starting transfers between devices  19.1 us (45%)
  Pallas kernels  9.7 us (23%)
  waiting for transfers between devices  8.83 us (21%)
  other arithmetic  3.58 us (8%)
  between operations  0.85 us (2%)
    all_to_all x1, waiting for transfers between devices, body(): lax.all_to_all(outgoing, 'sv', 0, 0, axis_index_groups=[turned_group(owne...  8.78 us
    ppermute x4, starting transfers between devices, to_partner(): lax.ppermute(x, 'sv', [(s, s ^ offset) for s in range(lax.axis_size('sv'))])  7.57 us
    all_to_all x1, starting transfers between devices, body(): lax.all_to_all(terms, ('sv', 'tv'), 0, 0, axis_index_groups=everyone, til...  5.49 us
    all_to_all x1, starting transfers between devices, body(): lax.all_to_all(outgoing, 'sv', 0, 0, axis_index_groups=[turned_group(owne...  5.28 us
    pallas_call x1, Pallas kernels, body(): pl.pallas_call(weight_kernel, out_shape=(shape((features, width), bf16),...  4.51 us
    pallas_call x1, Pallas kernels, body(): pl.pallas_call(map_rest_kernel, out_shape=shape(chunk, bf16), in_specs=[i...  2.57 us
    another operation x1, other arithmetic, body(): lax.reduce((wide, jnp.ones_like(wide)), (low, jnp.float32(0)), merge, (1,))  1.68 us
    pallas_call x1, Pallas kernels, body(): pl.pallas_call(map_own_kernel, out_shape=shape((rows + MASS_ROWS, tokens...  1.4 us
  transfers between devices with their start and end apart: 10, of which 1 were waited for; matrix products, arithmetic and copies ran while one was open for 3% of the time, Pallas kernels for 23%

profile of v26, /device:TPU:0, one launch (start us, length us, event | category | flops | bytes accessed | tf_op | source)
XLA Modules:
  0.0 42.2 jit_solution(4151482603815650095)
XLA Ops:
  0.6 1.7 %convert_reduce_fusion = (f32[64]{0:T(128)S(1)}, f32[64]{0:T(128)S(1)}) fusion(bf16[64,4096]{1,0:T(8,128)(2,1)} %param.10), kind=kLoop, calls=%fused_computation | loop fusion | flops 1834624 | bytes 524800 | tf_op jit(solution)/shard_map/reduce | solution.py:275
  2.3 0.5 %collective-permute-start = (bf16[16,40960]{1,0:T(8,128)(2,1)}, bf16[16,40960]{1,0:T(8,128)(2,1)S(1)}, u32[]{:S(2)}, u32[]{:S(2)}) collective-permute-start(bf16[16,40960]{1,0:T(8,128)(2,1)} %t_ref.1), channel_id=1, source_target_pairs={{0,1},{1,0},{2,3},{3,2},{4,5},{5,4},{6,7},{7,6},{8,9},{9,8},{10,11... | collective-permute-start | bytes 3932168 | tf_op jit(solution)/shard_map/ppermute | solution.py:235
  2.8 0.1 collective-permute-start.1
  2.9 4.0 %collective-permute-start.2 = (bf16[1,8,1920]{2,1,0:T(8,128)(2,1)}, bf16[1,8,1920]{2,1,0:T(8,128)(2,1)S(1)}, u32[]{:S(2)}, u32[]{:S(2)}) collective-permute-start(bf16[1,8,1920]{2,1,0:T(8,128)(2,1)} %bitcast.11), channel_id=1, source_target_pairs={{0,8},{2,10},{4,12},{6,14},{8,0},{10,2},{12,4},{14,6},{1,9},{3,11}... | collective-permute-start | bytes 92168 | tf_op jit(solution)/shard_map/ppermute | solution.py:239
  6.9 0.7 %fusion.5 = f32[640,2]{0,1:T(2,128)S(1)} fusion(bf16[640,2]{0,1:T(2,128)(2,1)} %param.9, s32[640,2]{0,1:T(2,128)} %param.7, s32[640,2]{0,1:T(2,128)} %param.8, s32[]{:T(128)S(6)} %mul.51), kind=kLoop, calls=%fused_computation.24 | loop fusion | flops 14080 | bytes 17924 | tf_op jit(solution)/shard_map/add | solution.py:282
  7.7 0.1 dynamic-slice_bitcast_fusion
  7.8 0.2 add_convert_fusion
  8.1 0.1 pad_maximum_fusion.3.stats_ref
  8.2 1.4 %map_own.1.p_ref = f32[144,2048]{1,0:T(8,128)S(1)} custom-call(bf16[144,320]{1,0:T(8,128)(2,1)S(1)} %get-tuple-element.57.w_ref, bf16[16,40960]{1,0:T(8,128)(2,1)S(1)} %copy-done, f32[2,128]{1,0:T(2,128)S(1)} %pad_maximum_fusion.3.stats_ref), custom_call_target="tpu_custom_call" | custom-call | flops 188743680 | bytes 3145728 | tf_op jit(solution)/shard_map/map_own/pallas_call | solution.py:288
  9.6 2.6 %map_rest.1 = bf16[8,16,2176]{2,1,0:T(8,128)(2,1)} custom-call(bf16[144,320]{1,0:T(8,128)(2,1)S(1)} %get-tuple-element.58.w_ref, bf16[16,40960]{1,0:T(8,128)(2,1)S(1)} %collective-permute-done.t_ref, f32[144,2048]{1,0:T(8,128)S(1)} %map_own.1.p_ref, f32[2,128]{1,0:T(2,128)S(1)} %pad_maximum_fusion.3.stats_ref), custom_call_target="tpu_custom_call" | custom-call | flops 188743680 | bytes 4194304 | tf_op jit(solution)/shard_map/map_rest/pallas_call | solution.py:299
  12.2 5.3 %all-to-all-start = ((bf16[8,16,2176]{2,1,0:T(8,128)(2,1)}), bf16[8,16,2176]{2,1,0:T(8,128)(2,1)S(1)}, u32[]{:S(2)}, u32[]{:S(2)}) async-start(bf16[8,16,2176]{2,1,0:T(8,128)(2,1)} %map_rest.1), calls=%async_computation | async-start | bytes 1114112 | tf_op jit(solution)/shard_map/all_to_all | solution.py:315
  17.5 0.1 collective-permute-start.3
  17.6 1.5 %collective-permute-start.6 = (bf16[2,8,1920]{2,1,0:T(8,128)(2,1)S(1)}, bf16[2,8,1920]{2,1,0:T(8,128)(2,1)S(1)}, u32[]{:S(2)}, u32[]{:S(2)}) collective-permute-start(bf16[2,8,1920]{2,1,0:T(8,128)(2,1)S(1)} %constant_dynamic-update-slice_fusion), channel_id=1, source_target_pairs={{0,6},{2,4},{4,2},{6,0},{8,14},{10,12},{12,10},{14,8},{1,7},{3,5},... | collective-permute-start | bytes 184328 | tf_op jit(solution)/shard_map/ppermute | solution.py:239
  19.1 1.5 %collective-permute-start.5 = (bf16[2,8,1920]{2,1,0:T(8,128)(2,1)S(1)}, bf16[2,8,1920]{2,1,0:T(8,128)(2,1)S(1)}, u32[]{:S(2)}, u32[]{:S(2)}) collective-permute-start(bf16[2,8,1920]{2,1,0:T(8,128)(2,1)S(1)} %constant_dynamic-update-slice_fusion), channel_id=1, source_target_pairs={{0,4},{2,6},{4,0},{6,2},{8,12},{10,14},{12,8},{14,10},{1,5},{3,7},... | collective-permute-start | bytes 184328 | tf_op jit(solution)/shard_map/ppermute | solution.py:239
  20.6 0.6 %collective-permute-start.4 = (bf16[2,8,1920]{2,1,0:T(8,128)(2,1)S(1)}, bf16[2,8,1920]{2,1,0:T(8,128)(2,1)S(1)}, u32[]{:S(2)}, u32[]{:S(2)}) collective-permute-start(bf16[2,8,1920]{2,1,0:T(8,128)(2,1)S(1)} %constant_dynamic-update-slice_fusion), channel_id=1, source_target_pairs={{0,2},{2,0},{4,6},{6,4},{8,10},{10,8},{12,14},{14,12},{1,3},{3,1},... | collective-permute-start | bytes 184328 | tf_op jit(solution)/shard_map/ppermute | solution.py:239
  21.2 0.1 broadcast_select_fusion.1
  21.3 8.8 %all-to-all-done.refs_0_ = bf16[8,16,2176]{2,1,0:T(8,128)(2,1)S(1)} async-done(((bf16[8,16,2176]{2,1,0:T(8,128)(2,1)}), bf16[8,16,2176]{2,1,0:T(8,128)(2,1)S(1)}, u32[]{:S(2)}, u32[]{:S(2)}) %all-to-all-start) | async-done | bytes 557088 | tf_op jit(solution)/shard_map/all_to_all | solution.py:315
  30.1 1.2 %logit_grad.1 = (bf16[128,2048]{1,0:T(8,128)(2,1)S(1)}, f32[16,8,128]{2,1,0:T(8,128)}) custom-call(bf16[8,16,2176]{2,1,0:T(8,128)(2,1)S(1)} %all-to-all-done.refs_0_, bf16[128,2048]{1,0:T(8,128)(2,1)S(1)} %pad_maximum_fusion.refs_1_), custom_call_target="tpu_custom_call" | custom-call | flops 2621440 | bytes 1572864 | tf_op jit(solution)/shard_map/logit_grad/pallas_call | solution.py:328
  31.5 0.1 collective-permute-start.7
  31.6 5.5 %all-to-all-start.1 = ((f32[16,8,128]{2,1,0:T(8,128)}), f32[16,8,128]{2,1,0:T(8,128)S(1)}, u32[]{:S(2)}, u32[]{:S(2)}) async-start(f32[16,8,128]{2,1,0:T(8,128)} %get-tuple-element.29), calls=%async_computation.1 | async-start | bytes 131072 | tf_op jit(solution)/shard_map/all_to_all | solution.py:346
  37.1 0.1 pad_add_fusion.place_ref
  37.2 4.5 %weight_grad.1 = (bf16[1920,2048]{1,0:T(8,128)(2,1)}, bf16[64,4096]{1,0:T(8,128)(2,1)}) custom-call(s32[2]{0:T(128)S(1)} %pad_add_fusion.place_ref, bf16[8,8,1920]{2,1,0:T(8,128)(2,1)S(1)} %constant_dynamic-update-slice_fusion.2.own_ref, bf16[64,3968]{1,0:T(8,128)(2,1)S(1)} %collective-permute-done.7.got_ref, bf16[128,2048]{1,0:T(8,128)(2,1)S(1)} %get-tuple-element.37.grad_ref), custom_call_target="tpu_custom_call" | custom-call | flops 1006632960 | bytes 8880128 | tf_op jit(solution)/shard_map/weight_grad/pallas_call | solution.py:351
  41.7 0.0 all-to-all-done.1
  41.7 0.5 %slice_reduce_fusion = f32[64]{0:T(128)} fusion(f32[16,8,128]{2,1,0:T(8,128)S(1)} %all-to-all-done.1), kind=kLoop, calls=%fused_computation.22 | loop fusion | flops 960 | bytes 4352 | tf_op jit(solution)/shard_map/reduce_sum | solution.py:371
  (29 shorter events, 0.3 us)
Async XLA Ops:
  0.6 7.5 %copy-start = (bf16[16,40960]{1,0:T(8,128)(2,1)S(1)}, bf16[16,40960]{1,0:T(8,128)(2,1)}, u32[]{:S(2)}) copy-start(bf16[16,40960]{1,0:T(8,128)(2,1)} %t_ref.1) | copy-start | bytes 3932164
  2.3 7.2 %collective-permute-start = (bf16[16,40960]{1,0:T(8,128)(2,1)}, bf16[16,40960]{1,0:T(8,128)(2,1)S(1)}, u32[]{:S(2)}, u32[]{:S(2)}) collective-permute-start(bf16[16,40960]{1,0:T(8,128)(2,1)} %t_ref.1), channel_id=1, source_target_pairs={{0,1},{1,0},{2,3},{3,2},{4,5},{5,4},{6,7},{7,6},{8,9},{9,8},{10,11... | collective-permute-start | bytes 3932168 | tf_op jit(solution)/shard_map/ppermute | solution.py:235
  2.8 5.2 %collective-permute-start.1 = (f32[2,64]{1,0:T(2,128)S(1)}, f32[2,64]{1,0:T(2,128)S(1)}, u32[]{:S(2)}, u32[]{:S(2)}) collective-permute-start(f32[2,64]{1,0:T(2,128)S(1)} %pad_maximum_fusion.2), channel_id=1, source_target_pairs={{0,1},{1,0},{2,3},{3,2},{4,5},{5,4},{6,7},{7,6},{8,9},{9,8},{10,11... | collective-permute-start | bytes 1544 | tf_op jit(solution)/shard_map/ppermute | solution.py:235
  2.9 9.3 %collective-permute-start.2 = (bf16[1,8,1920]{2,1,0:T(8,128)(2,1)}, bf16[1,8,1920]{2,1,0:T(8,128)(2,1)S(1)}, u32[]{:S(2)}, u32[]{:S(2)}) collective-permute-start(bf16[1,8,1920]{2,1,0:T(8,128)(2,1)} %bitcast.11), channel_id=1, source_target_pairs={{0,8},{2,10},{4,12},{6,14},{8,0},{10,2},{12,4},{14,6},{1,9},{3,11}... | collective-permute-start | bytes 92168 | tf_op jit(solution)/shard_map/ppermute | solution.py:239
  9.6 7.9 %copy-start.1 = (bf16[64,4096]{1,0:T(8,128)(2,1)S(1)}, bf16[64,4096]{1,0:T(8,128)(2,1)}, u32[]{:S(2)}) copy-start(bf16[64,4096]{1,0:T(8,128)(2,1)} %param.10) | copy-start | bytes 1572868
  12.2 5.4 %copy-start.2 = (bf16[8,1920]{1,0:T(8,128)(2,1)S(1)}, bf16[8,1920]{1,0:T(8,128)(2,1)}, u32[]{:S(2)}) copy-start(bf16[8,1920]{1,0:T(8,128)(2,1)} %param.11) | copy-start | bytes 92164
  12.2 17.9 %all-to-all-start = ((bf16[8,16,2176]{2,1,0:T(8,128)(2,1)}), bf16[8,16,2176]{2,1,0:T(8,128)(2,1)S(1)}, u32[]{:S(2)}, u32[]{:S(2)}) async-start(bf16[8,16,2176]{2,1,0:T(8,128)(2,1)} %map_rest.1), calls=%async_computation | async-start | bytes 1114112 | tf_op jit(solution)/shard_map/all_to_all | solution.py:315
  17.5 3.7 %collective-permute-start.3 = (bf16[64,2048]{1,0:T(8,128)(2,1)S(1)}, bf16[64,2048]{1,0:T(8,128)(2,1)S(1)}, u32[]{:S(2)}, u32[]{:S(2)}) collective-permute-start(bf16[64,2048]{1,0:T(8,128)(2,1)S(1)} %constant_dynamic-slice_fusion.1), channel_id=1, source_target_pairs={{0,1},{1,0},{2,3},{3,2},{4,5},{5,4},{6,7},{7,6},{8,9},{9,8},{10,11... | collective-permute-start | bytes 786440 | tf_op jit(solution)/shard_map/ppermute | solution.py:235
  17.6 13.7 %collective-permute-start.6 = (bf16[2,8,1920]{2,1,0:T(8,128)(2,1)S(1)}, bf16[2,8,1920]{2,1,0:T(8,128)(2,1)S(1)}, u32[]{:S(2)}, u32[]{:S(2)}) collective-permute-start(bf16[2,8,1920]{2,1,0:T(8,128)(2,1)S(1)} %constant_dynamic-update-slice_fusion), channel_id=1, source_target_pairs={{0,6},{2,4},{4,2},{6,0},{8,14},{10,12},{12,10},{14,8},{1,7},{3,5},... | collective-permute-start | bytes 184328 | tf_op jit(solution)/shard_map/ppermute | solution.py:239
  19.1 12.2 %collective-permute-start.5 = (bf16[2,8,1920]{2,1,0:T(8,128)(2,1)S(1)}, bf16[2,8,1920]{2,1,0:T(8,128)(2,1)S(1)}, u32[]{:S(2)}, u32[]{:S(2)}) collective-permute-start(bf16[2,8,1920]{2,1,0:T(8,128)(2,1)S(1)} %constant_dynamic-update-slice_fusion), channel_id=1, source_target_pairs={{0,4},{2,6},{4,0},{6,2},{8,12},{10,14},{12,8},{14,10},{1,5},{3,7},... | collective-permute-start | bytes 184328 | tf_op jit(solution)/shard_map/ppermute | solution.py:239
  20.6 10.8 %collective-permute-start.4 = (bf16[2,8,1920]{2,1,0:T(8,128)(2,1)S(1)}, bf16[2,8,1920]{2,1,0:T(8,128)(2,1)S(1)}, u32[]{:S(2)}, u32[]{:S(2)}) collective-permute-start(bf16[2,8,1920]{2,1,0:T(8,128)(2,1)S(1)} %constant_dynamic-update-slice_fusion), channel_id=1, source_target_pairs={{0,2},{2,0},{4,6},{6,4},{8,10},{10,8},{12,14},{14,12},{1,3},{3,1},... | collective-permute-start | bytes 184328 | tf_op jit(solution)/shard_map/ppermute | solution.py:239
  31.5 5.7 %collective-permute-start.7 = (bf16[64,3968]{1,0:T(8,128)(2,1)S(1)}, bf16[64,3968]{1,0:T(8,128)(2,1)S(1)}, u32[]{:S(2)}, u32[]{:S(2)}) collective-permute-start(bf16[64,3968]{1,0:T(8,128)(2,1)S(1)} %pad_maximum_fusion.1), channel_id=1, source_target_pairs={{0,1},{1,0},{2,3},{3,2},{4,5},{5,4},{6,7},{7,6},{8,9},{9,8},{10,11... | collective-permute-start | bytes 1523720 | tf_op jit(solution)/shard_map/ppermute | solution.py:235
  31.6 10.1 %all-to-all-start.1 = ((f32[16,8,128]{2,1,0:T(8,128)}), f32[16,8,128]{2,1,0:T(8,128)S(1)}, u32[]{:S(2)}, u32[]{:S(2)}) async-start(f32[16,8,128]{2,1,0:T(8,128)} %get-tuple-element.29), calls=%async_computation.1 | async-start | bytes 131072 | tf_op jit(solution)/shard_map/all_to_all | solution.py:346

commit v27 on v26

--- a/solution.py
+++ b/solution.py
@@ -196,13 +196,15 @@
         s_ref[other, :] = pair[i % 2 * held : (i % 2 + 1) * held]
     first = 0
     for i, size in enumerate(row_blocks(features)):
-        rows = slice(first, first + size)
         for j in range(first, first + size, BLK):
+            rows = slice(j, j + BLK)
             for t in range(0, s_ref.shape[0], BLK):
-                h_ref[j : j + BLK, t : t + BLK] = s_ref[t : t + BLK, j : j + BLK].T.astype(jnp.bfloat16)
-        block_ref[rows, :] = jnp.dot(
-            h_ref[rows, :], grad_ref[...], preferred_element_type=jnp.float32
-        ).astype(jnp.bfloat16)
+                h_ref[rows, t : t + BLK] = s_ref[t : t + BLK, rows].T.astype(jnp.bfloat16)
+            for n in range(0, width, 2 * BLK):
+                tile = jnp.dot(
+                    h_ref[rows, :], grad_ref[:, n : n + 2 * BLK], preferred_element_type=jnp.float32
+                )
+                block_ref[rows, n : n + 2 * BLK] = tile.astype(jnp.bfloat16)
         at = pl.ds(first, size)
         copies.append(pltpu.make_async_copy(block_ref.at[at, :], o_ref.at[at, :], sems.at[i]))
         copies[-1].start()

time: 42.6 us -> 42.6 us (level)
  no operation moved by 1% of the time
where the time goes in v27:
time: 42.6 us; the launch traced here: 42.2 us
  starting transfers between devices  19.1 us (45%)
  Pallas kernels  9.7 us (23%)
  waiting for transfers between devices  8.83 us (21%)
  other arithmetic  3.58 us (8%)
  between operations  0.85 us (2%)
    all_to_all x1, waiting for transfers between devices, body(): lax.all_to_all(outgoing, 'sv', 0, 0, axis_index_groups=[turned_group(owne...  8.78 us
    ppermute x4, starting transfers between devices, to_partner(): lax.ppermute(x, 'sv', [(s, s ^ offset) for s in range(lax.axis_size('sv'))])  7.57 us
    all_to_all x1, starting transfers between devices, body(): lax.all_to_all(terms, ('sv', 'tv'), 0, 0, axis_index_groups=everyone, til...  5.49 us
    all_to_all x1, starting transfers between devices, body(): lax.all_to_all(outgoing, 'sv', 0, 0, axis_index_groups=[turned_group(owne...  5.28 us
    pallas_call x1, Pallas kernels, body(): pl.pallas_call(weight_kernel, out_shape=(shape((features, width), bf16),...  4.51 us
    pallas_call x1, Pallas kernels, body(): pl.pallas_call(map_rest_kernel, out_shape=shape(chunk, bf16), in_specs=[i...  2.57 us
    another operation x1, other arithmetic, body(): lax.reduce((wide, jnp.ones_like(wide)), (low, jnp.float32(0)), merge, (1,))  1.68 us
    pallas_call x1, Pallas kernels, body(): pl.pallas_call(map_own_kernel, out_shape=shape((rows + MASS_ROWS, tokens...  1.4 us
  transfers between devices with their start and end apart: 10, of which 1 were waited for; matrix products, arithmetic and copies ran while one was open for 3% of the time, Pallas kernels for 23%

profile of v27, /device:TPU:0, one launch (start us, length us, event | category | flops | bytes accessed | tf_op | source)
XLA Modules:
  0.0 42.2 jit_solution(1540812302647856289)
XLA Ops:
  0.6 1.7 %convert_reduce_fusion = (f32[64]{0:T(128)S(1)}, f32[64]{0:T(128)S(1)}) fusion(bf16[64,4096]{1,0:T(8,128)(2,1)} %param.10), kind=kLoop, calls=%fused_computation | loop fusion | flops 1834624 | bytes 524800 | tf_op jit(solution)/shard_map/reduce | solution.py:277
  2.3 0.5 %collective-permute-start = (bf16[16,40960]{1,0:T(8,128)(2,1)}, bf16[16,40960]{1,0:T(8,128)(2,1)S(1)}, u32[]{:S(2)}, u32[]{:S(2)}) collective-permute-start(bf16[16,40960]{1,0:T(8,128)(2,1)} %t_ref.1), channel_id=1, source_target_pairs={{0,1},{1,0},{2,3},{3,2},{4,5},{5,4},{6,7},{7,6},{8,9},{9,8},{10,11... | collective-permute-start | bytes 3932168 | tf_op jit(solution)/shard_map/ppermute | solution.py:237
  2.8 0.1 collective-permute-start.1
  2.9 4.0 %collective-permute-start.2 = (bf16[1,8,1920]{2,1,0:T(8,128)(2,1)}, bf16[1,8,1920]{2,1,0:T(8,128)(2,1)S(1)}, u32[]{:S(2)}, u32[]{:S(2)}) collective-permute-start(bf16[1,8,1920]{2,1,0:T(8,128)(2,1)} %bitcast.11), channel_id=1, source_target_pairs={{0,8},{2,10},{4,12},{6,14},{8,0},{10,2},{12,4},{14,6},{1,9},{3,11}... | collective-permute-start | bytes 92168 | tf_op jit(solution)/shard_map/ppermute | solution.py:241
  6.9 0.7 %fusion.5 = f32[640,2]{0,1:T(2,128)S(1)} fusion(bf16[640,2]{0,1:T(2,128)(2,1)} %param.9, s32[640,2]{0,1:T(2,128)} %param.7, s32[640,2]{0,1:T(2,128)} %param.8, s32[]{:T(128)S(6)} %mul.51), kind=kLoop, calls=%fused_computation.24 | loop fusion | flops 14080 | bytes 17924 | tf_op jit(solution)/shard_map/add | solution.py:284
  7.7 0.1 dynamic-slice_bitcast_fusion
  7.8 0.2 add_convert_fusion
  8.1 0.1 pad_maximum_fusion.3.stats_ref
  8.2 1.4 %map_own.1.p_ref = f32[144,2048]{1,0:T(8,128)S(1)} custom-call(bf16[144,320]{1,0:T(8,128)(2,1)S(1)} %get-tuple-element.57.w_ref, bf16[16,40960]{1,0:T(8,128)(2,1)S(1)} %copy-done, f32[2,128]{1,0:T(2,128)S(1)} %pad_maximum_fusion.3.stats_ref), custom_call_target="tpu_custom_call" | custom-call | flops 188743680 | bytes 3145728 | tf_op jit(solution)/shard_map/map_own/pallas_call | solution.py:290
  9.6 2.6 %map_rest.1 = bf16[8,16,2176]{2,1,0:T(8,128)(2,1)} custom-call(bf16[144,320]{1,0:T(8,128)(2,1)S(1)} %get-tuple-element.58.w_ref, bf16[16,40960]{1,0:T(8,128)(2,1)S(1)} %collective-permute-done.t_ref, f32[144,2048]{1,0:T(8,128)S(1)} %map_own.1.p_ref, f32[2,128]{1,0:T(2,128)S(1)} %pad_maximum_fusion.3.stats_ref), custom_call_target="tpu_custom_call" | custom-call | flops 188743680 | bytes 4194304 | tf_op jit(solution)/shard_map/map_rest/pallas_call | solution.py:301
  12.2 5.3 %all-to-all-start = ((bf16[8,16,2176]{2,1,0:T(8,128)(2,1)}), bf16[8,16,2176]{2,1,0:T(8,128)(2,1)S(1)}, u32[]{:S(2)}, u32[]{:S(2)}) async-start(bf16[8,16,2176]{2,1,0:T(8,128)(2,1)} %map_rest.1), calls=%async_computation | async-start | bytes 1114112 | tf_op jit(solution)/shard_map/all_to_all | solution.py:317
  17.5 0.1 collective-permute-start.3
  17.6 1.5 %collective-permute-start.6 = (bf16[2,8,1920]{2,1,0:T(8,128)(2,1)S(1)}, bf16[2,8,1920]{2,1,0:T(8,128)(2,1)S(1)}, u32[]{:S(2)}, u32[]{:S(2)}) collective-permute-start(bf16[2,8,1920]{2,1,0:T(8,128)(2,1)S(1)} %constant_dynamic-update-slice_fusion), channel_id=1, source_target_pairs={{0,6},{2,4},{4,2},{6,0},{8,14},{10,12},{12,10},{14,8},{1,7},{3,5},... | collective-permute-start | bytes 184328 | tf_op jit(solution)/shard_map/ppermute | solution.py:241
  19.1 1.5 %collective-permute-start.5 = (bf16[2,8,1920]{2,1,0:T(8,128)(2,1)S(1)}, bf16[2,8,1920]{2,1,0:T(8,128)(2,1)S(1)}, u32[]{:S(2)}, u32[]{:S(2)}) collective-permute-start(bf16[2,8,1920]{2,1,0:T(8,128)(2,1)S(1)} %constant_dynamic-update-slice_fusion), channel_id=1, source_target_pairs={{0,4},{2,6},{4,0},{6,2},{8,12},{10,14},{12,8},{14,10},{1,5},{3,7},... | collective-permute-start | bytes 184328 | tf_op jit(solution)/shard_map/ppermute | solution.py:241
  20.6 0.6 %collective-permute-start.4 = (bf16[2,8,1920]{2,1,0:T(8,128)(2,1)S(1)}, bf16[2,8,1920]{2,1,0:T(8,128)(2,1)S(1)}, u32[]{:S(2)}, u32[]{:S(2)}) collective-permute-start(bf16[2,8,1920]{2,1,0:T(8,128)(2,1)S(1)} %constant_dynamic-update-slice_fusion), channel_id=1, source_target_pairs={{0,2},{2,0},{4,6},{6,4},{8,10},{10,8},{12,14},{14,12},{1,3},{3,1},... | collective-permute-start | bytes 184328 | tf_op jit(solution)/shard_map/ppermute | solution.py:241
  21.2 0.1 broadcast_select_fusion.1
  21.3 8.8 %all-to-all-done.refs_0_ = bf16[8,16,2176]{2,1,0:T(8,128)(2,1)S(1)} async-done(((bf16[8,16,2176]{2,1,0:T(8,128)(2,1)}), bf16[8,16,2176]{2,1,0:T(8,128)(2,1)S(1)}, u32[]{:S(2)}, u32[]{:S(2)}) %all-to-all-start) | async-done | bytes 557088 | tf_op jit(solution)/shard_map/all_to_all | solution.py:317
  30.1 1.2 %logit_grad.1 = (bf16[128,2048]{1,0:T(8,128)(2,1)S(1)}, f32[16,8,128]{2,1,0:T(8,128)}) custom-call(bf16[8,16,2176]{2,1,0:T(8,128)(2,1)S(1)} %all-to-all-done.refs_0_, bf16[128,2048]{1,0:T(8,128)(2,1)S(1)} %pad_maximum_fusion.refs_1_), custom_call_target="tpu_custom_call" | custom-call | flops 2621440 | bytes 1572864 | tf_op jit(solution)/shard_map/logit_grad/pallas_call | solution.py:330
  31.5 0.1 collective-permute-start.7
  31.6 5.5 %all-to-all-start.1 = ((f32[16,8,128]{2,1,0:T(8,128)}), f32[16,8,128]{2,1,0:T(8,128)S(1)}, u32[]{:S(2)}, u32[]{:S(2)}) async-start(f32[16,8,128]{2,1,0:T(8,128)} %get-tuple-element.29), calls=%async_computation.1 | async-start | bytes 131072 | tf_op jit(solution)/shard_map/all_to_all | solution.py:348
  37.1 0.1 pad_add_fusion.place_ref
  37.2 4.5 %weight_grad.1 = (bf16[1920,2048]{1,0:T(8,128)(2,1)}, bf16[64,4096]{1,0:T(8,128)(2,1)}) custom-call(s32[2]{0:T(128)S(1)} %pad_add_fusion.place_ref, bf16[8,8,1920]{2,1,0:T(8,128)(2,1)S(1)} %constant_dynamic-update-slice_fusion.2.own_ref, bf16[64,3968]{1,0:T(8,128)(2,1)S(1)} %collective-permute-done.7.got_ref, bf16[128,2048]{1,0:T(8,128)(2,1)S(1)} %get-tuple-element.37.grad_ref), custom_call_target="tpu_custom_call" | custom-call | flops 1006632960 | bytes 8880128 | tf_op jit(solution)/shard_map/weight_grad/pallas_call | solution.py:353
  41.7 0.0 all-to-all-done.1
  41.7 0.5 %slice_reduce_fusion = f32[64]{0:T(128)} fusion(f32[16,8,128]{2,1,0:T(8,128)S(1)} %all-to-all-done.1), kind=kLoop, calls=%fused_computation.22 | loop fusion | flops 960 | bytes 4352 | tf_op jit(solution)/shard_map/reduce_sum | solution.py:373
  (29 shorter events, 0.3 us)
Async XLA Ops:
  0.6 7.5 %copy-start = (bf16[16,40960]{1,0:T(8,128)(2,1)S(1)}, bf16[16,40960]{1,0:T(8,128)(2,1)}, u32[]{:S(2)}) copy-start(bf16[16,40960]{1,0:T(8,128)(2,1)} %t_ref.1) | copy-start | bytes 3932164
  2.3 7.2 %collective-permute-start = (bf16[16,40960]{1,0:T(8,128)(2,1)}, bf16[16,40960]{1,0:T(8,128)(2,1)S(1)}, u32[]{:S(2)}, u32[]{:S(2)}) collective-permute-start(bf16[16,40960]{1,0:T(8,128)(2,1)} %t_ref.1), channel_id=1, source_target_pairs={{0,1},{1,0},{2,3},{3,2},{4,5},{5,4},{6,7},{7,6},{8,9},{9,8},{10,11... | collective-permute-start | bytes 3932168 | tf_op jit(solution)/shard_map/ppermute | solution.py:237
  2.8 5.2 %collective-permute-start.1 = (f32[2,64]{1,0:T(2,128)S(1)}, f32[2,64]{1,0:T(2,128)S(1)}, u32[]{:S(2)}, u32[]{:S(2)}) collective-permute-start(f32[2,64]{1,0:T(2,128)S(1)} %pad_maximum_fusion.2), channel_id=1, source_target_pairs={{0,1},{1,0},{2,3},{3,2},{4,5},{5,4},{6,7},{7,6},{8,9},{9,8},{10,11... | collective-permute-start | bytes 1544 | tf_op jit(solution)/shard_map/ppermute | solution.py:237
  2.9 9.3 %collective-permute-start.2 = (bf16[1,8,1920]{2,1,0:T(8,128)(2,1)}, bf16[1,8,1920]{2,1,0:T(8,128)(2,1)S(1)}, u32[]{:S(2)}, u32[]{:S(2)}) collective-permute-start(bf16[1,8,1920]{2,1,0:T(8,128)(2,1)} %bitcast.11), channel_id=1, source_target_pairs={{0,8},{2,10},{4,12},{6,14},{8,0},{10,2},{12,4},{14,6},{1,9},{3,11}... | collective-permute-start | bytes 92168 | tf_op jit(solution)/shard_map/ppermute | solution.py:241
  9.6 7.9 %copy-start.1 = (bf16[64,4096]{1,0:T(8,128)(2,1)S(1)}, bf16[64,4096]{1,0:T(8,128)(2,1)}, u32[]{:S(2)}) copy-start(bf16[64,4096]{1,0:T(8,128)(2,1)} %param.10) | copy-start | bytes 1572868
  12.2 5.4 %copy-start.2 = (bf16[8,1920]{1,0:T(8,128)(2,1)S(1)}, bf16[8,1920]{1,0:T(8,128)(2,1)}, u32[]{:S(2)}) copy-start(bf16[8,1920]{1,0:T(8,128)(2,1)} %param.11) | copy-start | bytes 92164
  12.2 17.9 %all-to-all-start = ((bf16[8,16,2176]{2,1,0:T(8,128)(2,1)}), bf16[8,16,2176]{2,1,0:T(8,128)(2,1)S(1)}, u32[]{:S(2)}, u32[]{:S(2)}) async-start(bf16[8,16,2176]{2,1,0:T(8,128)(2,1)} %map_rest.1), calls=%async_computation | async-start | bytes 1114112 | tf_op jit(solution)/shard_map/all_to_all | solution.py:317
  17.5 3.7 %collective-permute-start.3 = (bf16[64,2048]{1,0:T(8,128)(2,1)S(1)}, bf16[64,2048]{1,0:T(8,128)(2,1)S(1)}, u32[]{:S(2)}, u32[]{:S(2)}) collective-permute-start(bf16[64,2048]{1,0:T(8,128)(2,1)S(1)} %constant_dynamic-slice_fusion.1), channel_id=1, source_target_pairs={{0,1},{1,0},{2,3},{3,2},{4,5},{5,4},{6,7},{7,6},{8,9},{9,8},{10,11... | collective-permute-start | bytes 786440 | tf_op jit(solution)/shard_map/ppermute | solution.py:237
  17.6 13.7 %collective-permute-start.6 = (bf16[2,8,1920]{2,1,0:T(8,128)(2,1)S(1)}, bf16[2,8,1920]{2,1,0:T(8,128)(2,1)S(1)}, u32[]{:S(2)}, u32[]{:S(2)}) collective-permute-start(bf16[2,8,1920]{2,1,0:T(8,128)(2,1)S(1)} %constant_dynamic-update-slice_fusion), channel_id=1, source_target_pairs={{0,6},{2,4},{4,2},{6,0},{8,14},{10,12},{12,10},{14,8},{1,7},{3,5},... | collective-permute-start | bytes 184328 | tf_op jit(solution)/shard_map/ppermute | solution.py:241
  19.1 12.2 %collective-permute-start.5 = (bf16[2,8,1920]{2,1,0:T(8,128)(2,1)S(1)}, bf16[2,8,1920]{2,1,0:T(8,128)(2,1)S(1)}, u32[]{:S(2)}, u32[]{:S(2)}) collective-permute-start(bf16[2,8,1920]{2,1,0:T(8,128)(2,1)S(1)} %constant_dynamic-update-slice_fusion), channel_id=1, source_target_pairs={{0,4},{2,6},{4,0},{6,2},{8,12},{10,14},{12,8},{14,10},{1,5},{3,7},... | collective-permute-start | bytes 184328 | tf_op jit(solution)/shard_map/ppermute | solution.py:241
  20.6 10.8 %collective-permute-start.4 = (bf16[2,8,1920]{2,1,0:T(8,128)(2,1)S(1)}, bf16[2,8,1920]{2,1,0:T(8,128)(2,1)S(1)}, u32[]{:S(2)}, u32[]{:S(2)}) collective-permute-start(bf16[2,8,1920]{2,1,0:T(8,128)(2,1)S(1)} %constant_dynamic-update-slice_fusion), channel_id=1, source_target_pairs={{0,2},{2,0},{4,6},{6,4},{8,10},{10,8},{12,14},{14,12},{1,3},{3,1},... | collective-permute-start | bytes 184328 | tf_op jit(solution)/shard_map/ppermute | solution.py:241
  31.5 5.7 %collective-permute-start.7 = (bf16[64,3968]{1,0:T(8,128)(2,1)S(1)}, bf16[64,3968]{1,0:T(8,128)(2,1)S(1)}, u32[]{:S(2)}, u32[]{:S(2)}) collective-permute-start(bf16[64,3968]{1,0:T(8,128)(2,1)S(1)} %pad_maximum_fusion.1), channel_id=1, source_target_pairs={{0,1},{1,0},{2,3},{3,2},{4,5},{5,4},{6,7},{7,6},{8,9},{9,8},{10,11... | collective-permute-start | bytes 1523720 | tf_op jit(solution)/shard_map/ppermute | solution.py:237
  31.6 10.1 %all-to-all-start.1 = ((f32[16,8,128]{2,1,0:T(8,128)}), f32[16,8,128]{2,1,0:T(8,128)S(1)}, u32[]{:S(2)}, u32[]{:S(2)}) async-start(f32[16,8,128]{2,1,0:T(8,128)} %get-tuple-element.29), calls=%async_computation.1 | async-start | bytes 131072 | tf_op jit(solution)/shard_map/all_to_all | solution.py:348

commit v28 on v27

--- a/solution.py
+++ b/solution.py
@@ -207,7 +207,7 @@
                 block_ref[rows, n : n + 2 * BLK] = tile.astype(jnp.bfloat16)
         at = pl.ds(first, size)
         copies.append(pltpu.make_async_copy(block_ref.at[at, :], o_ref.at[at, :], sems.at[i]))
-        copies[-1].start()
+        copies[-1].start(priority=i % 2)
         first += size
     for copy in copies:
         copy.wait()

time: 42.6 us -> 42.6 us (level)
  no operation moved by 1% of the time
where the time goes in v28:
time: 42.6 us; the launch traced here: 42.2 us
  starting transfers between devices  19.1 us (45%)
  Pallas kernels  9.7 us (23%)
  waiting for transfers between devices  8.83 us (21%)
  other arithmetic  3.58 us (8%)
  between operations  0.85 us (2%)
    all_to_all x1, waiting for transfers between devices, body(): lax.all_to_all(outgoing, 'sv', 0, 0, axis_index_groups=[turned_group(owne...  8.78 us
    ppermute x4, starting transfers between devices, to_partner(): lax.ppermute(x, 'sv', [(s, s ^ offset) for s in range(lax.axis_size('sv'))])  7.57 us
    all_to_all x1, starting transfers between devices, body(): lax.all_to_all(terms, ('sv', 'tv'), 0, 0, axis_index_groups=everyone, til...  5.49 us
    all_to_all x1, starting transfers between devices, body(): lax.all_to_all(outgoing, 'sv', 0, 0, axis_index_groups=[turned_group(owne...  5.28 us
    pallas_call x1, Pallas kernels, body(): pl.pallas_call(weight_kernel, out_shape=(shape((features, width), bf16),...  4.51 us
    pallas_call x1, Pallas kernels, body(): pl.pallas_call(map_rest_kernel, out_shape=shape(chunk, bf16), in_specs=[i...  2.57 us
    another operation x1, other arithmetic, body(): lax.reduce((wide, jnp.ones_like(wide)), (low, jnp.float32(0)), merge, (1,))  1.68 us
    pallas_call x1, Pallas kernels, body(): pl.pallas_call(map_own_kernel, out_shape=shape((rows + MASS_ROWS, tokens...  1.4 us
  transfers between devices with their start and end apart: 10, of which 1 were waited for; matrix products, arithmetic and copies ran while one was open for 3% of the time, Pallas kernels for 23%

profile of v28, /device:TPU:0, one launch (start us, length us, event | category | flops | bytes accessed | tf_op | source)
XLA Modules:
  0.0 42.2 jit_solution(3219811317509261073)
XLA Ops:
  0.6 1.7 %convert_reduce_fusion = (f32[64]{0:T(128)S(1)}, f32[64]{0:T(128)S(1)}) fusion(bf16[64,4096]{1,0:T(8,128)(2,1)} %param.10), kind=kLoop, calls=%fused_computation | loop fusion | flops 1834624 | bytes 524800 | tf_op jit(solution)/shard_map/reduce | solution.py:277
  2.3 0.5 %collective-permute-start = (bf16[16,40960]{1,0:T(8,128)(2,1)}, bf16[16,40960]{1,0:T(8,128)(2,1)S(1)}, u32[]{:S(2)}, u32[]{:S(2)}) collective-permute-start(bf16[16,40960]{1,0:T(8,128)(2,1)} %t_ref.1), channel_id=1, source_target_pairs={{0,1},{1,0},{2,3},{3,2},{4,5},{5,4},{6,7},{7,6},{8,9},{9,8},{10,11... | collective-permute-start | bytes 3932168 | tf_op jit(solution)/shard_map/ppermute | solution.py:237
  2.8 0.1 collective-permute-start.1
  2.9 4.0 %collective-permute-start.2 = (bf16[1,8,1920]{2,1,0:T(8,128)(2,1)}, bf16[1,8,1920]{2,1,0:T(8,128)(2,1)S(1)}, u32[]{:S(2)}, u32[]{:S(2)}) collective-permute-start(bf16[1,8,1920]{2,1,0:T(8,128)(2,1)} %bitcast.11), channel_id=1, source_target_pairs={{0,8},{2,10},{4,12},{6,14},{8,0},{10,2},{12,4},{14,6},{1,9},{3,11}... | collective-permute-start | bytes 92168 | tf_op jit(solution)/shard_map/ppermute | solution.py:241
  6.9 0.7 %fusion.5 = f32[640,2]{0,1:T(2,128)S(1)} fusion(bf16[640,2]{0,1:T(2,128)(2,1)} %param.9, s32[640,2]{0,1:T(2,128)} %param.7, s32[640,2]{0,1:T(2,128)} %param.8, s32[]{:T(128)S(6)} %mul.51), kind=kLoop, calls=%fused_computation.24 | loop fusion | flops 14080 | bytes 17924 | tf_op jit(solution)/shard_map/add | solution.py:284
  7.7 0.1 dynamic-slice_bitcast_fusion
  7.8 0.2 add_convert_fusion
  8.1 0.1 pad_maximum_fusion.3.stats_ref
  8.2 1.4 %map_own.1.p_ref = f32[144,2048]{1,0:T(8,128)S(1)} custom-call(bf16[144,320]{1,0:T(8,128)(2,1)S(1)} %get-tuple-element.57.w_ref, bf16[16,40960]{1,0:T(8,128)(2,1)S(1)} %copy-done, f32[2,128]{1,0:T(2,128)S(1)} %pad_maximum_fusion.3.stats_ref), custom_call_target="tpu_custom_call" | custom-call | flops 188743680 | bytes 3145728 | tf_op jit(solution)/shard_map/map_own/pallas_call | solution.py:290
  9.6 2.6 %map_rest.1 = bf16[8,16,2176]{2,1,0:T(8,128)(2,1)} custom-call(bf16[144,320]{1,0:T(8,128)(2,1)S(1)} %get-tuple-element.58.w_ref, bf16[16,40960]{1,0:T(8,128)(2,1)S(1)} %collective-permute-done.t_ref, f32[144,2048]{1,0:T(8,128)S(1)} %map_own.1.p_ref, f32[2,128]{1,0:T(2,128)S(1)} %pad_maximum_fusion.3.stats_ref), custom_call_target="tpu_custom_call" | custom-call | flops 188743680 | bytes 4194304 | tf_op jit(solution)/shard_map/map_rest/pallas_call | solution.py:301
  12.2 5.3 %all-to-all-start = ((bf16[8,16,2176]{2,1,0:T(8,128)(2,1)}), bf16[8,16,2176]{2,1,0:T(8,128)(2,1)S(1)}, u32[]{:S(2)}, u32[]{:S(2)}) async-start(bf16[8,16,2176]{2,1,0:T(8,128)(2,1)} %map_rest.1), calls=%async_computation | async-start | bytes 1114112 | tf_op jit(solution)/shard_map/all_to_all | solution.py:317
  17.5 0.1 collective-permute-start.3
  17.6 1.5 %collective-permute-start.6 = (bf16[2,8,1920]{2,1,0:T(8,128)(2,1)S(1)}, bf16[2,8,1920]{2,1,0:T(8,128)(2,1)S(1)}, u32[]{:S(2)}, u32[]{:S(2)}) collective-permute-start(bf16[2,8,1920]{2,1,0:T(8,128)(2,1)S(1)} %constant_dynamic-update-slice_fusion), channel_id=1, source_target_pairs={{0,6},{2,4},{4,2},{6,0},{8,14},{10,12},{12,10},{14,8},{1,7},{3,5},... | collective-permute-start | bytes 184328 | tf_op jit(solution)/shard_map/ppermute | solution.py:241
  19.1 1.5 %collective-permute-start.5 = (bf16[2,8,1920]{2,1,0:T(8,128)(2,1)S(1)}, bf16[2,8,1920]{2,1,0:T(8,128)(2,1)S(1)}, u32[]{:S(2)}, u32[]{:S(2)}) collective-permute-start(bf16[2,8,1920]{2,1,0:T(8,128)(2,1)S(1)} %constant_dynamic-update-slice_fusion), channel_id=1, source_target_pairs={{0,4},{2,6},{4,0},{6,2},{8,12},{10,14},{12,8},{14,10},{1,5},{3,7},... | collective-permute-start | bytes 184328 | tf_op jit(solution)/shard_map/ppermute | solution.py:241
  20.6 0.6 %collective-permute-start.4 = (bf16[2,8,1920]{2,1,0:T(8,128)(2,1)S(1)}, bf16[2,8,1920]{2,1,0:T(8,128)(2,1)S(1)}, u32[]{:S(2)}, u32[]{:S(2)}) collective-permute-start(bf16[2,8,1920]{2,1,0:T(8,128)(2,1)S(1)} %constant_dynamic-update-slice_fusion), channel_id=1, source_target_pairs={{0,2},{2,0},{4,6},{6,4},{8,10},{10,8},{12,14},{14,12},{1,3},{3,1},... | collective-permute-start | bytes 184328 | tf_op jit(solution)/shard_map/ppermute | solution.py:241
  21.2 0.1 broadcast_select_fusion.1
  21.3 8.8 %all-to-all-done.refs_0_ = bf16[8,16,2176]{2,1,0:T(8,128)(2,1)S(1)} async-done(((bf16[8,16,2176]{2,1,0:T(8,128)(2,1)}), bf16[8,16,2176]{2,1,0:T(8,128)(2,1)S(1)}, u32[]{:S(2)}, u32[]{:S(2)}) %all-to-all-start) | async-done | bytes 557088 | tf_op jit(solution)/shard_map/all_to_all | solution.py:317
  30.1 1.2 %logit_grad.1 = (bf16[128,2048]{1,0:T(8,128)(2,1)S(1)}, f32[16,8,128]{2,1,0:T(8,128)}) custom-call(bf16[8,16,2176]{2,1,0:T(8,128)(2,1)S(1)} %all-to-all-done.refs_0_, bf16[128,2048]{1,0:T(8,128)(2,1)S(1)} %pad_maximum_fusion.refs_1_), custom_call_target="tpu_custom_call" | custom-call | flops 2621440 | bytes 1572864 | tf_op jit(solution)/shard_map/logit_grad/pallas_call | solution.py:330
  31.5 0.1 collective-permute-start.7
  31.6 5.5 %all-to-all-start.1 = ((f32[16,8,128]{2,1,0:T(8,128)}), f32[16,8,128]{2,1,0:T(8,128)S(1)}, u32[]{:S(2)}, u32[]{:S(2)}) async-start(f32[16,8,128]{2,1,0:T(8,128)} %get-tuple-element.29), calls=%async_computation.1 | async-start | bytes 131072 | tf_op jit(solution)/shard_map/all_to_all | solution.py:348
  37.1 0.1 pad_add_fusion.place_ref
  37.2 4.5 %weight_grad.1 = (bf16[1920,2048]{1,0:T(8,128)(2,1)}, bf16[64,4096]{1,0:T(8,128)(2,1)}) custom-call(s32[2]{0:T(128)S(1)} %pad_add_fusion.place_ref, bf16[8,8,1920]{2,1,0:T(8,128)(2,1)S(1)} %constant_dynamic-update-slice_fusion.2.own_ref, bf16[64,3968]{1,0:T(8,128)(2,1)S(1)} %collective-permute-done.7.got_ref, bf16[128,2048]{1,0:T(8,128)(2,1)S(1)} %get-tuple-element.37.grad_ref), custom_call_target="tpu_custom_call" | custom-call | flops 1006632960 | bytes 8880128 | tf_op jit(solution)/shard_map/weight_grad/pallas_call | solution.py:353
  41.7 0.0 all-to-all-done.1
  41.7 0.5 %slice_reduce_fusion = f32[64]{0:T(128)} fusion(f32[16,8,128]{2,1,0:T(8,128)S(1)} %all-to-all-done.1), kind=kLoop, calls=%fused_computation.22 | loop fusion | flops 960 | bytes 4352 | tf_op jit(solution)/shard_map/reduce_sum | solution.py:373
  (29 shorter events, 0.3 us)
Async XLA Ops:
  0.6 7.5 %copy-start = (bf16[16,40960]{1,0:T(8,128)(2,1)S(1)}, bf16[16,40960]{1,0:T(8,128)(2,1)}, u32[]{:S(2)}) copy-start(bf16[16,40960]{1,0:T(8,128)(2,1)} %t_ref.1) | copy-start | bytes 3932164
  2.3 7.2 %collective-permute-start = (bf16[16,40960]{1,0:T(8,128)(2,1)}, bf16[16,40960]{1,0:T(8,128)(2,1)S(1)}, u32[]{:S(2)}, u32[]{:S(2)}) collective-permute-start(bf16[16,40960]{1,0:T(8,128)(2,1)} %t_ref.1), channel_id=1, source_target_pairs={{0,1},{1,0},{2,3},{3,2},{4,5},{5,4},{6,7},{7,6},{8,9},{9,8},{10,11... | collective-permute-start | bytes 3932168 | tf_op jit(solution)/shard_map/ppermute | solution.py:237
  2.8 5.2 %collective-permute-start.1 = (f32[2,64]{1,0:T(2,128)S(1)}, f32[2,64]{1,0:T(2,128)S(1)}, u32[]{:S(2)}, u32[]{:S(2)}) collective-permute-start(f32[2,64]{1,0:T(2,128)S(1)} %pad_maximum_fusion.2), channel_id=1, source_target_pairs={{0,1},{1,0},{2,3},{3,2},{4,5},{5,4},{6,7},{7,6},{8,9},{9,8},{10,11... | collective-permute-start | bytes 1544 | tf_op jit(solution)/shard_map/ppermute | solution.py:237
  2.9 9.3 %collective-permute-start.2 = (bf16[1,8,1920]{2,1,0:T(8,128)(2,1)}, bf16[1,8,1920]{2,1,0:T(8,128)(2,1)S(1)}, u32[]{:S(2)}, u32[]{:S(2)}) collective-permute-start(bf16[1,8,1920]{2,1,0:T(8,128)(2,1)} %bitcast.11), channel_id=1, source_target_pairs={{0,8},{2,10},{4,12},{6,14},{8,0},{10,2},{12,4},{14,6},{1,9},{3,11}... | collective-permute-start | bytes 92168 | tf_op jit(solution)/shard_map/ppermute | solution.py:241
  9.6 7.9 %copy-start.1 = (bf16[64,4096]{1,0:T(8,128)(2,1)S(1)}, bf16[64,4096]{1,0:T(8,128)(2,1)}, u32[]{:S(2)}) copy-start(bf16[64,4096]{1,0:T(8,128)(2,1)} %param.10) | copy-start | bytes 1572868
  12.2 5.4 %copy-start.2 = (bf16[8,1920]{1,0:T(8,128)(2,1)S(1)}, bf16[8,1920]{1,0:T(8,128)(2,1)}, u32[]{:S(2)}) copy-start(bf16[8,1920]{1,0:T(8,128)(2,1)} %param.11) | copy-start | bytes 92164
  12.2 17.9 %all-to-all-start = ((bf16[8,16,2176]{2,1,0:T(8,128)(2,1)}), bf16[8,16,2176]{2,1,0:T(8,128)(2,1)S(1)}, u32[]{:S(2)}, u32[]{:S(2)}) async-start(bf16[8,16,2176]{2,1,0:T(8,128)(2,1)} %map_rest.1), calls=%async_computation | async-start | bytes 1114112 | tf_op jit(solution)/shard_map/all_to_all | solution.py:317
  17.5 3.7 %collective-permute-start.3 = (bf16[64,2048]{1,0:T(8,128)(2,1)S(1)}, bf16[64,2048]{1,0:T(8,128)(2,1)S(1)}, u32[]{:S(2)}, u32[]{:S(2)}) collective-permute-start(bf16[64,2048]{1,0:T(8,128)(2,1)S(1)} %constant_dynamic-slice_fusion.1), channel_id=1, source_target_pairs={{0,1},{1,0},{2,3},{3,2},{4,5},{5,4},{6,7},{7,6},{8,9},{9,8},{10,11... | collective-permute-start | bytes 786440 | tf_op jit(solution)/shard_map/ppermute | solution.py:237
  17.6 13.7 %collective-permute-start.6 = (bf16[2,8,1920]{2,1,0:T(8,128)(2,1)S(1)}, bf16[2,8,1920]{2,1,0:T(8,128)(2,1)S(1)}, u32[]{:S(2)}, u32[]{:S(2)}) collective-permute-start(bf16[2,8,1920]{2,1,0:T(8,128)(2,1)S(1)} %constant_dynamic-update-slice_fusion), channel_id=1, source_target_pairs={{0,6},{2,4},{4,2},{6,0},{8,14},{10,12},{12,10},{14,8},{1,7},{3,5},... | collective-permute-start | bytes 184328 | tf_op jit(solution)/shard_map/ppermute | solution.py:241
  19.1 12.2 %collective-permute-start.5 = (bf16[2,8,1920]{2,1,0:T(8,128)(2,1)S(1)}, bf16[2,8,1920]{2,1,0:T(8,128)(2,1)S(1)}, u32[]{:S(2)}, u32[]{:S(2)}) collective-permute-start(bf16[2,8,1920]{2,1,0:T(8,128)(2,1)S(1)} %constant_dynamic-update-slice_fusion), channel_id=1, source_target_pairs={{0,4},{2,6},{4,0},{6,2},{8,12},{10,14},{12,8},{14,10},{1,5},{3,7},... | collective-permute-start | bytes 184328 | tf_op jit(solution)/shard_map/ppermute | solution.py:241
  20.6 10.8 %collective-permute-start.4 = (bf16[2,8,1920]{2,1,0:T(8,128)(2,1)S(1)}, bf16[2,8,1920]{2,1,0:T(8,128)(2,1)S(1)}, u32[]{:S(2)}, u32[]{:S(2)}) collective-permute-start(bf16[2,8,1920]{2,1,0:T(8,128)(2,1)S(1)} %constant_dynamic-update-slice_fusion), channel_id=1, source_target_pairs={{0,2},{2,0},{4,6},{6,4},{8,10},{10,8},{12,14},{14,12},{1,3},{3,1},... | collective-permute-start | bytes 184328 | tf_op jit(solution)/shard_map/ppermute | solution.py:241
  31.5 5.7 %collective-permute-start.7 = (bf16[64,3968]{1,0:T(8,128)(2,1)S(1)}, bf16[64,3968]{1,0:T(8,128)(2,1)S(1)}, u32[]{:S(2)}, u32[]{:S(2)}) collective-permute-start(bf16[64,3968]{1,0:T(8,128)(2,1)S(1)} %pad_maximum_fusion.1), channel_id=1, source_target_pairs={{0,1},{1,0},{2,3},{3,2},{4,5},{5,4},{6,7},{7,6},{8,9},{9,8},{10,11... | collective-permute-start | bytes 1523720 | tf_op jit(solution)/shard_map/ppermute | solution.py:237
  31.6 10.1 %all-to-all-start.1 = ((f32[16,8,128]{2,1,0:T(8,128)}), f32[16,8,128]{2,1,0:T(8,128)S(1)}, u32[]{:S(2)}, u32[]{:S(2)}) async-start(f32[16,8,128]{2,1,0:T(8,128)} %get-tuple-element.29), calls=%async_computation.1 | async-start | bytes 131072 | tf_op jit(solution)/shard_map/all_to_all | solution.py:348

commit v29 on v27

--- a/solution.py
+++ b/solution.py
@@ -9,7 +9,7 @@
 TB = 640
 TOPA = 2
 MASS_ROWS = 16
-STEP = 16
+STEP = 160
 
 
 def block_weights(code, rows):

time: 42.6 us -> 42.4 us (level)
  no operation moved by 1% of the time
where the time goes in v29:
time: 42.4 us; the launch traced here: 42.1 us
  starting transfers between devices  19.1 us (45%)
  Pallas kernels  9.51 us (22%)
  waiting for transfers between devices  8.83 us (21%)
  other arithmetic  3.58 us (8%)
  between operations  0.85 us (2%)
    all_to_all x1, waiting for transfers between devices, body(): lax.all_to_all(outgoing, 'sv', 0, 0, axis_index_groups=[turned_group(owne...  8.78 us
    ppermute x4, starting transfers between devices, to_partner(): lax.ppermute(x, 'sv', [(s, s ^ offset) for s in range(lax.axis_size('sv'))])  7.57 us
    all_to_all x1, starting transfers between devices, body(): lax.all_to_all(terms, ('sv', 'tv'), 0, 0, axis_index_groups=everyone, til...  5.49 us
    all_to_all x1, starting transfers between devices, body(): lax.all_to_all(outgoing, 'sv', 0, 0, axis_index_groups=[turned_group(owne...  5.28 us
    pallas_call x1, Pallas kernels, body(): pl.pallas_call(weight_kernel, out_shape=(shape((features, width), bf16),...  4.51 us
    pallas_call x1, Pallas kernels, body(): pl.pallas_call(map_rest_kernel, out_shape=shape(chunk, bf16), in_specs=[i...  2.48 us
    another operation x1, other arithmetic, body(): lax.reduce((wide, jnp.ones_like(wide)), (low, jnp.float32(0)), merge, (1,))  1.68 us
    pallas_call x1, Pallas kernels, body(): pl.pallas_call(map_own_kernel, out_shape=shape((rows + MASS_ROWS, tokens...  1.31 us
  transfers between devices with their start and end apart: 10, of which 1 were waited for; matrix products, arithmetic and copies ran while one was open for 3% of the time, Pallas kernels for 23%

profile of v29, /device:TPU:0, one launch (start us, length us, event | category | flops | bytes accessed | tf_op | source)
XLA Modules:
  0.0 42.1 jit_solution(7967358261924676226)
XLA Ops:
  0.6 1.7 %convert_reduce_fusion = (f32[64]{0:T(128)S(1)}, f32[64]{0:T(128)S(1)}) fusion(bf16[64,4096]{1,0:T(8,128)(2,1)} %param.10), kind=kLoop, calls=%fused_computation | loop fusion | flops 1834624 | bytes 524800 | tf_op jit(solution)/shard_map/reduce | solution.py:277
  2.3 0.5 %collective-permute-start = (bf16[16,40960]{1,0:T(8,128)(2,1)}, bf16[16,40960]{1,0:T(8,128)(2,1)S(1)}, u32[]{:S(2)}, u32[]{:S(2)}) collective-permute-start(bf16[16,40960]{1,0:T(8,128)(2,1)} %t_ref.1), channel_id=1, source_target_pairs={{0,1},{1,0},{2,3},{3,2},{4,5},{5,4},{6,7},{7,6},{8,9},{9,8},{10,11... | collective-permute-start | bytes 3932168 | tf_op jit(solution)/shard_map/ppermute | solution.py:237
  2.8 0.1 collective-permute-start.1
  2.9 4.0 %collective-permute-start.2 = (bf16[1,8,1920]{2,1,0:T(8,128)(2,1)}, bf16[1,8,1920]{2,1,0:T(8,128)(2,1)S(1)}, u32[]{:S(2)}, u32[]{:S(2)}) collective-permute-start(bf16[1,8,1920]{2,1,0:T(8,128)(2,1)} %bitcast.11), channel_id=1, source_target_pairs={{0,8},{2,10},{4,12},{6,14},{8,0},{10,2},{12,4},{14,6},{1,9},{3,11}... | collective-permute-start | bytes 92168 | tf_op jit(solution)/shard_map/ppermute | solution.py:241
  6.9 0.7 %fusion.5 = f32[640,2]{0,1:T(2,128)S(1)} fusion(bf16[640,2]{0,1:T(2,128)(2,1)} %param.9, s32[640,2]{0,1:T(2,128)} %param.7, s32[640,2]{0,1:T(2,128)} %param.8, s32[]{:T(128)S(6)} %mul.51), kind=kLoop, calls=%fused_computation.24 | loop fusion | flops 14080 | bytes 17924 | tf_op jit(solution)/shard_map/add | solution.py:284
  7.7 0.1 dynamic-slice_bitcast_fusion
  7.8 0.2 add_convert_fusion
  8.1 0.1 pad_maximum_fusion.3.stats_ref
  8.2 1.3 %map_own.1.p_ref = f32[144,2048]{1,0:T(8,128)S(1)} custom-call(bf16[144,320]{1,0:T(8,128)(2,1)S(1)} %get-tuple-element.57.w_ref, bf16[16,40960]{1,0:T(8,128)(2,1)S(1)} %copy-done, f32[2,128]{1,0:T(2,128)S(1)} %pad_maximum_fusion.3.stats_ref), custom_call_target="tpu_custom_call" | custom-call | flops 188743680 | bytes 3145728 | tf_op jit(solution)/shard_map/map_own/pallas_call | solution.py:290
  9.5 2.5 %map_rest.1 = bf16[8,16,2176]{2,1,0:T(8,128)(2,1)} custom-call(bf16[144,320]{1,0:T(8,128)(2,1)S(1)} %get-tuple-element.58.w_ref, bf16[16,40960]{1,0:T(8,128)(2,1)S(1)} %collective-permute-done.t_ref, f32[144,2048]{1,0:T(8,128)S(1)} %map_own.1.p_ref, f32[2,128]{1,0:T(2,128)S(1)} %pad_maximum_fusion.3.stats_ref), custom_call_target="tpu_custom_call" | custom-call | flops 188743680 | bytes 4194304 | tf_op jit(solution)/shard_map/map_rest/pallas_call | solution.py:301
  12.0 5.3 %all-to-all-start = ((bf16[8,16,2176]{2,1,0:T(8,128)(2,1)}), bf16[8,16,2176]{2,1,0:T(8,128)(2,1)S(1)}, u32[]{:S(2)}, u32[]{:S(2)}) async-start(bf16[8,16,2176]{2,1,0:T(8,128)(2,1)} %map_rest.1), calls=%async_computation | async-start | bytes 1114112 | tf_op jit(solution)/shard_map/all_to_all | solution.py:317
  17.3 0.1 collective-permute-start.3
  17.4 1.5 %collective-permute-start.6 = (bf16[2,8,1920]{2,1,0:T(8,128)(2,1)S(1)}, bf16[2,8,1920]{2,1,0:T(8,128)(2,1)S(1)}, u32[]{:S(2)}, u32[]{:S(2)}) collective-permute-start(bf16[2,8,1920]{2,1,0:T(8,128)(2,1)S(1)} %constant_dynamic-update-slice_fusion), channel_id=1, source_target_pairs={{0,6},{2,4},{4,2},{6,0},{8,14},{10,12},{12,10},{14,8},{1,7},{3,5},... | collective-permute-start | bytes 184328 | tf_op jit(solution)/shard_map/ppermute | solution.py:241
  18.9 1.5 %collective-permute-start.5 = (bf16[2,8,1920]{2,1,0:T(8,128)(2,1)S(1)}, bf16[2,8,1920]{2,1,0:T(8,128)(2,1)S(1)}, u32[]{:S(2)}, u32[]{:S(2)}) collective-permute-start(bf16[2,8,1920]{2,1,0:T(8,128)(2,1)S(1)} %constant_dynamic-update-slice_fusion), channel_id=1, source_target_pairs={{0,4},{2,6},{4,0},{6,2},{8,12},{10,14},{12,8},{14,10},{1,5},{3,7},... | collective-permute-start | bytes 184328 | tf_op jit(solution)/shard_map/ppermute | solution.py:241
  20.4 0.6 %collective-permute-start.4 = (bf16[2,8,1920]{2,1,0:T(8,128)(2,1)S(1)}, bf16[2,8,1920]{2,1,0:T(8,128)(2,1)S(1)}, u32[]{:S(2)}, u32[]{:S(2)}) collective-permute-start(bf16[2,8,1920]{2,1,0:T(8,128)(2,1)S(1)} %constant_dynamic-update-slice_fusion), channel_id=1, source_target_pairs={{0,2},{2,0},{4,6},{6,4},{8,10},{10,8},{12,14},{14,12},{1,3},{3,1},... | collective-permute-start | bytes 184328 | tf_op jit(solution)/shard_map/ppermute | solution.py:241
  21.0 0.1 broadcast_select_fusion.1
  21.1 8.8 %all-to-all-done.refs_0_ = bf16[8,16,2176]{2,1,0:T(8,128)(2,1)S(1)} async-done(((bf16[8,16,2176]{2,1,0:T(8,128)(2,1)}), bf16[8,16,2176]{2,1,0:T(8,128)(2,1)S(1)}, u32[]{:S(2)}, u32[]{:S(2)}) %all-to-all-start) | async-done | bytes 557088 | tf_op jit(solution)/shard_map/all_to_all | solution.py:317
  29.9 1.2 %logit_grad.1 = (bf16[128,2048]{1,0:T(8,128)(2,1)S(1)}, f32[16,8,128]{2,1,0:T(8,128)}) custom-call(bf16[8,16,2176]{2,1,0:T(8,128)(2,1)S(1)} %all-to-all-done.refs_0_, bf16[128,2048]{1,0:T(8,128)(2,1)S(1)} %pad_maximum_fusion.refs_1_), custom_call_target="tpu_custom_call" | custom-call | flops 2621440 | bytes 1572864 | tf_op jit(solution)/shard_map/logit_grad/pallas_call | solution.py:330
  31.3 0.1 collective-permute-start.7
  31.4 5.5 %all-to-all-start.1 = ((f32[16,8,128]{2,1,0:T(8,128)}), f32[16,8,128]{2,1,0:T(8,128)S(1)}, u32[]{:S(2)}, u32[]{:S(2)}) async-start(f32[16,8,128]{2,1,0:T(8,128)} %get-tuple-element.29), calls=%async_computation.1 | async-start | bytes 131072 | tf_op jit(solution)/shard_map/all_to_all | solution.py:348
  36.9 0.1 pad_add_fusion.place_ref
  37.0 4.5 %weight_grad.1 = (bf16[1920,2048]{1,0:T(8,128)(2,1)}, bf16[64,4096]{1,0:T(8,128)(2,1)}) custom-call(s32[2]{0:T(128)S(1)} %pad_add_fusion.place_ref, bf16[8,8,1920]{2,1,0:T(8,128)(2,1)S(1)} %constant_dynamic-update-slice_fusion.2.own_ref, bf16[64,3968]{1,0:T(8,128)(2,1)S(1)} %collective-permute-done.7.got_ref, bf16[128,2048]{1,0:T(8,128)(2,1)S(1)} %get-tuple-element.37.grad_ref), custom_call_target="tpu_custom_call" | custom-call | flops 1006632960 | bytes 8880128 | tf_op jit(solution)/shard_map/weight_grad/pallas_call | solution.py:353
  41.5 0.0 all-to-all-done.1
  41.5 0.5 %slice_reduce_fusion = f32[64]{0:T(128)} fusion(f32[16,8,128]{2,1,0:T(8,128)S(1)} %all-to-all-done.1), kind=kLoop, calls=%fused_computation.22 | loop fusion | flops 960 | bytes 4352 | tf_op jit(solution)/shard_map/reduce_sum | solution.py:373
  (29 shorter events, 0.3 us)
Async XLA Ops:
  0.6 7.5 %copy-start = (bf16[16,40960]{1,0:T(8,128)(2,1)S(1)}, bf16[16,40960]{1,0:T(8,128)(2,1)}, u32[]{:S(2)}) copy-start(bf16[16,40960]{1,0:T(8,128)(2,1)} %t_ref.1) | copy-start | bytes 3932164
  2.3 7.1 %collective-permute-start = (bf16[16,40960]{1,0:T(8,128)(2,1)}, bf16[16,40960]{1,0:T(8,128)(2,1)S(1)}, u32[]{:S(2)}, u32[]{:S(2)}) collective-permute-start(bf16[16,40960]{1,0:T(8,128)(2,1)} %t_ref.1), channel_id=1, source_target_pairs={{0,1},{1,0},{2,3},{3,2},{4,5},{5,4},{6,7},{7,6},{8,9},{9,8},{10,11... | collective-permute-start | bytes 3932168 | tf_op jit(solution)/shard_map/ppermute | solution.py:237
  2.8 5.2 %collective-permute-start.1 = (f32[2,64]{1,0:T(2,128)S(1)}, f32[2,64]{1,0:T(2,128)S(1)}, u32[]{:S(2)}, u32[]{:S(2)}) collective-permute-start(f32[2,64]{1,0:T(2,128)S(1)} %pad_maximum_fusion.2), channel_id=1, source_target_pairs={{0,1},{1,0},{2,3},{3,2},{4,5},{5,4},{6,7},{7,6},{8,9},{9,8},{10,11... | collective-permute-start | bytes 1544 | tf_op jit(solution)/shard_map/ppermute | solution.py:237
  2.9 9.1 %collective-permute-start.2 = (bf16[1,8,1920]{2,1,0:T(8,128)(2,1)}, bf16[1,8,1920]{2,1,0:T(8,128)(2,1)S(1)}, u32[]{:S(2)}, u32[]{:S(2)}) collective-permute-start(bf16[1,8,1920]{2,1,0:T(8,128)(2,1)} %bitcast.11), channel_id=1, source_target_pairs={{0,8},{2,10},{4,12},{6,14},{8,0},{10,2},{12,4},{14,6},{1,9},{3,11}... | collective-permute-start | bytes 92168 | tf_op jit(solution)/shard_map/ppermute | solution.py:241
  9.5 7.8 %copy-start.1 = (bf16[64,4096]{1,0:T(8,128)(2,1)S(1)}, bf16[64,4096]{1,0:T(8,128)(2,1)}, u32[]{:S(2)}) copy-start(bf16[64,4096]{1,0:T(8,128)(2,1)} %param.10) | copy-start | bytes 1572868
  12.0 5.4 %copy-start.2 = (bf16[8,1920]{1,0:T(8,128)(2,1)S(1)}, bf16[8,1920]{1,0:T(8,128)(2,1)}, u32[]{:S(2)}) copy-start(bf16[8,1920]{1,0:T(8,128)(2,1)} %param.11) | copy-start | bytes 92164
  12.0 17.9 %all-to-all-start = ((bf16[8,16,2176]{2,1,0:T(8,128)(2,1)}), bf16[8,16,2176]{2,1,0:T(8,128)(2,1)S(1)}, u32[]{:S(2)}, u32[]{:S(2)}) async-start(bf16[8,16,2176]{2,1,0:T(8,128)(2,1)} %map_rest.1), calls=%async_computation | async-start | bytes 1114112 | tf_op jit(solution)/shard_map/all_to_all | solution.py:317
  17.3 3.7 %collective-permute-start.3 = (bf16[64,2048]{1,0:T(8,128)(2,1)S(1)}, bf16[64,2048]{1,0:T(8,128)(2,1)S(1)}, u32[]{:S(2)}, u32[]{:S(2)}) collective-permute-start(bf16[64,2048]{1,0:T(8,128)(2,1)S(1)} %constant_dynamic-slice_fusion.1), channel_id=1, source_target_pairs={{0,1},{1,0},{2,3},{3,2},{4,5},{5,4},{6,7},{7,6},{8,9},{9,8},{10,11... | collective-permute-start | bytes 786440 | tf_op jit(solution)/shard_map/ppermute | solution.py:237
  17.4 13.7 %collective-permute-start.6 = (bf16[2,8,1920]{2,1,0:T(8,128)(2,1)S(1)}, bf16[2,8,1920]{2,1,0:T(8,128)(2,1)S(1)}, u32[]{:S(2)}, u32[]{:S(2)}) collective-permute-start(bf16[2,8,1920]{2,1,0:T(8,128)(2,1)S(1)} %constant_dynamic-update-slice_fusion), channel_id=1, source_target_pairs={{0,6},{2,4},{4,2},{6,0},{8,14},{10,12},{12,10},{14,8},{1,7},{3,5},... | collective-permute-start | bytes 184328 | tf_op jit(solution)/shard_map/ppermute | solution.py:241
  18.9 12.2 %collective-permute-start.5 = (bf16[2,8,1920]{2,1,0:T(8,128)(2,1)S(1)}, bf16[2,8,1920]{2,1,0:T(8,128)(2,1)S(1)}, u32[]{:S(2)}, u32[]{:S(2)}) collective-permute-start(bf16[2,8,1920]{2,1,0:T(8,128)(2,1)S(1)} %constant_dynamic-update-slice_fusion), channel_id=1, source_target_pairs={{0,4},{2,6},{4,0},{6,2},{8,12},{10,14},{12,8},{14,10},{1,5},{3,7},... | collective-permute-start | bytes 184328 | tf_op jit(solution)/shard_map/ppermute | solution.py:241
  20.4 10.8 %collective-permute-start.4 = (bf16[2,8,1920]{2,1,0:T(8,128)(2,1)S(1)}, bf16[2,8,1920]{2,1,0:T(8,128)(2,1)S(1)}, u32[]{:S(2)}, u32[]{:S(2)}) collective-permute-start(bf16[2,8,1920]{2,1,0:T(8,128)(2,1)S(1)} %constant_dynamic-update-slice_fusion), channel_id=1, source_target_pairs={{0,2},{2,0},{4,6},{6,4},{8,10},{10,8},{12,14},{14,12},{1,3},{3,1},... | collective-permute-start | bytes 184328 | tf_op jit(solution)/shard_map/ppermute | solution.py:241
  31.3 5.7 %collective-permute-start.7 = (bf16[64,3968]{1,0:T(8,128)(2,1)S(1)}, bf16[64,3968]{1,0:T(8,128)(2,1)S(1)}, u32[]{:S(2)}, u32[]{:S(2)}) collective-permute-start(bf16[64,3968]{1,0:T(8,128)(2,1)S(1)} %pad_maximum_fusion.1), channel_id=1, source_target_pairs={{0,1},{1,0},{2,3},{3,2},{4,5},{5,4},{6,7},{7,6},{8,9},{9,8},{10,11... | collective-permute-start | bytes 1523720 | tf_op jit(solution)/shard_map/ppermute | solution.py:237
  31.4 10.1 %all-to-all-start.1 = ((f32[16,8,128]{2,1,0:T(8,128)}), f32[16,8,128]{2,1,0:T(8,128)S(1)}, u32[]{:S(2)}, u32[]{:S(2)}) async-start(f32[16,8,128]{2,1,0:T(8,128)} %get-tuple-element.29), calls=%async_computation.1 | async-start | bytes 131072 | tf_op jit(solution)/shard_map/all_to_all | solution.py:348

commit v30 on v29

--- a/solution.py
+++ b/solution.py
@@ -90,10 +90,10 @@
         return pltpu.make_async_copy(o_buf.at[q], o_ref.at[q], out_sem.at[q])
 
     def owner(q, carry):
-        member = lax.rem(q + owners // 2, owners)
+        member = (q + owners // 2) % owners
         for b in range(mine):
-            first = pl.multiple_of((member * mine + b) * tokens, tokens)
-            tile = m_ref[pl.ds(first, tokens), :] * inverse
+            first = (member * mine + b) * tokens
+            tile = m_ref[first : first + tokens, :] * inverse
             o_buf[q, :, b * BLK : (b + 1) * BLK] = tile.astype(jnp.bfloat16)
         o_buf[q, :, mine * BLK :] = extra
         leaving(q).start()
@@ -103,8 +103,10 @@
         leaving(q).wait()
         return carry
 
-    lax.fori_loop(0, owners, owner, 0)
-    lax.fori_loop(0, owners, left, 0)
+    for q in range(owners):
+        owner(q, 0)
+    for q in range(owners):
+        left(q, 0)
 
 
 def grad_kernel(scale, target_ref, logits_ref, grad_ref, terms_ref, norm_ref, t_buf, sem):

time: 42.4 us -> 42.5 us (level)
  no operation moved by 1% of the time
where the time goes in v30:
time: 42.5 us; the launch traced here: 42.1 us
  starting transfers between devices  19.1 us (45%)
  Pallas kernels  9.56 us (22%)
  waiting for transfers between devices  8.83 us (21%)
  other arithmetic  3.58 us (8%)
  between operations  0.85 us (2%)
    all_to_all x1, waiting for transfers between devices, body(): lax.all_to_all(outgoing, 'sv', 0, 0, axis_index_groups=[turned_group(owne...  8.78 us
    ppermute x4, starting transfers between devices, to_partner(): lax.ppermute(x, 'sv', [(s, s ^ offset) for s in range(lax.axis_size('sv'))])  7.57 us
    all_to_all x1, starting transfers between devices, body(): lax.all_to_all(terms, ('sv', 'tv'), 0, 0, axis_index_groups=everyone, til...  5.49 us
    all_to_all x1, starting transfers between devices, body(): lax.all_to_all(outgoing, 'sv', 0, 0, axis_index_groups=[turned_group(owne...  5.28 us
    pallas_call x1, Pallas kernels, body(): pl.pallas_call(weight_kernel, out_shape=(shape((features, width), bf16),...  4.51 us
    pallas_call x1, Pallas kernels, body(): pl.pallas_call(map_rest_kernel, out_shape=shape(chunk, bf16), in_specs=[i...  2.52 us
    another operation x1, other arithmetic, body(): lax.reduce((wide, jnp.ones_like(wide)), (low, jnp.float32(0)), merge, (1,))  1.68 us
    pallas_call x1, Pallas kernels, body(): pl.pallas_call(map_own_kernel, out_shape=shape((rows + MASS_ROWS, tokens...  1.31 us
  transfers between devices with their start and end apart: 10, of which 1 were waited for; matrix products, arithmetic and copies ran while one was open for 3% of the time, Pallas kernels for 23%

profile of v30, /device:TPU:0, one launch (start us, length us, event | category | flops | bytes accessed | tf_op | source)
XLA Modules:
  0.0 42.1 jit_solution(15559879758498014301)
XLA Ops:
  0.6 1.7 %convert_reduce_fusion = (f32[64]{0:T(128)S(1)}, f32[64]{0:T(128)S(1)}) fusion(bf16[64,4096]{1,0:T(8,128)(2,1)} %param.10), kind=kLoop, calls=%fused_computation | loop fusion | flops 1834624 | bytes 524800 | tf_op jit(solution)/shard_map/reduce | solution.py:279
  2.3 0.5 %collective-permute-start = (bf16[16,40960]{1,0:T(8,128)(2,1)}, bf16[16,40960]{1,0:T(8,128)(2,1)S(1)}, u32[]{:S(2)}, u32[]{:S(2)}) collective-permute-start(bf16[16,40960]{1,0:T(8,128)(2,1)} %t_ref.1), channel_id=1, source_target_pairs={{0,1},{1,0},{2,3},{3,2},{4,5},{5,4},{6,7},{7,6},{8,9},{9,8},{10,11... | collective-permute-start | bytes 3932168 | tf_op jit(solution)/shard_map/ppermute | solution.py:239
  2.8 0.1 collective-permute-start.1
  2.9 4.0 %collective-permute-start.2 = (bf16[1,8,1920]{2,1,0:T(8,128)(2,1)}, bf16[1,8,1920]{2,1,0:T(8,128)(2,1)S(1)}, u32[]{:S(2)}, u32[]{:S(2)}) collective-permute-start(bf16[1,8,1920]{2,1,0:T(8,128)(2,1)} %bitcast.11), channel_id=1, source_target_pairs={{0,8},{2,10},{4,12},{6,14},{8,0},{10,2},{12,4},{14,6},{1,9},{3,11}... | collective-permute-start | bytes 92168 | tf_op jit(solution)/shard_map/ppermute | solution.py:243
  6.9 0.7 %fusion.5 = f32[640,2]{0,1:T(2,128)S(1)} fusion(bf16[640,2]{0,1:T(2,128)(2,1)} %param.9, s32[640,2]{0,1:T(2,128)} %param.7, s32[640,2]{0,1:T(2,128)} %param.8, s32[]{:T(128)S(6)} %mul.51), kind=kLoop, calls=%fused_computation.24 | loop fusion | flops 14080 | bytes 17924 | tf_op jit(solution)/shard_map/add | solution.py:286
  7.7 0.1 dynamic-slice_bitcast_fusion
  7.8 0.2 add_convert_fusion
  8.1 0.1 pad_maximum_fusion.3.stats_ref
  8.2 1.3 %map_own.1.p_ref = f32[144,2048]{1,0:T(8,128)S(1)} custom-call(bf16[144,320]{1,0:T(8,128)(2,1)S(1)} %get-tuple-element.57.w_ref, bf16[16,40960]{1,0:T(8,128)(2,1)S(1)} %copy-done, f32[2,128]{1,0:T(2,128)S(1)} %pad_maximum_fusion.3.stats_ref), custom_call_target="tpu_custom_call" | custom-call | flops 188743680 | bytes 3145728 | tf_op jit(solution)/shard_map/map_own/pallas_call | solution.py:292
  9.5 2.5 %map_rest.1 = bf16[8,16,2176]{2,1,0:T(8,128)(2,1)} custom-call(bf16[144,320]{1,0:T(8,128)(2,1)S(1)} %get-tuple-element.58.w_ref, bf16[16,40960]{1,0:T(8,128)(2,1)S(1)} %collective-permute-done.t_ref, f32[144,2048]{1,0:T(8,128)S(1)} %map_own.1.p_ref, f32[2,128]{1,0:T(2,128)S(1)} %pad_maximum_fusion.3.stats_ref), custom_call_target="tpu_custom_call" | custom-call | flops 188743680 | bytes 4194304 | tf_op jit(solution)/shard_map/map_rest/pallas_call | solution.py:303
  12.0 5.3 %all-to-all-start = ((bf16[8,16,2176]{2,1,0:T(8,128)(2,1)}), bf16[8,16,2176]{2,1,0:T(8,128)(2,1)S(1)}, u32[]{:S(2)}, u32[]{:S(2)}) async-start(bf16[8,16,2176]{2,1,0:T(8,128)(2,1)} %map_rest.1), calls=%async_computation | async-start | bytes 1114112 | tf_op jit(solution)/shard_map/all_to_all | solution.py:319
  17.3 0.1 collective-permute-start.3
  17.5 1.5 %collective-permute-start.6 = (bf16[2,8,1920]{2,1,0:T(8,128)(2,1)S(1)}, bf16[2,8,1920]{2,1,0:T(8,128)(2,1)S(1)}, u32[]{:S(2)}, u32[]{:S(2)}) collective-permute-start(bf16[2,8,1920]{2,1,0:T(8,128)(2,1)S(1)} %constant_dynamic-update-slice_fusion), channel_id=1, source_target_pairs={{0,6},{2,4},{4,2},{6,0},{8,14},{10,12},{12,10},{14,8},{1,7},{3,5},... | collective-permute-start | bytes 184328 | tf_op jit(solution)/shard_map/ppermute | solution.py:243
  19.0 1.5 %collective-permute-start.5 = (bf16[2,8,1920]{2,1,0:T(8,128)(2,1)S(1)}, bf16[2,8,1920]{2,1,0:T(8,128)(2,1)S(1)}, u32[]{:S(2)}, u32[]{:S(2)}) collective-permute-start(bf16[2,8,1920]{2,1,0:T(8,128)(2,1)S(1)} %constant_dynamic-update-slice_fusion), channel_id=1, source_target_pairs={{0,4},{2,6},{4,0},{6,2},{8,12},{10,14},{12,8},{14,10},{1,5},{3,7},... | collective-permute-start | bytes 184328 | tf_op jit(solution)/shard_map/ppermute | solution.py:243
  20.5 0.6 %collective-permute-start.4 = (bf16[2,8,1920]{2,1,0:T(8,128)(2,1)S(1)}, bf16[2,8,1920]{2,1,0:T(8,128)(2,1)S(1)}, u32[]{:S(2)}, u32[]{:S(2)}) collective-permute-start(bf16[2,8,1920]{2,1,0:T(8,128)(2,1)S(1)} %constant_dynamic-update-slice_fusion), channel_id=1, source_target_pairs={{0,2},{2,0},{4,6},{6,4},{8,10},{10,8},{12,14},{14,12},{1,3},{3,1},... | collective-permute-start | bytes 184328 | tf_op jit(solution)/shard_map/ppermute | solution.py:243
  21.0 0.1 broadcast_select_fusion.1
  21.2 8.8 %all-to-all-done.refs_0_ = bf16[8,16,2176]{2,1,0:T(8,128)(2,1)S(1)} async-done(((bf16[8,16,2176]{2,1,0:T(8,128)(2,1)}), bf16[8,16,2176]{2,1,0:T(8,128)(2,1)S(1)}, u32[]{:S(2)}, u32[]{:S(2)}) %all-to-all-start) | async-done | bytes 557088 | tf_op jit(solution)/shard_map/all_to_all | solution.py:319
  30.0 1.2 %logit_grad.1 = (bf16[128,2048]{1,0:T(8,128)(2,1)S(1)}, f32[16,8,128]{2,1,0:T(8,128)}) custom-call(bf16[8,16,2176]{2,1,0:T(8,128)(2,1)S(1)} %all-to-all-done.refs_0_, bf16[128,2048]{1,0:T(8,128)(2,1)S(1)} %pad_maximum_fusion.refs_1_), custom_call_target="tpu_custom_call" | custom-call | flops 2621440 | bytes 1572864 | tf_op jit(solution)/shard_map/logit_grad/pallas_call | solution.py:332
  31.4 0.1 collective-permute-start.7
  31.4 5.5 %all-to-all-start.1 = ((f32[16,8,128]{2,1,0:T(8,128)}), f32[16,8,128]{2,1,0:T(8,128)S(1)}, u32[]{:S(2)}, u32[]{:S(2)}) async-start(f32[16,8,128]{2,1,0:T(8,128)} %get-tuple-element.29), calls=%async_computation.1 | async-start | bytes 131072 | tf_op jit(solution)/shard_map/all_to_all | solution.py:350
  36.9 0.1 pad_add_fusion.place_ref
  37.0 4.5 %weight_grad.1 = (bf16[1920,2048]{1,0:T(8,128)(2,1)}, bf16[64,4096]{1,0:T(8,128)(2,1)}) custom-call(s32[2]{0:T(128)S(1)} %pad_add_fusion.place_ref, bf16[8,8,1920]{2,1,0:T(8,128)(2,1)S(1)} %constant_dynamic-update-slice_fusion.2.own_ref, bf16[64,3968]{1,0:T(8,128)(2,1)S(1)} %collective-permute-done.7.got_ref, bf16[128,2048]{1,0:T(8,128)(2,1)S(1)} %get-tuple-element.37.grad_ref), custom_call_target="tpu_custom_call" | custom-call | flops 1006632960 | bytes 8880128 | tf_op jit(solution)/shard_map/weight_grad/pallas_call | solution.py:355
  41.5 0.0 all-to-all-done.1
  41.6 0.5 %slice_reduce_fusion = f32[64]{0:T(128)} fusion(f32[16,8,128]{2,1,0:T(8,128)S(1)} %all-to-all-done.1), kind=kLoop, calls=%fused_computation.22 | loop fusion | flops 960 | bytes 4352 | tf_op jit(solution)/shard_map/reduce_sum | solution.py:375
  (29 shorter events, 0.3 us)
Async XLA Ops:
  0.6 7.5 %copy-start = (bf16[16,40960]{1,0:T(8,128)(2,1)S(1)}, bf16[16,40960]{1,0:T(8,128)(2,1)}, u32[]{:S(2)}) copy-start(bf16[16,40960]{1,0:T(8,128)(2,1)} %t_ref.1) | copy-start | bytes 3932164
  2.3 7.1 %collective-permute-start = (bf16[16,40960]{1,0:T(8,128)(2,1)}, bf16[16,40960]{1,0:T(8,128)(2,1)S(1)}, u32[]{:S(2)}, u32[]{:S(2)}) collective-permute-start(bf16[16,40960]{1,0:T(8,128)(2,1)} %t_ref.1), channel_id=1, source_target_pairs={{0,1},{1,0},{2,3},{3,2},{4,5},{5,4},{6,7},{7,6},{8,9},{9,8},{10,11... | collective-permute-start | bytes 3932168 | tf_op jit(solution)/shard_map/ppermute | solution.py:239
  2.8 5.2 %collective-permute-start.1 = (f32[2,64]{1,0:T(2,128)S(1)}, f32[2,64]{1,0:T(2,128)S(1)}, u32[]{:S(2)}, u32[]{:S(2)}) collective-permute-start(f32[2,64]{1,0:T(2,128)S(1)} %pad_maximum_fusion.2), channel_id=1, source_target_pairs={{0,1},{1,0},{2,3},{3,2},{4,5},{5,4},{6,7},{7,6},{8,9},{9,8},{10,11... | collective-permute-start | bytes 1544 | tf_op jit(solution)/shard_map/ppermute | solution.py:239
  2.9 9.1 %collective-permute-start.2 = (bf16[1,8,1920]{2,1,0:T(8,128)(2,1)}, bf16[1,8,1920]{2,1,0:T(8,128)(2,1)S(1)}, u32[]{:S(2)}, u32[]{:S(2)}) collective-permute-start(bf16[1,8,1920]{2,1,0:T(8,128)(2,1)} %bitcast.11), channel_id=1, source_target_pairs={{0,8},{2,10},{4,12},{6,14},{8,0},{10,2},{12,4},{14,6},{1,9},{3,11}... | collective-permute-start | bytes 92168 | tf_op jit(solution)/shard_map/ppermute | solution.py:243
  9.5 7.8 %copy-start.1 = (bf16[64,4096]{1,0:T(8,128)(2,1)S(1)}, bf16[64,4096]{1,0:T(8,128)(2,1)}, u32[]{:S(2)}) copy-start(bf16[64,4096]{1,0:T(8,128)(2,1)} %param.10) | copy-start | bytes 1572868
  12.0 5.4 %copy-start.2 = (bf16[8,1920]{1,0:T(8,128)(2,1)S(1)}, bf16[8,1920]{1,0:T(8,128)(2,1)}, u32[]{:S(2)}) copy-start(bf16[8,1920]{1,0:T(8,128)(2,1)} %param.11) | copy-start | bytes 92164
  12.0 17.9 %all-to-all-start = ((bf16[8,16,2176]{2,1,0:T(8,128)(2,1)}), bf16[8,16,2176]{2,1,0:T(8,128)(2,1)S(1)}, u32[]{:S(2)}, u32[]{:S(2)}) async-start(bf16[8,16,2176]{2,1,0:T(8,128)(2,1)} %map_rest.1), calls=%async_computation | async-start | bytes 1114112 | tf_op jit(solution)/shard_map/all_to_all | solution.py:319
  17.3 3.7 %collective-permute-start.3 = (bf16[64,2048]{1,0:T(8,128)(2,1)S(1)}, bf16[64,2048]{1,0:T(8,128)(2,1)S(1)}, u32[]{:S(2)}, u32[]{:S(2)}) collective-permute-start(bf16[64,2048]{1,0:T(8,128)(2,1)S(1)} %constant_dynamic-slice_fusion.1), channel_id=1, source_target_pairs={{0,1},{1,0},{2,3},{3,2},{4,5},{5,4},{6,7},{7,6},{8,9},{9,8},{10,11... | collective-permute-start | bytes 786440 | tf_op jit(solution)/shard_map/ppermute | solution.py:239
  17.5 13.7 %collective-permute-start.6 = (bf16[2,8,1920]{2,1,0:T(8,128)(2,1)S(1)}, bf16[2,8,1920]{2,1,0:T(8,128)(2,1)S(1)}, u32[]{:S(2)}, u32[]{:S(2)}) collective-permute-start(bf16[2,8,1920]{2,1,0:T(8,128)(2,1)S(1)} %constant_dynamic-update-slice_fusion), channel_id=1, source_target_pairs={{0,6},{2,4},{4,2},{6,0},{8,14},{10,12},{12,10},{14,8},{1,7},{3,5},... | collective-permute-start | bytes 184328 | tf_op jit(solution)/shard_map/ppermute | solution.py:243
  19.0 12.2 %collective-permute-start.5 = (bf16[2,8,1920]{2,1,0:T(8,128)(2,1)S(1)}, bf16[2,8,1920]{2,1,0:T(8,128)(2,1)S(1)}, u32[]{:S(2)}, u32[]{:S(2)}) collective-permute-start(bf16[2,8,1920]{2,1,0:T(8,128)(2,1)S(1)} %constant_dynamic-update-slice_fusion), channel_id=1, source_target_pairs={{0,4},{2,6},{4,0},{6,2},{8,12},{10,14},{12,8},{14,10},{1,5},{3,7},... | collective-permute-start | bytes 184328 | tf_op jit(solution)/shard_map/ppermute | solution.py:243
  20.5 10.8 %collective-permute-start.4 = (bf16[2,8,1920]{2,1,0:T(8,128)(2,1)S(1)}, bf16[2,8,1920]{2,1,0:T(8,128)(2,1)S(1)}, u32[]{:S(2)}, u32[]{:S(2)}) collective-permute-start(bf16[2,8,1920]{2,1,0:T(8,128)(2,1)S(1)} %constant_dynamic-update-slice_fusion), channel_id=1, source_target_pairs={{0,2},{2,0},{4,6},{6,4},{8,10},{10,8},{12,14},{14,12},{1,3},{3,1},... | collective-permute-start | bytes 184328 | tf_op jit(solution)/shard_map/ppermute | solution.py:243
  31.4 5.7 %collective-permute-start.7 = (bf16[64,3968]{1,0:T(8,128)(2,1)S(1)}, bf16[64,3968]{1,0:T(8,128)(2,1)S(1)}, u32[]{:S(2)}, u32[]{:S(2)}) collective-permute-start(bf16[64,3968]{1,0:T(8,128)(2,1)S(1)} %pad_maximum_fusion.1), channel_id=1, source_target_pairs={{0,1},{1,0},{2,3},{3,2},{4,5},{5,4},{6,7},{7,6},{8,9},{9,8},{10,11... | collective-permute-start | bytes 1523720 | tf_op jit(solution)/shard_map/ppermute | solution.py:239
  31.4 10.1 %all-to-all-start.1 = ((f32[16,8,128]{2,1,0:T(8,128)}), f32[16,8,128]{2,1,0:T(8,128)S(1)}, u32[]{:S(2)}, u32[]{:S(2)}) async-start(f32[16,8,128]{2,1,0:T(8,128)} %get-tuple-element.29), calls=%async_computation.1 | async-start | bytes 131072 | tf_op jit(solution)/shard_map/all_to_all | solution.py:350
